TPU v7x, 32 devices: a whole 2x2x4 slice. The times are simulated.
32 devices in a mesh: groups: 2 (over x), blk: 16 (over z, y, core).
Axes of the slice: x: 2, y: 2, z: 4, core: 2. Of those that a mesh axis runs over, the one named last changes fastest.
Arguments:
- rhs: bfloat16 [512, 64, 128], P(('groups', 'blk')), parts along dimension 0, may hold values from -6 to 6
- near_blocks: bfloat16 [4096, 128, 128], P(('groups', 'blk')), parts along dimension 0, may hold values from -0.1875 to 0.1875
- near_owner: int32 [4096, 1], P(('groups', 'blk')), parts along dimension 0, may hold values from 0 to 15; in each aligned block of 128 rows (0 to 127, 128 to 255, ...) at most 16 rows name the same one
- near_slot: int32 [4096], P(('groups', 'blk')), parts along dimension 0, may hold values from 0 to 15
- near_offset: int32 [4096], P(('groups', 'blk')), parts along dimension 0, may hold values from -16 to 16
- far_coupling: bfloat16 [8192, 16, 16], P(('groups', 'blk')), parts along dimension 0, may hold values from -1.5 to 1.5
- far_slot: int32 [8192], P(('groups', 'blk')), parts along dimension 0, may hold values from 0 to 15
- far_dev: int32 [8192, 1], P(('groups', 'blk')), parts along dimension 0, may hold values from 0 to 15; in each aligned block of 256 rows (0 to 255, 256 to 511, ...) at most 32 rows name the same one
- far_cslot: int32 [8192], P(('groups', 'blk')), parts along dimension 0, may hold values from 0 to 15
- basis_out: bfloat16 [512, 16, 128], P(('groups', 'blk')), parts along dimension 0, may hold values from -0.375 to 0.375
- basis_in: bfloat16 [512, 16, 128], P(('groups', 'blk')), parts along dimension 0, may hold values from -0.5 to 0.5
Outputs:
- field: bfloat16 [512, 64, 128], P(('groups', 'blk')), parts along dimension 0
There are 2 independent parts, one for each index of `groups`. A program takes and returns all parts, laid end to end along the dimension named above; each array names one. Nothing has to cross between parts.
Inputs may be any that keep to these rules, and one draw needn't show every extreme that they name: `near_owner`: among the rows of one device, at most 16 have the same owner, and some owner has exactly 16 of them in every draw. `far_dev`: among the rows of one device, at most 32 name the same device, and some device is named exactly 32 times in every draw.
All inputs are finite; a program needn't handle non-finite values.
Results may differ from a plain program's by a relative error of at most 0.0051.
Values may be sent and summed in bfloat16 or wider, within the bound.
No kernel may reach another device: no remote copies, remote signals or barrier semaphores. Data moves between devices by JAX's collectives and lax.ppermute only.
A program may use at most 128 MiB of HBM per device.

v0:
```python
import jax
import jax.numpy as jnp
from jax import lax
from jax.sharding import PartitionSpec as P


def with_halo(cells, sides, width):
    for axis, dim in sides:
        count = lax.axis_size(axis)
        head = lax.slice_in_dim(cells, 0, width, axis=dim)
        tail = lax.slice_in_dim(cells, cells.shape[dim] - width, cells.shape[dim], axis=dim)
        cells = jnp.concatenate(
            [
                lax.ppermute(tail, axis, [(i, (i + 1) % count) for i in range(count)]),
                cells,
                lax.ppermute(head, axis, [((i + 1) % count, i) for i in range(count)]),
            ],
            axis=dim,
        )
    return cells


def place_ranks(targets, count):
    onehot = (targets[:, None] == jnp.arange(count, dtype=jnp.int32)[None, :]).astype(jnp.int32)
    before = jnp.cumsum(onehot, axis=0) - onehot
    return jnp.sum(before * onehot, axis=1)


def on_device(
    rhs,
    near_blocks,
    near_owner,
    near_slot,
    near_offset,
    far_coupling,
    far_slot,
    far_dev,
    far_cslot,
    basis_out,
    basis_in,
):
    clusters = rhs.shape[0]
    directions = rhs.shape[1]
    unknowns = rhs.shape[2]
    cycle_size = lax.axis_size("blk")
    stored = near_blocks.shape[0]
    capacity = max(2, 2 * stored // cycle_size)
    owners = near_owner[:, 0]
    target = owners * capacity + place_ranks(owners, cycle_size)
    outbox = (
        jnp.zeros((cycle_size * capacity, unknowns, unknowns), near_blocks.dtype)
        .at[target]
        .set(near_blocks)
    )
    labels = (
        jnp.zeros((cycle_size * capacity, 2), jnp.int32)
        .at[target]
        .set(jnp.stack([near_slot, near_offset], axis=1))
    )
    window = with_halo(rhs, (("blk", 0),), clusters)
    inbox, in_labels = (
        lax.all_to_all(outbox, "blk", split_axis=0, concat_axis=0, tiled=True),
        lax.all_to_all(labels, "blk", split_axis=0, concat_axis=0, tiled=True),
    )
    position = clusters + in_labels[:, 0] + in_labels[:, 1]
    columns = jnp.take(window, position, axis=0)
    products = jnp.einsum("srj,sij->sri", columns, inbox, preferred_element_type=jnp.float32)
    selector = (in_labels[:, 0][None, :] == jnp.arange(clusters, dtype=jnp.int32)[:, None]).astype(
        jnp.float32
    )
    near_sum = jnp.dot(
        selector,
        products.reshape(products.shape[0], -1),
        precision=lax.Precision.HIGHEST,
        preferred_element_type=jnp.float32,
    ).reshape(clusters, directions, unknowns)
    coef_local = jnp.einsum(
        "ckj,crj->crk", basis_in, rhs, preferred_element_type=jnp.float32
    ).astype(jnp.bfloat16)
    rank_k = basis_in.shape[1]
    coef_local = coef_local.reshape(clusters, directions * rank_k)
    pairs = far_slot.shape[0]
    wanted = far_dev[:, 0] * clusters + far_cslot
    piece = lax.all_gather(coef_local, "blk", axis=0, tiled=True)
    inside = (wanted >= 0) & (wanted < piece.shape[0])
    found = jnp.take(piece, jnp.clip(wanted, 0, piece.shape[0] - 1), axis=0)
    chosen = jnp.where(
        inside[:, None], found, jnp.zeros((pairs, directions * rank_k), jnp.bfloat16)
    )
    coupled = jnp.einsum(
        "pkq,prq->prk",
        far_coupling,
        chosen.reshape(pairs, directions, rank_k),
        preferred_element_type=jnp.float32,
    )
    row_pick = (far_slot[None, :] == jnp.arange(clusters, dtype=jnp.int32)[:, None]).astype(
        jnp.float32
    )
    gathered = jnp.dot(
        row_pick,
        coupled.reshape(pairs, -1),
        precision=lax.Precision.HIGHEST,
        preferred_element_type=jnp.float32,
    )
    gathered = gathered.astype(jnp.bfloat16).reshape(clusters, directions, rank_k)
    far_sum = jnp.einsum("crk,ckb->crb", gathered, basis_out, preferred_element_type=jnp.float32)
    return (near_sum + far_sum).astype(jnp.bfloat16)


def solution(mesh):
    placed = (
        P(("groups", "blk"), None, None),
        P(("groups", "blk"), None, None),
        P(("groups", "blk"), None),
        P(("groups", "blk")),
        P(("groups", "blk")),
        P(("groups", "blk"), None, None),
        P(("groups", "blk")),
        P(("groups", "blk"), None),
        P(("groups", "blk")),
        P(("groups", "blk"), None, None),
        P(("groups", "blk"), None, None),
    )
    return jax.shard_map(
        on_device,
        mesh=mesh,
        in_specs=placed,
        out_specs=P(("groups", "blk"), None, None),
        check_vma=False,
    )
```

profile of v0, /device:TPU:19, one launch (start us, length us, event | category | flops | bytes accessed | tf_op | source)
XLA Modules:
  0.0 289.8 jit_solution(8119351048524281814)
XLA Ops:
  0.0 0.8 fusion.5
  0.9 0.8 select_reduce_fusion
  1.8 0.7 fusion.12
  2.5 0.7 pad_add_fusion
  3.2 0.9 scatter_custom_fusion
  4.2 0.8 copy.41
  4.9 6.5 %all-to-all-start = ((s32[16,16,2]{1,2,0:T(2,128)}), s32[16,16,2]{1,2,0:T(2,128)S(1)}, u32[]{:S(2)}, u32[]{:S(2)}) async-start(s32[16,16,2]{1,2,0:T(2,128)} %copy.41), calls=%async_computation | async-start | bytes 32768 | tf_op jit(solution)/shard_map/all_to_all | solution.py:63
  11.4 5.3 %broadcast_in_dim.49 = bf16[256,128,128]{2,1,0:T(8,128)(2,1)} broadcast(bf16[]{:T(256)} %constant.28.clone.1), dimensions={} | broadcast | bytes 8388610 | tf_op jit(solution)/shard_map/broadcast_in_dim | solution.py:51
  16.8 19.3 %scatter_fusion = bf16[256,128,128]{2,1,0:T(8,128)(2,1)} fusion(bf16[256,128,128]{2,1,0:T(8,128)(2,1)} %broadcast_in_dim.49, s32[128]{0:T(128)S(1)} %fusion.12, bf16[128,128,128]{2,1,0:T(8,128)(2,1)} %param.12), kind=kCustom, calls=%fused_computation.3 | custom fusion | bytes 12583424 | tf_op jit(solution)/shard_map/scatter | solution.py:53
  36.1 6.2 %all-to-all-start.1 = ((bf16[256,128,128]{2,1,0:T(8,128)(2,1)}), bf16[256,128,128]{2,1,0:T(8,128)(2,1)}, u32[]{:S(2)}, u32[]{:S(2)}) async-start(bf16[256,128,128]{2,1,0:T(8,128)(2,1)} %scatter_fusion), calls=%async_computation.1 | async-start | bytes 16777216 | tf_op jit(solution)/shard_map/all_to_all | solution.py:62
  42.3 0.4 collective-permute-start.1
  42.7 1.4 collective-permute-start
  44.1 0.9 copy.47
  45.1 0.2 convolution_convert_fusion
  45.3 0.2 copy.44
  45.5 0.3 reshape.44
  45.9 193.8 %all_gather.3 = bf16[256,1024]{1,0:T(8,128)(2,1)S(1)} all-gather(bf16[16,1024]{1,0:T(8,128)(2,1)S(1)} %reshape.44), channel_id=1, replica_groups=mesh['groups'=2,'blk'=16] {'blk'}, dimensions={0}, use_global_device_ids=true | all-gather | bytes 557056 | tf_op jit(solution)/shard_map/all_gather | solution.py:84
  239.7 1.2 gather_fusion.1
  240.8 0.2 copy.45
  241.1 2.2 copy.46
  243.3 1.9 fusion.15
  245.2 1.4 copy.48
  246.7 0.6 convolution_convert_fusion.1
  247.3 0.2 reshape.46
  247.5 0.2 fusion.14
  247.9 1.1 pad_maximum_fusion
  249.0 3.0 %gather_fusion = bf16[256,64,128]{2,1,0:T(8,128)(2,1)} fusion(bf16[48,64,128]{2,1,0:T(8,128)(2,1)S(1)} %pad_maximum_fusion, s32[1024]{0:T(1024)S(1)} %pad_clamp_fusion.1), kind=kCustom, calls=%fused_computation | custom fusion | bytes 8389632 | tf_op jit(solution)/shard_map/jit(_take)/gather | solution.py:66
  252.0 10.4 %fusion = f32[256,64,128]{2,1,0:T(8,128)S(1)} fusion(bf16[256,128,128]{2,1,0:T(8,128)(2,1)} %all-to-all-done.1, bf16[256,64,128]{2,1,0:T(8,128)(2,1)} %gather_fusion, pred[256]{0:T(512)(128)(4,1)S(1)} %get-tuple-element.7), kind=kOutput, calls=%fused_computation.5 | convolution fusion | flops 538968064 | bytes 20971776 | tf_op jit(solution)/shard_map/srj,sij->sri/dot_general | solution.py:67
  262.4 11.1 %copy.56 = f32[32,8,64,128]{3,1,2,0:T(8,128)} copy(f32[32,8,64,128]{3,2,1,0:T(8,128)S(1)} %bitcast.37) | data formatting | bytes 16777216
  273.5 9.0 %copy.43 = f32[8192,256]{1,0:T(8,128)} copy(f32[8192,256]{0,1:T(8,128)} %bitcast.39) | data formatting | bytes 16777216 | tf_op jit(solution)/shard_map/dot_general | solution.py:71
  282.5 6.5 %fusion.4 = bf16[16,64,128]{2,0,1:T(8,128)(2,1)S(1)} fusion(f32[64,128,256]{2,1,0:T(8,128)} %bitcast.38, f32[16,64,128]{2,1,0:T(8,128)S(1)} %fusion.14, s32[256]{0:T(256)S(1)} %bitcast.43), kind=kOutput, calls=%fused_computation.10 | convolution fusion | flops 402919424 | bytes 9176064 | tf_op jit(solution)/shard_map/dot_general | solution.py:71
  289.0 0.8 copy.51
  (32 shorter events, 0.5 us)
Async XLA Ops:
  0.0 247.5 %copy-start = (bf16[16,16,128]{2,1,0:T(8,128)(2,1)S(1)}, bf16[16,16,128]{2,1,0:T(8,128)(2,1)}, u32[]{:S(2)}) copy-start(bf16[16,16,128]{2,1,0:T(8,128)(2,1)} %param.20) | copy-start | bytes 196612
  4.9 31.2 %all-to-all-start = ((s32[16,16,2]{1,2,0:T(2,128)}), s32[16,16,2]{1,2,0:T(2,128)S(1)}, u32[]{:S(2)}, u32[]{:S(2)}) async-start(s32[16,16,2]{1,2,0:T(2,128)} %copy.41), calls=%async_computation | async-start | bytes 32768 | tf_op jit(solution)/shard_map/all_to_all | solution.py:63
  36.1 6.2 %copy-start.1 = (bf16[16,64,128]{2,1,0:T(8,128)(2,1)S(1)}, bf16[16,64,128]{2,1,0:T(8,128)(2,1)}, u32[]{:S(2)}) copy-start(bf16[16,64,128]{2,1,0:T(8,128)(2,1)} %param.11) | copy-start | bytes 786436
  36.1 8.0 %copy-start.2 = (bf16[256,16,16]{0,2,1:T(8,128)(2,1)S(1)}, bf16[256,16,16]{0,2,1:T(8,128)(2,1)}, u32[]{:S(2)}) copy-start(bf16[256,16,16]{0,2,1:T(8,128)(2,1)} %param.16) | copy-start | bytes 393220
  36.1 9.0 %copy-start.3 = (bf16[16,16,128]{2,1,0:T(8,128)(2,1)S(1)}, bf16[16,16,128]{2,1,0:T(8,128)(2,1)}, u32[]{:S(2)}) copy-start(bf16[16,16,128]{2,1,0:T(8,128)(2,1)} %param.21) | copy-start | bytes 196612
  36.1 9.7 %copy-start.6 = (s32[256,1]{0,1:T(1,128)S(1)}, s32[256,1]{0,1:T(1,128)}, u32[]{:S(2)}) copy-start(s32[256,1]{0,1:T(1,128)} %param.18) | copy-start | bytes 3076
  36.1 9.7 %copy-start.7 = (s32[256]{0:T(256)S(1)}, s32[256]{0:T(256)}, u32[]{:S(2)}) copy-start(s32[256]{0:T(256)} %param.19) | copy-start | bytes 3076
  36.1 215.9 %all-to-all-start.1 = ((bf16[256,128,128]{2,1,0:T(8,128)(2,1)}), bf16[256,128,128]{2,1,0:T(8,128)(2,1)}, u32[]{:S(2)}, u32[]{:S(2)}) async-start(bf16[256,128,128]{2,1,0:T(8,128)(2,1)} %scatter_fusion), calls=%async_computation.1 | async-start | bytes 16777216 | tf_op jit(solution)/shard_map/all_to_all | solution.py:62
  42.3 205.5 %collective-permute-start.1 = (bf16[16,64,128]{2,1,0:T(8,128)(2,1)S(1)}, bf16[16,64,128]{2,1,0:T(8,128)(2,1)}, u32[]{:S(2)}, u32[]{:S(2)}) collective-permute-start(bf16[16,64,128]{2,1,0:T(8,128)(2,1)S(1)} %copy-done.1), channel_id=1, source_target_pairs={{1,0},{2,1},{3,2},{4,3},{5,4},{6,5},{7,6},{8,7},{9,8},{10,9},{11,1... | collective-permute-start | bytes 786440 | tf_op jit(solution)/shard_map/ppermute | solution.py:16
  42.7 205.1 %collective-permute-start = (bf16[16,64,128]{2,1,0:T(8,128)(2,1)S(1)}, bf16[16,64,128]{2,1,0:T(8,128)(2,1)}, u32[]{:S(2)}, u32[]{:S(2)}) collective-permute-start(bf16[16,64,128]{2,1,0:T(8,128)(2,1)S(1)} %copy-done.1), channel_id=1, source_target_pairs={{0,1},{1,2},{2,3},{3,4},{4,5},{5,6},{6,7},{7,8},{8,9},{9,10},{10,1... | collective-permute-start | bytes 786440 | tf_op jit(solution)/shard_map/ppermute | solution.py:14
  241.1 5.6 %copy-start.5 = (s32[256]{0:T(256)S(1)}, s32[256]{0:T(256)}, u32[]{:S(2)}) copy-start(s32[256]{0:T(256)} %param.17) | copy-start | bytes 3076
  247.8 4.2 %copy-start.4 = (s32[256,2]{0,1:T(2,128)}, s32[256,2]{0,1:T(2,128)S(1)}, u32[]{:S(2)}) copy-start(s32[256,2]{0,1:T(2,128)S(1)} %all_to_all.13) | copy-start | bytes 6148
  273.5 9.0 %slice-start = ((s32[256,2]{0,1:T(2,128)}), s32[256,1]{0,1:T(1,128)S(1)}, s32[]{:S(2)}) async-start(s32[256,2]{0,1:T(2,128)} %copy-done.4), calls=%async_computation.2 | async-start | bytes 2048 | tf_op jit(solution)/shard_map/slice | solution.py:68
where the time goes:
time: 291 us; the launch traced here: 290 us
  blocking collectives  194 us (67%)
  local copies, waits for them, and re-layouts  57.2 us (20%)
  matrix products  19.8 us (7%)
  starting transfers between devices  14.5 us (5%)
  other arithmetic  4.35 us (1%)
    all_gather x1, blocking collectives, on_device(): piece = lax.all_gather(coef_local, 'blk', axis=0, tiled=True)  194 us
    scatter x1, local copies, waits for them, and re-layouts, on_device(): outbox = jnp.zeros((cycle_size * capacity, unknowns, unknowns), near_bloc...  19.3 us
    unnamed x18, local copies, waits for them, and re-layouts  12.1 us
    dot_general x1, matrix products, on_device(): jnp.einsum('srj,sij->sri', columns, inbox, preferred_element_type=jnp.flo...  10.4 us
    dot_general x1, local copies, waits for them, and re-layouts, on_device(): jnp.dot(selector, products.reshape(products.shape[0], -1), precision=lax....  8.99 us
    dot_general x1, matrix products, on_device(): jnp.dot(selector, products.reshape(products.shape[0], -1), precision=lax....  6.52 us
    all_to_all x1, starting transfers between devices, on_device(): lax.all_to_all(labels, 'blk', split_axis=0, concat_axis=0, tiled=True)  6.5 us
    all_to_all x1, starting transfers between devices, on_device(): lax.all_to_all(outbox, 'blk', split_axis=0, concat_axis=0, tiled=True)  6.17 us
  transfers between devices with their start and end apart: 4, of which 0 were waited for; matrix products, arithmetic and copies ran while one was open for 13% of the time, Pallas kernels for 0%

commit v1 on v0

--- a/solution.py
+++ b/solution.py
@@ -1,7 +1,15 @@
+import functools
+
 import jax
 import jax.numpy as jnp
 from jax import lax
+from jax.experimental import pallas as pl
+from jax.experimental.pallas import tpu as pltpu
 from jax.sharding import PartitionSpec as P
+
+CHUNKS = 2
+DENSE_BYTES = 16 << 20
+VMEM_BYTES = 48 << 20
 
 
 def with_halo(cells, sides, width):
@@ -26,7 +34,7 @@
     return jnp.sum(before * onehot, axis=1)
 
 
-def on_device(
+def routed(
     rhs,
     near_blocks,
     near_owner,
@@ -82,11 +90,7 @@
     pairs = far_slot.shape[0]
     wanted = far_dev[:, 0] * clusters + far_cslot
     piece = lax.all_gather(coef_local, "blk", axis=0, tiled=True)
-    inside = (wanted >= 0) & (wanted < piece.shape[0])
-    found = jnp.take(piece, jnp.clip(wanted, 0, piece.shape[0] - 1), axis=0)
-    chosen = jnp.where(
-        inside[:, None], found, jnp.zeros((pairs, directions * rank_k), jnp.bfloat16)
-    )
+    chosen = jnp.take(piece, wanted, axis=0)
     coupled = jnp.einsum(
         "pkq,prq->prk",
         far_coupling,
@@ -105,6 +109,230 @@
     gathered = gathered.astype(jnp.bfloat16).reshape(clusters, directions, rank_k)
     far_sum = jnp.einsum("crk,ckb->crb", gathered, basis_out, preferred_element_type=jnp.float32)
     return (near_sum + far_sum).astype(jnp.bfloat16)
+
+
+def vmem(*shape_dtype):
+    return pl.BlockSpec(memory_space=pltpu.VMEM)
+
+
+def payload_kernel(rhs_ref, basis_ref, out_ref):
+    clusters, directions, unknowns = rhs_ref.shape
+    rank_k = basis_ref.shape[1]
+    half = clusters // 2
+    base = clusters * directions
+    out_ref[0:base, :] = rhs_ref[...].reshape(base, unknowns)
+    for c in range(half):
+        parts = [
+            lax.dot_general(
+                basis_ref[e],
+                rhs_ref[e],
+                (((1,), (1,)), ((), ())),
+                preferred_element_type=jnp.float32,
+            )
+            for e in (c, c + half)
+        ]
+        out_ref[base + c * rank_k : base + (c + 1) * rank_k, :] = jnp.concatenate(
+            parts, axis=1
+        ).astype(out_ref.dtype)
+
+
+def near_kernel(batch, chunks, pos_ref, row_ref, all_ref, blocks_ref, *rest):
+    sends, keeps, acc = rest[:chunks], rest[chunks : 2 * chunks], rest[2 * chunks]
+    directions, unknowns = acc.shape[1:]
+    acc[...] = jnp.zeros_like(acc)
+
+    def body(step, carry):
+        first = step * batch
+        products = []
+        for k in range(batch):
+            start = pl.multiple_of(row_ref[first + k], directions)
+            products.append(
+                lax.dot_general(
+                    all_ref[pl.ds(start, directions), :],
+                    blocks_ref[first + k],
+                    (((1,), (1,)), ((), ())),
+                    preferred_element_type=jnp.float32,
+                )
+            )
+        for k in range(batch):
+            at = pos_ref[first + k]
+            acc[at] = acc[at] + products[k]
+        return carry
+
+    lax.fori_loop(0, blocks_ref.shape[0] // batch, body, 0)
+    size = sends[0].shape[0]
+    for j in range(chunks):
+        keeps[j][...] = acc[2 * j * size : (2 * j + 1) * size]
+        sends[j][...] = acc[(2 * j + 1) * size : (2 * j + 2) * size].astype(sends[j].dtype)
+
+
+def far_kernel(
+    step_pairs, row_ref, all_ref, couple_ref, low_ref, high_ref, basis_ref, out_ref, picked, weight
+):
+    clusters, rank_k, unknowns = basis_ref.shape
+    pairs = couple_ref.shape[1] // rank_k
+    directions = out_ref.shape[0] // clusters
+    span = step_pairs * rank_k
+
+    def pick(p, carry):
+        start = pl.multiple_of(row_ref[p], rank_k)
+        picked[pl.ds(pl.multiple_of(p * rank_k, rank_k), rank_k), :] = all_ref[
+            pl.ds(start, rank_k), :
+        ]
+        return carry
+
+    lax.fori_loop(0, pairs, pick, 0, unroll=8)
+    sums = []
+    for hot_ref in (low_ref, high_ref):
+        total = jnp.zeros((clusters * rank_k, unknowns), jnp.float32)
+        for j in range(pairs // step_pairs):
+            lanes = slice(j * span, (j + 1) * span)
+            couple = couple_ref[:, lanes]
+            for s in range(clusters):
+                weight[s * rank_k : (s + 1) * rank_k, :] = couple * hot_ref[s : s + 1, lanes]
+            total = total + jnp.dot(
+                weight[...], picked[lanes, :], preferred_element_type=jnp.float32
+            )
+        sums.append(total)
+    total = sums[0] + pltpu.roll(sums[1], unknowns // 2, axis=1)
+    gathered = jnp.transpose(total)[0:directions, :].astype(jnp.bfloat16)
+    lane = lax.broadcasted_iota(jnp.int32, gathered.shape, 1) // rank_k
+    basis = basis_ref[...].reshape(clusters * rank_k, unknowns)
+    for s in range(clusters):
+        own = jnp.where(lane == s, gathered.astype(jnp.float32), 0.0).astype(jnp.bfloat16)
+        out_ref[s * directions : (s + 1) * directions, :] = jnp.dot(
+            own, basis, preferred_element_type=jnp.float32
+        )
+
+
+def stationary(
+    rhs,
+    near_blocks,
+    near_owner,
+    near_slot,
+    near_offset,
+    far_coupling,
+    far_slot,
+    far_dev,
+    far_cslot,
+    basis_out,
+    basis_in,
+):
+    clusters, directions, unknowns = rhs.shape
+    rank_k = basis_in.shape[1]
+    count = lax.axis_size("blk")
+    depth = count // 4
+    me = lax.axis_index("blk")
+    stored = near_blocks.shape[0]
+    pairs = far_slot.shape[0]
+    params = pltpu.CompilerParams(vmem_limit_bytes=VMEM_BYTES)
+
+    rows = clusters * directions + clusters // 2 * rank_k
+    payload = pl.pallas_call(
+        payload_kernel,
+        out_shape=jax.ShapeDtypeStruct((rows, unknowns), jnp.bfloat16),
+        in_specs=[vmem(), vmem()],
+        out_specs=vmem(),
+        compiler_params=params,
+        name="payload",
+    )(rhs, basis_in)
+    everyone = lax.all_gather(payload, "blk", axis=0, tiled=True)
+
+    owner = near_owner[:, 0]
+    per = clusters // CHUNKS
+    relative = (
+        ((owner ^ me) & 1) * (2 * depth)
+        + (((owner ^ me) >> 1) & 1) * depth
+        + ((owner >> 2) - (me >> 2) + depth) % depth
+    )
+    chunk = near_slot // per
+    halves = 2 * depth * per
+    position = (
+        chunk * (2 * halves) + relative * per + near_slot % per
+    )
+    column = (owner * clusters + near_slot + near_offset) % (count * clusters)
+    column_row = (column // clusters) * rows + (column % clusters) * directions
+
+    send_shape = jax.ShapeDtypeStruct((halves, directions, unknowns), jnp.bfloat16)
+    keep_shape = jax.ShapeDtypeStruct((halves, directions, unknowns), jnp.float32)
+    partial_sums = pl.pallas_call(
+        functools.partial(near_kernel, 4, CHUNKS),
+        out_shape=[send_shape] * CHUNKS + [keep_shape] * CHUNKS,
+        grid_spec=pltpu.PrefetchScalarGridSpec(
+            num_scalar_prefetch=2,
+            grid=(1,),
+            in_specs=[vmem(), vmem()],
+            out_specs=[vmem()] * (2 * CHUNKS),
+            scratch_shapes=[
+                pltpu.VMEM((count * clusters, directions, unknowns), jnp.float32)
+            ],
+        ),
+        compiler_params=params,
+        name="near",
+    )(position, column_row, everyone, near_blocks)
+
+    picked_row = (
+        far_dev[:, 0] * rows + clusters * directions + (far_cslot % (clusters // 2)) * rank_k
+    )
+    couple = jnp.transpose(far_coupling, (1, 0, 2)).reshape(rank_k, pairs * rank_k)
+    slots = jnp.arange(clusters, dtype=jnp.int32)[:, None]
+    high = far_cslot >= clusters // 2
+
+    def hot(mask):
+        picks = ((far_slot[None, :] == slots) & mask[None, :]).astype(jnp.bfloat16)
+        return jnp.repeat(picks, rank_k, axis=1)
+
+    step_pairs = 32
+    far = pl.pallas_call(
+        functools.partial(far_kernel, step_pairs),
+        out_shape=jax.ShapeDtypeStruct((clusters * directions, unknowns), jnp.float32),
+        grid_spec=pltpu.PrefetchScalarGridSpec(
+            num_scalar_prefetch=1,
+            grid=(1,),
+            in_specs=[vmem()] * 5,
+            out_specs=vmem(),
+            scratch_shapes=[
+                pltpu.VMEM((pairs * rank_k, unknowns), jnp.bfloat16),
+                pltpu.VMEM((clusters * rank_k, step_pairs * rank_k), jnp.bfloat16),
+            ],
+        ),
+        compiler_params=params,
+        cost_estimate=pl.CostEstimate(
+            flops=4 * clusters * rank_k * pairs * rank_k * unknowns,
+            bytes_accessed=16 << 20,
+            transcendentals=0,
+        ),
+        name="far",
+    )(picked_row, everyone, couple, hot(~high), hot(high), basis_out)
+    far = far.reshape(clusters, directions, unknowns)
+
+    core = [(i, i ^ 1) for i in range(count)]
+    side = [(i, i ^ 2) for i in range(count)]
+    fields = []
+    for j in range(CHUNKS):
+        send, keep = partial_sums[j], partial_sums[CHUNKS + j]
+        got = lax.ppermute(send, "blk", core).astype(jnp.float32)
+        half = depth * per
+        got = lax.ppermute((keep + got)[half:].astype(jnp.bfloat16), "blk", side).astype(
+            jnp.float32
+        ) + (keep + got)[:half]
+        total = got[:per] + far[j * per : (j + 1) * per]
+        for k in range(1, depth):
+            total = total + lax.ppermute(
+                got[k * per : (k + 1) * per].astype(jnp.bfloat16),
+                "blk",
+                [(i, (i + 4 * k) % count) for i in range(count)],
+            ).astype(jnp.float32)
+        fields.append(total.astype(jnp.bfloat16))
+    return jnp.concatenate(fields, axis=0)
+
+
+def on_device(*args):
+    rhs = args[0]
+    count = lax.axis_size("blk")
+    if count % 4 == 0 and count * rhs.size * 4 <= DENSE_BYTES:
+        return stationary(*args)
+    return routed(*args)
 
 
 def solution(mesh):

time: 291 us -> 146 us (0.50)
  the two profiles are of different devices: /device:TPU:19 before, /device:TPU:0 now
where the time goes in v1:
time: 146 us
  waiting for transfers between devices  85 us (58%)
  Pallas kernels  16.9 us (12%)
  local copies, waits for them, and re-layouts  16.2 us (11%)
  between operations  13.6 us (9%)
  starting transfers between devices  9.78 us (7%)
  other arithmetic  4 us (3%)
    all_gather x1, waiting for transfers between devices, stationary(): everyone = lax.all_gather(payload, 'blk', axis=0, tiled=True)  55.6 us
    ppermute x2, waiting for transfers between devices, stationary(): lax.ppermute((keep + got)[half:].astype(jnp.bfloat16), 'blk', side)  18.5 us
    pallas_call x1, Pallas kernels, stationary(): pl.pallas_call(functools.partial(near_kernel, 4, CHUNKS), out_shape=[send...  13 us
    ppermute x6, waiting for transfers between devices, stationary(): lax.ppermute(got[k * per:(k + 1) * per].astype(jnp.bfloat16), 'blk', [(i,...  10.9 us
    ppermute x6, starting transfers between devices, stationary(): lax.ppermute(got[k * per:(k + 1) * per].astype(jnp.bfloat16), 'blk', [(i,...  7.86 us
    unnamed x18, local copies, waits for them, and re-layouts  6.04 us
    reshape x2, local copies, waits for them, and re-layouts, hot(): return jnp.repeat(picks, rank_k, axis=1)  3.55 us
    reshape x1, local copies, waits for them, and re-layouts, stationary(): jnp.transpose(far_coupling, (1, 0, 2)).reshape(rank_k, pairs * rank_k)  2.95 us
  transfers between devices with their start and end apart: 11, of which 6 were waited for; matrix products, arithmetic and copies ran while one was open for 9% of the time, Pallas kernels for 2%

profile of v1, /device:TPU:0, one launch (start us, length us, event | category | flops | bytes accessed | tf_op | source)
XLA Modules:
  0.0 145.5 jit_solution(2194487747834133149)
XLA Ops:
  6.5 0.9 copy-done.1
  7.5 0.8 copy-done.3
  8.3 1.1 payload.1
  9.4 0.7 fusion.18
  10.1 55.6 %all-gather.2.cloned.1.call-done.all_ref = bf16[18432,128]{1,0:T(8,128)(2,1)} async-done(((bf16[1152,128]{1,0:T(8,128)(2,1)}), bf16[18432,128]{1,0:T(8,128)(2,1)}) %all-gather.2.cloned.1.call-update) | async-done | bytes 4718608 | tf_op jit(solution)/shard_map/all_gather | solution.py:239
  65.8 13.0 %near.1 = (bf16[64,64,128]{2,1,0:T(8,128)(2,1)}, bf16[64,64,128]{2,1,0:T(8,128)(2,1)S(1)}, f32[64,64,128]{2,1,0:T(8,128)S(1)}, f32[64,64,128]{2,1,0:T(8,128)}) custom-call(s32[128]{0:T(128)S(1)} %get-tuple-element.28.pos_ref, s32[128]{0:T(128)S(1)} %get-tuple-element.27.row_ref, bf16[18432,128]{1,0:T(8,128)(2,1)} %all-gather.2.cloned.1.call-done.all_ref, ...), custom_call_target="tpu_custom_call" | custom-call | tf_op jit(solution)/shard_map/near/pallas_call | solution.py:258
  78.7 1.1 copy-done.4
  79.8 0.3 collective-permute-start
  80.1 0.6 broadcast_in_dim.5
  80.7 1.8 %reshape.41.high_ref = bf16[16,4096]{1,0:T(8,128)(2,1)S(1)} reshape(bf16[16,256,16]{2,1,0:T(8,128)(2,1)S(1)} %broadcast_in_dim.5) | data formatting | bytes 262144 | tf_op jit(solution)/shard_map/reshape | solution.py:283
  82.5 0.6 broadcast_in_dim.4
  83.1 1.8 %reshape.40.low_ref = bf16[16,4096]{1,0:T(8,128)(2,1)S(1)} reshape(bf16[16,256,16]{2,1,0:T(8,128)(2,1)S(1)} %broadcast_in_dim.4) | data formatting | bytes 262144 | tf_op jit(solution)/shard_map/reshape | solution.py:283
  84.9 2.2 %copy.13 = bf16[16,256,16]{2,1,0:T(8,128)(2,1)} copy(bf16[16,256,16]{1,2,0:T(8,128)(2,1)} %bitcast.22) | data formatting | bytes 262144 | tf_op jit(solution)/shard_map/transpose | solution.py:277
  87.1 2.9 %reshape.39.couple_ref = bf16[16,4096]{1,0:T(8,128)(2,1)S(1)} reshape(bf16[16,256,16]{2,1,0:T(8,128)(2,1)} %copy.13) | data formatting | bytes 262144 | tf_op jit(solution)/shard_map/reshape | solution.py:277
  90.1 0.3 collective-permute-start.5
  90.4 2.3 %copy-done = bf16[18432,128]{1,0:T(8,128)(2,1)S(1)} copy-done((bf16[18432,128]{1,0:T(8,128)(2,1)S(1)}, bf16[18432,128]{1,0:T(8,128)(2,1)}, u32[]{:S(2)}) %copy-start) | copy-done | bytes 4718616
  92.7 2.9 %far.1 = f32[1024,128]{1,0:T(8,128)S(1)} custom-call(s32[256]{0:T(256)S(1)} %fusion.13.row_ref, bf16[18432,128]{1,0:T(8,128)(2,1)S(1)} %copy-done, bf16[16,4096]{1,0:T(8,128)(2,1)S(1)} %reshape.39.couple_ref, bf16[16,4096]{1,0:T(8,128)(2,1)S(1)} %reshape.40.low_ref, bf16[16,4096]{1,0:T(8,128)(2,1)S(1)} %reshape.41.high_ref, bf16[16,16,128]{2,1,0:T(8,128)(2,1)S(1)} %copy-done.2), custom_call_target="tpu_custom_call" | custom-call | flops 536870912 | bytes 16777216 | tf_op jit(solution)/shard_map/far/pallas_call | solution.py:286
  95.7 1.5 %convert_add_fusion.1 = f32[64,64,128]{2,1,0:T(8,128)S(1)} fusion(f32[64,64,128]{2,1,0:T(8,128)S(1)} %get-tuple-element.9, bf16[64,64,128]{2,1,0:T(8,128)(2,1)} %collective-permute-done), kind=kLoop, calls=%fused_computation.1 | loop fusion | flops 1048576 | bytes 5242880 | tf_op jit(solution)/shard_map/add | solution.py:316
  97.3 0.6 collective-permute-start.1
  98.0 0.8 copy-done.5
  98.8 0.4 convert_add_fusion
  99.3 0.7 collective-permute-start.6
  100.1 12.1 %collective-permute-done.1 = bf16[32,64,128]{2,1,0:T(8,128)(2,1)S(1)} collective-permute-done((bf16[32,64,128]{2,1,0:T(8,128)(2,1)S(1)}, bf16[32,64,128]{2,1,0:T(8,128)(2,1)S(1)}, u32[]{:S(2)}, u32[]{:S(2)}) %collective-permute-start.1) | collective-permute-done | bytes 524320 | tf_op jit(solution)/shard_map/ppermute | solution.py:316
  112.4 1.6 %collective-permute-start.2 = (bf16[8,64,128]{2,1,0:T(8,128)(2,1)S(1)}, bf16[8,64,128]{2,1,0:T(8,128)(2,1)S(1)}, u32[]{:S(2)}, u32[]{:S(2)}) collective-permute-start(bf16[8,64,128]{2,1,0:T(8,128)(2,1)S(1)} %get-tuple-element.19), channel_id=1, source_target_pairs={{0,4},{1,5},{2,6},{3,7},{4,8},{5,9},{6,10},{7,11},{8,12},{9,13},{1... | collective-permute-start | bytes 393224 | tf_op jit(solution)/shard_map/ppermute | solution.py:321
  113.9 2.3 %collective-permute-start.4 = (bf16[8,64,128]{2,1,0:T(8,128)(2,1)S(1)}, bf16[8,64,128]{2,1,0:T(8,128)(2,1)S(1)}, u32[]{:S(2)}, u32[]{:S(2)}) collective-permute-start(bf16[8,64,128]{2,1,0:T(8,128)(2,1)S(1)} %get-tuple-element.20), channel_id=1, source_target_pairs={{0,12},{1,13},{2,14},{3,15},{4,0},{5,1},{6,2},{7,3},{8,4},{9,5},{1... | collective-permute-start | bytes 393224 | tf_op jit(solution)/shard_map/ppermute | solution.py:321
  116.3 6.4 %collective-permute-done.6 = bf16[32,64,128]{2,1,0:T(8,128)(2,1)S(1)} collective-permute-done((bf16[32,64,128]{2,1,0:T(8,128)(2,1)S(1)}, bf16[32,64,128]{2,1,0:T(8,128)(2,1)S(1)}, u32[]{:S(2)}, u32[]{:S(2)}) %collective-permute-start.6) | collective-permute-done | bytes 524320 | tf_op jit(solution)/shard_map/ppermute | solution.py:316
  122.9 1.6 %collective-permute-start.7 = (bf16[8,64,128]{2,1,0:T(8,128)(2,1)S(1)}, bf16[8,64,128]{2,1,0:T(8,128)(2,1)S(1)}, u32[]{:S(2)}, u32[]{:S(2)}) collective-permute-start(bf16[8,64,128]{2,1,0:T(8,128)(2,1)S(1)} %get-tuple-element.24), channel_id=1, source_target_pairs={{0,4},{1,5},{2,6},{3,7},{4,8},{5,9},{6,10},{7,11},{8,12},{9,13},{1... | collective-permute-start | bytes 393224 | tf_op jit(solution)/shard_map/ppermute | solution.py:321
  124.5 2.3 %collective-permute-start.9 = (bf16[8,64,128]{2,1,0:T(8,128)(2,1)S(1)}, bf16[8,64,128]{2,1,0:T(8,128)(2,1)S(1)}, u32[]{:S(2)}, u32[]{:S(2)}) collective-permute-start(bf16[8,64,128]{2,1,0:T(8,128)(2,1)S(1)} %get-tuple-element.25), channel_id=1, source_target_pairs={{0,12},{1,13},{2,14},{3,15},{4,0},{5,1},{6,2},{7,3},{8,4},{9,5},{1... | collective-permute-start | bytes 393224 | tf_op jit(solution)/shard_map/ppermute | solution.py:321
  127.0 4.3 %collective-permute-done.7 = bf16[8,64,128]{2,1,0:T(8,128)(2,1)S(1)} collective-permute-done((bf16[8,64,128]{2,1,0:T(8,128)(2,1)S(1)}, bf16[8,64,128]{2,1,0:T(8,128)(2,1)S(1)}, u32[]{:S(2)}, u32[]{:S(2)}) %collective-permute-start.7) | collective-permute-done | bytes 131104 | tf_op jit(solution)/shard_map/ppermute | solution.py:321
  131.2 1.0 collective-permute-done.9
  132.2 5.6 %collective-permute-done.8 = bf16[8,64,128]{2,1,0:T(8,128)(2,1)S(1)} collective-permute-done((bf16[8,64,128]{2,1,0:T(8,128)(2,1)S(1)}, bf16[8,64,128]{2,1,0:T(8,128)(2,1)S(1)}, u32[]{:S(2)}, u32[]{:S(2)}) %collective-permute-start.8) | collective-permute-done | bytes 131104 | tf_op jit(solution)/shard_map/ppermute | solution.py:321
  137.9 0.7 pad_maximum_fusion
  (35 shorter events, 1.0 us)
Async XLA Ops:
  6.5 59.2 %all-gather.2.cloned.1.call-start = ((), (), s32[]{:S(2)}) async-start(), calls=%async_computation | async-start | bytes 5013504 | tf_op jit(solution)/shard_map/all_gather | solution.py:239
  6.5 0.9 copy-start.1
  7.5 0.8 copy-start.3
  65.8 14.3 %copy-start.6 = (s32[256]{0:T(256)S(1)}, s32[256]{0:T(256)}, u32[]{:S(2)}) copy-start(s32[256]{0:T(256)} %param.19) | copy-start | bytes 3076
  65.8 14.3 %copy-start.7 = (s32[256]{0:T(256)S(1)}, s32[256]{0:T(256)}, u32[]{:S(2)}) copy-start(s32[256]{0:T(256)} %param.17) | copy-start | bytes 3076
  78.7 1.1 copy-start.4
  79.8 15.9 %collective-permute-start = (bf16[64,64,128]{2,1,0:T(8,128)(2,1)}, bf16[64,64,128]{2,1,0:T(8,128)(2,1)}, u32[]{:S(2)}, u32[]{:S(2)}) collective-permute-start(bf16[64,64,128]{2,1,0:T(8,128)(2,1)} %get-tuple-element.10), channel_id=1, source_target_pairs={{0,1},{1,0},{2,3},{3,2},{4,5},{5,4},{6,7},{7,6},{8,9},{9,8},{10,11... | collective-permute-start | bytes 3145736 | tf_op jit(solution)/shard_map/ppermute | solution.py:314
  82.5 7.9 %copy-start.8 = (s32[256,1]{0,1:T(1,128)S(1)}, s32[256,1]{0,1:T(1,128)}, u32[]{:S(2)}) copy-start(s32[256,1]{0,1:T(1,128)} %param.18) | copy-start | bytes 3076
  82.5 7.9 %copy-start.2 = (bf16[16,16,128]{2,1,0:T(8,128)(2,1)S(1)}, bf16[16,16,128]{2,1,0:T(8,128)(2,1)}, u32[]{:S(2)}) copy-start(bf16[16,16,128]{2,1,0:T(8,128)(2,1)} %basis_ref.3) | copy-start | bytes 196612
  90.1 7.9 %collective-permute-start.5 = (bf16[64,64,128]{2,1,0:T(8,128)(2,1)}, bf16[64,64,128]{2,1,0:T(8,128)(2,1)S(1)}, u32[]{:S(2)}, u32[]{:S(2)}) collective-permute-start(bf16[64,64,128]{2,1,0:T(8,128)(2,1)} %copy-done.4), channel_id=1, source_target_pairs={{0,1},{1,0},{2,3},{3,2},{4,5},{5,4},{6,7},{7,6},{8,9},{9,8},{10,11... | collective-permute-start | bytes 3145736 | tf_op jit(solution)/shard_map/ppermute | solution.py:314
  90.4 2.3 %copy-start = (bf16[18432,128]{1,0:T(8,128)(2,1)S(1)}, bf16[18432,128]{1,0:T(8,128)(2,1)}, u32[]{:S(2)}) copy-start(bf16[18432,128]{1,0:T(8,128)(2,1)} %all-gather.2.cloned.1.call-done.all_ref) | copy-start | bytes 14155780
  97.2 1.6 %copy-start.5 = (f32[64,64,128]{2,1,0:T(8,128)S(1)}, f32[64,64,128]{2,1,0:T(8,128)}, u32[]{:S(2)}) copy-start(f32[64,64,128]{2,1,0:T(8,128)} %get-tuple-element.11) | copy-start | bytes 6291460
  97.3 14.8 %collective-permute-start.1 = (bf16[32,64,128]{2,1,0:T(8,128)(2,1)S(1)}, bf16[32,64,128]{2,1,0:T(8,128)(2,1)S(1)}, u32[]{:S(2)}, u32[]{:S(2)}) collective-permute-start(bf16[32,64,128]{2,1,0:T(8,128)(2,1)S(1)} %slice.109), channel_id=1, source_target_pairs={{0,2},{1,3},{2,0},{3,1},{4,6},{5,7},{6,4},{7,5},{8,10},{9,11},{10,... | collective-permute-start | bytes 1572872 | tf_op jit(solution)/shard_map/ppermute | solution.py:316
  99.3 23.3 %collective-permute-start.6 = (bf16[32,64,128]{2,1,0:T(8,128)(2,1)S(1)}, bf16[32,64,128]{2,1,0:T(8,128)(2,1)S(1)}, u32[]{:S(2)}, u32[]{:S(2)}) collective-permute-start(bf16[32,64,128]{2,1,0:T(8,128)(2,1)S(1)} %slice.108), channel_id=1, source_target_pairs={{0,2},{1,3},{2,0},{3,1},{4,6},{5,7},{6,4},{7,5},{8,10},{9,11},{10,... | collective-permute-start | bytes 1572872 | tf_op jit(solution)/shard_map/ppermute | solution.py:316
  112.4 14.5 %collective-permute-start.2 = (bf16[8,64,128]{2,1,0:T(8,128)(2,1)S(1)}, bf16[8,64,128]{2,1,0:T(8,128)(2,1)S(1)}, u32[]{:S(2)}, u32[]{:S(2)}) collective-permute-start(bf16[8,64,128]{2,1,0:T(8,128)(2,1)S(1)} %get-tuple-element.19), channel_id=1, source_target_pairs={{0,4},{1,5},{2,6},{3,7},{4,8},{5,9},{6,10},{7,11},{8,12},{9,13},{1... | collective-permute-start | bytes 393224 | tf_op jit(solution)/shard_map/ppermute | solution.py:321
  113.9 13.0 %collective-permute-start.4 = (bf16[8,64,128]{2,1,0:T(8,128)(2,1)S(1)}, bf16[8,64,128]{2,1,0:T(8,128)(2,1)S(1)}, u32[]{:S(2)}, u32[]{:S(2)}) collective-permute-start(bf16[8,64,128]{2,1,0:T(8,128)(2,1)S(1)} %get-tuple-element.20), channel_id=1, source_target_pairs={{0,12},{1,13},{2,14},{3,15},{4,0},{5,1},{6,2},{7,3},{8,4},{9,5},{1... | collective-permute-start | bytes 393224 | tf_op jit(solution)/shard_map/ppermute | solution.py:321
  116.2 10.6 %collective-permute-start.3 = (bf16[8,64,128]{2,1,0:T(8,128)(2,1)S(1)}, bf16[8,64,128]{2,1,0:T(8,128)(2,1)S(1)}, u32[]{:S(2)}, u32[]{:S(2)}) collective-permute-start(bf16[8,64,128]{2,1,0:T(8,128)(2,1)S(1)} %get-tuple-element.21), channel_id=1, source_target_pairs={{0,8},{1,9},{2,10},{3,11},{4,12},{5,13},{6,14},{7,15},{8,0},{9,1},... | collective-permute-start | bytes 393224 | tf_op jit(solution)/shard_map/ppermute | solution.py:321
  122.9 8.3 %collective-permute-start.7 = (bf16[8,64,128]{2,1,0:T(8,128)(2,1)S(1)}, bf16[8,64,128]{2,1,0:T(8,128)(2,1)S(1)}, u32[]{:S(2)}, u32[]{:S(2)}) collective-permute-start(bf16[8,64,128]{2,1,0:T(8,128)(2,1)S(1)} %get-tuple-element.24), channel_id=1, source_target_pairs={{0,4},{1,5},{2,6},{3,7},{4,8},{5,9},{6,10},{7,11},{8,12},{9,13},{1... | collective-permute-start | bytes 393224 | tf_op jit(solution)/shard_map/ppermute | solution.py:321
  124.5 7.7 %collective-permute-start.9 = (bf16[8,64,128]{2,1,0:T(8,128)(2,1)S(1)}, bf16[8,64,128]{2,1,0:T(8,128)(2,1)S(1)}, u32[]{:S(2)}, u32[]{:S(2)}) collective-permute-start(bf16[8,64,128]{2,1,0:T(8,128)(2,1)S(1)} %get-tuple-element.25), channel_id=1, source_target_pairs={{0,12},{1,13},{2,14},{3,15},{4,0},{5,1},{6,2},{7,3},{8,4},{9,5},{1... | collective-permute-start | bytes 393224 | tf_op jit(solution)/shard_map/ppermute | solution.py:321
  126.8 11.0 %collective-permute-start.8 = (bf16[8,64,128]{2,1,0:T(8,128)(2,1)S(1)}, bf16[8,64,128]{2,1,0:T(8,128)(2,1)S(1)}, u32[]{:S(2)}, u32[]{:S(2)}) collective-permute-start(bf16[8,64,128]{2,1,0:T(8,128)(2,1)S(1)} %get-tuple-element.26), channel_id=1, source_target_pairs={{0,8},{1,9},{2,10},{3,11},{4,12},{5,13},{6,14},{7,15},{8,0},{9,1},... | collective-permute-start | bytes 393224 | tf_op jit(solution)/shard_map/ppermute | solution.py:321
Sparse Core Ops, SparseCore 0:
  9.6 56.0 all-gather.1

commit v2 on v0

--- a/solution.py
+++ b/solution.py
@@ -1,7 +1,17 @@
+import functools
+
 import jax
 import jax.numpy as jnp
 from jax import lax
+from jax.experimental import pallas as pl
+from jax.experimental.pallas import tpu as pltpu
 from jax.sharding import PartitionSpec as P
+
+NEAR = 2
+SUBS = 1
+DENSE_BYTES = 16 << 20
+NEAR_VMEM = 24 << 20
+FAR_VMEM = 16 << 20
 
 
 def with_halo(cells, sides, width):
@@ -26,7 +36,7 @@
     return jnp.sum(before * onehot, axis=1)
 
 
-def on_device(
+def routed(
     rhs,
     near_blocks,
     near_owner,
@@ -82,11 +92,7 @@
     pairs = far_slot.shape[0]
     wanted = far_dev[:, 0] * clusters + far_cslot
     piece = lax.all_gather(coef_local, "blk", axis=0, tiled=True)
-    inside = (wanted >= 0) & (wanted < piece.shape[0])
-    found = jnp.take(piece, jnp.clip(wanted, 0, piece.shape[0] - 1), axis=0)
-    chosen = jnp.where(
-        inside[:, None], found, jnp.zeros((pairs, directions * rank_k), jnp.bfloat16)
-    )
+    chosen = jnp.take(piece, wanted, axis=0)
     coupled = jnp.einsum(
         "pkq,prq->prk",
         far_coupling,
@@ -105,6 +111,284 @@
     gathered = gathered.astype(jnp.bfloat16).reshape(clusters, directions, rank_k)
     far_sum = jnp.einsum("crk,ckb->crb", gathered, basis_out, preferred_element_type=jnp.float32)
     return (near_sum + far_sum).astype(jnp.bfloat16)
+
+
+def whole(space=pltpu.VMEM):
+    return pl.BlockSpec(memory_space=space)
+
+
+def coef_kernel(rhs_ref, basis_ref, out_ref):
+    clusters = rhs_ref.shape[0]
+    rank_k = basis_ref.shape[1]
+    half = clusters // 2
+    rows = []
+    for c in range(half):
+        parts = [
+            lax.dot_general(
+                basis_ref[e],
+                rhs_ref[e],
+                (((1,), (1,)), ((), ())),
+                preferred_element_type=jnp.float32,
+            )
+            for e in (c, c + half)
+        ]
+        rows.append(jnp.concatenate(parts, axis=1))
+    for q in range(rank_k):
+        out_ref[q * half : (q + 1) * half, :] = jnp.concatenate(
+            [row[q : q + 1] for row in rows], axis=0
+        )
+
+
+def near_kernel(part, batch, starts_ref, block_ref, pos_ref, row_ref, *rest):
+    shards, rest = rest[: part["shards"]], rest[part["shards"] :]
+    blocks_hbm, rest = rest[0], rest[1:]
+    subs = part["subs"]
+    sends, keeps = rest[:subs], rest[subs : 2 * subs]
+    columns, blocks, acc, sems = rest[2 * subs :]
+    directions, unknowns = acc.shape[1:]
+    load = pltpu.make_async_copy(blocks_hbm, blocks, sems.at[len(shards)])
+    load.start()
+    copies = [
+        pltpu.make_async_copy(shard, columns.at[k], sems.at[k]) for k, shard in enumerate(shards)
+    ]
+    for copy in copies:
+        copy.start()
+    acc[...] = jnp.zeros_like(acc)
+    for copy in copies:
+        copy.wait()
+    load.wait()
+    begin, end = starts_ref[part["at"]], starts_ref[part["at"] + 1]
+    last = blocks.shape[0] - 1
+    dummy = acc.shape[0] - 1
+
+    def body(step, carry):
+        first = begin + step * batch
+        products = []
+        for k in range(batch):
+            at = jnp.minimum(first + k, last)
+            row = row_ref[at]
+            products.append(
+                lax.dot_general(
+                    columns[row // columns.shape[1], row % columns.shape[1]],
+                    blocks[block_ref[at]],
+                    (((1,), (1,)), ((), ())),
+                    preferred_element_type=jnp.float32,
+                )
+            )
+        for k in range(batch):
+            at = jnp.where(first + k < end, pos_ref[jnp.minimum(first + k, last)], dummy)
+            acc[at] = acc[at] + products[k]
+        return carry
+
+    lax.fori_loop(0, (end - begin + batch - 1) // batch, body, 0)
+    size = sends[0].shape[0]
+    for j in range(subs):
+        keeps[j][...] = acc[2 * j * size : (2 * j + 1) * size]
+        sends[j][...] = acc[(2 * j + 1) * size : (2 * j + 2) * size].astype(sends[j].dtype)
+
+
+def far_kernel(coef_ref, couple_ref, slot_ref, pick_ref, half_ref, basis_ref, out_ref):
+    clusters, rank_k, unknowns = basis_ref.shape
+    pairs = couple_ref.shape[2]
+    directions = out_ref.shape[1]
+    half = clusters // 2
+    count = coef_ref.shape[0] // (rank_k * half)
+    coef = coef_ref[...].astype(jnp.float32).reshape(count, rank_k, half, unknowns)
+    hot = (
+        lax.broadcasted_iota(jnp.int32, (clusters, pairs), 0)
+        == jnp.broadcast_to(slot_ref[...], (clusters, pairs))
+    ).astype(jnp.float32).astype(jnp.bfloat16)
+    pick = pick_ref[...]
+    keep = half_ref[...]
+    total = jnp.zeros((clusters * rank_k, unknowns), jnp.float32)
+    for q in range(rank_k):
+        table = coef[:, q].reshape(count * half, unknowns).astype(jnp.bfloat16)
+        chosen = jnp.dot(pick, table, preferred_element_type=jnp.float32).astype(jnp.bfloat16)
+        chosen = chosen * keep
+        couple = couple_ref[q]
+        weight = jnp.concatenate([couple * hot[s : s + 1] for s in range(clusters)], axis=0)
+        total = total + jnp.dot(weight, chosen, preferred_element_type=jnp.float32)
+    total = total + pltpu.roll(total, unknowns // 2, axis=1)
+    gathered = jnp.transpose(total)[0:directions, :].astype(jnp.bfloat16).astype(jnp.float32)
+    lane = lax.broadcasted_iota(jnp.int32, gathered.shape, 1) // rank_k
+    basis = basis_ref[...].reshape(clusters * rank_k, unknowns)
+    for s in range(clusters):
+        own = jnp.where(lane == s, gathered, 0.0).astype(jnp.bfloat16)
+        out_ref[s] = jnp.dot(own, basis, preferred_element_type=jnp.float32)
+
+
+def ring_gather(shard, count):
+    chips = count // 2
+    depth = chips // 2
+
+    def device(place, core):
+        place = place % chips
+        z, y = (place, 0) if place < depth else (chips - 1 - place, 1)
+        return (z * 2 + y) * 2 + core
+
+    ring = [(device(p, c), device(p + 1 - 2 * c, c)) for p in range(chips) for c in range(2)]
+    mate = [(i, i ^ 1) for i in range(count)]
+    slots = {0: shard, 1: lax.ppermute(shard, "blk", mate)}
+    flow = [slots[0], slots[1]]
+    for t in range(1, depth + 1):
+        for x in range(2 if t < depth else 1):
+            flow[x] = lax.ppermute(flow[x], "blk", ring)
+            slots[2 * t + x] = flow[x]
+            slots[2 * (chips - t) + 1 - x] = lax.ppermute(flow[x], "blk", mate)
+    return [slots[k] for k in range(count)]
+
+
+def ring_slot(device, me, count):
+    chips = count // 2
+    depth = chips // 2
+
+    def place(d):
+        z, y = d >> 2, (d >> 1) & 1
+        return jnp.where(y == 0, z, chips - 1 - z)
+
+    sign = 1 - 2 * (me & 1)
+    back = (sign * (place(me) - place(device)) + chips) % chips
+    return 2 * back + ((device ^ me) & 1)
+
+
+def stationary(
+    rhs,
+    near_blocks,
+    near_owner,
+    near_slot,
+    near_offset,
+    far_coupling,
+    far_slot,
+    far_dev,
+    far_cslot,
+    basis_out,
+    basis_in,
+):
+    clusters, directions, unknowns = rhs.shape
+    rank_k = basis_in.shape[1]
+    count = lax.axis_size("blk")
+    depth = count // 4
+    me = lax.axis_index("blk")
+    stored = near_blocks.shape[0]
+    pairs = far_slot.shape[0]
+    half = clusters // 2
+
+    shards = ring_gather(rhs, count)
+
+    coef = pl.pallas_call(
+        coef_kernel,
+        out_shape=jax.ShapeDtypeStruct((half * rank_k, unknowns), jnp.float32),
+        in_specs=[whole(), whole()],
+        out_specs=whole(),
+        name="coef",
+    )(rhs, basis_in).astype(jnp.bfloat16)
+
+    owner = near_owner[:, 0]
+    chunks = NEAR * SUBS
+    per = clusters // chunks
+    relative = (
+        ((owner ^ me) & 1) * (2 * depth)
+        + (((owner ^ me) >> 1) & 1) * depth
+        + ((owner >> 2) - (me >> 2) + depth) % depth
+    )
+    size = 2 * depth * per
+    position = (near_slot // per) % SUBS * (2 * size) + relative * per + near_slot % per
+    column = (owner * clusters + near_slot + near_offset) % (count * clusters)
+    column_row = ring_slot(column // clusters, me, count) * clusters + column % clusters
+    key = near_slot // (per * SUBS)
+    index = jnp.arange(stored, dtype=jnp.int32)
+    ahead = (key[None, :] < key[:, None]) | (
+        (key[None, :] == key[:, None]) & (index[None, :] < index[:, None])
+    )
+    rank = jnp.sum(ahead.astype(jnp.int32), axis=1)
+    here = rank[None, :] == index[:, None]
+    block_at, position, column_row = [
+        jnp.sum(jnp.where(here, values[None, :], 0), axis=1)
+        for values in (index, position, column_row)
+    ]
+    starts = jnp.sum(
+        (key[None, :] < jnp.arange(NEAR + 1, dtype=jnp.int32)[:, None]).astype(jnp.int32), axis=1
+    )
+
+    low = far_cslot % half
+    pick = (
+        (far_dev[:, 0] * half + low)[:, None] == jnp.arange(count * half, dtype=jnp.int32)[None, :]
+    ).astype(jnp.bfloat16)
+    keep = (
+        (far_cslot // half)[:, None] == (jnp.arange(unknowns, dtype=jnp.int32) // directions)[None, :]
+    ).astype(jnp.bfloat16)
+    couple = jnp.transpose(far_coupling, (2, 1, 0))
+
+    coef, pick, keep, couple, starts, block_at, position, column_row, shards[-1] = (
+        lax.optimization_barrier(
+            (coef, pick, keep, couple, starts, block_at, position, column_row, shards[-1])
+        )
+    )
+    coef_all = lax.all_gather(coef, "blk", axis=0, tiled=True)
+
+    near_sums = []
+    for j in range(NEAR):
+        out = pl.pallas_call(
+            functools.partial(near_kernel, dict(shards=count, subs=SUBS, at=j), 4),
+            out_shape=[jax.ShapeDtypeStruct((size, directions, unknowns), jnp.bfloat16)] * SUBS
+            + [jax.ShapeDtypeStruct((size, directions, unknowns), jnp.float32)] * SUBS,
+            in_specs=[whole(pltpu.SMEM)] * 4 + [whole(pl.ANY)] * (count + 1),
+            out_specs=[whole()] * (2 * SUBS),
+            scratch_shapes=[
+                pltpu.VMEM((count, clusters, directions, unknowns), jnp.bfloat16),
+                pltpu.VMEM(near_blocks.shape, jnp.bfloat16),
+                pltpu.VMEM((2 * SUBS * size + 1, directions, unknowns), jnp.float32),
+                pltpu.SemaphoreType.DMA((count + 1,)),
+            ],
+            compiler_params=pltpu.CompilerParams(vmem_limit_bytes=NEAR_VMEM),
+            cost_estimate=pl.CostEstimate(
+                flops=2 * stored * directions * unknowns * unknowns * 8,
+                bytes_accessed=12 << 20,
+                transcendentals=0,
+            ),
+            name="near",
+        )(starts, block_at, position, column_row, *shards, near_blocks)
+        near_sums += list(zip(out[:SUBS], out[SUBS:]))
+
+    far = pl.pallas_call(
+        far_kernel,
+        out_shape=jax.ShapeDtypeStruct((clusters, directions, unknowns), jnp.float32),
+        in_specs=[whole()] * 6,
+        out_specs=whole(),
+        compiler_params=pltpu.CompilerParams(vmem_limit_bytes=FAR_VMEM),
+        cost_estimate=pl.CostEstimate(
+            flops=4 * clusters * rank_k * pairs * rank_k * unknowns,
+            bytes_accessed=8 << 20,
+            transcendentals=0,
+        ),
+        name="far",
+    )(coef_all, couple, far_slot.reshape(1, pairs), pick, keep, basis_out)
+
+    core = [(i, i ^ 1) for i in range(count)]
+    side = [(i, i ^ 2) for i in range(count)]
+    quarter = depth * per
+    fields = []
+    for j, (send, own) in enumerate(near_sums):
+        total = own + lax.ppermute(send, "blk", core).astype(jnp.float32)
+        got = lax.ppermute(total[quarter:].astype(jnp.bfloat16), "blk", side)
+        total = total[:quarter] + got.astype(jnp.float32)
+        field = total[:per] + far[j * per : (j + 1) * per]
+        for k in range(1, depth):
+            field = field + lax.ppermute(
+                total[k * per : (k + 1) * per].astype(jnp.bfloat16),
+                "blk",
+                [(i, (i + 4 * k) % count) for i in range(count)],
+            ).astype(jnp.float32)
+        fields.append(field.astype(jnp.bfloat16))
+    return jnp.concatenate(fields, axis=0)
+
+
+def on_device(*args):
+    rhs = args[0]
+    count = lax.axis_size("blk")
+    if count % 4 == 0 and count * rhs.size * 4 <= DENSE_BYTES:
+        return stationary(*args)
+    return routed(*args)
 
 
 def solution(mesh):

time: 291 us -> 108 us (0.37)
  the two profiles are of different devices: /device:TPU:19 before, /device:TPU:0 now
where the time goes in v2:
time: 108 us; the launch traced here: 107 us
  starting transfers between devices  33.3 us (31%)
  waiting for transfers between devices  24.8 us (23%)
  blocking collectives  21.6 us (20%)
  Pallas kernels  15.9 us (15%)
  other arithmetic  7.23 us (7%)
  local copies, waits for them, and re-layouts  4.3 us (4%)
    all_gather x1, blocking collectives, stationary(): coef_all = lax.all_gather(coef, 'blk', axis=0, tiled=True)  21.6 us
    ppermute x7, starting transfers between devices, ring_gather(): flow[x] = lax.ppermute(flow[x], 'blk', ring)  15 us
    ppermute x2, waiting for transfers between devices, stationary(): got = lax.ppermute(total[quarter:].astype(jnp.bfloat16), 'blk', side)  14.6 us
    ppermute x6, starting transfers between devices, stationary(): lax.ppermute(total[k * per:(k + 1) * per].astype(jnp.bfloat16), 'blk', [(...  12.1 us
    pallas_call x2, Pallas kernels, stationary(): pl.pallas_call(functools.partial(near_kernel, dict(shards=count, subs=SUB...  11.6 us
    ppermute x7, waiting for transfers between devices, ring_gather(): flow[x] = lax.ppermute(flow[x], 'blk', ring)  9.79 us
    unnamed x9, local copies, waits for them, and re-layouts  4.09 us
    ppermute x2, starting transfers between devices, stationary(): got = lax.ppermute(total[quarter:].astype(jnp.bfloat16), 'blk', side)  3.78 us
  transfers between devices with their start and end apart: 25, of which 9 were waited for; matrix products, arithmetic and copies ran while one was open for 7% of the time, Pallas kernels for 10%

profile of v2, /device:TPU:0, one launch (start us, length us, event | category | flops | bytes accessed | tf_op | source)
XLA Modules:
  0.0 107.3 jit_solution(2408112234593325402)
XLA Ops:
  0.0 3.0 %collective-permute-start = (bf16[16,64,128]{2,1,0:T(8,128)(2,1)}, bf16[16,64,128]{2,1,0:T(8,128)(2,1)S(1)}, u32[]{:S(2)}, u32[]{:S(2)}) collective-permute-start(bf16[16,64,128]{2,1,0:T(8,128)(2,1)} %rest_0_.3), channel_id=1, source_target_pairs={{0,4},{1,3},{4,8},{5,1},{8,12},{9,5},{12,14},{13,9},{14,10},{15,13... | collective-permute-start | bytes 786440 | tf_op jit(solution)/shard_map/ppermute | solution.py:235
  3.0 4.5 %collective-permute-done.rest_2_ = bf16[16,64,128]{2,1,0:T(8,128)(2,1)S(1)} collective-permute-done((bf16[16,64,128]{2,1,0:T(8,128)(2,1)}, bf16[16,64,128]{2,1,0:T(8,128)(2,1)S(1)}, u32[]{:S(2)}, u32[]{:S(2)}) %collective-permute-start) | collective-permute-done | bytes 262176 | tf_op jit(solution)/shard_map/ppermute | solution.py:235
  7.5 2.1 %collective-permute-start.4 = (bf16[16,64,128]{2,1,0:T(8,128)(2,1)S(1)}, bf16[16,64,128]{2,1,0:T(8,128)(2,1)S(1)}, u32[]{:S(2)}, u32[]{:S(2)}) collective-permute-start(bf16[16,64,128]{2,1,0:T(8,128)(2,1)S(1)} %collective-permute-done.rest_2_), channel_id=1, source_target_pairs={{0,4},{1,3},{4,8},{5,1},{8,12},{9,5},{12,14},{13,9},{14,10},{15,13... | collective-permute-start | bytes 786440 | tf_op jit(solution)/shard_map/ppermute | solution.py:235
  9.6 1.6 %collective-permute-start.3 = (bf16[16,64,128]{2,1,0:T(8,128)(2,1)S(1)}, bf16[16,64,128]{2,1,0:T(8,128)(2,1)S(1)}, u32[]{:S(2)}, u32[]{:S(2)}) collective-permute-start(bf16[16,64,128]{2,1,0:T(8,128)(2,1)S(1)} %collective-permute-done.2.rest_1_), channel_id=1, source_target_pairs={{0,4},{1,3},{4,8},{5,1},{8,12},{9,5},{12,14},{13,9},{14,10},{15,13... | collective-permute-start | bytes 786440 | tf_op jit(solution)/shard_map/ppermute | solution.py:235
  12.1 1.8 %collective-permute-done.4.rest_4_ = bf16[16,64,128]{2,1,0:T(8,128)(2,1)S(1)} collective-permute-done((bf16[16,64,128]{2,1,0:T(8,128)(2,1)S(1)}, bf16[16,64,128]{2,1,0:T(8,128)(2,1)S(1)}, u32[]{:S(2)}, u32[]{:S(2)}) %collective-permute-start.4) | collective-permute-done | bytes 262176 | tf_op jit(solution)/shard_map/ppermute | solution.py:235
  13.9 2.1 %collective-permute-start.6 = (bf16[16,64,128]{2,1,0:T(8,128)(2,1)S(1)}, bf16[16,64,128]{2,1,0:T(8,128)(2,1)S(1)}, u32[]{:S(2)}, u32[]{:S(2)}) collective-permute-start(bf16[16,64,128]{2,1,0:T(8,128)(2,1)S(1)} %collective-permute-done.4.rest_4_), channel_id=1, source_target_pairs={{0,4},{1,3},{4,8},{5,1},{8,12},{9,5},{12,14},{13,9},{14,10},{15,13... | collective-permute-start | bytes 786440 | tf_op jit(solution)/shard_map/ppermute | solution.py:235
  16.7 2.1 %collective-permute-start.5 = (bf16[16,64,128]{2,1,0:T(8,128)(2,1)S(1)}, bf16[16,64,128]{2,1,0:T(8,128)(2,1)S(1)}, u32[]{:S(2)}, u32[]{:S(2)}) collective-permute-start(bf16[16,64,128]{2,1,0:T(8,128)(2,1)S(1)} %collective-permute-done.3.rest_3_), channel_id=1, source_target_pairs={{0,4},{1,3},{4,8},{5,1},{8,12},{9,5},{12,14},{13,9},{14,10},{15,13... | collective-permute-start | bytes 786440 | tf_op jit(solution)/shard_map/ppermute | solution.py:235
  20.3 2.1 %collective-permute-start.8 = (bf16[16,64,128]{2,1,0:T(8,128)(2,1)S(1)}, bf16[16,64,128]{2,1,0:T(8,128)(2,1)S(1)}, u32[]{:S(2)}, u32[]{:S(2)}) collective-permute-start(bf16[16,64,128]{2,1,0:T(8,128)(2,1)S(1)} %collective-permute-done.6.rest_6_), channel_id=1, source_target_pairs={{0,4},{1,3},{4,8},{5,1},{8,12},{9,5},{12,14},{13,9},{14,10},{15,13... | collective-permute-start | bytes 786440 | tf_op jit(solution)/shard_map/ppermute | solution.py:235
  23.1 2.1 %collective-permute-start.7 = (bf16[16,64,128]{2,1,0:T(8,128)(2,1)S(1)}, bf16[16,64,128]{2,1,0:T(8,128)(2,1)S(1)}, u32[]{:S(2)}, u32[]{:S(2)}) collective-permute-start(bf16[16,64,128]{2,1,0:T(8,128)(2,1)S(1)} %collective-permute-done.5.rest_5_), channel_id=1, source_target_pairs={{0,4},{1,3},{4,8},{5,1},{8,12},{9,5},{12,14},{13,9},{14,10},{15,13... | collective-permute-start | bytes 786440 | tf_op jit(solution)/shard_map/ppermute | solution.py:235
  25.3 1.3 %and_select_fusion.8 = (s32[256]{0:T(256)}, s32[256]{0:T(256)}) fusion(s32[256]{0:T(256)} %param.19, s32[256]{0:T(256)S(1)} %bitcast.23), kind=kLoop, calls=%fused_computation.46 | loop fusion | flops 5120 | bytes 4096 | tf_op jit(solution)/shard_map/jit(floor_divide)/jit(_where)/select_n | solution.py:318
  27.6 1.9 %collective-permute-done.7.rest_7_ = bf16[16,64,128]{2,1,0:T(8,128)(2,1)S(1)} collective-permute-done((bf16[16,64,128]{2,1,0:T(8,128)(2,1)S(1)}, bf16[16,64,128]{2,1,0:T(8,128)(2,1)S(1)}, u32[]{:S(2)}, u32[]{:S(2)}) %collective-permute-start.7) | collective-permute-done | bytes 262176 | tf_op jit(solution)/shard_map/ppermute | solution.py:235
  30.0 0.9 copy.15
  31.0 1.9 %coef.1 = f32[128,128]{1,0:T(8,128)} custom-call(bf16[16,64,128]{2,1,0:T(8,128)(2,1)} %rest_0_.3, bf16[16,16,128]{2,1,0:T(8,128)(2,1)} %basis_ref.2), custom_call_target="tpu_custom_call" | custom-call | tf_op jit(solution)/shard_map/coef/pallas_call | solution.py:278
  32.9 0.8 convert_element_type.59
  33.7 0.8 fusion.8
  34.6 2.2 %copy-done = bf16[128,128,128]{2,1,0:T(8,128)(2,1)S(1)} copy-done((bf16[128,128,128]{2,1,0:T(8,128)(2,1)S(1)}, bf16[128,128,128]{2,1,0:T(8,128)(2,1)}, u32[]{:S(2)}) %copy-start) | copy-done | bytes 4194328
  36.8 0.9 copy-done.1
  37.7 5.7 %near.3 = (bf16[64,64,128]{2,1,0:T(8,128)(2,1)S(1)}, f32[64,64,128]{2,1,0:T(8,128)S(1)}) custom-call(s32[3]{0:T(128)S(1)} %convert_reduce_fusion.1.starts_ref, s32[128]{0:T(128)S(1)} %get-tuple-element.19.block_ref, s32[128]{0:T(128)S(1)} %get-tuple-element.20.pos_ref, s32[128]{0:T(128)S(1)} %get-tuple-element.21.row_ref, ...), custom_call_target="tpu_custom_call" | custom-call | flops 2147483648 | bytes 12582912 | tf_op jit(solution)/shard_map/near/pallas_call | solution.py:331
  43.4 0.8 collective-permute-start.20
  44.2 5.9 %near.2 = (bf16[64,64,128]{2,1,0:T(8,128)(2,1)S(1)}, f32[64,64,128]{2,1,0:T(8,128)S(1)}) custom-call(s32[3]{0:T(128)S(1)} %convert_reduce_fusion.1.starts_ref, s32[128]{0:T(128)S(1)} %get-tuple-element.19.block_ref, s32[128]{0:T(128)S(1)} %get-tuple-element.20.pos_ref, s32[128]{0:T(128)S(1)} %get-tuple-element.21.row_ref, ...), custom_call_target="tpu_custom_call" | custom-call | flops 2147483648 | bytes 12582912 | tf_op jit(solution)/shard_map/near/pallas_call | solution.py:331
  50.6 1.9 %collective-permute-start.21 = (bf16[32,64,128]{2,1,0:T(8,128)(2,1)S(1)}, bf16[32,64,128]{2,1,0:T(8,128)(2,1)S(1)}, u32[]{:S(2)}, u32[]{:S(2)}) collective-permute-start(bf16[32,64,128]{2,1,0:T(8,128)(2,1)S(1)} %slice.102), channel_id=1, source_target_pairs={{0,2},{1,3},{2,0},{3,1},{4,6},{5,7},{6,4},{7,5},{8,10},{9,11},{10,... | collective-permute-start | bytes 1572872 | tf_op jit(solution)/shard_map/ppermute | solution.py:373
  53.2 1.9 %collective-permute-start.16 = (bf16[32,64,128]{2,1,0:T(8,128)(2,1)S(1)}, bf16[32,64,128]{2,1,0:T(8,128)(2,1)S(1)}, u32[]{:S(2)}, u32[]{:S(2)}) collective-permute-start(bf16[32,64,128]{2,1,0:T(8,128)(2,1)S(1)} %slice.103), channel_id=1, source_target_pairs={{0,2},{1,3},{2,0},{3,1},{4,6},{5,7},{6,4},{7,5},{8,10},{9,11},{10,... | collective-permute-start | bytes 1572872 | tf_op jit(solution)/shard_map/ppermute | solution.py:373
  55.1 10.3 %collective-permute-done.21 = bf16[32,64,128]{2,1,0:T(8,128)(2,1)S(1)} collective-permute-done((bf16[32,64,128]{2,1,0:T(8,128)(2,1)S(1)}, bf16[32,64,128]{2,1,0:T(8,128)(2,1)S(1)}, u32[]{:S(2)}, u32[]{:S(2)}) %collective-permute-start.21) | collective-permute-done | bytes 524320 | tf_op jit(solution)/shard_map/ppermute | solution.py:373
  65.6 2.2 %collective-permute-start.22 = (bf16[8,64,128]{2,1,0:T(8,128)(2,1)S(1)}, bf16[8,64,128]{2,1,0:T(8,128)(2,1)S(1)}, u32[]{:S(2)}, u32[]{:S(2)}) collective-permute-start(bf16[8,64,128]{2,1,0:T(8,128)(2,1)S(1)} %get-tuple-element.43), channel_id=1, source_target_pairs={{0,4},{1,5},{2,6},{3,7},{4,8},{5,9},{6,10},{7,11},{8,12},{9,13},{1... | collective-permute-start | bytes 393224 | tf_op jit(solution)/shard_map/ppermute | solution.py:377
  67.8 2.5 %collective-permute-start.23 = (bf16[8,64,128]{2,1,0:T(8,128)(2,1)S(1)}, bf16[8,64,128]{2,1,0:T(8,128)(2,1)S(1)}, u32[]{:S(2)}, u32[]{:S(2)}) collective-permute-start(bf16[8,64,128]{2,1,0:T(8,128)(2,1)S(1)} %get-tuple-element.45), channel_id=1, source_target_pairs={{0,8},{1,9},{2,10},{3,11},{4,12},{5,13},{6,14},{7,15},{8,0},{9,1},... | collective-permute-start | bytes 393224 | tf_op jit(solution)/shard_map/ppermute | solution.py:377
  70.3 1.6 %collective-permute-start.24 = (bf16[8,64,128]{2,1,0:T(8,128)(2,1)S(1)}, bf16[8,64,128]{2,1,0:T(8,128)(2,1)S(1)}, u32[]{:S(2)}, u32[]{:S(2)}) collective-permute-start(bf16[8,64,128]{2,1,0:T(8,128)(2,1)S(1)} %get-tuple-element.44), channel_id=1, source_target_pairs={{0,12},{1,13},{2,14},{3,15},{4,0},{5,1},{6,2},{7,3},{8,4},{9,5},{1... | collective-permute-start | bytes 393224 | tf_op jit(solution)/shard_map/ppermute | solution.py:377
  71.9 4.4 %collective-permute-done.16 = bf16[32,64,128]{2,1,0:T(8,128)(2,1)S(1)} collective-permute-done((bf16[32,64,128]{2,1,0:T(8,128)(2,1)S(1)}, bf16[32,64,128]{2,1,0:T(8,128)(2,1)S(1)}, u32[]{:S(2)}, u32[]{:S(2)}) %collective-permute-start.16) | collective-permute-done | bytes 524320 | tf_op jit(solution)/shard_map/ppermute | solution.py:373
  76.5 1.8 %collective-permute-start.17 = (bf16[8,64,128]{2,1,0:T(8,128)(2,1)S(1)}, bf16[8,64,128]{2,1,0:T(8,128)(2,1)S(1)}, u32[]{:S(2)}, u32[]{:S(2)}) collective-permute-start(bf16[8,64,128]{2,1,0:T(8,128)(2,1)S(1)} %get-tuple-element.40), channel_id=1, source_target_pairs={{0,4},{1,5},{2,6},{3,7},{4,8},{5,9},{6,10},{7,11},{8,12},{9,13},{1... | collective-permute-start | bytes 393224 | tf_op jit(solution)/shard_map/ppermute | solution.py:377
  78.4 2.8 %collective-permute-start.18 = (bf16[8,64,128]{2,1,0:T(8,128)(2,1)S(1)}, bf16[8,64,128]{2,1,0:T(8,128)(2,1)S(1)}, u32[]{:S(2)}, u32[]{:S(2)}) collective-permute-start(bf16[8,64,128]{2,1,0:T(8,128)(2,1)S(1)} %get-tuple-element.42), channel_id=1, source_target_pairs={{0,8},{1,9},{2,10},{3,11},{4,12},{5,13},{6,14},{7,15},{8,0},{9,1},... | collective-permute-start | bytes 393224 | tf_op jit(solution)/shard_map/ppermute | solution.py:377
  81.2 1.2 %collective-permute-start.19 = (bf16[8,64,128]{2,1,0:T(8,128)(2,1)S(1)}, bf16[8,64,128]{2,1,0:T(8,128)(2,1)S(1)}, u32[]{:S(2)}, u32[]{:S(2)}) collective-permute-start(bf16[8,64,128]{2,1,0:T(8,128)(2,1)S(1)} %get-tuple-element.41), channel_id=1, source_target_pairs={{0,12},{1,13},{2,14},{3,15},{4,0},{5,1},{6,2},{7,3},{8,4},{9,5},{1... | collective-permute-start | bytes 393224 | tf_op jit(solution)/shard_map/ppermute | solution.py:377
  82.3 21.6 %all_gather.3.coef_ref = bf16[2048,128]{1,0:T(8,128)(2,1)S(1)} all-gather(bf16[128,128]{1,0:T(8,128)(2,1)S(1)} %convert_element_type.59), channel_id=1, replica_groups=mesh['groups'=2,'blk'=16] {'blk'}, dimensions={0}, use_global_device_ids=true | all-gather | bytes 557056 | tf_op jit(solution)/shard_map/all_gather | solution.py:327
  103.9 2.4 %far.1 = f32[16,64,128]{2,1,0:T(8,128)S(1)} custom-call(bf16[2048,128]{1,0:T(8,128)(2,1)S(1)} %all_gather.3.coef_ref, bf16[16,16,256]{2,1,0:T(8,128)(2,1)S(1)} %bitcast.21, s32[1,256]{1,0:T(1,128)S(1)} %bitcast.22, bf16[256,128]{1,0:T(8,128)(2,1)S(1)} %get-tuple-element.27.pick_ref, bf16[256,128]{1,0:T(8,128)(2,1)S(1)} %get-tuple-element.28.half_ref, ...), custom_call_target="tpu_custom_call" | custom-call | flops 536870912 | bytes 8388608 | tf_op jit(solution)/shard_map/far/pallas_call | solution.py:353
  (51 shorter events, 8.1 us)
Async XLA Ops:
  0.0 7.5 %collective-permute-start = (bf16[16,64,128]{2,1,0:T(8,128)(2,1)}, bf16[16,64,128]{2,1,0:T(8,128)(2,1)S(1)}, u32[]{:S(2)}, u32[]{:S(2)}) collective-permute-start(bf16[16,64,128]{2,1,0:T(8,128)(2,1)} %rest_0_.3), channel_id=1, source_target_pairs={{0,4},{1,3},{4,8},{5,1},{8,12},{9,5},{12,14},{13,9},{14,10},{15,13... | collective-permute-start | bytes 786440 | tf_op jit(solution)/shard_map/ppermute | solution.py:235
  3.0 6.6 %collective-permute-start.2 = (bf16[16,64,128]{2,1,0:T(8,128)(2,1)}, bf16[16,64,128]{2,1,0:T(8,128)(2,1)S(1)}, u32[]{:S(2)}, u32[]{:S(2)}) collective-permute-start(bf16[16,64,128]{2,1,0:T(8,128)(2,1)} %rest_0_.3), channel_id=1, source_target_pairs={{0,1},{1,0},{2,3},{3,2},{4,5},{5,4},{6,7},{7,6},{8,9},{9,8},{10,11... | collective-permute-start | bytes 786440 | tf_op jit(solution)/shard_map/ppermute | solution.py:231
  7.5 6.4 %collective-permute-start.4 = (bf16[16,64,128]{2,1,0:T(8,128)(2,1)S(1)}, bf16[16,64,128]{2,1,0:T(8,128)(2,1)S(1)}, u32[]{:S(2)}, u32[]{:S(2)}) collective-permute-start(bf16[16,64,128]{2,1,0:T(8,128)(2,1)S(1)} %collective-permute-done.rest_2_), channel_id=1, source_target_pairs={{0,4},{1,3},{4,8},{5,1},{8,12},{9,5},{12,14},{13,9},{14,10},{15,13... | collective-permute-start | bytes 786440 | tf_op jit(solution)/shard_map/ppermute | solution.py:235
  9.6 7.1 %collective-permute-start.3 = (bf16[16,64,128]{2,1,0:T(8,128)(2,1)S(1)}, bf16[16,64,128]{2,1,0:T(8,128)(2,1)S(1)}, u32[]{:S(2)}, u32[]{:S(2)}) collective-permute-start(bf16[16,64,128]{2,1,0:T(8,128)(2,1)S(1)} %collective-permute-done.2.rest_1_), channel_id=1, source_target_pairs={{0,4},{1,3},{4,8},{5,1},{8,12},{9,5},{12,14},{13,9},{14,10},{15,13... | collective-permute-start | bytes 786440 | tf_op jit(solution)/shard_map/ppermute | solution.py:235
  13.9 6.4 %collective-permute-start.6 = (bf16[16,64,128]{2,1,0:T(8,128)(2,1)S(1)}, bf16[16,64,128]{2,1,0:T(8,128)(2,1)S(1)}, u32[]{:S(2)}, u32[]{:S(2)}) collective-permute-start(bf16[16,64,128]{2,1,0:T(8,128)(2,1)S(1)} %collective-permute-done.4.rest_4_), channel_id=1, source_target_pairs={{0,4},{1,3},{4,8},{5,1},{8,12},{9,5},{12,14},{13,9},{14,10},{15,13... | collective-permute-start | bytes 786440 | tf_op jit(solution)/shard_map/ppermute | solution.py:235
  16.7 6.4 %collective-permute-start.5 = (bf16[16,64,128]{2,1,0:T(8,128)(2,1)S(1)}, bf16[16,64,128]{2,1,0:T(8,128)(2,1)S(1)}, u32[]{:S(2)}, u32[]{:S(2)}) collective-permute-start(bf16[16,64,128]{2,1,0:T(8,128)(2,1)S(1)} %collective-permute-done.3.rest_3_), channel_id=1, source_target_pairs={{0,4},{1,3},{4,8},{5,1},{8,12},{9,5},{12,14},{13,9},{14,10},{15,13... | collective-permute-start | bytes 786440 | tf_op jit(solution)/shard_map/ppermute | solution.py:235
  19.6 6.9 %collective-permute-start.1 = (bf16[16,64,128]{2,1,0:T(8,128)(2,1)S(1)}, bf16[16,64,128]{2,1,0:T(8,128)(2,1)S(1)}, u32[]{:S(2)}, u32[]{:S(2)}) collective-permute-start(bf16[16,64,128]{2,1,0:T(8,128)(2,1)S(1)} %collective-permute-done.rest_2_), channel_id=1, source_target_pairs={{0,1},{1,0},{2,3},{3,2},{4,5},{5,4},{6,7},{7,6},{8,9},{9,8},{10,11... | collective-permute-start | bytes 786440 | tf_op jit(solution)/shard_map/ppermute | solution.py:237
  19.6 7.4 %collective-permute-start.13 = (bf16[16,64,128]{2,1,0:T(8,128)(2,1)S(1)}, bf16[16,64,128]{2,1,0:T(8,128)(2,1)S(1)}, u32[]{:S(2)}, u32[]{:S(2)}) collective-permute-start(bf16[16,64,128]{2,1,0:T(8,128)(2,1)S(1)} %collective-permute-done.4.rest_4_), channel_id=1, source_target_pairs={{0,1},{1,0},{2,3},{3,2},{4,5},{5,4},{6,7},{7,6},{8,9},{9,8},{10,11... | collective-permute-start | bytes 786440 | tf_op jit(solution)/shard_map/ppermute | solution.py:237
  20.3 6.9 %collective-permute-start.8 = (bf16[16,64,128]{2,1,0:T(8,128)(2,1)S(1)}, bf16[16,64,128]{2,1,0:T(8,128)(2,1)S(1)}, u32[]{:S(2)}, u32[]{:S(2)}) collective-permute-start(bf16[16,64,128]{2,1,0:T(8,128)(2,1)S(1)} %collective-permute-done.6.rest_6_), channel_id=1, source_target_pairs={{0,4},{1,3},{4,8},{5,1},{8,12},{9,5},{12,14},{13,9},{14,10},{15,13... | collective-permute-start | bytes 786440 | tf_op jit(solution)/shard_map/ppermute | solution.py:235
  23.1 6.4 %collective-permute-start.7 = (bf16[16,64,128]{2,1,0:T(8,128)(2,1)S(1)}, bf16[16,64,128]{2,1,0:T(8,128)(2,1)S(1)}, u32[]{:S(2)}, u32[]{:S(2)}) collective-permute-start(bf16[16,64,128]{2,1,0:T(8,128)(2,1)S(1)} %collective-permute-done.5.rest_5_), channel_id=1, source_target_pairs={{0,4},{1,3},{4,8},{5,1},{8,12},{9,5},{12,14},{13,9},{14,10},{15,13... | collective-permute-start | bytes 786440 | tf_op jit(solution)/shard_map/ppermute | solution.py:235
  26.5 8.0 %collective-permute-start.14 = (bf16[16,64,128]{2,1,0:T(8,128)(2,1)S(1)}, bf16[16,64,128]{2,1,0:T(8,128)(2,1)S(1)}, u32[]{:S(2)}, u32[]{:S(2)}) collective-permute-start(bf16[16,64,128]{2,1,0:T(8,128)(2,1)S(1)} %collective-permute-done.3.rest_3_), channel_id=1, source_target_pairs={{0,1},{1,0},{2,3},{3,2},{4,5},{5,4},{6,7},{7,6},{8,9},{9,8},{10,11... | collective-permute-start | bytes 786440 | tf_op jit(solution)/shard_map/ppermute | solution.py:237
  26.5 8.0 %collective-permute-start.11 = (bf16[16,64,128]{2,1,0:T(8,128)(2,1)S(1)}, bf16[16,64,128]{2,1,0:T(8,128)(2,1)S(1)}, u32[]{:S(2)}, u32[]{:S(2)}) collective-permute-start(bf16[16,64,128]{2,1,0:T(8,128)(2,1)S(1)} %collective-permute-done.6.rest_6_), channel_id=1, source_target_pairs={{0,1},{1,0},{2,3},{3,2},{4,5},{5,4},{6,7},{7,6},{8,9},{9,8},{10,11... | collective-permute-start | bytes 786440 | tf_op jit(solution)/shard_map/ppermute | solution.py:237
  27.1 7.5 %collective-permute-start.12 = (bf16[16,64,128]{2,1,0:T(8,128)(2,1)S(1)}, bf16[16,64,128]{2,1,0:T(8,128)(2,1)S(1)}, u32[]{:S(2)}, u32[]{:S(2)}) collective-permute-start(bf16[16,64,128]{2,1,0:T(8,128)(2,1)S(1)} %collective-permute-done.5.rest_5_), channel_id=1, source_target_pairs={{0,1},{1,0},{2,3},{3,2},{4,5},{5,4},{6,7},{7,6},{8,9},{9,8},{10,11... | collective-permute-start | bytes 786440 | tf_op jit(solution)/shard_map/ppermute | solution.py:237
  27.1 7.4 %collective-permute-start.9 = (bf16[16,64,128]{2,1,0:T(8,128)(2,1)S(1)}, bf16[16,64,128]{2,1,0:T(8,128)(2,1)}, u32[]{:S(2)}, u32[]{:S(2)}) collective-permute-start(bf16[16,64,128]{2,1,0:T(8,128)(2,1)S(1)} %collective-permute-done.8.rest_8_), channel_id=1, source_target_pairs={{0,1},{1,0},{2,3},{3,2},{4,5},{5,4},{6,7},{7,6},{8,9},{9,8},{10,11... | collective-permute-start | bytes 786440 | tf_op jit(solution)/shard_map/ppermute | solution.py:237
  29.5 5.1 %collective-permute-start.10 = (bf16[16,64,128]{2,1,0:T(8,128)(2,1)S(1)}, bf16[16,64,128]{2,1,0:T(8,128)(2,1)}, u32[]{:S(2)}, u32[]{:S(2)}) collective-permute-start(bf16[16,64,128]{2,1,0:T(8,128)(2,1)S(1)} %collective-permute-done.7.rest_7_), channel_id=1, source_target_pairs={{0,1},{1,0},{2,3},{3,2},{4,5},{5,4},{6,7},{7,6},{8,9},{9,8},{10,11... | collective-permute-start | bytes 786440 | tf_op jit(solution)/shard_map/ppermute | solution.py:237
  34.6 2.2 %copy-start = (bf16[128,128,128]{2,1,0:T(8,128)(2,1)S(1)}, bf16[128,128,128]{2,1,0:T(8,128)(2,1)}, u32[]{:S(2)}) copy-start(bf16[128,128,128]{2,1,0:T(8,128)(2,1)} %rest_16_.3) | copy-start | bytes 12582916
  36.8 0.9 copy-start.1
  43.4 6.8 %collective-permute-start.20 = (bf16[64,64,128]{2,1,0:T(8,128)(2,1)S(1)}, bf16[64,64,128]{2,1,0:T(8,128)(2,1)S(1)}, u32[]{:S(2)}, u32[]{:S(2)}) collective-permute-start(bf16[64,64,128]{2,1,0:T(8,128)(2,1)S(1)} %get-tuple-element.30), channel_id=1, source_target_pairs={{0,1},{1,0},{2,3},{3,2},{4,5},{5,4},{6,7},{7,6},{8,9},{9,8},{10,11... | collective-permute-start | bytes 3145736 | tf_op jit(solution)/shard_map/ppermute | solution.py:372
  50.1 2.7 %collective-permute-start.15 = (bf16[64,64,128]{2,1,0:T(8,128)(2,1)S(1)}, bf16[64,64,128]{2,1,0:T(8,128)(2,1)S(1)}, u32[]{:S(2)}, u32[]{:S(2)}) collective-permute-start(bf16[64,64,128]{2,1,0:T(8,128)(2,1)S(1)} %get-tuple-element.24), channel_id=1, source_target_pairs={{0,1},{1,0},{2,3},{3,2},{4,5},{5,4},{6,7},{7,6},{8,9},{9,8},{10,11... | collective-permute-start | bytes 3145736 | tf_op jit(solution)/shard_map/ppermute | solution.py:372
  50.6 14.8 %collective-permute-start.21 = (bf16[32,64,128]{2,1,0:T(8,128)(2,1)S(1)}, bf16[32,64,128]{2,1,0:T(8,128)(2,1)S(1)}, u32[]{:S(2)}, u32[]{:S(2)}) collective-permute-start(bf16[32,64,128]{2,1,0:T(8,128)(2,1)S(1)} %slice.102), channel_id=1, source_target_pairs={{0,2},{1,3},{2,0},{3,1},{4,6},{5,7},{6,4},{7,5},{8,10},{9,11},{10,... | collective-permute-start | bytes 1572872 | tf_op jit(solution)/shard_map/ppermute | solution.py:373
  53.2 23.1 %collective-permute-start.16 = (bf16[32,64,128]{2,1,0:T(8,128)(2,1)S(1)}, bf16[32,64,128]{2,1,0:T(8,128)(2,1)S(1)}, u32[]{:S(2)}, u32[]{:S(2)}) collective-permute-start(bf16[32,64,128]{2,1,0:T(8,128)(2,1)S(1)} %slice.103), channel_id=1, source_target_pairs={{0,2},{1,3},{2,0},{3,1},{4,6},{5,7},{6,4},{7,5},{8,10},{9,11},{10,... | collective-permute-start | bytes 1572872 | tf_op jit(solution)/shard_map/ppermute | solution.py:373
  65.6 15.5 %collective-permute-start.22 = (bf16[8,64,128]{2,1,0:T(8,128)(2,1)S(1)}, bf16[8,64,128]{2,1,0:T(8,128)(2,1)S(1)}, u32[]{:S(2)}, u32[]{:S(2)}) collective-permute-start(bf16[8,64,128]{2,1,0:T(8,128)(2,1)S(1)} %get-tuple-element.43), channel_id=1, source_target_pairs={{0,4},{1,5},{2,6},{3,7},{4,8},{5,9},{6,10},{7,11},{8,12},{9,13},{1... | collective-permute-start | bytes 393224 | tf_op jit(solution)/shard_map/ppermute | solution.py:377
  67.8 38.6 %collective-permute-start.23 = (bf16[8,64,128]{2,1,0:T(8,128)(2,1)S(1)}, bf16[8,64,128]{2,1,0:T(8,128)(2,1)S(1)}, u32[]{:S(2)}, u32[]{:S(2)}) collective-permute-start(bf16[8,64,128]{2,1,0:T(8,128)(2,1)S(1)} %get-tuple-element.45), channel_id=1, source_target_pairs={{0,8},{1,9},{2,10},{3,11},{4,12},{5,13},{6,14},{7,15},{8,0},{9,1},... | collective-permute-start | bytes 393224 | tf_op jit(solution)/shard_map/ppermute | solution.py:377
  70.3 33.6 %copy-start.2 = (bf16[16,16,128]{2,1,0:T(8,128)(2,1)S(1)}, bf16[16,16,128]{2,1,0:T(8,128)(2,1)}, u32[]{:S(2)}) copy-start(bf16[16,16,128]{2,1,0:T(8,128)(2,1)} %basis_ref.3) | copy-start | bytes 196612
  70.3 33.6 %copy-start.3 = (s32[256]{0:T(256)S(1)}, s32[256]{0:T(256)}, u32[]{:S(2)}) copy-start(s32[256]{0:T(256)} %param.17) | copy-start | bytes 3076
  70.3 36.0 %collective-permute-start.24 = (bf16[8,64,128]{2,1,0:T(8,128)(2,1)S(1)}, bf16[8,64,128]{2,1,0:T(8,128)(2,1)S(1)}, u32[]{:S(2)}, u32[]{:S(2)}) collective-permute-start(bf16[8,64,128]{2,1,0:T(8,128)(2,1)S(1)} %get-tuple-element.44), channel_id=1, source_target_pairs={{0,12},{1,13},{2,14},{3,15},{4,0},{5,1},{6,2},{7,3},{8,4},{9,5},{1... | collective-permute-start | bytes 393224 | tf_op jit(solution)/shard_map/ppermute | solution.py:377
  76.5 29.8 %collective-permute-start.17 = (bf16[8,64,128]{2,1,0:T(8,128)(2,1)S(1)}, bf16[8,64,128]{2,1,0:T(8,128)(2,1)S(1)}, u32[]{:S(2)}, u32[]{:S(2)}) collective-permute-start(bf16[8,64,128]{2,1,0:T(8,128)(2,1)S(1)} %get-tuple-element.40), channel_id=1, source_target_pairs={{0,4},{1,5},{2,6},{3,7},{4,8},{5,9},{6,10},{7,11},{8,12},{9,13},{1... | collective-permute-start | bytes 393224 | tf_op jit(solution)/shard_map/ppermute | solution.py:377
  78.4 28.0 %collective-permute-start.18 = (bf16[8,64,128]{2,1,0:T(8,128)(2,1)S(1)}, bf16[8,64,128]{2,1,0:T(8,128)(2,1)S(1)}, u32[]{:S(2)}, u32[]{:S(2)}) collective-permute-start(bf16[8,64,128]{2,1,0:T(8,128)(2,1)S(1)} %get-tuple-element.42), channel_id=1, source_target_pairs={{0,8},{1,9},{2,10},{3,11},{4,12},{5,13},{6,14},{7,15},{8,0},{9,1},... | collective-permute-start | bytes 393224 | tf_op jit(solution)/shard_map/ppermute | solution.py:377
  81.2 25.2 %collective-permute-start.19 = (bf16[8,64,128]{2,1,0:T(8,128)(2,1)S(1)}, bf16[8,64,128]{2,1,0:T(8,128)(2,1)S(1)}, u32[]{:S(2)}, u32[]{:S(2)}) collective-permute-start(bf16[8,64,128]{2,1,0:T(8,128)(2,1)S(1)} %get-tuple-element.41), channel_id=1, source_target_pairs={{0,12},{1,13},{2,14},{3,15},{4,0},{5,1},{6,2},{7,3},{8,4},{9,5},{1... | collective-permute-start | bytes 393224 | tf_op jit(solution)/shard_map/ppermute | solution.py:377

commit v3 on v2

--- a/solution.py
+++ b/solution.py
@@ -7,10 +7,8 @@
 from jax.experimental.pallas import tpu as pltpu
 from jax.sharding import PartitionSpec as P
 
-NEAR = 2
-SUBS = 1
 DENSE_BYTES = 16 << 20
-NEAR_VMEM = 24 << 20
+NEAR_VMEM = 46 << 20
 FAR_VMEM = 16 << 20
 
 
@@ -117,7 +115,8 @@
     return pl.BlockSpec(memory_space=space)
 
 
-def coef_kernel(rhs_ref, basis_ref, out_ref):
+def coef_kernel(rhs_ref, basis_ref, out_ref, copy_ref):
+    copy_ref[...] = rhs_ref[...]
     clusters = rhs_ref.shape[0]
     rank_k = basis_ref.shape[1]
     half = clusters // 2
@@ -142,9 +141,7 @@
 def near_kernel(part, batch, starts_ref, block_ref, pos_ref, row_ref, *rest):
     shards, rest = rest[: part["shards"]], rest[part["shards"] :]
     blocks_hbm, rest = rest[0], rest[1:]
-    subs = part["subs"]
-    sends, keeps = rest[:subs], rest[subs : 2 * subs]
-    columns, blocks, acc, sems = rest[2 * subs :]
+    send_ref, keep_ref, columns, blocks, acc, sems = rest
     directions, unknowns = acc.shape[1:]
     load = pltpu.make_async_copy(blocks_hbm, blocks, sems.at[len(shards)])
     load.start()
@@ -181,19 +178,20 @@
         return carry
 
     lax.fori_loop(0, (end - begin + batch - 1) // batch, body, 0)
-    size = sends[0].shape[0]
-    for j in range(subs):
-        keeps[j][...] = acc[2 * j * size : (2 * j + 1) * size]
-        sends[j][...] = acc[(2 * j + 1) * size : (2 * j + 2) * size].astype(sends[j].dtype)
-
-
-def far_kernel(coef_ref, couple_ref, slot_ref, pick_ref, half_ref, basis_ref, out_ref):
+    size = send_ref.shape[0]
+    keep_ref[...] = acc[0:size]
+    send_ref[...] = acc[size : 2 * size].astype(send_ref.dtype)
+
+
+def far_kernel(*refs):
+    coef_refs, (couple_ref, slot_ref, pick_ref, half_ref, basis_ref, out_ref) = refs[:4], refs[4:]
     clusters, rank_k, unknowns = basis_ref.shape
     pairs = couple_ref.shape[2]
     directions = out_ref.shape[1]
     half = clusters // 2
-    count = coef_ref.shape[0] // (rank_k * half)
-    coef = coef_ref[...].astype(jnp.float32).reshape(count, rank_k, half, unknowns)
+    coef = jnp.concatenate([ref[...].astype(jnp.float32) for ref in coef_refs], axis=0)
+    coef = coef.reshape(-1, rank_k, half, unknowns)
+    count = coef.shape[0]
     hot = (
         lax.broadcasted_iota(jnp.int32, (clusters, pairs), 0)
         == jnp.broadcast_to(slot_ref[...], (clusters, pairs))
@@ -217,38 +215,42 @@
         out_ref[s] = jnp.dot(own, basis, preferred_element_type=jnp.float32)
 
 
-def ring_gather(shard, count):
+def ring_device(place, core, chips):
+    depth = chips // 2
+    place = place % chips
+    z, y = (place, 0) if place < depth else (chips - 1 - place, 1)
+    return (z * 2 + y) * 2 + core
+
+
+def ring_pairs(count):
     chips = count // 2
-    depth = chips // 2
-
-    def device(place, core):
-        place = place % chips
-        z, y = (place, 0) if place < depth else (chips - 1 - place, 1)
-        return (z * 2 + y) * 2 + core
-
-    ring = [(device(p, c), device(p + 1 - 2 * c, c)) for p in range(chips) for c in range(2)]
-    mate = [(i, i ^ 1) for i in range(count)]
-    slots = {0: shard, 1: lax.ppermute(shard, "blk", mate)}
-    flow = [slots[0], slots[1]]
-    for t in range(1, depth + 1):
-        for x in range(2 if t < depth else 1):
-            flow[x] = lax.ppermute(flow[x], "blk", ring)
-            slots[2 * t + x] = flow[x]
-            slots[2 * (chips - t) + 1 - x] = lax.ppermute(flow[x], "blk", mate)
-    return [slots[k] for k in range(count)]
-
-
-def ring_slot(device, me, count):
+    cores = [(p, c) for p in range(chips) for c in range(2)]
+    ahead = [(ring_device(p, c, chips), ring_device(p + 1 - 2 * c, c, chips)) for p, c in cores]
+    cross = [
+        (ring_device(p, c, chips), ring_device(p - 1 + 2 * c, 1 - c, chips)) for p, c in cores
+    ]
+    return ahead, cross
+
+
+def ring_place(device, chips):
+    z, y = device >> 2, (device >> 1) & 1
+    return jnp.where(y == 0, z, chips - 1 - z)
+
+
+def gather_slot(device, me, count):
     chips = count // 2
-    depth = chips // 2
-
-    def place(d):
-        z, y = d >> 2, (d >> 1) & 1
-        return jnp.where(y == 0, z, chips - 1 - z)
-
-    sign = 1 - 2 * (me & 1)
-    back = (sign * (place(me) - place(device)) + chips) % chips
-    return 2 * back + ((device ^ me) & 1)
+    back = (1 - 2 * (me & 1)) * (ring_place(me, chips) - ring_place(device, chips))
+    return 2 * ((back + chips) % chips) + ((device ^ me) & 1)
+
+
+def scatter_place(device, me, count):
+    chips = count // 2
+    half = chips // 2
+    ahead = (ring_place(device, chips) - ring_place(me, chips) + chips) % chips
+    core = device & 1
+    handler = jnp.where(ahead % half == 0, core, (ahead > half).astype(jnp.int32))
+    steps = jnp.where(handler == 0, ahead, (chips - ahead) % chips)
+    return handler, steps, core ^ handler
 
 
 def stationary(
@@ -267,93 +269,140 @@
     clusters, directions, unknowns = rhs.shape
     rank_k = basis_in.shape[1]
     count = lax.axis_size("blk")
-    depth = count // 4
+    chips = count // 2
+    depth = chips // 2
     me = lax.axis_index("blk")
     stored = near_blocks.shape[0]
     pairs = far_slot.shape[0]
     half = clusters // 2
-
-    shards = ring_gather(rhs, count)
-
-    coef = pl.pallas_call(
+    ahead, cross = ring_pairs(count)
+    mate = [(i, i ^ 1) for i in range(count)]
+    side = [(i, i ^ 2) for i in range(count)]
+
+    def move(values, where):
+        return lax.ppermute(values, "blk", where)
+
+    coef, here_rhs = pl.pallas_call(
         coef_kernel,
-        out_shape=jax.ShapeDtypeStruct((half * rank_k, unknowns), jnp.float32),
+        out_shape=[
+            jax.ShapeDtypeStruct((half * rank_k, unknowns), jnp.float32),
+            jax.ShapeDtypeStruct(rhs.shape, rhs.dtype),
+        ],
         in_specs=[whole(), whole()],
-        out_specs=whole(),
+        out_specs=[whole(), whole()],
         name="coef",
-    )(rhs, basis_in).astype(jnp.bfloat16)
+    )(rhs, basis_in)
+    coef = coef.astype(jnp.bfloat16)
 
     owner = near_owner[:, 0]
-    chunks = NEAR * SUBS
-    per = clusters // chunks
-    relative = (
-        ((owner ^ me) & 1) * (2 * depth)
-        + (((owner ^ me) >> 1) & 1) * depth
-        + ((owner >> 2) - (me >> 2) + depth) % depth
-    )
-    size = 2 * depth * per
-    position = (near_slot // per) % SUBS * (2 * size) + relative * per + near_slot % per
+    handler, steps, other = scatter_place(owner, me, count)
+    group = (steps < depth - 1).astype(jnp.int32)
+    sizes = (3, 2 * (depth - 2) + 1)
+    shard_at = jnp.where(
+        group == 0,
+        jnp.where(steps == depth, 0, 1 + other),
+        jnp.where(steps == 0, 2 * (depth - 2), 2 * (depth - 2 - steps) + other),
+    )
+    shard_at = shard_at + jnp.where(
+        handler == (me & 1), 0, jnp.where(group == 0, sizes[0], sizes[1])
+    )
+    position = shard_at * clusters + near_slot
     column = (owner * clusters + near_slot + near_offset) % (count * clusters)
-    column_row = ring_slot(column // clusters, me, count) * clusters + column % clusters
-    key = near_slot // (per * SUBS)
+    column_row = gather_slot(column // clusters, me, count) * clusters + column % clusters
     index = jnp.arange(stored, dtype=jnp.int32)
-    ahead = (key[None, :] < key[:, None]) | (
-        (key[None, :] == key[:, None]) & (index[None, :] < index[:, None])
-    )
-    rank = jnp.sum(ahead.astype(jnp.int32), axis=1)
+    before = (group[None, :] < group[:, None]) | (
+        (group[None, :] == group[:, None]) & (index[None, :] < index[:, None])
+    )
+    rank = jnp.sum(before.astype(jnp.int32), axis=1)
     here = rank[None, :] == index[:, None]
     block_at, position, column_row = [
         jnp.sum(jnp.where(here, values[None, :], 0), axis=1)
         for values in (index, position, column_row)
     ]
     starts = jnp.sum(
-        (key[None, :] < jnp.arange(NEAR + 1, dtype=jnp.int32)[:, None]).astype(jnp.int32), axis=1
-    )
-
-    low = far_cslot % half
+        (group[None, :] < jnp.arange(3, dtype=jnp.int32)[:, None]).astype(jnp.int32), axis=1
+    )
+
+    far_at = far_dev[:, 0]
+    far_at = (
+        ((far_at ^ me) & 1) * (2 * depth)
+        + (((far_at ^ me) >> 1) & 1) * depth
+        + ((me >> 2) - (far_at >> 2) + depth) % depth
+    )
     pick = (
-        (far_dev[:, 0] * half + low)[:, None] == jnp.arange(count * half, dtype=jnp.int32)[None, :]
+        (far_at * half + far_cslot % half)[:, None]
+        == jnp.arange(count * half, dtype=jnp.int32)[None, :]
     ).astype(jnp.bfloat16)
     keep = (
         (far_cslot // half)[:, None] == (jnp.arange(unknowns, dtype=jnp.int32) // directions)[None, :]
     ).astype(jnp.bfloat16)
     couple = jnp.transpose(far_coupling, (2, 1, 0))
 
-    coef, pick, keep, couple, starts, block_at, position, column_row, shards[-1] = (
-        lax.optimization_barrier(
-            (coef, pick, keep, couple, starts, block_at, position, column_row, shards[-1])
+    slots = {0: here_rhs}
+    flow = [move(rhs, ahead), move(rhs, cross)]
+    slots[1] = move(rhs, mate)
+    for t in range(1, depth + 1):
+        if t == 2:
+            flow[0], coef, starts, block_at, position, column_row = lax.optimization_barrier(
+                (flow[0], coef, starts, block_at, position, column_row)
+            )
+            coefs = [coef] + [
+                move(coef, [(i, (i + 4 * k) % count) for i in range(count)])
+                for k in range(1, depth)
+            ]
+        if t == 3:
+            flow[0], couple, pick, keep = lax.optimization_barrier((flow[0], couple, pick, keep))
+        if t == 4:
+            flow[0], coefs = lax.optimization_barrier((flow[0], jnp.concatenate(coefs, axis=0)))
+            coefs = [coefs, move(coefs, side)]
+        for x in range(2 if t < depth else 1):
+            slots[2 * t + x] = flow[x]
+            slots[2 * (chips - t) + 1 - x] = move(flow[x], mate)
+            if t + x < depth:
+                flow[x] = move(flow[x], ahead)
+
+    sums = []
+    for j, size in enumerate(sizes):
+        if j == 1:
+            starts, coefs = lax.optimization_barrier((starts, coefs))
+            coefs = coefs + [move(part, mate) for part in coefs]
+        sums.append(
+            pl.pallas_call(
+                functools.partial(near_kernel, dict(shards=count, at=j), 4),
+                out_shape=[
+                    jax.ShapeDtypeStruct((size * clusters, directions, unknowns), jnp.bfloat16),
+                    jax.ShapeDtypeStruct((size * clusters, directions, unknowns), jnp.float32),
+                ],
+                in_specs=[whole(pltpu.SMEM)] * 4
+                + [whole(pl.ANY)] * (count + 1),
+                out_specs=[whole()] * 2,
+                scratch_shapes=[
+                    pltpu.VMEM((count, clusters, directions, unknowns), jnp.bfloat16),
+                    pltpu.VMEM(near_blocks.shape, jnp.bfloat16),
+                    pltpu.VMEM((2 * size * clusters + 1, directions, unknowns), jnp.float32),
+                    pltpu.SemaphoreType.DMA((count + 1,)),
+                ],
+                compiler_params=pltpu.CompilerParams(vmem_limit_bytes=NEAR_VMEM),
+                cost_estimate=pl.CostEstimate(
+                    flops=2 * stored * directions * unknowns * unknowns * 8,
+                    bytes_accessed=12 << 20,
+                    transcendentals=0,
+                ),
+                name="near",
+            )(
+                starts,
+                block_at,
+                position,
+                column_row,
+                *[slots[k] for k in range(count)],
+                near_blocks,
+            )
         )
-    )
-    coef_all = lax.all_gather(coef, "blk", axis=0, tiled=True)
-
-    near_sums = []
-    for j in range(NEAR):
-        out = pl.pallas_call(
-            functools.partial(near_kernel, dict(shards=count, subs=SUBS, at=j), 4),
-            out_shape=[jax.ShapeDtypeStruct((size, directions, unknowns), jnp.bfloat16)] * SUBS
-            + [jax.ShapeDtypeStruct((size, directions, unknowns), jnp.float32)] * SUBS,
-            in_specs=[whole(pltpu.SMEM)] * 4 + [whole(pl.ANY)] * (count + 1),
-            out_specs=[whole()] * (2 * SUBS),
-            scratch_shapes=[
-                pltpu.VMEM((count, clusters, directions, unknowns), jnp.bfloat16),
-                pltpu.VMEM(near_blocks.shape, jnp.bfloat16),
-                pltpu.VMEM((2 * SUBS * size + 1, directions, unknowns), jnp.float32),
-                pltpu.SemaphoreType.DMA((count + 1,)),
-            ],
-            compiler_params=pltpu.CompilerParams(vmem_limit_bytes=NEAR_VMEM),
-            cost_estimate=pl.CostEstimate(
-                flops=2 * stored * directions * unknowns * unknowns * 8,
-                bytes_accessed=12 << 20,
-                transcendentals=0,
-            ),
-            name="near",
-        )(starts, block_at, position, column_row, *shards, near_blocks)
-        near_sums += list(zip(out[:SUBS], out[SUBS:]))
 
     far = pl.pallas_call(
         far_kernel,
         out_shape=jax.ShapeDtypeStruct((clusters, directions, unknowns), jnp.float32),
-        in_specs=[whole()] * 6,
+        in_specs=[whole()] * 9,
         out_specs=whole(),
         compiler_params=pltpu.CompilerParams(vmem_limit_bytes=FAR_VMEM),
         cost_estimate=pl.CostEstimate(
@@ -362,31 +411,41 @@
             transcendentals=0,
         ),
         name="far",
-    )(coef_all, couple, far_slot.reshape(1, pairs), pick, keep, basis_out)
-
-    core = [(i, i ^ 1) for i in range(count)]
-    side = [(i, i ^ 2) for i in range(count)]
-    quarter = depth * per
-    fields = []
-    for j, (send, own) in enumerate(near_sums):
-        total = own + lax.ppermute(send, "blk", core).astype(jnp.float32)
-        got = lax.ppermute(total[quarter:].astype(jnp.bfloat16), "blk", side)
-        total = total[:quarter] + got.astype(jnp.float32)
-        field = total[:per] + far[j * per : (j + 1) * per]
-        for k in range(1, depth):
-            field = field + lax.ppermute(
-                total[k * per : (k + 1) * per].astype(jnp.bfloat16),
-                "blk",
-                [(i, (i + 4 * k) % count) for i in range(count)],
-            ).astype(jnp.float32)
-        fields.append(field.astype(jnp.bfloat16))
-    return jnp.concatenate(fields, axis=0)
+    )(*coefs, couple, far_slot.reshape(1, pairs), pick, keep, basis_out)
+
+    own = [kept for _, kept in sums]
+    mates = [move(sent, mate) for sent, _ in sums]
+
+    def term(j, k):
+        at = slice(k * clusters, (k + 1) * clusters)
+        return own[j][at] + mates[j][at].astype(jnp.float32)
+
+    def add(flow, j, k):
+        step = (flow.astype(jnp.float32) + term(j, k)).astype(jnp.bfloat16)
+        step, mates[j] = lax.optimization_barrier((step, mates[j]))
+        return step
+
+    flow = lax.optimization_barrier(
+        [term(0, 0).astype(jnp.bfloat16), term(0, 2).astype(jnp.bfloat16)]
+    )
+    for t in range(depth - 1, -1, -1):
+        flow = [move(part, ahead) for part in flow]
+        if t == 0:
+            break
+        flow[0] = add(flow[0], 0, 1) if t == depth - 1 else add(flow[0], 1, 2 * (depth - 2 - t))
+        if t > 1:
+            flow[1] = add(flow[1], 1, 2 * (depth - 1 - t) + 1)
+        else:
+            last = move(flow[1], mate)
+            flow = flow[:1]
+    total = far + term(1, 2 * (depth - 2)) + last.astype(jnp.float32) + flow[0].astype(jnp.float32)
+    return total.astype(jnp.bfloat16)
 
 
 def on_device(*args):
     rhs = args[0]
     count = lax.axis_size("blk")
-    if count % 4 == 0 and count * rhs.size * 4 <= DENSE_BYTES:
+    if count % 4 == 0 and count >= 16 and count * rhs.size * 4 <= DENSE_BYTES:
         return stationary(*args)
     return routed(*args)
 

time: 108 us -> 79 us (0.73)
  blocking collectives: 21.6 us -> 0 us
  waiting for transfers between devices: 24.8 us -> 16.1 us
  starting transfers between devices: 33.3 us -> 36.5 us
  local copies, waits for them, and re-layouts: 4.3 us -> 1.91 us
  Pallas kernels: 15.9 us -> 17.3 us
    all_gather x1 -> x0, blocking collectives: 21.6 us -> none  [stationary(): coef_all = lax.all_gather(coef, 'blk', axis=0, tiled=True)]
    ppermute x25 -> x31, waiting for transfers between devices: 24.8 us -> 16.1 us  [move(): return lax.ppermute(values, 'blk', where)]
    ppermute x25 -> x31, starting transfers between devices: 33.3 us -> 36.5 us  [move(): return lax.ppermute(values, 'blk', where)]
    unnamed x9 -> x7, local copies, waits for them, and re-layouts: 4.09 us -> 1.91 us
    pallas_call x3, Pallas kernels: 13.5 us -> 14.9 us  [the longest x2 13 us: stationary(): pl.pallas_call(functools.partial(near_kernel, dict(shards=count, at=j), 4...]
    convert_element_type x3 -> x10, other arithmetic: 1.84 us -> 2.5 us  [the longest x1 0.89 us: stationary(): return total.astype(jnp.bfloat16)]
  transfers between devices with their start and end apart: 25 -> 31, of which waited for: 9 -> 14; matrix products, arithmetic and copies ran while one was open for 7% -> 8% of each run, Pallas kernels for 10% -> 22%
where the time goes in v3:
time: 79 us; the launch traced here: 78.4 us
  starting transfers between devices  36.5 us (46%)
  Pallas kernels  17.3 us (22%)
  waiting for transfers between devices  16.1 us (20%)
  other arithmetic  6.43 us (8%)
  local copies, waits for them, and re-layouts  1.91 us (2%)
    ppermute x31, starting transfers between devices, move(): return lax.ppermute(values, 'blk', where)  36.5 us
    ppermute x31, waiting for transfers between devices, move(): return lax.ppermute(values, 'blk', where)  16.1 us
    pallas_call x2, Pallas kernels, stationary(): pl.pallas_call(functools.partial(near_kernel, dict(shards=count, at=j), 4...  13 us
    pallas_call x1, Pallas kernels, stationary(): pl.pallas_call(far_kernel, out_shape=jax.ShapeDtypeStruct((clusters, dire...  2.42 us
    pallas_call x1, Pallas kernels, stationary(): pl.pallas_call(coef_kernel, out_shape=[jax.ShapeDtypeStruct((half * rank_...  1.92 us
    unnamed x7, local copies, waits for them, and re-layouts  1.91 us
  transfers between devices with their start and end apart: 31, of which 14 were waited for; matrix products, arithmetic and copies ran while one was open for 8% of the time, Pallas kernels for 22%

profile of v3, /device:TPU:0, one launch (start us, length us, event | category | flops | bytes accessed | tf_op | source)
XLA Modules:
  0.0 78.4 jit_solution(16670904817564262182)
XLA Ops:
  0.0 3.0 %collective-permute-start = (bf16[16,64,128]{2,1,0:T(8,128)(2,1)}, bf16[16,64,128]{2,1,0:T(8,128)(2,1)S(1)}, u32[]{:S(2)}, u32[]{:S(2)}) collective-permute-start(bf16[16,64,128]{2,1,0:T(8,128)(2,1)} %rhs_ref.1), channel_id=1, source_target_pairs={{0,4},{1,3},{4,8},{5,1},{8,12},{9,5},{12,14},{13,9},{14,10},{15,13... | collective-permute-start | bytes 786440 | tf_op jit(solution)/shard_map/ppermute | solution.py:283
  6.8 2.2 %collective-permute-done.rest_2_ = bf16[16,64,128]{2,1,0:T(8,128)(2,1)S(1)} collective-permute-done((bf16[16,64,128]{2,1,0:T(8,128)(2,1)}, bf16[16,64,128]{2,1,0:T(8,128)(2,1)S(1)}, u32[]{:S(2)}, u32[]{:S(2)}) %collective-permute-start) | collective-permute-done | bytes 262176 | tf_op jit(solution)/shard_map/ppermute | solution.py:283
  9.0 2.4 %collective-permute-start.1 = (bf16[16,64,128]{2,1,0:T(8,128)(2,1)S(1)}, bf16[16,64,128]{2,1,0:T(8,128)(2,1)S(1)}, u32[]{:S(2)}, u32[]{:S(2)}) collective-permute-start(bf16[16,64,128]{2,1,0:T(8,128)(2,1)S(1)} %collective-permute-done.rest_2_), channel_id=1, source_target_pairs={{0,4},{1,3},{4,8},{5,1},{8,12},{9,5},{12,14},{13,9},{14,10},{15,13... | collective-permute-start | bytes 786440 | tf_op jit(solution)/shard_map/ppermute | solution.py:283
  11.5 1.9 %coef.1 = (f32[128,128]{1,0:T(8,128)}, bf16[16,64,128]{2,1,0:T(8,128)(2,1)}) custom-call(bf16[16,64,128]{2,1,0:T(8,128)(2,1)} %rhs_ref.1, bf16[16,16,128]{2,1,0:T(8,128)(2,1)} %basis_ref.1), custom_call_target="tpu_custom_call" | custom-call | tf_op jit(solution)/shard_map/coef/pallas_call | solution.py:285
  13.4 0.8 %convert_element_type.102 = bf16[128,128]{1,0:T(8,128)(2,1)S(1)} convert(f32[128,128]{1,0:T(8,128)} %get-tuple-element.37) | non-fusion elementwise | flops 16384 | bytes 98304 | tf_op jit(solution)/shard_map/convert_element_type | solution.py:295
  15.0 1.6 %collective-permute-start.12 = (bf16[16,64,128]{2,1,0:T(8,128)(2,1)S(1)}, bf16[16,64,128]{2,1,0:T(8,128)(2,1)S(1)}, u32[]{:S(2)}, u32[]{:S(2)}) collective-permute-start(bf16[16,64,128]{2,1,0:T(8,128)(2,1)S(1)} %collective-permute-done.11.rest_3_), channel_id=1, source_target_pairs={{0,4},{1,3},{4,8},{5,1},{8,12},{9,5},{12,14},{13,9},{14,10},{15,13... | collective-permute-start | bytes 786440 | tf_op jit(solution)/shard_map/ppermute | solution.py:283
  16.7 1.6 %collective-permute-start.2 = (bf16[16,64,128]{2,1,0:T(8,128)(2,1)S(1)}, bf16[16,64,128]{2,1,0:T(8,128)(2,1)S(1)}, u32[]{:S(2)}, u32[]{:S(2)}) collective-permute-start(bf16[16,64,128]{2,1,0:T(8,128)(2,1)S(1)} %collective-permute-done.1.rest_4_), channel_id=1, source_target_pairs={{0,4},{1,3},{4,8},{5,1},{8,12},{9,5},{12,14},{13,9},{14,10},{15,13... | collective-permute-start | bytes 786440 | tf_op jit(solution)/shard_map/ppermute | solution.py:283
  18.3 3.9 %collective-permute-start.6 = (bf16[128,128]{1,0:T(8,128)(2,1)S(1)}, bf16[128,128]{1,0:T(8,128)(2,1)S(1)}, u32[]{:S(2)}, u32[]{:S(2)}) collective-permute-start(bf16[128,128]{1,0:T(8,128)(2,1)S(1)} %convert_element_type.102), channel_id=1, source_target_pairs={{0,12},{1,13},{2,14},{3,15},{4,0},{5,1},{6,2},{7,3},{8,4},{9,5},{1... | collective-permute-start | bytes 98312 | tf_op jit(solution)/shard_map/ppermute | solution.py:283
  22.9 0.9 %copy.15 = bf16[256,16,16]{0,1,2:T(8,128)(2,1)S(1)} copy(bf16[256,16,16]{0,2,1:T(8,128)(2,1)} %param.16) | data formatting | bytes 262144 | tf_op args[5]
  24.4 2.5 %collective-permute-start.3 = (bf16[16,64,128]{2,1,0:T(8,128)(2,1)S(1)}, bf16[16,64,128]{2,1,0:T(8,128)(2,1)S(1)}, u32[]{:S(2)}, u32[]{:S(2)}) collective-permute-start(bf16[16,64,128]{2,1,0:T(8,128)(2,1)S(1)} %collective-permute-done.2.rest_6_), channel_id=1, source_target_pairs={{0,4},{1,3},{4,8},{5,1},{8,12},{9,5},{12,14},{13,9},{14,10},{15,13... | collective-permute-start | bytes 786440 | tf_op jit(solution)/shard_map/ppermute | solution.py:283
  27.4 2.3 %collective-permute-start.13 = (bf16[16,64,128]{2,1,0:T(8,128)(2,1)S(1)}, bf16[16,64,128]{2,1,0:T(8,128)(2,1)S(1)}, u32[]{:S(2)}, u32[]{:S(2)}) collective-permute-start(bf16[16,64,128]{2,1,0:T(8,128)(2,1)S(1)} %collective-permute-done.12.rest_5_), channel_id=1, source_target_pairs={{0,4},{1,3},{4,8},{5,1},{8,12},{9,5},{12,14},{13,9},{14,10},{15,13... | collective-permute-start | bytes 786440 | tf_op jit(solution)/shard_map/ppermute | solution.py:283
  29.7 1.0 %collective-permute-done.3.rest_8_ = bf16[16,64,128]{2,1,0:T(8,128)(2,1)S(1)} collective-permute-done((bf16[16,64,128]{2,1,0:T(8,128)(2,1)S(1)}, bf16[16,64,128]{2,1,0:T(8,128)(2,1)S(1)}, u32[]{:S(2)}, u32[]{:S(2)}) %collective-permute-start.3) | collective-permute-done | bytes 262176 | tf_op jit(solution)/shard_map/ppermute | solution.py:283
  31.3 2.5 %collective-permute-done.13.rest_7_ = bf16[16,64,128]{2,1,0:T(8,128)(2,1)S(1)} collective-permute-done((bf16[16,64,128]{2,1,0:T(8,128)(2,1)S(1)}, bf16[16,64,128]{2,1,0:T(8,128)(2,1)S(1)}, u32[]{:S(2)}, u32[]{:S(2)}) %collective-permute-start.13) | collective-permute-done | bytes 262176 | tf_op jit(solution)/shard_map/ppermute | solution.py:283
  34.3 1.8 %collective-permute-start.7 = (bf16[512,128]{1,0:T(8,128)(2,1)S(1)}, bf16[512,128]{1,0:T(8,128)(2,1)S(1)}, u32[]{:S(2)}, u32[]{:S(2)}) collective-permute-start(bf16[512,128]{1,0:T(8,128)(2,1)S(1)} %pad_maximum_fusion.refs_0_), channel_id=1, source_target_pairs={{0,2},{1,3},{2,0},{3,1},{4,6},{5,7},{6,4},{7,5},{8,10},{9,11},{10,... | collective-permute-start | bytes 393224 | tf_op jit(solution)/shard_map/ppermute | solution.py:283
  36.1 0.9 %copy-done = bf16[16,64,128]{2,1,0:T(8,128)(2,1)S(1)} copy-done((bf16[16,64,128]{2,1,0:T(8,128)(2,1)S(1)}, bf16[16,64,128]{2,1,0:T(8,128)(2,1)}, u32[]{:S(2)}) %copy-start) | copy-done | bytes 262168
  37.1 5.3 %near.3 = (bf16[48,64,128]{2,1,0:T(8,128)(2,1)S(1)}, f32[48,64,128]{2,1,0:T(8,128)S(1)}) custom-call(s32[3]{0:T(128)S(1)} %convert_reduce_fusion.1.starts_ref, s32[128]{0:T(128)S(1)} %get-tuple-element.49.block_ref, s32[128]{0:T(128)S(1)} %get-tuple-element.50.pos_ref, s32[128]{0:T(128)S(1)} %get-tuple-element.51.row_ref, bf16[16,64,128]{2,1,0:T(8,128)(2,1)S(1)} %copy-done, ...), custom_call_target="tpu_custom_call" | custom-call | flops 2147483648 | bytes 12582912 | tf_op jit(solution)/shard_map/near/pallas_call | solution.py:370
  42.5 7.7 %near.2 = (bf16[80,64,128]{2,1,0:T(8,128)(2,1)S(1)}, f32[80,64,128]{2,1,0:T(8,128)S(1)}) custom-call(s32[3]{0:T(128)S(1)} %convert_reduce_fusion.1.starts_ref, s32[128]{0:T(128)S(1)} %get-tuple-element.49.block_ref, s32[128]{0:T(128)S(1)} %get-tuple-element.50.pos_ref, s32[128]{0:T(128)S(1)} %get-tuple-element.51.row_ref, bf16[16,64,128]{2,1,0:T(8,128)(2,1)S(1)} %copy-done, ...), custom_call_target="tpu_custom_call" | custom-call | flops 2147483648 | bytes 12582912 | tf_op jit(solution)/shard_map/near/pallas_call | solution.py:370
  50.9 1.9 %collective-permute-start.22 = (bf16[16,64,128]{2,1,0:T(8,128)(2,1)S(1)}, bf16[16,64,128]{2,1,0:T(8,128)(2,1)S(1)}, u32[]{:S(2)}, u32[]{:S(2)}) collective-permute-start(bf16[16,64,128]{2,1,0:T(8,128)(2,1)S(1)} %get-tuple-element.57), channel_id=1, source_target_pairs={{0,4},{1,3},{4,8},{5,1},{8,12},{9,5},{12,14},{13,9},{14,10},{15,13... | collective-permute-start | bytes 786440 | tf_op jit(solution)/shard_map/ppermute | solution.py:283
  52.7 2.2 %collective-permute-start.24 = (bf16[16,64,128]{2,1,0:T(8,128)(2,1)S(1)}, bf16[16,64,128]{2,1,0:T(8,128)(2,1)S(1)}, u32[]{:S(2)}, u32[]{:S(2)}) collective-permute-start(bf16[16,64,128]{2,1,0:T(8,128)(2,1)S(1)} %get-tuple-element.59), channel_id=1, source_target_pairs={{0,4},{1,3},{4,8},{5,1},{8,12},{9,5},{12,14},{13,9},{14,10},{15,13... | collective-permute-start | bytes 786440 | tf_op jit(solution)/shard_map/ppermute | solution.py:283
  55.0 2.3 %collective-permute-done.22 = bf16[16,64,128]{2,1,0:T(8,128)(2,1)S(1)} collective-permute-done((bf16[16,64,128]{2,1,0:T(8,128)(2,1)S(1)}, bf16[16,64,128]{2,1,0:T(8,128)(2,1)S(1)}, u32[]{:S(2)}, u32[]{:S(2)}) %collective-permute-start.22) | collective-permute-done | bytes 262176 | tf_op jit(solution)/shard_map/ppermute | solution.py:283
  57.4 1.9 %collective-permute-start.23 = (bf16[16,64,128]{2,1,0:T(8,128)(2,1)S(1)}, bf16[16,64,128]{2,1,0:T(8,128)(2,1)S(1)}, u32[]{:S(2)}, u32[]{:S(2)}) collective-permute-start(bf16[16,64,128]{2,1,0:T(8,128)(2,1)S(1)} %add_convert_fusion.5), channel_id=1, source_target_pairs={{0,4},{1,3},{4,8},{5,1},{8,12},{9,5},{12,14},{13,9},{14,10},{15,13... | collective-permute-start | bytes 786440 | tf_op jit(solution)/shard_map/ppermute | solution.py:283
  59.3 0.8 %collective-permute-done.24 = bf16[16,64,128]{2,1,0:T(8,128)(2,1)S(1)} collective-permute-done((bf16[16,64,128]{2,1,0:T(8,128)(2,1)S(1)}, bf16[16,64,128]{2,1,0:T(8,128)(2,1)S(1)}, u32[]{:S(2)}, u32[]{:S(2)}) %collective-permute-start.24) | collective-permute-done | bytes 262176 | tf_op jit(solution)/shard_map/ppermute | solution.py:283
  60.2 1.9 %collective-permute-start.27 = (bf16[16,64,128]{2,1,0:T(8,128)(2,1)S(1)}, bf16[16,64,128]{2,1,0:T(8,128)(2,1)S(1)}, u32[]{:S(2)}, u32[]{:S(2)}) collective-permute-start(bf16[16,64,128]{2,1,0:T(8,128)(2,1)S(1)} %add_convert_fusion.4), channel_id=1, source_target_pairs={{0,4},{1,3},{4,8},{5,1},{8,12},{9,5},{12,14},{13,9},{14,10},{15,13... | collective-permute-start | bytes 786440 | tf_op jit(solution)/shard_map/ppermute | solution.py:283
  62.1 1.7 %collective-permute-done.23 = bf16[16,64,128]{2,1,0:T(8,128)(2,1)S(1)} collective-permute-done((bf16[16,64,128]{2,1,0:T(8,128)(2,1)S(1)}, bf16[16,64,128]{2,1,0:T(8,128)(2,1)S(1)}, u32[]{:S(2)}, u32[]{:S(2)}) %collective-permute-start.23) | collective-permute-done | bytes 262176 | tf_op jit(solution)/shard_map/ppermute | solution.py:283
  64.0 1.9 %collective-permute-start.26 = (bf16[16,64,128]{2,1,0:T(8,128)(2,1)S(1)}, bf16[16,64,128]{2,1,0:T(8,128)(2,1)S(1)}, u32[]{:S(2)}, u32[]{:S(2)}) collective-permute-start(bf16[16,64,128]{2,1,0:T(8,128)(2,1)S(1)} %add_convert_fusion.3), channel_id=1, source_target_pairs={{0,4},{1,3},{4,8},{5,1},{8,12},{9,5},{12,14},{13,9},{14,10},{15,13... | collective-permute-start | bytes 786440 | tf_op jit(solution)/shard_map/ppermute | solution.py:283
  66.7 1.9 %collective-permute-start.28 = (bf16[16,64,128]{2,1,0:T(8,128)(2,1)S(1)}, bf16[16,64,128]{2,1,0:T(8,128)(2,1)S(1)}, u32[]{:S(2)}, u32[]{:S(2)}) collective-permute-start(bf16[16,64,128]{2,1,0:T(8,128)(2,1)S(1)} %add_convert_fusion.2), channel_id=1, source_target_pairs={{0,4},{1,3},{4,8},{5,1},{8,12},{9,5},{12,14},{13,9},{14,10},{15,13... | collective-permute-start | bytes 786440 | tf_op jit(solution)/shard_map/ppermute | solution.py:283
  68.6 1.8 %collective-permute-done.26 = bf16[16,64,128]{2,1,0:T(8,128)(2,1)S(1)} collective-permute-done((bf16[16,64,128]{2,1,0:T(8,128)(2,1)S(1)}, bf16[16,64,128]{2,1,0:T(8,128)(2,1)S(1)}, u32[]{:S(2)}, u32[]{:S(2)}) %collective-permute-start.26) | collective-permute-done | bytes 262176 | tf_op jit(solution)/shard_map/ppermute | solution.py:283
  70.5 1.9 %collective-permute-start.30 = (bf16[16,64,128]{2,1,0:T(8,128)(2,1)S(1)}, bf16[16,64,128]{2,1,0:T(8,128)(2,1)S(1)}, u32[]{:S(2)}, u32[]{:S(2)}) collective-permute-start(bf16[16,64,128]{2,1,0:T(8,128)(2,1)S(1)} %add_convert_fusion.1), channel_id=1, source_target_pairs={{0,4},{1,3},{4,8},{5,1},{8,12},{9,5},{12,14},{13,9},{14,10},{15,13... | collective-permute-start | bytes 786440 | tf_op jit(solution)/shard_map/ppermute | solution.py:283
  72.4 0.8 %collective-permute-done.28 = bf16[16,64,128]{2,1,0:T(8,128)(2,1)S(1)} collective-permute-done((bf16[16,64,128]{2,1,0:T(8,128)(2,1)S(1)}, bf16[16,64,128]{2,1,0:T(8,128)(2,1)S(1)}, u32[]{:S(2)}, u32[]{:S(2)}) %collective-permute-start.28) | collective-permute-done | bytes 262176 | tf_op jit(solution)/shard_map/ppermute | solution.py:283
  73.7 1.2 %collective-permute-done.8.refs_2_ = bf16[512,128]{1,0:T(8,128)(2,1)S(1)} collective-permute-done((bf16[512,128]{1,0:T(8,128)(2,1)S(1)}, bf16[512,128]{1,0:T(8,128)(2,1)S(1)}, u32[]{:S(2)}, u32[]{:S(2)}) %collective-permute-start.8) | collective-permute-done | bytes 131104 | tf_op jit(solution)/shard_map/ppermute | solution.py:283
  75.1 2.4 %far.1 = f32[16,64,128]{2,1,0:T(8,128)S(1)} custom-call(bf16[512,128]{1,0:T(8,128)(2,1)S(1)} %pad_maximum_fusion.refs_0_, bf16[512,128]{1,0:T(8,128)(2,1)S(1)} %collective-permute-done.7.refs_1_, bf16[512,128]{1,0:T(8,128)(2,1)S(1)} %collective-permute-done.8.refs_2_, bf16[512,128]{1,0:T(8,128)(2,1)S(1)} %collective-permute-done.9.refs_3_, ...), custom_call_target="tpu_custom_call" | custom-call | flops 536870912 | bytes 8388608 | tf_op jit(solution)/shard_map/far/pallas_call | solution.py:402
  77.5 0.9 %add_convert_fusion = bf16[16,64,128]{2,1,0:T(8,128)(2,1)} fusion(bf16[16,64,128]{2,1,0:T(8,128)(2,1)S(1)} %collective-permute-done.30, bf16[16,64,128]{2,1,0:T(8,128)(2,1)S(1)} %collective-permute-done.29, f32[16,64,128]{2,1,0:T(8,128)S(1)} %far.1, f32[80,64,128]{2,1,0:T(8,128)S(1)} %get-tuple-element.54, bf16[80,64,128]{2,1,0:T(8,128)(2,1)S(1)} %collective-permute-done.25), kind=kLoop, calls=%fused_computation | loop fusion | flops 1048576 | bytes 2097152 | tf_op jit(solution)/shard_map/convert_element_type | solution.py:442
  (61 shorter events, 10.4 us)
Async XLA Ops:
  0.0 9.0 %collective-permute-start = (bf16[16,64,128]{2,1,0:T(8,128)(2,1)}, bf16[16,64,128]{2,1,0:T(8,128)(2,1)S(1)}, u32[]{:S(2)}, u32[]{:S(2)}) collective-permute-start(bf16[16,64,128]{2,1,0:T(8,128)(2,1)} %rhs_ref.1), channel_id=1, source_target_pairs={{0,4},{1,3},{4,8},{5,1},{8,12},{9,5},{12,14},{13,9},{14,10},{15,13... | collective-permute-start | bytes 786440 | tf_op jit(solution)/shard_map/ppermute | solution.py:283
  3.0 12.0 %collective-permute-start.11 = (bf16[16,64,128]{2,1,0:T(8,128)(2,1)}, bf16[16,64,128]{2,1,0:T(8,128)(2,1)S(1)}, u32[]{:S(2)}, u32[]{:S(2)}) collective-permute-start(bf16[16,64,128]{2,1,0:T(8,128)(2,1)} %rhs_ref.1), channel_id=1, source_target_pairs={{0,3},{1,4},{4,1},{5,8},{8,5},{9,12},{12,9},{13,14},{14,13},{15,10... | collective-permute-start | bytes 786440 | tf_op jit(solution)/shard_map/ppermute | solution.py:283
  9.0 7.6 %collective-permute-start.1 = (bf16[16,64,128]{2,1,0:T(8,128)(2,1)S(1)}, bf16[16,64,128]{2,1,0:T(8,128)(2,1)S(1)}, u32[]{:S(2)}, u32[]{:S(2)}) collective-permute-start(bf16[16,64,128]{2,1,0:T(8,128)(2,1)S(1)} %collective-permute-done.rest_2_), channel_id=1, source_target_pairs={{0,4},{1,3},{4,8},{5,1},{8,12},{9,5},{12,14},{13,9},{14,10},{15,13... | collective-permute-start | bytes 786440 | tf_op jit(solution)/shard_map/ppermute | solution.py:283
  15.0 11.9 %collective-permute-start.12 = (bf16[16,64,128]{2,1,0:T(8,128)(2,1)S(1)}, bf16[16,64,128]{2,1,0:T(8,128)(2,1)S(1)}, u32[]{:S(2)}, u32[]{:S(2)}) collective-permute-start(bf16[16,64,128]{2,1,0:T(8,128)(2,1)S(1)} %collective-permute-done.11.rest_3_), channel_id=1, source_target_pairs={{0,4},{1,3},{4,8},{5,1},{8,12},{9,5},{12,14},{13,9},{14,10},{15,13... | collective-permute-start | bytes 786440 | tf_op jit(solution)/shard_map/ppermute | solution.py:283
  16.7 7.7 %collective-permute-start.2 = (bf16[16,64,128]{2,1,0:T(8,128)(2,1)S(1)}, bf16[16,64,128]{2,1,0:T(8,128)(2,1)S(1)}, u32[]{:S(2)}, u32[]{:S(2)}) collective-permute-start(bf16[16,64,128]{2,1,0:T(8,128)(2,1)S(1)} %collective-permute-done.1.rest_4_), channel_id=1, source_target_pairs={{0,4},{1,3},{4,8},{5,1},{8,12},{9,5},{12,14},{13,9},{14,10},{15,13... | collective-permute-start | bytes 786440 | tf_op jit(solution)/shard_map/ppermute | solution.py:283
  18.3 8.6 %collective-permute-start.6 = (bf16[128,128]{1,0:T(8,128)(2,1)S(1)}, bf16[128,128]{1,0:T(8,128)(2,1)S(1)}, u32[]{:S(2)}, u32[]{:S(2)}) collective-permute-start(bf16[128,128]{1,0:T(8,128)(2,1)S(1)} %convert_element_type.102), channel_id=1, source_target_pairs={{0,12},{1,13},{2,14},{3,15},{4,0},{5,1},{6,2},{7,3},{8,4},{9,5},{1... | collective-permute-start | bytes 98312 | tf_op jit(solution)/shard_map/ppermute | solution.py:283
  22.2 5.2 %collective-permute-start.5 = (bf16[128,128]{1,0:T(8,128)(2,1)S(1)}, bf16[128,128]{1,0:T(8,128)(2,1)S(1)}, u32[]{:S(2)}, u32[]{:S(2)}) collective-permute-start(bf16[128,128]{1,0:T(8,128)(2,1)S(1)} %convert_element_type.102), channel_id=1, source_target_pairs={{0,8},{1,9},{2,10},{3,11},{4,12},{5,13},{6,14},{7,15},{8,0},{9,1},... | collective-permute-start | bytes 98312 | tf_op jit(solution)/shard_map/ppermute | solution.py:283
  22.2 7.5 %collective-permute-start.4 = (bf16[128,128]{1,0:T(8,128)(2,1)S(1)}, bf16[128,128]{1,0:T(8,128)(2,1)S(1)}, u32[]{:S(2)}, u32[]{:S(2)}) collective-permute-start(bf16[128,128]{1,0:T(8,128)(2,1)S(1)} %convert_element_type.102), channel_id=1, source_target_pairs={{0,4},{1,5},{2,6},{3,7},{4,8},{5,9},{6,10},{7,11},{8,12},{9,13},{1... | collective-permute-start | bytes 98312 | tf_op jit(solution)/shard_map/ppermute | solution.py:283
  24.4 6.4 %collective-permute-start.3 = (bf16[16,64,128]{2,1,0:T(8,128)(2,1)S(1)}, bf16[16,64,128]{2,1,0:T(8,128)(2,1)S(1)}, u32[]{:S(2)}, u32[]{:S(2)}) collective-permute-start(bf16[16,64,128]{2,1,0:T(8,128)(2,1)S(1)} %collective-permute-done.2.rest_6_), channel_id=1, source_target_pairs={{0,4},{1,3},{4,8},{5,1},{8,12},{9,5},{12,14},{13,9},{14,10},{15,13... | collective-permute-start | bytes 786440 | tf_op jit(solution)/shard_map/ppermute | solution.py:283
  26.9 3.9 %collective-permute-start.10 = (bf16[16,64,128]{2,1,0:T(8,128)(2,1)}, bf16[16,64,128]{2,1,0:T(8,128)(2,1)S(1)}, u32[]{:S(2)}, u32[]{:S(2)}) collective-permute-start(bf16[16,64,128]{2,1,0:T(8,128)(2,1)} %rhs_ref.1), channel_id=1, source_target_pairs={{0,1},{1,0},{2,3},{3,2},{4,5},{5,4},{6,7},{7,6},{8,9},{9,8},{10,11... | collective-permute-start | bytes 786440 | tf_op jit(solution)/shard_map/ppermute | solution.py:283
  26.9 4.4 %collective-permute-start.20 = (bf16[16,64,128]{2,1,0:T(8,128)(2,1)S(1)}, bf16[16,64,128]{2,1,0:T(8,128)(2,1)S(1)}, u32[]{:S(2)}, u32[]{:S(2)}) collective-permute-start(bf16[16,64,128]{2,1,0:T(8,128)(2,1)S(1)} %collective-permute-done.rest_2_), channel_id=1, source_target_pairs={{0,1},{1,0},{2,3},{3,2},{4,5},{5,4},{6,7},{7,6},{8,9},{9,8},{10,11... | collective-permute-start | bytes 786440 | tf_op jit(solution)/shard_map/ppermute | solution.py:283
  27.4 6.4 %collective-permute-start.13 = (bf16[16,64,128]{2,1,0:T(8,128)(2,1)S(1)}, bf16[16,64,128]{2,1,0:T(8,128)(2,1)S(1)}, u32[]{:S(2)}, u32[]{:S(2)}) collective-permute-start(bf16[16,64,128]{2,1,0:T(8,128)(2,1)S(1)} %collective-permute-done.12.rest_5_), channel_id=1, source_target_pairs={{0,4},{1,3},{4,8},{5,1},{8,12},{9,5},{12,14},{13,9},{14,10},{15,13... | collective-permute-start | bytes 786440 | tf_op jit(solution)/shard_map/ppermute | solution.py:283
  29.7 4.1 %collective-permute-start.19 = (bf16[16,64,128]{2,1,0:T(8,128)(2,1)S(1)}, bf16[16,64,128]{2,1,0:T(8,128)(2,1)S(1)}, u32[]{:S(2)}, u32[]{:S(2)}) collective-permute-start(bf16[16,64,128]{2,1,0:T(8,128)(2,1)S(1)} %collective-permute-done.11.rest_3_), channel_id=1, source_target_pairs={{0,1},{1,0},{2,3},{3,2},{4,5},{5,4},{6,7},{7,6},{8,9},{9,8},{10,11... | collective-permute-start | bytes 786440 | tf_op jit(solution)/shard_map/ppermute | solution.py:283
  30.7 5.3 %collective-permute-start.18 = (bf16[16,64,128]{2,1,0:T(8,128)(2,1)S(1)}, bf16[16,64,128]{2,1,0:T(8,128)(2,1)S(1)}, u32[]{:S(2)}, u32[]{:S(2)}) collective-permute-start(bf16[16,64,128]{2,1,0:T(8,128)(2,1)S(1)} %collective-permute-done.1.rest_4_), channel_id=1, source_target_pairs={{0,1},{1,0},{2,3},{3,2},{4,5},{5,4},{6,7},{7,6},{8,9},{9,8},{10,11... | collective-permute-start | bytes 786440 | tf_op jit(solution)/shard_map/ppermute | solution.py:283
  30.8 3.6 %collective-permute-start.17 = (bf16[16,64,128]{2,1,0:T(8,128)(2,1)S(1)}, bf16[16,64,128]{2,1,0:T(8,128)(2,1)S(1)}, u32[]{:S(2)}, u32[]{:S(2)}) collective-permute-start(bf16[16,64,128]{2,1,0:T(8,128)(2,1)S(1)} %collective-permute-done.12.rest_5_), channel_id=1, source_target_pairs={{0,1},{1,0},{2,3},{3,2},{4,5},{5,4},{6,7},{7,6},{8,9},{9,8},{10,11... | collective-permute-start | bytes 786440 | tf_op jit(solution)/shard_map/ppermute | solution.py:283
  31.3 4.8 %collective-permute-start.16 = (bf16[16,64,128]{2,1,0:T(8,128)(2,1)S(1)}, bf16[16,64,128]{2,1,0:T(8,128)(2,1)S(1)}, u32[]{:S(2)}, u32[]{:S(2)}) collective-permute-start(bf16[16,64,128]{2,1,0:T(8,128)(2,1)S(1)} %collective-permute-done.2.rest_6_), channel_id=1, source_target_pairs={{0,1},{1,0},{2,3},{3,2},{4,5},{5,4},{6,7},{7,6},{8,9},{9,8},{10,11... | collective-permute-start | bytes 786440 | tf_op jit(solution)/shard_map/ppermute | solution.py:283
  33.8 2.3 %collective-permute-start.15 = (bf16[16,64,128]{2,1,0:T(8,128)(2,1)S(1)}, bf16[16,64,128]{2,1,0:T(8,128)(2,1)S(1)}, u32[]{:S(2)}, u32[]{:S(2)}) collective-permute-start(bf16[16,64,128]{2,1,0:T(8,128)(2,1)S(1)} %collective-permute-done.13.rest_7_), channel_id=1, source_target_pairs={{0,1},{1,0},{2,3},{3,2},{4,5},{5,4},{6,7},{7,6},{8,9},{9,8},{10,11... | collective-permute-start | bytes 786440 | tf_op jit(solution)/shard_map/ppermute | solution.py:283
  33.8 2.3 %collective-permute-start.14 = (bf16[16,64,128]{2,1,0:T(8,128)(2,1)S(1)}, bf16[16,64,128]{2,1,0:T(8,128)(2,1)S(1)}, u32[]{:S(2)}, u32[]{:S(2)}) collective-permute-start(bf16[16,64,128]{2,1,0:T(8,128)(2,1)S(1)} %collective-permute-done.3.rest_8_), channel_id=1, source_target_pairs={{0,1},{1,0},{2,3},{3,2},{4,5},{5,4},{6,7},{7,6},{8,9},{9,8},{10,11... | collective-permute-start | bytes 786440 | tf_op jit(solution)/shard_map/ppermute | solution.py:283
  34.3 8.1 %collective-permute-start.7 = (bf16[512,128]{1,0:T(8,128)(2,1)S(1)}, bf16[512,128]{1,0:T(8,128)(2,1)S(1)}, u32[]{:S(2)}, u32[]{:S(2)}) collective-permute-start(bf16[512,128]{1,0:T(8,128)(2,1)S(1)} %pad_maximum_fusion.refs_0_), channel_id=1, source_target_pairs={{0,2},{1,3},{2,0},{3,1},{4,6},{5,7},{6,4},{7,5},{8,10},{9,11},{10,... | collective-permute-start | bytes 393224 | tf_op jit(solution)/shard_map/ppermute | solution.py:283
  42.4 8.3 %collective-permute-start.21 = (bf16[48,64,128]{2,1,0:T(8,128)(2,1)S(1)}, bf16[48,64,128]{2,1,0:T(8,128)(2,1)S(1)}, u32[]{:S(2)}, u32[]{:S(2)}) collective-permute-start(bf16[48,64,128]{2,1,0:T(8,128)(2,1)S(1)} %get-tuple-element.56), channel_id=1, source_target_pairs={{0,1},{1,0},{2,3},{3,2},{4,5},{5,4},{6,7},{7,6},{8,9},{9,8},{10,11... | collective-permute-start | bytes 2359304 | tf_op jit(solution)/shard_map/ppermute | solution.py:283
  50.2 9.9 %collective-permute-start.25 = (bf16[80,64,128]{2,1,0:T(8,128)(2,1)S(1)}, bf16[80,64,128]{2,1,0:T(8,128)(2,1)S(1)}, u32[]{:S(2)}, u32[]{:S(2)}) collective-permute-start(bf16[80,64,128]{2,1,0:T(8,128)(2,1)S(1)} %get-tuple-element.60), channel_id=1, source_target_pairs={{0,1},{1,0},{2,3},{3,2},{4,5},{5,4},{6,7},{7,6},{8,9},{9,8},{10,11... | collective-permute-start | bytes 3932168 | tf_op jit(solution)/shard_map/ppermute | solution.py:283
  50.9 6.4 %collective-permute-start.22 = (bf16[16,64,128]{2,1,0:T(8,128)(2,1)S(1)}, bf16[16,64,128]{2,1,0:T(8,128)(2,1)S(1)}, u32[]{:S(2)}, u32[]{:S(2)}) collective-permute-start(bf16[16,64,128]{2,1,0:T(8,128)(2,1)S(1)} %get-tuple-element.57), channel_id=1, source_target_pairs={{0,4},{1,3},{4,8},{5,1},{8,12},{9,5},{12,14},{13,9},{14,10},{15,13... | collective-permute-start | bytes 786440 | tf_op jit(solution)/shard_map/ppermute | solution.py:283
  52.7 7.4 %collective-permute-start.24 = (bf16[16,64,128]{2,1,0:T(8,128)(2,1)S(1)}, bf16[16,64,128]{2,1,0:T(8,128)(2,1)S(1)}, u32[]{:S(2)}, u32[]{:S(2)}) collective-permute-start(bf16[16,64,128]{2,1,0:T(8,128)(2,1)S(1)} %get-tuple-element.59), channel_id=1, source_target_pairs={{0,4},{1,3},{4,8},{5,1},{8,12},{9,5},{12,14},{13,9},{14,10},{15,13... | collective-permute-start | bytes 786440 | tf_op jit(solution)/shard_map/ppermute | solution.py:283
  57.4 6.4 %collective-permute-start.23 = (bf16[16,64,128]{2,1,0:T(8,128)(2,1)S(1)}, bf16[16,64,128]{2,1,0:T(8,128)(2,1)S(1)}, u32[]{:S(2)}, u32[]{:S(2)}) collective-permute-start(bf16[16,64,128]{2,1,0:T(8,128)(2,1)S(1)} %add_convert_fusion.5), channel_id=1, source_target_pairs={{0,4},{1,3},{4,8},{5,1},{8,12},{9,5},{12,14},{13,9},{14,10},{15,13... | collective-permute-start | bytes 786440 | tf_op jit(solution)/shard_map/ppermute | solution.py:283
  60.2 6.4 %collective-permute-start.27 = (bf16[16,64,128]{2,1,0:T(8,128)(2,1)S(1)}, bf16[16,64,128]{2,1,0:T(8,128)(2,1)S(1)}, u32[]{:S(2)}, u32[]{:S(2)}) collective-permute-start(bf16[16,64,128]{2,1,0:T(8,128)(2,1)S(1)} %add_convert_fusion.4), channel_id=1, source_target_pairs={{0,4},{1,3},{4,8},{5,1},{8,12},{9,5},{12,14},{13,9},{14,10},{15,13... | collective-permute-start | bytes 786440 | tf_op jit(solution)/shard_map/ppermute | solution.py:283
  63.9 11.2 %copy-start.1 = (bf16[16,16,128]{2,1,0:T(8,128)(2,1)S(1)}, bf16[16,16,128]{2,1,0:T(8,128)(2,1)}, u32[]{:S(2)}) copy-start(bf16[16,16,128]{2,1,0:T(8,128)(2,1)} %refs_8_.1) | copy-start | bytes 196612
  64.0 6.4 %collective-permute-start.26 = (bf16[16,64,128]{2,1,0:T(8,128)(2,1)S(1)}, bf16[16,64,128]{2,1,0:T(8,128)(2,1)S(1)}, u32[]{:S(2)}, u32[]{:S(2)}) collective-permute-start(bf16[16,64,128]{2,1,0:T(8,128)(2,1)S(1)} %add_convert_fusion.3), channel_id=1, source_target_pairs={{0,4},{1,3},{4,8},{5,1},{8,12},{9,5},{12,14},{13,9},{14,10},{15,13... | collective-permute-start | bytes 786440 | tf_op jit(solution)/shard_map/ppermute | solution.py:283
  66.7 6.4 %collective-permute-start.28 = (bf16[16,64,128]{2,1,0:T(8,128)(2,1)S(1)}, bf16[16,64,128]{2,1,0:T(8,128)(2,1)S(1)}, u32[]{:S(2)}, u32[]{:S(2)}) collective-permute-start(bf16[16,64,128]{2,1,0:T(8,128)(2,1)S(1)} %add_convert_fusion.2), channel_id=1, source_target_pairs={{0,4},{1,3},{4,8},{5,1},{8,12},{9,5},{12,14},{13,9},{14,10},{15,13... | collective-permute-start | bytes 786440 | tf_op jit(solution)/shard_map/ppermute | solution.py:283
  70.5 7.0 %collective-permute-start.30 = (bf16[16,64,128]{2,1,0:T(8,128)(2,1)S(1)}, bf16[16,64,128]{2,1,0:T(8,128)(2,1)S(1)}, u32[]{:S(2)}, u32[]{:S(2)}) collective-permute-start(bf16[16,64,128]{2,1,0:T(8,128)(2,1)S(1)} %add_convert_fusion.1), channel_id=1, source_target_pairs={{0,4},{1,3},{4,8},{5,1},{8,12},{9,5},{12,14},{13,9},{14,10},{15,13... | collective-permute-start | bytes 786440 | tf_op jit(solution)/shard_map/ppermute | solution.py:283
  73.2 4.3 %collective-permute-start.29 = (bf16[16,64,128]{2,1,0:T(8,128)(2,1)S(1)}, bf16[16,64,128]{2,1,0:T(8,128)(2,1)S(1)}, u32[]{:S(2)}, u32[]{:S(2)}) collective-permute-start(bf16[16,64,128]{2,1,0:T(8,128)(2,1)S(1)} %collective-permute-done.28), channel_id=1, source_target_pairs={{0,1},{1,0},{2,3},{3,2},{4,5},{5,4},{6,7},{7,6},{8,9},{9,8},{10,11... | collective-permute-start | bytes 786440 | tf_op jit(solution)/shard_map/ppermute | solution.py:283
  73.2 1.7 %collective-permute-start.8 = (bf16[512,128]{1,0:T(8,128)(2,1)S(1)}, bf16[512,128]{1,0:T(8,128)(2,1)S(1)}, u32[]{:S(2)}, u32[]{:S(2)}) collective-permute-start(bf16[512,128]{1,0:T(8,128)(2,1)S(1)} %pad_maximum_fusion.refs_0_), channel_id=1, source_target_pairs={{0,1},{1,0},{2,3},{3,2},{4,5},{5,4},{6,7},{7,6},{8,9},{9,8},{10,11... | collective-permute-start | bytes 393224 | tf_op jit(solution)/shard_map/ppermute | solution.py:283
  73.7 1.4 %collective-permute-start.9 = (bf16[512,128]{1,0:T(8,128)(2,1)S(1)}, bf16[512,128]{1,0:T(8,128)(2,1)S(1)}, u32[]{:S(2)}, u32[]{:S(2)}) collective-permute-start(bf16[512,128]{1,0:T(8,128)(2,1)S(1)} %collective-permute-done.7.refs_1_), channel_id=1, source_target_pairs={{0,1},{1,0},{2,3},{3,2},{4,5},{5,4},{6,7},{7,6},{8,9},{9,8},{10,11... | collective-permute-start | bytes 393224 | tf_op jit(solution)/shard_map/ppermute | solution.py:283
  (2 other events, 12.1 us)

commit v4 on v3

--- a/solution.py
+++ b/solution.py
@@ -115,11 +115,14 @@
     return pl.BlockSpec(memory_space=space)
 
 
-def coef_kernel(rhs_ref, basis_ref, out_ref, copy_ref):
-    copy_ref[...] = rhs_ref[...]
+def prologue_kernel(
+    count, me_ref, owner_ref, slot_ref, offset_ref, rhs_ref, basis_ref, coef_ref, copy_ref, list_ref
+):
     clusters = rhs_ref.shape[0]
     rank_k = basis_ref.shape[1]
+    stored = owner_ref.shape[1]
     half = clusters // 2
+    copy_ref[...] = rhs_ref[...]
     rows = []
     for c in range(half):
         parts = [
@@ -132,16 +135,51 @@
             for e in (c, c + half)
         ]
         rows.append(jnp.concatenate(parts, axis=1))
-    for q in range(rank_k):
-        out_ref[q * half : (q + 1) * half, :] = jnp.concatenate(
-            [row[q : q + 1] for row in rows], axis=0
-        )
-
-
-def near_kernel(part, batch, starts_ref, block_ref, pos_ref, row_ref, *rest):
-    shards, rest = rest[: part["shards"]], rest[part["shards"] :]
-    blocks_hbm, rest = rest[0], rest[1:]
-    send_ref, keep_ref, columns, blocks, acc, sems = rest
+    coef_ref[...] = jnp.concatenate(
+        [row[q : q + 1] for q in range(rank_k) for row in rows], axis=0
+    ).astype(coef_ref.dtype)
+
+    me, owner, slot = me_ref[0], owner_ref[...], slot_ref[...]
+    chips = count // 2
+    depth = chips // 2
+    handler, steps, other = scatter_place(owner, me, count)
+    early = steps >= depth - 1
+    shard_at = jnp.where(
+        early,
+        jnp.where(steps == depth, 0, 2 - other),
+        jnp.where(steps == 0, 2 * (depth - 2), 2 * (depth - 2 - steps) + 1 - other),
+    )
+    shard_at = shard_at + jnp.where(handler == (me & 1), 0, jnp.where(early, 3, 2 * depth - 3))
+    column = (owner * clusters + slot + offset_ref[...]) & (count * clusters - 1)
+    column_slot = gather_slot(column // clusters, me, count)
+    column_row = column_slot * clusters + (column & (clusters - 1))
+    square = (stored, stored)
+    group = jnp.broadcast_to(jnp.where(early, 0.0, 1.0), square)
+    group_of_row = jnp.transpose(group)
+    row_at = lax.broadcasted_iota(jnp.int32, square, 0)
+    lane_at = lax.broadcasted_iota(jnp.int32, square, 1)
+    before = (group_of_row < group) | ((group_of_row == group) & (row_at < lane_at))
+    rank = jnp.sum(jnp.where(before, 1.0, 0.0), axis=0, keepdims=True)
+    rank = jnp.transpose(jnp.broadcast_to(rank, square))
+    here = jnp.where(rank == lane_at.astype(jnp.float32), 1.0, 0.0).astype(jnp.bfloat16)
+    first = stored - jnp.sum(group[0:1], axis=1, keepdims=True)
+    values = jnp.concatenate(
+        [
+            lane_at[0:1].astype(jnp.float32),
+            (shard_at * clusters + slot).astype(jnp.float32),
+            column_row.astype(jnp.float32),
+            jnp.broadcast_to(first, (1, stored)),
+            jnp.zeros((4, stored), jnp.float32),
+        ],
+        axis=0,
+    )
+    ordered = jnp.dot(values.astype(jnp.bfloat16), here, preferred_element_type=jnp.float32)
+    list_ref[...] = ordered.astype(jnp.int32)
+
+
+def near_kernel(late, batch, count, list_ref, *rest):
+    shards, blocks_hbm, rest = rest[:count], rest[count], rest[count + 1 :]
+    sends, (keep_ref, columns, blocks, acc, sems) = rest[:-5], rest[-5:]
     directions, unknowns = acc.shape[1:]
     load = pltpu.make_async_copy(blocks_hbm, blocks, sems.at[len(shards)])
     load.start()
@@ -154,7 +192,8 @@
     for copy in copies:
         copy.wait()
     load.wait()
-    begin, end = starts_ref[part["at"]], starts_ref[part["at"] + 1]
+    begin = list_ref[3, 0] if late else 0
+    end = blocks.shape[0] if late else list_ref[3, 0]
     last = blocks.shape[0] - 1
     dummy = acc.shape[0] - 1
 
@@ -163,28 +202,32 @@
         products = []
         for k in range(batch):
             at = jnp.minimum(first + k, last)
-            row = row_ref[at]
+            row = list_ref[2, at]
             products.append(
                 lax.dot_general(
                     columns[row // columns.shape[1], row % columns.shape[1]],
-                    blocks[block_ref[at]],
+                    blocks[list_ref[0, at]],
                     (((1,), (1,)), ((), ())),
                     preferred_element_type=jnp.float32,
                 )
             )
         for k in range(batch):
-            at = jnp.where(first + k < end, pos_ref[jnp.minimum(first + k, last)], dummy)
+            at = jnp.where(first + k < end, list_ref[1, jnp.minimum(first + k, last)], dummy)
             acc[at] = acc[at] + products[k]
         return carry
 
     lax.fori_loop(0, (end - begin + batch - 1) // batch, body, 0)
-    size = send_ref.shape[0]
-    keep_ref[...] = acc[0:size]
-    send_ref[...] = acc[size : 2 * size].astype(send_ref.dtype)
+    at = keep_ref.shape[0]
+    keep_ref[...] = acc[0:at]
+    for send_ref in sends:
+        size = send_ref.shape[0]
+        send_ref[...] = acc[at : at + size].astype(send_ref.dtype)
+        at += size
 
 
 def far_kernel(*refs):
-    coef_refs, (couple_ref, slot_ref, pick_ref, half_ref, basis_ref, out_ref) = refs[:4], refs[4:]
+    coef_refs = refs[:4]
+    me_ref, couple_ref, slot_ref, dev_ref, cslot_ref, basis_ref, out_ref = refs[4:]
     clusters, rank_k, unknowns = basis_ref.shape
     pairs = couple_ref.shape[2]
     directions = out_ref.shape[1]
@@ -196,8 +239,23 @@
         lax.broadcasted_iota(jnp.int32, (clusters, pairs), 0)
         == jnp.broadcast_to(slot_ref[...], (clusters, pairs))
     ).astype(jnp.float32).astype(jnp.bfloat16)
-    pick = pick_ref[...]
-    keep = half_ref[...]
+    away = dev_ref[...] ^ me_ref[0]
+    away = (away & 1) * (count // 2) + ((away >> 1) & 1) * (count // 4) + (away >> 2)
+    cslot = cslot_ref[...]
+    high = (cslot >= half).astype(jnp.int32)
+    at = away * half + cslot - high * half
+    table_rows = (count * half, pairs)
+    pick = jnp.where(
+        lax.broadcasted_iota(jnp.int32, table_rows, 0) == jnp.broadcast_to(at, table_rows), 1.0, 0.0
+    )
+    pick = jnp.transpose(pick).astype(jnp.bfloat16)
+    lanes = (unknowns, pairs)
+    keep = jnp.where(
+        lax.broadcasted_iota(jnp.int32, lanes, 0) // directions == jnp.broadcast_to(high, lanes),
+        1.0,
+        0.0,
+    )
+    keep = jnp.transpose(keep).astype(jnp.bfloat16)
     total = jnp.zeros((clusters * rank_k, unknowns), jnp.float32)
     for q in range(rank_k):
         table = coef[:, q].reshape(count * half, unknowns).astype(jnp.bfloat16)
@@ -275,6 +333,7 @@
     stored = near_blocks.shape[0]
     pairs = far_slot.shape[0]
     half = clusters // 2
+    assert stored == unknowns and 2 * directions == unknowns
     ahead, cross = ring_pairs(count)
     mate = [(i, i ^ 1) for i in range(count)]
     side = [(i, i ^ 2) for i in range(count)]
@@ -282,127 +341,101 @@
     def move(values, where):
         return lax.ppermute(values, "blk", where)
 
-    coef, here_rhs = pl.pallas_call(
-        coef_kernel,
+    def after(values, *others):
+        return lax.optimization_barrier((values, *others))[0]
+
+    flow = [move(rhs, ahead), move(rhs, cross)]
+    here = me.astype(jnp.int32).reshape(1)
+    coef, here_rhs, lists = pl.pallas_call(
+        functools.partial(prologue_kernel, count),
         out_shape=[
-            jax.ShapeDtypeStruct((half * rank_k, unknowns), jnp.float32),
+            jax.ShapeDtypeStruct((half * rank_k, unknowns), jnp.bfloat16),
             jax.ShapeDtypeStruct(rhs.shape, rhs.dtype),
+            jax.ShapeDtypeStruct((8, stored), jnp.int32),
         ],
-        in_specs=[whole(), whole()],
-        out_specs=[whole(), whole()],
-        name="coef",
-    )(rhs, basis_in)
-    coef = coef.astype(jnp.bfloat16)
-
-    owner = near_owner[:, 0]
-    handler, steps, other = scatter_place(owner, me, count)
-    group = (steps < depth - 1).astype(jnp.int32)
-    sizes = (3, 2 * (depth - 2) + 1)
-    shard_at = jnp.where(
-        group == 0,
-        jnp.where(steps == depth, 0, 1 + other),
-        jnp.where(steps == 0, 2 * (depth - 2), 2 * (depth - 2 - steps) + other),
-    )
-    shard_at = shard_at + jnp.where(
-        handler == (me & 1), 0, jnp.where(group == 0, sizes[0], sizes[1])
-    )
-    position = shard_at * clusters + near_slot
-    column = (owner * clusters + near_slot + near_offset) % (count * clusters)
-    column_row = gather_slot(column // clusters, me, count) * clusters + column % clusters
-    index = jnp.arange(stored, dtype=jnp.int32)
-    before = (group[None, :] < group[:, None]) | (
-        (group[None, :] == group[:, None]) & (index[None, :] < index[:, None])
-    )
-    rank = jnp.sum(before.astype(jnp.int32), axis=1)
-    here = rank[None, :] == index[:, None]
-    block_at, position, column_row = [
-        jnp.sum(jnp.where(here, values[None, :], 0), axis=1)
-        for values in (index, position, column_row)
-    ]
-    starts = jnp.sum(
-        (group[None, :] < jnp.arange(3, dtype=jnp.int32)[:, None]).astype(jnp.int32), axis=1
-    )
-
-    far_at = far_dev[:, 0]
-    far_at = (
-        ((far_at ^ me) & 1) * (2 * depth)
-        + (((far_at ^ me) >> 1) & 1) * depth
-        + ((me >> 2) - (far_at >> 2) + depth) % depth
-    )
-    pick = (
-        (far_at * half + far_cslot % half)[:, None]
-        == jnp.arange(count * half, dtype=jnp.int32)[None, :]
-    ).astype(jnp.bfloat16)
-    keep = (
-        (far_cslot // half)[:, None] == (jnp.arange(unknowns, dtype=jnp.int32) // directions)[None, :]
-    ).astype(jnp.bfloat16)
+        in_specs=[whole(pltpu.SMEM)] + [whole()] * 5,
+        out_specs=[whole()] * 3,
+        name="prologue",
+    )(
+        here,
+        near_owner.reshape(1, stored),
+        near_slot.reshape(1, stored),
+        near_offset.reshape(1, stored),
+        rhs,
+        basis_in,
+    )
+    slots = {0: here_rhs, 1: move(rhs, mate)}
+    coefs, level = coef, 1
+    waits = [[coef, here_rhs, lists], []]
+    for t in range(1, depth + 1):
+        for x in range(2 if t < depth else 1):
+            flow[x] = after(flow[x], *waits[x])
+            slots[2 * t + x] = flow[x]
+            opposite = 2 * (chips - t) + 1 - x
+            if t + x < depth:
+                moving = move(flow[x], ahead)
+            slots[opposite] = move(flow[x], mate)
+            waits[x] = [slots[opposite]]
+            if t + x < depth:
+                flow[x] = moving
+            if x == 0 and level < depth:
+                got = move(coefs, [(i, i ^ (4 * level)) for i in range(count)])
+                coefs, level = jnp.concatenate([coefs, got], axis=0), 2 * level
+                waits[1].append(coefs)
+    coefs = [coefs, move(coefs, side)]
     couple = jnp.transpose(far_coupling, (2, 1, 0))
 
-    slots = {0: here_rhs}
-    flow = [move(rhs, ahead), move(rhs, cross)]
-    slots[1] = move(rhs, mate)
-    for t in range(1, depth + 1):
-        if t == 2:
-            flow[0], coef, starts, block_at, position, column_row = lax.optimization_barrier(
-                (flow[0], coef, starts, block_at, position, column_row)
-            )
-            coefs = [coef] + [
-                move(coef, [(i, (i + 4 * k) % count) for i in range(count)])
-                for k in range(1, depth)
+    def near(late, lists):
+        parts = [1, 2 * depth - 4] if late else [1, 1, 1]
+        size = sum(parts) * clusters
+        *sends, kept = pl.pallas_call(
+            functools.partial(near_kernel, late, 4, count),
+            out_shape=[
+                jax.ShapeDtypeStruct((part * clusters, directions, unknowns), jnp.bfloat16)
+                for part in parts
             ]
-        if t == 3:
-            flow[0], couple, pick, keep = lax.optimization_barrier((flow[0], couple, pick, keep))
-        if t == 4:
-            flow[0], coefs = lax.optimization_barrier((flow[0], jnp.concatenate(coefs, axis=0)))
-            coefs = [coefs, move(coefs, side)]
-        for x in range(2 if t < depth else 1):
-            slots[2 * t + x] = flow[x]
-            slots[2 * (chips - t) + 1 - x] = move(flow[x], mate)
-            if t + x < depth:
-                flow[x] = move(flow[x], ahead)
-
-    sums = []
-    for j, size in enumerate(sizes):
-        if j == 1:
-            starts, coefs = lax.optimization_barrier((starts, coefs))
-            coefs = coefs + [move(part, mate) for part in coefs]
-        sums.append(
-            pl.pallas_call(
-                functools.partial(near_kernel, dict(shards=count, at=j), 4),
-                out_shape=[
-                    jax.ShapeDtypeStruct((size * clusters, directions, unknowns), jnp.bfloat16),
-                    jax.ShapeDtypeStruct((size * clusters, directions, unknowns), jnp.float32),
-                ],
-                in_specs=[whole(pltpu.SMEM)] * 4
-                + [whole(pl.ANY)] * (count + 1),
-                out_specs=[whole()] * 2,
-                scratch_shapes=[
-                    pltpu.VMEM((count, clusters, directions, unknowns), jnp.bfloat16),
-                    pltpu.VMEM(near_blocks.shape, jnp.bfloat16),
-                    pltpu.VMEM((2 * size * clusters + 1, directions, unknowns), jnp.float32),
-                    pltpu.SemaphoreType.DMA((count + 1,)),
-                ],
-                compiler_params=pltpu.CompilerParams(vmem_limit_bytes=NEAR_VMEM),
-                cost_estimate=pl.CostEstimate(
-                    flops=2 * stored * directions * unknowns * unknowns * 8,
-                    bytes_accessed=12 << 20,
-                    transcendentals=0,
-                ),
-                name="near",
-            )(
-                starts,
-                block_at,
-                position,
-                column_row,
-                *[slots[k] for k in range(count)],
-                near_blocks,
-            )
-        )
-
+            + [jax.ShapeDtypeStruct((size, directions, unknowns), jnp.float32)],
+            in_specs=[whole(pltpu.SMEM)] + [whole(pl.ANY)] * (count + 1),
+            out_specs=[whole()] * (len(parts) + 1),
+            scratch_shapes=[
+                pltpu.VMEM((count, clusters, directions, unknowns), jnp.bfloat16),
+                pltpu.VMEM(near_blocks.shape, jnp.bfloat16),
+                pltpu.VMEM((2 * size + 1, directions, unknowns), jnp.float32),
+                pltpu.SemaphoreType.DMA((count + 1,)),
+            ],
+            compiler_params=pltpu.CompilerParams(vmem_limit_bytes=NEAR_VMEM),
+            cost_estimate=pl.CostEstimate(
+                flops=2 * stored * directions * unknowns * unknowns * 8,
+                bytes_accessed=12 << 20,
+                transcendentals=0,
+            ),
+            name="near",
+        )(lists, *[slots[k] for k in range(count)], near_blocks)
+        return [move(send, mate) for send in sends], kept
+
+    own, mates = [None, None], [None, None]
+
+    def term(late, k):
+        part, skip = (min(k, 1), min(k, 1)) if late else (k, k)
+        at = slice(k * clusters, (k + 1) * clusters)
+        got = mates[late][part][(k - skip) * clusters : (k - skip + 1) * clusters]
+        return own[late][at] + got.astype(jnp.float32)
+
+    def add(flow, late, k, *others):
+        step = (flow.astype(jnp.float32) + term(late, k)).astype(jnp.bfloat16)
+        step, mates[late], *_ = lax.optimization_barrier((step, mates[late], *others))
+        return step
+
+    mates[0], own[0] = near(False, lists)
+    flow = [term(0, 0).astype(jnp.bfloat16), term(0, 1).astype(jnp.bfloat16)]
+    *flow, lists, coefs[0], coefs[1] = lax.optimization_barrier((*flow, lists, *coefs))
+    flow = [move(part, ahead) for part in flow]
+    coefs = coefs + [move(part, mate) for part in coefs]
+    mates[1], own[1] = near(True, lists)
     far = pl.pallas_call(
         far_kernel,
         out_shape=jax.ShapeDtypeStruct((clusters, directions, unknowns), jnp.float32),
-        in_specs=[whole()] * 9,
+        in_specs=[whole()] * 4 + [whole(pltpu.SMEM)] + [whole()] * 5,
         out_specs=whole(),
         compiler_params=pltpu.CompilerParams(vmem_limit_bytes=FAR_VMEM),
         cost_estimate=pl.CostEstimate(
@@ -411,35 +444,29 @@
             transcendentals=0,
         ),
         name="far",
-    )(*coefs, couple, far_slot.reshape(1, pairs), pick, keep, basis_out)
-
-    own = [kept for _, kept in sums]
-    mates = [move(sent, mate) for sent, _ in sums]
-
-    def term(j, k):
-        at = slice(k * clusters, (k + 1) * clusters)
-        return own[j][at] + mates[j][at].astype(jnp.float32)
-
-    def add(flow, j, k):
-        step = (flow.astype(jnp.float32) + term(j, k)).astype(jnp.bfloat16)
-        step, mates[j] = lax.optimization_barrier((step, mates[j]))
-        return step
-
-    flow = lax.optimization_barrier(
-        [term(0, 0).astype(jnp.bfloat16), term(0, 2).astype(jnp.bfloat16)]
-    )
-    for t in range(depth - 1, -1, -1):
-        flow = [move(part, ahead) for part in flow]
-        if t == 0:
-            break
-        flow[0] = add(flow[0], 0, 1) if t == depth - 1 else add(flow[0], 1, 2 * (depth - 2 - t))
+    )(
+        *coefs,
+        here,
+        couple,
+        far_slot.reshape(1, pairs),
+        far_dev.reshape(1, pairs),
+        far_cslot.reshape(1, pairs),
+        basis_out,
+    )
+    for t in range(depth - 1, 0, -1):
+        if t == depth - 1:
+            flow[0] = add(flow[0], 0, 2)
+        elif t > 1:
+            flow[0] = add(flow[0], 1, 2 * (depth - 2 - t) + 1)
+        else:
+            flow[0] = add(flow[0], 1, 2 * (depth - 2 - t) + 1, far)
+        flow[0] = move(flow[0], ahead)
         if t > 1:
-            flow[1] = add(flow[1], 1, 2 * (depth - 1 - t) + 1)
+            flow[1] = move(add(flow[1], 1, 2 * (depth - 1 - t)), ahead)
         else:
-            last = move(flow[1], mate)
-            flow = flow[:1]
-    total = far + term(1, 2 * (depth - 2)) + last.astype(jnp.float32) + flow[0].astype(jnp.float32)
-    return total.astype(jnp.bfloat16)
+            flow[1] = move(flow[1], mate)
+    total = far + term(1, 2 * (depth - 2)) + flow[1].astype(jnp.float32)
+    return (total + flow[0].astype(jnp.float32)).astype(jnp.bfloat16)
 
 
 def on_device(*args):

time: 79 us -> 89.8 us (1.14)
  waiting for transfers between devices: 16.1 us -> 36.3 us
  other arithmetic: 6.43 us -> 1.52 us
  starting transfers between devices: 36.5 us -> 31.7 us
    ppermute x31 -> x33, waiting for transfers between devices: 16.1 us -> 36.3 us  [move(): return lax.ppermute(values, 'blk', where)]
    ppermute x31 -> x33, starting transfers between devices: 36.5 us -> 31.7 us  [move(): return lax.ppermute(values, 'blk', where)]
    add x2 -> x0, other arithmetic: 1.42 us -> none  [the longest x1 0.73 us: stationary(): position = shard_at * clusters + near_slot]
    select_n x3 -> x0, other arithmetic: 1.37 us -> none  [the longest x1 0.69 us: stationary(): far_cslot // half]
    convert_element_type x10 -> x7, other arithmetic: 2.5 us -> 1.52 us  [the longest x1 0.89 us: stationary(): return (total + flow[0].astype(jnp.float32)).astype(jnp.bfloat16)]
    unnamed x7 -> x17, local copies, waits for them, and re-layouts: 1.91 us -> 2.5 us
  transfers between devices with their start and end apart: 31 -> 33, of which waited for: 14 -> 14; matrix products, arithmetic and copies ran while one was open for 8% -> 2% of each run, Pallas kernels for 22% -> 5%
where the time goes in v4:
time: 89.8 us; the launch traced here: 89.7 us
  waiting for transfers between devices  36.3 us (40%)
  starting transfers between devices  31.7 us (35%)
  Pallas kernels  17.5 us (19%)
  local copies, waits for them, and re-layouts  2.52 us (3%)
  other arithmetic  1.52 us (2%)
    ppermute x33, waiting for transfers between devices, move(): return lax.ppermute(values, 'blk', where)  36.3 us
    ppermute x33, starting transfers between devices, move(): return lax.ppermute(values, 'blk', where)  31.7 us
    pallas_call x2, Pallas kernels, near(): pl.pallas_call(functools.partial(near_kernel, late, 4, count), out_shape=...  13.1 us
    unnamed x17, local copies, waits for them, and re-layouts  2.5 us
    pallas_call x1, Pallas kernels, stationary(): pl.pallas_call(far_kernel, out_shape=jax.ShapeDtypeStruct((clusters, dire...  2.5 us
    pallas_call x1, Pallas kernels, stationary(): pl.pallas_call(functools.partial(prologue_kernel, count), out_shape=[jax....  1.98 us
  transfers between devices with their start and end apart: 33, of which 14 were waited for; matrix products, arithmetic and copies ran while one was open for 2% of the time, Pallas kernels for 5%

profile of v4, /device:TPU:0, one launch (start us, length us, event | category | flops | bytes accessed | tf_op | source)
XLA Modules:
  0.0 89.7 jit_solution(13539330368802871322)
XLA Ops:
  0.0 3.0 %collective-permute-start.1 = (bf16[16,64,128]{2,1,0:T(8,128)(2,1)}, bf16[16,64,128]{2,1,0:T(8,128)(2,1)S(1)}, u32[]{:S(2)}, u32[]{:S(2)}) collective-permute-start(bf16[16,64,128]{2,1,0:T(8,128)(2,1)} %rhs_ref.1), channel_id=1, source_target_pairs={{0,4},{1,3},{4,8},{5,1},{8,12},{9,5},{12,14},{13,9},{14,10},{15,13... | collective-permute-start | bytes 786440 | tf_op jit(solution)/shard_map/ppermute | solution.py:342
  3.7 2.0 %prologue.1 = (bf16[128,128]{1,0:T(8,128)(2,1)}, bf16[16,64,128]{2,1,0:T(8,128)(2,1)}, s32[8,128]{1,0:T(8,128)}) custom-call(s32[1]{0:T(128)} %bitcast.me_ref.refs_4_, s32[1,128]{1,0:T(1,128)} %bitcast.14, s32[1,128]{1,0:T(1,128)} %bitcast.15, s32[1,128]{1,0:T(1,128)} %bitcast.16, bf16[16,64,128]{2,1,0:T(8,128)(2,1)} %rhs_ref.1, bf16[16,16,128]{2,1,0:T(8,128)(2,1)} %basis_ref.1), custom_call_target="tpu_custom_call" | custom-call | tf_op jit(solution)/shard_map/prologue/pallas_call | solution.py:349
  5.7 3.4 %collective-permute-done.1.rest_2_ = bf16[16,64,128]{2,1,0:T(8,128)(2,1)S(1)} collective-permute-done((bf16[16,64,128]{2,1,0:T(8,128)(2,1)}, bf16[16,64,128]{2,1,0:T(8,128)(2,1)S(1)}, u32[]{:S(2)}, u32[]{:S(2)}) %collective-permute-start.1) | collective-permute-done | bytes 262176 | tf_op jit(solution)/shard_map/ppermute | solution.py:342
  9.0 2.4 %collective-permute-start.4 = (bf16[16,64,128]{2,1,0:T(8,128)(2,1)S(1)}, bf16[16,64,128]{2,1,0:T(8,128)(2,1)S(1)}, u32[]{:S(2)}, u32[]{:S(2)}) collective-permute-start(bf16[16,64,128]{2,1,0:T(8,128)(2,1)S(1)} %collective-permute-done.1.rest_2_), channel_id=1, source_target_pairs={{0,4},{1,3},{4,8},{5,1},{8,12},{9,5},{12,14},{13,9},{14,10},{15,13... | collective-permute-start | bytes 786440 | tf_op jit(solution)/shard_map/ppermute | solution.py:342
  11.4 1.6 %collective-permute-start.3 = (bf16[128,128]{1,0:T(8,128)(2,1)}, bf16[128,128]{1,0:T(8,128)(2,1)S(1)}, u32[]{:S(2)}, u32[]{:S(2)}) collective-permute-start(bf16[128,128]{1,0:T(8,128)(2,1)} %get-tuple-element.38), channel_id=1, source_target_pairs={{0,4},{1,5},{2,6},{3,7},{4,0},{5,1},{6,2},{7,3},{8,12},{9,13},{10,... | collective-permute-start | bytes 98312 | tf_op jit(solution)/shard_map/ppermute | solution.py:342
  13.8 2.3 %collective-permute-done.3 = bf16[128,128]{1,0:T(8,128)(2,1)S(1)} collective-permute-done((bf16[128,128]{1,0:T(8,128)(2,1)}, bf16[128,128]{1,0:T(8,128)(2,1)S(1)}, u32[]{:S(2)}, u32[]{:S(2)}) %collective-permute-start.3) | collective-permute-done | bytes 32800 | tf_op jit(solution)/shard_map/ppermute | solution.py:342
  16.1 2.4 %collective-permute-start.6 = (bf16[16,64,128]{2,1,0:T(8,128)(2,1)S(1)}, bf16[16,64,128]{2,1,0:T(8,128)(2,1)S(1)}, u32[]{:S(2)}, u32[]{:S(2)}) collective-permute-start(bf16[16,64,128]{2,1,0:T(8,128)(2,1)S(1)} %collective-permute-done.2.rest_3_), channel_id=1, source_target_pairs={{0,4},{1,3},{4,8},{5,1},{8,12},{9,5},{12,14},{13,9},{14,10},{15,13... | collective-permute-start | bytes 786440 | tf_op jit(solution)/shard_map/ppermute | solution.py:342
  19.8 2.0 %collective-permute-start.8 = (bf16[256,128]{1,0:T(8,128)(2,1)S(1)}, bf16[256,128]{1,0:T(8,128)(2,1)S(1)}, u32[]{:S(2)}, u32[]{:S(2)}) collective-permute-start(bf16[256,128]{1,0:T(8,128)(2,1)S(1)} %get-tuple-element.70), channel_id=1, source_target_pairs={{0,8},{1,9},{2,10},{3,11},{4,12},{5,13},{6,14},{7,15},{8,0},{9,1},... | collective-permute-start | bytes 196616 | tf_op jit(solution)/shard_map/ppermute | solution.py:342
  21.8 4.8 %collective-permute-done.8 = bf16[256,128]{1,0:T(8,128)(2,1)S(1)} collective-permute-done((bf16[256,128]{1,0:T(8,128)(2,1)S(1)}, bf16[256,128]{1,0:T(8,128)(2,1)S(1)}, u32[]{:S(2)}, u32[]{:S(2)}) %collective-permute-start.8) | collective-permute-done | bytes 65568 | tf_op jit(solution)/shard_map/ppermute | solution.py:342
  26.7 2.3 %collective-permute-start.11 = (bf16[16,64,128]{2,1,0:T(8,128)(2,1)S(1)}, bf16[16,64,128]{2,1,0:T(8,128)(2,1)S(1)}, u32[]{:S(2)}, u32[]{:S(2)}) collective-permute-start(bf16[16,64,128]{2,1,0:T(8,128)(2,1)S(1)} %collective-permute-done.6.rest_5_), channel_id=1, source_target_pairs={{0,4},{1,3},{4,8},{5,1},{8,12},{9,5},{12,14},{13,9},{14,10},{15,13... | collective-permute-start | bytes 786440 | tf_op jit(solution)/shard_map/ppermute | solution.py:342
  29.0 1.9 %collective-permute-start.13 = (bf16[16,64,128]{2,1,0:T(8,128)(2,1)S(1)}, bf16[16,64,128]{2,1,0:T(8,128)(2,1)S(1)}, u32[]{:S(2)}, u32[]{:S(2)}) collective-permute-start(bf16[16,64,128]{2,1,0:T(8,128)(2,1)S(1)} %collective-permute-done.9.rest_6_), channel_id=1, source_target_pairs={{0,4},{1,3},{4,8},{5,1},{8,12},{9,5},{12,14},{13,9},{14,10},{15,13... | collective-permute-start | bytes 786440 | tf_op jit(solution)/shard_map/ppermute | solution.py:342
  31.7 4.0 %collective-permute-done.11.rest_7_ = bf16[16,64,128]{2,1,0:T(8,128)(2,1)S(1)} collective-permute-done((bf16[16,64,128]{2,1,0:T(8,128)(2,1)S(1)}, bf16[16,64,128]{2,1,0:T(8,128)(2,1)S(1)}, u32[]{:S(2)}, u32[]{:S(2)}) %collective-permute-start.11) | collective-permute-done | bytes 262176 | tf_op jit(solution)/shard_map/ppermute | solution.py:342
  35.7 2.8 %collective-permute-done.13.rest_8_ = bf16[16,64,128]{2,1,0:T(8,128)(2,1)S(1)} collective-permute-done((bf16[16,64,128]{2,1,0:T(8,128)(2,1)S(1)}, bf16[16,64,128]{2,1,0:T(8,128)(2,1)S(1)}, u32[]{:S(2)}, u32[]{:S(2)}) %collective-permute-start.13) | collective-permute-done | bytes 262176 | tf_op jit(solution)/shard_map/ppermute | solution.py:342
  38.5 1.5 %collective-permute-done.15.rest_9_ = bf16[16,64,128]{2,1,0:T(8,128)(2,1)S(1)} collective-permute-done((bf16[16,64,128]{2,1,0:T(8,128)(2,1)S(1)}, bf16[16,64,128]{2,1,0:T(8,128)(2,1)S(1)}, u32[]{:S(2)}, u32[]{:S(2)}) %collective-permute-start.15) | collective-permute-done | bytes 262176 | tf_op jit(solution)/shard_map/ppermute | solution.py:342
  40.0 0.9 %copy-done = bf16[16,64,128]{2,1,0:T(8,128)(2,1)S(1)} copy-done((bf16[16,64,128]{2,1,0:T(8,128)(2,1)S(1)}, bf16[16,64,128]{2,1,0:T(8,128)(2,1)}, u32[]{:S(2)}) %copy-start) | copy-done | bytes 262168
  41.7 5.1 %near.2 = (bf16[16,64,128]{2,1,0:T(8,128)(2,1)S(1)}, bf16[16,64,128]{2,1,0:T(8,128)(2,1)S(1)}, bf16[16,64,128]{2,1,0:T(8,128)(2,1)S(1)}, f32[48,64,128]{2,1,0:T(8,128)S(1)}) custom-call(s32[8,128]{1,0:T(8,128)S(1)} %copy-done.1, bf16[16,64,128]{2,1,0:T(8,128)(2,1)S(1)} %copy-done, bf16[16,64,128]{2,1,0:T(8,128)(2,1)S(1)} %collective-permute-done.rest_1_, ...), custom_call_target="tpu_custom_call" | custom-call | flops 2147483648 | bytes 12582912 | tf_op jit(solution)/shard_map/near/pallas_call | solution.py:391
  47.4 2.4 %collective-permute-start.19 = (bf16[512,128]{1,0:T(8,128)(2,1)S(1)}, bf16[512,128]{1,0:T(8,128)(2,1)S(1)}, u32[]{:S(2)}, u32[]{:S(2)}) collective-permute-start(bf16[512,128]{1,0:T(8,128)(2,1)S(1)} %constant_dynamic-update-slice_fusion.2.refs_0_), channel_id=1, source_target_pairs={{0,2},{1,3},{2,0},{3,1},{4,6},{5,7},{6,4},{7,5},{8,10},{9,11},{10,... | collective-permute-start | bytes 393224 | tf_op jit(solution)/shard_map/ppermute | solution.py:342
  50.0 3.8 %collective-permute-done.19.refs_1_ = bf16[512,128]{1,0:T(8,128)(2,1)S(1)} collective-permute-done((bf16[512,128]{1,0:T(8,128)(2,1)S(1)}, bf16[512,128]{1,0:T(8,128)(2,1)S(1)}, u32[]{:S(2)}, u32[]{:S(2)}) %collective-permute-start.19) | collective-permute-done | bytes 131104 | tf_op jit(solution)/shard_map/ppermute | solution.py:342
  53.8 7.9 %near.3 = (bf16[16,64,128]{2,1,0:T(8,128)(2,1)S(1)}, bf16[64,64,128]{2,1,0:T(8,128)(2,1)S(1)}, f32[80,64,128]{2,1,0:T(8,128)S(1)}) custom-call(s32[8,128]{1,0:T(8,128)S(1)} %copy-done.1, bf16[16,64,128]{2,1,0:T(8,128)(2,1)S(1)} %copy-done, bf16[16,64,128]{2,1,0:T(8,128)(2,1)S(1)} %collective-permute-done.rest_1_, ...), custom_call_target="tpu_custom_call" | custom-call | flops 2147483648 | bytes 12582912 | tf_op jit(solution)/shard_map/near/pallas_call | solution.py:391
  62.3 1.5 %collective-permute-start.22 = (bf16[16,64,128]{2,1,0:T(8,128)(2,1)S(1)}, bf16[16,64,128]{2,1,0:T(8,128)(2,1)S(1)}, u32[]{:S(2)}, u32[]{:S(2)}) collective-permute-start(bf16[16,64,128]{2,1,0:T(8,128)(2,1)S(1)} %get-tuple-element.53), channel_id=1, source_target_pairs={{0,4},{1,3},{4,8},{5,1},{8,12},{9,5},{12,14},{13,9},{14,10},{15,13... | collective-permute-start | bytes 786440 | tf_op jit(solution)/shard_map/ppermute | solution.py:342
  64.9 3.8 %collective-permute-done.22 = bf16[16,64,128]{2,1,0:T(8,128)(2,1)S(1)} collective-permute-done((bf16[16,64,128]{2,1,0:T(8,128)(2,1)S(1)}, bf16[16,64,128]{2,1,0:T(8,128)(2,1)S(1)}, u32[]{:S(2)}, u32[]{:S(2)}) %collective-permute-start.22) | collective-permute-done | bytes 262176 | tf_op jit(solution)/shard_map/ppermute | solution.py:342
  68.8 1.6 %collective-permute-start.24 = (bf16[16,64,128]{2,1,0:T(8,128)(2,1)S(1)}, bf16[16,64,128]{2,1,0:T(8,128)(2,1)S(1)}, u32[]{:S(2)}, u32[]{:S(2)}) collective-permute-start(bf16[16,64,128]{2,1,0:T(8,128)(2,1)S(1)} %add_convert_fusion.5), channel_id=1, source_target_pairs={{0,4},{1,3},{4,8},{5,1},{8,12},{9,5},{12,14},{13,9},{14,10},{15,13... | collective-permute-start | bytes 786440 | tf_op jit(solution)/shard_map/ppermute | solution.py:342
  70.4 1.1 %collective-permute-done.25 = bf16[16,64,128]{2,1,0:T(8,128)(2,1)S(1)} collective-permute-done((bf16[16,64,128]{2,1,0:T(8,128)(2,1)S(1)}, bf16[16,64,128]{2,1,0:T(8,128)(2,1)S(1)}, u32[]{:S(2)}, u32[]{:S(2)}) %collective-permute-start.25) | collective-permute-done | bytes 262176 | tf_op jit(solution)/shard_map/ppermute | solution.py:342
  71.6 1.6 %collective-permute-start.29 = (bf16[16,64,128]{2,1,0:T(8,128)(2,1)S(1)}, bf16[16,64,128]{2,1,0:T(8,128)(2,1)S(1)}, u32[]{:S(2)}, u32[]{:S(2)}) collective-permute-start(bf16[16,64,128]{2,1,0:T(8,128)(2,1)S(1)} %add_convert_fusion.4), channel_id=1, source_target_pairs={{0,4},{1,3},{4,8},{5,1},{8,12},{9,5},{12,14},{13,9},{14,10},{15,13... | collective-permute-start | bytes 786440 | tf_op jit(solution)/shard_map/ppermute | solution.py:342
  73.8 1.4 %collective-permute-done.24 = bf16[16,64,128]{2,1,0:T(8,128)(2,1)S(1)} collective-permute-done((bf16[16,64,128]{2,1,0:T(8,128)(2,1)S(1)}, bf16[16,64,128]{2,1,0:T(8,128)(2,1)S(1)}, u32[]{:S(2)}, u32[]{:S(2)}) %collective-permute-start.24) | collective-permute-done | bytes 262176 | tf_op jit(solution)/shard_map/ppermute | solution.py:342
  75.3 1.6 %collective-permute-start.28 = (bf16[16,64,128]{2,1,0:T(8,128)(2,1)S(1)}, bf16[16,64,128]{2,1,0:T(8,128)(2,1)S(1)}, u32[]{:S(2)}, u32[]{:S(2)}) collective-permute-start(bf16[16,64,128]{2,1,0:T(8,128)(2,1)S(1)} %add_convert_fusion.3), channel_id=1, source_target_pairs={{0,4},{1,3},{4,8},{5,1},{8,12},{9,5},{12,14},{13,9},{14,10},{15,13... | collective-permute-start | bytes 786440 | tf_op jit(solution)/shard_map/ppermute | solution.py:342
  76.9 1.1 %collective-permute-done.29 = bf16[16,64,128]{2,1,0:T(8,128)(2,1)S(1)} collective-permute-done((bf16[16,64,128]{2,1,0:T(8,128)(2,1)S(1)}, bf16[16,64,128]{2,1,0:T(8,128)(2,1)S(1)}, u32[]{:S(2)}, u32[]{:S(2)}) %collective-permute-start.29) | collective-permute-done | bytes 262176 | tf_op jit(solution)/shard_map/ppermute | solution.py:342
  78.2 1.6 %collective-permute-start.30 = (bf16[16,64,128]{2,1,0:T(8,128)(2,1)S(1)}, bf16[16,64,128]{2,1,0:T(8,128)(2,1)S(1)}, u32[]{:S(2)}, u32[]{:S(2)}) collective-permute-start(bf16[16,64,128]{2,1,0:T(8,128)(2,1)S(1)} %add_convert_fusion.2), channel_id=1, source_target_pairs={{0,4},{1,3},{4,8},{5,1},{8,12},{9,5},{12,14},{13,9},{14,10},{15,13... | collective-permute-start | bytes 786440 | tf_op jit(solution)/shard_map/ppermute | solution.py:342
  79.8 2.5 %far.1 = f32[16,64,128]{2,1,0:T(8,128)S(1)} custom-call(bf16[512,128]{1,0:T(8,128)(2,1)S(1)} %constant_dynamic-update-slice_fusion.2.refs_0_, bf16[512,128]{1,0:T(8,128)(2,1)S(1)} %collective-permute-done.19.refs_1_, bf16[512,128]{1,0:T(8,128)(2,1)S(1)} %collective-permute-done.20.refs_2_, bf16[512,128]{1,0:T(8,128)(2,1)S(1)} %collective-permute-done.21.refs_3_, ...), custom_call_target="tpu_custom_call" | custom-call | flops 536870912 | bytes 8388608 | tf_op jit(solution)/shard_map/far/pallas_call | solution.py:435
  82.4 1.0 %collective-permute-start.32 = (bf16[16,64,128]{2,1,0:T(8,128)(2,1)S(1)}, bf16[16,64,128]{2,1,0:T(8,128)(2,1)S(1)}, u32[]{:S(2)}, u32[]{:S(2)}) collective-permute-start(bf16[16,64,128]{2,1,0:T(8,128)(2,1)S(1)} %add_convert_fusion.1), channel_id=1, source_target_pairs={{0,4},{1,3},{4,8},{5,1},{8,12},{9,5},{12,14},{13,9},{14,10},{15,13... | collective-permute-start | bytes 786440 | tf_op jit(solution)/shard_map/ppermute | solution.py:342
  83.4 1.1 %collective-permute-done.30 = bf16[16,64,128]{2,1,0:T(8,128)(2,1)S(1)} collective-permute-done((bf16[16,64,128]{2,1,0:T(8,128)(2,1)S(1)}, bf16[16,64,128]{2,1,0:T(8,128)(2,1)S(1)}, u32[]{:S(2)}, u32[]{:S(2)}) %collective-permute-start.30) | collective-permute-done | bytes 262176 | tf_op jit(solution)/shard_map/ppermute | solution.py:342
  84.6 4.2 %collective-permute-done.32 = bf16[16,64,128]{2,1,0:T(8,128)(2,1)S(1)} collective-permute-done((bf16[16,64,128]{2,1,0:T(8,128)(2,1)S(1)}, bf16[16,64,128]{2,1,0:T(8,128)(2,1)S(1)}, u32[]{:S(2)}, u32[]{:S(2)}) %collective-permute-start.32) | collective-permute-done | bytes 262176 | tf_op jit(solution)/shard_map/ppermute | solution.py:342
  (63 shorter events, 8.5 us)
Async XLA Ops:
  0.0 9.0 %collective-permute-start.1 = (bf16[16,64,128]{2,1,0:T(8,128)(2,1)}, bf16[16,64,128]{2,1,0:T(8,128)(2,1)S(1)}, u32[]{:S(2)}, u32[]{:S(2)}) collective-permute-start(bf16[16,64,128]{2,1,0:T(8,128)(2,1)} %rhs_ref.1), channel_id=1, source_target_pairs={{0,4},{1,3},{4,8},{5,1},{8,12},{9,5},{12,14},{13,9},{14,10},{15,13... | collective-permute-start | bytes 786440 | tf_op jit(solution)/shard_map/ppermute | solution.py:342
  3.0 13.1 %collective-permute-start.2 = (bf16[16,64,128]{2,1,0:T(8,128)(2,1)}, bf16[16,64,128]{2,1,0:T(8,128)(2,1)S(1)}, u32[]{:S(2)}, u32[]{:S(2)}) collective-permute-start(bf16[16,64,128]{2,1,0:T(8,128)(2,1)} %rhs_ref.1), channel_id=1, source_target_pairs={{0,3},{1,4},{4,1},{5,8},{8,5},{9,12},{12,9},{13,14},{14,13},{15,10... | collective-permute-start | bytes 786440 | tf_op jit(solution)/shard_map/ppermute | solution.py:342
  9.0 9.5 %collective-permute-start.4 = (bf16[16,64,128]{2,1,0:T(8,128)(2,1)S(1)}, bf16[16,64,128]{2,1,0:T(8,128)(2,1)S(1)}, u32[]{:S(2)}, u32[]{:S(2)}) collective-permute-start(bf16[16,64,128]{2,1,0:T(8,128)(2,1)S(1)} %collective-permute-done.1.rest_2_), channel_id=1, source_target_pairs={{0,4},{1,3},{4,8},{5,1},{8,12},{9,5},{12,14},{13,9},{14,10},{15,13... | collective-permute-start | bytes 786440 | tf_op jit(solution)/shard_map/ppermute | solution.py:342
  11.4 7.2 %collective-permute-start.5 = (bf16[16,64,128]{2,1,0:T(8,128)(2,1)S(1)}, bf16[16,64,128]{2,1,0:T(8,128)(2,1)S(1)}, u32[]{:S(2)}, u32[]{:S(2)}) collective-permute-start(bf16[16,64,128]{2,1,0:T(8,128)(2,1)S(1)} %collective-permute-done.1.rest_2_), channel_id=1, source_target_pairs={{0,1},{1,0},{2,3},{3,2},{4,5},{5,4},{6,7},{7,6},{8,9},{9,8},{10,11... | collective-permute-start | bytes 786440 | tf_op jit(solution)/shard_map/ppermute | solution.py:342
  11.4 4.7 %collective-permute-start.3 = (bf16[128,128]{1,0:T(8,128)(2,1)}, bf16[128,128]{1,0:T(8,128)(2,1)S(1)}, u32[]{:S(2)}, u32[]{:S(2)}) collective-permute-start(bf16[128,128]{1,0:T(8,128)(2,1)} %get-tuple-element.38), channel_id=1, source_target_pairs={{0,4},{1,5},{2,6},{3,7},{4,0},{5,1},{6,2},{7,3},{8,12},{9,13},{10,... | collective-permute-start | bytes 98312 | tf_op jit(solution)/shard_map/ppermute | solution.py:342
  16.1 10.5 %collective-permute-start.6 = (bf16[16,64,128]{2,1,0:T(8,128)(2,1)S(1)}, bf16[16,64,128]{2,1,0:T(8,128)(2,1)S(1)}, u32[]{:S(2)}, u32[]{:S(2)}) collective-permute-start(bf16[16,64,128]{2,1,0:T(8,128)(2,1)S(1)} %collective-permute-done.2.rest_3_), channel_id=1, source_target_pairs={{0,4},{1,3},{4,8},{5,1},{8,12},{9,5},{12,14},{13,9},{14,10},{15,13... | collective-permute-start | bytes 786440 | tf_op jit(solution)/shard_map/ppermute | solution.py:342
  18.6 8.1 %collective-permute-start.7 = (bf16[16,64,128]{2,1,0:T(8,128)(2,1)S(1)}, bf16[16,64,128]{2,1,0:T(8,128)(2,1)S(1)}, u32[]{:S(2)}, u32[]{:S(2)}) collective-permute-start(bf16[16,64,128]{2,1,0:T(8,128)(2,1)S(1)} %collective-permute-done.2.rest_3_), channel_id=1, source_target_pairs={{0,1},{1,0},{2,3},{3,2},{4,5},{5,4},{6,7},{7,6},{8,9},{9,8},{10,11... | collective-permute-start | bytes 786440 | tf_op jit(solution)/shard_map/ppermute | solution.py:342
  18.6 10.4 %collective-permute-start.9 = (bf16[16,64,128]{2,1,0:T(8,128)(2,1)S(1)}, bf16[16,64,128]{2,1,0:T(8,128)(2,1)S(1)}, u32[]{:S(2)}, u32[]{:S(2)}) collective-permute-start(bf16[16,64,128]{2,1,0:T(8,128)(2,1)S(1)} %collective-permute-done.4.rest_4_), channel_id=1, source_target_pairs={{0,4},{1,3},{4,8},{5,1},{8,12},{9,5},{12,14},{13,9},{14,10},{15,13... | collective-permute-start | bytes 786440 | tf_op jit(solution)/shard_map/ppermute | solution.py:342
  19.5 9.5 %collective-permute-start.10 = (bf16[16,64,128]{2,1,0:T(8,128)(2,1)S(1)}, bf16[16,64,128]{2,1,0:T(8,128)(2,1)S(1)}, u32[]{:S(2)}, u32[]{:S(2)}) collective-permute-start(bf16[16,64,128]{2,1,0:T(8,128)(2,1)S(1)} %collective-permute-done.4.rest_4_), channel_id=1, source_target_pairs={{0,1},{1,0},{2,3},{3,2},{4,5},{5,4},{6,7},{7,6},{8,9},{9,8},{10,11... | collective-permute-start | bytes 786440 | tf_op jit(solution)/shard_map/ppermute | solution.py:342
  19.8 6.9 %collective-permute-start.8 = (bf16[256,128]{1,0:T(8,128)(2,1)S(1)}, bf16[256,128]{1,0:T(8,128)(2,1)S(1)}, u32[]{:S(2)}, u32[]{:S(2)}) collective-permute-start(bf16[256,128]{1,0:T(8,128)(2,1)S(1)} %get-tuple-element.70), channel_id=1, source_target_pairs={{0,8},{1,9},{2,10},{3,11},{4,12},{5,13},{6,14},{7,15},{8,0},{9,1},... | collective-permute-start | bytes 196616 | tf_op jit(solution)/shard_map/ppermute | solution.py:342
  26.7 9.0 %collective-permute-start.11 = (bf16[16,64,128]{2,1,0:T(8,128)(2,1)S(1)}, bf16[16,64,128]{2,1,0:T(8,128)(2,1)S(1)}, u32[]{:S(2)}, u32[]{:S(2)}) collective-permute-start(bf16[16,64,128]{2,1,0:T(8,128)(2,1)S(1)} %collective-permute-done.6.rest_5_), channel_id=1, source_target_pairs={{0,4},{1,3},{4,8},{5,1},{8,12},{9,5},{12,14},{13,9},{14,10},{15,13... | collective-permute-start | bytes 786440 | tf_op jit(solution)/shard_map/ppermute | solution.py:342
  29.0 6.7 %collective-permute-start.12 = (bf16[16,64,128]{2,1,0:T(8,128)(2,1)S(1)}, bf16[16,64,128]{2,1,0:T(8,128)(2,1)S(1)}, u32[]{:S(2)}, u32[]{:S(2)}) collective-permute-start(bf16[16,64,128]{2,1,0:T(8,128)(2,1)S(1)} %collective-permute-done.6.rest_5_), channel_id=1, source_target_pairs={{0,1},{1,0},{2,3},{3,2},{4,5},{5,4},{6,7},{7,6},{8,9},{9,8},{10,11... | collective-permute-start | bytes 786440 | tf_op jit(solution)/shard_map/ppermute | solution.py:342
  29.0 9.5 %collective-permute-start.13 = (bf16[16,64,128]{2,1,0:T(8,128)(2,1)S(1)}, bf16[16,64,128]{2,1,0:T(8,128)(2,1)S(1)}, u32[]{:S(2)}, u32[]{:S(2)}) collective-permute-start(bf16[16,64,128]{2,1,0:T(8,128)(2,1)S(1)} %collective-permute-done.9.rest_6_), channel_id=1, source_target_pairs={{0,4},{1,3},{4,8},{5,1},{8,12},{9,5},{12,14},{13,9},{14,10},{15,13... | collective-permute-start | bytes 786440 | tf_op jit(solution)/shard_map/ppermute | solution.py:342
  30.9 7.6 %collective-permute-start.14 = (bf16[16,64,128]{2,1,0:T(8,128)(2,1)S(1)}, bf16[16,64,128]{2,1,0:T(8,128)(2,1)S(1)}, u32[]{:S(2)}, u32[]{:S(2)}) collective-permute-start(bf16[16,64,128]{2,1,0:T(8,128)(2,1)S(1)} %collective-permute-done.9.rest_6_), channel_id=1, source_target_pairs={{0,1},{1,0},{2,3},{3,2},{4,5},{5,4},{6,7},{7,6},{8,9},{9,8},{10,11... | collective-permute-start | bytes 786440 | tf_op jit(solution)/shard_map/ppermute | solution.py:342
  31.6 6.9 %collective-permute-start = (bf16[16,64,128]{2,1,0:T(8,128)(2,1)}, bf16[16,64,128]{2,1,0:T(8,128)(2,1)S(1)}, u32[]{:S(2)}, u32[]{:S(2)}) collective-permute-start(bf16[16,64,128]{2,1,0:T(8,128)(2,1)} %rhs_ref.1), channel_id=1, source_target_pairs={{0,1},{1,0},{2,3},{3,2},{4,5},{5,4},{6,7},{7,6},{8,9},{9,8},{10,11... | collective-permute-start | bytes 786440 | tf_op jit(solution)/shard_map/ppermute | solution.py:342
  35.7 2.8 %collective-permute-start.16 = (bf16[16,64,128]{2,1,0:T(8,128)(2,1)S(1)}, bf16[16,64,128]{2,1,0:T(8,128)(2,1)S(1)}, u32[]{:S(2)}, u32[]{:S(2)}) collective-permute-start(bf16[16,64,128]{2,1,0:T(8,128)(2,1)S(1)} %collective-permute-done.11.rest_7_), channel_id=1, source_target_pairs={{0,1},{1,0},{2,3},{3,2},{4,5},{5,4},{6,7},{7,6},{8,9},{9,8},{10,11... | collective-permute-start | bytes 786440 | tf_op jit(solution)/shard_map/ppermute | solution.py:342
  46.8 3.0 %collective-permute-start.18 = (bf16[16,64,128]{2,1,0:T(8,128)(2,1)S(1)}, bf16[16,64,128]{2,1,0:T(8,128)(2,1)S(1)}, u32[]{:S(2)}, u32[]{:S(2)}) collective-permute-start(bf16[16,64,128]{2,1,0:T(8,128)(2,1)S(1)} %get-tuple-element.48), channel_id=1, source_target_pairs={{0,1},{1,0},{2,3},{3,2},{4,5},{5,4},{6,7},{7,6},{8,9},{9,8},{10,11... | collective-permute-start | bytes 786440 | tf_op jit(solution)/shard_map/ppermute | solution.py:342
  47.0 2.8 %collective-permute-start.17 = (bf16[16,64,128]{2,1,0:T(8,128)(2,1)S(1)}, bf16[16,64,128]{2,1,0:T(8,128)(2,1)S(1)}, u32[]{:S(2)}, u32[]{:S(2)}) collective-permute-start(bf16[16,64,128]{2,1,0:T(8,128)(2,1)S(1)} %get-tuple-element.47), channel_id=1, source_target_pairs={{0,1},{1,0},{2,3},{3,2},{4,5},{5,4},{6,7},{7,6},{8,9},{9,8},{10,11... | collective-permute-start | bytes 786440 | tf_op jit(solution)/shard_map/ppermute | solution.py:342
  47.4 6.4 %collective-permute-start.19 = (bf16[512,128]{1,0:T(8,128)(2,1)S(1)}, bf16[512,128]{1,0:T(8,128)(2,1)S(1)}, u32[]{:S(2)}, u32[]{:S(2)}) collective-permute-start(bf16[512,128]{1,0:T(8,128)(2,1)S(1)} %constant_dynamic-update-slice_fusion.2.refs_0_), channel_id=1, source_target_pairs={{0,2},{1,3},{2,0},{3,1},{4,6},{5,7},{6,4},{7,5},{8,10},{9,11},{10,... | collective-permute-start | bytes 393224 | tf_op jit(solution)/shard_map/ppermute | solution.py:342
  61.8 9.9 %collective-permute-start.27 = (bf16[64,64,128]{2,1,0:T(8,128)(2,1)S(1)}, bf16[64,64,128]{2,1,0:T(8,128)(2,1)S(1)}, u32[]{:S(2)}, u32[]{:S(2)}) collective-permute-start(bf16[64,64,128]{2,1,0:T(8,128)(2,1)S(1)} %get-tuple-element.58), channel_id=1, source_target_pairs={{0,1},{1,0},{2,3},{3,2},{4,5},{5,4},{6,7},{7,6},{8,9},{9,8},{10,11... | collective-permute-start | bytes 3145736 | tf_op jit(solution)/shard_map/ppermute | solution.py:342
  61.8 3.0 %collective-permute-start.23 = (bf16[16,64,128]{2,1,0:T(8,128)(2,1)S(1)}, bf16[16,64,128]{2,1,0:T(8,128)(2,1)S(1)}, u32[]{:S(2)}, u32[]{:S(2)}) collective-permute-start(bf16[16,64,128]{2,1,0:T(8,128)(2,1)S(1)} %get-tuple-element.54), channel_id=1, source_target_pairs={{0,1},{1,0},{2,3},{3,2},{4,5},{5,4},{6,7},{7,6},{8,9},{9,8},{10,11... | collective-permute-start | bytes 786440 | tf_op jit(solution)/shard_map/ppermute | solution.py:342
  62.3 6.4 %collective-permute-start.22 = (bf16[16,64,128]{2,1,0:T(8,128)(2,1)S(1)}, bf16[16,64,128]{2,1,0:T(8,128)(2,1)S(1)}, u32[]{:S(2)}, u32[]{:S(2)}) collective-permute-start(bf16[16,64,128]{2,1,0:T(8,128)(2,1)S(1)} %get-tuple-element.53), channel_id=1, source_target_pairs={{0,4},{1,3},{4,8},{5,1},{8,12},{9,5},{12,14},{13,9},{14,10},{15,13... | collective-permute-start | bytes 786440 | tf_op jit(solution)/shard_map/ppermute | solution.py:342
  63.9 6.5 %collective-permute-start.26 = (bf16[16,64,128]{2,1,0:T(8,128)(2,1)S(1)}, bf16[16,64,128]{2,1,0:T(8,128)(2,1)S(1)}, u32[]{:S(2)}, u32[]{:S(2)}) collective-permute-start(bf16[16,64,128]{2,1,0:T(8,128)(2,1)S(1)} %get-tuple-element.57), channel_id=1, source_target_pairs={{0,1},{1,0},{2,3},{3,2},{4,5},{5,4},{6,7},{7,6},{8,9},{9,8},{10,11... | collective-permute-start | bytes 786440 | tf_op jit(solution)/shard_map/ppermute | solution.py:342
  63.9 7.6 %collective-permute-start.25 = (bf16[16,64,128]{2,1,0:T(8,128)(2,1)S(1)}, bf16[16,64,128]{2,1,0:T(8,128)(2,1)S(1)}, u32[]{:S(2)}, u32[]{:S(2)}) collective-permute-start(bf16[16,64,128]{2,1,0:T(8,128)(2,1)S(1)} %get-tuple-element.56), channel_id=1, source_target_pairs={{0,4},{1,3},{4,8},{5,1},{8,12},{9,5},{12,14},{13,9},{14,10},{15,13... | collective-permute-start | bytes 786440 | tf_op jit(solution)/shard_map/ppermute | solution.py:342
  68.8 6.4 %collective-permute-start.24 = (bf16[16,64,128]{2,1,0:T(8,128)(2,1)S(1)}, bf16[16,64,128]{2,1,0:T(8,128)(2,1)S(1)}, u32[]{:S(2)}, u32[]{:S(2)}) collective-permute-start(bf16[16,64,128]{2,1,0:T(8,128)(2,1)S(1)} %add_convert_fusion.5), channel_id=1, source_target_pairs={{0,4},{1,3},{4,8},{5,1},{8,12},{9,5},{12,14},{13,9},{14,10},{15,13... | collective-permute-start | bytes 786440 | tf_op jit(solution)/shard_map/ppermute | solution.py:342
  71.6 6.4 %collective-permute-start.29 = (bf16[16,64,128]{2,1,0:T(8,128)(2,1)S(1)}, bf16[16,64,128]{2,1,0:T(8,128)(2,1)S(1)}, u32[]{:S(2)}, u32[]{:S(2)}) collective-permute-start(bf16[16,64,128]{2,1,0:T(8,128)(2,1)S(1)} %add_convert_fusion.4), channel_id=1, source_target_pairs={{0,4},{1,3},{4,8},{5,1},{8,12},{9,5},{12,14},{13,9},{14,10},{15,13... | collective-permute-start | bytes 786440 | tf_op jit(solution)/shard_map/ppermute | solution.py:342
  73.2 6.5 %collective-permute-start.20 = (bf16[512,128]{1,0:T(8,128)(2,1)S(1)}, bf16[512,128]{1,0:T(8,128)(2,1)S(1)}, u32[]{:S(2)}, u32[]{:S(2)}) collective-permute-start(bf16[512,128]{1,0:T(8,128)(2,1)S(1)} %constant_dynamic-update-slice_fusion.2.refs_0_), channel_id=1, source_target_pairs={{0,1},{1,0},{2,3},{3,2},{4,5},{5,4},{6,7},{7,6},{8,9},{9,8},{10,11... | collective-permute-start | bytes 393224 | tf_op jit(solution)/shard_map/ppermute | solution.py:342
  73.3 6.4 %collective-permute-start.21 = (bf16[512,128]{1,0:T(8,128)(2,1)S(1)}, bf16[512,128]{1,0:T(8,128)(2,1)S(1)}, u32[]{:S(2)}, u32[]{:S(2)}) collective-permute-start(bf16[512,128]{1,0:T(8,128)(2,1)S(1)} %collective-permute-done.19.refs_1_), channel_id=1, source_target_pairs={{0,1},{1,0},{2,3},{3,2},{4,5},{5,4},{6,7},{7,6},{8,9},{9,8},{10,11... | collective-permute-start | bytes 393224 | tf_op jit(solution)/shard_map/ppermute | solution.py:342
  75.3 6.9 %collective-permute-start.28 = (bf16[16,64,128]{2,1,0:T(8,128)(2,1)S(1)}, bf16[16,64,128]{2,1,0:T(8,128)(2,1)S(1)}, u32[]{:S(2)}, u32[]{:S(2)}) collective-permute-start(bf16[16,64,128]{2,1,0:T(8,128)(2,1)S(1)} %add_convert_fusion.3), channel_id=1, source_target_pairs={{0,4},{1,3},{4,8},{5,1},{8,12},{9,5},{12,14},{13,9},{14,10},{15,13... | collective-permute-start | bytes 786440 | tf_op jit(solution)/shard_map/ppermute | solution.py:342
  78.2 6.4 %collective-permute-start.30 = (bf16[16,64,128]{2,1,0:T(8,128)(2,1)S(1)}, bf16[16,64,128]{2,1,0:T(8,128)(2,1)S(1)}, u32[]{:S(2)}, u32[]{:S(2)}) collective-permute-start(bf16[16,64,128]{2,1,0:T(8,128)(2,1)S(1)} %add_convert_fusion.2), channel_id=1, source_target_pairs={{0,4},{1,3},{4,8},{5,1},{8,12},{9,5},{12,14},{13,9},{14,10},{15,13... | collective-permute-start | bytes 786440 | tf_op jit(solution)/shard_map/ppermute | solution.py:342
  82.4 6.4 %collective-permute-start.32 = (bf16[16,64,128]{2,1,0:T(8,128)(2,1)S(1)}, bf16[16,64,128]{2,1,0:T(8,128)(2,1)S(1)}, u32[]{:S(2)}, u32[]{:S(2)}) collective-permute-start(bf16[16,64,128]{2,1,0:T(8,128)(2,1)S(1)} %add_convert_fusion.1), channel_id=1, source_target_pairs={{0,4},{1,3},{4,8},{5,1},{8,12},{9,5},{12,14},{13,9},{14,10},{15,13... | collective-permute-start | bytes 786440 | tf_op jit(solution)/shard_map/ppermute | solution.py:342
  84.6 4.2 %collective-permute-start.31 = (bf16[16,64,128]{2,1,0:T(8,128)(2,1)S(1)}, bf16[16,64,128]{2,1,0:T(8,128)(2,1)S(1)}, u32[]{:S(2)}, u32[]{:S(2)}) collective-permute-start(bf16[16,64,128]{2,1,0:T(8,128)(2,1)S(1)} %collective-permute-done.30), channel_id=1, source_target_pairs={{0,1},{1,0},{2,3},{3,2},{4,5},{5,4},{6,7},{7,6},{8,9},{9,8},{10,11... | collective-permute-start | bytes 786440 | tf_op jit(solution)/shard_map/ppermute | solution.py:342
  (8 other events, 78.2 us)

commit v5 on v4

--- a/solution.py
+++ b/solution.py
@@ -7,8 +7,7 @@
 from jax.experimental.pallas import tpu as pltpu
 from jax.sharding import PartitionSpec as P
 
-DENSE_BYTES = 16 << 20
-NEAR_VMEM = 46 << 20
+NEAR_VMEM = 16 << 20
 FAR_VMEM = 16 << 20
 
 
@@ -116,12 +115,14 @@
 
 
 def prologue_kernel(
-    count, me_ref, owner_ref, slot_ref, offset_ref, rhs_ref, basis_ref, coef_ref, copy_ref, list_ref
+    count, me_ref, own_ref, mate_ref, rhs_ref, basis_ref, blocks_ref, *outs
 ):
     clusters = rhs_ref.shape[0]
     rank_k = basis_ref.shape[1]
-    stored = owner_ref.shape[1]
     half = clusters // 2
+    coef_ref, copy_ref, list_ref, held_ref, sem = outs
+    hold = pltpu.make_async_copy(blocks_ref, held_ref, sem)
+    hold.start()
     copy_ref[...] = rhs_ref[...]
     rows = []
     for c in range(half):
@@ -139,89 +140,70 @@
         [row[q : q + 1] for q in range(rank_k) for row in rows], axis=0
     ).astype(coef_ref.dtype)
 
-    me, owner, slot = me_ref[0], owner_ref[...], slot_ref[...]
-    chips = count // 2
-    depth = chips // 2
-    handler, steps, other = scatter_place(owner, me, count)
-    early = steps >= depth - 1
-    shard_at = jnp.where(
-        early,
-        jnp.where(steps == depth, 0, 2 - other),
-        jnp.where(steps == 0, 2 * (depth - 2), 2 * (depth - 2 - steps) + 1 - other),
-    )
-    shard_at = shard_at + jnp.where(handler == (me & 1), 0, jnp.where(early, 3, 2 * depth - 3))
-    column = (owner * clusters + slot + offset_ref[...]) & (count * clusters - 1)
-    column_slot = gather_slot(column // clusters, me, count)
-    column_row = column_slot * clusters + (column & (clusters - 1))
+    lists = [ordered_blocks(ref[...], me_ref[0], count, clusters) for ref in (own_ref, mate_ref)]
+    list_ref[...] = jnp.concatenate(lists, axis=0).astype(jnp.int32)
+    hold.wait()
+
+
+def ordered_blocks(labels, me, count, clusters):
+    stored = labels.shape[1]
+    owner, slot, offset = labels[0:1], labels[1:2], labels[2:3]
+    place = scatter_place(owner, me, count) * clusters + slot
+    column = (owner * clusters + slot + offset) & (count * clusters - 1)
+    shard = gather_place(column // clusters, me, count).astype(jnp.float32)
     square = (stored, stored)
-    group = jnp.broadcast_to(jnp.where(early, 0.0, 1.0), square)
-    group_of_row = jnp.transpose(group)
+    shard = jnp.broadcast_to(shard, square)
+    shard_of_row = jnp.transpose(shard)
     row_at = lax.broadcasted_iota(jnp.int32, square, 0)
     lane_at = lax.broadcasted_iota(jnp.int32, square, 1)
-    before = (group_of_row < group) | ((group_of_row == group) & (row_at < lane_at))
+    lane = lane_at.astype(jnp.float32)
+    before = (shard_of_row < shard) | ((shard_of_row == shard) & (row_at < lane_at))
     rank = jnp.sum(jnp.where(before, 1.0, 0.0), axis=0, keepdims=True)
     rank = jnp.transpose(jnp.broadcast_to(rank, square))
-    here = jnp.where(rank == lane_at.astype(jnp.float32), 1.0, 0.0).astype(jnp.bfloat16)
-    first = stored - jnp.sum(group[0:1], axis=1, keepdims=True)
+    here = jnp.where(rank == lane, 1.0, 0.0).astype(jnp.bfloat16)
+    starts = jnp.sum(jnp.where(shard_of_row < lane, 1.0, 0.0), axis=0, keepdims=True)
     values = jnp.concatenate(
-        [
-            lane_at[0:1].astype(jnp.float32),
-            (shard_at * clusters + slot).astype(jnp.float32),
-            column_row.astype(jnp.float32),
-            jnp.broadcast_to(first, (1, stored)),
-            jnp.zeros((4, stored), jnp.float32),
-        ],
+        [lane[0:1], place.astype(jnp.float32), (column & (clusters - 1)).astype(jnp.float32)]
+        + [jnp.zeros((5, stored), jnp.float32)],
         axis=0,
     )
-    ordered = jnp.dot(values.astype(jnp.bfloat16), here, preferred_element_type=jnp.float32)
-    list_ref[...] = ordered.astype(jnp.int32)
-
-
-def near_kernel(late, batch, count, list_ref, *rest):
-    shards, blocks_hbm, rest = rest[:count], rest[count], rest[count + 1 :]
-    sends, (keep_ref, columns, blocks, acc, sems) = rest[:-5], rest[-5:]
-    directions, unknowns = acc.shape[1:]
-    load = pltpu.make_async_copy(blocks_hbm, blocks, sems.at[len(shards)])
-    load.start()
-    copies = [
-        pltpu.make_async_copy(shard, columns.at[k], sems.at[k]) for k, shard in enumerate(shards)
-    ]
-    for copy in copies:
-        copy.start()
-    acc[...] = jnp.zeros_like(acc)
-    for copy in copies:
-        copy.wait()
-    load.wait()
-    begin = list_ref[3, 0] if late else 0
-    end = blocks.shape[0] if late else list_ref[3, 0]
-    last = blocks.shape[0] - 1
-    dummy = acc.shape[0] - 1
-
-    def body(step, carry):
-        first = begin + step * batch
-        products = []
-        for k in range(batch):
-            at = jnp.minimum(first + k, last)
-            row = list_ref[2, at]
-            products.append(
-                lax.dot_general(
-                    columns[row // columns.shape[1], row % columns.shape[1]],
-                    blocks[list_ref[0, at]],
-                    (((1,), (1,)), ((), ())),
-                    preferred_element_type=jnp.float32,
+    values = jnp.dot(values.astype(jnp.bfloat16), here, preferred_element_type=jnp.float32)
+    return jnp.concatenate([values[0:3], starts], axis=0)
+
+
+def near_kernel(k, batch, sends, list_ref, column_ref, own_ref, mate_ref, *rest):
+    sum_ref = rest[-1 - sends]
+    if k == 0:
+        sum_ref[...] = jnp.zeros_like(sum_ref)
+    last = own_ref.shape[0] - 1
+    dummy = sum_ref.shape[0] - 1
+    for base, blocks_ref in ((0, own_ref), (4, mate_ref)):
+        begin, end = list_ref[base + 3, k], list_ref[base + 3, k + 1]
+
+        def body(step, carry, base=base, blocks_ref=blocks_ref, begin=begin, end=end):
+            first = begin + step * batch
+            products = []
+            for i in range(batch):
+                at = jnp.minimum(first + i, last)
+                products.append(
+                    lax.dot_general(
+                        column_ref[list_ref[base + 2, at]],
+                        blocks_ref[list_ref[base, at]],
+                        (((1,), (1,)), ((), ())),
+                        preferred_element_type=jnp.float32,
+                    )
                 )
-            )
-        for k in range(batch):
-            at = jnp.where(first + k < end, list_ref[1, jnp.minimum(first + k, last)], dummy)
-            acc[at] = acc[at] + products[k]
-        return carry
-
-    lax.fori_loop(0, (end - begin + batch - 1) // batch, body, 0)
-    at = keep_ref.shape[0]
-    keep_ref[...] = acc[0:at]
-    for send_ref in sends:
+            for i in range(batch):
+                at = jnp.minimum(first + i, last)
+                at = jnp.where(first + i < end, list_ref[base + 1, at], dummy)
+                sum_ref[at] = sum_ref[at] + products[i]
+            return carry
+
+        lax.fori_loop(0, (end - begin + batch - 1) // batch, body, 0)
+    at = dummy // 2
+    for send_ref in rest[len(rest) - sends :]:
         size = send_ref.shape[0]
-        send_ref[...] = acc[at : at + size].astype(send_ref.dtype)
+        send_ref[...] = sum_ref[at : at + size].astype(send_ref.dtype)
         at += size
 
 
@@ -295,20 +277,29 @@
     return jnp.where(y == 0, z, chips - 1 - z)
 
 
-def gather_slot(device, me, count):
+def gather_place(device, me, count):
     chips = count // 2
+    depth = chips // 2
     back = (1 - 2 * (me & 1)) * (ring_place(me, chips) - ring_place(device, chips))
-    return 2 * ((back + chips) % chips) + ((device ^ me) & 1)
+    back = (back + chips) & (chips - 1)
+    other = (device ^ me) & 1
+    here = (back < depth) & (back > 0) | ((back & (depth - 1)) == 0) & (other == 0)
+    return jnp.where(here, jnp.where(back == 0, 0, 2 * back - 1 + other), chips)
 
 
 def scatter_place(device, me, count):
     chips = count // 2
-    half = chips // 2
-    ahead = (ring_place(device, chips) - ring_place(me, chips) + chips) % chips
+    depth = chips // 2
+    ahead = (ring_place(device, chips) - ring_place(me, chips) + chips) & (chips - 1)
     core = device & 1
-    handler = jnp.where(ahead % half == 0, core, (ahead > half).astype(jnp.int32))
-    steps = jnp.where(handler == 0, ahead, (chips - ahead) % chips)
-    return handler, steps, core ^ handler
+    handler = jnp.where((ahead & (depth - 1)) == 0, core, (ahead > depth).astype(jnp.int32))
+    steps = jnp.where(handler == 0, ahead, (chips - ahead) & (chips - 1))
+    place = jnp.where(
+        steps == depth,
+        0,
+        jnp.where(steps == 0, chips - 1, 2 * (depth - steps) - (core ^ handler)),
+    )
+    return place + jnp.where(handler == (me & 1), 0, chips)
 
 
 def stationary(
@@ -333,7 +324,6 @@
     stored = near_blocks.shape[0]
     pairs = far_slot.shape[0]
     half = clusters // 2
-    assert stored == unknowns and 2 * directions == unknowns
     ahead, cross = ring_pairs(count)
     mate = [(i, i ^ 1) for i in range(count)]
     side = [(i, i ^ 2) for i in range(count)]
@@ -344,94 +334,93 @@
     def after(values, *others):
         return lax.optimization_barrier((values, *others))[0]
 
+    def after(values, *others):
+        return lax.optimization_barrier((values, *others))[0]
+
     flow = [move(rhs, ahead), move(rhs, cross)]
+    labels = jnp.stack([near_owner[:, 0], near_slot, near_offset], axis=0)
+    mate_labels = move(labels, mate)
+    mate_blocks = move(near_blocks, mate)
     here = me.astype(jnp.int32).reshape(1)
-    coef, here_rhs, lists = pl.pallas_call(
+    coef, here_rhs, lists, own_blocks = pl.pallas_call(
         functools.partial(prologue_kernel, count),
         out_shape=[
             jax.ShapeDtypeStruct((half * rank_k, unknowns), jnp.bfloat16),
             jax.ShapeDtypeStruct(rhs.shape, rhs.dtype),
             jax.ShapeDtypeStruct((8, stored), jnp.int32),
+            jax.ShapeDtypeStruct(near_blocks.shape, near_blocks.dtype),
         ],
-        in_specs=[whole(pltpu.SMEM)] + [whole()] * 5,
-        out_specs=[whole()] * 3,
+        in_specs=[whole(pltpu.SMEM)] + [whole()] * 4 + [whole(pl.ANY)],
+        out_specs=[whole()] * 4,
+        scratch_shapes=[pltpu.SemaphoreType.DMA],
         name="prologue",
-    )(
-        here,
-        near_owner.reshape(1, stored),
-        near_slot.reshape(1, stored),
-        near_offset.reshape(1, stored),
-        rhs,
-        basis_in,
-    )
-    slots = {0: here_rhs, 1: move(rhs, mate)}
-    coefs, level = coef, 1
-    waits = [[coef, here_rhs, lists], []]
-    for t in range(1, depth + 1):
-        for x in range(2 if t < depth else 1):
-            flow[x] = after(flow[x], *waits[x])
-            slots[2 * t + x] = flow[x]
-            opposite = 2 * (chips - t) + 1 - x
-            if t + x < depth:
-                moving = move(flow[x], ahead)
-            slots[opposite] = move(flow[x], mate)
-            waits[x] = [slots[opposite]]
-            if t + x < depth:
-                flow[x] = moving
-            if x == 0 and level < depth:
-                got = move(coefs, [(i, i ^ (4 * level)) for i in range(count)])
-                coefs, level = jnp.concatenate([coefs, got], axis=0), 2 * level
-                waits[1].append(coefs)
-    coefs = [coefs, move(coefs, side)]
-    couple = jnp.transpose(far_coupling, (2, 1, 0))
-
-    def near(late, lists):
-        parts = [1, 2 * depth - 4] if late else [1, 1, 1]
-        size = sum(parts) * clusters
-        *sends, kept = pl.pallas_call(
-            functools.partial(near_kernel, late, 4, count),
-            out_shape=[
+    )(here, labels, mate_labels, rhs, basis_in, near_blocks)
+    got = move(coef, [(i, i ^ 4) for i in range(count)])
+
+    pieces = [1, 1, chips - 2]
+
+    def near(k, shard, sums):
+        sends = pieces if k == chips - 1 else []
+        sum_shape = jax.ShapeDtypeStruct((count * clusters + 1, directions, unknowns), jnp.float32)
+        return pl.pallas_call(
+            functools.partial(near_kernel, k, 4, len(sends)),
+            out_shape=[sum_shape]
+            + [
                 jax.ShapeDtypeStruct((part * clusters, directions, unknowns), jnp.bfloat16)
-                for part in parts
-            ]
-            + [jax.ShapeDtypeStruct((size, directions, unknowns), jnp.float32)],
-            in_specs=[whole(pltpu.SMEM)] + [whole(pl.ANY)] * (count + 1),
-            out_specs=[whole()] * (len(parts) + 1),
-            scratch_shapes=[
-                pltpu.VMEM((count, clusters, directions, unknowns), jnp.bfloat16),
-                pltpu.VMEM(near_blocks.shape, jnp.bfloat16),
-                pltpu.VMEM((2 * size + 1, directions, unknowns), jnp.float32),
-                pltpu.SemaphoreType.DMA((count + 1,)),
+                for part in sends
             ],
+            in_specs=[whole(pltpu.SMEM)] + [whole()] * (3 + len(sums)),
+            out_specs=[whole()] * (1 + len(sends)),
+            input_output_aliases={4: 0} if sums else {},
             compiler_params=pltpu.CompilerParams(vmem_limit_bytes=NEAR_VMEM),
             cost_estimate=pl.CostEstimate(
-                flops=2 * stored * directions * unknowns * unknowns * 8,
-                bytes_accessed=12 << 20,
+                flops=2 * stored * directions * unknowns * unknowns,
+                bytes_accessed=2 << 20,
                 transcendentals=0,
             ),
             name="near",
-        )(lists, *[slots[k] for k in range(count)], near_blocks)
-        return [move(send, mate) for send in sends], kept
-
-    own, mates = [None, None], [None, None]
-
-    def term(late, k):
-        part, skip = (min(k, 1), min(k, 1)) if late else (k, k)
-        at = slice(k * clusters, (k + 1) * clusters)
-        got = mates[late][part][(k - skip) * clusters : (k - skip + 1) * clusters]
-        return own[late][at] + got.astype(jnp.float32)
-
-    def add(flow, late, k, *others):
-        step = (flow.astype(jnp.float32) + term(late, k)).astype(jnp.bfloat16)
-        step, mates[late], *_ = lax.optimization_barrier((step, mates[late], *others))
-        return step
-
-    mates[0], own[0] = near(False, lists)
-    flow = [term(0, 0).astype(jnp.bfloat16), term(0, 1).astype(jnp.bfloat16)]
-    *flow, lists, coefs[0], coefs[1] = lax.optimization_barrier((*flow, lists, *coefs))
+        )(lists, shard, own_blocks, mate_blocks, *sums)
+
+    sums, passed = near(0, here_rhs, []), None
+    waits = [coef, here_rhs, lists]
+    for k in range(1, chips):
+        x = 1 - k % 2
+        shard = after(flow[x], *waits)
+        if k < chips - 2:
+            flow[x] = move(shard, ahead)
+        waits = [sums[0], got] if k == depth else [sums[0]]
+        sums = near(k, shard, sums)
+    sums, *sends = sums
+    couple = jnp.transpose(far_coupling, (2, 1, 0))
+
+    mates = [move(part, mate) for part in sends]
+
+    def term(k):
+        part = min(k, 2)
+        got = mates[part][(k - part) * clusters : (k - part + 1) * clusters]
+        return sums[k * clusters : (k + 1) * clusters] + got.astype(jnp.float32)
+
+    def tied(values, *others):
+        values, mates[2], *others = lax.optimization_barrier((values, mates[2], *others))
+        return values, *others
+
+    def add(flow, k):
+        return (flow.astype(jnp.float32) + term(k)).astype(jnp.bfloat16)
+
+    flow = [term(0).astype(jnp.bfloat16), term(1).astype(jnp.bfloat16)]
+    *flow, coef, got = lax.optimization_barrier((*flow, coef, got))
     flow = [move(part, ahead) for part in flow]
-    coefs = coefs + [move(part, mate) for part in coefs]
-    mates[1], own[1] = near(True, lists)
+    coefs = jnp.concatenate([coef, got], axis=0)
+    got = move(coefs, [(i, i ^ 8) for i in range(count)])
+    flow[0] = move(tied(add(flow[0], 2))[0], ahead)
+    flow[1], coefs, got = tied(add(flow[1], 3), coefs, got)
+    flow[1] = move(flow[1], ahead)
+    coefs = jnp.concatenate([coefs, got], axis=0)
+    got = move(coefs, side)
+    flow[0], coefs, got = tied(add(flow[0], 4), coefs, got)
+    flow[0] = move(flow[0], ahead)
+    coefs = [coefs, got, move(coefs, mate), move(got, mate)]
+    flow[1] = move(tied(add(flow[1], 5))[0], ahead)
     far = pl.pallas_call(
         far_kernel,
         out_shape=jax.ShapeDtypeStruct((clusters, directions, unknowns), jnp.float32),
@@ -453,26 +442,17 @@
         far_cslot.reshape(1, pairs),
         basis_out,
     )
-    for t in range(depth - 1, 0, -1):
-        if t == depth - 1:
-            flow[0] = add(flow[0], 0, 2)
-        elif t > 1:
-            flow[0] = add(flow[0], 1, 2 * (depth - 2 - t) + 1)
-        else:
-            flow[0] = add(flow[0], 1, 2 * (depth - 2 - t) + 1, far)
-        flow[0] = move(flow[0], ahead)
-        if t > 1:
-            flow[1] = move(add(flow[1], 1, 2 * (depth - 1 - t)), ahead)
-        else:
-            flow[1] = move(flow[1], mate)
-    total = far + term(1, 2 * (depth - 2)) + flow[1].astype(jnp.float32)
+    flow[0] = move(tied(add(flow[0], 6), far)[0], ahead)
+    flow[1] = move(flow[1], mate)
+    total = far + term(chips - 1) + flow[1].astype(jnp.float32)
     return (total + flow[0].astype(jnp.float32)).astype(jnp.bfloat16)
 
 
 def on_device(*args):
-    rhs = args[0]
-    count = lax.axis_size("blk")
-    if count % 4 == 0 and count >= 16 and count * rhs.size * 4 <= DENSE_BYTES:
+    rhs, near_blocks = args[0], args[1]
+    clusters, directions, unknowns = rhs.shape
+    small = lax.axis_size("blk") == 16 and clusters == 16
+    if small and near_blocks.shape[0] == unknowns and 2 * directions == unknowns:
         return stationary(*args)
     return routed(*args)
 

time: 89.8 us -> 92.7 us (1.032)
  Pallas kernels: 17.5 us -> 34 us
  waiting for transfers between devices: 36.3 us -> 25.2 us
  starting transfers between devices: 31.7 us -> 26.1 us
  local copies, waits for them, and re-layouts: 2.52 us -> 4.5 us
    pallas_call x2 -> x8, Pallas kernels: 13.1 us -> 26.2 us  [near(): pl.pallas_call(functools.partial(near_kernel, k, 4, len(sends)), out_shap...]
    ppermute x33 -> x25, waiting for transfers between devices: 36.3 us -> 25.2 us  [move(): return lax.ppermute(values, 'blk', where)]
    ppermute x33 -> x25, starting transfers between devices: 31.7 us -> 26.1 us  [move(): return lax.ppermute(values, 'blk', where)]
    pallas_call x1, Pallas kernels: 1.98 us -> 5.33 us  [stationary(): pl.pallas_call(functools.partial(prologue_kernel, count), out_shape=[jax....]
    unnamed x17 -> x27, local copies, waits for them, and re-layouts: 2.5 us -> 4.48 us
  transfers between devices with their start and end apart: 33 -> 25, of which waited for: 14 -> 12; matrix products, arithmetic and copies ran while one was open for 2% -> 2% of each run, Pallas kernels for 5% -> 30%
where the time goes in v5:
time: 92.7 us; the launch traced here: 92.3 us
  Pallas kernels  34 us (37%)
  starting transfers between devices  26.1 us (28%)
  waiting for transfers between devices  25.2 us (27%)
  local copies, waits for them, and re-layouts  4.5 us (5%)
  other arithmetic  2.28 us (2%)
    pallas_call x8, Pallas kernels, near(): pl.pallas_call(functools.partial(near_kernel, k, 4, len(sends)), out_shap...  26.2 us
    ppermute x25, starting transfers between devices, move(): return lax.ppermute(values, 'blk', where)  26.1 us
    ppermute x25, waiting for transfers between devices, move(): return lax.ppermute(values, 'blk', where)  25.2 us
    pallas_call x1, Pallas kernels, stationary(): pl.pallas_call(functools.partial(prologue_kernel, count), out_shape=[jax....  5.33 us
    unnamed x27, local copies, waits for them, and re-layouts  4.48 us
    pallas_call x1, Pallas kernels, stationary(): pl.pallas_call(far_kernel, out_shape=jax.ShapeDtypeStruct((clusters, dire...  2.49 us
  transfers between devices with their start and end apart: 25, of which 12 were waited for; matrix products, arithmetic and copies ran while one was open for 2% of the time, Pallas kernels for 30%

profile of v5, /device:TPU:0, one launch (start us, length us, event | category | flops | bytes accessed | tf_op | source)
XLA Modules:
  0.0 92.3 jit_solution(3192643597652214333)
XLA Ops:
  0.5 2.6 %collective-permute-start.1 = (bf16[16,64,128]{2,1,0:T(8,128)(2,1)}, bf16[16,64,128]{2,1,0:T(8,128)(2,1)S(1)}, u32[]{:S(2)}, u32[]{:S(2)}) collective-permute-start(bf16[16,64,128]{2,1,0:T(8,128)(2,1)} %rhs_ref.1), channel_id=1, source_target_pairs={{0,4},{1,3},{4,8},{5,1},{8,12},{9,5},{12,14},{13,9},{14,10},{15,13... | collective-permute-start | bytes 786440 | tf_op jit(solution)/shard_map/ppermute | solution.py:332
  3.0 1.4 %collective-permute-start.5 = (bf16[16,64,128]{2,1,0:T(8,128)(2,1)}, bf16[16,64,128]{2,1,0:T(8,128)(2,1)S(1)}, u32[]{:S(2)}, u32[]{:S(2)}) collective-permute-start(bf16[16,64,128]{2,1,0:T(8,128)(2,1)} %rhs_ref.1), channel_id=1, source_target_pairs={{0,3},{1,4},{4,1},{5,8},{8,5},{9,12},{12,9},{13,14},{14,13},{15,10... | collective-permute-start | bytes 786440 | tf_op jit(solution)/shard_map/ppermute | solution.py:332
  4.4 0.7 pad_add_fusion.own_ref
  5.5 1.8 %collective-permute-done.mate_ref = s32[3,128]{1,0:T(4,128)S(1)} collective-permute-done((s32[3,128]{1,0:T(4,128)S(1)}, s32[3,128]{1,0:T(4,128)S(1)}, u32[]{:S(2)}, u32[]{:S(2)}) %collective-permute-start) | collective-permute-done | bytes 1568 | tf_op jit(solution)/shard_map/ppermute | solution.py:332
  7.8 5.3 %prologue.1 = (bf16[128,128]{1,0:T(8,128)(2,1)}, bf16[16,64,128]{2,1,0:T(8,128)(2,1)}, s32[8,128]{1,0:T(8,128)}, bf16[128,128,128]{2,1,0:T(8,128)(2,1)}) custom-call(s32[1]{0:T(128)} %bitcast.me_ref.refs_4_, s32[3,128]{1,0:T(4,128)} %copy-done.10, s32[3,128]{1,0:T(4,128)} %copy-done.11, bf16[16,64,128]{2,1,0:T(8,128)(2,1)} %rhs_ref.1, ...), custom_call_target="tpu_custom_call" | custom-call | tf_op jit(solution)/shard_map/prologue/pallas_call | solution.py:345
  13.2 3.0 %collective-permute-start.2 = (bf16[16,64,128]{2,1,0:T(8,128)(2,1)S(1)}, bf16[16,64,128]{2,1,0:T(8,128)(2,1)S(1)}, u32[]{:S(2)}, u32[]{:S(2)}) collective-permute-start(bf16[16,64,128]{2,1,0:T(8,128)(2,1)S(1)} %collective-permute-done.1.column_ref), channel_id=1, source_target_pairs={{0,4},{1,3},{4,8},{5,1},{8,12},{9,5},{12,14},{13,9},{14,10},{15,13... | collective-permute-start | bytes 786440 | tf_op jit(solution)/shard_map/ppermute | solution.py:332
  16.2 2.2 %copy-done = bf16[128,128,128]{2,1,0:T(8,128)(2,1)S(1)} copy-done((bf16[128,128,128]{2,1,0:T(8,128)(2,1)S(1)}, bf16[128,128,128]{2,1,0:T(8,128)(2,1)}, u32[]{:S(2)}) %copy-start) | copy-done | bytes 4194328
  18.4 0.9 %copy-done.2 = bf16[16,64,128]{2,1,0:T(8,128)(2,1)S(1)} copy-done((bf16[16,64,128]{2,1,0:T(8,128)(2,1)S(1)}, bf16[16,64,128]{2,1,0:T(8,128)(2,1)}, u32[]{:S(2)}) %copy-start.2) | copy-done | bytes 262168
  20.0 3.7 %near.8.rest_0_ = f32[257,64,128]{2,1,0:T(8,128)S(1)} custom-call(s32[8,128]{1,0:T(8,128)S(1)} %copy-done.3, bf16[16,64,128]{2,1,0:T(8,128)(2,1)S(1)} %copy-done.2, bf16[128,128,128]{2,1,0:T(8,128)(2,1)S(1)} %copy-done, bf16[128,128,128]{2,1,0:T(8,128)(2,1)} %collective-permute-done.3.mate_ref), custom_call_target="tpu_custom_call" | custom-call | flops 268435456 | bytes 2097152 | tf_op jit(solution)/shard_map/near/pallas_call | solution.py:365
  23.7 1.8 %collective-permute-start.8 = (bf16[16,64,128]{2,1,0:T(8,128)(2,1)S(1)}, bf16[16,64,128]{2,1,0:T(8,128)(2,1)S(1)}, u32[]{:S(2)}, u32[]{:S(2)}) collective-permute-start(bf16[16,64,128]{2,1,0:T(8,128)(2,1)S(1)} %collective-permute-done.5.column_ref), channel_id=1, source_target_pairs={{0,4},{1,3},{4,8},{5,1},{8,12},{9,5},{12,14},{13,9},{14,10},{15,13... | collective-permute-start | bytes 786440 | tf_op jit(solution)/shard_map/ppermute | solution.py:332
  25.6 3.3 %near.9.rest_0_ = f32[257,64,128]{2,1,0:T(8,128)S(1)} custom-call(s32[8,128]{1,0:T(8,128)S(1)} %copy-done.3, bf16[16,64,128]{2,1,0:T(8,128)(2,1)S(1)} %collective-permute-done.1.column_ref, bf16[128,128,128]{2,1,0:T(8,128)(2,1)S(1)} %copy-done.1, bf16[128,128,128]{2,1,0:T(8,128)(2,1)} %collective-permute-done.3.mate_ref, ...), custom_call_target="tpu_custom_call", output_to_operand_aliasing={{}: (4, {})} | custom-call | flops 268435456 | bytes 2097152 | tf_op jit(solution)/shard_map/near/pallas_call | solution.py:365
  28.8 1.4 %collective-permute-start.4 = (bf16[16,64,128]{2,1,0:T(8,128)(2,1)S(1)}, bf16[16,64,128]{2,1,0:T(8,128)(2,1)S(1)}, u32[]{:S(2)}, u32[]{:S(2)}) collective-permute-start(bf16[16,64,128]{2,1,0:T(8,128)(2,1)S(1)} %collective-permute-done.2.column_ref), channel_id=1, source_target_pairs={{0,4},{1,3},{4,8},{5,1},{8,12},{9,5},{12,14},{13,9},{14,10},{15,13... | collective-permute-start | bytes 786440 | tf_op jit(solution)/shard_map/ppermute | solution.py:332
  30.3 2.1 %collective-permute-start.6 = (bf16[128,128]{1,0:T(8,128)(2,1)S(1)}, bf16[128,128]{1,0:T(8,128)(2,1)S(1)}, u32[]{:S(2)}, u32[]{:S(2)}) collective-permute-start(bf16[128,128]{1,0:T(8,128)(2,1)S(1)} %copy-done.9), channel_id=1, source_target_pairs={{0,4},{1,5},{2,6},{3,7},{4,0},{5,1},{6,2},{7,3},{8,12},{9,13},{10,... | collective-permute-start | bytes 98312 | tf_op jit(solution)/shard_map/ppermute | solution.py:332
  32.4 3.2 %near.10.rest_0_ = f32[257,64,128]{2,1,0:T(8,128)S(1)} custom-call(s32[8,128]{1,0:T(8,128)S(1)} %copy-done.3, bf16[16,64,128]{2,1,0:T(8,128)(2,1)S(1)} %collective-permute-done.5.column_ref, bf16[128,128,128]{2,1,0:T(8,128)(2,1)S(1)} %copy-done.1, bf16[128,128,128]{2,1,0:T(8,128)(2,1)} %collective-permute-done.3.mate_ref, ...), custom_call_target="tpu_custom_call", output_to_operand_aliasing={{}: (4, {})} | custom-call | flops 268435456 | bytes 2097152 | tf_op jit(solution)/shard_map/near/pallas_call | solution.py:365
  35.9 3.2 %near.11.rest_0_ = f32[257,64,128]{2,1,0:T(8,128)S(1)} custom-call(s32[8,128]{1,0:T(8,128)S(1)} %copy-done.3, bf16[16,64,128]{2,1,0:T(8,128)(2,1)S(1)} %collective-permute-done.2.column_ref, bf16[128,128,128]{2,1,0:T(8,128)(2,1)S(1)} %copy-done.1, bf16[128,128,128]{2,1,0:T(8,128)(2,1)} %collective-permute-done.3.mate_ref, ...), custom_call_target="tpu_custom_call", output_to_operand_aliasing={{}: (4, {})} | custom-call | flops 268435456 | bytes 2097152 | tf_op jit(solution)/shard_map/near/pallas_call | solution.py:365
  39.7 3.3 %near.12.rest_0_ = f32[257,64,128]{2,1,0:T(8,128)S(1)} custom-call(s32[8,128]{1,0:T(8,128)S(1)} %copy-done.3, bf16[16,64,128]{2,1,0:T(8,128)(2,1)S(1)} %collective-permute-done.8.column_ref, bf16[128,128,128]{2,1,0:T(8,128)(2,1)S(1)} %copy-done.1, bf16[128,128,128]{2,1,0:T(8,128)(2,1)} %collective-permute-done.3.mate_ref, ...), custom_call_target="tpu_custom_call", output_to_operand_aliasing={{}: (4, {})} | custom-call | flops 268435456 | bytes 2097152 | tf_op jit(solution)/shard_map/near/pallas_call | solution.py:365
  43.0 3.5 %near.13.rest_0_ = f32[257,64,128]{2,1,0:T(8,128)S(1)} custom-call(s32[8,128]{1,0:T(8,128)S(1)} %copy-done.3, bf16[16,64,128]{2,1,0:T(8,128)(2,1)S(1)} %collective-permute-done.4.column_ref, bf16[128,128,128]{2,1,0:T(8,128)(2,1)S(1)} %copy-done.1, bf16[128,128,128]{2,1,0:T(8,128)(2,1)} %collective-permute-done.3.mate_ref, ...), custom_call_target="tpu_custom_call", output_to_operand_aliasing={{}: (4, {})} | custom-call | flops 268435456 | bytes 2097152 | tf_op jit(solution)/shard_map/near/pallas_call | solution.py:365
  46.5 2.6 %near.14.rest_0_ = f32[257,64,128]{2,1,0:T(8,128)S(1)} custom-call(s32[8,128]{1,0:T(8,128)S(1)} %copy-done.3, bf16[16,64,128]{2,1,0:T(8,128)(2,1)S(1)} %collective-permute-done.9.column_ref, bf16[128,128,128]{2,1,0:T(8,128)(2,1)S(1)} %copy-done.1, bf16[128,128,128]{2,1,0:T(8,128)(2,1)} %collective-permute-done.3.mate_ref, ...), custom_call_target="tpu_custom_call", output_to_operand_aliasing={{}: (4, {})} | custom-call | flops 268435456 | bytes 2097152 | tf_op jit(solution)/shard_map/near/pallas_call | solution.py:365
  49.2 3.3 %near.15 = (f32[257,64,128]{2,1,0:T(8,128)S(1)}, bf16[16,64,128]{2,1,0:T(8,128)(2,1)S(1)}, bf16[16,64,128]{2,1,0:T(8,128)(2,1)S(1)}, bf16[96,64,128]{2,1,0:T(8,128)(2,1)S(1)}) custom-call(s32[8,128]{1,0:T(8,128)S(1)} %copy-done.3, bf16[16,64,128]{2,1,0:T(8,128)(2,1)S(1)} %collective-permute-done.7.column_ref, ...), custom_call_target="tpu_custom_call", output_to_operand_aliasing={{0}: (4, {})} | custom-call | flops 268435456 | bytes 2097152 | tf_op jit(solution)/shard_map/near/pallas_call | solution.py:365
  53.2 3.2 %collective-permute-done.10 = bf16[16,64,128]{2,1,0:T(8,128)(2,1)S(1)} collective-permute-done((bf16[16,64,128]{2,1,0:T(8,128)(2,1)S(1)}, bf16[16,64,128]{2,1,0:T(8,128)(2,1)S(1)}, u32[]{:S(2)}, u32[]{:S(2)}) %collective-permute-start.10) | collective-permute-done | bytes 262176 | tf_op jit(solution)/shard_map/ppermute | solution.py:332
  56.9 2.3 %collective-permute-start.12 = (bf16[16,64,128]{2,1,0:T(8,128)(2,1)S(1)}, bf16[16,64,128]{2,1,0:T(8,128)(2,1)S(1)}, u32[]{:S(2)}, u32[]{:S(2)}) collective-permute-start(bf16[16,64,128]{2,1,0:T(8,128)(2,1)S(1)} %get-tuple-element.52), channel_id=1, source_target_pairs={{0,4},{1,3},{4,8},{5,1},{8,12},{9,5},{12,14},{13,9},{14,10},{15,13... | collective-permute-start | bytes 786440 | tf_op jit(solution)/shard_map/ppermute | solution.py:332
  59.3 1.4 %collective-permute-start.16 = (bf16[256,128]{1,0:T(8,128)(2,1)S(1)}, bf16[256,128]{1,0:T(8,128)(2,1)S(1)}, u32[]{:S(2)}, u32[]{:S(2)}) collective-permute-start(bf16[256,128]{1,0:T(8,128)(2,1)S(1)} %constant_dynamic-update-slice_fusion), channel_id=1, source_target_pairs={{0,8},{1,9},{2,10},{3,11},{4,12},{5,13},{6,14},{7,15},{8,0},{9,1},... | collective-permute-start | bytes 196616 | tf_op jit(solution)/shard_map/ppermute | solution.py:332
  60.7 3.1 %collective-permute-done.12 = bf16[16,64,128]{2,1,0:T(8,128)(2,1)S(1)} collective-permute-done((bf16[16,64,128]{2,1,0:T(8,128)(2,1)S(1)}, bf16[16,64,128]{2,1,0:T(8,128)(2,1)S(1)}, u32[]{:S(2)}, u32[]{:S(2)}) %collective-permute-start.12) | collective-permute-done | bytes 262176 | tf_op jit(solution)/shard_map/ppermute | solution.py:332
  63.9 2.5 %collective-permute-start.14 = (bf16[16,64,128]{2,1,0:T(8,128)(2,1)S(1)}, bf16[16,64,128]{2,1,0:T(8,128)(2,1)S(1)}, u32[]{:S(2)}, u32[]{:S(2)}) collective-permute-start(bf16[16,64,128]{2,1,0:T(8,128)(2,1)S(1)} %add_convert_fusion.5), channel_id=1, source_target_pairs={{0,4},{1,3},{4,8},{5,1},{8,12},{9,5},{12,14},{13,9},{14,10},{15,13... | collective-permute-start | bytes 786440 | tf_op jit(solution)/shard_map/ppermute | solution.py:332
  67.3 2.0 %collective-permute-start.21 = (bf16[16,64,128]{2,1,0:T(8,128)(2,1)S(1)}, bf16[16,64,128]{2,1,0:T(8,128)(2,1)S(1)}, u32[]{:S(2)}, u32[]{:S(2)}) collective-permute-start(bf16[16,64,128]{2,1,0:T(8,128)(2,1)S(1)} %add_convert_fusion.4), channel_id=1, source_target_pairs={{0,4},{1,3},{4,8},{5,1},{8,12},{9,5},{12,14},{13,9},{14,10},{15,13... | collective-permute-start | bytes 786440 | tf_op jit(solution)/shard_map/ppermute | solution.py:332
  69.3 2.7 %collective-permute-start.17 = (bf16[512,128]{1,0:T(8,128)(2,1)S(1)}, bf16[512,128]{1,0:T(8,128)(2,1)S(1)}, u32[]{:S(2)}, u32[]{:S(2)}) collective-permute-start(bf16[512,128]{1,0:T(8,128)(2,1)S(1)} %constant_dynamic-update-slice_fusion.2.refs_0_), channel_id=1, source_target_pairs={{0,2},{1,3},{2,0},{3,1},{4,6},{5,7},{6,4},{7,5},{8,10},{9,11},{10,... | collective-permute-start | bytes 393224 | tf_op jit(solution)/shard_map/ppermute | solution.py:332
  72.1 6.0 %collective-permute-done.17.refs_1_ = bf16[512,128]{1,0:T(8,128)(2,1)S(1)} collective-permute-done((bf16[512,128]{1,0:T(8,128)(2,1)S(1)}, bf16[512,128]{1,0:T(8,128)(2,1)S(1)}, u32[]{:S(2)}, u32[]{:S(2)}) %collective-permute-start.17) | collective-permute-done | bytes 131104 | tf_op jit(solution)/shard_map/ppermute | solution.py:332
  79.6 2.5 %far.1 = f32[16,64,128]{2,1,0:T(8,128)S(1)} custom-call(bf16[512,128]{1,0:T(8,128)(2,1)S(1)} %constant_dynamic-update-slice_fusion.2.refs_0_, bf16[512,128]{1,0:T(8,128)(2,1)S(1)} %collective-permute-done.17.refs_1_, bf16[512,128]{1,0:T(8,128)(2,1)S(1)} %collective-permute-done.18.refs_2_, bf16[512,128]{1,0:T(8,128)(2,1)S(1)} %collective-permute-done.19.refs_3_, ...), custom_call_target="tpu_custom_call" | custom-call | flops 536870912 | bytes 8388608 | tf_op jit(solution)/shard_map/far/pallas_call | solution.py:424
  82.1 2.8 %collective-permute-done.20 = bf16[16,64,128]{2,1,0:T(8,128)(2,1)S(1)} collective-permute-done((bf16[16,64,128]{2,1,0:T(8,128)(2,1)S(1)}, bf16[16,64,128]{2,1,0:T(8,128)(2,1)S(1)}, u32[]{:S(2)}, u32[]{:S(2)}) %collective-permute-start.20) | collective-permute-done | bytes 262176 | tf_op jit(solution)/shard_map/ppermute | solution.py:332
  85.1 2.6 %collective-permute-done.22 = bf16[16,64,128]{2,1,0:T(8,128)(2,1)S(1)} collective-permute-done((bf16[16,64,128]{2,1,0:T(8,128)(2,1)S(1)}, bf16[16,64,128]{2,1,0:T(8,128)(2,1)S(1)}, u32[]{:S(2)}, u32[]{:S(2)}) %collective-permute-start.22) | collective-permute-done | bytes 262176 | tf_op jit(solution)/shard_map/ppermute | solution.py:332
  87.7 3.7 %collective-permute-done.24 = bf16[16,64,128]{2,1,0:T(8,128)(2,1)S(1)} collective-permute-done((bf16[16,64,128]{2,1,0:T(8,128)(2,1)S(1)}, bf16[16,64,128]{2,1,0:T(8,128)(2,1)S(1)}, u32[]{:S(2)}, u32[]{:S(2)}) %collective-permute-start.24) | collective-permute-done | bytes 262176 | tf_op jit(solution)/shard_map/ppermute | solution.py:332
  91.4 0.9 add_convert_fusion
  (65 shorter events, 7.1 us)
Async XLA Ops:
  0.0 16.2 %collective-permute-start.3 = (bf16[128,128,128]{2,1,0:T(8,128)(2,1)}, bf16[128,128,128]{2,1,0:T(8,128)(2,1)}, u32[]{:S(2)}, u32[]{:S(2)}) collective-permute-start(bf16[128,128,128]{2,1,0:T(8,128)(2,1)} %blocks_ref.1), channel_id=1, source_target_pairs={{0,1},{1,0},{2,3},{3,2},{4,5},{5,4},{6,7},{7,6},{8,9},{9,8},{10,11... | collective-permute-start | bytes 12582920 | tf_op jit(solution)/shard_map/ppermute | solution.py:332
  0.5 12.7 %collective-permute-start.1 = (bf16[16,64,128]{2,1,0:T(8,128)(2,1)}, bf16[16,64,128]{2,1,0:T(8,128)(2,1)S(1)}, u32[]{:S(2)}, u32[]{:S(2)}) collective-permute-start(bf16[16,64,128]{2,1,0:T(8,128)(2,1)} %rhs_ref.1), channel_id=1, source_target_pairs={{0,4},{1,3},{4,8},{5,1},{8,12},{9,5},{12,14},{13,9},{14,10},{15,13... | collective-permute-start | bytes 786440 | tf_op jit(solution)/shard_map/ppermute | solution.py:332
  3.0 20.7 %collective-permute-start.5 = (bf16[16,64,128]{2,1,0:T(8,128)(2,1)}, bf16[16,64,128]{2,1,0:T(8,128)(2,1)S(1)}, u32[]{:S(2)}, u32[]{:S(2)}) collective-permute-start(bf16[16,64,128]{2,1,0:T(8,128)(2,1)} %rhs_ref.1), channel_id=1, source_target_pairs={{0,3},{1,4},{4,1},{5,8},{8,5},{9,12},{12,9},{13,14},{14,13},{15,10... | collective-permute-start | bytes 786440 | tf_op jit(solution)/shard_map/ppermute | solution.py:332
  5.1 2.2 %collective-permute-start = (s32[3,128]{1,0:T(4,128)S(1)}, s32[3,128]{1,0:T(4,128)S(1)}, u32[]{:S(2)}, u32[]{:S(2)}) collective-permute-start(s32[3,128]{1,0:T(4,128)S(1)} %pad_add_fusion.own_ref), channel_id=1, source_target_pairs={{0,1},{1,0},{2,3},{3,2},{4,5},{5,4},{6,7},{7,6},{8,9},{9,8},{10,11... | collective-permute-start | bytes 4616 | tf_op jit(solution)/shard_map/ppermute | solution.py:332
  13.2 15.7 %collective-permute-start.2 = (bf16[16,64,128]{2,1,0:T(8,128)(2,1)S(1)}, bf16[16,64,128]{2,1,0:T(8,128)(2,1)S(1)}, u32[]{:S(2)}, u32[]{:S(2)}) collective-permute-start(bf16[16,64,128]{2,1,0:T(8,128)(2,1)S(1)} %collective-permute-done.1.column_ref), channel_id=1, source_target_pairs={{0,4},{1,3},{4,8},{5,1},{8,12},{9,5},{12,14},{13,9},{14,10},{15,13... | collective-permute-start | bytes 786440 | tf_op jit(solution)/shard_map/ppermute | solution.py:332
  20.0 5.6 %copy-start.1 = (bf16[128,128,128]{2,1,0:T(8,128)(2,1)S(1)}, bf16[128,128,128]{2,1,0:T(8,128)(2,1)}, u32[]{:S(2)}) copy-start(bf16[128,128,128]{2,1,0:T(8,128)(2,1)} %get-tuple-element.42.own_ref) | copy-start | bytes 12582916
  23.7 6.6 %copy-start.9 = (bf16[128,128]{1,0:T(8,128)(2,1)S(1)}, bf16[128,128]{1,0:T(8,128)(2,1)}, u32[]{:S(2)}) copy-start(bf16[128,128]{1,0:T(8,128)(2,1)} %get-tuple-element.57) | copy-start | bytes 98308
  23.7 11.9 %collective-permute-start.8 = (bf16[16,64,128]{2,1,0:T(8,128)(2,1)S(1)}, bf16[16,64,128]{2,1,0:T(8,128)(2,1)S(1)}, u32[]{:S(2)}, u32[]{:S(2)}) collective-permute-start(bf16[16,64,128]{2,1,0:T(8,128)(2,1)S(1)} %collective-permute-done.5.column_ref), channel_id=1, source_target_pairs={{0,4},{1,3},{4,8},{5,1},{8,12},{9,5},{12,14},{13,9},{14,10},{15,13... | collective-permute-start | bytes 786440 | tf_op jit(solution)/shard_map/ppermute | solution.py:332
  28.8 10.4 %collective-permute-start.4 = (bf16[16,64,128]{2,1,0:T(8,128)(2,1)S(1)}, bf16[16,64,128]{2,1,0:T(8,128)(2,1)S(1)}, u32[]{:S(2)}, u32[]{:S(2)}) collective-permute-start(bf16[16,64,128]{2,1,0:T(8,128)(2,1)S(1)} %collective-permute-done.2.column_ref), channel_id=1, source_target_pairs={{0,4},{1,3},{4,8},{5,1},{8,12},{9,5},{12,14},{13,9},{14,10},{15,13... | collective-permute-start | bytes 786440 | tf_op jit(solution)/shard_map/ppermute | solution.py:332
  30.3 8.9 %collective-permute-start.6 = (bf16[128,128]{1,0:T(8,128)(2,1)S(1)}, bf16[128,128]{1,0:T(8,128)(2,1)S(1)}, u32[]{:S(2)}, u32[]{:S(2)}) collective-permute-start(bf16[128,128]{1,0:T(8,128)(2,1)S(1)} %copy-done.9), channel_id=1, source_target_pairs={{0,4},{1,5},{2,6},{3,7},{4,0},{5,1},{6,2},{7,3},{8,12},{9,13},{10,... | collective-permute-start | bytes 98312 | tf_op jit(solution)/shard_map/ppermute | solution.py:332
  35.7 7.3 %collective-permute-start.9 = (bf16[16,64,128]{2,1,0:T(8,128)(2,1)S(1)}, bf16[16,64,128]{2,1,0:T(8,128)(2,1)S(1)}, u32[]{:S(2)}, u32[]{:S(2)}) collective-permute-start(bf16[16,64,128]{2,1,0:T(8,128)(2,1)S(1)} %collective-permute-done.8.column_ref), channel_id=1, source_target_pairs={{0,4},{1,3},{4,8},{5,1},{8,12},{9,5},{12,14},{13,9},{14,10},{15,13... | collective-permute-start | bytes 786440 | tf_op jit(solution)/shard_map/ppermute | solution.py:332
  39.2 7.3 %collective-permute-start.7 = (bf16[16,64,128]{2,1,0:T(8,128)(2,1)S(1)}, bf16[16,64,128]{2,1,0:T(8,128)(2,1)S(1)}, u32[]{:S(2)}, u32[]{:S(2)}) collective-permute-start(bf16[16,64,128]{2,1,0:T(8,128)(2,1)S(1)} %collective-permute-done.4.column_ref), channel_id=1, source_target_pairs={{0,4},{1,3},{4,8},{5,1},{8,12},{9,5},{12,14},{13,9},{14,10},{15,13... | collective-permute-start | bytes 786440 | tf_op jit(solution)/shard_map/ppermute | solution.py:332
  49.1 10.1 %copy-start.8 = (bf16[256,16,16]{0,2,1:T(8,128)(2,1)S(1)}, bf16[256,16,16]{0,2,1:T(8,128)(2,1)}, u32[]{:S(2)}) copy-start(bf16[256,16,16]{0,2,1:T(8,128)(2,1)} %param.16) | copy-start | bytes 393220
  49.1 30.4 %copy-start.4 = (bf16[16,16,128]{2,1,0:T(8,128)(2,1)S(1)}, bf16[16,16,128]{2,1,0:T(8,128)(2,1)}, u32[]{:S(2)}) copy-start(bf16[16,16,128]{2,1,0:T(8,128)(2,1)} %refs_9_.1) | copy-start | bytes 196612
  49.1 30.4 %copy-start.5 = (s32[256]{0:T(256)S(1)}, s32[256]{0:T(256)}, u32[]{:S(2)}) copy-start(s32[256]{0:T(256)} %param.17) | copy-start | bytes 3076
  49.2 30.4 %copy-start.6 = (s32[256,1]{0,1:T(1,128)S(1)}, s32[256,1]{0,1:T(1,128)}, u32[]{:S(2)}) copy-start(s32[256,1]{0,1:T(1,128)} %param.18) | copy-start | bytes 3076
  49.2 30.4 %copy-start.7 = (s32[256]{0:T(256)S(1)}, s32[256]{0:T(256)}, u32[]{:S(2)}) copy-start(s32[256]{0:T(256)} %param.19) | copy-start | bytes 3076
  52.5 11.3 %collective-permute-start.13 = (bf16[96,64,128]{2,1,0:T(8,128)(2,1)S(1)}, bf16[96,64,128]{2,1,0:T(8,128)(2,1)S(1)}, u32[]{:S(2)}, u32[]{:S(2)}) collective-permute-start(bf16[96,64,128]{2,1,0:T(8,128)(2,1)S(1)} %get-tuple-element.53), channel_id=1, source_target_pairs={{0,1},{1,0},{2,3},{3,2},{4,5},{5,4},{6,7},{7,6},{8,9},{9,8},{10,11... | collective-permute-start | bytes 4718600 | tf_op jit(solution)/shard_map/ppermute | solution.py:332
  52.6 3.8 %collective-permute-start.10 = (bf16[16,64,128]{2,1,0:T(8,128)(2,1)S(1)}, bf16[16,64,128]{2,1,0:T(8,128)(2,1)S(1)}, u32[]{:S(2)}, u32[]{:S(2)}) collective-permute-start(bf16[16,64,128]{2,1,0:T(8,128)(2,1)S(1)} %get-tuple-element.50), channel_id=1, source_target_pairs={{0,1},{1,0},{2,3},{3,2},{4,5},{5,4},{6,7},{7,6},{8,9},{9,8},{10,11... | collective-permute-start | bytes 786440 | tf_op jit(solution)/shard_map/ppermute | solution.py:332
  53.1 3.6 %collective-permute-start.11 = (bf16[16,64,128]{2,1,0:T(8,128)(2,1)S(1)}, bf16[16,64,128]{2,1,0:T(8,128)(2,1)S(1)}, u32[]{:S(2)}, u32[]{:S(2)}) collective-permute-start(bf16[16,64,128]{2,1,0:T(8,128)(2,1)S(1)} %get-tuple-element.51), channel_id=1, source_target_pairs={{0,1},{1,0},{2,3},{3,2},{4,5},{5,4},{6,7},{7,6},{8,9},{9,8},{10,11... | collective-permute-start | bytes 786440 | tf_op jit(solution)/shard_map/ppermute | solution.py:332
  56.9 6.9 %collective-permute-start.12 = (bf16[16,64,128]{2,1,0:T(8,128)(2,1)S(1)}, bf16[16,64,128]{2,1,0:T(8,128)(2,1)S(1)}, u32[]{:S(2)}, u32[]{:S(2)}) collective-permute-start(bf16[16,64,128]{2,1,0:T(8,128)(2,1)S(1)} %get-tuple-element.52), channel_id=1, source_target_pairs={{0,4},{1,3},{4,8},{5,1},{8,12},{9,5},{12,14},{13,9},{14,10},{15,13... | collective-permute-start | bytes 786440 | tf_op jit(solution)/shard_map/ppermute | solution.py:332
  59.2 7.4 %collective-permute-start.15 = (bf16[16,64,128]{2,1,0:T(8,128)(2,1)S(1)}, bf16[16,64,128]{2,1,0:T(8,128)(2,1)S(1)}, u32[]{:S(2)}, u32[]{:S(2)}) collective-permute-start(bf16[16,64,128]{2,1,0:T(8,128)(2,1)S(1)} %get-tuple-element.55), channel_id=1, source_target_pairs={{0,4},{1,3},{4,8},{5,1},{8,12},{9,5},{12,14},{13,9},{14,10},{15,13... | collective-permute-start | bytes 786440 | tf_op jit(solution)/shard_map/ppermute | solution.py:332
  59.3 8.0 %collective-permute-start.16 = (bf16[256,128]{1,0:T(8,128)(2,1)S(1)}, bf16[256,128]{1,0:T(8,128)(2,1)S(1)}, u32[]{:S(2)}, u32[]{:S(2)}) collective-permute-start(bf16[256,128]{1,0:T(8,128)(2,1)S(1)} %constant_dynamic-update-slice_fusion), channel_id=1, source_target_pairs={{0,8},{1,9},{2,10},{3,11},{4,12},{5,13},{6,14},{7,15},{8,0},{9,1},... | collective-permute-start | bytes 196616 | tf_op jit(solution)/shard_map/ppermute | solution.py:332
  63.9 8.0 %collective-permute-start.14 = (bf16[16,64,128]{2,1,0:T(8,128)(2,1)S(1)}, bf16[16,64,128]{2,1,0:T(8,128)(2,1)S(1)}, u32[]{:S(2)}, u32[]{:S(2)}) collective-permute-start(bf16[16,64,128]{2,1,0:T(8,128)(2,1)S(1)} %add_convert_fusion.5), channel_id=1, source_target_pairs={{0,4},{1,3},{4,8},{5,1},{8,12},{9,5},{12,14},{13,9},{14,10},{15,13... | collective-permute-start | bytes 786440 | tf_op jit(solution)/shard_map/ppermute | solution.py:332
  67.3 11.2 %collective-permute-start.21 = (bf16[16,64,128]{2,1,0:T(8,128)(2,1)S(1)}, bf16[16,64,128]{2,1,0:T(8,128)(2,1)S(1)}, u32[]{:S(2)}, u32[]{:S(2)}) collective-permute-start(bf16[16,64,128]{2,1,0:T(8,128)(2,1)S(1)} %add_convert_fusion.4), channel_id=1, source_target_pairs={{0,4},{1,3},{4,8},{5,1},{8,12},{9,5},{12,14},{13,9},{14,10},{15,13... | collective-permute-start | bytes 786440 | tf_op jit(solution)/shard_map/ppermute | solution.py:332
  69.3 8.7 %collective-permute-start.17 = (bf16[512,128]{1,0:T(8,128)(2,1)S(1)}, bf16[512,128]{1,0:T(8,128)(2,1)S(1)}, u32[]{:S(2)}, u32[]{:S(2)}) collective-permute-start(bf16[512,128]{1,0:T(8,128)(2,1)S(1)} %constant_dynamic-update-slice_fusion.2.refs_0_), channel_id=1, source_target_pairs={{0,2},{1,3},{2,0},{3,1},{4,6},{5,7},{6,4},{7,5},{8,10},{9,11},{10,... | collective-permute-start | bytes 393224 | tf_op jit(solution)/shard_map/ppermute | solution.py:332
  78.0 1.3 %collective-permute-start.18 = (bf16[512,128]{1,0:T(8,128)(2,1)S(1)}, bf16[512,128]{1,0:T(8,128)(2,1)S(1)}, u32[]{:S(2)}, u32[]{:S(2)}) collective-permute-start(bf16[512,128]{1,0:T(8,128)(2,1)S(1)} %constant_dynamic-update-slice_fusion.2.refs_0_), channel_id=1, source_target_pairs={{0,1},{1,0},{2,3},{3,2},{4,5},{5,4},{6,7},{7,6},{8,9},{9,8},{10,11... | collective-permute-start | bytes 393224 | tf_op jit(solution)/shard_map/ppermute | solution.py:332
  78.0 1.5 %collective-permute-start.19 = (bf16[512,128]{1,0:T(8,128)(2,1)S(1)}, bf16[512,128]{1,0:T(8,128)(2,1)S(1)}, u32[]{:S(2)}, u32[]{:S(2)}) collective-permute-start(bf16[512,128]{1,0:T(8,128)(2,1)S(1)} %collective-permute-done.17.refs_1_), channel_id=1, source_target_pairs={{0,1},{1,0},{2,3},{3,2},{4,5},{5,4},{6,7},{7,6},{8,9},{9,8},{10,11... | collective-permute-start | bytes 393224 | tf_op jit(solution)/shard_map/ppermute | solution.py:332
  78.5 6.4 %collective-permute-start.20 = (bf16[16,64,128]{2,1,0:T(8,128)(2,1)S(1)}, bf16[16,64,128]{2,1,0:T(8,128)(2,1)S(1)}, u32[]{:S(2)}, u32[]{:S(2)}) collective-permute-start(bf16[16,64,128]{2,1,0:T(8,128)(2,1)S(1)} %add_convert_fusion.3), channel_id=1, source_target_pairs={{0,4},{1,3},{4,8},{5,1},{8,12},{9,5},{12,14},{13,9},{14,10},{15,13... | collective-permute-start | bytes 786440 | tf_op jit(solution)/shard_map/ppermute | solution.py:332
  78.7 9.1 %collective-permute-start.22 = (bf16[16,64,128]{2,1,0:T(8,128)(2,1)S(1)}, bf16[16,64,128]{2,1,0:T(8,128)(2,1)S(1)}, u32[]{:S(2)}, u32[]{:S(2)}) collective-permute-start(bf16[16,64,128]{2,1,0:T(8,128)(2,1)S(1)} %add_convert_fusion.2), channel_id=1, source_target_pairs={{0,4},{1,3},{4,8},{5,1},{8,12},{9,5},{12,14},{13,9},{14,10},{15,13... | collective-permute-start | bytes 786440 | tf_op jit(solution)/shard_map/ppermute | solution.py:332
  85.0 6.4 %collective-permute-start.24 = (bf16[16,64,128]{2,1,0:T(8,128)(2,1)S(1)}, bf16[16,64,128]{2,1,0:T(8,128)(2,1)S(1)}, u32[]{:S(2)}, u32[]{:S(2)}) collective-permute-start(bf16[16,64,128]{2,1,0:T(8,128)(2,1)S(1)} %add_convert_fusion.1), channel_id=1, source_target_pairs={{0,4},{1,3},{4,8},{5,1},{8,12},{9,5},{12,14},{13,9},{14,10},{15,13... | collective-permute-start | bytes 786440 | tf_op jit(solution)/shard_map/ppermute | solution.py:332
  87.7 3.7 %collective-permute-start.23 = (bf16[16,64,128]{2,1,0:T(8,128)(2,1)S(1)}, bf16[16,64,128]{2,1,0:T(8,128)(2,1)S(1)}, u32[]{:S(2)}, u32[]{:S(2)}) collective-permute-start(bf16[16,64,128]{2,1,0:T(8,128)(2,1)S(1)} %collective-permute-done.22), channel_id=1, source_target_pairs={{0,1},{1,0},{2,3},{3,2},{4,5},{5,4},{6,7},{7,6},{8,9},{9,8},{10,11... | collective-permute-start | bytes 786440 | tf_op jit(solution)/shard_map/ppermute | solution.py:332
  (5 other events, 6.6 us)

commit v6 on v5

--- a/solution.py
+++ b/solution.py
@@ -7,7 +7,10 @@
 from jax.experimental.pallas import tpu as pltpu
 from jax.sharding import PartitionSpec as P
 
-NEAR_VMEM = 16 << 20
+CHUNKS = 4
+BATCH = 8
+PROLOGUE_VMEM = 16 << 20
+NEAR_VMEM = 44 << 20
 FAR_VMEM = 16 << 20
 
 
@@ -115,15 +118,11 @@
 
 
 def prologue_kernel(
-    count, me_ref, own_ref, mate_ref, rhs_ref, basis_ref, blocks_ref, *outs
+    count, me_ref, owner_ref, slot_ref, offset_ref, rhs_ref, basis_ref, coef_ref, list_ref
 ):
     clusters = rhs_ref.shape[0]
     rank_k = basis_ref.shape[1]
     half = clusters // 2
-    coef_ref, copy_ref, list_ref, held_ref, sem = outs
-    hold = pltpu.make_async_copy(blocks_ref, held_ref, sem)
-    hold.start()
-    copy_ref[...] = rhs_ref[...]
     rows = []
     for c in range(half):
         parts = [
@@ -140,71 +139,114 @@
         [row[q : q + 1] for q in range(rank_k) for row in rows], axis=0
     ).astype(coef_ref.dtype)
 
-    lists = [ordered_blocks(ref[...], me_ref[0], count, clusters) for ref in (own_ref, mate_ref)]
-    list_ref[...] = jnp.concatenate(lists, axis=0).astype(jnp.int32)
-    hold.wait()
-
-
-def ordered_blocks(labels, me, count, clusters):
-    stored = labels.shape[1]
-    owner, slot, offset = labels[0:1], labels[1:2], labels[2:3]
+    me, owner, slot = me_ref[0], owner_ref[...], slot_ref[...]
+    stored = owner.shape[1]
     place = scatter_place(owner, me, count) * clusters + slot
-    column = (owner * clusters + slot + offset) & (count * clusters - 1)
-    shard = gather_place(column // clusters, me, count).astype(jnp.float32)
+    column = (owner * clusters + slot + offset_ref[...]) & (count * clusters - 1)
+    shard = gather_place(column // clusters, me, count)
+    theirs = shard == count // 2
+    shard = jnp.where(theirs, gather_place(column // clusters, me ^ 1, count), shard)
+    column_place = shard * clusters + (column & (clusters - 1))
     square = (stored, stored)
-    shard = jnp.broadcast_to(shard, square)
-    shard_of_row = jnp.transpose(shard)
+    late = jnp.broadcast_to(jnp.where(theirs, 1.0, 0.0), square)
+    late_of_row = jnp.transpose(late)
     row_at = lax.broadcasted_iota(jnp.int32, square, 0)
     lane_at = lax.broadcasted_iota(jnp.int32, square, 1)
     lane = lane_at.astype(jnp.float32)
-    before = (shard_of_row < shard) | ((shard_of_row == shard) & (row_at < lane_at))
+    before = (late_of_row < late) | ((late_of_row == late) & (row_at < lane_at))
     rank = jnp.sum(jnp.where(before, 1.0, 0.0), axis=0, keepdims=True)
     rank = jnp.transpose(jnp.broadcast_to(rank, square))
     here = jnp.where(rank == lane, 1.0, 0.0).astype(jnp.bfloat16)
-    starts = jnp.sum(jnp.where(shard_of_row < lane, 1.0, 0.0), axis=0, keepdims=True)
+    chunk = row_at < lane_at * (stored // CHUNKS)
+    mine = jnp.sum(jnp.where(chunk, 1.0 - late_of_row, 0.0), axis=0, keepdims=True)
+    other = jnp.sum(jnp.where(chunk, late_of_row, 0.0), axis=0, keepdims=True)
+    other = other + (stored - jnp.sum(late[0:1], axis=1, keepdims=True))
     values = jnp.concatenate(
-        [lane[0:1], place.astype(jnp.float32), (column & (clusters - 1)).astype(jnp.float32)]
+        [lane[0:1], place.astype(jnp.float32), column_place.astype(jnp.float32)]
         + [jnp.zeros((5, stored), jnp.float32)],
         axis=0,
     )
     values = jnp.dot(values.astype(jnp.bfloat16), here, preferred_element_type=jnp.float32)
-    return jnp.concatenate([values[0:3], starts], axis=0)
-
-
-def near_kernel(k, batch, sends, list_ref, column_ref, own_ref, mate_ref, *rest):
-    sum_ref = rest[-1 - sends]
-    if k == 0:
-        sum_ref[...] = jnp.zeros_like(sum_ref)
-    last = own_ref.shape[0] - 1
-    dummy = sum_ref.shape[0] - 1
-    for base, blocks_ref in ((0, own_ref), (4, mate_ref)):
-        begin, end = list_ref[base + 3, k], list_ref[base + 3, k + 1]
-
-        def body(step, carry, base=base, blocks_ref=blocks_ref, begin=begin, end=end):
-            first = begin + step * batch
-            products = []
-            for i in range(batch):
-                at = jnp.minimum(first + i, last)
-                products.append(
-                    lax.dot_general(
-                        column_ref[list_ref[base + 2, at]],
-                        blocks_ref[list_ref[base, at]],
-                        (((1,), (1,)), ((), ())),
-                        preferred_element_type=jnp.float32,
+    values = jnp.concatenate([values[0:3], mine, other, values[5:8]], axis=0)
+    list_ref[...] = values.astype(jnp.int32)
+
+
+def near_kernel(batch, shards, sends, list_ref, mate_list_ref, *refs):
+    shard_refs, (own_hbm, mate_hbm) = refs[:shards], refs[shards : shards + 2]
+    keep_ref, refs = refs[shards + 2], refs[shards + 3 :]
+    send_refs, (columns, blocks, sums, column_sem, block_sem) = refs[:sends], refs[sends:]
+    clusters = shard_refs[0].shape[0]
+    chunk = blocks.shape[1] // CHUNKS
+
+    def load(source, half, c):
+        at = pl.ds(c * chunk, chunk)
+        return pltpu.make_async_copy(
+            source.at[at], blocks.at[half, at], block_sem.at[half * CHUNKS + c]
+        )
+
+    copies = [
+        pltpu.make_async_copy(ref, columns.at[pl.ds(k * clusters, clusters)], column_sem.at[k])
+        for k, ref in enumerate(shard_refs)
+    ]
+    for copy in copies:
+        copy.start()
+    for half, source in enumerate((own_hbm, mate_hbm)):
+        for c in range(CHUNKS):
+            load(source, half, c).start()
+
+    dummy = sums.shape[0] - 1
+
+    def clear(i, carry):
+        sums[i] = jnp.zeros(sums.shape[1:], sums.dtype)
+        return carry
+
+    lax.fori_loop(0, dummy, clear, 0)
+    for copy in copies:
+        copy.wait()
+    for half, (source, ref) in enumerate(((own_hbm, list_ref), (mate_hbm, mate_list_ref))):
+        swap = half * (dummy // 2)
+
+        def run(c, carry, half=half, source=source, ref=ref, swap=swap):
+            load(source, half, c).wait()
+            begin, end = ref[3 + half, c], ref[3 + half, c + 1]
+
+            def body(step, carry):
+                first = begin + step * batch
+                products = []
+                for i in range(batch):
+                    at = jnp.minimum(first + i, end - 1)
+                    products.append(
+                        lax.dot_general(
+                            columns[ref[2, at]],
+                            blocks[half, ref[0, at]],
+                            (((1,), (1,)), ((), ())),
+                            preferred_element_type=jnp.float32,
+                        )
                     )
-                )
-            for i in range(batch):
-                at = jnp.minimum(first + i, last)
-                at = jnp.where(first + i < end, list_ref[base + 1, at], dummy)
-                sum_ref[at] = sum_ref[at] + products[i]
+                for i in range(batch):
+                    at = jnp.minimum(first + i, end - 1)
+                    at = jnp.where(first + i < end, ref[1, at] ^ swap, dummy)
+                    sums[at] = sums[at] + products[i]
+                return carry
+
+            return lax.fori_loop(0, (end - begin + batch - 1) // batch, body, carry)
+
+        lax.fori_loop(0, CHUNKS, run, 0)
+
+    def keep(i, carry):
+        keep_ref[i] = sums[i]
+        return carry
+
+    lax.fori_loop(0, dummy // 2, keep, 0, unroll=2)
+    at = dummy // 2
+    for send_ref in send_refs:
+
+        def pack(i, carry, at=at, send_ref=send_ref):
+            send_ref[i] = sums[at + i].astype(send_ref.dtype)
             return carry
 
-        lax.fori_loop(0, (end - begin + batch - 1) // batch, body, 0)
-    at = dummy // 2
-    for send_ref in rest[len(rest) - sends :]:
-        size = send_ref.shape[0]
-        send_ref[...] = sum_ref[at : at + size].astype(send_ref.dtype)
-        at += size
+        lax.fori_loop(0, send_ref.shape[0], pack, 0, unroll=2)
+        at += send_ref.shape[0]
 
 
 def far_kernel(*refs):
@@ -334,93 +376,93 @@
     def after(values, *others):
         return lax.optimization_barrier((values, *others))[0]
 
-    def after(values, *others):
-        return lax.optimization_barrier((values, *others))[0]
-
     flow = [move(rhs, ahead), move(rhs, cross)]
-    labels = jnp.stack([near_owner[:, 0], near_slot, near_offset], axis=0)
-    mate_labels = move(labels, mate)
     mate_blocks = move(near_blocks, mate)
     here = me.astype(jnp.int32).reshape(1)
-    coef, here_rhs, lists, own_blocks = pl.pallas_call(
+    coef, lists = pl.pallas_call(
         functools.partial(prologue_kernel, count),
         out_shape=[
             jax.ShapeDtypeStruct((half * rank_k, unknowns), jnp.bfloat16),
-            jax.ShapeDtypeStruct(rhs.shape, rhs.dtype),
             jax.ShapeDtypeStruct((8, stored), jnp.int32),
-            jax.ShapeDtypeStruct(near_blocks.shape, near_blocks.dtype),
         ],
-        in_specs=[whole(pltpu.SMEM)] + [whole()] * 4 + [whole(pl.ANY)],
-        out_specs=[whole()] * 4,
-        scratch_shapes=[pltpu.SemaphoreType.DMA],
+        in_specs=[whole(pltpu.SMEM)] + [whole()] * 5,
+        out_specs=[whole()] * 2,
+        compiler_params=pltpu.CompilerParams(vmem_limit_bytes=PROLOGUE_VMEM),
         name="prologue",
-    )(here, labels, mate_labels, rhs, basis_in, near_blocks)
+    )(
+        here,
+        near_owner.reshape(1, stored),
+        near_slot.reshape(1, stored),
+        near_offset.reshape(1, stored),
+        rhs,
+        basis_in,
+    )
     got = move(coef, [(i, i ^ 4) for i in range(count)])
-
-    pieces = [1, 1, chips - 2]
-
-    def near(k, shard, sums):
-        sends = pieces if k == chips - 1 else []
-        sum_shape = jax.ShapeDtypeStruct((count * clusters + 1, directions, unknowns), jnp.float32)
-        return pl.pallas_call(
-            functools.partial(near_kernel, k, 4, len(sends)),
-            out_shape=[sum_shape]
-            + [
-                jax.ShapeDtypeStruct((part * clusters, directions, unknowns), jnp.bfloat16)
-                for part in sends
-            ],
-            in_specs=[whole(pltpu.SMEM)] + [whole()] * (3 + len(sums)),
-            out_specs=[whole()] * (1 + len(sends)),
-            input_output_aliases={4: 0} if sums else {},
-            compiler_params=pltpu.CompilerParams(vmem_limit_bytes=NEAR_VMEM),
-            cost_estimate=pl.CostEstimate(
-                flops=2 * stored * directions * unknowns * unknowns,
-                bytes_accessed=2 << 20,
-                transcendentals=0,
-            ),
-            name="near",
-        )(lists, shard, own_blocks, mate_blocks, *sums)
-
-    sums, passed = near(0, here_rhs, []), None
-    waits = [coef, here_rhs, lists]
+    flow[0] = after(flow[0], coef, lists)
+    shards = [rhs]
     for k in range(1, chips):
         x = 1 - k % 2
-        shard = after(flow[x], *waits)
+        if k == 3:
+            flow[x], mate_blocks, lists = lax.optimization_barrier((flow[x], mate_blocks, lists))
+        shards.append(flow[x])
         if k < chips - 2:
-            flow[x] = move(shard, ahead)
-        waits = [sums[0], got] if k == depth else [sums[0]]
-        sums = near(k, shard, sums)
-    sums, *sends = sums
-    couple = jnp.transpose(far_coupling, (2, 1, 0))
+            flow[x] = move(flow[x], ahead)
+        if k == 1:
+            mate_lists = move(lists, mate)
+        if k == 2:
+            coef = jnp.concatenate([coef, after(got, shards[k])], axis=0)
+            got = move(coef, [(i, i ^ 8) for i in range(count)])
+        if k == 3:
+            couple = after(jnp.transpose(far_coupling, (2, 1, 0)), shards[k])
+        if k == 4:
+            coef = jnp.concatenate([coef, after(got, shards[k])], axis=0)
+            got = move(coef, side)
+    coefs = [coef, got, move(coef, mate), move(got, mate)]
+    lists = after(lists, couple, *coefs)
+
+    pieces = [1, 1, chips - 2]
+    kept, *sends = pl.pallas_call(
+        functools.partial(near_kernel, BATCH, chips, len(pieces)),
+        out_shape=[jax.ShapeDtypeStruct((chips * clusters, directions, unknowns), jnp.float32)]
+        + [
+            jax.ShapeDtypeStruct((part * clusters, directions, unknowns), jnp.bfloat16)
+            for part in pieces
+        ],
+        in_specs=[whole(pltpu.SMEM)] * 2 + [whole(pl.ANY)] * (chips + 2),
+        out_specs=[whole()] * (1 + len(pieces)),
+        scratch_shapes=[
+            pltpu.VMEM((chips * clusters, directions, unknowns), jnp.bfloat16),
+            pltpu.VMEM((2, *near_blocks.shape), jnp.bfloat16),
+            pltpu.VMEM((count * clusters + 1, directions, unknowns), jnp.float32),
+            pltpu.SemaphoreType.DMA((chips,)),
+            pltpu.SemaphoreType.DMA((2 * CHUNKS,)),
+        ],
+        compiler_params=pltpu.CompilerParams(vmem_limit_bytes=NEAR_VMEM),
+        cost_estimate=pl.CostEstimate(
+            flops=16 * stored * directions * unknowns * unknowns,
+            bytes_accessed=16 << 20,
+            transcendentals=0,
+        ),
+        name="near",
+    )(lists, mate_lists, *shards, near_blocks, mate_blocks)
 
     mates = [move(part, mate) for part in sends]
 
     def term(k):
         part = min(k, 2)
         got = mates[part][(k - part) * clusters : (k - part + 1) * clusters]
-        return sums[k * clusters : (k + 1) * clusters] + got.astype(jnp.float32)
+        return kept[k * clusters : (k + 1) * clusters] + got.astype(jnp.float32)
 
     def tied(values, *others):
         values, mates[2], *others = lax.optimization_barrier((values, mates[2], *others))
-        return values, *others
+        return values
 
     def add(flow, k):
         return (flow.astype(jnp.float32) + term(k)).astype(jnp.bfloat16)
 
-    flow = [term(0).astype(jnp.bfloat16), term(1).astype(jnp.bfloat16)]
-    *flow, coef, got = lax.optimization_barrier((*flow, coef, got))
+    flow = lax.optimization_barrier([term(0).astype(jnp.bfloat16), term(1).astype(jnp.bfloat16)])
+    couple = after(couple, *flow)
     flow = [move(part, ahead) for part in flow]
-    coefs = jnp.concatenate([coef, got], axis=0)
-    got = move(coefs, [(i, i ^ 8) for i in range(count)])
-    flow[0] = move(tied(add(flow[0], 2))[0], ahead)
-    flow[1], coefs, got = tied(add(flow[1], 3), coefs, got)
-    flow[1] = move(flow[1], ahead)
-    coefs = jnp.concatenate([coefs, got], axis=0)
-    got = move(coefs, side)
-    flow[0], coefs, got = tied(add(flow[0], 4), coefs, got)
-    flow[0] = move(flow[0], ahead)
-    coefs = [coefs, got, move(coefs, mate), move(got, mate)]
-    flow[1] = move(tied(add(flow[1], 5))[0], ahead)
     far = pl.pallas_call(
         far_kernel,
         out_shape=jax.ShapeDtypeStruct((clusters, directions, unknowns), jnp.float32),
@@ -442,7 +484,9 @@
         far_cslot.reshape(1, pairs),
         basis_out,
     )
-    flow[0] = move(tied(add(flow[0], 6), far)[0], ahead)
+    for k in range(2, chips - 1):
+        x = k % 2
+        flow[x] = move(tied(add(flow[x], k), *([far] if k == 2 else [])), ahead)
     flow[1] = move(flow[1], mate)
     total = far + term(chips - 1) + flow[1].astype(jnp.float32)
     return (total + flow[0].astype(jnp.float32)).astype(jnp.bfloat16)

time: 92.7 us -> 80.5 us (0.87)
  Pallas kernels: 34 us -> 12 us
  starting transfers between devices: 26.1 us -> 34.6 us
  local copies, waits for them, and re-layouts: 4.5 us -> 5.76 us
  waiting for transfers between devices: 25.2 us -> 26.4 us
    pallas_call x8 -> x1, Pallas kernels: 26.2 us -> 9.21 us  [stationary(): pl.pallas_call(functools.partial(near_kernel, BATCH, chips, len(pieces)),...]
    ppermute x25, starting transfers between devices: 26.1 us -> 34.6 us  [move(): return lax.ppermute(values, 'blk', where)]
    pallas_call x1, Pallas kernels: 5.33 us -> 0.35 us  [stationary(): pl.pallas_call(functools.partial(prologue_kernel, count), out_shape=[jax....]
    unnamed x27 -> x23, local copies, waits for them, and re-layouts: 4.48 us -> 5.74 us
    ppermute x25, waiting for transfers between devices: 25.2 us -> 26.4 us  [move(): return lax.ppermute(values, 'blk', where)]
  transfers between devices with their start and end apart: 25 -> 25, of which waited for: 12 -> 16; matrix products, arithmetic and copies ran while one was open for 2% -> 2% of each run, Pallas kernels for 30% -> 4%
where the time goes in v6:
time: 80.5 us
  starting transfers between devices  34.6 us (43%)
  waiting for transfers between devices  26.4 us (33%)
  Pallas kernels  12 us (15%)
  local copies, waits for them, and re-layouts  5.76 us (7%)
  other arithmetic  1.59 us (2%)
    ppermute x25, starting transfers between devices, move(): return lax.ppermute(values, 'blk', where)  34.6 us
    ppermute x25, waiting for transfers between devices, move(): return lax.ppermute(values, 'blk', where)  26.4 us
    pallas_call x1, Pallas kernels, stationary(): pl.pallas_call(functools.partial(near_kernel, BATCH, chips, len(pieces)),...  9.21 us
    unnamed x23, local copies, waits for them, and re-layouts  5.74 us
    pallas_call x1, Pallas kernels, stationary(): pl.pallas_call(far_kernel, out_shape=jax.ShapeDtypeStruct((clusters, dire...  2.49 us
  transfers between devices with their start and end apart: 25, of which 16 were waited for; matrix products, arithmetic and copies ran while one was open for 2% of the time, Pallas kernels for 4%

profile of v6, /device:TPU:0, one launch (start us, length us, event | category | flops | bytes accessed | tf_op | source)
XLA Modules:
  0.0 80.5 jit_solution(3413693893127440295)
XLA Ops:
  0.5 2.6 %collective-permute-start.7 = (bf16[16,64,128]{2,1,0:T(8,128)(2,1)}, bf16[16,64,128]{2,1,0:T(8,128)(2,1)S(1)}, u32[]{:S(2)}, u32[]{:S(2)}) collective-permute-start(bf16[16,64,128]{2,1,0:T(8,128)(2,1)} %refs_0_.1), channel_id=1, source_target_pairs={{0,4},{1,3},{4,8},{5,1},{8,12},{9,5},{12,14},{13,9},{14,10},{15,13... | collective-permute-start | bytes 786440 | tf_op jit(solution)/shard_map/ppermute | solution.py:374
  3.0 1.4 %collective-permute-start.1 = (bf16[16,64,128]{2,1,0:T(8,128)(2,1)}, bf16[16,64,128]{2,1,0:T(8,128)(2,1)S(1)}, u32[]{:S(2)}, u32[]{:S(2)}) collective-permute-start(bf16[16,64,128]{2,1,0:T(8,128)(2,1)} %refs_0_.1), channel_id=1, source_target_pairs={{0,3},{1,4},{4,1},{5,8},{8,5},{9,12},{12,9},{13,14},{14,13},{15,10... | collective-permute-start | bytes 786440 | tf_op jit(solution)/shard_map/ppermute | solution.py:374
  4.4 1.0 %copy-done = bf16[16,64,128]{2,1,0:T(8,128)(2,1)S(1)} copy-done((bf16[16,64,128]{2,1,0:T(8,128)(2,1)S(1)}, bf16[16,64,128]{2,1,0:T(8,128)(2,1)}, u32[]{:S(2)}) %copy-start) | copy-done | bytes 262168
  5.4 0.8 %copy-done.2 = bf16[16,16,128]{2,1,0:T(8,128)(2,1)S(1)} copy-done((bf16[16,16,128]{2,1,0:T(8,128)(2,1)S(1)}, bf16[16,16,128]{2,1,0:T(8,128)(2,1)}, u32[]{:S(2)}) %copy-start.2) | copy-done | bytes 65560
  9.0 2.4 %collective-permute-start.8 = (bf16[16,64,128]{2,1,0:T(8,128)(2,1)S(1)}, bf16[16,64,128]{2,1,0:T(8,128)(2,1)S(1)}, u32[]{:S(2)}, u32[]{:S(2)}) collective-permute-start(bf16[16,64,128]{2,1,0:T(8,128)(2,1)S(1)} %collective-permute-done.7.refs_1_), channel_id=1, source_target_pairs={{0,4},{1,3},{4,8},{5,1},{8,12},{9,5},{12,14},{13,9},{14,10},{15,13... | collective-permute-start | bytes 786440 | tf_op jit(solution)/shard_map/ppermute | solution.py:374
  11.4 1.6 %collective-permute-start = (bf16[128,128]{1,0:T(8,128)(2,1)S(1)}, bf16[128,128]{1,0:T(8,128)(2,1)S(1)}, u32[]{:S(2)}, u32[]{:S(2)}) collective-permute-start(bf16[128,128]{1,0:T(8,128)(2,1)S(1)} %get-tuple-element.32), channel_id=1, source_target_pairs={{0,4},{1,5},{2,6},{3,7},{4,0},{5,1},{6,2},{7,3},{8,12},{9,13},{10,... | collective-permute-start | bytes 98312 | tf_op jit(solution)/shard_map/ppermute | solution.py:374
  13.5 2.3 %collective-permute-done = bf16[128,128]{1,0:T(8,128)(2,1)S(1)} collective-permute-done((bf16[128,128]{1,0:T(8,128)(2,1)S(1)}, bf16[128,128]{1,0:T(8,128)(2,1)S(1)}, u32[]{:S(2)}, u32[]{:S(2)}) %collective-permute-start) | collective-permute-done | bytes 32800 | tf_op jit(solution)/shard_map/ppermute | solution.py:374
  16.1 2.1 %collective-permute-start.11 = (bf16[16,64,128]{2,1,0:T(8,128)(2,1)S(1)}, bf16[16,64,128]{2,1,0:T(8,128)(2,1)S(1)}, u32[]{:S(2)}, u32[]{:S(2)}) collective-permute-start(bf16[16,64,128]{2,1,0:T(8,128)(2,1)S(1)} %collective-permute-done.8.refs_3_), channel_id=1, source_target_pairs={{0,4},{1,3},{4,8},{5,1},{8,12},{9,5},{12,14},{13,9},{14,10},{15,13... | collective-permute-start | bytes 786440 | tf_op jit(solution)/shard_map/ppermute | solution.py:374
  18.2 2.7 %collective-permute-start.2 = (bf16[256,128]{1,0:T(8,128)(2,1)S(1)}, bf16[256,128]{1,0:T(8,128)(2,1)S(1)}, u32[]{:S(2)}, u32[]{:S(2)}) collective-permute-start(bf16[256,128]{1,0:T(8,128)(2,1)S(1)} %pad_maximum_fusion), channel_id=1, source_target_pairs={{0,8},{1,9},{2,10},{3,11},{4,12},{5,13},{6,14},{7,15},{8,0},{9,1},... | collective-permute-start | bytes 196616 | tf_op jit(solution)/shard_map/ppermute | solution.py:374
  20.8 2.5 %collective-permute-done.2 = bf16[256,128]{1,0:T(8,128)(2,1)S(1)} collective-permute-done((bf16[256,128]{1,0:T(8,128)(2,1)S(1)}, bf16[256,128]{1,0:T(8,128)(2,1)S(1)}, u32[]{:S(2)}, u32[]{:S(2)}) %collective-permute-start.2) | collective-permute-done | bytes 65568 | tf_op jit(solution)/shard_map/ppermute | solution.py:374
  23.3 3.9 %collective-permute-start.4 = (bf16[512,128]{1,0:T(8,128)(2,1)S(1)}, bf16[512,128]{1,0:T(8,128)(2,1)S(1)}, u32[]{:S(2)}, u32[]{:S(2)}) collective-permute-start(bf16[512,128]{1,0:T(8,128)(2,1)S(1)} %constant_dynamic-update-slice_fusion.refs_0_), channel_id=1, source_target_pairs={{0,2},{1,3},{2,0},{3,1},{4,6},{5,7},{6,4},{7,5},{8,10},{9,11},{10,... | collective-permute-start | bytes 393224 | tf_op jit(solution)/shard_map/ppermute | solution.py:374
  27.2 1.5 %collective-permute-start.12 = (bf16[16,64,128]{2,1,0:T(8,128)(2,1)S(1)}, bf16[16,64,128]{2,1,0:T(8,128)(2,1)S(1)}, u32[]{:S(2)}, u32[]{:S(2)}) collective-permute-start(bf16[16,64,128]{2,1,0:T(8,128)(2,1)S(1)} %collective-permute-done.3.refs_4_), channel_id=1, source_target_pairs={{0,4},{1,3},{4,8},{5,1},{8,12},{9,5},{12,14},{13,9},{14,10},{15,13... | collective-permute-start | bytes 786440 | tf_op jit(solution)/shard_map/ppermute | solution.py:374
  28.8 2.4 %collective-permute-done.4.refs_1_ = bf16[512,128]{1,0:T(8,128)(2,1)S(1)} collective-permute-done((bf16[512,128]{1,0:T(8,128)(2,1)S(1)}, bf16[512,128]{1,0:T(8,128)(2,1)S(1)}, u32[]{:S(2)}, u32[]{:S(2)}) %collective-permute-start.4) | collective-permute-done | bytes 131104 | tf_op jit(solution)/shard_map/ppermute | solution.py:374
  31.7 1.0 %copy.14 = bf16[256,16,16]{0,1,2:T(8,128)(2,1)S(1)} copy(bf16[256,16,16]{0,2,1:T(8,128)(2,1)} %param.16) | data formatting | bytes 262144 | tf_op args[5]
  32.7 0.9 %collective-permute-done.12.refs_6_ = bf16[16,64,128]{2,1,0:T(8,128)(2,1)S(1)} collective-permute-done((bf16[16,64,128]{2,1,0:T(8,128)(2,1)S(1)}, bf16[16,64,128]{2,1,0:T(8,128)(2,1)S(1)}, u32[]{:S(2)}, u32[]{:S(2)}) %collective-permute-start.12) | collective-permute-done | bytes 262176 | tf_op jit(solution)/shard_map/ppermute | solution.py:374
  33.6 2.8 %collective-permute-done.13.refs_7_ = bf16[16,64,128]{2,1,0:T(8,128)(2,1)S(1)} collective-permute-done((bf16[16,64,128]{2,1,0:T(8,128)(2,1)S(1)}, bf16[16,64,128]{2,1,0:T(8,128)(2,1)S(1)}, u32[]{:S(2)}, u32[]{:S(2)}) %collective-permute-start.13) | collective-permute-done | bytes 262176 | tf_op jit(solution)/shard_map/ppermute | solution.py:374
  36.4 0.9 %copy-done.1 = bf16[16,64,128]{2,1,0:T(8,128)(2,1)S(1)} copy-done((bf16[16,64,128]{2,1,0:T(8,128)(2,1)S(1)}, bf16[16,64,128]{2,1,0:T(8,128)(2,1)}, u32[]{:S(2)}) %copy-start.1) | copy-done | bytes 262168
  37.3 9.2 %near.1 = (f32[128,64,128]{2,1,0:T(8,128)S(1)}, bf16[16,64,128]{2,1,0:T(8,128)(2,1)S(1)}, bf16[16,64,128]{2,1,0:T(8,128)(2,1)S(1)}, bf16[96,64,128]{2,1,0:T(8,128)(2,1)S(1)}) custom-call(s32[8,128]{1,0:T(8,128)S(1)} %get-tuple-element.40.list_ref, s32[8,128]{1,0:T(8,128)S(1)} %collective-permute-done.10.mate_list_ref, bf16[16,64,128]{2,1,0:T(8,128)(2,1)S(1)} %copy-done.1, ...), custom_call_target="tpu_custom_call" | custom-call | flops 2147483648 | bytes 16777216 | tf_op jit(solution)/shard_map/near/pallas_call | solution.py:424
  47.2 3.2 %collective-permute-done.14 = bf16[16,64,128]{2,1,0:T(8,128)(2,1)S(1)} collective-permute-done((bf16[16,64,128]{2,1,0:T(8,128)(2,1)S(1)}, bf16[16,64,128]{2,1,0:T(8,128)(2,1)S(1)}, u32[]{:S(2)}, u32[]{:S(2)}) %collective-permute-start.14) | collective-permute-done | bytes 262176 | tf_op jit(solution)/shard_map/ppermute | solution.py:374
  50.9 2.4 %collective-permute-start.16 = (bf16[16,64,128]{2,1,0:T(8,128)(2,1)S(1)}, bf16[16,64,128]{2,1,0:T(8,128)(2,1)S(1)}, u32[]{:S(2)}, u32[]{:S(2)}) collective-permute-start(bf16[16,64,128]{2,1,0:T(8,128)(2,1)S(1)} %get-tuple-element.45), channel_id=1, source_target_pairs={{0,4},{1,3},{4,8},{5,1},{8,12},{9,5},{12,14},{13,9},{14,10},{15,13... | collective-permute-start | bytes 786440 | tf_op jit(solution)/shard_map/ppermute | solution.py:374
  53.4 2.5 %far.1 = f32[16,64,128]{2,1,0:T(8,128)S(1)} custom-call(bf16[512,128]{1,0:T(8,128)(2,1)S(1)} %constant_dynamic-update-slice_fusion.refs_0_, bf16[512,128]{1,0:T(8,128)(2,1)S(1)} %collective-permute-done.4.refs_1_, bf16[512,128]{1,0:T(8,128)(2,1)S(1)} %collective-permute-done.5.refs_2_, bf16[512,128]{1,0:T(8,128)(2,1)S(1)} %collective-permute-done.6.refs_3_, ...), custom_call_target="tpu_custom_call" | custom-call | flops 536870912 | bytes 8388608 | tf_op jit(solution)/shard_map/far/pallas_call | solution.py:466
  55.9 1.4 %collective-permute-done.16 = bf16[16,64,128]{2,1,0:T(8,128)(2,1)S(1)} collective-permute-done((bf16[16,64,128]{2,1,0:T(8,128)(2,1)S(1)}, bf16[16,64,128]{2,1,0:T(8,128)(2,1)S(1)}, u32[]{:S(2)}, u32[]{:S(2)}) %collective-permute-start.16) | collective-permute-done | bytes 262176 | tf_op jit(solution)/shard_map/ppermute | solution.py:374
  57.5 2.4 %collective-permute-start.18 = (bf16[16,64,128]{2,1,0:T(8,128)(2,1)S(1)}, bf16[16,64,128]{2,1,0:T(8,128)(2,1)S(1)}, u32[]{:S(2)}, u32[]{:S(2)}) collective-permute-start(bf16[16,64,128]{2,1,0:T(8,128)(2,1)S(1)} %add_convert_fusion.5), channel_id=1, source_target_pairs={{0,4},{1,3},{4,8},{5,1},{8,12},{9,5},{12,14},{13,9},{14,10},{15,13... | collective-permute-start | bytes 786440 | tf_op jit(solution)/shard_map/ppermute | solution.py:374
  60.3 2.4 %collective-permute-start.21 = (bf16[16,64,128]{2,1,0:T(8,128)(2,1)S(1)}, bf16[16,64,128]{2,1,0:T(8,128)(2,1)S(1)}, u32[]{:S(2)}, u32[]{:S(2)}) collective-permute-start(bf16[16,64,128]{2,1,0:T(8,128)(2,1)S(1)} %add_convert_fusion.4), channel_id=1, source_target_pairs={{0,4},{1,3},{4,8},{5,1},{8,12},{9,5},{12,14},{13,9},{14,10},{15,13... | collective-permute-start | bytes 786440 | tf_op jit(solution)/shard_map/ppermute | solution.py:374
  62.7 1.2 %collective-permute-done.18 = bf16[16,64,128]{2,1,0:T(8,128)(2,1)S(1)} collective-permute-done((bf16[16,64,128]{2,1,0:T(8,128)(2,1)S(1)}, bf16[16,64,128]{2,1,0:T(8,128)(2,1)S(1)}, u32[]{:S(2)}, u32[]{:S(2)}) %collective-permute-start.18) | collective-permute-done | bytes 262176 | tf_op jit(solution)/shard_map/ppermute | solution.py:374
  64.0 2.4 %collective-permute-start.20 = (bf16[16,64,128]{2,1,0:T(8,128)(2,1)S(1)}, bf16[16,64,128]{2,1,0:T(8,128)(2,1)S(1)}, u32[]{:S(2)}, u32[]{:S(2)}) collective-permute-start(bf16[16,64,128]{2,1,0:T(8,128)(2,1)S(1)} %add_convert_fusion.3), channel_id=1, source_target_pairs={{0,4},{1,3},{4,8},{5,1},{8,12},{9,5},{12,14},{13,9},{14,10},{15,13... | collective-permute-start | bytes 786440 | tf_op jit(solution)/shard_map/ppermute | solution.py:374
  66.8 2.4 %collective-permute-start.22 = (bf16[16,64,128]{2,1,0:T(8,128)(2,1)S(1)}, bf16[16,64,128]{2,1,0:T(8,128)(2,1)S(1)}, u32[]{:S(2)}, u32[]{:S(2)}) collective-permute-start(bf16[16,64,128]{2,1,0:T(8,128)(2,1)S(1)} %add_convert_fusion.2), channel_id=1, source_target_pairs={{0,4},{1,3},{4,8},{5,1},{8,12},{9,5},{12,14},{13,9},{14,10},{15,13... | collective-permute-start | bytes 786440 | tf_op jit(solution)/shard_map/ppermute | solution.py:374
  69.3 1.2 %collective-permute-done.20 = bf16[16,64,128]{2,1,0:T(8,128)(2,1)S(1)} collective-permute-done((bf16[16,64,128]{2,1,0:T(8,128)(2,1)S(1)}, bf16[16,64,128]{2,1,0:T(8,128)(2,1)S(1)}, u32[]{:S(2)}, u32[]{:S(2)}) %collective-permute-start.20) | collective-permute-done | bytes 262176 | tf_op jit(solution)/shard_map/ppermute | solution.py:374
  70.6 2.7 %collective-permute-done.22 = bf16[16,64,128]{2,1,0:T(8,128)(2,1)S(1)} collective-permute-done((bf16[16,64,128]{2,1,0:T(8,128)(2,1)S(1)}, bf16[16,64,128]{2,1,0:T(8,128)(2,1)S(1)}, u32[]{:S(2)}, u32[]{:S(2)}) %collective-permute-start.22) | collective-permute-done | bytes 262176 | tf_op jit(solution)/shard_map/ppermute | solution.py:374
  73.3 2.4 %collective-permute-start.24 = (bf16[16,64,128]{2,1,0:T(8,128)(2,1)S(1)}, bf16[16,64,128]{2,1,0:T(8,128)(2,1)S(1)}, u32[]{:S(2)}, u32[]{:S(2)}) collective-permute-start(bf16[16,64,128]{2,1,0:T(8,128)(2,1)S(1)} %add_convert_fusion.1), channel_id=1, source_target_pairs={{0,4},{1,3},{4,8},{5,1},{8,12},{9,5},{12,14},{13,9},{14,10},{15,13... | collective-permute-start | bytes 786440 | tf_op jit(solution)/shard_map/ppermute | solution.py:374
  75.6 4.0 %collective-permute-done.24 = bf16[16,64,128]{2,1,0:T(8,128)(2,1)S(1)} collective-permute-done((bf16[16,64,128]{2,1,0:T(8,128)(2,1)S(1)}, bf16[16,64,128]{2,1,0:T(8,128)(2,1)S(1)}, u32[]{:S(2)}, u32[]{:S(2)}) %collective-permute-start.24) | collective-permute-done | bytes 262176 | tf_op jit(solution)/shard_map/ppermute | solution.py:374
  79.6 0.9 %add_convert_fusion = bf16[16,64,128]{2,1,0:T(8,128)(2,1)} fusion(bf16[16,64,128]{2,1,0:T(8,128)(2,1)S(1)} %collective-permute-done.24, bf16[16,64,128]{2,1,0:T(8,128)(2,1)S(1)} %collective-permute-done.23, f32[16,64,128]{2,1,0:T(8,128)S(1)} %far.1, f32[128,64,128]{2,1,0:T(8,128)S(1)} %get-tuple-element.42, bf16[96,64,128]{2,1,0:T(8,128)(2,1)S(1)} %collective-permute-done.17), kind=kLoop, calls=%fused_computation | loop fusion | flops 1048576 | bytes 2097152 | tf_op jit(solution)/shard_map/convert_element_type | solution.py:492
  (53 shorter events, 7.0 us)
Async XLA Ops:
  0.0 16.1 %collective-permute-start.9 = (bf16[128,128,128]{2,1,0:T(8,128)(2,1)}, bf16[128,128,128]{2,1,0:T(8,128)(2,1)}, u32[]{:S(2)}, u32[]{:S(2)}) collective-permute-start(bf16[128,128,128]{2,1,0:T(8,128)(2,1)} %refs_8_.1), channel_id=1, source_target_pairs={{0,1},{1,0},{2,3},{3,2},{4,5},{5,4},{6,7},{7,6},{8,9},{9,8},{10,11... | collective-permute-start | bytes 12582920 | tf_op jit(solution)/shard_map/ppermute | solution.py:374
  0.5 8.6 %collective-permute-start.7 = (bf16[16,64,128]{2,1,0:T(8,128)(2,1)}, bf16[16,64,128]{2,1,0:T(8,128)(2,1)S(1)}, u32[]{:S(2)}, u32[]{:S(2)}) collective-permute-start(bf16[16,64,128]{2,1,0:T(8,128)(2,1)} %refs_0_.1), channel_id=1, source_target_pairs={{0,4},{1,3},{4,8},{5,1},{8,12},{9,5},{12,14},{13,9},{14,10},{15,13... | collective-permute-start | bytes 786440 | tf_op jit(solution)/shard_map/ppermute | solution.py:374
  3.0 10.0 %collective-permute-start.1 = (bf16[16,64,128]{2,1,0:T(8,128)(2,1)}, bf16[16,64,128]{2,1,0:T(8,128)(2,1)S(1)}, u32[]{:S(2)}, u32[]{:S(2)}) collective-permute-start(bf16[16,64,128]{2,1,0:T(8,128)(2,1)} %refs_0_.1), channel_id=1, source_target_pairs={{0,3},{1,4},{4,1},{5,8},{8,5},{9,12},{12,9},{13,14},{14,13},{15,10... | collective-permute-start | bytes 786440 | tf_op jit(solution)/shard_map/ppermute | solution.py:374
  4.4 1.0 %copy-start = (bf16[16,64,128]{2,1,0:T(8,128)(2,1)S(1)}, bf16[16,64,128]{2,1,0:T(8,128)(2,1)}, u32[]{:S(2)}) copy-start(bf16[16,64,128]{2,1,0:T(8,128)(2,1)} %refs_0_.1) | copy-start | bytes 786436
  5.4 0.8 %copy-start.2 = (bf16[16,16,128]{2,1,0:T(8,128)(2,1)S(1)}, bf16[16,16,128]{2,1,0:T(8,128)(2,1)}, u32[]{:S(2)}) copy-start(bf16[16,16,128]{2,1,0:T(8,128)(2,1)} %basis_ref.1) | copy-start | bytes 196612
  9.0 7.0 %collective-permute-start.8 = (bf16[16,64,128]{2,1,0:T(8,128)(2,1)S(1)}, bf16[16,64,128]{2,1,0:T(8,128)(2,1)S(1)}, u32[]{:S(2)}, u32[]{:S(2)}) collective-permute-start(bf16[16,64,128]{2,1,0:T(8,128)(2,1)S(1)} %collective-permute-done.7.refs_1_), channel_id=1, source_target_pairs={{0,4},{1,3},{4,8},{5,1},{8,12},{9,5},{12,14},{13,9},{14,10},{15,13... | collective-permute-start | bytes 786440 | tf_op jit(solution)/shard_map/ppermute | solution.py:374
  11.4 4.3 %collective-permute-start = (bf16[128,128]{1,0:T(8,128)(2,1)S(1)}, bf16[128,128]{1,0:T(8,128)(2,1)S(1)}, u32[]{:S(2)}, u32[]{:S(2)}) collective-permute-start(bf16[128,128]{1,0:T(8,128)(2,1)S(1)} %get-tuple-element.32), channel_id=1, source_target_pairs={{0,4},{1,5},{2,6},{3,7},{4,0},{5,1},{6,2},{7,3},{8,12},{9,13},{10,... | collective-permute-start | bytes 98312 | tf_op jit(solution)/shard_map/ppermute | solution.py:374
  13.0 10.3 %collective-permute-start.3 = (bf16[16,64,128]{2,1,0:T(8,128)(2,1)S(1)}, bf16[16,64,128]{2,1,0:T(8,128)(2,1)S(1)}, u32[]{:S(2)}, u32[]{:S(2)}) collective-permute-start(bf16[16,64,128]{2,1,0:T(8,128)(2,1)S(1)} %collective-permute-done.1.refs_2_), channel_id=1, source_target_pairs={{0,4},{1,3},{4,8},{5,1},{8,12},{9,5},{12,14},{13,9},{14,10},{15,13... | collective-permute-start | bytes 786440 | tf_op jit(solution)/shard_map/ppermute | solution.py:374
  16.1 12.7 %collective-permute-start.11 = (bf16[16,64,128]{2,1,0:T(8,128)(2,1)S(1)}, bf16[16,64,128]{2,1,0:T(8,128)(2,1)S(1)}, u32[]{:S(2)}, u32[]{:S(2)}) collective-permute-start(bf16[16,64,128]{2,1,0:T(8,128)(2,1)S(1)} %collective-permute-done.8.refs_3_), channel_id=1, source_target_pairs={{0,4},{1,3},{4,8},{5,1},{8,12},{9,5},{12,14},{13,9},{14,10},{15,13... | collective-permute-start | bytes 786440 | tf_op jit(solution)/shard_map/ppermute | solution.py:374
  18.2 5.2 %collective-permute-start.2 = (bf16[256,128]{1,0:T(8,128)(2,1)S(1)}, bf16[256,128]{1,0:T(8,128)(2,1)S(1)}, u32[]{:S(2)}, u32[]{:S(2)}) collective-permute-start(bf16[256,128]{1,0:T(8,128)(2,1)S(1)} %pad_maximum_fusion), channel_id=1, source_target_pairs={{0,8},{1,9},{2,10},{3,11},{4,12},{5,13},{6,14},{7,15},{8,0},{9,1},... | collective-permute-start | bytes 196616 | tf_op jit(solution)/shard_map/ppermute | solution.py:374
  23.3 7.8 %collective-permute-start.4 = (bf16[512,128]{1,0:T(8,128)(2,1)S(1)}, bf16[512,128]{1,0:T(8,128)(2,1)S(1)}, u32[]{:S(2)}, u32[]{:S(2)}) collective-permute-start(bf16[512,128]{1,0:T(8,128)(2,1)S(1)} %constant_dynamic-update-slice_fusion.refs_0_), channel_id=1, source_target_pairs={{0,2},{1,3},{2,0},{3,1},{4,6},{5,7},{6,4},{7,5},{8,10},{9,11},{10,... | collective-permute-start | bytes 393224 | tf_op jit(solution)/shard_map/ppermute | solution.py:374
  27.2 6.4 %collective-permute-start.12 = (bf16[16,64,128]{2,1,0:T(8,128)(2,1)S(1)}, bf16[16,64,128]{2,1,0:T(8,128)(2,1)S(1)}, u32[]{:S(2)}, u32[]{:S(2)}) collective-permute-start(bf16[16,64,128]{2,1,0:T(8,128)(2,1)S(1)} %collective-permute-done.3.refs_4_), channel_id=1, source_target_pairs={{0,4},{1,3},{4,8},{5,1},{8,12},{9,5},{12,14},{13,9},{14,10},{15,13... | collective-permute-start | bytes 786440 | tf_op jit(solution)/shard_map/ppermute | solution.py:374
  28.7 7.7 %collective-permute-start.13 = (bf16[16,64,128]{2,1,0:T(8,128)(2,1)S(1)}, bf16[16,64,128]{2,1,0:T(8,128)(2,1)S(1)}, u32[]{:S(2)}, u32[]{:S(2)}) collective-permute-start(bf16[16,64,128]{2,1,0:T(8,128)(2,1)S(1)} %collective-permute-done.11.refs_5_), channel_id=1, source_target_pairs={{0,4},{1,3},{4,8},{5,1},{8,12},{9,5},{12,14},{13,9},{14,10},{15,13... | collective-permute-start | bytes 786440 | tf_op jit(solution)/shard_map/ppermute | solution.py:374
  28.8 3.9 %collective-permute-start.5 = (bf16[512,128]{1,0:T(8,128)(2,1)S(1)}, bf16[512,128]{1,0:T(8,128)(2,1)S(1)}, u32[]{:S(2)}, u32[]{:S(2)}) collective-permute-start(bf16[512,128]{1,0:T(8,128)(2,1)S(1)} %constant_dynamic-update-slice_fusion.refs_0_), channel_id=1, source_target_pairs={{0,1},{1,0},{2,3},{3,2},{4,5},{5,4},{6,7},{7,6},{8,9},{9,8},{10,11... | collective-permute-start | bytes 393224 | tf_op jit(solution)/shard_map/ppermute | solution.py:374
  31.2 1.5 %collective-permute-start.6 = (bf16[512,128]{1,0:T(8,128)(2,1)S(1)}, bf16[512,128]{1,0:T(8,128)(2,1)S(1)}, u32[]{:S(2)}, u32[]{:S(2)}) collective-permute-start(bf16[512,128]{1,0:T(8,128)(2,1)S(1)} %collective-permute-done.4.refs_1_), channel_id=1, source_target_pairs={{0,1},{1,0},{2,3},{3,2},{4,5},{5,4},{6,7},{7,6},{8,9},{9,8},{10,11... | collective-permute-start | bytes 393224 | tf_op jit(solution)/shard_map/ppermute | solution.py:374
  31.2 1.5 %collective-permute-start.10 = (s32[8,128]{1,0:T(8,128)S(1)}, s32[8,128]{1,0:T(8,128)S(1)}, u32[]{:S(2)}, u32[]{:S(2)}) collective-permute-start(s32[8,128]{1,0:T(8,128)S(1)} %get-tuple-element.40.list_ref), channel_id=1, source_target_pairs={{0,1},{1,0},{2,3},{3,2},{4,5},{5,4},{6,7},{7,6},{8,9},{9,8},{10,11... | collective-permute-start | bytes 12296 | tf_op jit(solution)/shard_map/ppermute | solution.py:374
  31.7 21.8 %copy-start.6 = (bf16[16,16,128]{2,1,0:T(8,128)(2,1)S(1)}, bf16[16,16,128]{2,1,0:T(8,128)(2,1)}, u32[]{:S(2)}) copy-start(bf16[16,16,128]{2,1,0:T(8,128)(2,1)} %refs_9_.1) | copy-start | bytes 196612
  31.7 21.8 %copy-start.8 = (s32[256,1]{0,1:T(1,128)S(1)}, s32[256,1]{0,1:T(1,128)}, u32[]{:S(2)}) copy-start(s32[256,1]{0,1:T(1,128)} %param.18) | copy-start | bytes 3076
  31.7 21.8 %copy-start.9 = (s32[256]{0:T(256)S(1)}, s32[256]{0:T(256)}, u32[]{:S(2)}) copy-start(s32[256]{0:T(256)} %param.19) | copy-start | bytes 3076
  32.7 20.8 %copy-start.7 = (s32[256]{0:T(256)S(1)}, s32[256]{0:T(256)}, u32[]{:S(2)}) copy-start(s32[256]{0:T(256)} %param.17) | copy-start | bytes 3076
  36.4 1.0 %copy-start.1 = (bf16[16,64,128]{2,1,0:T(8,128)(2,1)S(1)}, bf16[16,64,128]{2,1,0:T(8,128)(2,1)}, u32[]{:S(2)}) copy-start(bf16[16,64,128]{2,1,0:T(8,128)(2,1)} %refs_0_.1) | copy-start | bytes 786436
  46.6 10.8 %collective-permute-start.17 = (bf16[96,64,128]{2,1,0:T(8,128)(2,1)S(1)}, bf16[96,64,128]{2,1,0:T(8,128)(2,1)S(1)}, u32[]{:S(2)}, u32[]{:S(2)}) collective-permute-start(bf16[96,64,128]{2,1,0:T(8,128)(2,1)S(1)} %get-tuple-element.48), channel_id=1, source_target_pairs={{0,1},{1,0},{2,3},{3,2},{4,5},{5,4},{6,7},{7,6},{8,9},{9,8},{10,11... | collective-permute-start | bytes 4718600 | tf_op jit(solution)/shard_map/ppermute | solution.py:374
  46.6 3.8 %collective-permute-start.14 = (bf16[16,64,128]{2,1,0:T(8,128)(2,1)S(1)}, bf16[16,64,128]{2,1,0:T(8,128)(2,1)S(1)}, u32[]{:S(2)}, u32[]{:S(2)}) collective-permute-start(bf16[16,64,128]{2,1,0:T(8,128)(2,1)S(1)} %get-tuple-element.43), channel_id=1, source_target_pairs={{0,1},{1,0},{2,3},{3,2},{4,5},{5,4},{6,7},{7,6},{8,9},{9,8},{10,11... | collective-permute-start | bytes 786440 | tf_op jit(solution)/shard_map/ppermute | solution.py:374
  47.1 3.6 %collective-permute-start.15 = (bf16[16,64,128]{2,1,0:T(8,128)(2,1)S(1)}, bf16[16,64,128]{2,1,0:T(8,128)(2,1)S(1)}, u32[]{:S(2)}, u32[]{:S(2)}) collective-permute-start(bf16[16,64,128]{2,1,0:T(8,128)(2,1)S(1)} %get-tuple-element.44), channel_id=1, source_target_pairs={{0,1},{1,0},{2,3},{3,2},{4,5},{5,4},{6,7},{7,6},{8,9},{9,8},{10,11... | collective-permute-start | bytes 786440 | tf_op jit(solution)/shard_map/ppermute | solution.py:374
  50.9 6.4 %collective-permute-start.16 = (bf16[16,64,128]{2,1,0:T(8,128)(2,1)S(1)}, bf16[16,64,128]{2,1,0:T(8,128)(2,1)S(1)}, u32[]{:S(2)}, u32[]{:S(2)}) collective-permute-start(bf16[16,64,128]{2,1,0:T(8,128)(2,1)S(1)} %get-tuple-element.45), channel_id=1, source_target_pairs={{0,4},{1,3},{4,8},{5,1},{8,12},{9,5},{12,14},{13,9},{14,10},{15,13... | collective-permute-start | bytes 786440 | tf_op jit(solution)/shard_map/ppermute | solution.py:374
  53.4 6.8 %collective-permute-start.19 = (bf16[16,64,128]{2,1,0:T(8,128)(2,1)S(1)}, bf16[16,64,128]{2,1,0:T(8,128)(2,1)S(1)}, u32[]{:S(2)}, u32[]{:S(2)}) collective-permute-start(bf16[16,64,128]{2,1,0:T(8,128)(2,1)S(1)} %get-tuple-element.46), channel_id=1, source_target_pairs={{0,4},{1,3},{4,8},{5,1},{8,12},{9,5},{12,14},{13,9},{14,10},{15,13... | collective-permute-start | bytes 786440 | tf_op jit(solution)/shard_map/ppermute | solution.py:374
  57.5 6.4 %collective-permute-start.18 = (bf16[16,64,128]{2,1,0:T(8,128)(2,1)S(1)}, bf16[16,64,128]{2,1,0:T(8,128)(2,1)S(1)}, u32[]{:S(2)}, u32[]{:S(2)}) collective-permute-start(bf16[16,64,128]{2,1,0:T(8,128)(2,1)S(1)} %add_convert_fusion.5), channel_id=1, source_target_pairs={{0,4},{1,3},{4,8},{5,1},{8,12},{9,5},{12,14},{13,9},{14,10},{15,13... | collective-permute-start | bytes 786440 | tf_op jit(solution)/shard_map/ppermute | solution.py:374
  60.3 6.4 %collective-permute-start.21 = (bf16[16,64,128]{2,1,0:T(8,128)(2,1)S(1)}, bf16[16,64,128]{2,1,0:T(8,128)(2,1)S(1)}, u32[]{:S(2)}, u32[]{:S(2)}) collective-permute-start(bf16[16,64,128]{2,1,0:T(8,128)(2,1)S(1)} %add_convert_fusion.4), channel_id=1, source_target_pairs={{0,4},{1,3},{4,8},{5,1},{8,12},{9,5},{12,14},{13,9},{14,10},{15,13... | collective-permute-start | bytes 786440 | tf_op jit(solution)/shard_map/ppermute | solution.py:374
  64.0 6.4 %collective-permute-start.20 = (bf16[16,64,128]{2,1,0:T(8,128)(2,1)S(1)}, bf16[16,64,128]{2,1,0:T(8,128)(2,1)S(1)}, u32[]{:S(2)}, u32[]{:S(2)}) collective-permute-start(bf16[16,64,128]{2,1,0:T(8,128)(2,1)S(1)} %add_convert_fusion.3), channel_id=1, source_target_pairs={{0,4},{1,3},{4,8},{5,1},{8,12},{9,5},{12,14},{13,9},{14,10},{15,13... | collective-permute-start | bytes 786440 | tf_op jit(solution)/shard_map/ppermute | solution.py:374
  66.8 6.4 %collective-permute-start.22 = (bf16[16,64,128]{2,1,0:T(8,128)(2,1)S(1)}, bf16[16,64,128]{2,1,0:T(8,128)(2,1)S(1)}, u32[]{:S(2)}, u32[]{:S(2)}) collective-permute-start(bf16[16,64,128]{2,1,0:T(8,128)(2,1)S(1)} %add_convert_fusion.2), channel_id=1, source_target_pairs={{0,4},{1,3},{4,8},{5,1},{8,12},{9,5},{12,14},{13,9},{14,10},{15,13... | collective-permute-start | bytes 786440 | tf_op jit(solution)/shard_map/ppermute | solution.py:374
  73.3 2.4 %collective-permute-start.23 = (bf16[16,64,128]{2,1,0:T(8,128)(2,1)S(1)}, bf16[16,64,128]{2,1,0:T(8,128)(2,1)S(1)}, u32[]{:S(2)}, u32[]{:S(2)}) collective-permute-start(bf16[16,64,128]{2,1,0:T(8,128)(2,1)S(1)} %collective-permute-done.22), channel_id=1, source_target_pairs={{0,1},{1,0},{2,3},{3,2},{4,5},{5,4},{6,7},{7,6},{8,9},{9,8},{10,11... | collective-permute-start | bytes 786440 | tf_op jit(solution)/shard_map/ppermute | solution.py:374
  73.3 6.4 %collective-permute-start.24 = (bf16[16,64,128]{2,1,0:T(8,128)(2,1)S(1)}, bf16[16,64,128]{2,1,0:T(8,128)(2,1)S(1)}, u32[]{:S(2)}, u32[]{:S(2)}) collective-permute-start(bf16[16,64,128]{2,1,0:T(8,128)(2,1)S(1)} %add_convert_fusion.1), channel_id=1, source_target_pairs={{0,4},{1,3},{4,8},{5,1},{8,12},{9,5},{12,14},{13,9},{14,10},{15,13... | collective-permute-start | bytes 786440 | tf_op jit(solution)/shard_map/ppermute | solution.py:374
  (3 other events, 2.0 us)

commit v7 on v6

--- a/solution.py
+++ b/solution.py
@@ -9,7 +9,7 @@
 
 CHUNKS = 4
 BATCH = 8
-PROLOGUE_VMEM = 16 << 20
+PROLOGUE_VMEM = 58 << 20
 NEAR_VMEM = 44 << 20
 FAR_VMEM = 16 << 20
 
@@ -118,9 +118,11 @@
 
 
 def prologue_kernel(
-    count, me_ref, owner_ref, slot_ref, offset_ref, rhs_ref, basis_ref, coef_ref, list_ref
+    count, me_ref, owner_ref, slot_ref, offset_ref, rhs_ref, basis_ref, payload_ref, list_ref
 ):
-    clusters = rhs_ref.shape[0]
+    clusters, directions, unknowns = rhs_ref.shape
+    base = clusters * directions
+    payload_ref[0:base, :] = rhs_ref[...].reshape(base, unknowns)
     rank_k = basis_ref.shape[1]
     half = clusters // 2
     rows = []
@@ -135,9 +137,9 @@
             for e in (c, c + half)
         ]
         rows.append(jnp.concatenate(parts, axis=1))
-    coef_ref[...] = jnp.concatenate(
+    payload_ref[base:, :] = jnp.concatenate(
         [row[q : q + 1] for q in range(rank_k) for row in rows], axis=0
-    ).astype(coef_ref.dtype)
+    ).astype(payload_ref.dtype)
 
     me, owner, slot = me_ref[0], owner_ref[...], slot_ref[...]
     stored = owner.shape[1]
@@ -173,9 +175,11 @@
 
 def near_kernel(batch, shards, sends, list_ref, mate_list_ref, *refs):
     shard_refs, (own_hbm, mate_hbm) = refs[:shards], refs[shards : shards + 2]
-    keep_ref, refs = refs[shards + 2], refs[shards + 3 :]
-    send_refs, (columns, blocks, sums, column_sem, block_sem) = refs[:sends], refs[sends:]
-    clusters = shard_refs[0].shape[0]
+    keep_ref, coef_ref, refs = refs[shards + 2], refs[shards + 3], refs[shards + 4 :]
+    send_refs, (columns, blocks, sums, column_sem, coef_sem, block_sem) = refs[:sends], refs[sends:]
+    directions = sums.shape[1]
+    span = columns.shape[0] // shards
+    tail = coef_ref.shape[0] // shards
     chunk = blocks.shape[1] // CHUNKS
 
     def load(source, half, c):
@@ -185,10 +189,20 @@
         )
 
     copies = [
-        pltpu.make_async_copy(ref, columns.at[pl.ds(k * clusters, clusters)], column_sem.at[k])
+        pltpu.make_async_copy(
+            ref.at[pl.ds(0, span)], columns.at[pl.ds(k * span, span)], column_sem.at[k]
+        )
         for k, ref in enumerate(shard_refs)
     ]
     for copy in copies:
+        copy.start()
+    tails = [
+        pltpu.make_async_copy(
+            ref.at[pl.ds(span, tail)], coef_ref.at[pl.ds(k * tail, tail)], coef_sem.at[k]
+        )
+        for k, ref in enumerate(shard_refs)
+    ]
+    for copy in tails:
         copy.start()
     for half, source in enumerate((own_hbm, mate_hbm)):
         for c in range(CHUNKS):
@@ -217,7 +231,9 @@
                     at = jnp.minimum(first + i, end - 1)
                     products.append(
                         lax.dot_general(
-                            columns[ref[2, at]],
+                            columns[
+                                pl.ds(pl.multiple_of(ref[2, at] * directions, directions), directions)
+                            ],
                             blocks[half, ref[0, at]],
                             (((1,), (1,)), ((), ())),
                             preferred_element_type=jnp.float32,
@@ -247,11 +263,13 @@
 
         lax.fori_loop(0, send_ref.shape[0], pack, 0, unroll=2)
         at += send_ref.shape[0]
+    for copy in tails:
+        copy.wait()
 
 
 def far_kernel(*refs):
-    coef_refs = refs[:4]
-    me_ref, couple_ref, slot_ref, dev_ref, cslot_ref, basis_ref, out_ref = refs[4:]
+    coef_refs = refs[:2]
+    me_ref, couple_ref, slot_ref, dev_ref, cslot_ref, basis_ref, out_ref = refs[2:]
     clusters, rank_k, unknowns = basis_ref.shape
     pairs = couple_ref.shape[2]
     directions = out_ref.shape[1]
@@ -263,8 +281,9 @@
         lax.broadcasted_iota(jnp.int32, (clusters, pairs), 0)
         == jnp.broadcast_to(slot_ref[...], (clusters, pairs))
     ).astype(jnp.float32).astype(jnp.bfloat16)
-    away = dev_ref[...] ^ me_ref[0]
-    away = (away & 1) * (count // 2) + ((away >> 1) & 1) * (count // 4) + (away >> 2)
+    away = gather_place(dev_ref[...], me_ref[0], count)
+    theirs = count // 2 + gather_place(dev_ref[...], me_ref[0] ^ 1, count)
+    away = jnp.where(away == count // 2, theirs, away)
     cslot = cslot_ref[...]
     high = (cslot >= half).astype(jnp.int32)
     at = away * half + cslot - high * half
@@ -376,13 +395,13 @@
     def after(values, *others):
         return lax.optimization_barrier((values, *others))[0]
 
-    flow = [move(rhs, ahead), move(rhs, cross)]
     mate_blocks = move(near_blocks, mate)
     here = me.astype(jnp.int32).reshape(1)
-    coef, lists = pl.pallas_call(
+    base = clusters * directions
+    payload, lists = pl.pallas_call(
         functools.partial(prologue_kernel, count),
         out_shape=[
-            jax.ShapeDtypeStruct((half * rank_k, unknowns), jnp.bfloat16),
+            jax.ShapeDtypeStruct((base + half * rank_k, unknowns), jnp.bfloat16),
             jax.ShapeDtypeStruct((8, stored), jnp.int32),
         ],
         in_specs=[whole(pltpu.SMEM)] + [whole()] * 5,
@@ -397,43 +416,38 @@
         rhs,
         basis_in,
     )
-    got = move(coef, [(i, i ^ 4) for i in range(count)])
-    flow[0] = after(flow[0], coef, lists)
-    shards = [rhs]
+    flow = [move(payload, ahead), move(payload, cross)]
+    mate_lists = move(lists, mate)
+    couple = after(jnp.transpose(far_coupling, (2, 1, 0)), payload)
+    shards = [payload]
     for k in range(1, chips):
         x = 1 - k % 2
         if k == 3:
-            flow[x], mate_blocks, lists = lax.optimization_barrier((flow[x], mate_blocks, lists))
+            flow[x], mate_blocks, lists, mate_lists, couple = lax.optimization_barrier(
+                (flow[x], mate_blocks, lists, mate_lists, couple)
+            )
         shards.append(flow[x])
         if k < chips - 2:
             flow[x] = move(flow[x], ahead)
-        if k == 1:
-            mate_lists = move(lists, mate)
-        if k == 2:
-            coef = jnp.concatenate([coef, after(got, shards[k])], axis=0)
-            got = move(coef, [(i, i ^ 8) for i in range(count)])
-        if k == 3:
-            couple = after(jnp.transpose(far_coupling, (2, 1, 0)), shards[k])
-        if k == 4:
-            coef = jnp.concatenate([coef, after(got, shards[k])], axis=0)
-            got = move(coef, side)
-    coefs = [coef, got, move(coef, mate), move(got, mate)]
-    lists = after(lists, couple, *coefs)
 
     pieces = [1, 1, chips - 2]
-    kept, *sends = pl.pallas_call(
+    kept, coef, *sends = pl.pallas_call(
         functools.partial(near_kernel, BATCH, chips, len(pieces)),
-        out_shape=[jax.ShapeDtypeStruct((chips * clusters, directions, unknowns), jnp.float32)]
+        out_shape=[
+            jax.ShapeDtypeStruct((chips * clusters, directions, unknowns), jnp.float32),
+            jax.ShapeDtypeStruct((chips * half * rank_k, unknowns), jnp.bfloat16),
+        ]
         + [
             jax.ShapeDtypeStruct((part * clusters, directions, unknowns), jnp.bfloat16)
             for part in pieces
         ],
         in_specs=[whole(pltpu.SMEM)] * 2 + [whole(pl.ANY)] * (chips + 2),
-        out_specs=[whole()] * (1 + len(pieces)),
+        out_specs=[whole()] * (2 + len(pieces)),
         scratch_shapes=[
-            pltpu.VMEM((chips * clusters, directions, unknowns), jnp.bfloat16),
+            pltpu.VMEM((chips * base, unknowns), jnp.bfloat16),
             pltpu.VMEM((2, *near_blocks.shape), jnp.bfloat16),
             pltpu.VMEM((count * clusters + 1, directions, unknowns), jnp.float32),
+            pltpu.SemaphoreType.DMA((chips,)),
             pltpu.SemaphoreType.DMA((chips,)),
             pltpu.SemaphoreType.DMA((2 * CHUNKS,)),
         ],
@@ -446,7 +460,8 @@
         name="near",
     )(lists, mate_lists, *shards, near_blocks, mate_blocks)
 
-    mates = [move(part, mate) for part in sends]
+    mates = [move(sends[0], mate), move(sends[1], mate)]
+    coefs = [coef, move(coef, mate)]
 
     def term(k):
         part = min(k, 2)
@@ -461,12 +476,13 @@
         return (flow.astype(jnp.float32) + term(k)).astype(jnp.bfloat16)
 
     flow = lax.optimization_barrier([term(0).astype(jnp.bfloat16), term(1).astype(jnp.bfloat16)])
-    couple = after(couple, *flow)
+    couple, sends[2] = after(couple, *flow), after(sends[2], *flow)
     flow = [move(part, ahead) for part in flow]
+    mates.append(move(sends[2], mate))
     far = pl.pallas_call(
         far_kernel,
         out_shape=jax.ShapeDtypeStruct((clusters, directions, unknowns), jnp.float32),
-        in_specs=[whole()] * 4 + [whole(pltpu.SMEM)] + [whole()] * 5,
+        in_specs=[whole()] * 2 + [whole(pltpu.SMEM)] + [whole()] * 5,
         out_specs=whole(),
         compiler_params=pltpu.CompilerParams(vmem_limit_bytes=FAR_VMEM),
         cost_estimate=pl.CostEstimate(
@@ -488,8 +504,9 @@
         x = k % 2
         flow[x] = move(tied(add(flow[x], k), *([far] if k == 2 else [])), ahead)
     flow[1] = move(flow[1], mate)
-    total = far + term(chips - 1) + flow[1].astype(jnp.float32)
-    return (total + flow[0].astype(jnp.float32)).astype(jnp.bfloat16)
+    total = far + term(chips - 1) + flow[0].astype(jnp.float32)
+    total = lax.optimization_barrier(total)
+    return (total + flow[1].astype(jnp.float32)).astype(jnp.bfloat16)
 
 
 def on_device(*args):

time: 80.5 us -> 74.4 us (0.924)
  starting transfers between devices: 34.6 us -> 23.3 us
  waiting for transfers between devices: 26.4 us -> 32 us
  local copies, waits for them, and re-layouts: 5.76 us -> 2.66 us
  Pallas kernels: 12 us -> 14.2 us
    ppermute x25 -> x21, starting transfers between devices: 34.6 us -> 23.3 us  [move(): return lax.ppermute(values, 'blk', where)]
    ppermute x25 -> x21, waiting for transfers between devices: 26.4 us -> 32 us  [move(): return lax.ppermute(values, 'blk', where)]
    unnamed x23 -> x13, local copies, waits for them, and re-layouts: 5.74 us -> 2.66 us
    pallas_call x1, Pallas kernels: 0.35 us -> 2.01 us  [stationary(): pl.pallas_call(functools.partial(prologue_kernel, count), out_shape=[jax....]
  transfers between devices with their start and end apart: 25 -> 21, of which waited for: 16 -> 16; matrix products, arithmetic and copies ran while one was open for 2% -> 2% of each run, Pallas kernels for 4% -> 6%
where the time goes in v7:
time: 74.4 us; the launch traced here: 73.7 us
  waiting for transfers between devices  32 us (43%)
  starting transfers between devices  23.3 us (31%)
  Pallas kernels  14.2 us (19%)
  local copies, waits for them, and re-layouts  2.66 us (4%)
  other arithmetic  1.54 us (2%)
    ppermute x21, waiting for transfers between devices, move(): return lax.ppermute(values, 'blk', where)  32 us
    ppermute x21, starting transfers between devices, move(): return lax.ppermute(values, 'blk', where)  23.3 us
    pallas_call x1, Pallas kernels, stationary(): pl.pallas_call(functools.partial(near_kernel, BATCH, chips, len(pieces)),...  9.63 us
    unnamed x13, local copies, waits for them, and re-layouts  2.66 us
    pallas_call x1, Pallas kernels, stationary(): pl.pallas_call(far_kernel, out_shape=jax.ShapeDtypeStruct((clusters, dire...  2.51 us
    pallas_call x1, Pallas kernels, stationary(): pl.pallas_call(functools.partial(prologue_kernel, count), out_shape=[jax....  2.01 us
  transfers between devices with their start and end apart: 21, of which 16 were waited for; matrix products, arithmetic and copies ran while one was open for 2% of the time, Pallas kernels for 6%

profile of v7, /device:TPU:0, one launch (start us, length us, event | category | flops | bytes accessed | tf_op | source)
XLA Modules:
  0.0 73.7 jit_solution(4300557500953810059)
XLA Ops:
  0.5 2.0 %prologue.1 = (bf16[1152,128]{1,0:T(8,128)(2,1)}, s32[8,128]{1,0:T(8,128)}) custom-call(s32[1]{0:T(128)} %bitcast.me_ref.refs_2_, s32[1,128]{1,0:T(1,128)} %bitcast.14, s32[1,128]{1,0:T(1,128)} %bitcast.15, s32[1,128]{1,0:T(1,128)} %bitcast.16, bf16[16,64,128]{2,1,0:T(8,128)(2,1)} %rhs_ref.1, bf16[16,16,128]{2,1,0:T(8,128)(2,1)} %basis_ref.1), custom_call_target="tpu_custom_call" | custom-call | tf_op jit(solution)/shard_map/prologue/pallas_call | solution.py:401
  2.5 2.6 %collective-permute-start = (bf16[1152,128]{1,0:T(8,128)(2,1)}, bf16[1152,128]{1,0:T(8,128)(2,1)S(1)}, u32[]{:S(2)}, u32[]{:S(2)}) collective-permute-start(bf16[1152,128]{1,0:T(8,128)(2,1)} %get-tuple-element.32.refs_0_), channel_id=1, source_target_pairs={{0,4},{1,3},{4,8},{5,1},{8,12},{9,5},{12,14},{13,9},{14,10},{15,13... | collective-permute-start | bytes 884744 | tf_op jit(solution)/shard_map/ppermute | solution.py:393
  5.0 1.4 %collective-permute-start.4 = (bf16[1152,128]{1,0:T(8,128)(2,1)}, bf16[1152,128]{1,0:T(8,128)(2,1)S(1)}, u32[]{:S(2)}, u32[]{:S(2)}) collective-permute-start(bf16[1152,128]{1,0:T(8,128)(2,1)} %get-tuple-element.32.refs_0_), channel_id=1, source_target_pairs={{0,3},{1,4},{4,1},{5,8},{8,5},{9,12},{12,9},{13,14},{14,13},{15,10... | collective-permute-start | bytes 884744 | tf_op jit(solution)/shard_map/ppermute | solution.py:393
  6.4 5.4 %collective-permute-done.refs_1_ = bf16[1152,128]{1,0:T(8,128)(2,1)S(1)} collective-permute-done((bf16[1152,128]{1,0:T(8,128)(2,1)}, bf16[1152,128]{1,0:T(8,128)(2,1)S(1)}, u32[]{:S(2)}, u32[]{:S(2)}) %collective-permute-start) | collective-permute-done | bytes 294944 | tf_op jit(solution)/shard_map/ppermute | solution.py:393
  11.8 2.4 %collective-permute-start.1 = (bf16[1152,128]{1,0:T(8,128)(2,1)S(1)}, bf16[1152,128]{1,0:T(8,128)(2,1)S(1)}, u32[]{:S(2)}, u32[]{:S(2)}) collective-permute-start(bf16[1152,128]{1,0:T(8,128)(2,1)S(1)} %collective-permute-done.refs_1_), channel_id=1, source_target_pairs={{0,4},{1,3},{4,8},{5,1},{8,12},{9,5},{12,14},{13,9},{14,10},{15,13... | collective-permute-start | bytes 884744 | tf_op jit(solution)/shard_map/ppermute | solution.py:393
  14.1 1.0 %copy.14 = bf16[256,16,16]{0,1,2:T(8,128)(2,1)S(1)} copy(bf16[256,16,16]{0,2,1:T(8,128)(2,1)} %param.16) | data formatting | bytes 262144 | tf_op args[5]
  15.2 1.6 %collective-permute-start.5 = (bf16[1152,128]{1,0:T(8,128)(2,1)S(1)}, bf16[1152,128]{1,0:T(8,128)(2,1)S(1)}, u32[]{:S(2)}, u32[]{:S(2)}) collective-permute-start(bf16[1152,128]{1,0:T(8,128)(2,1)S(1)} %collective-permute-done.4.refs_2_), channel_id=1, source_target_pairs={{0,4},{1,3},{4,8},{5,1},{8,12},{9,5},{12,14},{13,9},{14,10},{15,13... | collective-permute-start | bytes 884744 | tf_op jit(solution)/shard_map/ppermute | solution.py:393
  16.8 2.3 %collective-permute-done.1.refs_3_ = bf16[1152,128]{1,0:T(8,128)(2,1)S(1)} collective-permute-done((bf16[1152,128]{1,0:T(8,128)(2,1)S(1)}, bf16[1152,128]{1,0:T(8,128)(2,1)S(1)}, u32[]{:S(2)}, u32[]{:S(2)}) %collective-permute-start.1) | collective-permute-done | bytes 294944 | tf_op jit(solution)/shard_map/ppermute | solution.py:393
  19.1 1.7 %collective-permute-start.6 = (bf16[1152,128]{1,0:T(8,128)(2,1)S(1)}, bf16[1152,128]{1,0:T(8,128)(2,1)S(1)}, u32[]{:S(2)}, u32[]{:S(2)}) collective-permute-start(bf16[1152,128]{1,0:T(8,128)(2,1)S(1)} %collective-permute-done.1.refs_3_), channel_id=1, source_target_pairs={{0,4},{1,3},{4,8},{5,1},{8,12},{9,5},{12,14},{13,9},{14,10},{15,13... | collective-permute-start | bytes 884744 | tf_op jit(solution)/shard_map/ppermute | solution.py:393
  20.9 1.4 %collective-permute-done.5.refs_4_ = bf16[1152,128]{1,0:T(8,128)(2,1)S(1)} collective-permute-done((bf16[1152,128]{1,0:T(8,128)(2,1)S(1)}, bf16[1152,128]{1,0:T(8,128)(2,1)S(1)}, u32[]{:S(2)}, u32[]{:S(2)}) %collective-permute-start.5) | collective-permute-done | bytes 294944 | tf_op jit(solution)/shard_map/ppermute | solution.py:393
  22.3 1.7 %collective-permute-start.7 = (bf16[1152,128]{1,0:T(8,128)(2,1)S(1)}, bf16[1152,128]{1,0:T(8,128)(2,1)S(1)}, u32[]{:S(2)}, u32[]{:S(2)}) collective-permute-start(bf16[1152,128]{1,0:T(8,128)(2,1)S(1)} %collective-permute-done.5.refs_4_), channel_id=1, source_target_pairs={{0,4},{1,3},{4,8},{5,1},{8,12},{9,5},{12,14},{13,9},{14,10},{15,13... | collective-permute-start | bytes 884744 | tf_op jit(solution)/shard_map/ppermute | solution.py:393
  24.0 1.8 %collective-permute-done.6.refs_5_ = bf16[1152,128]{1,0:T(8,128)(2,1)S(1)} collective-permute-done((bf16[1152,128]{1,0:T(8,128)(2,1)S(1)}, bf16[1152,128]{1,0:T(8,128)(2,1)S(1)}, u32[]{:S(2)}, u32[]{:S(2)}) %collective-permute-start.6) | collective-permute-done | bytes 294944 | tf_op jit(solution)/shard_map/ppermute | solution.py:393
  25.9 1.7 %collective-permute-start.8 = (bf16[1152,128]{1,0:T(8,128)(2,1)S(1)}, bf16[1152,128]{1,0:T(8,128)(2,1)S(1)}, u32[]{:S(2)}, u32[]{:S(2)}) collective-permute-start(bf16[1152,128]{1,0:T(8,128)(2,1)S(1)} %collective-permute-done.6.refs_5_), channel_id=1, source_target_pairs={{0,4},{1,3},{4,8},{5,1},{8,12},{9,5},{12,14},{13,9},{14,10},{15,13... | collective-permute-start | bytes 884744 | tf_op jit(solution)/shard_map/ppermute | solution.py:393
  27.6 1.4 %collective-permute-done.7.refs_6_ = bf16[1152,128]{1,0:T(8,128)(2,1)S(1)} collective-permute-done((bf16[1152,128]{1,0:T(8,128)(2,1)S(1)}, bf16[1152,128]{1,0:T(8,128)(2,1)S(1)}, u32[]{:S(2)}, u32[]{:S(2)}) %collective-permute-start.7) | collective-permute-done | bytes 294944 | tf_op jit(solution)/shard_map/ppermute | solution.py:393
  29.0 3.6 %collective-permute-done.8.refs_7_ = bf16[1152,128]{1,0:T(8,128)(2,1)S(1)} collective-permute-done((bf16[1152,128]{1,0:T(8,128)(2,1)S(1)}, bf16[1152,128]{1,0:T(8,128)(2,1)S(1)}, u32[]{:S(2)}, u32[]{:S(2)}) %collective-permute-start.8) | collective-permute-done | bytes 294944 | tf_op jit(solution)/shard_map/ppermute | solution.py:393
  32.6 1.0 %copy-done = bf16[1152,128]{1,0:T(8,128)(2,1)S(1)} copy-done((bf16[1152,128]{1,0:T(8,128)(2,1)S(1)}, bf16[1152,128]{1,0:T(8,128)(2,1)}, u32[]{:S(2)}) %copy-start) | copy-done | bytes 294936
  34.2 9.6 %near.1 = (f32[128,64,128]{2,1,0:T(8,128)S(1)}, bf16[1024,128]{1,0:T(8,128)(2,1)S(1)}, bf16[16,64,128]{2,1,0:T(8,128)(2,1)S(1)}, bf16[16,64,128]{2,1,0:T(8,128)(2,1)S(1)}, bf16[96,64,128]{2,1,0:T(8,128)(2,1)S(1)}) custom-call(s32[8,128]{1,0:T(8,128)S(1)} %copy-done.1, s32[8,128]{1,0:T(8,128)S(1)} %collective-permute-done.3.mate_list_ref, ...), custom_call_target="tpu_custom_call" | custom-call | flops 2147483648 | bytes 16777216 | tf_op jit(solution)/shard_map/near/pallas_call | solution.py:434
  44.4 1.0 %collective-permute-done.10 = bf16[16,64,128]{2,1,0:T(8,128)(2,1)S(1)} collective-permute-done((bf16[16,64,128]{2,1,0:T(8,128)(2,1)S(1)}, bf16[16,64,128]{2,1,0:T(8,128)(2,1)S(1)}, u32[]{:S(2)}, u32[]{:S(2)}) %collective-permute-start.10) | collective-permute-done | bytes 262176 | tf_op jit(solution)/shard_map/ppermute | solution.py:393
  46.6 1.4 %collective-permute-start.12 = (bf16[16,64,128]{2,1,0:T(8,128)(2,1)S(1)}, bf16[16,64,128]{2,1,0:T(8,128)(2,1)S(1)}, u32[]{:S(2)}, u32[]{:S(2)}) collective-permute-start(bf16[16,64,128]{2,1,0:T(8,128)(2,1)S(1)} %get-tuple-element.44), channel_id=1, source_target_pairs={{0,4},{1,3},{4,8},{5,1},{8,12},{9,5},{12,14},{13,9},{14,10},{15,13... | collective-permute-start | bytes 786440 | tf_op jit(solution)/shard_map/ppermute | solution.py:393
  48.0 1.0 %collective-permute-start.15 = (bf16[16,64,128]{2,1,0:T(8,128)(2,1)S(1)}, bf16[16,64,128]{2,1,0:T(8,128)(2,1)S(1)}, u32[]{:S(2)}, u32[]{:S(2)}) collective-permute-start(bf16[16,64,128]{2,1,0:T(8,128)(2,1)S(1)} %get-tuple-element.45), channel_id=1, source_target_pairs={{0,4},{1,3},{4,8},{5,1},{8,12},{9,5},{12,14},{13,9},{14,10},{15,13... | collective-permute-start | bytes 786440 | tf_op jit(solution)/shard_map/ppermute | solution.py:393
  49.8 2.5 %far.1 = f32[16,64,128]{2,1,0:T(8,128)S(1)} custom-call(bf16[1024,128]{1,0:T(8,128)(2,1)S(1)} %get-tuple-element.39.refs_0_, bf16[1024,128]{1,0:T(8,128)(2,1)S(1)} %collective-permute-done.9.refs_1_, s32[1]{0:T(128)} %bitcast.me_ref.refs_2_, bf16[16,16,256]{2,1,0:T(8,128)(2,1)S(1)} %bitcast.10, s32[1,256]{1,0:T(1,128)S(1)} %bitcast.11, ...), custom_call_target="tpu_custom_call" | custom-call | flops 536870912 | bytes 8388608 | tf_op jit(solution)/shard_map/far/pallas_call | solution.py:482
  53.3 1.2 %collective-permute-start.14 = (bf16[16,64,128]{2,1,0:T(8,128)(2,1)S(1)}, bf16[16,64,128]{2,1,0:T(8,128)(2,1)S(1)}, u32[]{:S(2)}, u32[]{:S(2)}) collective-permute-start(bf16[16,64,128]{2,1,0:T(8,128)(2,1)S(1)} %add_convert_fusion.5), channel_id=1, source_target_pairs={{0,4},{1,3},{4,8},{5,1},{8,12},{9,5},{12,14},{13,9},{14,10},{15,13... | collective-permute-start | bytes 786440 | tf_op jit(solution)/shard_map/ppermute | solution.py:393
  54.5 1.5 %collective-permute-done.15 = bf16[16,64,128]{2,1,0:T(8,128)(2,1)S(1)} collective-permute-done((bf16[16,64,128]{2,1,0:T(8,128)(2,1)S(1)}, bf16[16,64,128]{2,1,0:T(8,128)(2,1)S(1)}, u32[]{:S(2)}, u32[]{:S(2)}) %collective-permute-start.15) | collective-permute-done | bytes 262176 | tf_op jit(solution)/shard_map/ppermute | solution.py:393
  56.1 1.2 %collective-permute-start.17 = (bf16[16,64,128]{2,1,0:T(8,128)(2,1)S(1)}, bf16[16,64,128]{2,1,0:T(8,128)(2,1)S(1)}, u32[]{:S(2)}, u32[]{:S(2)}) collective-permute-start(bf16[16,64,128]{2,1,0:T(8,128)(2,1)S(1)} %add_convert_fusion.4), channel_id=1, source_target_pairs={{0,4},{1,3},{4,8},{5,1},{8,12},{9,5},{12,14},{13,9},{14,10},{15,13... | collective-permute-start | bytes 786440 | tf_op jit(solution)/shard_map/ppermute | solution.py:393
  57.3 2.4 %collective-permute-done.14 = bf16[16,64,128]{2,1,0:T(8,128)(2,1)S(1)} collective-permute-done((bf16[16,64,128]{2,1,0:T(8,128)(2,1)S(1)}, bf16[16,64,128]{2,1,0:T(8,128)(2,1)S(1)}, u32[]{:S(2)}, u32[]{:S(2)}) %collective-permute-start.14) | collective-permute-done | bytes 262176 | tf_op jit(solution)/shard_map/ppermute | solution.py:393
  59.8 1.2 %collective-permute-start.16 = (bf16[16,64,128]{2,1,0:T(8,128)(2,1)S(1)}, bf16[16,64,128]{2,1,0:T(8,128)(2,1)S(1)}, u32[]{:S(2)}, u32[]{:S(2)}) collective-permute-start(bf16[16,64,128]{2,1,0:T(8,128)(2,1)S(1)} %add_convert_fusion.3), channel_id=1, source_target_pairs={{0,4},{1,3},{4,8},{5,1},{8,12},{9,5},{12,14},{13,9},{14,10},{15,13... | collective-permute-start | bytes 786440 | tf_op jit(solution)/shard_map/ppermute | solution.py:393
  61.1 1.5 %collective-permute-done.17 = bf16[16,64,128]{2,1,0:T(8,128)(2,1)S(1)} collective-permute-done((bf16[16,64,128]{2,1,0:T(8,128)(2,1)S(1)}, bf16[16,64,128]{2,1,0:T(8,128)(2,1)S(1)}, u32[]{:S(2)}, u32[]{:S(2)}) %collective-permute-start.17) | collective-permute-done | bytes 262176 | tf_op jit(solution)/shard_map/ppermute | solution.py:393
  62.7 1.2 %collective-permute-start.19 = (bf16[16,64,128]{2,1,0:T(8,128)(2,1)S(1)}, bf16[16,64,128]{2,1,0:T(8,128)(2,1)S(1)}, u32[]{:S(2)}, u32[]{:S(2)}) collective-permute-start(bf16[16,64,128]{2,1,0:T(8,128)(2,1)S(1)} %add_convert_fusion.2), channel_id=1, source_target_pairs={{0,4},{1,3},{4,8},{5,1},{8,12},{9,5},{12,14},{13,9},{14,10},{15,13... | collective-permute-start | bytes 786440 | tf_op jit(solution)/shard_map/ppermute | solution.py:393
  63.9 2.4 %collective-permute-done.16 = bf16[16,64,128]{2,1,0:T(8,128)(2,1)S(1)} collective-permute-done((bf16[16,64,128]{2,1,0:T(8,128)(2,1)S(1)}, bf16[16,64,128]{2,1,0:T(8,128)(2,1)S(1)}, u32[]{:S(2)}, u32[]{:S(2)}) %collective-permute-start.16) | collective-permute-done | bytes 262176 | tf_op jit(solution)/shard_map/ppermute | solution.py:393
  66.4 1.2 %collective-permute-start.18 = (bf16[16,64,128]{2,1,0:T(8,128)(2,1)S(1)}, bf16[16,64,128]{2,1,0:T(8,128)(2,1)S(1)}, u32[]{:S(2)}, u32[]{:S(2)}) collective-permute-start(bf16[16,64,128]{2,1,0:T(8,128)(2,1)S(1)} %add_convert_fusion.1), channel_id=1, source_target_pairs={{0,4},{1,3},{4,8},{5,1},{8,12},{9,5},{12,14},{13,9},{14,10},{15,13... | collective-permute-start | bytes 786440 | tf_op jit(solution)/shard_map/ppermute | solution.py:393
  67.6 1.5 %collective-permute-done.19 = bf16[16,64,128]{2,1,0:T(8,128)(2,1)S(1)} collective-permute-done((bf16[16,64,128]{2,1,0:T(8,128)(2,1)S(1)}, bf16[16,64,128]{2,1,0:T(8,128)(2,1)S(1)}, u32[]{:S(2)}, u32[]{:S(2)}) %collective-permute-start.19) | collective-permute-done | bytes 262176 | tf_op jit(solution)/shard_map/ppermute | solution.py:393
  69.1 3.7 %collective-permute-done.18 = bf16[16,64,128]{2,1,0:T(8,128)(2,1)S(1)} collective-permute-done((bf16[16,64,128]{2,1,0:T(8,128)(2,1)S(1)}, bf16[16,64,128]{2,1,0:T(8,128)(2,1)S(1)}, u32[]{:S(2)}, u32[]{:S(2)}) %collective-permute-start.18) | collective-permute-done | bytes 262176 | tf_op jit(solution)/shard_map/ppermute | solution.py:393
  (34 shorter events, 5.9 us)
Async XLA Ops:
  0.0 19.1 %collective-permute-start.2 = (bf16[128,128,128]{2,1,0:T(8,128)(2,1)}, bf16[128,128,128]{2,1,0:T(8,128)(2,1)}, u32[]{:S(2)}, u32[]{:S(2)}) collective-permute-start(bf16[128,128,128]{2,1,0:T(8,128)(2,1)} %refs_8_.1), channel_id=1, source_target_pairs={{0,1},{1,0},{2,3},{3,2},{4,5},{5,4},{6,7},{7,6},{8,9},{9,8},{10,11... | collective-permute-start | bytes 12582920 | tf_op jit(solution)/shard_map/ppermute | solution.py:393
  2.5 9.3 %collective-permute-start = (bf16[1152,128]{1,0:T(8,128)(2,1)}, bf16[1152,128]{1,0:T(8,128)(2,1)S(1)}, u32[]{:S(2)}, u32[]{:S(2)}) collective-permute-start(bf16[1152,128]{1,0:T(8,128)(2,1)} %get-tuple-element.32.refs_0_), channel_id=1, source_target_pairs={{0,4},{1,3},{4,8},{5,1},{8,12},{9,5},{12,14},{13,9},{14,10},{15,13... | collective-permute-start | bytes 884744 | tf_op jit(solution)/shard_map/ppermute | solution.py:393
  5.0 10.1 %collective-permute-start.4 = (bf16[1152,128]{1,0:T(8,128)(2,1)}, bf16[1152,128]{1,0:T(8,128)(2,1)S(1)}, u32[]{:S(2)}, u32[]{:S(2)}) collective-permute-start(bf16[1152,128]{1,0:T(8,128)(2,1)} %get-tuple-element.32.refs_0_), channel_id=1, source_target_pairs={{0,3},{1,4},{4,1},{5,8},{8,5},{9,12},{12,9},{13,14},{14,13},{15,10... | collective-permute-start | bytes 884744 | tf_op jit(solution)/shard_map/ppermute | solution.py:393
  11.8 7.4 %collective-permute-start.1 = (bf16[1152,128]{1,0:T(8,128)(2,1)S(1)}, bf16[1152,128]{1,0:T(8,128)(2,1)S(1)}, u32[]{:S(2)}, u32[]{:S(2)}) collective-permute-start(bf16[1152,128]{1,0:T(8,128)(2,1)S(1)} %collective-permute-done.refs_1_), channel_id=1, source_target_pairs={{0,4},{1,3},{4,8},{5,1},{8,12},{9,5},{12,14},{13,9},{14,10},{15,13... | collective-permute-start | bytes 884744 | tf_op jit(solution)/shard_map/ppermute | solution.py:393
  14.1 2.7 %collective-permute-start.3 = (s32[8,128]{1,0:T(8,128)}, s32[8,128]{1,0:T(8,128)S(1)}, u32[]{:S(2)}, u32[]{:S(2)}) collective-permute-start(s32[8,128]{1,0:T(8,128)} %get-tuple-element.35.list_ref), channel_id=1, source_target_pairs={{0,1},{1,0},{2,3},{3,2},{4,5},{5,4},{6,7},{7,6},{8,9},{9,8},{10,11... | collective-permute-start | bytes 12296 | tf_op jit(solution)/shard_map/ppermute | solution.py:393
  14.1 35.7 %copy-start.2 = (bf16[16,16,128]{2,1,0:T(8,128)(2,1)S(1)}, bf16[16,16,128]{2,1,0:T(8,128)(2,1)}, u32[]{:S(2)}) copy-start(bf16[16,16,128]{2,1,0:T(8,128)(2,1)} %refs_7_.1) | copy-start | bytes 196612
  14.1 35.7 %copy-start.4 = (s32[256,1]{0,1:T(1,128)S(1)}, s32[256,1]{0,1:T(1,128)}, u32[]{:S(2)}) copy-start(s32[256,1]{0,1:T(1,128)} %param.18) | copy-start | bytes 3076
  14.1 35.7 %copy-start.5 = (s32[256]{0:T(256)S(1)}, s32[256]{0:T(256)}, u32[]{:S(2)}) copy-start(s32[256]{0:T(256)} %param.19) | copy-start | bytes 3076
  15.1 34.7 %copy-start.3 = (s32[256]{0:T(256)S(1)}, s32[256]{0:T(256)}, u32[]{:S(2)}) copy-start(s32[256]{0:T(256)} %param.17) | copy-start | bytes 3076
  15.2 7.1 %collective-permute-start.5 = (bf16[1152,128]{1,0:T(8,128)(2,1)S(1)}, bf16[1152,128]{1,0:T(8,128)(2,1)S(1)}, u32[]{:S(2)}, u32[]{:S(2)}) collective-permute-start(bf16[1152,128]{1,0:T(8,128)(2,1)S(1)} %collective-permute-done.4.refs_2_), channel_id=1, source_target_pairs={{0,4},{1,3},{4,8},{5,1},{8,12},{9,5},{12,14},{13,9},{14,10},{15,13... | collective-permute-start | bytes 884744 | tf_op jit(solution)/shard_map/ppermute | solution.py:393
  19.1 6.7 %collective-permute-start.6 = (bf16[1152,128]{1,0:T(8,128)(2,1)S(1)}, bf16[1152,128]{1,0:T(8,128)(2,1)S(1)}, u32[]{:S(2)}, u32[]{:S(2)}) collective-permute-start(bf16[1152,128]{1,0:T(8,128)(2,1)S(1)} %collective-permute-done.1.refs_3_), channel_id=1, source_target_pairs={{0,4},{1,3},{4,8},{5,1},{8,12},{9,5},{12,14},{13,9},{14,10},{15,13... | collective-permute-start | bytes 884744 | tf_op jit(solution)/shard_map/ppermute | solution.py:393
  22.3 6.7 %collective-permute-start.7 = (bf16[1152,128]{1,0:T(8,128)(2,1)S(1)}, bf16[1152,128]{1,0:T(8,128)(2,1)S(1)}, u32[]{:S(2)}, u32[]{:S(2)}) collective-permute-start(bf16[1152,128]{1,0:T(8,128)(2,1)S(1)} %collective-permute-done.5.refs_4_), channel_id=1, source_target_pairs={{0,4},{1,3},{4,8},{5,1},{8,12},{9,5},{12,14},{13,9},{14,10},{15,13... | collective-permute-start | bytes 884744 | tf_op jit(solution)/shard_map/ppermute | solution.py:393
  25.9 6.7 %collective-permute-start.8 = (bf16[1152,128]{1,0:T(8,128)(2,1)S(1)}, bf16[1152,128]{1,0:T(8,128)(2,1)S(1)}, u32[]{:S(2)}, u32[]{:S(2)}) collective-permute-start(bf16[1152,128]{1,0:T(8,128)(2,1)S(1)} %collective-permute-done.6.refs_5_), channel_id=1, source_target_pairs={{0,4},{1,3},{4,8},{5,1},{8,12},{9,5},{12,14},{13,9},{14,10},{15,13... | collective-permute-start | bytes 884744 | tf_op jit(solution)/shard_map/ppermute | solution.py:393
  32.6 1.0 %copy-start = (bf16[1152,128]{1,0:T(8,128)(2,1)S(1)}, bf16[1152,128]{1,0:T(8,128)(2,1)}, u32[]{:S(2)}) copy-start(bf16[1152,128]{1,0:T(8,128)(2,1)} %get-tuple-element.32.refs_0_) | copy-start | bytes 884740
  33.5 0.7 copy-start.1
  43.9 1.6 %collective-permute-start.10 = (bf16[16,64,128]{2,1,0:T(8,128)(2,1)S(1)}, bf16[16,64,128]{2,1,0:T(8,128)(2,1)S(1)}, u32[]{:S(2)}, u32[]{:S(2)}) collective-permute-start(bf16[16,64,128]{2,1,0:T(8,128)(2,1)S(1)} %get-tuple-element.42), channel_id=1, source_target_pairs={{0,1},{1,0},{2,3},{3,2},{4,5},{5,4},{6,7},{7,6},{8,9},{9,8},{10,11... | collective-permute-start | bytes 786440 | tf_op jit(solution)/shard_map/ppermute | solution.py:393
  43.9 1.9 %collective-permute-start.11 = (bf16[16,64,128]{2,1,0:T(8,128)(2,1)S(1)}, bf16[16,64,128]{2,1,0:T(8,128)(2,1)S(1)}, u32[]{:S(2)}, u32[]{:S(2)}) collective-permute-start(bf16[16,64,128]{2,1,0:T(8,128)(2,1)S(1)} %get-tuple-element.43), channel_id=1, source_target_pairs={{0,1},{1,0},{2,3},{3,2},{4,5},{5,4},{6,7},{7,6},{8,9},{9,8},{10,11... | collective-permute-start | bytes 786440 | tf_op jit(solution)/shard_map/ppermute | solution.py:393
  46.0 7.2 %collective-permute-start.13 = (bf16[96,64,128]{2,1,0:T(8,128)(2,1)S(1)}, bf16[96,64,128]{2,1,0:T(8,128)(2,1)S(1)}, u32[]{:S(2)}, u32[]{:S(2)}) collective-permute-start(bf16[96,64,128]{2,1,0:T(8,128)(2,1)S(1)} %get-tuple-element.48), channel_id=1, source_target_pairs={{0,1},{1,0},{2,3},{3,2},{4,5},{5,4},{6,7},{7,6},{8,9},{9,8},{10,11... | collective-permute-start | bytes 4718600 | tf_op jit(solution)/shard_map/ppermute | solution.py:393
  46.2 3.6 %collective-permute-start.9 = (bf16[1024,128]{1,0:T(8,128)(2,1)S(1)}, bf16[1024,128]{1,0:T(8,128)(2,1)S(1)}, u32[]{:S(2)}, u32[]{:S(2)}) collective-permute-start(bf16[1024,128]{1,0:T(8,128)(2,1)S(1)} %get-tuple-element.39.refs_0_), channel_id=1, source_target_pairs={{0,1},{1,0},{2,3},{3,2},{4,5},{5,4},{6,7},{7,6},{8,9},{9,8},{10,11... | collective-permute-start | bytes 786440 | tf_op jit(solution)/shard_map/ppermute | solution.py:393
  46.6 6.7 %collective-permute-start.12 = (bf16[16,64,128]{2,1,0:T(8,128)(2,1)S(1)}, bf16[16,64,128]{2,1,0:T(8,128)(2,1)S(1)}, u32[]{:S(2)}, u32[]{:S(2)}) collective-permute-start(bf16[16,64,128]{2,1,0:T(8,128)(2,1)S(1)} %get-tuple-element.44), channel_id=1, source_target_pairs={{0,4},{1,3},{4,8},{5,1},{8,12},{9,5},{12,14},{13,9},{14,10},{15,13... | collective-permute-start | bytes 786440 | tf_op jit(solution)/shard_map/ppermute | solution.py:393
  48.0 8.0 %collective-permute-start.15 = (bf16[16,64,128]{2,1,0:T(8,128)(2,1)S(1)}, bf16[16,64,128]{2,1,0:T(8,128)(2,1)S(1)}, u32[]{:S(2)}, u32[]{:S(2)}) collective-permute-start(bf16[16,64,128]{2,1,0:T(8,128)(2,1)S(1)} %get-tuple-element.45), channel_id=1, source_target_pairs={{0,4},{1,3},{4,8},{5,1},{8,12},{9,5},{12,14},{13,9},{14,10},{15,13... | collective-permute-start | bytes 786440 | tf_op jit(solution)/shard_map/ppermute | solution.py:393
  53.3 6.4 %collective-permute-start.14 = (bf16[16,64,128]{2,1,0:T(8,128)(2,1)S(1)}, bf16[16,64,128]{2,1,0:T(8,128)(2,1)S(1)}, u32[]{:S(2)}, u32[]{:S(2)}) collective-permute-start(bf16[16,64,128]{2,1,0:T(8,128)(2,1)S(1)} %add_convert_fusion.5), channel_id=1, source_target_pairs={{0,4},{1,3},{4,8},{5,1},{8,12},{9,5},{12,14},{13,9},{14,10},{15,13... | collective-permute-start | bytes 786440 | tf_op jit(solution)/shard_map/ppermute | solution.py:393
  56.1 6.4 %collective-permute-start.17 = (bf16[16,64,128]{2,1,0:T(8,128)(2,1)S(1)}, bf16[16,64,128]{2,1,0:T(8,128)(2,1)S(1)}, u32[]{:S(2)}, u32[]{:S(2)}) collective-permute-start(bf16[16,64,128]{2,1,0:T(8,128)(2,1)S(1)} %add_convert_fusion.4), channel_id=1, source_target_pairs={{0,4},{1,3},{4,8},{5,1},{8,12},{9,5},{12,14},{13,9},{14,10},{15,13... | collective-permute-start | bytes 786440 | tf_op jit(solution)/shard_map/ppermute | solution.py:393
  59.8 6.4 %collective-permute-start.16 = (bf16[16,64,128]{2,1,0:T(8,128)(2,1)S(1)}, bf16[16,64,128]{2,1,0:T(8,128)(2,1)S(1)}, u32[]{:S(2)}, u32[]{:S(2)}) collective-permute-start(bf16[16,64,128]{2,1,0:T(8,128)(2,1)S(1)} %add_convert_fusion.3), channel_id=1, source_target_pairs={{0,4},{1,3},{4,8},{5,1},{8,12},{9,5},{12,14},{13,9},{14,10},{15,13... | collective-permute-start | bytes 786440 | tf_op jit(solution)/shard_map/ppermute | solution.py:393
  62.7 6.4 %collective-permute-start.19 = (bf16[16,64,128]{2,1,0:T(8,128)(2,1)S(1)}, bf16[16,64,128]{2,1,0:T(8,128)(2,1)S(1)}, u32[]{:S(2)}, u32[]{:S(2)}) collective-permute-start(bf16[16,64,128]{2,1,0:T(8,128)(2,1)S(1)} %add_convert_fusion.2), channel_id=1, source_target_pairs={{0,4},{1,3},{4,8},{5,1},{8,12},{9,5},{12,14},{13,9},{14,10},{15,13... | collective-permute-start | bytes 786440 | tf_op jit(solution)/shard_map/ppermute | solution.py:393
  66.4 6.4 %collective-permute-start.18 = (bf16[16,64,128]{2,1,0:T(8,128)(2,1)S(1)}, bf16[16,64,128]{2,1,0:T(8,128)(2,1)S(1)}, u32[]{:S(2)}, u32[]{:S(2)}) collective-permute-start(bf16[16,64,128]{2,1,0:T(8,128)(2,1)S(1)} %add_convert_fusion.1), channel_id=1, source_target_pairs={{0,4},{1,3},{4,8},{5,1},{8,12},{9,5},{12,14},{13,9},{14,10},{15,13... | collective-permute-start | bytes 786440 | tf_op jit(solution)/shard_map/ppermute | solution.py:393
  69.1 3.9 %collective-permute-start.20 = (bf16[16,64,128]{2,1,0:T(8,128)(2,1)S(1)}, bf16[16,64,128]{2,1,0:T(8,128)(2,1)S(1)}, u32[]{:S(2)}, u32[]{:S(2)}) collective-permute-start(bf16[16,64,128]{2,1,0:T(8,128)(2,1)S(1)} %collective-permute-done.19), channel_id=1, source_target_pairs={{0,1},{1,0},{2,3},{3,2},{4,5},{5,4},{6,7},{7,6},{8,9},{9,8},{10,11... | collective-permute-start | bytes 786440 | tf_op jit(solution)/shard_map/ppermute | solution.py:393

commit v8 on v7

--- a/solution.py
+++ b/solution.py
@@ -8,9 +8,10 @@
 from jax.sharding import PartitionSpec as P
 
 CHUNKS = 4
-BATCH = 8
+BATCH = 16
+LAG = 4
 PROLOGUE_VMEM = 58 << 20
-NEAR_VMEM = 44 << 20
+NEAR_VMEM = 48 << 20
 FAR_VMEM = 16 << 20
 
 
@@ -173,20 +174,16 @@
     list_ref[...] = values.astype(jnp.int32)
 
 
-def near_kernel(batch, shards, sends, list_ref, mate_list_ref, *refs):
-    shard_refs, (own_hbm, mate_hbm) = refs[:shards], refs[shards : shards + 2]
-    keep_ref, coef_ref, refs = refs[shards + 2], refs[shards + 3], refs[shards + 4 :]
-    send_refs, (columns, blocks, sums, column_sem, coef_sem, block_sem) = refs[:sends], refs[sends:]
+def near_kernel(batch, lag, shards, sends, list_ref, *refs):
+    shard_refs, (own_hbm, mate_hbm, sums, coef_ref) = refs[:shards], refs[shards : shards + 4]
+    refs = refs[shards + 4 :]
+    send_refs, (columns, blocks, column_sem, coef_sem, block_sem) = refs[:sends], refs[sends:]
     directions = sums.shape[1]
     span = columns.shape[0] // shards
     tail = coef_ref.shape[0] // shards
-    chunk = blocks.shape[1] // CHUNKS
-
-    def load(source, half, c):
-        at = pl.ds(c * chunk, chunk)
-        return pltpu.make_async_copy(
-            source.at[at], blocks.at[half, at], block_sem.at[half * CHUNKS + c]
-        )
+    stored = blocks.shape[1]
+    chunk = stored // CHUNKS
+    dummy = sums.shape[0] - 1
 
     copies = [
         pltpu.make_async_copy(
@@ -196,6 +193,12 @@
     ]
     for copy in copies:
         copy.start()
+    for half, source in enumerate((own_hbm, mate_hbm)):
+        for c in range(CHUNKS):
+            at = pl.ds(c * chunk, chunk)
+            pltpu.make_async_copy(
+                source.at[at], blocks.at[half, at], block_sem.at[half * CHUNKS + c]
+            ).start()
     tails = [
         pltpu.make_async_copy(
             ref.at[pl.ds(span, tail)], coef_ref.at[pl.ds(k * tail, tail)], coef_sem.at[k]
@@ -204,11 +207,6 @@
     ]
     for copy in tails:
         copy.start()
-    for half, source in enumerate((own_hbm, mate_hbm)):
-        for c in range(CHUNKS):
-            load(source, half, c).start()
-
-    dummy = sums.shape[0] - 1
 
     def clear(i, carry):
         sums[i] = jnp.zeros(sums.shape[1:], sums.dtype)
@@ -217,43 +215,53 @@
     lax.fori_loop(0, dummy, clear, 0)
     for copy in copies:
         copy.wait()
-    for half, (source, ref) in enumerate(((own_hbm, list_ref), (mate_hbm, mate_list_ref))):
-        swap = half * (dummy // 2)
-
-        def run(c, carry, half=half, source=source, ref=ref, swap=swap):
-            load(source, half, c).wait()
-            begin, end = ref[3 + half, c], ref[3 + half, c + 1]
-
-            def body(step, carry):
-                first = begin + step * batch
-                products = []
-                for i in range(batch):
-                    at = jnp.minimum(first + i, end - 1)
-                    products.append(
-                        lax.dot_general(
-                            columns[
-                                pl.ds(pl.multiple_of(ref[2, at] * directions, directions), directions)
-                            ],
-                            blocks[half, ref[0, at]],
-                            (((1,), (1,)), ((), ())),
-                            preferred_element_type=jnp.float32,
-                        )
-                    )
-                for i in range(batch):
-                    at = jnp.minimum(first + i, end - 1)
-                    at = jnp.where(first + i < end, ref[1, at] ^ swap, dummy)
-                    sums[at] = sums[at] + products[i]
-                return carry
-
-            return lax.fori_loop(0, (end - begin + batch - 1) // batch, body, carry)
-
-        lax.fori_loop(0, CHUNKS, run, 0)
-
-    def keep(i, carry):
-        keep_ref[i] = sums[i]
+
+    here = list_ref[3, CHUNKS]
+    there = list_ref[8 + 4, 0]
+    total = here + stored - there
+
+    def entry(j):
+        j = jnp.minimum(j, total - 1)
+        half = (j >= here).astype(jnp.int32)
+        return half, half * 8, j + half * (there - here)
+
+    def wait(c, carry):
+        at = pl.ds(0, chunk)
+        pltpu.make_async_copy(own_hbm.at[at], blocks.at[0, at], block_sem.at[c]).wait()
         return carry
 
-    lax.fori_loop(0, dummy // 2, keep, 0, unroll=2)
+    def body(step, ready):
+        first = step * batch
+        half, row, at = entry(first + batch - 1)
+        needed = half * CHUNKS + list_ref[row, at] // chunk + 1
+        lax.fori_loop(ready, needed, wait, 0)
+        products = []
+
+        def add(i):
+            half, row, at = entry(first + i)
+            place = list_ref[row + 1, at] ^ (half * (dummy // 2))
+            place = jnp.where(first + i < total, place, dummy)
+            sums[place] = sums[place] + products[i]
+
+        for i in range(batch):
+            half, row, at = entry(first + i)
+            start = pl.multiple_of(list_ref[row + 2, at] * directions, directions)
+            products.append(
+                lax.dot_general(
+                    columns[pl.ds(start, directions)],
+                    blocks[half, list_ref[row, at]],
+                    (((1,), (1,)), ((), ())),
+                    preferred_element_type=jnp.float32,
+                )
+            )
+            if i >= lag:
+                add(i - lag)
+        for i in range(batch - lag, batch):
+            add(i)
+        return jnp.maximum(ready, needed)
+
+    ready = lax.fori_loop(0, (total + batch - 1) // batch, body, 0)
+    lax.fori_loop(ready, 2 * CHUNKS, wait, 0)
     at = dummy // 2
     for send_ref in send_refs:
 
@@ -326,9 +334,9 @@
 def ring_pairs(count):
     chips = count // 2
     cores = [(p, c) for p in range(chips) for c in range(2)]
-    ahead = [(ring_device(p, c, chips), ring_device(p + 1 - 2 * c, c, chips)) for p, c in cores]
+    ahead = [(ring_device(p, c, chips), ring_device(p - 1 + 2 * c, c, chips)) for p, c in cores]
     cross = [
-        (ring_device(p, c, chips), ring_device(p - 1 + 2 * c, 1 - c, chips)) for p, c in cores
+        (ring_device(p, c, chips), ring_device(p + 1 - 2 * c, 1 - c, chips)) for p, c in cores
     ]
     return ahead, cross
 
@@ -341,17 +349,17 @@
 def gather_place(device, me, count):
     chips = count // 2
     depth = chips // 2
-    back = (1 - 2 * (me & 1)) * (ring_place(me, chips) - ring_place(device, chips))
+    back = (2 * (me & 1) - 1) * (ring_place(me, chips) - ring_place(device, chips))
     back = (back + chips) & (chips - 1)
     other = (device ^ me) & 1
-    here = (back < depth) & (back > 0) | ((back & (depth - 1)) == 0) & (other == 0)
+    here = (back < depth) & (back > 0) | (back == 0) & (other == 1) | (back == depth) & (other == 0)
     return jnp.where(here, jnp.where(back == 0, 0, 2 * back - 1 + other), chips)
 
 
 def scatter_place(device, me, count):
     chips = count // 2
     depth = chips // 2
-    ahead = (ring_place(device, chips) - ring_place(me, chips) + chips) & (chips - 1)
+    ahead = (ring_place(me, chips) - ring_place(device, chips) + chips) & (chips - 1)
     core = device & 1
     handler = jnp.where((ahead & (depth - 1)) == 0, core, (ahead > depth).astype(jnp.int32))
     steps = jnp.where(handler == 0, ahead, (chips - ahead) & (chips - 1))
@@ -417,14 +425,14 @@
         basis_in,
     )
     flow = [move(payload, ahead), move(payload, cross)]
-    mate_lists = move(lists, mate)
+    shards = [move(payload, mate)]
+    lists = jnp.concatenate([lists, move(lists, mate)], axis=0)
     couple = after(jnp.transpose(far_coupling, (2, 1, 0)), payload)
-    shards = [payload]
     for k in range(1, chips):
         x = 1 - k % 2
         if k == 3:
-            flow[x], mate_blocks, lists, mate_lists, couple = lax.optimization_barrier(
-                (flow[x], mate_blocks, lists, mate_lists, couple)
+            flow[x], mate_blocks, shards[0], lists, couple = lax.optimization_barrier(
+                (flow[x], mate_blocks, shards[0], lists, couple)
             )
         shards.append(flow[x])
         if k < chips - 2:
@@ -432,21 +440,20 @@
 
     pieces = [1, 1, chips - 2]
     kept, coef, *sends = pl.pallas_call(
-        functools.partial(near_kernel, BATCH, chips, len(pieces)),
+        functools.partial(near_kernel, BATCH, LAG, chips, len(pieces)),
         out_shape=[
-            jax.ShapeDtypeStruct((chips * clusters, directions, unknowns), jnp.float32),
+            jax.ShapeDtypeStruct((count * clusters + 1, directions, unknowns), jnp.float32),
             jax.ShapeDtypeStruct((chips * half * rank_k, unknowns), jnp.bfloat16),
         ]
         + [
             jax.ShapeDtypeStruct((part * clusters, directions, unknowns), jnp.bfloat16)
             for part in pieces
         ],
-        in_specs=[whole(pltpu.SMEM)] * 2 + [whole(pl.ANY)] * (chips + 2),
+        in_specs=[whole(pltpu.SMEM)] + [whole(pl.ANY)] * (chips + 2),
         out_specs=[whole()] * (2 + len(pieces)),
         scratch_shapes=[
             pltpu.VMEM((chips * base, unknowns), jnp.bfloat16),
             pltpu.VMEM((2, *near_blocks.shape), jnp.bfloat16),
-            pltpu.VMEM((count * clusters + 1, directions, unknowns), jnp.float32),
             pltpu.SemaphoreType.DMA((chips,)),
             pltpu.SemaphoreType.DMA((chips,)),
             pltpu.SemaphoreType.DMA((2 * CHUNKS,)),
@@ -458,7 +465,7 @@
             transcendentals=0,
         ),
         name="near",
-    )(lists, mate_lists, *shards, near_blocks, mate_blocks)
+    )(lists, *shards, near_blocks, mate_blocks)
 
     mates = [move(sends[0], mate), move(sends[1], mate)]
     coefs = [coef, move(coef, mate)]

time: 74.4 us -> 79.2 us (1.065)
  other arithmetic: 1.54 us -> 9.71 us
  waiting for transfers between devices: 32 us -> 24.1 us
  starting transfers between devices: 23.3 us -> 28.8 us
  local copies, waits for them, and re-layouts: 2.66 us -> 0.96 us
  Pallas kernels: 14.2 us -> 15 us
    ppermute x21 -> x22, waiting for transfers between devices: 32 us -> 24.1 us  [move(): return lax.ppermute(values, 'blk', where)]
    ppermute x21 -> x22, starting transfers between devices: 23.3 us -> 28.8 us  [move(): return lax.ppermute(values, 'blk', where)]
    convert_element_type x5, other arithmetic: 0.5 us -> 5.73 us  [add(): return (flow.astype(jnp.float32) + term(k)).astype(jnp.bfloat16)]
    unnamed x13 -> x9, local copies, waits for them, and re-layouts: 2.66 us -> 0.96 us
    convert_element_type x1, other arithmetic: 0.13 us -> 1.35 us  [stationary(): term(1).astype(jnp.bfloat16)]
    add x1, other arithmetic: 0.13 us -> 1.16 us  [stationary(): total = far + term(chips - 1) + flow[0].astype(jnp.float32)]
    pallas_call x1, Pallas kernels: 9.63 us -> 10.4 us  [stationary(): pl.pallas_call(functools.partial(near_kernel, BATCH, LAG, chips, len(piec...]
  transfers between devices with their start and end apart: 21 -> 22, of which waited for: 16 -> 12; matrix products, arithmetic and copies ran while one was open for 2% -> 11% of each run, Pallas kernels for 6% -> 6%
where the time goes in v8:
time: 79.2 us; the launch traced here: 78.7 us
  starting transfers between devices  28.8 us (36%)
  waiting for transfers between devices  24.1 us (30%)
  Pallas kernels  15 us (19%)
  other arithmetic  9.71 us (12%)
  local copies, waits for them, and re-layouts  0.96 us (1%)
    ppermute x22, starting transfers between devices, move(): return lax.ppermute(values, 'blk', where)  28.8 us
    ppermute x22, waiting for transfers between devices, move(): return lax.ppermute(values, 'blk', where)  24.1 us
    pallas_call x1, Pallas kernels, stationary(): pl.pallas_call(functools.partial(near_kernel, BATCH, LAG, chips, len(piec...  10.4 us
    convert_element_type x5, other arithmetic, add(): return (flow.astype(jnp.float32) + term(k)).astype(jnp.bfloat16)  5.73 us
    pallas_call x1, Pallas kernels, stationary(): pl.pallas_call(far_kernel, out_shape=jax.ShapeDtypeStruct((clusters, dire...  2.51 us
    pallas_call x1, Pallas kernels, stationary(): pl.pallas_call(functools.partial(prologue_kernel, count), out_shape=[jax....  2.02 us
  transfers between devices with their start and end apart: 22, of which 12 were waited for; matrix products, arithmetic and copies ran while one was open for 11% of the time, Pallas kernels for 6%

profile of v8, /device:TPU:0, one launch (start us, length us, event | category | flops | bytes accessed | tf_op | source)
XLA Modules:
  0.0 78.7 jit_solution(8535150183737559259)
XLA Ops:
  0.5 2.0 %prologue.1 = (bf16[1152,128]{1,0:T(8,128)(2,1)}, s32[8,128]{1,0:T(8,128)}) custom-call(s32[1]{0:T(128)} %bitcast.me_ref.refs_2_, s32[1,128]{1,0:T(1,128)} %bitcast.14, s32[1,128]{1,0:T(1,128)} %bitcast.15, s32[1,128]{1,0:T(1,128)} %bitcast.16, bf16[16,64,128]{2,1,0:T(8,128)(2,1)} %rhs_ref.1, bf16[16,16,128]{2,1,0:T(8,128)(2,1)} %basis_ref.1), custom_call_target="tpu_custom_call" | custom-call | tf_op jit(solution)/shard_map/prologue/pallas_call | solution.py:409
  2.5 2.5 %collective-permute-start = (bf16[1152,128]{1,0:T(8,128)(2,1)}, bf16[1152,128]{1,0:T(8,128)(2,1)S(1)}, u32[]{:S(2)}, u32[]{:S(2)}) collective-permute-start(bf16[1152,128]{1,0:T(8,128)(2,1)} %get-tuple-element.32), channel_id=1, source_target_pairs={{0,2},{1,5},{4,0},{5,9},{8,4},{9,13},{12,8},{13,15},{14,12},{15,11... | collective-permute-start | bytes 884744 | tf_op jit(solution)/shard_map/ppermute | solution.py:401
  5.0 1.5 %collective-permute-start.5 = (bf16[1152,128]{1,0:T(8,128)(2,1)}, bf16[1152,128]{1,0:T(8,128)(2,1)S(1)}, u32[]{:S(2)}, u32[]{:S(2)}) collective-permute-start(bf16[1152,128]{1,0:T(8,128)(2,1)} %get-tuple-element.32), channel_id=1, source_target_pairs={{0,5},{1,2},{4,9},{5,0},{8,13},{9,4},{12,15},{13,8},{14,11},{15,12... | collective-permute-start | bytes 884744 | tf_op jit(solution)/shard_map/ppermute | solution.py:401
  6.7 5.0 %collective-permute-done.refs_1_ = bf16[1152,128]{1,0:T(8,128)(2,1)S(1)} collective-permute-done((bf16[1152,128]{1,0:T(8,128)(2,1)}, bf16[1152,128]{1,0:T(8,128)(2,1)S(1)}, u32[]{:S(2)}, u32[]{:S(2)}) %collective-permute-start) | collective-permute-done | bytes 294944 | tf_op jit(solution)/shard_map/ppermute | solution.py:401
  11.7 2.4 %collective-permute-start.1 = (bf16[1152,128]{1,0:T(8,128)(2,1)S(1)}, bf16[1152,128]{1,0:T(8,128)(2,1)S(1)}, u32[]{:S(2)}, u32[]{:S(2)}) collective-permute-start(bf16[1152,128]{1,0:T(8,128)(2,1)S(1)} %collective-permute-done.refs_1_), channel_id=1, source_target_pairs={{0,2},{1,5},{4,0},{5,9},{8,4},{9,13},{12,8},{13,15},{14,12},{15,11... | collective-permute-start | bytes 884744 | tf_op jit(solution)/shard_map/ppermute | solution.py:401
  16.2 1.6 %collective-permute-start.6 = (bf16[1152,128]{1,0:T(8,128)(2,1)S(1)}, bf16[1152,128]{1,0:T(8,128)(2,1)S(1)}, u32[]{:S(2)}, u32[]{:S(2)}) collective-permute-start(bf16[1152,128]{1,0:T(8,128)(2,1)S(1)} %collective-permute-done.5.refs_2_), channel_id=1, source_target_pairs={{0,2},{1,5},{4,0},{5,9},{8,4},{9,13},{12,8},{13,15},{14,12},{15,11... | collective-permute-start | bytes 884744 | tf_op jit(solution)/shard_map/ppermute | solution.py:401
  17.8 1.4 %collective-permute-done.1.refs_3_ = bf16[1152,128]{1,0:T(8,128)(2,1)S(1)} collective-permute-done((bf16[1152,128]{1,0:T(8,128)(2,1)S(1)}, bf16[1152,128]{1,0:T(8,128)(2,1)S(1)}, u32[]{:S(2)}, u32[]{:S(2)}) %collective-permute-start.1) | collective-permute-done | bytes 294944 | tf_op jit(solution)/shard_map/ppermute | solution.py:401
  19.2 1.6 %collective-permute-start.7 = (bf16[1152,128]{1,0:T(8,128)(2,1)S(1)}, bf16[1152,128]{1,0:T(8,128)(2,1)S(1)}, u32[]{:S(2)}, u32[]{:S(2)}) collective-permute-start(bf16[1152,128]{1,0:T(8,128)(2,1)S(1)} %collective-permute-done.1.refs_3_), channel_id=1, source_target_pairs={{0,2},{1,5},{4,0},{5,9},{8,4},{9,13},{12,8},{13,15},{14,12},{15,11... | collective-permute-start | bytes 884744 | tf_op jit(solution)/shard_map/ppermute | solution.py:401
  20.8 2.1 %collective-permute-done.6.refs_4_ = bf16[1152,128]{1,0:T(8,128)(2,1)S(1)} collective-permute-done((bf16[1152,128]{1,0:T(8,128)(2,1)S(1)}, bf16[1152,128]{1,0:T(8,128)(2,1)S(1)}, u32[]{:S(2)}, u32[]{:S(2)}) %collective-permute-start.6) | collective-permute-done | bytes 294944 | tf_op jit(solution)/shard_map/ppermute | solution.py:401
  22.9 1.6 %collective-permute-start.8 = (bf16[1152,128]{1,0:T(8,128)(2,1)S(1)}, bf16[1152,128]{1,0:T(8,128)(2,1)S(1)}, u32[]{:S(2)}, u32[]{:S(2)}) collective-permute-start(bf16[1152,128]{1,0:T(8,128)(2,1)S(1)} %collective-permute-done.6.refs_4_), channel_id=1, source_target_pairs={{0,2},{1,5},{4,0},{5,9},{8,4},{9,13},{12,8},{13,15},{14,12},{15,11... | collective-permute-start | bytes 884744 | tf_op jit(solution)/shard_map/ppermute | solution.py:401
  24.5 1.6 %collective-permute-done.7.refs_5_ = bf16[1152,128]{1,0:T(8,128)(2,1)S(1)} collective-permute-done((bf16[1152,128]{1,0:T(8,128)(2,1)S(1)}, bf16[1152,128]{1,0:T(8,128)(2,1)S(1)}, u32[]{:S(2)}, u32[]{:S(2)}) %collective-permute-start.7) | collective-permute-done | bytes 294944 | tf_op jit(solution)/shard_map/ppermute | solution.py:401
  26.1 1.6 %collective-permute-start.9 = (bf16[1152,128]{1,0:T(8,128)(2,1)S(1)}, bf16[1152,128]{1,0:T(8,128)(2,1)S(1)}, u32[]{:S(2)}, u32[]{:S(2)}) collective-permute-start(bf16[1152,128]{1,0:T(8,128)(2,1)S(1)} %collective-permute-done.7.refs_5_), channel_id=1, source_target_pairs={{0,2},{1,5},{4,0},{5,9},{8,4},{9,13},{12,8},{13,15},{14,12},{15,11... | collective-permute-start | bytes 884744 | tf_op jit(solution)/shard_map/ppermute | solution.py:401
  27.7 2.0 %collective-permute-done.8.refs_6_ = bf16[1152,128]{1,0:T(8,128)(2,1)S(1)} collective-permute-done((bf16[1152,128]{1,0:T(8,128)(2,1)S(1)}, bf16[1152,128]{1,0:T(8,128)(2,1)S(1)}, u32[]{:S(2)}, u32[]{:S(2)}) %collective-permute-start.8) | collective-permute-done | bytes 294944 | tf_op jit(solution)/shard_map/ppermute | solution.py:401
  29.7 3.2 %collective-permute-done.9.refs_7_ = bf16[1152,128]{1,0:T(8,128)(2,1)S(1)} collective-permute-done((bf16[1152,128]{1,0:T(8,128)(2,1)S(1)}, bf16[1152,128]{1,0:T(8,128)(2,1)S(1)}, u32[]{:S(2)}, u32[]{:S(2)}) %collective-permute-start.9) | collective-permute-done | bytes 294944 | tf_op jit(solution)/shard_map/ppermute | solution.py:401
  32.8 10.4 %near.1 = (f32[257,64,128]{2,1,0:T(8,128)}, bf16[1024,128]{1,0:T(8,128)(2,1)S(1)}, bf16[16,64,128]{2,1,0:T(8,128)(2,1)S(1)}, bf16[16,64,128]{2,1,0:T(8,128)(2,1)S(1)}, bf16[96,64,128]{2,1,0:T(8,128)(2,1)S(1)}) custom-call(s32[16,128]{1,0:T(8,128)S(1)} %pad_add_fusion.list_ref, bf16[1152,128]{1,0:T(8,128)(2,1)S(1)} %collective-permute-done.3.refs_0_, ...), custom_call_target="tpu_custom_call" | custom-call | flops 2147483648 | bytes 16777216 | tf_op jit(solution)/shard_map/near/pallas_call | solution.py:442
  45.2 1.3 %add_convert_fusion.6 = (bf16[16,64,128]{2,1,0:T(8,128)(2,1)S(1)}, bf16[16,64,128]{2,1,0:T(8,128)(2,1)S(1)}) fusion(bf16[16,64,128]{2,1,0:T(8,128)(2,1)S(1)} %collective-permute-done.12, f32[257,64,128]{2,1,0:T(8,128)} %get-tuple-element.41, bf16[16,64,128]{2,1,0:T(8,128)(2,1)S(1)} %collective-permute-done.11), kind=kLoop, calls=%fused_computation.7 | loop fusion | flops 786432 | bytes 2097152 | tf_op jit(solution)/shard_map/convert_element_type | solution.py:485
  47.2 2.6 %collective-permute-start.13 = (bf16[16,64,128]{2,1,0:T(8,128)(2,1)S(1)}, bf16[16,64,128]{2,1,0:T(8,128)(2,1)S(1)}, u32[]{:S(2)}, u32[]{:S(2)}) collective-permute-start(bf16[16,64,128]{2,1,0:T(8,128)(2,1)S(1)} %get-tuple-element.44), channel_id=1, source_target_pairs={{0,2},{1,5},{4,0},{5,9},{8,4},{9,13},{12,8},{13,15},{14,12},{15,11... | collective-permute-start | bytes 786440 | tf_op jit(solution)/shard_map/ppermute | solution.py:401
  49.7 1.7 %collective-permute-start.16 = (bf16[16,64,128]{2,1,0:T(8,128)(2,1)S(1)}, bf16[16,64,128]{2,1,0:T(8,128)(2,1)S(1)}, u32[]{:S(2)}, u32[]{:S(2)}) collective-permute-start(bf16[16,64,128]{2,1,0:T(8,128)(2,1)S(1)} %get-tuple-element.45), channel_id=1, source_target_pairs={{0,2},{1,5},{4,0},{5,9},{8,4},{9,13},{12,8},{13,15},{14,12},{15,11... | collective-permute-start | bytes 786440 | tf_op jit(solution)/shard_map/ppermute | solution.py:401
  51.5 2.5 %far.1 = f32[16,64,128]{2,1,0:T(8,128)S(1)} custom-call(bf16[1024,128]{1,0:T(8,128)(2,1)S(1)} %get-tuple-element.39.refs_0_, bf16[1024,128]{1,0:T(8,128)(2,1)S(1)} %collective-permute-done.10.refs_1_, s32[1]{0:T(128)} %bitcast.me_ref.refs_2_, bf16[16,16,256]{2,1,0:T(8,128)(2,1)S(1)} %bitcast.10, s32[1,256]{1,0:T(1,128)S(1)} %bitcast.11, ...), custom_call_target="tpu_custom_call" | custom-call | flops 536870912 | bytes 8388608 | tf_op jit(solution)/shard_map/far/pallas_call | solution.py:489
  54.0 1.1 %add_convert_fusion.5 = bf16[16,64,128]{2,1,0:T(8,128)(2,1)S(1)} fusion(f32[257,64,128]{2,1,0:T(8,128)} %get-tuple-element.41, bf16[16,64,128]{2,1,0:T(8,128)(2,1)S(1)} %collective-permute-done.13, bf16[96,64,128]{2,1,0:T(8,128)(2,1)S(1)} %collective-permute-done.14), kind=kLoop, calls=%fused_computation.6 | loop fusion | flops 655360 | bytes 1310720 | tf_op jit(solution)/shard_map/convert_element_type | solution.py:483
  55.2 2.1 %collective-permute-start.15 = (bf16[16,64,128]{2,1,0:T(8,128)(2,1)S(1)}, bf16[16,64,128]{2,1,0:T(8,128)(2,1)S(1)}, u32[]{:S(2)}, u32[]{:S(2)}) collective-permute-start(bf16[16,64,128]{2,1,0:T(8,128)(2,1)S(1)} %add_convert_fusion.5), channel_id=1, source_target_pairs={{0,2},{1,5},{4,0},{5,9},{8,4},{9,13},{12,8},{13,15},{14,12},{15,11... | collective-permute-start | bytes 786440 | tf_op jit(solution)/shard_map/ppermute | solution.py:401
  58.5 1.8 %collective-permute-start.18 = (bf16[16,64,128]{2,1,0:T(8,128)(2,1)S(1)}, bf16[16,64,128]{2,1,0:T(8,128)(2,1)S(1)}, u32[]{:S(2)}, u32[]{:S(2)}) collective-permute-start(bf16[16,64,128]{2,1,0:T(8,128)(2,1)S(1)} %add_convert_fusion.4), channel_id=1, source_target_pairs={{0,2},{1,5},{4,0},{5,9},{8,4},{9,13},{12,8},{13,15},{14,12},{15,11... | collective-permute-start | bytes 786440 | tf_op jit(solution)/shard_map/ppermute | solution.py:401
  60.2 1.4 %collective-permute-done.15 = bf16[16,64,128]{2,1,0:T(8,128)(2,1)S(1)} collective-permute-done((bf16[16,64,128]{2,1,0:T(8,128)(2,1)S(1)}, bf16[16,64,128]{2,1,0:T(8,128)(2,1)S(1)}, u32[]{:S(2)}, u32[]{:S(2)}) %collective-permute-start.15) | collective-permute-done | bytes 262176 | tf_op jit(solution)/shard_map/ppermute | solution.py:401
  61.6 1.1 %add_convert_fusion.3 = bf16[16,64,128]{2,1,0:T(8,128)(2,1)S(1)} fusion(f32[257,64,128]{2,1,0:T(8,128)} %get-tuple-element.41, bf16[16,64,128]{2,1,0:T(8,128)(2,1)S(1)} %collective-permute-done.15, bf16[96,64,128]{2,1,0:T(8,128)(2,1)S(1)} %collective-permute-done.14), kind=kLoop, calls=%fused_computation.4 | loop fusion | flops 655360 | bytes 1310720 | tf_op jit(solution)/shard_map/convert_element_type | solution.py:483
  62.7 2.1 %collective-permute-start.17 = (bf16[16,64,128]{2,1,0:T(8,128)(2,1)S(1)}, bf16[16,64,128]{2,1,0:T(8,128)(2,1)S(1)}, u32[]{:S(2)}, u32[]{:S(2)}) collective-permute-start(bf16[16,64,128]{2,1,0:T(8,128)(2,1)S(1)} %add_convert_fusion.3), channel_id=1, source_target_pairs={{0,2},{1,5},{4,0},{5,9},{8,4},{9,13},{12,8},{13,15},{14,12},{15,11... | collective-permute-start | bytes 786440 | tf_op jit(solution)/shard_map/ppermute | solution.py:401
  64.9 1.1 %add_convert_fusion.2 = bf16[16,64,128]{2,1,0:T(8,128)(2,1)S(1)} fusion(f32[257,64,128]{2,1,0:T(8,128)} %get-tuple-element.41, bf16[16,64,128]{2,1,0:T(8,128)(2,1)S(1)} %collective-permute-done.18, bf16[96,64,128]{2,1,0:T(8,128)(2,1)S(1)} %collective-permute-done.14), kind=kLoop, calls=%fused_computation.3 | loop fusion | flops 655360 | bytes 1310720 | tf_op jit(solution)/shard_map/convert_element_type | solution.py:483
  66.0 1.8 %collective-permute-start.20 = (bf16[16,64,128]{2,1,0:T(8,128)(2,1)S(1)}, bf16[16,64,128]{2,1,0:T(8,128)(2,1)S(1)}, u32[]{:S(2)}, u32[]{:S(2)}) collective-permute-start(bf16[16,64,128]{2,1,0:T(8,128)(2,1)S(1)} %add_convert_fusion.2), channel_id=1, source_target_pairs={{0,2},{1,5},{4,0},{5,9},{8,4},{9,13},{12,8},{13,15},{14,12},{15,11... | collective-permute-start | bytes 786440 | tf_op jit(solution)/shard_map/ppermute | solution.py:401
  67.8 1.4 %collective-permute-done.17 = bf16[16,64,128]{2,1,0:T(8,128)(2,1)S(1)} collective-permute-done((bf16[16,64,128]{2,1,0:T(8,128)(2,1)S(1)}, bf16[16,64,128]{2,1,0:T(8,128)(2,1)S(1)}, u32[]{:S(2)}, u32[]{:S(2)}) %collective-permute-start.17) | collective-permute-done | bytes 262176 | tf_op jit(solution)/shard_map/ppermute | solution.py:401
  69.2 1.1 %add_convert_fusion.1 = bf16[16,64,128]{2,1,0:T(8,128)(2,1)S(1)} fusion(f32[257,64,128]{2,1,0:T(8,128)} %get-tuple-element.41, bf16[16,64,128]{2,1,0:T(8,128)(2,1)S(1)} %collective-permute-done.17, bf16[96,64,128]{2,1,0:T(8,128)(2,1)S(1)} %collective-permute-done.14), kind=kLoop, calls=%fused_computation.2 | loop fusion | flops 655360 | bytes 1310720 | tf_op jit(solution)/shard_map/convert_element_type | solution.py:483
  70.3 2.1 %collective-permute-start.19 = (bf16[16,64,128]{2,1,0:T(8,128)(2,1)S(1)}, bf16[16,64,128]{2,1,0:T(8,128)(2,1)S(1)}, u32[]{:S(2)}, u32[]{:S(2)}) collective-permute-start(bf16[16,64,128]{2,1,0:T(8,128)(2,1)S(1)} %add_convert_fusion.1), channel_id=1, source_target_pairs={{0,2},{1,5},{4,0},{5,9},{8,4},{9,13},{12,8},{13,15},{14,12},{15,11... | collective-permute-start | bytes 786440 | tf_op jit(solution)/shard_map/ppermute | solution.py:401
  72.5 4.3 %collective-permute-done.19 = bf16[16,64,128]{2,1,0:T(8,128)(2,1)S(1)} collective-permute-done((bf16[16,64,128]{2,1,0:T(8,128)(2,1)S(1)}, bf16[16,64,128]{2,1,0:T(8,128)(2,1)S(1)}, u32[]{:S(2)}, u32[]{:S(2)}) %collective-permute-start.19) | collective-permute-done | bytes 262176 | tf_op jit(solution)/shard_map/ppermute | solution.py:401
  76.7 1.2 %convert_add_fusion = f32[16,64,128]{2,1,0:T(8,128)S(1)} fusion(bf16[16,64,128]{2,1,0:T(8,128)(2,1)S(1)} %collective-permute-done.19, f32[16,64,128]{2,1,0:T(8,128)S(1)} %far.1, f32[257,64,128]{2,1,0:T(8,128)} %get-tuple-element.41, bf16[96,64,128]{2,1,0:T(8,128)(2,1)S(1)} %collective-permute-done.14), kind=kLoop, calls=%fused_computation.1 | loop fusion | flops 655360 | bytes 2097152 | tf_op jit(solution)/shard_map/add | solution.py:514
  (33 shorter events, 7.2 us)
Async XLA Ops:
  0.0 19.2 %collective-permute-start.2 = (bf16[128,128,128]{2,1,0:T(8,128)(2,1)}, bf16[128,128,128]{2,1,0:T(8,128)(2,1)}, u32[]{:S(2)}, u32[]{:S(2)}) collective-permute-start(bf16[128,128,128]{2,1,0:T(8,128)(2,1)} %refs_8_.1), channel_id=1, source_target_pairs={{0,1},{1,0},{2,3},{3,2},{4,5},{5,4},{6,7},{7,6},{8,9},{9,8},{10,11... | collective-permute-start | bytes 12582920 | tf_op jit(solution)/shard_map/ppermute | solution.py:401
  2.5 9.2 %collective-permute-start = (bf16[1152,128]{1,0:T(8,128)(2,1)}, bf16[1152,128]{1,0:T(8,128)(2,1)S(1)}, u32[]{:S(2)}, u32[]{:S(2)}) collective-permute-start(bf16[1152,128]{1,0:T(8,128)(2,1)} %get-tuple-element.32), channel_id=1, source_target_pairs={{0,2},{1,5},{4,0},{5,9},{8,4},{9,13},{12,8},{13,15},{14,12},{15,11... | collective-permute-start | bytes 884744 | tf_op jit(solution)/shard_map/ppermute | solution.py:401
  5.0 11.2 %collective-permute-start.5 = (bf16[1152,128]{1,0:T(8,128)(2,1)}, bf16[1152,128]{1,0:T(8,128)(2,1)S(1)}, u32[]{:S(2)}, u32[]{:S(2)}) collective-permute-start(bf16[1152,128]{1,0:T(8,128)(2,1)} %get-tuple-element.32), channel_id=1, source_target_pairs={{0,5},{1,2},{4,9},{5,0},{8,13},{9,4},{12,15},{13,8},{14,11},{15,12... | collective-permute-start | bytes 884744 | tf_op jit(solution)/shard_map/ppermute | solution.py:401
  6.5 11.3 %collective-permute-start.3 = (bf16[1152,128]{1,0:T(8,128)(2,1)}, bf16[1152,128]{1,0:T(8,128)(2,1)S(1)}, u32[]{:S(2)}, u32[]{:S(2)}) collective-permute-start(bf16[1152,128]{1,0:T(8,128)(2,1)} %get-tuple-element.32), channel_id=1, source_target_pairs={{0,1},{1,0},{2,3},{3,2},{4,5},{5,4},{6,7},{7,6},{8,9},{9,8},{10,11... | collective-permute-start | bytes 884744 | tf_op jit(solution)/shard_map/ppermute | solution.py:401
  11.7 7.5 %collective-permute-start.1 = (bf16[1152,128]{1,0:T(8,128)(2,1)S(1)}, bf16[1152,128]{1,0:T(8,128)(2,1)S(1)}, u32[]{:S(2)}, u32[]{:S(2)}) collective-permute-start(bf16[1152,128]{1,0:T(8,128)(2,1)S(1)} %collective-permute-done.refs_1_), channel_id=1, source_target_pairs={{0,2},{1,5},{4,0},{5,9},{8,4},{9,13},{12,8},{13,15},{14,12},{15,11... | collective-permute-start | bytes 884744 | tf_op jit(solution)/shard_map/ppermute | solution.py:401
  14.1 1.4 %collective-permute-start.4 = (s32[8,128]{1,0:T(8,128)}, s32[8,128]{1,0:T(8,128)S(1)}, u32[]{:S(2)}, u32[]{:S(2)}) collective-permute-start(s32[8,128]{1,0:T(8,128)} %get-tuple-element.33), channel_id=1, source_target_pairs={{0,1},{1,0},{2,3},{3,2},{4,5},{5,4},{6,7},{7,6},{8,9},{9,8},{10,11... | collective-permute-start | bytes 12296 | tf_op jit(solution)/shard_map/ppermute | solution.py:401
  16.1 35.3 %copy-start = (bf16[16,16,128]{2,1,0:T(8,128)(2,1)S(1)}, bf16[16,16,128]{2,1,0:T(8,128)(2,1)}, u32[]{:S(2)}) copy-start(bf16[16,16,128]{2,1,0:T(8,128)(2,1)} %refs_7_.1) | copy-start | bytes 196612
  16.2 35.3 %copy-start.1 = (s32[256]{0:T(256)S(1)}, s32[256]{0:T(256)}, u32[]{:S(2)}) copy-start(s32[256]{0:T(256)} %param.17) | copy-start | bytes 3076
  16.2 35.3 %copy-start.2 = (s32[256,1]{0,1:T(1,128)S(1)}, s32[256,1]{0,1:T(1,128)}, u32[]{:S(2)}) copy-start(s32[256,1]{0,1:T(1,128)} %param.18) | copy-start | bytes 3076
  16.2 35.3 %copy-start.3 = (s32[256]{0:T(256)S(1)}, s32[256]{0:T(256)}, u32[]{:S(2)}) copy-start(s32[256]{0:T(256)} %param.19) | copy-start | bytes 3076
  16.2 6.8 %collective-permute-start.6 = (bf16[1152,128]{1,0:T(8,128)(2,1)S(1)}, bf16[1152,128]{1,0:T(8,128)(2,1)S(1)}, u32[]{:S(2)}, u32[]{:S(2)}) collective-permute-start(bf16[1152,128]{1,0:T(8,128)(2,1)S(1)} %collective-permute-done.5.refs_2_), channel_id=1, source_target_pairs={{0,2},{1,5},{4,0},{5,9},{8,4},{9,13},{12,8},{13,15},{14,12},{15,11... | collective-permute-start | bytes 884744 | tf_op jit(solution)/shard_map/ppermute | solution.py:401
  19.2 6.9 %collective-permute-start.7 = (bf16[1152,128]{1,0:T(8,128)(2,1)S(1)}, bf16[1152,128]{1,0:T(8,128)(2,1)S(1)}, u32[]{:S(2)}, u32[]{:S(2)}) collective-permute-start(bf16[1152,128]{1,0:T(8,128)(2,1)S(1)} %collective-permute-done.1.refs_3_), channel_id=1, source_target_pairs={{0,2},{1,5},{4,0},{5,9},{8,4},{9,13},{12,8},{13,15},{14,12},{15,11... | collective-permute-start | bytes 884744 | tf_op jit(solution)/shard_map/ppermute | solution.py:401
  22.9 6.7 %collective-permute-start.8 = (bf16[1152,128]{1,0:T(8,128)(2,1)S(1)}, bf16[1152,128]{1,0:T(8,128)(2,1)S(1)}, u32[]{:S(2)}, u32[]{:S(2)}) collective-permute-start(bf16[1152,128]{1,0:T(8,128)(2,1)S(1)} %collective-permute-done.6.refs_4_), channel_id=1, source_target_pairs={{0,2},{1,5},{4,0},{5,9},{8,4},{9,13},{12,8},{13,15},{14,12},{15,11... | collective-permute-start | bytes 884744 | tf_op jit(solution)/shard_map/ppermute | solution.py:401
  26.1 6.7 %collective-permute-start.9 = (bf16[1152,128]{1,0:T(8,128)(2,1)S(1)}, bf16[1152,128]{1,0:T(8,128)(2,1)S(1)}, u32[]{:S(2)}, u32[]{:S(2)}) collective-permute-start(bf16[1152,128]{1,0:T(8,128)(2,1)S(1)} %collective-permute-done.7.refs_5_), channel_id=1, source_target_pairs={{0,2},{1,5},{4,0},{5,9},{8,4},{9,13},{12,8},{13,15},{14,12},{15,11... | collective-permute-start | bytes 884744 | tf_op jit(solution)/shard_map/ppermute | solution.py:401
  43.3 1.6 %collective-permute-start.11 = (bf16[16,64,128]{2,1,0:T(8,128)(2,1)S(1)}, bf16[16,64,128]{2,1,0:T(8,128)(2,1)S(1)}, u32[]{:S(2)}, u32[]{:S(2)}) collective-permute-start(bf16[16,64,128]{2,1,0:T(8,128)(2,1)S(1)} %get-tuple-element.42), channel_id=1, source_target_pairs={{0,1},{1,0},{2,3},{3,2},{4,5},{5,4},{6,7},{7,6},{8,9},{9,8},{10,11... | collective-permute-start | bytes 786440 | tf_op jit(solution)/shard_map/ppermute | solution.py:401
  43.4 1.9 %collective-permute-start.12 = (bf16[16,64,128]{2,1,0:T(8,128)(2,1)S(1)}, bf16[16,64,128]{2,1,0:T(8,128)(2,1)S(1)}, u32[]{:S(2)}, u32[]{:S(2)}) collective-permute-start(bf16[16,64,128]{2,1,0:T(8,128)(2,1)S(1)} %get-tuple-element.43), channel_id=1, source_target_pairs={{0,1},{1,0},{2,3},{3,2},{4,5},{5,4},{6,7},{7,6},{8,9},{9,8},{10,11... | collective-permute-start | bytes 786440 | tf_op jit(solution)/shard_map/ppermute | solution.py:401
  46.6 7.4 %collective-permute-start.14 = (bf16[96,64,128]{2,1,0:T(8,128)(2,1)S(1)}, bf16[96,64,128]{2,1,0:T(8,128)(2,1)S(1)}, u32[]{:S(2)}, u32[]{:S(2)}) collective-permute-start(bf16[96,64,128]{2,1,0:T(8,128)(2,1)S(1)} %get-tuple-element.48), channel_id=1, source_target_pairs={{0,1},{1,0},{2,3},{3,2},{4,5},{5,4},{6,7},{7,6},{8,9},{9,8},{10,11... | collective-permute-start | bytes 4718600 | tf_op jit(solution)/shard_map/ppermute | solution.py:401
  46.8 4.6 %collective-permute-start.10 = (bf16[1024,128]{1,0:T(8,128)(2,1)S(1)}, bf16[1024,128]{1,0:T(8,128)(2,1)S(1)}, u32[]{:S(2)}, u32[]{:S(2)}) collective-permute-start(bf16[1024,128]{1,0:T(8,128)(2,1)S(1)} %get-tuple-element.39.refs_0_), channel_id=1, source_target_pairs={{0,1},{1,0},{2,3},{3,2},{4,5},{5,4},{6,7},{7,6},{8,9},{9,8},{10,11... | collective-permute-start | bytes 786440 | tf_op jit(solution)/shard_map/ppermute | solution.py:401
  47.2 6.8 %collective-permute-start.13 = (bf16[16,64,128]{2,1,0:T(8,128)(2,1)S(1)}, bf16[16,64,128]{2,1,0:T(8,128)(2,1)S(1)}, u32[]{:S(2)}, u32[]{:S(2)}) collective-permute-start(bf16[16,64,128]{2,1,0:T(8,128)(2,1)S(1)} %get-tuple-element.44), channel_id=1, source_target_pairs={{0,2},{1,5},{4,0},{5,9},{8,4},{9,13},{12,8},{13,15},{14,12},{15,11... | collective-permute-start | bytes 786440 | tf_op jit(solution)/shard_map/ppermute | solution.py:401
  49.7 7.6 %collective-permute-start.16 = (bf16[16,64,128]{2,1,0:T(8,128)(2,1)S(1)}, bf16[16,64,128]{2,1,0:T(8,128)(2,1)S(1)}, u32[]{:S(2)}, u32[]{:S(2)}) collective-permute-start(bf16[16,64,128]{2,1,0:T(8,128)(2,1)S(1)} %get-tuple-element.45), channel_id=1, source_target_pairs={{0,2},{1,5},{4,0},{5,9},{8,4},{9,13},{12,8},{13,15},{14,12},{15,11... | collective-permute-start | bytes 786440 | tf_op jit(solution)/shard_map/ppermute | solution.py:401
  55.2 6.4 %collective-permute-start.15 = (bf16[16,64,128]{2,1,0:T(8,128)(2,1)S(1)}, bf16[16,64,128]{2,1,0:T(8,128)(2,1)S(1)}, u32[]{:S(2)}, u32[]{:S(2)}) collective-permute-start(bf16[16,64,128]{2,1,0:T(8,128)(2,1)S(1)} %add_convert_fusion.5), channel_id=1, source_target_pairs={{0,2},{1,5},{4,0},{5,9},{8,4},{9,13},{12,8},{13,15},{14,12},{15,11... | collective-permute-start | bytes 786440 | tf_op jit(solution)/shard_map/ppermute | solution.py:401
  58.5 6.4 %collective-permute-start.18 = (bf16[16,64,128]{2,1,0:T(8,128)(2,1)S(1)}, bf16[16,64,128]{2,1,0:T(8,128)(2,1)S(1)}, u32[]{:S(2)}, u32[]{:S(2)}) collective-permute-start(bf16[16,64,128]{2,1,0:T(8,128)(2,1)S(1)} %add_convert_fusion.4), channel_id=1, source_target_pairs={{0,2},{1,5},{4,0},{5,9},{8,4},{9,13},{12,8},{13,15},{14,12},{15,11... | collective-permute-start | bytes 786440 | tf_op jit(solution)/shard_map/ppermute | solution.py:401
  62.7 6.4 %collective-permute-start.17 = (bf16[16,64,128]{2,1,0:T(8,128)(2,1)S(1)}, bf16[16,64,128]{2,1,0:T(8,128)(2,1)S(1)}, u32[]{:S(2)}, u32[]{:S(2)}) collective-permute-start(bf16[16,64,128]{2,1,0:T(8,128)(2,1)S(1)} %add_convert_fusion.3), channel_id=1, source_target_pairs={{0,2},{1,5},{4,0},{5,9},{8,4},{9,13},{12,8},{13,15},{14,12},{15,11... | collective-permute-start | bytes 786440 | tf_op jit(solution)/shard_map/ppermute | solution.py:401
  66.0 6.4 %collective-permute-start.20 = (bf16[16,64,128]{2,1,0:T(8,128)(2,1)S(1)}, bf16[16,64,128]{2,1,0:T(8,128)(2,1)S(1)}, u32[]{:S(2)}, u32[]{:S(2)}) collective-permute-start(bf16[16,64,128]{2,1,0:T(8,128)(2,1)S(1)} %add_convert_fusion.2), channel_id=1, source_target_pairs={{0,2},{1,5},{4,0},{5,9},{8,4},{9,13},{12,8},{13,15},{14,12},{15,11... | collective-permute-start | bytes 786440 | tf_op jit(solution)/shard_map/ppermute | solution.py:401
  70.3 6.4 %collective-permute-start.19 = (bf16[16,64,128]{2,1,0:T(8,128)(2,1)S(1)}, bf16[16,64,128]{2,1,0:T(8,128)(2,1)S(1)}, u32[]{:S(2)}, u32[]{:S(2)}) collective-permute-start(bf16[16,64,128]{2,1,0:T(8,128)(2,1)S(1)} %add_convert_fusion.1), channel_id=1, source_target_pairs={{0,2},{1,5},{4,0},{5,9},{8,4},{9,13},{12,8},{13,15},{14,12},{15,11... | collective-permute-start | bytes 786440 | tf_op jit(solution)/shard_map/ppermute | solution.py:401
  72.5 5.4 %collective-permute-start.21 = (bf16[16,64,128]{2,1,0:T(8,128)(2,1)S(1)}, bf16[16,64,128]{2,1,0:T(8,128)(2,1)S(1)}, u32[]{:S(2)}, u32[]{:S(2)}) collective-permute-start(bf16[16,64,128]{2,1,0:T(8,128)(2,1)S(1)} %collective-permute-done.20), channel_id=1, source_target_pairs={{0,1},{1,0},{2,3},{3,2},{4,5},{5,4},{6,7},{7,6},{8,9},{9,8},{10,11... | collective-permute-start | bytes 786440 | tf_op jit(solution)/shard_map/ppermute | solution.py:401

commit v9 on v8

--- a/solution.py
+++ b/solution.py
@@ -144,43 +144,44 @@
 
     me, owner, slot = me_ref[0], owner_ref[...], slot_ref[...]
     stored = owner.shape[1]
-    place = scatter_place(owner, me, count) * clusters + slot
+    place = scatter_place(owner, me, count)
+    quarter = count // 4
+    late = (place // quarter) & 1
+    place = (place // (2 * quarter) * quarter + (place & (quarter - 1))) * clusters + slot
     column = (owner * clusters + slot + offset_ref[...]) & (count * clusters - 1)
     shard = gather_place(column // clusters, me, count)
-    theirs = shard == count // 2
-    shard = jnp.where(theirs, gather_place(column // clusters, me ^ 1, count), shard)
+    theirs = (shard == count // 2).astype(jnp.int32)
+    shard = jnp.where(theirs == 1, gather_place(column // clusters, me ^ 1, count), shard)
     column_place = shard * clusters + (column & (clusters - 1))
     square = (stored, stored)
-    late = jnp.broadcast_to(jnp.where(theirs, 1.0, 0.0), square)
-    late_of_row = jnp.transpose(late)
+    group = jnp.broadcast_to((2 * theirs + late).astype(jnp.float32), square)
+    group_of_row = jnp.transpose(group)
     row_at = lax.broadcasted_iota(jnp.int32, square, 0)
     lane_at = lax.broadcasted_iota(jnp.int32, square, 1)
     lane = lane_at.astype(jnp.float32)
-    before = (late_of_row < late) | ((late_of_row == late) & (row_at < lane_at))
+    before = (group_of_row < group) | ((group_of_row == group) & (row_at < lane_at))
     rank = jnp.sum(jnp.where(before, 1.0, 0.0), axis=0, keepdims=True)
     rank = jnp.transpose(jnp.broadcast_to(rank, square))
     here = jnp.where(rank == lane, 1.0, 0.0).astype(jnp.bfloat16)
-    chunk = row_at < lane_at * (stored // CHUNKS)
-    mine = jnp.sum(jnp.where(chunk, 1.0 - late_of_row, 0.0), axis=0, keepdims=True)
-    other = jnp.sum(jnp.where(chunk, late_of_row, 0.0), axis=0, keepdims=True)
-    other = other + (stored - jnp.sum(late[0:1], axis=1, keepdims=True))
+    starts = jnp.sum(jnp.where(group_of_row < lane, 1.0, 0.0), axis=0, keepdims=True)
     values = jnp.concatenate(
         [lane[0:1], place.astype(jnp.float32), column_place.astype(jnp.float32)]
         + [jnp.zeros((5, stored), jnp.float32)],
         axis=0,
     )
     values = jnp.dot(values.astype(jnp.bfloat16), here, preferred_element_type=jnp.float32)
-    values = jnp.concatenate([values[0:3], mine, other, values[5:8]], axis=0)
+    values = jnp.concatenate([values[0:3], starts, values[4:8]], axis=0)
     list_ref[...] = values.astype(jnp.int32)
 
 
-def near_kernel(batch, lag, shards, sends, list_ref, *refs):
-    shard_refs, (own_hbm, mate_hbm, sums, coef_ref) = refs[:shards], refs[shards : shards + 4]
-    refs = refs[shards + 4 :]
-    send_refs, (columns, blocks, column_sem, coef_sem, block_sem) = refs[:sends], refs[sends:]
+def near_kernel(late, batch, lag, shards, sends, list_ref, *refs):
+    shard_refs, (own_hbm, mate_hbm, keep_ref) = refs[:shards], refs[shards : shards + 3]
+    send_refs, refs = refs[shards + 3 : shards + 3 + sends], refs[shards + 3 + sends :]
+    if not late:
+        coef_ref, refs = refs[0], refs[1:]
+    columns, blocks, sums, column_sem, coef_sem, block_sem = refs
     directions = sums.shape[1]
     span = columns.shape[0] // shards
-    tail = coef_ref.shape[0] // shards
     stored = blocks.shape[1]
     chunk = stored // CHUNKS
     dummy = sums.shape[0] - 1
@@ -199,12 +200,15 @@
             pltpu.make_async_copy(
                 source.at[at], blocks.at[half, at], block_sem.at[half * CHUNKS + c]
             ).start()
-    tails = [
-        pltpu.make_async_copy(
-            ref.at[pl.ds(span, tail)], coef_ref.at[pl.ds(k * tail, tail)], coef_sem.at[k]
-        )
-        for k, ref in enumerate(shard_refs)
-    ]
+    tails = []
+    if not late:
+        tail = coef_ref.shape[0] // shards
+        tails = [
+            pltpu.make_async_copy(
+                ref.at[pl.ds(span, tail)], coef_ref.at[pl.ds(k * tail, tail)], coef_sem.at[k]
+            )
+            for k, ref in enumerate(shard_refs)
+        ]
     for copy in tails:
         copy.start()
 
@@ -216,14 +220,14 @@
     for copy in copies:
         copy.wait()
 
-    here = list_ref[3, CHUNKS]
-    there = list_ref[8 + 4, 0]
-    total = here + stored - there
+    begin, begin_there = list_ref[3, late], list_ref[11, 2 + late]
+    here = list_ref[3, late + 1] - begin
+    total = here + list_ref[11, 3 + late] - begin_there
 
     def entry(j):
         j = jnp.minimum(j, total - 1)
         half = (j >= here).astype(jnp.int32)
-        return half, half * 8, j + half * (there - here)
+        return half, half * 8, j + jnp.where(half == 1, begin_there - here, begin)
 
     def wait(c, carry):
         at = pl.ds(0, chunk)
@@ -262,6 +266,12 @@
 
     ready = lax.fori_loop(0, (total + batch - 1) // batch, body, 0)
     lax.fori_loop(ready, 2 * CHUNKS, wait, 0)
+
+    def keep(i, carry):
+        keep_ref[i] = sums[i]
+        return carry
+
+    lax.fori_loop(0, dummy // 2, keep, 0, unroll=2)
     at = dummy // 2
     for send_ref in send_refs:
 
@@ -334,9 +344,9 @@
 def ring_pairs(count):
     chips = count // 2
     cores = [(p, c) for p in range(chips) for c in range(2)]
-    ahead = [(ring_device(p, c, chips), ring_device(p - 1 + 2 * c, c, chips)) for p, c in cores]
+    ahead = [(ring_device(p, c, chips), ring_device(p + 1 - 2 * c, c, chips)) for p, c in cores]
     cross = [
-        (ring_device(p, c, chips), ring_device(p + 1 - 2 * c, 1 - c, chips)) for p, c in cores
+        (ring_device(p, c, chips), ring_device(p - 1 + 2 * c, 1 - c, chips)) for p, c in cores
     ]
     return ahead, cross
 
@@ -349,7 +359,7 @@
 def gather_place(device, me, count):
     chips = count // 2
     depth = chips // 2
-    back = (2 * (me & 1) - 1) * (ring_place(me, chips) - ring_place(device, chips))
+    back = (1 - 2 * (me & 1)) * (ring_place(me, chips) - ring_place(device, chips))
     back = (back + chips) & (chips - 1)
     other = (device ^ me) & 1
     here = (back < depth) & (back > 0) | (back == 0) & (other == 1) | (back == depth) & (other == 0)
@@ -359,7 +369,7 @@
 def scatter_place(device, me, count):
     chips = count // 2
     depth = chips // 2
-    ahead = (ring_place(me, chips) - ring_place(device, chips) + chips) & (chips - 1)
+    ahead = (ring_place(device, chips) - ring_place(me, chips) + chips) & (chips - 1)
     core = device & 1
     handler = jnp.where((ahead & (depth - 1)) == 0, core, (ahead > depth).astype(jnp.int32))
     steps = jnp.where(handler == 0, ahead, (chips - ahead) & (chips - 1))
@@ -438,54 +448,63 @@
         if k < chips - 2:
             flow[x] = move(flow[x], ahead)
 
-    pieces = [1, 1, chips - 2]
-    kept, coef, *sends = pl.pallas_call(
-        functools.partial(near_kernel, BATCH, LAG, chips, len(pieces)),
-        out_shape=[
-            jax.ShapeDtypeStruct((count * clusters + 1, directions, unknowns), jnp.float32),
-            jax.ShapeDtypeStruct((chips * half * rank_k, unknowns), jnp.bfloat16),
-        ]
-        + [
-            jax.ShapeDtypeStruct((part * clusters, directions, unknowns), jnp.bfloat16)
-            for part in pieces
-        ],
-        in_specs=[whole(pltpu.SMEM)] + [whole(pl.ANY)] * (chips + 2),
-        out_specs=[whole()] * (2 + len(pieces)),
-        scratch_shapes=[
-            pltpu.VMEM((chips * base, unknowns), jnp.bfloat16),
-            pltpu.VMEM((2, *near_blocks.shape), jnp.bfloat16),
-            pltpu.SemaphoreType.DMA((chips,)),
-            pltpu.SemaphoreType.DMA((chips,)),
-            pltpu.SemaphoreType.DMA((2 * CHUNKS,)),
-        ],
-        compiler_params=pltpu.CompilerParams(vmem_limit_bytes=NEAR_VMEM),
-        cost_estimate=pl.CostEstimate(
-            flops=16 * stored * directions * unknowns * unknowns,
-            bytes_accessed=16 << 20,
-            transcendentals=0,
-        ),
-        name="near",
-    )(lists, *shards, near_blocks, mate_blocks)
-
+    quarter = chips // 2
+
+    def near(late, lists):
+        pieces = [1] * quarter
+        kept, *sends = pl.pallas_call(
+            functools.partial(near_kernel, late, BATCH, LAG, chips, len(pieces)),
+            out_shape=[
+                jax.ShapeDtypeStruct((quarter * clusters, directions, unknowns), jnp.float32)
+            ]
+            + [
+                jax.ShapeDtypeStruct((part * clusters, directions, unknowns), jnp.bfloat16)
+                for part in pieces
+            ]
+            + [jax.ShapeDtypeStruct((chips * half * rank_k, unknowns), jnp.bfloat16)] * (1 - late),
+            in_specs=[whole(pltpu.SMEM)] + [whole(pl.ANY)] * (chips + 2),
+            out_specs=[whole()] * (2 + len(pieces) - late),
+            scratch_shapes=[
+                pltpu.VMEM((chips * base, unknowns), jnp.bfloat16),
+                pltpu.VMEM((2, *near_blocks.shape), jnp.bfloat16),
+                pltpu.VMEM((2 * quarter * clusters + 1, directions, unknowns), jnp.float32),
+                pltpu.SemaphoreType.DMA((chips,)),
+                pltpu.SemaphoreType.DMA((chips,)),
+                pltpu.SemaphoreType.DMA((2 * CHUNKS,)),
+            ],
+            compiler_params=pltpu.CompilerParams(vmem_limit_bytes=NEAR_VMEM),
+            cost_estimate=pl.CostEstimate(
+                flops=16 * stored * directions * unknowns * unknowns,
+                bytes_accessed=16 << 20,
+                transcendentals=0,
+            ),
+            name="near",
+        )(lists, *shards, near_blocks, mate_blocks)
+        return kept, sends
+
+    early, (*sends, coef) = near(0, lists)
     mates = [move(sends[0], mate), move(sends[1], mate)]
     coefs = [coef, move(coef, mate)]
+    kept = [early]
 
     def term(k):
-        part = min(k, 2)
-        got = mates[part][(k - part) * clusters : (k - part + 1) * clusters]
-        return kept[k * clusters : (k + 1) * clusters] + got.astype(jnp.float32)
-
-    def tied(values, *others):
-        values, mates[2], *others = lax.optimization_barrier((values, mates[2], *others))
+        at = k % quarter * clusters
+        return kept[k // quarter][at : at + clusters] + mates[k].astype(jnp.float32)
+
+    def tied(values, k, *others):
+        values, mates[k + 1], *others = lax.optimization_barrier((values, mates[k + 1], *others))
         return values
 
     def add(flow, k):
         return (flow.astype(jnp.float32) + term(k)).astype(jnp.bfloat16)
 
     flow = lax.optimization_barrier([term(0).astype(jnp.bfloat16), term(1).astype(jnp.bfloat16)])
-    couple, sends[2] = after(couple, *flow), after(sends[2], *flow)
+    lists, couple = after(lists, *flow), after(couple, *flow)
+    mates += [move(after(send, *flow), mate) for send in sends[2:]]
     flow = [move(part, ahead) for part in flow]
-    mates.append(move(sends[2], mate))
+    late, sends = near(1, lists)
+    kept.append(late)
+    mates += [move(send, mate) for send in sends]
     far = pl.pallas_call(
         far_kernel,
         out_shape=jax.ShapeDtypeStruct((clusters, directions, unknowns), jnp.float32),
@@ -509,7 +528,7 @@
     )
     for k in range(2, chips - 1):
         x = k % 2
-        flow[x] = move(tied(add(flow[x], k), *([far] if k == 2 else [])), ahead)
+        flow[x] = move(tied(add(flow[x], k), k, *([far] if k == chips - 3 else [])), ahead)
     flow[1] = move(flow[1], mate)
     total = far + term(chips - 1) + flow[0].astype(jnp.float32)
     total = lax.optimization_barrier(total)

time: 79.2 us -> 74.1 us (0.936)
  other arithmetic: 9.71 us -> 2.23 us
  starting transfers between devices: 28.8 us -> 29.9 us
  Pallas kernels: 15 us -> 15.9 us
    convert_element_type x5, other arithmetic: 5.73 us -> 0.49 us  [add(): return (flow.astype(jnp.float32) + term(k)).astype(jnp.bfloat16)]
    convert_element_type x1, other arithmetic: 1.35 us -> 0.14 us  [stationary(): term(1).astype(jnp.bfloat16)]
    ppermute x22 -> x27, starting transfers between devices: 28.8 us -> 29.9 us  [move(): return lax.ppermute(values, 'blk', where)]
    add x1, other arithmetic: 1.16 us -> 0.14 us  [stationary(): total = far + term(chips - 1) + flow[0].astype(jnp.float32)]
    pallas_call x1 -> x2, Pallas kernels: 10.4 us -> 11.4 us  [near(): pl.pallas_call(functools.partial(near_kernel, late, BATCH, LAG, chips, le...]
    ppermute x22 -> x27, waiting for transfers between devices: 24.1 us -> 24.4 us  [move(): return lax.ppermute(values, 'blk', where)]
  transfers between devices with their start and end apart: 22 -> 27, of which waited for: 12 -> 13; matrix products, arithmetic and copies ran while one was open for 11% -> 3% of each run, Pallas kernels for 6% -> 14%
where the time goes in v9:
time: 74.1 us; the launch traced here: 73.7 us
  starting transfers between devices  29.9 us (40%)
  waiting for transfers between devices  24.4 us (33%)
  Pallas kernels  15.9 us (21%)
  other arithmetic  2.23 us (3%)
  local copies, waits for them, and re-layouts  0.97 us (1%)
    ppermute x27, starting transfers between devices, move(): return lax.ppermute(values, 'blk', where)  29.9 us
    ppermute x27, waiting for transfers between devices, move(): return lax.ppermute(values, 'blk', where)  24.4 us
    pallas_call x2, Pallas kernels, near(): pl.pallas_call(functools.partial(near_kernel, late, BATCH, LAG, chips, le...  11.4 us
    pallas_call x1, Pallas kernels, stationary(): pl.pallas_call(far_kernel, out_shape=jax.ShapeDtypeStruct((clusters, dire...  2.51 us
    pallas_call x1, Pallas kernels, stationary(): pl.pallas_call(functools.partial(prologue_kernel, count), out_shape=[jax....  2.03 us
  transfers between devices with their start and end apart: 27, of which 13 were waited for; matrix products, arithmetic and copies ran while one was open for 3% of the time, Pallas kernels for 14%

profile of v9, /device:TPU:0, one launch (start us, length us, event | category | flops | bytes accessed | tf_op | source)
XLA Modules:
  0.0 73.7 jit_solution(5099324547478594365)
XLA Ops:
  0.5 2.0 %prologue.1 = (bf16[1152,128]{1,0:T(8,128)(2,1)}, s32[8,128]{1,0:T(8,128)}) custom-call(s32[1]{0:T(128)} %bitcast.me_ref.refs_2_, s32[1,128]{1,0:T(1,128)} %bitcast.14, s32[1,128]{1,0:T(1,128)} %bitcast.15, s32[1,128]{1,0:T(1,128)} %bitcast.16, bf16[16,64,128]{2,1,0:T(8,128)(2,1)} %rhs_ref.1, bf16[16,16,128]{2,1,0:T(8,128)(2,1)} %basis_ref.1), custom_call_target="tpu_custom_call" | custom-call | tf_op jit(solution)/shard_map/prologue/pallas_call | solution.py:419
  2.5 2.6 %collective-permute-start = (bf16[1152,128]{1,0:T(8,128)(2,1)}, bf16[1152,128]{1,0:T(8,128)(2,1)S(1)}, u32[]{:S(2)}, u32[]{:S(2)}) collective-permute-start(bf16[1152,128]{1,0:T(8,128)(2,1)} %get-tuple-element.40), channel_id=1, source_target_pairs={{0,4},{1,3},{4,8},{5,1},{8,12},{9,5},{12,14},{13,9},{14,10},{15,13... | collective-permute-start | bytes 884744 | tf_op jit(solution)/shard_map/ppermute | solution.py:411
  5.1 1.4 %collective-permute-start.5 = (bf16[1152,128]{1,0:T(8,128)(2,1)}, bf16[1152,128]{1,0:T(8,128)(2,1)S(1)}, u32[]{:S(2)}, u32[]{:S(2)}) collective-permute-start(bf16[1152,128]{1,0:T(8,128)(2,1)} %get-tuple-element.40), channel_id=1, source_target_pairs={{0,3},{1,4},{4,1},{5,8},{8,5},{9,12},{12,9},{13,14},{14,13},{15,10... | collective-permute-start | bytes 884744 | tf_op jit(solution)/shard_map/ppermute | solution.py:411
  6.7 5.0 %collective-permute-done.refs_1_ = bf16[1152,128]{1,0:T(8,128)(2,1)S(1)} collective-permute-done((bf16[1152,128]{1,0:T(8,128)(2,1)}, bf16[1152,128]{1,0:T(8,128)(2,1)S(1)}, u32[]{:S(2)}, u32[]{:S(2)}) %collective-permute-start) | collective-permute-done | bytes 294944 | tf_op jit(solution)/shard_map/ppermute | solution.py:411
  11.8 2.4 %collective-permute-start.1 = (bf16[1152,128]{1,0:T(8,128)(2,1)S(1)}, bf16[1152,128]{1,0:T(8,128)(2,1)S(1)}, u32[]{:S(2)}, u32[]{:S(2)}) collective-permute-start(bf16[1152,128]{1,0:T(8,128)(2,1)S(1)} %collective-permute-done.refs_1_), channel_id=1, source_target_pairs={{0,4},{1,3},{4,8},{5,1},{8,12},{9,5},{12,14},{13,9},{14,10},{15,13... | collective-permute-start | bytes 884744 | tf_op jit(solution)/shard_map/ppermute | solution.py:411
  14.1 0.9 %copy.14 = bf16[256,16,16]{0,1,2:T(8,128)(2,1)S(1)} copy(bf16[256,16,16]{0,2,1:T(8,128)(2,1)} %param.16) | data formatting | bytes 262144 | tf_op args[5]
  15.5 0.7 pad_add_fusion.list_ref
  16.2 1.6 %collective-permute-start.6 = (bf16[1152,128]{1,0:T(8,128)(2,1)S(1)}, bf16[1152,128]{1,0:T(8,128)(2,1)S(1)}, u32[]{:S(2)}, u32[]{:S(2)}) collective-permute-start(bf16[1152,128]{1,0:T(8,128)(2,1)S(1)} %collective-permute-done.5.refs_2_), channel_id=1, source_target_pairs={{0,4},{1,3},{4,8},{5,1},{8,12},{9,5},{12,14},{13,9},{14,10},{15,13... | collective-permute-start | bytes 884744 | tf_op jit(solution)/shard_map/ppermute | solution.py:411
  17.8 1.3 %collective-permute-done.1.refs_3_ = bf16[1152,128]{1,0:T(8,128)(2,1)S(1)} collective-permute-done((bf16[1152,128]{1,0:T(8,128)(2,1)S(1)}, bf16[1152,128]{1,0:T(8,128)(2,1)S(1)}, u32[]{:S(2)}, u32[]{:S(2)}) %collective-permute-start.1) | collective-permute-done | bytes 294944 | tf_op jit(solution)/shard_map/ppermute | solution.py:411
  19.1 1.7 %collective-permute-start.7 = (bf16[1152,128]{1,0:T(8,128)(2,1)S(1)}, bf16[1152,128]{1,0:T(8,128)(2,1)S(1)}, u32[]{:S(2)}, u32[]{:S(2)}) collective-permute-start(bf16[1152,128]{1,0:T(8,128)(2,1)S(1)} %collective-permute-done.1.refs_3_), channel_id=1, source_target_pairs={{0,4},{1,3},{4,8},{5,1},{8,12},{9,5},{12,14},{13,9},{14,10},{15,13... | collective-permute-start | bytes 884744 | tf_op jit(solution)/shard_map/ppermute | solution.py:411
  20.9 2.1 %collective-permute-done.6.refs_4_ = bf16[1152,128]{1,0:T(8,128)(2,1)S(1)} collective-permute-done((bf16[1152,128]{1,0:T(8,128)(2,1)S(1)}, bf16[1152,128]{1,0:T(8,128)(2,1)S(1)}, u32[]{:S(2)}, u32[]{:S(2)}) %collective-permute-start.6) | collective-permute-done | bytes 294944 | tf_op jit(solution)/shard_map/ppermute | solution.py:411
  22.9 1.6 %collective-permute-start.8 = (bf16[1152,128]{1,0:T(8,128)(2,1)S(1)}, bf16[1152,128]{1,0:T(8,128)(2,1)S(1)}, u32[]{:S(2)}, u32[]{:S(2)}) collective-permute-start(bf16[1152,128]{1,0:T(8,128)(2,1)S(1)} %collective-permute-done.6.refs_4_), channel_id=1, source_target_pairs={{0,4},{1,3},{4,8},{5,1},{8,12},{9,5},{12,14},{13,9},{14,10},{15,13... | collective-permute-start | bytes 884744 | tf_op jit(solution)/shard_map/ppermute | solution.py:411
  24.5 1.6 %collective-permute-done.7.refs_5_ = bf16[1152,128]{1,0:T(8,128)(2,1)S(1)} collective-permute-done((bf16[1152,128]{1,0:T(8,128)(2,1)S(1)}, bf16[1152,128]{1,0:T(8,128)(2,1)S(1)}, u32[]{:S(2)}, u32[]{:S(2)}) %collective-permute-start.7) | collective-permute-done | bytes 294944 | tf_op jit(solution)/shard_map/ppermute | solution.py:411
  26.1 1.6 %collective-permute-start.9 = (bf16[1152,128]{1,0:T(8,128)(2,1)S(1)}, bf16[1152,128]{1,0:T(8,128)(2,1)S(1)}, u32[]{:S(2)}, u32[]{:S(2)}) collective-permute-start(bf16[1152,128]{1,0:T(8,128)(2,1)S(1)} %collective-permute-done.7.refs_5_), channel_id=1, source_target_pairs={{0,4},{1,3},{4,8},{5,1},{8,12},{9,5},{12,14},{13,9},{14,10},{15,13... | collective-permute-start | bytes 884744 | tf_op jit(solution)/shard_map/ppermute | solution.py:411
  27.7 2.0 %collective-permute-done.8.refs_6_ = bf16[1152,128]{1,0:T(8,128)(2,1)S(1)} collective-permute-done((bf16[1152,128]{1,0:T(8,128)(2,1)S(1)}, bf16[1152,128]{1,0:T(8,128)(2,1)S(1)}, u32[]{:S(2)}, u32[]{:S(2)}) %collective-permute-start.8) | collective-permute-done | bytes 294944 | tf_op jit(solution)/shard_map/ppermute | solution.py:411
  29.7 3.2 %collective-permute-done.9.refs_7_ = bf16[1152,128]{1,0:T(8,128)(2,1)S(1)} collective-permute-done((bf16[1152,128]{1,0:T(8,128)(2,1)S(1)}, bf16[1152,128]{1,0:T(8,128)(2,1)S(1)}, u32[]{:S(2)}, u32[]{:S(2)}) %collective-permute-start.9) | collective-permute-done | bytes 294944 | tf_op jit(solution)/shard_map/ppermute | solution.py:411
  32.8 5.8 %near.2 = (f32[64,64,128]{2,1,0:T(8,128)S(1)}, bf16[16,64,128]{2,1,0:T(8,128)(2,1)S(1)}, bf16[16,64,128]{2,1,0:T(8,128)(2,1)S(1)}, bf16[16,64,128]{2,1,0:T(8,128...) custom-call(s32[16,128]{1,0:T(8,128)S(1)} %pad_add_fusion.list_ref, ...), custom_call_target="tpu_custom_call" | custom-call | flops 2147483648 | bytes 16777216 | tf_op jit(solution)/shard_map/near/pallas_call | solution.py:455
  39.3 1.0 %collective-permute-done.12 = bf16[16,64,128]{2,1,0:T(8,128)(2,1)S(1)} collective-permute-done((bf16[16,64,128]{2,1,0:T(8,128)(2,1)S(1)}, bf16[16,64,128]{2,1,0:T(8,128)(2,1)S(1)}, u32[]{:S(2)}, u32[]{:S(2)}) %collective-permute-start.12) | collective-permute-done | bytes 262176 | tf_op jit(solution)/shard_map/ppermute | solution.py:411
  41.0 1.6 %collective-permute-start.13 = (bf16[16,64,128]{2,1,0:T(8,128)(2,1)S(1)}, bf16[16,64,128]{2,1,0:T(8,128)(2,1)S(1)}, u32[]{:S(2)}, u32[]{:S(2)}) collective-permute-start(bf16[16,64,128]{2,1,0:T(8,128)(2,1)S(1)} %get-tuple-element.52), channel_id=1, source_target_pairs={{0,4},{1,3},{4,8},{5,1},{8,12},{9,5},{12,14},{13,9},{14,10},{15,13... | collective-permute-start | bytes 786440 | tf_op jit(solution)/shard_map/ppermute | solution.py:411
  42.6 1.6 %collective-permute-start.17 = (bf16[16,64,128]{2,1,0:T(8,128)(2,1)S(1)}, bf16[16,64,128]{2,1,0:T(8,128)(2,1)S(1)}, u32[]{:S(2)}, u32[]{:S(2)}) collective-permute-start(bf16[16,64,128]{2,1,0:T(8,128)(2,1)S(1)} %get-tuple-element.53), channel_id=1, source_target_pairs={{0,4},{1,3},{4,8},{5,1},{8,12},{9,5},{12,14},{13,9},{14,10},{15,13... | collective-permute-start | bytes 786440 | tf_op jit(solution)/shard_map/ppermute | solution.py:411
  44.3 5.5 %near.3 = (f32[64,64,128]{2,1,0:T(8,128)S(1)}, bf16[16,64,128]{2,1,0:T(8,128)(2,1)S(1)}, bf16[16,64,128]{2,1,0:T(8,128)(2,1)S(1)}, bf16[16,64,128]{2,1,0:T(8,128)(2,1)S(1)}, bf16[16,64,128]{2,1,0:T(8,128)(2,1)S(1)}) custom-call(s32[16,128]{1,0:T(8,128)S(1)} %pad_add_fusion.list_ref, bf16[1152,128]{1,0:T(8,128)(2,1)S(1)} %collective-permute-done.3.refs_0_, ...), custom_call_target="tpu_custom_call" | custom-call | flops 2147483648 | bytes 16777216 | tf_op jit(solution)/shard_map/near/pallas_call | solution.py:455
  50.3 2.4 %collective-permute-start.16 = (bf16[16,64,128]{2,1,0:T(8,128)(2,1)S(1)}, bf16[16,64,128]{2,1,0:T(8,128)(2,1)S(1)}, u32[]{:S(2)}, u32[]{:S(2)}) collective-permute-start(bf16[16,64,128]{2,1,0:T(8,128)(2,1)S(1)} %add_convert_fusion.5), channel_id=1, source_target_pairs={{0,4},{1,3},{4,8},{5,1},{8,12},{9,5},{12,14},{13,9},{14,10},{15,13... | collective-permute-start | bytes 786440 | tf_op jit(solution)/shard_map/ppermute | solution.py:411
  53.4 0.6 collective-permute-start.23
  53.9 2.8 %collective-permute-done.16 = bf16[16,64,128]{2,1,0:T(8,128)(2,1)S(1)} collective-permute-done((bf16[16,64,128]{2,1,0:T(8,128)(2,1)S(1)}, bf16[16,64,128]{2,1,0:T(8,128)(2,1)S(1)}, u32[]{:S(2)}, u32[]{:S(2)}) %collective-permute-start.16) | collective-permute-done | bytes 262176 | tf_op jit(solution)/shard_map/ppermute | solution.py:411
  56.8 2.3 %collective-permute-start.21 = (bf16[16,64,128]{2,1,0:T(8,128)(2,1)S(1)}, bf16[16,64,128]{2,1,0:T(8,128)(2,1)S(1)}, u32[]{:S(2)}, u32[]{:S(2)}) collective-permute-start(bf16[16,64,128]{2,1,0:T(8,128)(2,1)S(1)} %add_convert_fusion.4), channel_id=1, source_target_pairs={{0,4},{1,3},{4,8},{5,1},{8,12},{9,5},{12,14},{13,9},{14,10},{15,13... | collective-permute-start | bytes 786440 | tf_op jit(solution)/shard_map/ppermute | solution.py:411
  59.2 1.6 %collective-permute-start.20 = (bf16[16,64,128]{2,1,0:T(8,128)(2,1)S(1)}, bf16[16,64,128]{2,1,0:T(8,128)(2,1)S(1)}, u32[]{:S(2)}, u32[]{:S(2)}) collective-permute-start(bf16[16,64,128]{2,1,0:T(8,128)(2,1)S(1)} %add_convert_fusion.3), channel_id=1, source_target_pairs={{0,4},{1,3},{4,8},{5,1},{8,12},{9,5},{12,14},{13,9},{14,10},{15,13... | collective-permute-start | bytes 786440 | tf_op jit(solution)/shard_map/ppermute | solution.py:411
  60.9 2.5 %far.1 = f32[16,64,128]{2,1,0:T(8,128)S(1)} custom-call(bf16[1024,128]{1,0:T(8,128)(2,1)S(1)} %get-tuple-element.47.refs_0_, bf16[1024,128]{1,0:T(8,128)(2,1)S(1)} %collective-permute-done.10.refs_1_, s32[1]{0:T(128)} %bitcast.me_ref.refs_2_, bf16[16,16,256]{2,1,0:T(8,128)(2,1)S(1)} %bitcast.10, s32[1,256]{1,0:T(1,128)S(1)} %bitcast.11, ...), custom_call_target="tpu_custom_call" | custom-call | flops 536870912 | bytes 8388608 | tf_op jit(solution)/shard_map/far/pallas_call | solution.py:508
  63.5 2.1 %collective-permute-start.25 = (bf16[16,64,128]{2,1,0:T(8,128)(2,1)S(1)}, bf16[16,64,128]{2,1,0:T(8,128)(2,1)S(1)}, u32[]{:S(2)}, u32[]{:S(2)}) collective-permute-start(bf16[16,64,128]{2,1,0:T(8,128)(2,1)S(1)} %add_convert_fusion.2), channel_id=1, source_target_pairs={{0,4},{1,3},{4,8},{5,1},{8,12},{9,5},{12,14},{13,9},{14,10},{15,13... | collective-permute-start | bytes 786440 | tf_op jit(solution)/shard_map/ppermute | solution.py:411
  66.1 2.4 %collective-permute-start.24 = (bf16[16,64,128]{2,1,0:T(8,128)(2,1)S(1)}, bf16[16,64,128]{2,1,0:T(8,128)(2,1)S(1)}, u32[]{:S(2)}, u32[]{:S(2)}) collective-permute-start(bf16[16,64,128]{2,1,0:T(8,128)(2,1)S(1)} %add_convert_fusion.1), channel_id=1, source_target_pairs={{0,4},{1,3},{4,8},{5,1},{8,12},{9,5},{12,14},{13,9},{14,10},{15,13... | collective-permute-start | bytes 786440 | tf_op jit(solution)/shard_map/ppermute | solution.py:411
  68.5 1.5 %collective-permute-done.25 = bf16[16,64,128]{2,1,0:T(8,128)(2,1)S(1)} collective-permute-done((bf16[16,64,128]{2,1,0:T(8,128)(2,1)S(1)}, bf16[16,64,128]{2,1,0:T(8,128)(2,1)S(1)}, u32[]{:S(2)}, u32[]{:S(2)}) %collective-permute-start.25) | collective-permute-done | bytes 262176 | tf_op jit(solution)/shard_map/ppermute | solution.py:411
  69.9 2.8 %collective-permute-done.24 = bf16[16,64,128]{2,1,0:T(8,128)(2,1)S(1)} collective-permute-done((bf16[16,64,128]{2,1,0:T(8,128)(2,1)S(1)}, bf16[16,64,128]{2,1,0:T(8,128)(2,1)S(1)}, u32[]{:S(2)}, u32[]{:S(2)}) %collective-permute-start.24) | collective-permute-done | bytes 262176 | tf_op jit(solution)/shard_map/ppermute | solution.py:411
  72.9 0.8 %add_convert_fusion = bf16[16,64,128]{2,1,0:T(8,128)(2,1)} fusion(f32[16,64,128]{2,1,0:T(8,128)S(1)} %convert_add_fusion, bf16[16,64,128]{2,1,0:T(8,128)(2,1)S(1)} %collective-permute-done.26), kind=kLoop, calls=%fused_computation | loop fusion | flops 393216 | bytes 1048576 | tf_op jit(solution)/shard_map/convert_element_type | solution.py:535
  (44 shorter events, 4.4 us)
Async XLA Ops:
  0.0 19.1 %collective-permute-start.2 = (bf16[128,128,128]{2,1,0:T(8,128)(2,1)}, bf16[128,128,128]{2,1,0:T(8,128)(2,1)}, u32[]{:S(2)}, u32[]{:S(2)}) collective-permute-start(bf16[128,128,128]{2,1,0:T(8,128)(2,1)} %refs_8_.3), channel_id=1, source_target_pairs={{0,1},{1,0},{2,3},{3,2},{4,5},{5,4},{6,7},{7,6},{8,9},{9,8},{10,11... | collective-permute-start | bytes 12582920 | tf_op jit(solution)/shard_map/ppermute | solution.py:411
  2.5 9.3 %collective-permute-start = (bf16[1152,128]{1,0:T(8,128)(2,1)}, bf16[1152,128]{1,0:T(8,128)(2,1)S(1)}, u32[]{:S(2)}, u32[]{:S(2)}) collective-permute-start(bf16[1152,128]{1,0:T(8,128)(2,1)} %get-tuple-element.40), channel_id=1, source_target_pairs={{0,4},{1,3},{4,8},{5,1},{8,12},{9,5},{12,14},{13,9},{14,10},{15,13... | collective-permute-start | bytes 884744 | tf_op jit(solution)/shard_map/ppermute | solution.py:411
  5.1 11.2 %collective-permute-start.5 = (bf16[1152,128]{1,0:T(8,128)(2,1)}, bf16[1152,128]{1,0:T(8,128)(2,1)S(1)}, u32[]{:S(2)}, u32[]{:S(2)}) collective-permute-start(bf16[1152,128]{1,0:T(8,128)(2,1)} %get-tuple-element.40), channel_id=1, source_target_pairs={{0,3},{1,4},{4,1},{5,8},{8,5},{9,12},{12,9},{13,14},{14,13},{15,10... | collective-permute-start | bytes 884744 | tf_op jit(solution)/shard_map/ppermute | solution.py:411
  6.4 11.4 %collective-permute-start.3 = (bf16[1152,128]{1,0:T(8,128)(2,1)}, bf16[1152,128]{1,0:T(8,128)(2,1)S(1)}, u32[]{:S(2)}, u32[]{:S(2)}) collective-permute-start(bf16[1152,128]{1,0:T(8,128)(2,1)} %get-tuple-element.40), channel_id=1, source_target_pairs={{0,1},{1,0},{2,3},{3,2},{4,5},{5,4},{6,7},{7,6},{8,9},{9,8},{10,11... | collective-permute-start | bytes 884744 | tf_op jit(solution)/shard_map/ppermute | solution.py:411
  11.8 7.4 %collective-permute-start.1 = (bf16[1152,128]{1,0:T(8,128)(2,1)S(1)}, bf16[1152,128]{1,0:T(8,128)(2,1)S(1)}, u32[]{:S(2)}, u32[]{:S(2)}) collective-permute-start(bf16[1152,128]{1,0:T(8,128)(2,1)S(1)} %collective-permute-done.refs_1_), channel_id=1, source_target_pairs={{0,4},{1,3},{4,8},{5,1},{8,12},{9,5},{12,14},{13,9},{14,10},{15,13... | collective-permute-start | bytes 884744 | tf_op jit(solution)/shard_map/ppermute | solution.py:411
  14.1 1.4 %collective-permute-start.4 = (s32[8,128]{1,0:T(8,128)}, s32[8,128]{1,0:T(8,128)S(1)}, u32[]{:S(2)}, u32[]{:S(2)}) collective-permute-start(s32[8,128]{1,0:T(8,128)} %get-tuple-element.41), channel_id=1, source_target_pairs={{0,1},{1,0},{2,3},{3,2},{4,5},{5,4},{6,7},{7,6},{8,9},{9,8},{10,11... | collective-permute-start | bytes 12296 | tf_op jit(solution)/shard_map/ppermute | solution.py:411
  16.2 6.7 %collective-permute-start.6 = (bf16[1152,128]{1,0:T(8,128)(2,1)S(1)}, bf16[1152,128]{1,0:T(8,128)(2,1)S(1)}, u32[]{:S(2)}, u32[]{:S(2)}) collective-permute-start(bf16[1152,128]{1,0:T(8,128)(2,1)S(1)} %collective-permute-done.5.refs_2_), channel_id=1, source_target_pairs={{0,4},{1,3},{4,8},{5,1},{8,12},{9,5},{12,14},{13,9},{14,10},{15,13... | collective-permute-start | bytes 884744 | tf_op jit(solution)/shard_map/ppermute | solution.py:411
  19.1 7.0 %collective-permute-start.7 = (bf16[1152,128]{1,0:T(8,128)(2,1)S(1)}, bf16[1152,128]{1,0:T(8,128)(2,1)S(1)}, u32[]{:S(2)}, u32[]{:S(2)}) collective-permute-start(bf16[1152,128]{1,0:T(8,128)(2,1)S(1)} %collective-permute-done.1.refs_3_), channel_id=1, source_target_pairs={{0,4},{1,3},{4,8},{5,1},{8,12},{9,5},{12,14},{13,9},{14,10},{15,13... | collective-permute-start | bytes 884744 | tf_op jit(solution)/shard_map/ppermute | solution.py:411
  22.9 6.7 %collective-permute-start.8 = (bf16[1152,128]{1,0:T(8,128)(2,1)S(1)}, bf16[1152,128]{1,0:T(8,128)(2,1)S(1)}, u32[]{:S(2)}, u32[]{:S(2)}) collective-permute-start(bf16[1152,128]{1,0:T(8,128)(2,1)S(1)} %collective-permute-done.6.refs_4_), channel_id=1, source_target_pairs={{0,4},{1,3},{4,8},{5,1},{8,12},{9,5},{12,14},{13,9},{14,10},{15,13... | collective-permute-start | bytes 884744 | tf_op jit(solution)/shard_map/ppermute | solution.py:411
  26.1 6.7 %collective-permute-start.9 = (bf16[1152,128]{1,0:T(8,128)(2,1)S(1)}, bf16[1152,128]{1,0:T(8,128)(2,1)S(1)}, u32[]{:S(2)}, u32[]{:S(2)}) collective-permute-start(bf16[1152,128]{1,0:T(8,128)(2,1)S(1)} %collective-permute-done.7.refs_5_), channel_id=1, source_target_pairs={{0,4},{1,3},{4,8},{5,1},{8,12},{9,5},{12,14},{13,9},{14,10},{15,13... | collective-permute-start | bytes 884744 | tf_op jit(solution)/shard_map/ppermute | solution.py:411
  38.7 1.6 %collective-permute-start.12 = (bf16[16,64,128]{2,1,0:T(8,128)(2,1)S(1)}, bf16[16,64,128]{2,1,0:T(8,128)(2,1)S(1)}, u32[]{:S(2)}, u32[]{:S(2)}) collective-permute-start(bf16[16,64,128]{2,1,0:T(8,128)(2,1)S(1)} %get-tuple-element.51), channel_id=1, source_target_pairs={{0,1},{1,0},{2,3},{3,2},{4,5},{5,4},{6,7},{7,6},{8,9},{9,8},{10,11... | collective-permute-start | bytes 786440 | tf_op jit(solution)/shard_map/ppermute | solution.py:411
  38.8 1.9 %collective-permute-start.11 = (bf16[16,64,128]{2,1,0:T(8,128)(2,1)S(1)}, bf16[16,64,128]{2,1,0:T(8,128)(2,1)S(1)}, u32[]{:S(2)}, u32[]{:S(2)}) collective-permute-start(bf16[16,64,128]{2,1,0:T(8,128)(2,1)S(1)} %get-tuple-element.50), channel_id=1, source_target_pairs={{0,1},{1,0},{2,3},{3,2},{4,5},{5,4},{6,7},{7,6},{8,9},{9,8},{10,11... | collective-permute-start | bytes 786440 | tf_op jit(solution)/shard_map/ppermute | solution.py:411
  40.8 9.4 %collective-permute-start.14 = (bf16[16,64,128]{2,1,0:T(8,128)(2,1)S(1)}, bf16[16,64,128]{2,1,0:T(8,128)(2,1)S(1)}, u32[]{:S(2)}, u32[]{:S(2)}) collective-permute-start(bf16[16,64,128]{2,1,0:T(8,128)(2,1)S(1)} %get-tuple-element.58), channel_id=1, source_target_pairs={{0,1},{1,0},{2,3},{3,2},{4,5},{5,4},{6,7},{7,6},{8,9},{9,8},{10,11... | collective-permute-start | bytes 786440 | tf_op jit(solution)/shard_map/ppermute | solution.py:411
  41.0 9.2 %collective-permute-start.13 = (bf16[16,64,128]{2,1,0:T(8,128)(2,1)S(1)}, bf16[16,64,128]{2,1,0:T(8,128)(2,1)S(1)}, u32[]{:S(2)}, u32[]{:S(2)}) collective-permute-start(bf16[16,64,128]{2,1,0:T(8,128)(2,1)S(1)} %get-tuple-element.52), channel_id=1, source_target_pairs={{0,4},{1,3},{4,8},{5,1},{8,12},{9,5},{12,14},{13,9},{14,10},{15,13... | collective-permute-start | bytes 786440 | tf_op jit(solution)/shard_map/ppermute | solution.py:411
  42.6 10.7 %collective-permute-start.17 = (bf16[16,64,128]{2,1,0:T(8,128)(2,1)S(1)}, bf16[16,64,128]{2,1,0:T(8,128)(2,1)S(1)}, u32[]{:S(2)}, u32[]{:S(2)}) collective-permute-start(bf16[16,64,128]{2,1,0:T(8,128)(2,1)S(1)} %get-tuple-element.53), channel_id=1, source_target_pairs={{0,4},{1,3},{4,8},{5,1},{8,12},{9,5},{12,14},{13,9},{14,10},{15,13... | collective-permute-start | bytes 786440 | tf_op jit(solution)/shard_map/ppermute | solution.py:411
  44.2 6.1 %collective-permute-start.15 = (bf16[16,64,128]{2,1,0:T(8,128)(2,1)S(1)}, bf16[16,64,128]{2,1,0:T(8,128)(2,1)S(1)}, u32[]{:S(2)}, u32[]{:S(2)}) collective-permute-start(bf16[16,64,128]{2,1,0:T(8,128)(2,1)S(1)} %get-tuple-element.60), channel_id=1, source_target_pairs={{0,1},{1,0},{2,3},{3,2},{4,5},{5,4},{6,7},{7,6},{8,9},{9,8},{10,11... | collective-permute-start | bytes 786440 | tf_op jit(solution)/shard_map/ppermute | solution.py:411
  49.9 10.9 %copy-start = (bf16[16,16,128]{2,1,0:T(8,128)(2,1)S(1)}, bf16[16,16,128]{2,1,0:T(8,128)(2,1)}, u32[]{:S(2)}) copy-start(bf16[16,16,128]{2,1,0:T(8,128)(2,1)} %refs_7_.1) | copy-start | bytes 196612
  49.9 10.9 %copy-start.1 = (s32[256]{0:T(256)S(1)}, s32[256]{0:T(256)}, u32[]{:S(2)}) copy-start(s32[256]{0:T(256)} %param.17) | copy-start | bytes 3076
  49.9 10.9 %copy-start.2 = (s32[256,1]{0,1:T(1,128)S(1)}, s32[256,1]{0,1:T(1,128)}, u32[]{:S(2)}) copy-start(s32[256,1]{0,1:T(1,128)} %param.18) | copy-start | bytes 3076
  49.9 10.9 %copy-start.3 = (s32[256]{0:T(256)S(1)}, s32[256]{0:T(256)}, u32[]{:S(2)}) copy-start(s32[256]{0:T(256)} %param.19) | copy-start | bytes 3076
  49.9 3.4 %collective-permute-start.18 = (bf16[16,64,128]{2,1,0:T(8,128)(2,1)S(1)}, bf16[16,64,128]{2,1,0:T(8,128)(2,1)S(1)}, u32[]{:S(2)}, u32[]{:S(2)}) collective-permute-start(bf16[16,64,128]{2,1,0:T(8,128)(2,1)S(1)} %get-tuple-element.63), channel_id=1, source_target_pairs={{0,1},{1,0},{2,3},{3,2},{4,5},{5,4},{6,7},{7,6},{8,9},{9,8},{10,11... | collective-permute-start | bytes 786440 | tf_op jit(solution)/shard_map/ppermute | solution.py:411
  50.3 6.4 %collective-permute-start.16 = (bf16[16,64,128]{2,1,0:T(8,128)(2,1)S(1)}, bf16[16,64,128]{2,1,0:T(8,128)(2,1)S(1)}, u32[]{:S(2)}, u32[]{:S(2)}) collective-permute-start(bf16[16,64,128]{2,1,0:T(8,128)(2,1)S(1)} %add_convert_fusion.5), channel_id=1, source_target_pairs={{0,4},{1,3},{4,8},{5,1},{8,12},{9,5},{12,14},{13,9},{14,10},{15,13... | collective-permute-start | bytes 786440 | tf_op jit(solution)/shard_map/ppermute | solution.py:411
  52.7 8.1 %collective-permute-start.10 = (bf16[1024,128]{1,0:T(8,128)(2,1)S(1)}, bf16[1024,128]{1,0:T(8,128)(2,1)S(1)}, u32[]{:S(2)}, u32[]{:S(2)}) collective-permute-start(bf16[1024,128]{1,0:T(8,128)(2,1)S(1)} %get-tuple-element.47.refs_0_), channel_id=1, source_target_pairs={{0,1},{1,0},{2,3},{3,2},{4,5},{5,4},{6,7},{7,6},{8,9},{9,8},{10,11... | collective-permute-start | bytes 786440 | tf_op jit(solution)/shard_map/ppermute | solution.py:411
  52.7 6.5 %collective-permute-start.19 = (bf16[16,64,128]{2,1,0:T(8,128)(2,1)S(1)}, bf16[16,64,128]{2,1,0:T(8,128)(2,1)S(1)}, u32[]{:S(2)}, u32[]{:S(2)}) collective-permute-start(bf16[16,64,128]{2,1,0:T(8,128)(2,1)S(1)} %get-tuple-element.65), channel_id=1, source_target_pairs={{0,1},{1,0},{2,3},{3,2},{4,5},{5,4},{6,7},{7,6},{8,9},{9,8},{10,11... | collective-permute-start | bytes 786440 | tf_op jit(solution)/shard_map/ppermute | solution.py:411
  53.2 10.3 %collective-permute-start.22 = (bf16[16,64,128]{2,1,0:T(8,128)(2,1)S(1)}, bf16[16,64,128]{2,1,0:T(8,128)(2,1)S(1)}, u32[]{:S(2)}, u32[]{:S(2)}) collective-permute-start(bf16[16,64,128]{2,1,0:T(8,128)(2,1)S(1)} %get-tuple-element.69), channel_id=1, source_target_pairs={{0,1},{1,0},{2,3},{3,2},{4,5},{5,4},{6,7},{7,6},{8,9},{9,8},{10,11... | collective-permute-start | bytes 786440 | tf_op jit(solution)/shard_map/ppermute | solution.py:411
  53.4 12.7 %collective-permute-start.23 = (bf16[16,64,128]{2,1,0:T(8,128)(2,1)S(1)}, bf16[16,64,128]{2,1,0:T(8,128)(2,1)S(1)}, u32[]{:S(2)}, u32[]{:S(2)}) collective-permute-start(bf16[16,64,128]{2,1,0:T(8,128)(2,1)S(1)} %get-tuple-element.71), channel_id=1, source_target_pairs={{0,1},{1,0},{2,3},{3,2},{4,5},{5,4},{6,7},{7,6},{8,9},{9,8},{10,11... | collective-permute-start | bytes 786440 | tf_op jit(solution)/shard_map/ppermute | solution.py:411
  56.8 6.6 %collective-permute-start.21 = (bf16[16,64,128]{2,1,0:T(8,128)(2,1)S(1)}, bf16[16,64,128]{2,1,0:T(8,128)(2,1)S(1)}, u32[]{:S(2)}, u32[]{:S(2)}) collective-permute-start(bf16[16,64,128]{2,1,0:T(8,128)(2,1)S(1)} %add_convert_fusion.4), channel_id=1, source_target_pairs={{0,4},{1,3},{4,8},{5,1},{8,12},{9,5},{12,14},{13,9},{14,10},{15,13... | collective-permute-start | bytes 786440 | tf_op jit(solution)/shard_map/ppermute | solution.py:411
  59.2 6.7 %collective-permute-start.20 = (bf16[16,64,128]{2,1,0:T(8,128)(2,1)S(1)}, bf16[16,64,128]{2,1,0:T(8,128)(2,1)S(1)}, u32[]{:S(2)}, u32[]{:S(2)}) collective-permute-start(bf16[16,64,128]{2,1,0:T(8,128)(2,1)S(1)} %add_convert_fusion.3), channel_id=1, source_target_pairs={{0,4},{1,3},{4,8},{5,1},{8,12},{9,5},{12,14},{13,9},{14,10},{15,13... | collective-permute-start | bytes 786440 | tf_op jit(solution)/shard_map/ppermute | solution.py:411
  63.5 6.4 %collective-permute-start.25 = (bf16[16,64,128]{2,1,0:T(8,128)(2,1)S(1)}, bf16[16,64,128]{2,1,0:T(8,128)(2,1)S(1)}, u32[]{:S(2)}, u32[]{:S(2)}) collective-permute-start(bf16[16,64,128]{2,1,0:T(8,128)(2,1)S(1)} %add_convert_fusion.2), channel_id=1, source_target_pairs={{0,4},{1,3},{4,8},{5,1},{8,12},{9,5},{12,14},{13,9},{14,10},{15,13... | collective-permute-start | bytes 786440 | tf_op jit(solution)/shard_map/ppermute | solution.py:411
  66.1 6.7 %collective-permute-start.24 = (bf16[16,64,128]{2,1,0:T(8,128)(2,1)S(1)}, bf16[16,64,128]{2,1,0:T(8,128)(2,1)S(1)}, u32[]{:S(2)}, u32[]{:S(2)}) collective-permute-start(bf16[16,64,128]{2,1,0:T(8,128)(2,1)S(1)} %add_convert_fusion.1), channel_id=1, source_target_pairs={{0,4},{1,3},{4,8},{5,1},{8,12},{9,5},{12,14},{13,9},{14,10},{15,13... | collective-permute-start | bytes 786440 | tf_op jit(solution)/shard_map/ppermute | solution.py:411
  69.9 3.0 %collective-permute-start.26 = (bf16[16,64,128]{2,1,0:T(8,128)(2,1)S(1)}, bf16[16,64,128]{2,1,0:T(8,128)(2,1)S(1)}, u32[]{:S(2)}, u32[]{:S(2)}) collective-permute-start(bf16[16,64,128]{2,1,0:T(8,128)(2,1)S(1)} %collective-permute-done.25), channel_id=1, source_target_pairs={{0,1},{1,0},{2,3},{3,2},{4,5},{5,4},{6,7},{7,6},{8,9},{9,8},{10,11... | collective-permute-start | bytes 786440 | tf_op jit(solution)/shard_map/ppermute | solution.py:411

commit v10 on v9

--- a/solution.py
+++ b/solution.py
@@ -345,10 +345,8 @@
     chips = count // 2
     cores = [(p, c) for p in range(chips) for c in range(2)]
     ahead = [(ring_device(p, c, chips), ring_device(p + 1 - 2 * c, c, chips)) for p, c in cores]
-    cross = [
-        (ring_device(p, c, chips), ring_device(p - 1 + 2 * c, 1 - c, chips)) for p, c in cores
-    ]
-    return ahead, cross
+    behind = [(target, source) for source, target in ahead]
+    return ahead, behind
 
 
 def ring_place(device, chips):
@@ -362,23 +360,19 @@
     back = (1 - 2 * (me & 1)) * (ring_place(me, chips) - ring_place(device, chips))
     back = (back + chips) & (chips - 1)
     other = (device ^ me) & 1
-    here = (back < depth) & (back > 0) | (back == 0) & (other == 1) | (back == depth) & (other == 0)
-    return jnp.where(here, jnp.where(back == 0, 0, 2 * back - 1 + other), chips)
+    arrival = jnp.where(back <= depth, 2 * back - 1, 2 * (chips - back))
+    arrival = jnp.where(back == 0, 0, arrival)
+    return jnp.where((other == 1) == (back == 0), arrival, chips)
 
 
 def scatter_place(device, me, count):
     chips = count // 2
     depth = chips // 2
-    ahead = (ring_place(device, chips) - ring_place(me, chips) + chips) & (chips - 1)
-    core = device & 1
-    handler = jnp.where((ahead & (depth - 1)) == 0, core, (ahead > depth).astype(jnp.int32))
-    steps = jnp.where(handler == 0, ahead, (chips - ahead) & (chips - 1))
-    place = jnp.where(
-        steps == depth,
-        0,
-        jnp.where(steps == 0, chips - 1, 2 * (depth - steps) - (core ^ handler)),
-    )
-    return place + jnp.where(handler == (me & 1), 0, chips)
+    away = (1 - 2 * (device & 1)) * (ring_place(device, chips) - ring_place(me, chips))
+    away = (away + chips) & (chips - 1)
+    hop = jnp.where(away > depth, 2 * (away - depth) - 1, 2 * (depth - away))
+    hop = jnp.where(away == 0, chips - 1, hop)
+    return hop + chips * ((device ^ me) & 1)
 
 
 def stationary(
@@ -403,7 +397,7 @@
     stored = near_blocks.shape[0]
     pairs = far_slot.shape[0]
     half = clusters // 2
-    ahead, cross = ring_pairs(count)
+    ways = ring_pairs(count)
     mate = [(i, i ^ 1) for i in range(count)]
     side = [(i, i ^ 2) for i in range(count)]
 
@@ -434,7 +428,7 @@
         rhs,
         basis_in,
     )
-    flow = [move(payload, ahead), move(payload, cross)]
+    flow = [move(payload, way) for way in ways]
     shards = [move(payload, mate)]
     lists = jnp.concatenate([lists, move(lists, mate)], axis=0)
     couple = after(jnp.transpose(far_coupling, (2, 1, 0)), payload)
@@ -446,7 +440,7 @@
             )
         shards.append(flow[x])
         if k < chips - 2:
-            flow[x] = move(flow[x], ahead)
+            flow[x] = move(flow[x], ways[x])
 
     quarter = chips // 2
 
@@ -482,6 +476,29 @@
         )(lists, *shards, near_blocks, mate_blocks)
         return kept, sends
 
+    def far_field(couple):
+        return pl.pallas_call(
+            far_kernel,
+            out_shape=jax.ShapeDtypeStruct((clusters, directions, unknowns), jnp.float32),
+            in_specs=[whole()] * 2 + [whole(pltpu.SMEM)] + [whole()] * 5,
+            out_specs=whole(),
+            compiler_params=pltpu.CompilerParams(vmem_limit_bytes=FAR_VMEM),
+            cost_estimate=pl.CostEstimate(
+                flops=4 * clusters * rank_k * pairs * rank_k * unknowns,
+                bytes_accessed=8 << 20,
+                transcendentals=0,
+            ),
+            name="far",
+        )(
+            *coefs,
+            here,
+            couple,
+            far_slot.reshape(1, pairs),
+            far_dev.reshape(1, pairs),
+            far_cslot.reshape(1, pairs),
+            basis_out,
+        )
+
     early, (*sends, coef) = near(0, lists)
     mates = [move(sends[0], mate), move(sends[1], mate)]
     coefs = [coef, move(coef, mate)]
@@ -499,40 +516,21 @@
         return (flow.astype(jnp.float32) + term(k)).astype(jnp.bfloat16)
 
     flow = lax.optimization_barrier([term(0).astype(jnp.bfloat16), term(1).astype(jnp.bfloat16)])
-    lists, couple = after(lists, *flow), after(couple, *flow)
+    lists = after(lists, *flow)
     mates += [move(after(send, *flow), mate) for send in sends[2:]]
-    flow = [move(part, ahead) for part in flow]
+    flow = [move(part, way) for part, way in zip(flow, ways)]
     late, sends = near(1, lists)
     kept.append(late)
     mates += [move(send, mate) for send in sends]
-    far = pl.pallas_call(
-        far_kernel,
-        out_shape=jax.ShapeDtypeStruct((clusters, directions, unknowns), jnp.float32),
-        in_specs=[whole()] * 2 + [whole(pltpu.SMEM)] + [whole()] * 5,
-        out_specs=whole(),
-        compiler_params=pltpu.CompilerParams(vmem_limit_bytes=FAR_VMEM),
-        cost_estimate=pl.CostEstimate(
-            flops=4 * clusters * rank_k * pairs * rank_k * unknowns,
-            bytes_accessed=8 << 20,
-            transcendentals=0,
-        ),
-        name="far",
-    )(
-        *coefs,
-        here,
-        couple,
-        far_slot.reshape(1, pairs),
-        far_dev.reshape(1, pairs),
-        far_cslot.reshape(1, pairs),
-        basis_out,
-    )
     for k in range(2, chips - 1):
         x = k % 2
-        flow[x] = move(tied(add(flow[x], k), k, *([far] if k == chips - 3 else [])), ahead)
-    flow[1] = move(flow[1], mate)
-    total = far + term(chips - 1) + flow[0].astype(jnp.float32)
-    total = lax.optimization_barrier(total)
-    return (total + flow[1].astype(jnp.float32)).astype(jnp.bfloat16)
+        flow[x] = tied(add(flow[x], k), k)
+        if k == chips - 2:
+            couple = after(couple, flow[x])
+        flow[x] = move(flow[x], ways[x])
+    far = far_field(couple)
+    total = far + term(chips - 1) + flow[1].astype(jnp.float32)
+    return (total + flow[0].astype(jnp.float32)).astype(jnp.bfloat16)
 
 
 def on_device(*args):

time: 74.1 us -> 79.1 us (1.067)
  the two profiles are of different devices: /device:TPU:0 before, /device:TPU:28 now
where the time goes in v10:
time: 79.1 us; the launch traced here: 78.7 us
  waiting for transfers between devices  43.9 us (55%)
  Pallas kernels  15.9 us (20%)
  starting transfers between devices  15.5 us (20%)
  other arithmetic  2.22 us (3%)
  local copies, waits for them, and re-layouts  0.97 us (1%)
    ppermute x26, waiting for transfers between devices, move(): return lax.ppermute(values, 'blk', where)  43.9 us
    ppermute x26, starting transfers between devices, move(): return lax.ppermute(values, 'blk', where)  15.5 us
    pallas_call x2, Pallas kernels, near(): pl.pallas_call(functools.partial(near_kernel, late, BATCH, LAG, chips, le...  11.4 us
    pallas_call x1, Pallas kernels, far_field(): pl.pallas_call(far_kernel, out_shape=jax.ShapeDtypeStruct((clusters, dire...  2.51 us
    pallas_call x1, Pallas kernels, stationary(): pl.pallas_call(functools.partial(prologue_kernel, count), out_shape=[jax....  2.01 us
  transfers between devices with their start and end apart: 26, of which 13 were waited for; matrix products, arithmetic and copies ran while one was open for 3% of the time, Pallas kernels for 13%

profile of v10, /device:TPU:28, one launch (start us, length us, event | category | flops | bytes accessed | tf_op | source)
XLA Modules:
  0.0 78.7 jit_solution(10423459862379101617)
XLA Ops:
  0.0 2.0 %prologue.1 = (bf16[1152,128]{1,0:T(8,128)(2,1)}, s32[8,128]{1,0:T(8,128)}) custom-call(s32[1]{0:T(128)} %bitcast.me_ref.refs_2_, s32[1,128]{1,0:T(1,128)} %bitcast.14, s32[1,128]{1,0:T(1,128)} %bitcast.15, s32[1,128]{1,0:T(1,128)} %bitcast.16, bf16[16,64,128]{2,1,0:T(8,128)(2,1)} %rhs_ref.1, bf16[16,16,128]{2,1,0:T(8,128)(2,1)} %basis_ref.1), custom_call_target="tpu_custom_call" | custom-call | tf_op jit(solution)/shard_map/prologue/pallas_call | solution.py:413
  2.0 0.4 collective-permute-start
  2.5 1.6 %collective-permute-start.5 = (bf16[1152,128]{1,0:T(8,128)(2,1)}, bf16[1152,128]{1,0:T(8,128)(2,1)S(1)}, u32[]{:S(2)}, u32[]{:S(2)}) collective-permute-start(bf16[1152,128]{1,0:T(8,128)(2,1)} %get-tuple-element.40), channel_id=1, source_target_pairs={{4,0},{3,1},{8,4},{1,5},{12,8},{5,9},{14,12},{9,13},{10,14},{13,15... | collective-permute-start | bytes 884744 | tf_op jit(solution)/shard_map/ppermute | solution.py:405
  4.0 7.8 %collective-permute-done.refs_1_ = bf16[1152,128]{1,0:T(8,128)(2,1)S(1)} collective-permute-done((bf16[1152,128]{1,0:T(8,128)(2,1)}, bf16[1152,128]{1,0:T(8,128)(2,1)S(1)}, u32[]{:S(2)}, u32[]{:S(2)}) %collective-permute-start) | collective-permute-done | bytes 294944 | tf_op jit(solution)/shard_map/ppermute | solution.py:405
  11.9 0.9 %copy.14 = bf16[256,16,16]{0,1,2:T(8,128)(2,1)S(1)} copy(bf16[256,16,16]{0,2,1:T(8,128)(2,1)} %param.16) | data formatting | bytes 262144 | tf_op args[5]
  12.8 0.4 collective-permute-done.4
  13.3 0.7 pad_add_fusion.list_ref
  13.9 2.0 %collective-permute-start.6 = (bf16[1152,128]{1,0:T(8,128)(2,1)S(1)}, bf16[1152,128]{1,0:T(8,128)(2,1)S(1)}, u32[]{:S(2)}, u32[]{:S(2)}) collective-permute-start(bf16[1152,128]{1,0:T(8,128)(2,1)S(1)} %collective-permute-done.5.refs_2_), channel_id=1, source_target_pairs={{4,0},{3,1},{8,4},{1,5},{12,8},{5,9},{14,12},{9,13},{10,14},{13,15... | collective-permute-start | bytes 884744 | tf_op jit(solution)/shard_map/ppermute | solution.py:405
  16.0 4.2 %collective-permute-done.1.refs_3_ = bf16[1152,128]{1,0:T(8,128)(2,1)S(1)} collective-permute-done((bf16[1152,128]{1,0:T(8,128)(2,1)S(1)}, bf16[1152,128]{1,0:T(8,128)(2,1)S(1)}, u32[]{:S(2)}, u32[]{:S(2)}) %collective-permute-start.1) | collective-permute-done | bytes 294944 | tf_op jit(solution)/shard_map/ppermute | solution.py:405
  20.1 3.1 %collective-permute-done.6.refs_4_ = bf16[1152,128]{1,0:T(8,128)(2,1)S(1)} collective-permute-done((bf16[1152,128]{1,0:T(8,128)(2,1)S(1)}, bf16[1152,128]{1,0:T(8,128)(2,1)S(1)}, u32[]{:S(2)}, u32[]{:S(2)}) %collective-permute-start.6) | collective-permute-done | bytes 294944 | tf_op jit(solution)/shard_map/ppermute | solution.py:405
  23.3 2.5 %collective-permute-start.8 = (bf16[1152,128]{1,0:T(8,128)(2,1)S(1)}, bf16[1152,128]{1,0:T(8,128)(2,1)S(1)}, u32[]{:S(2)}, u32[]{:S(2)}) collective-permute-start(bf16[1152,128]{1,0:T(8,128)(2,1)S(1)} %collective-permute-done.6.refs_4_), channel_id=1, source_target_pairs={{4,0},{3,1},{8,4},{1,5},{12,8},{5,9},{14,12},{9,13},{10,14},{13,15... | collective-permute-start | bytes 884744 | tf_op jit(solution)/shard_map/ppermute | solution.py:405
  25.8 3.5 %collective-permute-done.7.refs_5_ = bf16[1152,128]{1,0:T(8,128)(2,1)S(1)} collective-permute-done((bf16[1152,128]{1,0:T(8,128)(2,1)S(1)}, bf16[1152,128]{1,0:T(8,128)(2,1)S(1)}, u32[]{:S(2)}, u32[]{:S(2)}) %collective-permute-start.7) | collective-permute-done | bytes 294944 | tf_op jit(solution)/shard_map/ppermute | solution.py:405
  29.3 3.6 %collective-permute-done.8.refs_6_ = bf16[1152,128]{1,0:T(8,128)(2,1)S(1)} collective-permute-done((bf16[1152,128]{1,0:T(8,128)(2,1)S(1)}, bf16[1152,128]{1,0:T(8,128)(2,1)S(1)}, u32[]{:S(2)}, u32[]{:S(2)}) %collective-permute-start.8) | collective-permute-done | bytes 294944 | tf_op jit(solution)/shard_map/ppermute | solution.py:405
  32.9 3.2 %collective-permute-done.9.refs_7_ = bf16[1152,128]{1,0:T(8,128)(2,1)S(1)} collective-permute-done((bf16[1152,128]{1,0:T(8,128)(2,1)S(1)}, bf16[1152,128]{1,0:T(8,128)(2,1)S(1)}, u32[]{:S(2)}, u32[]{:S(2)}) %collective-permute-start.9) | collective-permute-done | bytes 294944 | tf_op jit(solution)/shard_map/ppermute | solution.py:405
  36.0 5.8 %near.2 = (f32[64,64,128]{2,1,0:T(8,128)S(1)}, bf16[16,64,128]{2,1,0:T(8,128)(2,1)S(1)}, bf16[16,64,128]{2,1,0:T(8,128)(2,1)S(1)}, bf16[16,64,128]{2,1,0:T(8,128...) custom-call(s32[16,128]{1,0:T(8,128)S(1)} %pad_add_fusion.list_ref, ...), custom_call_target="tpu_custom_call" | custom-call | flops 2147483648 | bytes 16777216 | tf_op jit(solution)/shard_map/near/pallas_call | solution.py:449
  42.0 0.5 collective-permute-start.11
  42.5 1.0 %collective-permute-done.12 = bf16[16,64,128]{2,1,0:T(8,128)(2,1)S(1)} collective-permute-done((bf16[16,64,128]{2,1,0:T(8,128)(2,1)S(1)}, bf16[16,64,128]{2,1,0:T(8,128)(2,1)S(1)}, u32[]{:S(2)}, u32[]{:S(2)}) %collective-permute-start.12) | collective-permute-done | bytes 262176 | tf_op jit(solution)/shard_map/ppermute | solution.py:405
  43.5 0.4 collective-permute-done.11
  44.0 0.2 collective-permute-start.14
  44.2 2.0 %collective-permute-start.17 = (bf16[16,64,128]{2,1,0:T(8,128)(2,1)S(1)}, bf16[16,64,128]{2,1,0:T(8,128)(2,1)S(1)}, u32[]{:S(2)}, u32[]{:S(2)}) collective-permute-start(bf16[16,64,128]{2,1,0:T(8,128)(2,1)S(1)} %get-tuple-element.54), channel_id=1, source_target_pairs={{4,0},{3,1},{8,4},{1,5},{12,8},{5,9},{14,12},{9,13},{10,14},{13,15... | collective-permute-start | bytes 786440 | tf_op jit(solution)/shard_map/ppermute | solution.py:405
  46.3 5.5 %near.3 = (f32[64,64,128]{2,1,0:T(8,128)S(1)}, bf16[16,64,128]{2,1,0:T(8,128)(2,1)S(1)}, bf16[16,64,128]{2,1,0:T(8,128)(2,1)S(1)}, bf16[16,64,128]{2,1,0:T(8,128)(2,1)S(1)}, bf16[16,64,128]{2,1,0:T(8,128)(2,1)S(1)}) custom-call(s32[16,128]{1,0:T(8,128)S(1)} %pad_add_fusion.list_ref, bf16[1152,128]{1,0:T(8,128)(2,1)S(1)} %collective-permute-done.3.refs_0_, ...), custom_call_target="tpu_custom_call" | custom-call | flops 2147483648 | bytes 16777216 | tf_op jit(solution)/shard_map/near/pallas_call | solution.py:449
  51.8 1.1 %collective-permute-start.18 = (bf16[16,64,128]{2,1,0:T(8,128)(2,1)S(1)}, bf16[16,64,128]{2,1,0:T(8,128)(2,1)S(1)}, u32[]{:S(2)}, u32[]{:S(2)}) collective-permute-start(bf16[16,64,128]{2,1,0:T(8,128)(2,1)S(1)} %get-tuple-element.62), channel_id=1, source_target_pairs={{0,1},{1,0},{2,3},{3,2},{4,5},{5,4},{6,7},{7,6},{8,9},{9,8},{10,11... | collective-permute-start | bytes 786440 | tf_op jit(solution)/shard_map/ppermute | solution.py:405
  53.2 0.5 collective-permute-start.22
  53.8 0.2 collective-permute-done.18
  54.1 1.8 %collective-permute-start.21 = (bf16[16,64,128]{2,1,0:T(8,128)(2,1)S(1)}, bf16[16,64,128]{2,1,0:T(8,128)(2,1)S(1)}, u32[]{:S(2)}, u32[]{:S(2)}) collective-permute-start(bf16[16,64,128]{2,1,0:T(8,128)(2,1)S(1)} %add_convert_fusion.4), channel_id=1, source_target_pairs={{4,0},{3,1},{8,4},{1,5},{12,8},{5,9},{14,12},{9,13},{10,14},{13,15... | collective-permute-start | bytes 786440 | tf_op jit(solution)/shard_map/ppermute | solution.py:405
  55.8 6.1 %collective-permute-done.16 = bf16[16,64,128]{2,1,0:T(8,128)(2,1)S(1)} collective-permute-done((bf16[16,64,128]{2,1,0:T(8,128)(2,1)S(1)}, bf16[16,64,128]{2,1,0:T(8,128)(2,1)S(1)}, u32[]{:S(2)}, u32[]{:S(2)}) %collective-permute-start.16) | collective-permute-done | bytes 262176 | tf_op jit(solution)/shard_map/ppermute | solution.py:405
  62.2 0.5 collective-permute-start.23
  62.8 2.0 %collective-permute-start.24 = (bf16[16,64,128]{2,1,0:T(8,128)(2,1)S(1)}, bf16[16,64,128]{2,1,0:T(8,128)(2,1)S(1)}, u32[]{:S(2)}, u32[]{:S(2)}) collective-permute-start(bf16[16,64,128]{2,1,0:T(8,128)(2,1)S(1)} %add_convert_fusion.2), channel_id=1, source_target_pairs={{4,0},{3,1},{8,4},{1,5},{12,8},{5,9},{14,12},{9,13},{10,14},{13,15... | collective-permute-start | bytes 786440 | tf_op jit(solution)/shard_map/ppermute | solution.py:405
  64.8 6.5 %collective-permute-done.20 = bf16[16,64,128]{2,1,0:T(8,128)(2,1)S(1)} collective-permute-done((bf16[16,64,128]{2,1,0:T(8,128)(2,1)S(1)}, bf16[16,64,128]{2,1,0:T(8,128)(2,1)S(1)}, u32[]{:S(2)}, u32[]{:S(2)}) %collective-permute-start.20) | collective-permute-done | bytes 262176 | tf_op jit(solution)/shard_map/ppermute | solution.py:405
  71.5 2.5 %far.1 = f32[16,64,128]{2,1,0:T(8,128)S(1)} custom-call(bf16[1024,128]{1,0:T(8,128)(2,1)S(1)} %get-tuple-element.47.refs_0_, bf16[1024,128]{1,0:T(8,128)(2,1)S(1)} %collective-permute-done.10.refs_1_, s32[1]{0:T(128)} %bitcast.me_ref.refs_2_, bf16[16,16,256]{2,1,0:T(8,128)(2,1)S(1)} %bitcast.10, s32[1,256]{1,0:T(1,128)S(1)} %bitcast.11, ...), custom_call_target="tpu_custom_call" | custom-call | flops 536870912 | bytes 8388608 | tf_op jit(solution)/shard_map/far/pallas_call | solution.py:480
  74.0 3.8 %collective-permute-done.25 = bf16[16,64,128]{2,1,0:T(8,128)(2,1)S(1)} collective-permute-done((bf16[16,64,128]{2,1,0:T(8,128)(2,1)S(1)}, bf16[16,64,128]{2,1,0:T(8,128)(2,1)S(1)}, u32[]{:S(2)}, u32[]{:S(2)}) %collective-permute-start.25) | collective-permute-done | bytes 262176 | tf_op jit(solution)/shard_map/ppermute | solution.py:405
  77.8 0.9 %add_convert_fusion = bf16[16,64,128]{2,1,0:T(8,128)(2,1)} fusion(bf16[16,64,128]{2,1,0:T(8,128)(2,1)S(1)} %collective-permute-done.25, bf16[16,64,128]{2,1,0:T(8,128)(2,1)S(1)} %collective-permute-done.24, f32[16,64,128]{2,1,0:T(8,128)S(1)} %far.1, bf16[16,64,128]{2,1,0:T(8,128)(2,1)S(1)} %collective-permute-done.23, f32[64,64,128]{2,1,0:T(8,128)S(1)} %get-tuple-element.60), kind=kLoop, calls=%fused_computation | loop fusion | flops 1048576 | bytes 2097152 | tf_op jit(solution)/shard_map/convert_element_type | solution.py:533
  (41 shorter events, 1.1 us)
Async XLA Ops:
  0.0 20.1 %collective-permute-start.2 = (bf16[128,128,128]{2,1,0:T(8,128)(2,1)}, bf16[128,128,128]{2,1,0:T(8,128)(2,1)}, u32[]{:S(2)}, u32[]{:S(2)}) collective-permute-start(bf16[128,128,128]{2,1,0:T(8,128)(2,1)} %refs_8_.3), channel_id=1, source_target_pairs={{0,1},{1,0},{2,3},{3,2},{4,5},{5,4},{6,7},{7,6},{8,9},{9,8},{10,11... | collective-permute-start | bytes 12582920 | tf_op jit(solution)/shard_map/ppermute | solution.py:405
  2.0 9.9 %collective-permute-start = (bf16[1152,128]{1,0:T(8,128)(2,1)}, bf16[1152,128]{1,0:T(8,128)(2,1)S(1)}, u32[]{:S(2)}, u32[]{:S(2)}) collective-permute-start(bf16[1152,128]{1,0:T(8,128)(2,1)} %get-tuple-element.40), channel_id=1, source_target_pairs={{0,4},{1,3},{4,8},{5,1},{8,12},{9,5},{12,14},{13,9},{14,10},{15,13... | collective-permute-start | bytes 884744 | tf_op jit(solution)/shard_map/ppermute | solution.py:405
  2.5 11.5 %collective-permute-start.5 = (bf16[1152,128]{1,0:T(8,128)(2,1)}, bf16[1152,128]{1,0:T(8,128)(2,1)S(1)}, u32[]{:S(2)}, u32[]{:S(2)}) collective-permute-start(bf16[1152,128]{1,0:T(8,128)(2,1)} %get-tuple-element.40), channel_id=1, source_target_pairs={{4,0},{3,1},{8,4},{1,5},{12,8},{5,9},{14,12},{9,13},{10,14},{13,15... | collective-permute-start | bytes 884744 | tf_op jit(solution)/shard_map/ppermute | solution.py:405
  4.0 11.9 %collective-permute-start.3 = (bf16[1152,128]{1,0:T(8,128)(2,1)}, bf16[1152,128]{1,0:T(8,128)(2,1)S(1)}, u32[]{:S(2)}, u32[]{:S(2)}) collective-permute-start(bf16[1152,128]{1,0:T(8,128)(2,1)} %get-tuple-element.40), channel_id=1, source_target_pairs={{0,1},{1,0},{2,3},{3,2},{4,5},{5,4},{6,7},{7,6},{8,9},{9,8},{10,11... | collective-permute-start | bytes 884744 | tf_op jit(solution)/shard_map/ppermute | solution.py:405
  11.9 8.3 %collective-permute-start.1 = (bf16[1152,128]{1,0:T(8,128)(2,1)S(1)}, bf16[1152,128]{1,0:T(8,128)(2,1)S(1)}, u32[]{:S(2)}, u32[]{:S(2)}) collective-permute-start(bf16[1152,128]{1,0:T(8,128)(2,1)S(1)} %collective-permute-done.refs_1_), channel_id=1, source_target_pairs={{0,4},{1,3},{4,8},{5,1},{8,12},{9,5},{12,14},{13,9},{14,10},{15,13... | collective-permute-start | bytes 884744 | tf_op jit(solution)/shard_map/ppermute | solution.py:405
  11.9 1.4 %collective-permute-start.4 = (s32[8,128]{1,0:T(8,128)}, s32[8,128]{1,0:T(8,128)S(1)}, u32[]{:S(2)}, u32[]{:S(2)}) collective-permute-start(s32[8,128]{1,0:T(8,128)} %get-tuple-element.41), channel_id=1, source_target_pairs={{0,1},{1,0},{2,3},{3,2},{4,5},{5,4},{6,7},{7,6},{8,9},{9,8},{10,11... | collective-permute-start | bytes 12296 | tf_op jit(solution)/shard_map/ppermute | solution.py:405
  13.9 9.3 %collective-permute-start.6 = (bf16[1152,128]{1,0:T(8,128)(2,1)S(1)}, bf16[1152,128]{1,0:T(8,128)(2,1)S(1)}, u32[]{:S(2)}, u32[]{:S(2)}) collective-permute-start(bf16[1152,128]{1,0:T(8,128)(2,1)S(1)} %collective-permute-done.5.refs_2_), channel_id=1, source_target_pairs={{4,0},{3,1},{8,4},{1,5},{12,8},{5,9},{14,12},{9,13},{10,14},{13,15... | collective-permute-start | bytes 884744 | tf_op jit(solution)/shard_map/ppermute | solution.py:405
  20.1 9.2 %collective-permute-start.7 = (bf16[1152,128]{1,0:T(8,128)(2,1)S(1)}, bf16[1152,128]{1,0:T(8,128)(2,1)S(1)}, u32[]{:S(2)}, u32[]{:S(2)}) collective-permute-start(bf16[1152,128]{1,0:T(8,128)(2,1)S(1)} %collective-permute-done.1.refs_3_), channel_id=1, source_target_pairs={{0,4},{1,3},{4,8},{5,1},{8,12},{9,5},{12,14},{13,9},{14,10},{15,13... | collective-permute-start | bytes 884744 | tf_op jit(solution)/shard_map/ppermute | solution.py:405
  23.3 9.6 %collective-permute-start.8 = (bf16[1152,128]{1,0:T(8,128)(2,1)S(1)}, bf16[1152,128]{1,0:T(8,128)(2,1)S(1)}, u32[]{:S(2)}, u32[]{:S(2)}) collective-permute-start(bf16[1152,128]{1,0:T(8,128)(2,1)S(1)} %collective-permute-done.6.refs_4_), channel_id=1, source_target_pairs={{4,0},{3,1},{8,4},{1,5},{12,8},{5,9},{14,12},{9,13},{10,14},{13,15... | collective-permute-start | bytes 884744 | tf_op jit(solution)/shard_map/ppermute | solution.py:405
  29.3 6.7 %collective-permute-start.9 = (bf16[1152,128]{1,0:T(8,128)(2,1)S(1)}, bf16[1152,128]{1,0:T(8,128)(2,1)S(1)}, u32[]{:S(2)}, u32[]{:S(2)}) collective-permute-start(bf16[1152,128]{1,0:T(8,128)(2,1)S(1)} %collective-permute-done.7.refs_5_), channel_id=1, source_target_pairs={{0,4},{1,3},{4,8},{5,1},{8,12},{9,5},{12,14},{13,9},{14,10},{15,13... | collective-permute-start | bytes 884744 | tf_op jit(solution)/shard_map/ppermute | solution.py:405
  41.9 1.6 %collective-permute-start.12 = (bf16[16,64,128]{2,1,0:T(8,128)(2,1)S(1)}, bf16[16,64,128]{2,1,0:T(8,128)(2,1)S(1)}, u32[]{:S(2)}, u32[]{:S(2)}) collective-permute-start(bf16[16,64,128]{2,1,0:T(8,128)(2,1)S(1)} %get-tuple-element.51), channel_id=1, source_target_pairs={{0,1},{1,0},{2,3},{3,2},{4,5},{5,4},{6,7},{7,6},{8,9},{9,8},{10,11... | collective-permute-start | bytes 786440 | tf_op jit(solution)/shard_map/ppermute | solution.py:405
  42.0 1.9 %collective-permute-start.11 = (bf16[16,64,128]{2,1,0:T(8,128)(2,1)S(1)}, bf16[16,64,128]{2,1,0:T(8,128)(2,1)S(1)}, u32[]{:S(2)}, u32[]{:S(2)}) collective-permute-start(bf16[16,64,128]{2,1,0:T(8,128)(2,1)S(1)} %get-tuple-element.50), channel_id=1, source_target_pairs={{0,1},{1,0},{2,3},{3,2},{4,5},{5,4},{6,7},{7,6},{8,9},{9,8},{10,11... | collective-permute-start | bytes 786440 | tf_op jit(solution)/shard_map/ppermute | solution.py:405
  44.0 8.9 %collective-permute-start.14 = (bf16[16,64,128]{2,1,0:T(8,128)(2,1)S(1)}, bf16[16,64,128]{2,1,0:T(8,128)(2,1)S(1)}, u32[]{:S(2)}, u32[]{:S(2)}) collective-permute-start(bf16[16,64,128]{2,1,0:T(8,128)(2,1)S(1)} %get-tuple-element.55), channel_id=1, source_target_pairs={{0,1},{1,0},{2,3},{3,2},{4,5},{5,4},{6,7},{7,6},{8,9},{9,8},{10,11... | collective-permute-start | bytes 786440 | tf_op jit(solution)/shard_map/ppermute | solution.py:405
  44.2 8.7 %collective-permute-start.13 = (bf16[16,64,128]{2,1,0:T(8,128)(2,1)S(1)}, bf16[16,64,128]{2,1,0:T(8,128)(2,1)S(1)}, u32[]{:S(2)}, u32[]{:S(2)}) collective-permute-start(bf16[16,64,128]{2,1,0:T(8,128)(2,1)S(1)} %get-tuple-element.52), channel_id=1, source_target_pairs={{0,4},{1,3},{4,8},{5,1},{8,12},{9,5},{12,14},{13,9},{14,10},{15,13... | collective-permute-start | bytes 786440 | tf_op jit(solution)/shard_map/ppermute | solution.py:405
  44.2 9.4 %collective-permute-start.17 = (bf16[16,64,128]{2,1,0:T(8,128)(2,1)S(1)}, bf16[16,64,128]{2,1,0:T(8,128)(2,1)S(1)}, u32[]{:S(2)}, u32[]{:S(2)}) collective-permute-start(bf16[16,64,128]{2,1,0:T(8,128)(2,1)S(1)} %get-tuple-element.54), channel_id=1, source_target_pairs={{4,0},{3,1},{8,4},{1,5},{12,8},{5,9},{14,12},{9,13},{10,14},{13,15... | collective-permute-start | bytes 786440 | tf_op jit(solution)/shard_map/ppermute | solution.py:405
  46.3 6.8 %collective-permute-start.15 = (bf16[16,64,128]{2,1,0:T(8,128)(2,1)S(1)}, bf16[16,64,128]{2,1,0:T(8,128)(2,1)S(1)}, u32[]{:S(2)}, u32[]{:S(2)}) collective-permute-start(bf16[16,64,128]{2,1,0:T(8,128)(2,1)S(1)} %get-tuple-element.57), channel_id=1, source_target_pairs={{0,1},{1,0},{2,3},{3,2},{4,5},{5,4},{6,7},{7,6},{8,9},{9,8},{10,11... | collective-permute-start | bytes 786440 | tf_op jit(solution)/shard_map/ppermute | solution.py:405
  51.8 2.2 %collective-permute-start.18 = (bf16[16,64,128]{2,1,0:T(8,128)(2,1)S(1)}, bf16[16,64,128]{2,1,0:T(8,128)(2,1)S(1)}, u32[]{:S(2)}, u32[]{:S(2)}) collective-permute-start(bf16[16,64,128]{2,1,0:T(8,128)(2,1)S(1)} %get-tuple-element.62), channel_id=1, source_target_pairs={{0,1},{1,0},{2,3},{3,2},{4,5},{5,4},{6,7},{7,6},{8,9},{9,8},{10,11... | collective-permute-start | bytes 786440 | tf_op jit(solution)/shard_map/ppermute | solution.py:405
  53.0 8.9 %collective-permute-start.16 = (bf16[16,64,128]{2,1,0:T(8,128)(2,1)S(1)}, bf16[16,64,128]{2,1,0:T(8,128)(2,1)S(1)}, u32[]{:S(2)}, u32[]{:S(2)}) collective-permute-start(bf16[16,64,128]{2,1,0:T(8,128)(2,1)S(1)} %add_convert_fusion.5), channel_id=1, source_target_pairs={{0,4},{1,3},{4,8},{5,1},{8,12},{9,5},{12,14},{13,9},{14,10},{15,13... | collective-permute-start | bytes 786440 | tf_op jit(solution)/shard_map/ppermute | solution.py:405
  53.1 9.0 %collective-permute-start.19 = (bf16[16,64,128]{2,1,0:T(8,128)(2,1)S(1)}, bf16[16,64,128]{2,1,0:T(8,128)(2,1)S(1)}, u32[]{:S(2)}, u32[]{:S(2)}) collective-permute-start(bf16[16,64,128]{2,1,0:T(8,128)(2,1)S(1)} %get-tuple-element.64), channel_id=1, source_target_pairs={{0,1},{1,0},{2,3},{3,2},{4,5},{5,4},{6,7},{7,6},{8,9},{9,8},{10,11... | collective-permute-start | bytes 786440 | tf_op jit(solution)/shard_map/ppermute | solution.py:405
  53.2 9.6 %collective-permute-start.22 = (bf16[16,64,128]{2,1,0:T(8,128)(2,1)S(1)}, bf16[16,64,128]{2,1,0:T(8,128)(2,1)S(1)}, u32[]{:S(2)}, u32[]{:S(2)}) collective-permute-start(bf16[16,64,128]{2,1,0:T(8,128)(2,1)S(1)} %get-tuple-element.68), channel_id=1, source_target_pairs={{0,1},{1,0},{2,3},{3,2},{4,5},{5,4},{6,7},{7,6},{8,9},{9,8},{10,11... | collective-permute-start | bytes 786440 | tf_op jit(solution)/shard_map/ppermute | solution.py:405
  53.8 17.7 %copy-start = (bf16[16,16,128]{2,1,0:T(8,128)(2,1)S(1)}, bf16[16,16,128]{2,1,0:T(8,128)(2,1)}, u32[]{:S(2)}) copy-start(bf16[16,16,128]{2,1,0:T(8,128)(2,1)} %refs_7_.1) | copy-start | bytes 196612
  53.8 17.7 %copy-start.1 = (s32[256]{0:T(256)S(1)}, s32[256]{0:T(256)}, u32[]{:S(2)}) copy-start(s32[256]{0:T(256)} %param.17) | copy-start | bytes 3076
  53.8 17.7 %copy-start.2 = (s32[256,1]{0,1:T(1,128)S(1)}, s32[256,1]{0,1:T(1,128)}, u32[]{:S(2)}) copy-start(s32[256,1]{0,1:T(1,128)} %param.18) | copy-start | bytes 3076
  53.8 17.7 %copy-start.3 = (s32[256]{0:T(256)S(1)}, s32[256]{0:T(256)}, u32[]{:S(2)}) copy-start(s32[256]{0:T(256)} %param.19) | copy-start | bytes 3076
  54.1 8.7 %collective-permute-start.21 = (bf16[16,64,128]{2,1,0:T(8,128)(2,1)S(1)}, bf16[16,64,128]{2,1,0:T(8,128)(2,1)S(1)}, u32[]{:S(2)}, u32[]{:S(2)}) collective-permute-start(bf16[16,64,128]{2,1,0:T(8,128)(2,1)S(1)} %add_convert_fusion.4), channel_id=1, source_target_pairs={{4,0},{3,1},{8,4},{1,5},{12,8},{5,9},{14,12},{9,13},{10,14},{13,15... | collective-permute-start | bytes 786440 | tf_op jit(solution)/shard_map/ppermute | solution.py:405
  62.1 9.2 %collective-permute-start.20 = (bf16[16,64,128]{2,1,0:T(8,128)(2,1)S(1)}, bf16[16,64,128]{2,1,0:T(8,128)(2,1)S(1)}, u32[]{:S(2)}, u32[]{:S(2)}) collective-permute-start(bf16[16,64,128]{2,1,0:T(8,128)(2,1)S(1)} %add_convert_fusion.3), channel_id=1, source_target_pairs={{0,4},{1,3},{4,8},{5,1},{8,12},{9,5},{12,14},{13,9},{14,10},{15,13... | collective-permute-start | bytes 786440 | tf_op jit(solution)/shard_map/ppermute | solution.py:405
  62.1 9.3 %collective-permute-start.10 = (bf16[1024,128]{1,0:T(8,128)(2,1)S(1)}, bf16[1024,128]{1,0:T(8,128)(2,1)S(1)}, u32[]{:S(2)}, u32[]{:S(2)}) collective-permute-start(bf16[1024,128]{1,0:T(8,128)(2,1)S(1)} %get-tuple-element.47.refs_0_), channel_id=1, source_target_pairs={{0,1},{1,0},{2,3},{3,2},{4,5},{5,4},{6,7},{7,6},{8,9},{9,8},{10,11... | collective-permute-start | bytes 786440 | tf_op jit(solution)/shard_map/ppermute | solution.py:405
  62.2 9.2 %collective-permute-start.23 = (bf16[16,64,128]{2,1,0:T(8,128)(2,1)S(1)}, bf16[16,64,128]{2,1,0:T(8,128)(2,1)S(1)}, u32[]{:S(2)}, u32[]{:S(2)}) collective-permute-start(bf16[16,64,128]{2,1,0:T(8,128)(2,1)S(1)} %get-tuple-element.70), channel_id=1, source_target_pairs={{0,1},{1,0},{2,3},{3,2},{4,5},{5,4},{6,7},{7,6},{8,9},{9,8},{10,11... | collective-permute-start | bytes 786440 | tf_op jit(solution)/shard_map/ppermute | solution.py:405
  62.8 11.2 %collective-permute-start.24 = (bf16[16,64,128]{2,1,0:T(8,128)(2,1)S(1)}, bf16[16,64,128]{2,1,0:T(8,128)(2,1)S(1)}, u32[]{:S(2)}, u32[]{:S(2)}) collective-permute-start(bf16[16,64,128]{2,1,0:T(8,128)(2,1)S(1)} %add_convert_fusion.2), channel_id=1, source_target_pairs={{4,0},{3,1},{8,4},{1,5},{12,8},{5,9},{14,12},{9,13},{10,14},{13,15... | collective-permute-start | bytes 786440 | tf_op jit(solution)/shard_map/ppermute | solution.py:405
  71.4 6.4 %collective-permute-start.25 = (bf16[16,64,128]{2,1,0:T(8,128)(2,1)S(1)}, bf16[16,64,128]{2,1,0:T(8,128)(2,1)S(1)}, u32[]{:S(2)}, u32[]{:S(2)}) collective-permute-start(bf16[16,64,128]{2,1,0:T(8,128)(2,1)S(1)} %add_convert_fusion.1), channel_id=1, source_target_pairs={{0,4},{1,3},{4,8},{5,1},{8,12},{9,5},{12,14},{13,9},{14,10},{15,13... | collective-permute-start | bytes 786440 | tf_op jit(solution)/shard_map/ppermute | solution.py:405

commit v11 on v10

--- a/solution.py
+++ b/solution.py
@@ -345,8 +345,7 @@
     chips = count // 2
     cores = [(p, c) for p in range(chips) for c in range(2)]
     ahead = [(ring_device(p, c, chips), ring_device(p + 1 - 2 * c, c, chips)) for p, c in cores]
-    behind = [(target, source) for source, target in ahead]
-    return ahead, behind
+    return ahead
 
 
 def ring_place(device, chips):
@@ -360,19 +359,23 @@
     back = (1 - 2 * (me & 1)) * (ring_place(me, chips) - ring_place(device, chips))
     back = (back + chips) & (chips - 1)
     other = (device ^ me) & 1
-    arrival = jnp.where(back <= depth, 2 * back - 1, 2 * (chips - back))
-    arrival = jnp.where(back == 0, 0, arrival)
-    return jnp.where((other == 1) == (back == 0), arrival, chips)
+    here = (back < depth) & (back > 0) | (back == 0) & (other == 1) | (back == depth) & (other == 0)
+    return jnp.where(here, jnp.where(back == 0, 0, 2 * back - 1 + other), chips)
 
 
 def scatter_place(device, me, count):
     chips = count // 2
     depth = chips // 2
-    away = (1 - 2 * (device & 1)) * (ring_place(device, chips) - ring_place(me, chips))
-    away = (away + chips) & (chips - 1)
-    hop = jnp.where(away > depth, 2 * (away - depth) - 1, 2 * (depth - away))
-    hop = jnp.where(away == 0, chips - 1, hop)
-    return hop + chips * ((device ^ me) & 1)
+    ahead = (ring_place(device, chips) - ring_place(me, chips) + chips) & (chips - 1)
+    core = device & 1
+    handler = jnp.where((ahead & (depth - 1)) == 0, core, (ahead > depth).astype(jnp.int32))
+    steps = jnp.where(handler == 0, ahead, (chips - ahead) & (chips - 1))
+    place = jnp.where(
+        steps == depth,
+        0,
+        jnp.where(steps == 0, chips - 1, 2 * (depth - steps) - (core ^ handler)),
+    )
+    return place + jnp.where(handler == (me & 1), 0, chips)
 
 
 def stationary(
@@ -397,7 +400,7 @@
     stored = near_blocks.shape[0]
     pairs = far_slot.shape[0]
     half = clusters // 2
-    ways = ring_pairs(count)
+    ahead = ring_pairs(count)
     mate = [(i, i ^ 1) for i in range(count)]
     side = [(i, i ^ 2) for i in range(count)]
 
@@ -407,7 +410,6 @@
     def after(values, *others):
         return lax.optimization_barrier((values, *others))[0]
 
-    mate_blocks = move(near_blocks, mate)
     here = me.astype(jnp.int32).reshape(1)
     base = clusters * directions
     payload, lists = pl.pallas_call(
@@ -428,8 +430,9 @@
         rhs,
         basis_in,
     )
-    flow = [move(payload, way) for way in ways]
     shards = [move(payload, mate)]
+    flow = [move(payload, ahead), move(shards[0], ahead)]
+    mate_blocks = move(after(near_blocks, shards[0]), mate)
     lists = jnp.concatenate([lists, move(lists, mate)], axis=0)
     couple = after(jnp.transpose(far_coupling, (2, 1, 0)), payload)
     for k in range(1, chips):
@@ -440,7 +443,7 @@
             )
         shards.append(flow[x])
         if k < chips - 2:
-            flow[x] = move(flow[x], ways[x])
+            flow[x] = move(flow[x], ahead)
 
     quarter = chips // 2
 
@@ -518,7 +521,7 @@
     flow = lax.optimization_barrier([term(0).astype(jnp.bfloat16), term(1).astype(jnp.bfloat16)])
     lists = after(lists, *flow)
     mates += [move(after(send, *flow), mate) for send in sends[2:]]
-    flow = [move(part, way) for part, way in zip(flow, ways)]
+    flow = [move(part, ahead) for part in flow]
     late, sends = near(1, lists)
     kept.append(late)
     mates += [move(send, mate) for send in sends]
@@ -527,10 +530,11 @@
         flow[x] = tied(add(flow[x], k), k)
         if k == chips - 2:
             couple = after(couple, flow[x])
-        flow[x] = move(flow[x], ways[x])
-    far = far_field(couple)
-    total = far + term(chips - 1) + flow[1].astype(jnp.float32)
-    return (total + flow[0].astype(jnp.float32)).astype(jnp.bfloat16)
+        flow[x] = move(flow[x], ahead)
+    flow[1] = move(flow[1], mate)
+    total = far_field(couple) + term(chips - 1) + flow[0].astype(jnp.float32)
+    total = lax.optimization_barrier(total)
+    return (total + flow[1].astype(jnp.float32)).astype(jnp.bfloat16)
 
 
 def on_device(*args):

time: 79.1 us -> 70.8 us (0.90)
  the two profiles are of different devices: /device:TPU:28 before, /device:TPU:0 now
where the time goes in v11:
time: 70.8 us; the launch traced here: 70.5 us
  starting transfers between devices  27.1 us (38%)
  waiting for transfers between devices  24 us (34%)
  Pallas kernels  15.9 us (22%)
  other arithmetic  2.31 us (3%)
  local copies, waits for them, and re-layouts  0.97 us (1%)
    ppermute x27, starting transfers between devices, move(): return lax.ppermute(values, 'blk', where)  27.1 us
    ppermute x27, waiting for transfers between devices, move(): return lax.ppermute(values, 'blk', where)  24 us
    pallas_call x2, Pallas kernels, near(): pl.pallas_call(functools.partial(near_kernel, late, BATCH, LAG, chips, le...  11.4 us
    pallas_call x1, Pallas kernels, far_field(): pl.pallas_call(far_kernel, out_shape=jax.ShapeDtypeStruct((clusters, dire...  2.5 us
    pallas_call x1, Pallas kernels, stationary(): pl.pallas_call(functools.partial(prologue_kernel, count), out_shape=[jax....  2.01 us
  transfers between devices with their start and end apart: 27, of which 15 were waited for; matrix products, arithmetic and copies ran while one was open for 3% of the time, Pallas kernels for 12%

profile of v11, /device:TPU:0, one launch (start us, length us, event | category | flops | bytes accessed | tf_op | source)
XLA Modules:
  0.0 70.5 jit_solution(16873008349443383306)
XLA Ops:
  0.0 2.0 %prologue.1 = (bf16[1152,128]{1,0:T(8,128)(2,1)}, s32[8,128]{1,0:T(8,128)}) custom-call(s32[1]{0:T(128)} %bitcast.me_ref.refs_2_, s32[1,128]{1,0:T(1,128)} %bitcast.14, s32[1,128]{1,0:T(1,128)} %bitcast.15, s32[1,128]{1,0:T(1,128)} %bitcast.16, bf16[16,64,128]{2,1,0:T(8,128)(2,1)} %rhs_ref.1, bf16[16,16,128]{2,1,0:T(8,128)(2,1)} %basis_ref.1), custom_call_target="tpu_custom_call" | custom-call | tf_op jit(solution)/shard_map/prologue/pallas_call | solution.py:415
  2.5 1.4 %collective-permute-done.2.refs_0_ = bf16[1152,128]{1,0:T(8,128)(2,1)S(1)} collective-permute-done((bf16[1152,128]{1,0:T(8,128)(2,1)}, bf16[1152,128]{1,0:T(8,128)(2,1)S(1)}, u32[]{:S(2)}, u32[]{:S(2)}) %collective-permute-start.2) | collective-permute-done | bytes 294944 | tf_op jit(solution)/shard_map/ppermute | solution.py:408
  4.3 2.7 %collective-permute-start = (bf16[1152,128]{1,0:T(8,128)(2,1)}, bf16[1152,128]{1,0:T(8,128)(2,1)S(1)}, u32[]{:S(2)}, u32[]{:S(2)}) collective-permute-start(bf16[1152,128]{1,0:T(8,128)(2,1)} %get-tuple-element.41), channel_id=1, source_target_pairs={{0,4},{1,3},{4,8},{5,1},{8,12},{9,5},{12,14},{13,9},{14,10},{15,13... | collective-permute-start | bytes 884744 | tf_op jit(solution)/shard_map/ppermute | solution.py:408
  7.0 1.6 %collective-permute-start.5 = (bf16[1152,128]{1,0:T(8,128)(2,1)S(1)}, bf16[1152,128]{1,0:T(8,128)(2,1)S(1)}, u32[]{:S(2)}, u32[]{:S(2)}) collective-permute-start(bf16[1152,128]{1,0:T(8,128)(2,1)S(1)} %collective-permute-done.2.refs_0_), channel_id=1, source_target_pairs={{0,4},{1,3},{4,8},{5,1},{8,12},{9,5},{12,14},{13,9},{14,10},{15,13... | collective-permute-start | bytes 884744 | tf_op jit(solution)/shard_map/ppermute | solution.py:408
  8.5 3.3 %collective-permute-done.refs_1_ = bf16[1152,128]{1,0:T(8,128)(2,1)S(1)} collective-permute-done((bf16[1152,128]{1,0:T(8,128)(2,1)}, bf16[1152,128]{1,0:T(8,128)(2,1)S(1)}, u32[]{:S(2)}, u32[]{:S(2)}) %collective-permute-start) | collective-permute-done | bytes 294944 | tf_op jit(solution)/shard_map/ppermute | solution.py:408
  11.8 2.1 %collective-permute-start.1 = (bf16[1152,128]{1,0:T(8,128)(2,1)S(1)}, bf16[1152,128]{1,0:T(8,128)(2,1)S(1)}, u32[]{:S(2)}, u32[]{:S(2)}) collective-permute-start(bf16[1152,128]{1,0:T(8,128)(2,1)S(1)} %collective-permute-done.refs_1_), channel_id=1, source_target_pairs={{0,4},{1,3},{4,8},{5,1},{8,12},{9,5},{12,14},{13,9},{14,10},{15,13... | collective-permute-start | bytes 884744 | tf_op jit(solution)/shard_map/ppermute | solution.py:408
  13.9 0.9 %copy.14 = bf16[256,16,16]{0,1,2:T(8,128)(2,1)S(1)} copy(bf16[256,16,16]{0,2,1:T(8,128)(2,1)} %param.16) | data formatting | bytes 262144 | tf_op args[5]
  16.0 1.6 %collective-permute-start.6 = (bf16[1152,128]{1,0:T(8,128)(2,1)S(1)}, bf16[1152,128]{1,0:T(8,128)(2,1)S(1)}, u32[]{:S(2)}, u32[]{:S(2)}) collective-permute-start(bf16[1152,128]{1,0:T(8,128)(2,1)S(1)} %collective-permute-done.5.refs_2_), channel_id=1, source_target_pairs={{0,4},{1,3},{4,8},{5,1},{8,12},{9,5},{12,14},{13,9},{14,10},{15,13... | collective-permute-start | bytes 884744 | tf_op jit(solution)/shard_map/ppermute | solution.py:408
  17.5 1.0 %collective-permute-done.1.refs_3_ = bf16[1152,128]{1,0:T(8,128)(2,1)S(1)} collective-permute-done((bf16[1152,128]{1,0:T(8,128)(2,1)S(1)}, bf16[1152,128]{1,0:T(8,128)(2,1)S(1)}, u32[]{:S(2)}, u32[]{:S(2)}) %collective-permute-start.1) | collective-permute-done | bytes 294944 | tf_op jit(solution)/shard_map/ppermute | solution.py:408
  18.5 2.1 %collective-permute-start.7 = (bf16[1152,128]{1,0:T(8,128)(2,1)S(1)}, bf16[1152,128]{1,0:T(8,128)(2,1)S(1)}, u32[]{:S(2)}, u32[]{:S(2)}) collective-permute-start(bf16[1152,128]{1,0:T(8,128)(2,1)S(1)} %collective-permute-done.1.refs_3_), channel_id=1, source_target_pairs={{0,4},{1,3},{4,8},{5,1},{8,12},{9,5},{12,14},{13,9},{14,10},{15,13... | collective-permute-start | bytes 884744 | tf_op jit(solution)/shard_map/ppermute | solution.py:408
  20.6 2.1 %collective-permute-done.6.refs_4_ = bf16[1152,128]{1,0:T(8,128)(2,1)S(1)} collective-permute-done((bf16[1152,128]{1,0:T(8,128)(2,1)S(1)}, bf16[1152,128]{1,0:T(8,128)(2,1)S(1)}, u32[]{:S(2)}, u32[]{:S(2)}) %collective-permute-start.6) | collective-permute-done | bytes 294944 | tf_op jit(solution)/shard_map/ppermute | solution.py:408
  22.7 1.6 %collective-permute-start.8 = (bf16[1152,128]{1,0:T(8,128)(2,1)S(1)}, bf16[1152,128]{1,0:T(8,128)(2,1)S(1)}, u32[]{:S(2)}, u32[]{:S(2)}) collective-permute-start(bf16[1152,128]{1,0:T(8,128)(2,1)S(1)} %collective-permute-done.6.refs_4_), channel_id=1, source_target_pairs={{0,4},{1,3},{4,8},{5,1},{8,12},{9,5},{12,14},{13,9},{14,10},{15,13... | collective-permute-start | bytes 884744 | tf_op jit(solution)/shard_map/ppermute | solution.py:408
  24.3 1.6 %collective-permute-done.7.refs_5_ = bf16[1152,128]{1,0:T(8,128)(2,1)S(1)} collective-permute-done((bf16[1152,128]{1,0:T(8,128)(2,1)S(1)}, bf16[1152,128]{1,0:T(8,128)(2,1)S(1)}, u32[]{:S(2)}, u32[]{:S(2)}) %collective-permute-start.7) | collective-permute-done | bytes 294944 | tf_op jit(solution)/shard_map/ppermute | solution.py:408
  25.9 1.6 %collective-permute-start.9 = (bf16[1152,128]{1,0:T(8,128)(2,1)S(1)}, bf16[1152,128]{1,0:T(8,128)(2,1)S(1)}, u32[]{:S(2)}, u32[]{:S(2)}) collective-permute-start(bf16[1152,128]{1,0:T(8,128)(2,1)S(1)} %collective-permute-done.7.refs_5_), channel_id=1, source_target_pairs={{0,4},{1,3},{4,8},{5,1},{8,12},{9,5},{12,14},{13,9},{14,10},{15,13... | collective-permute-start | bytes 884744 | tf_op jit(solution)/shard_map/ppermute | solution.py:408
  27.4 2.0 %collective-permute-done.8.refs_6_ = bf16[1152,128]{1,0:T(8,128)(2,1)S(1)} collective-permute-done((bf16[1152,128]{1,0:T(8,128)(2,1)S(1)}, bf16[1152,128]{1,0:T(8,128)(2,1)S(1)}, u32[]{:S(2)}, u32[]{:S(2)}) %collective-permute-start.8) | collective-permute-done | bytes 294944 | tf_op jit(solution)/shard_map/ppermute | solution.py:408
  29.4 3.2 %collective-permute-done.9.refs_7_ = bf16[1152,128]{1,0:T(8,128)(2,1)S(1)} collective-permute-done((bf16[1152,128]{1,0:T(8,128)(2,1)S(1)}, bf16[1152,128]{1,0:T(8,128)(2,1)S(1)}, u32[]{:S(2)}, u32[]{:S(2)}) %collective-permute-start.9) | collective-permute-done | bytes 294944 | tf_op jit(solution)/shard_map/ppermute | solution.py:408
  32.6 5.6 %near.2 = (f32[64,64,128]{2,1,0:T(8,128)S(1)}, bf16[16,64,128]{2,1,0:T(8,128)(2,1)S(1)}, bf16[16,64,128]{2,1,0:T(8,128)(2,1)S(1)}, bf16[16,64,128]{2,1,0:T(8,128...) custom-call(s32[16,128]{1,0:T(8,128)S(1)} %pad_add_fusion.list_ref, ...), custom_call_target="tpu_custom_call" | custom-call | flops 2147483648 | bytes 16777216 | tf_op jit(solution)/shard_map/near/pallas_call | solution.py:452
  38.7 1.0 %collective-permute-done.12 = bf16[16,64,128]{2,1,0:T(8,128)(2,1)S(1)} collective-permute-done((bf16[16,64,128]{2,1,0:T(8,128)(2,1)S(1)}, bf16[16,64,128]{2,1,0:T(8,128)(2,1)S(1)}, u32[]{:S(2)}, u32[]{:S(2)}) %collective-permute-start.12) | collective-permute-done | bytes 262176 | tf_op jit(solution)/shard_map/ppermute | solution.py:408
  40.5 1.8 %collective-permute-start.13 = (bf16[16,64,128]{2,1,0:T(8,128)(2,1)S(1)}, bf16[16,64,128]{2,1,0:T(8,128)(2,1)S(1)}, u32[]{:S(2)}, u32[]{:S(2)}) collective-permute-start(bf16[16,64,128]{2,1,0:T(8,128)(2,1)S(1)} %get-tuple-element.54), channel_id=1, source_target_pairs={{0,4},{1,3},{4,8},{5,1},{8,12},{9,5},{12,14},{13,9},{14,10},{15,13... | collective-permute-start | bytes 786440 | tf_op jit(solution)/shard_map/ppermute | solution.py:408
  42.4 1.3 %collective-permute-start.17 = (bf16[16,64,128]{2,1,0:T(8,128)(2,1)S(1)}, bf16[16,64,128]{2,1,0:T(8,128)(2,1)S(1)}, u32[]{:S(2)}, u32[]{:S(2)}) collective-permute-start(bf16[16,64,128]{2,1,0:T(8,128)(2,1)S(1)} %get-tuple-element.56), channel_id=1, source_target_pairs={{0,4},{1,3},{4,8},{5,1},{8,12},{9,5},{12,14},{13,9},{14,10},{15,13... | collective-permute-start | bytes 786440 | tf_op jit(solution)/shard_map/ppermute | solution.py:408
  43.8 5.8 %near.3 = (f32[64,64,128]{2,1,0:T(8,128)S(1)}, bf16[16,64,128]{2,1,0:T(8,128)(2,1)S(1)}, bf16[16,64,128]{2,1,0:T(8,128)(2,1)S(1)}, bf16[16,64,128]{2,1,0:T(8,128)(2,1)S(1)}, bf16[16,64,128]{2,1,0:T(8,128)(2,1)S(1)}) custom-call(s32[16,128]{1,0:T(8,128)S(1)} %pad_add_fusion.list_ref, bf16[1152,128]{1,0:T(8,128)(2,1)S(1)} %collective-permute-done.2.refs_0_, ...), custom_call_target="tpu_custom_call" | custom-call | flops 2147483648 | bytes 16777216 | tf_op jit(solution)/shard_map/near/pallas_call | solution.py:452
  50.1 1.4 %collective-permute-start.16 = (bf16[16,64,128]{2,1,0:T(8,128)(2,1)S(1)}, bf16[16,64,128]{2,1,0:T(8,128)(2,1)S(1)}, u32[]{:S(2)}, u32[]{:S(2)}) collective-permute-start(bf16[16,64,128]{2,1,0:T(8,128)(2,1)S(1)} %add_convert_fusion.5), channel_id=1, source_target_pairs={{0,4},{1,3},{4,8},{5,1},{8,12},{9,5},{12,14},{13,9},{14,10},{15,13... | collective-permute-start | bytes 786440 | tf_op jit(solution)/shard_map/ppermute | solution.py:408
  52.2 2.0 %collective-permute-start.21 = (bf16[16,64,128]{2,1,0:T(8,128)(2,1)S(1)}, bf16[16,64,128]{2,1,0:T(8,128)(2,1)S(1)}, u32[]{:S(2)}, u32[]{:S(2)}) collective-permute-start(bf16[16,64,128]{2,1,0:T(8,128)(2,1)S(1)} %add_convert_fusion.4), channel_id=1, source_target_pairs={{0,4},{1,3},{4,8},{5,1},{8,12},{9,5},{12,14},{13,9},{14,10},{15,13... | collective-permute-start | bytes 786440 | tf_op jit(solution)/shard_map/ppermute | solution.py:408
  54.2 2.3 %collective-permute-done.16 = bf16[16,64,128]{2,1,0:T(8,128)(2,1)S(1)} collective-permute-done((bf16[16,64,128]{2,1,0:T(8,128)(2,1)S(1)}, bf16[16,64,128]{2,1,0:T(8,128)(2,1)S(1)}, u32[]{:S(2)}, u32[]{:S(2)}) %collective-permute-start.16) | collective-permute-done | bytes 262176 | tf_op jit(solution)/shard_map/ppermute | solution.py:408
  56.6 1.4 %collective-permute-start.20 = (bf16[16,64,128]{2,1,0:T(8,128)(2,1)S(1)}, bf16[16,64,128]{2,1,0:T(8,128)(2,1)S(1)}, u32[]{:S(2)}, u32[]{:S(2)}) collective-permute-start(bf16[16,64,128]{2,1,0:T(8,128)(2,1)S(1)} %add_convert_fusion.3), channel_id=1, source_target_pairs={{0,4},{1,3},{4,8},{5,1},{8,12},{9,5},{12,14},{13,9},{14,10},{15,13... | collective-permute-start | bytes 786440 | tf_op jit(solution)/shard_map/ppermute | solution.py:408
  59.4 1.4 %collective-permute-start.25 = (bf16[16,64,128]{2,1,0:T(8,128)(2,1)S(1)}, bf16[16,64,128]{2,1,0:T(8,128)(2,1)S(1)}, u32[]{:S(2)}, u32[]{:S(2)}) collective-permute-start(bf16[16,64,128]{2,1,0:T(8,128)(2,1)S(1)} %add_convert_fusion.2), channel_id=1, source_target_pairs={{0,4},{1,3},{4,8},{5,1},{8,12},{9,5},{12,14},{13,9},{14,10},{15,13... | collective-permute-start | bytes 786440 | tf_op jit(solution)/shard_map/ppermute | solution.py:408
  60.9 2.2 %collective-permute-done.20 = bf16[16,64,128]{2,1,0:T(8,128)(2,1)S(1)} collective-permute-done((bf16[16,64,128]{2,1,0:T(8,128)(2,1)S(1)}, bf16[16,64,128]{2,1,0:T(8,128)(2,1)S(1)}, u32[]{:S(2)}, u32[]{:S(2)}) %collective-permute-start.20) | collective-permute-done | bytes 262176 | tf_op jit(solution)/shard_map/ppermute | solution.py:408
  63.2 1.4 %collective-permute-start.24 = (bf16[16,64,128]{2,1,0:T(8,128)(2,1)S(1)}, bf16[16,64,128]{2,1,0:T(8,128)(2,1)S(1)}, u32[]{:S(2)}, u32[]{:S(2)}) collective-permute-start(bf16[16,64,128]{2,1,0:T(8,128)(2,1)S(1)} %add_convert_fusion.1), channel_id=1, source_target_pairs={{0,4},{1,3},{4,8},{5,1},{8,12},{9,5},{12,14},{13,9},{14,10},{15,13... | collective-permute-start | bytes 786440 | tf_op jit(solution)/shard_map/ppermute | solution.py:408
  64.6 1.3 %collective-permute-done.25 = bf16[16,64,128]{2,1,0:T(8,128)(2,1)S(1)} collective-permute-done((bf16[16,64,128]{2,1,0:T(8,128)(2,1)S(1)}, bf16[16,64,128]{2,1,0:T(8,128)(2,1)S(1)}, u32[]{:S(2)}, u32[]{:S(2)}) %collective-permute-start.25) | collective-permute-done | bytes 262176 | tf_op jit(solution)/shard_map/ppermute | solution.py:408
  65.9 2.5 %far.1 = f32[16,64,128]{2,1,0:T(8,128)S(1)} custom-call(bf16[1024,128]{1,0:T(8,128)(2,1)S(1)} %get-tuple-element.49.refs_0_, bf16[1024,128]{1,0:T(8,128)(2,1)S(1)} %collective-permute-done.10.refs_1_, s32[1]{0:T(128)} %bitcast.me_ref.refs_2_, bf16[16,16,256]{2,1,0:T(8,128)(2,1)S(1)} %bitcast.10, s32[1,256]{1,0:T(1,128)S(1)} %bitcast.11, ...), custom_call_target="tpu_custom_call" | custom-call | flops 536870912 | bytes 8388608 | tf_op jit(solution)/shard_map/far/pallas_call | solution.py:483
  68.4 1.2 %collective-permute-done.24 = bf16[16,64,128]{2,1,0:T(8,128)(2,1)S(1)} collective-permute-done((bf16[16,64,128]{2,1,0:T(8,128)(2,1)S(1)}, bf16[16,64,128]{2,1,0:T(8,128)(2,1)S(1)}, u32[]{:S(2)}, u32[]{:S(2)}) %collective-permute-start.24) | collective-permute-done | bytes 262176 | tf_op jit(solution)/shard_map/ppermute | solution.py:408
  69.7 0.8 %add_convert_fusion = bf16[16,64,128]{2,1,0:T(8,128)(2,1)} fusion(f32[16,64,128]{2,1,0:T(8,128)S(1)} %convert_add_fusion, bf16[16,64,128]{2,1,0:T(8,128)(2,1)S(1)} %collective-permute-done.26), kind=kLoop, calls=%fused_computation | loop fusion | flops 393216 | bytes 1048576 | tf_op jit(solution)/shard_map/convert_element_type | solution.py:537
  (46 shorter events, 6.2 us)
Async XLA Ops:
  2.0 1.9 %collective-permute-start.2 = (bf16[1152,128]{1,0:T(8,128)(2,1)}, bf16[1152,128]{1,0:T(8,128)(2,1)S(1)}, u32[]{:S(2)}, u32[]{:S(2)}) collective-permute-start(bf16[1152,128]{1,0:T(8,128)(2,1)} %get-tuple-element.41), channel_id=1, source_target_pairs={{0,1},{1,0},{2,3},{3,2},{4,5},{5,4},{6,7},{7,6},{8,9},{9,8},{10,11... | collective-permute-start | bytes 884744 | tf_op jit(solution)/shard_map/ppermute | solution.py:408
  3.9 14.7 %collective-permute-start.3 = (bf16[128,128,128]{2,1,0:T(8,128)(2,1)}, bf16[128,128,128]{2,1,0:T(8,128)(2,1)S(1)}, u32[]{:S(2)}, u32[]{:S(2)}) collective-permute-start(bf16[128,128,128]{2,1,0:T(8,128)(2,1)} %refs_8_.3), channel_id=1, source_target_pairs={{0,1},{1,0},{2,3},{3,2},{4,5},{5,4},{6,7},{7,6},{8,9},{9,8},{10,11... | collective-permute-start | bytes 12582920 | tf_op jit(solution)/shard_map/ppermute | solution.py:408
  4.3 7.6 %collective-permute-start = (bf16[1152,128]{1,0:T(8,128)(2,1)}, bf16[1152,128]{1,0:T(8,128)(2,1)S(1)}, u32[]{:S(2)}, u32[]{:S(2)}) collective-permute-start(bf16[1152,128]{1,0:T(8,128)(2,1)} %get-tuple-element.41), channel_id=1, source_target_pairs={{0,4},{1,3},{4,8},{5,1},{8,12},{9,5},{12,14},{13,9},{14,10},{15,13... | collective-permute-start | bytes 884744 | tf_op jit(solution)/shard_map/ppermute | solution.py:408
  7.0 9.0 %collective-permute-start.5 = (bf16[1152,128]{1,0:T(8,128)(2,1)S(1)}, bf16[1152,128]{1,0:T(8,128)(2,1)S(1)}, u32[]{:S(2)}, u32[]{:S(2)}) collective-permute-start(bf16[1152,128]{1,0:T(8,128)(2,1)S(1)} %collective-permute-done.2.refs_0_), channel_id=1, source_target_pairs={{0,4},{1,3},{4,8},{5,1},{8,12},{9,5},{12,14},{13,9},{14,10},{15,13... | collective-permute-start | bytes 884744 | tf_op jit(solution)/shard_map/ppermute | solution.py:408
  11.8 6.7 %collective-permute-start.1 = (bf16[1152,128]{1,0:T(8,128)(2,1)S(1)}, bf16[1152,128]{1,0:T(8,128)(2,1)S(1)}, u32[]{:S(2)}, u32[]{:S(2)}) collective-permute-start(bf16[1152,128]{1,0:T(8,128)(2,1)S(1)} %collective-permute-done.refs_1_), channel_id=1, source_target_pairs={{0,4},{1,3},{4,8},{5,1},{8,12},{9,5},{12,14},{13,9},{14,10},{15,13... | collective-permute-start | bytes 884744 | tf_op jit(solution)/shard_map/ppermute | solution.py:408
  13.9 1.4 %collective-permute-start.4 = (s32[8,128]{1,0:T(8,128)}, s32[8,128]{1,0:T(8,128)S(1)}, u32[]{:S(2)}, u32[]{:S(2)}) collective-permute-start(s32[8,128]{1,0:T(8,128)} %get-tuple-element.43), channel_id=1, source_target_pairs={{0,1},{1,0},{2,3},{3,2},{4,5},{5,4},{6,7},{7,6},{8,9},{9,8},{10,11... | collective-permute-start | bytes 12296 | tf_op jit(solution)/shard_map/ppermute | solution.py:408
  16.0 6.7 %collective-permute-start.6 = (bf16[1152,128]{1,0:T(8,128)(2,1)S(1)}, bf16[1152,128]{1,0:T(8,128)(2,1)S(1)}, u32[]{:S(2)}, u32[]{:S(2)}) collective-permute-start(bf16[1152,128]{1,0:T(8,128)(2,1)S(1)} %collective-permute-done.5.refs_2_), channel_id=1, source_target_pairs={{0,4},{1,3},{4,8},{5,1},{8,12},{9,5},{12,14},{13,9},{14,10},{15,13... | collective-permute-start | bytes 884744 | tf_op jit(solution)/shard_map/ppermute | solution.py:408
  18.5 14.0 %copy-start.4 = (bf16[128,128,128]{2,1,0:T(8,128)(2,1)}, bf16[128,128,128]{2,1,0:T(8,128)(2,1)S(1)}, u32[]{:S(2)}) copy-start(bf16[128,128,128]{2,1,0:T(8,128)(2,1)S(1)} %collective-permute-done.3.refs_9_) | copy-start | bytes 12582916
  18.5 7.3 %collective-permute-start.7 = (bf16[1152,128]{1,0:T(8,128)(2,1)S(1)}, bf16[1152,128]{1,0:T(8,128)(2,1)S(1)}, u32[]{:S(2)}, u32[]{:S(2)}) collective-permute-start(bf16[1152,128]{1,0:T(8,128)(2,1)S(1)} %collective-permute-done.1.refs_3_), channel_id=1, source_target_pairs={{0,4},{1,3},{4,8},{5,1},{8,12},{9,5},{12,14},{13,9},{14,10},{15,13... | collective-permute-start | bytes 884744 | tf_op jit(solution)/shard_map/ppermute | solution.py:408
  22.7 6.7 %collective-permute-start.8 = (bf16[1152,128]{1,0:T(8,128)(2,1)S(1)}, bf16[1152,128]{1,0:T(8,128)(2,1)S(1)}, u32[]{:S(2)}, u32[]{:S(2)}) collective-permute-start(bf16[1152,128]{1,0:T(8,128)(2,1)S(1)} %collective-permute-done.6.refs_4_), channel_id=1, source_target_pairs={{0,4},{1,3},{4,8},{5,1},{8,12},{9,5},{12,14},{13,9},{14,10},{15,13... | collective-permute-start | bytes 884744 | tf_op jit(solution)/shard_map/ppermute | solution.py:408
  25.9 6.7 %collective-permute-start.9 = (bf16[1152,128]{1,0:T(8,128)(2,1)S(1)}, bf16[1152,128]{1,0:T(8,128)(2,1)S(1)}, u32[]{:S(2)}, u32[]{:S(2)}) collective-permute-start(bf16[1152,128]{1,0:T(8,128)(2,1)S(1)} %collective-permute-done.7.refs_5_), channel_id=1, source_target_pairs={{0,4},{1,3},{4,8},{5,1},{8,12},{9,5},{12,14},{13,9},{14,10},{15,13... | collective-permute-start | bytes 884744 | tf_op jit(solution)/shard_map/ppermute | solution.py:408
  38.2 1.6 %collective-permute-start.12 = (bf16[16,64,128]{2,1,0:T(8,128)(2,1)S(1)}, bf16[16,64,128]{2,1,0:T(8,128)(2,1)S(1)}, u32[]{:S(2)}, u32[]{:S(2)}) collective-permute-start(bf16[16,64,128]{2,1,0:T(8,128)(2,1)S(1)} %get-tuple-element.53), channel_id=1, source_target_pairs={{0,1},{1,0},{2,3},{3,2},{4,5},{5,4},{6,7},{7,6},{8,9},{9,8},{10,11... | collective-permute-start | bytes 786440 | tf_op jit(solution)/shard_map/ppermute | solution.py:408
  38.3 1.9 %collective-permute-start.11 = (bf16[16,64,128]{2,1,0:T(8,128)(2,1)S(1)}, bf16[16,64,128]{2,1,0:T(8,128)(2,1)S(1)}, u32[]{:S(2)}, u32[]{:S(2)}) collective-permute-start(bf16[16,64,128]{2,1,0:T(8,128)(2,1)S(1)} %get-tuple-element.52), channel_id=1, source_target_pairs={{0,1},{1,0},{2,3},{3,2},{4,5},{5,4},{6,7},{7,6},{8,9},{9,8},{10,11... | collective-permute-start | bytes 786440 | tf_op jit(solution)/shard_map/ppermute | solution.py:408
  40.3 9.6 %collective-permute-start.14 = (bf16[16,64,128]{2,1,0:T(8,128)(2,1)S(1)}, bf16[16,64,128]{2,1,0:T(8,128)(2,1)S(1)}, u32[]{:S(2)}, u32[]{:S(2)}) collective-permute-start(bf16[16,64,128]{2,1,0:T(8,128)(2,1)S(1)} %get-tuple-element.57), channel_id=1, source_target_pairs={{0,1},{1,0},{2,3},{3,2},{4,5},{5,4},{6,7},{7,6},{8,9},{9,8},{10,11... | collective-permute-start | bytes 786440 | tf_op jit(solution)/shard_map/ppermute | solution.py:408
  40.5 9.4 %collective-permute-start.13 = (bf16[16,64,128]{2,1,0:T(8,128)(2,1)S(1)}, bf16[16,64,128]{2,1,0:T(8,128)(2,1)S(1)}, u32[]{:S(2)}, u32[]{:S(2)}) collective-permute-start(bf16[16,64,128]{2,1,0:T(8,128)(2,1)S(1)} %get-tuple-element.54), channel_id=1, source_target_pairs={{0,4},{1,3},{4,8},{5,1},{8,12},{9,5},{12,14},{13,9},{14,10},{15,13... | collective-permute-start | bytes 786440 | tf_op jit(solution)/shard_map/ppermute | solution.py:408
  42.4 9.7 %collective-permute-start.17 = (bf16[16,64,128]{2,1,0:T(8,128)(2,1)S(1)}, bf16[16,64,128]{2,1,0:T(8,128)(2,1)S(1)}, u32[]{:S(2)}, u32[]{:S(2)}) collective-permute-start(bf16[16,64,128]{2,1,0:T(8,128)(2,1)S(1)} %get-tuple-element.56), channel_id=1, source_target_pairs={{0,4},{1,3},{4,8},{5,1},{8,12},{9,5},{12,14},{13,9},{14,10},{15,13... | collective-permute-start | bytes 786440 | tf_op jit(solution)/shard_map/ppermute | solution.py:408
  43.6 6.4 %collective-permute-start.15 = (bf16[16,64,128]{2,1,0:T(8,128)(2,1)S(1)}, bf16[16,64,128]{2,1,0:T(8,128)(2,1)S(1)}, u32[]{:S(2)}, u32[]{:S(2)}) collective-permute-start(bf16[16,64,128]{2,1,0:T(8,128)(2,1)S(1)} %get-tuple-element.59), channel_id=1, source_target_pairs={{0,1},{1,0},{2,3},{3,2},{4,5},{5,4},{6,7},{7,6},{8,9},{9,8},{10,11... | collective-permute-start | bytes 786440 | tf_op jit(solution)/shard_map/ppermute | solution.py:408
  49.7 2.5 %collective-permute-start.18 = (bf16[16,64,128]{2,1,0:T(8,128)(2,1)S(1)}, bf16[16,64,128]{2,1,0:T(8,128)(2,1)S(1)}, u32[]{:S(2)}, u32[]{:S(2)}) collective-permute-start(bf16[16,64,128]{2,1,0:T(8,128)(2,1)S(1)} %get-tuple-element.64), channel_id=1, source_target_pairs={{0,1},{1,0},{2,3},{3,2},{4,5},{5,4},{6,7},{7,6},{8,9},{9,8},{10,11... | collective-permute-start | bytes 786440 | tf_op jit(solution)/shard_map/ppermute | solution.py:408
  50.1 6.4 %collective-permute-start.16 = (bf16[16,64,128]{2,1,0:T(8,128)(2,1)S(1)}, bf16[16,64,128]{2,1,0:T(8,128)(2,1)S(1)}, u32[]{:S(2)}, u32[]{:S(2)}) collective-permute-start(bf16[16,64,128]{2,1,0:T(8,128)(2,1)S(1)} %add_convert_fusion.5), channel_id=1, source_target_pairs={{0,4},{1,3},{4,8},{5,1},{8,12},{9,5},{12,14},{13,9},{14,10},{15,13... | collective-permute-start | bytes 786440 | tf_op jit(solution)/shard_map/ppermute | solution.py:408
  51.5 5.1 %collective-permute-start.19 = (bf16[16,64,128]{2,1,0:T(8,128)(2,1)S(1)}, bf16[16,64,128]{2,1,0:T(8,128)(2,1)S(1)}, u32[]{:S(2)}, u32[]{:S(2)}) collective-permute-start(bf16[16,64,128]{2,1,0:T(8,128)(2,1)S(1)} %get-tuple-element.66), channel_id=1, source_target_pairs={{0,1},{1,0},{2,3},{3,2},{4,5},{5,4},{6,7},{7,6},{8,9},{9,8},{10,11... | collective-permute-start | bytes 786440 | tf_op jit(solution)/shard_map/ppermute | solution.py:408
  51.5 7.9 %collective-permute-start.22 = (bf16[16,64,128]{2,1,0:T(8,128)(2,1)S(1)}, bf16[16,64,128]{2,1,0:T(8,128)(2,1)S(1)}, u32[]{:S(2)}, u32[]{:S(2)}) collective-permute-start(bf16[16,64,128]{2,1,0:T(8,128)(2,1)S(1)} %get-tuple-element.70), channel_id=1, source_target_pairs={{0,1},{1,0},{2,3},{3,2},{4,5},{5,4},{6,7},{7,6},{8,9},{9,8},{10,11... | collective-permute-start | bytes 786440 | tf_op jit(solution)/shard_map/ppermute | solution.py:408
  52.1 13.7 %copy-start = (bf16[16,16,128]{2,1,0:T(8,128)(2,1)S(1)}, bf16[16,16,128]{2,1,0:T(8,128)(2,1)}, u32[]{:S(2)}) copy-start(bf16[16,16,128]{2,1,0:T(8,128)(2,1)} %refs_7_.1) | copy-start | bytes 196612
  52.2 13.7 %copy-start.1 = (s32[256]{0:T(256)S(1)}, s32[256]{0:T(256)}, u32[]{:S(2)}) copy-start(s32[256]{0:T(256)} %param.17) | copy-start | bytes 3076
  52.2 13.7 %copy-start.2 = (s32[256,1]{0,1:T(1,128)S(1)}, s32[256,1]{0,1:T(1,128)}, u32[]{:S(2)}) copy-start(s32[256,1]{0,1:T(1,128)} %param.18) | copy-start | bytes 3076
  52.2 13.7 %copy-start.3 = (s32[256]{0:T(256)S(1)}, s32[256]{0:T(256)}, u32[]{:S(2)}) copy-start(s32[256]{0:T(256)} %param.19) | copy-start | bytes 3076
  52.2 7.1 %collective-permute-start.21 = (bf16[16,64,128]{2,1,0:T(8,128)(2,1)S(1)}, bf16[16,64,128]{2,1,0:T(8,128)(2,1)S(1)}, u32[]{:S(2)}, u32[]{:S(2)}) collective-permute-start(bf16[16,64,128]{2,1,0:T(8,128)(2,1)S(1)} %add_convert_fusion.4), channel_id=1, source_target_pairs={{0,4},{1,3},{4,8},{5,1},{8,12},{9,5},{12,14},{13,9},{14,10},{15,13... | collective-permute-start | bytes 786440 | tf_op jit(solution)/shard_map/ppermute | solution.py:408
  56.6 6.4 %collective-permute-start.20 = (bf16[16,64,128]{2,1,0:T(8,128)(2,1)S(1)}, bf16[16,64,128]{2,1,0:T(8,128)(2,1)S(1)}, u32[]{:S(2)}, u32[]{:S(2)}) collective-permute-start(bf16[16,64,128]{2,1,0:T(8,128)(2,1)S(1)} %add_convert_fusion.3), channel_id=1, source_target_pairs={{0,4},{1,3},{4,8},{5,1},{8,12},{9,5},{12,14},{13,9},{14,10},{15,13... | collective-permute-start | bytes 786440 | tf_op jit(solution)/shard_map/ppermute | solution.py:408
  58.1 7.8 %collective-permute-start.10 = (bf16[1024,128]{1,0:T(8,128)(2,1)S(1)}, bf16[1024,128]{1,0:T(8,128)(2,1)S(1)}, u32[]{:S(2)}, u32[]{:S(2)}) collective-permute-start(bf16[1024,128]{1,0:T(8,128)(2,1)S(1)} %get-tuple-element.49.refs_0_), channel_id=1, source_target_pairs={{0,1},{1,0},{2,3},{3,2},{4,5},{5,4},{6,7},{7,6},{8,9},{9,8},{10,11... | collective-permute-start | bytes 786440 | tf_op jit(solution)/shard_map/ppermute | solution.py:408
  58.1 5.1 %collective-permute-start.23 = (bf16[16,64,128]{2,1,0:T(8,128)(2,1)S(1)}, bf16[16,64,128]{2,1,0:T(8,128)(2,1)S(1)}, u32[]{:S(2)}, u32[]{:S(2)}) collective-permute-start(bf16[16,64,128]{2,1,0:T(8,128)(2,1)S(1)} %get-tuple-element.72), channel_id=1, source_target_pairs={{0,1},{1,0},{2,3},{3,2},{4,5},{5,4},{6,7},{7,6},{8,9},{9,8},{10,11... | collective-permute-start | bytes 786440 | tf_op jit(solution)/shard_map/ppermute | solution.py:408
  59.4 6.4 %collective-permute-start.25 = (bf16[16,64,128]{2,1,0:T(8,128)(2,1)S(1)}, bf16[16,64,128]{2,1,0:T(8,128)(2,1)S(1)}, u32[]{:S(2)}, u32[]{:S(2)}) collective-permute-start(bf16[16,64,128]{2,1,0:T(8,128)(2,1)S(1)} %add_convert_fusion.2), channel_id=1, source_target_pairs={{0,4},{1,3},{4,8},{5,1},{8,12},{9,5},{12,14},{13,9},{14,10},{15,13... | collective-permute-start | bytes 786440 | tf_op jit(solution)/shard_map/ppermute | solution.py:408
  63.2 6.4 %collective-permute-start.24 = (bf16[16,64,128]{2,1,0:T(8,128)(2,1)S(1)}, bf16[16,64,128]{2,1,0:T(8,128)(2,1)S(1)}, u32[]{:S(2)}, u32[]{:S(2)}) collective-permute-start(bf16[16,64,128]{2,1,0:T(8,128)(2,1)S(1)} %add_convert_fusion.1), channel_id=1, source_target_pairs={{0,4},{1,3},{4,8},{5,1},{8,12},{9,5},{12,14},{13,9},{14,10},{15,13... | collective-permute-start | bytes 786440 | tf_op jit(solution)/shard_map/ppermute | solution.py:408
  65.9 3.9 %collective-permute-start.26 = (bf16[16,64,128]{2,1,0:T(8,128)(2,1)S(1)}, bf16[16,64,128]{2,1,0:T(8,128)(2,1)S(1)}, u32[]{:S(2)}, u32[]{:S(2)}) collective-permute-start(bf16[16,64,128]{2,1,0:T(8,128)(2,1)S(1)} %collective-permute-done.25), channel_id=1, source_target_pairs={{0,1},{1,0},{2,3},{3,2},{4,5},{5,4},{6,7},{7,6},{8,9},{9,8},{10,11... | collective-permute-start | bytes 786440 | tf_op jit(solution)/shard_map/ppermute | solution.py:408

commit v12 on v11

--- a/solution.py
+++ b/solution.py
@@ -7,7 +7,6 @@
 from jax.experimental.pallas import tpu as pltpu
 from jax.sharding import PartitionSpec as P
 
-CHUNKS = 4
 BATCH = 16
 LAG = 4
 PROLOGUE_VMEM = 58 << 20
@@ -182,8 +181,6 @@
     columns, blocks, sums, column_sem, coef_sem, block_sem = refs
     directions = sums.shape[1]
     span = columns.shape[0] // shards
-    stored = blocks.shape[1]
-    chunk = stored // CHUNKS
     dummy = sums.shape[0] - 1
 
     copies = [
@@ -194,12 +191,6 @@
     ]
     for copy in copies:
         copy.start()
-    for half, source in enumerate((own_hbm, mate_hbm)):
-        for c in range(CHUNKS):
-            at = pl.ds(c * chunk, chunk)
-            pltpu.make_async_copy(
-                source.at[at], blocks.at[half, at], block_sem.at[half * CHUNKS + c]
-            ).start()
     tails = []
     if not late:
         tail = coef_ref.shape[0] // shards
@@ -212,14 +203,6 @@
     for copy in tails:
         copy.start()
 
-    def clear(i, carry):
-        sums[i] = jnp.zeros(sums.shape[1:], sums.dtype)
-        return carry
-
-    lax.fori_loop(0, dummy, clear, 0)
-    for copy in copies:
-        copy.wait()
-
     begin, begin_there = list_ref[3, late], list_ref[11, 2 + late]
     here = list_ref[3, late + 1] - begin
     total = here + list_ref[11, 3 + late] - begin_there
@@ -229,16 +212,36 @@
         half = (j >= here).astype(jnp.int32)
         return half, half * 8, j + jnp.where(half == 1, begin_there - here, begin)
 
-    def wait(c, carry):
-        at = pl.ds(0, chunk)
-        pltpu.make_async_copy(own_hbm.at[at], blocks.at[0, at], block_sem.at[c]).wait()
+    def fetch(j, carry):
+        half, row, at = entry(j)
+
+        for side, source in enumerate((own_hbm, mate_hbm)):
+
+            @pl.when(half == side)
+            def _():
+                pltpu.make_async_copy(
+                    source.at[list_ref[row, at]], blocks.at[j], block_sem.at[j // batch]
+                ).start()
+
         return carry
 
-    def body(step, ready):
+    steps = (total + batch - 1) // batch
+    lax.fori_loop(0, steps * batch, fetch, 0)
+
+    def clear(i, carry):
+        sums[i] = jnp.zeros(sums.shape[1:], sums.dtype)
+        return carry
+
+    lax.fori_loop(0, dummy, clear, 0)
+    for copy in copies:
+        copy.wait()
+
+    def body(step, carry):
         first = step * batch
-        half, row, at = entry(first + batch - 1)
-        needed = half * CHUNKS + list_ref[row, at] // chunk + 1
-        lax.fori_loop(ready, needed, wait, 0)
+        here_blocks = pl.ds(first, batch)
+        pltpu.make_async_copy(
+            own_hbm.at[pl.ds(0, batch)], blocks.at[here_blocks], block_sem.at[step]
+        ).wait()
         products = []
 
         def add(i):
@@ -253,7 +256,7 @@
             products.append(
                 lax.dot_general(
                     columns[pl.ds(start, directions)],
-                    blocks[half, list_ref[row, at]],
+                    blocks[first + i],
                     (((1,), (1,)), ((), ())),
                     preferred_element_type=jnp.float32,
                 )
@@ -262,10 +265,9 @@
                 add(i - lag)
         for i in range(batch - lag, batch):
             add(i)
-        return jnp.maximum(ready, needed)
-
-    ready = lax.fori_loop(0, (total + batch - 1) // batch, body, 0)
-    lax.fori_loop(ready, 2 * CHUNKS, wait, 0)
+        return carry
+
+    lax.fori_loop(0, steps, body, 0)
 
     def keep(i, carry):
         keep_ref[i] = sums[i]
@@ -345,7 +347,10 @@
     chips = count // 2
     cores = [(p, c) for p in range(chips) for c in range(2)]
     ahead = [(ring_device(p, c, chips), ring_device(p + 1 - 2 * c, c, chips)) for p, c in cores]
-    return ahead
+    cross = [
+        (ring_device(p, c, chips), ring_device(p - 1 + 2 * c, 1 - c, chips)) for p, c in cores
+    ]
+    return ahead, cross
 
 
 def ring_place(device, chips):
@@ -400,7 +405,7 @@
     stored = near_blocks.shape[0]
     pairs = far_slot.shape[0]
     half = clusters // 2
-    ahead = ring_pairs(count)
+    ahead, cross = ring_pairs(count)
     mate = [(i, i ^ 1) for i in range(count)]
     side = [(i, i ^ 2) for i in range(count)]
 
@@ -430,16 +435,17 @@
         rhs,
         basis_in,
     )
+    flow = [move(payload, ahead)]
+    mate_blocks = move(near_blocks, mate)
+    lists = jnp.concatenate([lists, move(lists, mate)], axis=0)
+    couple = jnp.transpose(far_coupling, (2, 1, 0))
+    flow.append(move(after(payload, couple), cross))
     shards = [move(payload, mate)]
-    flow = [move(payload, ahead), move(shards[0], ahead)]
-    mate_blocks = move(after(near_blocks, shards[0]), mate)
-    lists = jnp.concatenate([lists, move(lists, mate)], axis=0)
-    couple = after(jnp.transpose(far_coupling, (2, 1, 0)), payload)
     for k in range(1, chips):
         x = 1 - k % 2
         if k == 3:
-            flow[x], mate_blocks, shards[0], lists, couple = lax.optimization_barrier(
-                (flow[x], mate_blocks, shards[0], lists, couple)
+            flow[x], mate_blocks, shards[0], lists = lax.optimization_barrier(
+                (flow[x], mate_blocks, shards[0], lists)
             )
         shards.append(flow[x])
         if k < chips - 2:
@@ -463,11 +469,11 @@
             out_specs=[whole()] * (2 + len(pieces) - late),
             scratch_shapes=[
                 pltpu.VMEM((chips * base, unknowns), jnp.bfloat16),
-                pltpu.VMEM((2, *near_blocks.shape), jnp.bfloat16),
+                pltpu.VMEM((2 * stored, unknowns, unknowns), jnp.bfloat16),
                 pltpu.VMEM((2 * quarter * clusters + 1, directions, unknowns), jnp.float32),
                 pltpu.SemaphoreType.DMA((chips,)),
                 pltpu.SemaphoreType.DMA((chips,)),
-                pltpu.SemaphoreType.DMA((2 * CHUNKS,)),
+                pltpu.SemaphoreType.DMA((2 * stored // BATCH,)),
             ],
             compiler_params=pltpu.CompilerParams(vmem_limit_bytes=NEAR_VMEM),
             cost_estimate=pl.CostEstimate(

time: 70.8 us -> 71.6 us (1.011); the launches traced: 70.5 us -> 72.3 us
  starting transfers between devices: 27.1 us -> 28.6 us
    ppermute x27, starting transfers between devices: 27.1 us -> 28.6 us  [move(): return lax.ppermute(values, 'blk', where)]
  transfers between devices with their start and end apart: 27 -> 27, of which waited for: 15 -> 14; matrix products, arithmetic and copies ran while one was open for 3% -> 3% of each run, Pallas kernels for 12% -> 15%
where the time goes in v12:
time: 71.6 us; the launch traced here: 72.3 us
  starting transfers between devices  28.6 us (40%)
  waiting for transfers between devices  24 us (34%)
  Pallas kernels  16.3 us (23%)
  other arithmetic  2.26 us (3%)
  local copies, waits for them, and re-layouts  0.97 us (1%)
    ppermute x27, starting transfers between devices, move(): return lax.ppermute(values, 'blk', where)  28.6 us
    ppermute x27, waiting for transfers between devices, move(): return lax.ppermute(values, 'blk', where)  24 us
    pallas_call x2, Pallas kernels, near(): pl.pallas_call(functools.partial(near_kernel, late, BATCH, LAG, chips, le...  11.8 us
    pallas_call x1, Pallas kernels, far_field(): pl.pallas_call(far_kernel, out_shape=jax.ShapeDtypeStruct((clusters, dire...  2.51 us
    pallas_call x1, Pallas kernels, stationary(): pl.pallas_call(functools.partial(prologue_kernel, count), out_shape=[jax....  2.03 us
  transfers between devices with their start and end apart: 27, of which 14 were waited for; matrix products, arithmetic and copies ran while one was open for 3% of the time, Pallas kernels for 15%

profile of v12, /device:TPU:0, one launch (start us, length us, event | category | flops | bytes accessed | tf_op | source)
XLA Modules:
  0.0 72.3 jit_solution(2714209222488230286)
XLA Ops:
  0.5 2.0 %prologue.1 = (bf16[1152,128]{1,0:T(8,128)(2,1)}, s32[8,128]{1,0:T(8,128)}) custom-call(s32[1]{0:T(128)} %bitcast.me_ref.refs_2_, s32[1,128]{1,0:T(1,128)} %bitcast.14, s32[1,128]{1,0:T(1,128)} %bitcast.15, s32[1,128]{1,0:T(1,128)} %bitcast.16, bf16[16,64,128]{2,1,0:T(8,128)(2,1)} %rhs_ref.1, bf16[16,16,128]{2,1,0:T(8,128)(2,1)} %basis_ref.1), custom_call_target="tpu_custom_call" | custom-call | tf_op jit(solution)/shard_map/prologue/pallas_call | solution.py:420
  2.5 2.6 %collective-permute-start = (bf16[1152,128]{1,0:T(8,128)(2,1)}, bf16[1152,128]{1,0:T(8,128)(2,1)S(1)}, u32[]{:S(2)}, u32[]{:S(2)}) collective-permute-start(bf16[1152,128]{1,0:T(8,128)(2,1)} %get-tuple-element.43), channel_id=1, source_target_pairs={{0,4},{1,3},{4,8},{5,1},{8,12},{9,5},{12,14},{13,9},{14,10},{15,13... | collective-permute-start | bytes 884744 | tf_op jit(solution)/shard_map/ppermute | solution.py:413
  5.1 0.9 %copy.14 = bf16[256,16,16]{0,1,2:T(8,128)(2,1)S(1)} copy(bf16[256,16,16]{0,2,1:T(8,128)(2,1)} %param.16) | data formatting | bytes 262144 | tf_op args[5]
  6.0 1.4 %collective-permute-start.5 = (bf16[1152,128]{1,0:T(8,128)(2,1)}, bf16[1152,128]{1,0:T(8,128)(2,1)S(1)}, u32[]{:S(2)}, u32[]{:S(2)}) collective-permute-start(bf16[1152,128]{1,0:T(8,128)(2,1)} %get-tuple-element.43), channel_id=1, source_target_pairs={{0,3},{1,4},{4,1},{5,8},{8,5},{9,12},{12,9},{13,14},{14,13},{15,10... | collective-permute-start | bytes 884744 | tf_op jit(solution)/shard_map/ppermute | solution.py:413
  7.8 2.9 %collective-permute-done.refs_1_ = bf16[1152,128]{1,0:T(8,128)(2,1)S(1)} collective-permute-done((bf16[1152,128]{1,0:T(8,128)(2,1)}, bf16[1152,128]{1,0:T(8,128)(2,1)S(1)}, u32[]{:S(2)}, u32[]{:S(2)}) %collective-permute-start) | collective-permute-done | bytes 294944 | tf_op jit(solution)/shard_map/ppermute | solution.py:413
  10.7 2.4 %collective-permute-start.1 = (bf16[1152,128]{1,0:T(8,128)(2,1)S(1)}, bf16[1152,128]{1,0:T(8,128)(2,1)S(1)}, u32[]{:S(2)}, u32[]{:S(2)}) collective-permute-start(bf16[1152,128]{1,0:T(8,128)(2,1)S(1)} %collective-permute-done.refs_1_), channel_id=1, source_target_pairs={{0,4},{1,3},{4,8},{5,1},{8,12},{9,5},{12,14},{13,9},{14,10},{15,13... | collective-permute-start | bytes 884744 | tf_op jit(solution)/shard_map/ppermute | solution.py:413
  13.1 1.4 %collective-permute-done.4 = s32[8,128]{1,0:T(8,128)S(1)} collective-permute-done((s32[8,128]{1,0:T(8,128)}, s32[8,128]{1,0:T(8,128)S(1)}, u32[]{:S(2)}, u32[]{:S(2)}) %collective-permute-start.4) | collective-permute-done | bytes 4128 | tf_op jit(solution)/shard_map/ppermute | solution.py:413
  14.4 0.7 pad_add_fusion.list_ref
  15.1 1.6 %collective-permute-start.6 = (bf16[1152,128]{1,0:T(8,128)(2,1)S(1)}, bf16[1152,128]{1,0:T(8,128)(2,1)S(1)}, u32[]{:S(2)}, u32[]{:S(2)}) collective-permute-start(bf16[1152,128]{1,0:T(8,128)(2,1)S(1)} %collective-permute-done.5.refs_2_), channel_id=1, source_target_pairs={{0,4},{1,3},{4,8},{5,1},{8,12},{9,5},{12,14},{13,9},{14,10},{15,13... | collective-permute-start | bytes 884744 | tf_op jit(solution)/shard_map/ppermute | solution.py:413
  16.7 1.3 %collective-permute-done.1.refs_3_ = bf16[1152,128]{1,0:T(8,128)(2,1)S(1)} collective-permute-done((bf16[1152,128]{1,0:T(8,128)(2,1)S(1)}, bf16[1152,128]{1,0:T(8,128)(2,1)S(1)}, u32[]{:S(2)}, u32[]{:S(2)}) %collective-permute-start.1) | collective-permute-done | bytes 294944 | tf_op jit(solution)/shard_map/ppermute | solution.py:413
  18.0 1.7 %collective-permute-start.7 = (bf16[1152,128]{1,0:T(8,128)(2,1)S(1)}, bf16[1152,128]{1,0:T(8,128)(2,1)S(1)}, u32[]{:S(2)}, u32[]{:S(2)}) collective-permute-start(bf16[1152,128]{1,0:T(8,128)(2,1)S(1)} %collective-permute-done.1.refs_3_), channel_id=1, source_target_pairs={{0,4},{1,3},{4,8},{5,1},{8,12},{9,5},{12,14},{13,9},{14,10},{15,13... | collective-permute-start | bytes 884744 | tf_op jit(solution)/shard_map/ppermute | solution.py:413
  19.8 2.1 %collective-permute-done.6.refs_4_ = bf16[1152,128]{1,0:T(8,128)(2,1)S(1)} collective-permute-done((bf16[1152,128]{1,0:T(8,128)(2,1)S(1)}, bf16[1152,128]{1,0:T(8,128)(2,1)S(1)}, u32[]{:S(2)}, u32[]{:S(2)}) %collective-permute-start.6) | collective-permute-done | bytes 294944 | tf_op jit(solution)/shard_map/ppermute | solution.py:413
  21.9 1.6 %collective-permute-start.8 = (bf16[1152,128]{1,0:T(8,128)(2,1)S(1)}, bf16[1152,128]{1,0:T(8,128)(2,1)S(1)}, u32[]{:S(2)}, u32[]{:S(2)}) collective-permute-start(bf16[1152,128]{1,0:T(8,128)(2,1)S(1)} %collective-permute-done.6.refs_4_), channel_id=1, source_target_pairs={{0,4},{1,3},{4,8},{5,1},{8,12},{9,5},{12,14},{13,9},{14,10},{15,13... | collective-permute-start | bytes 884744 | tf_op jit(solution)/shard_map/ppermute | solution.py:413
  23.4 1.6 %collective-permute-done.7.refs_5_ = bf16[1152,128]{1,0:T(8,128)(2,1)S(1)} collective-permute-done((bf16[1152,128]{1,0:T(8,128)(2,1)S(1)}, bf16[1152,128]{1,0:T(8,128)(2,1)S(1)}, u32[]{:S(2)}, u32[]{:S(2)}) %collective-permute-start.7) | collective-permute-done | bytes 294944 | tf_op jit(solution)/shard_map/ppermute | solution.py:413
  25.0 1.6 %collective-permute-start.9 = (bf16[1152,128]{1,0:T(8,128)(2,1)S(1)}, bf16[1152,128]{1,0:T(8,128)(2,1)S(1)}, u32[]{:S(2)}, u32[]{:S(2)}) collective-permute-start(bf16[1152,128]{1,0:T(8,128)(2,1)S(1)} %collective-permute-done.7.refs_5_), channel_id=1, source_target_pairs={{0,4},{1,3},{4,8},{5,1},{8,12},{9,5},{12,14},{13,9},{14,10},{15,13... | collective-permute-start | bytes 884744 | tf_op jit(solution)/shard_map/ppermute | solution.py:413
  26.6 2.0 %collective-permute-done.8.refs_6_ = bf16[1152,128]{1,0:T(8,128)(2,1)S(1)} collective-permute-done((bf16[1152,128]{1,0:T(8,128)(2,1)S(1)}, bf16[1152,128]{1,0:T(8,128)(2,1)S(1)}, u32[]{:S(2)}, u32[]{:S(2)}) %collective-permute-start.8) | collective-permute-done | bytes 294944 | tf_op jit(solution)/shard_map/ppermute | solution.py:413
  28.6 3.2 %collective-permute-done.9.refs_7_ = bf16[1152,128]{1,0:T(8,128)(2,1)S(1)} collective-permute-done((bf16[1152,128]{1,0:T(8,128)(2,1)S(1)}, bf16[1152,128]{1,0:T(8,128)(2,1)S(1)}, u32[]{:S(2)}, u32[]{:S(2)}) %collective-permute-start.9) | collective-permute-done | bytes 294944 | tf_op jit(solution)/shard_map/ppermute | solution.py:413
  31.7 5.7 %near.2 = (f32[64,64,128]{2,1,0:T(8,128)S(1)}, bf16[16,64,128]{2,1,0:T(8,128)(2,1)S(1)}, bf16[16,64,128]{2,1,0:T(8,128)(2,1)S(1)}, bf16[16,64,128]{2,1,0:T(8,128...) custom-call(s32[16,128]{1,0:T(8,128)S(1)} %pad_add_fusion.list_ref, ...), custom_call_target="tpu_custom_call" | custom-call | flops 2147483648 | bytes 16777216 | tf_op jit(solution)/shard_map/near/pallas_call | solution.py:458
  38.0 1.0 %collective-permute-done.12 = bf16[16,64,128]{2,1,0:T(8,128)(2,1)S(1)} collective-permute-done((bf16[16,64,128]{2,1,0:T(8,128)(2,1)S(1)}, bf16[16,64,128]{2,1,0:T(8,128)(2,1)S(1)}, u32[]{:S(2)}, u32[]{:S(2)}) %collective-permute-start.12) | collective-permute-done | bytes 262176 | tf_op jit(solution)/shard_map/ppermute | solution.py:413
  39.8 3.1 %collective-permute-start.13 = (bf16[16,64,128]{2,1,0:T(8,128)(2,1)S(1)}, bf16[16,64,128]{2,1,0:T(8,128)(2,1)S(1)}, u32[]{:S(2)}, u32[]{:S(2)}) collective-permute-start(bf16[16,64,128]{2,1,0:T(8,128)(2,1)S(1)} %get-tuple-element.50), channel_id=1, source_target_pairs={{0,4},{1,3},{4,8},{5,1},{8,12},{9,5},{12,14},{13,9},{14,10},{15,13... | collective-permute-start | bytes 786440 | tf_op jit(solution)/shard_map/ppermute | solution.py:413
  42.9 2.7 %collective-permute-start.17 = (bf16[16,64,128]{2,1,0:T(8,128)(2,1)S(1)}, bf16[16,64,128]{2,1,0:T(8,128)(2,1)S(1)}, u32[]{:S(2)}, u32[]{:S(2)}) collective-permute-start(bf16[16,64,128]{2,1,0:T(8,128)(2,1)S(1)} %get-tuple-element.52), channel_id=1, source_target_pairs={{0,4},{1,3},{4,8},{5,1},{8,12},{9,5},{12,14},{13,9},{14,10},{15,13... | collective-permute-start | bytes 786440 | tf_op jit(solution)/shard_map/ppermute | solution.py:413
  45.6 6.1 %near.3 = (f32[64,64,128]{2,1,0:T(8,128)S(1)}, bf16[16,64,128]{2,1,0:T(8,128)(2,1)S(1)}, bf16[16,64,128]{2,1,0:T(8,128)(2,1)S(1)}, bf16[16,64,128]{2,1,0:T(8,128)(2,1)S(1)}, bf16[16,64,128]{2,1,0:T(8,128)(2,1)S(1)}) custom-call(s32[16,128]{1,0:T(8,128)S(1)} %pad_add_fusion.list_ref, bf16[1152,128]{1,0:T(8,128)(2,1)S(1)} %collective-permute-done.3.refs_0_, ...), custom_call_target="tpu_custom_call" | custom-call | flops 2147483648 | bytes 16777216 | tf_op jit(solution)/shard_map/near/pallas_call | solution.py:458
  51.9 1.7 %collective-permute-start.16 = (bf16[16,64,128]{2,1,0:T(8,128)(2,1)S(1)}, bf16[16,64,128]{2,1,0:T(8,128)(2,1)S(1)}, u32[]{:S(2)}, u32[]{:S(2)}) collective-permute-start(bf16[16,64,128]{2,1,0:T(8,128)(2,1)S(1)} %add_convert_fusion.5), channel_id=1, source_target_pairs={{0,4},{1,3},{4,8},{5,1},{8,12},{9,5},{12,14},{13,9},{14,10},{15,13... | collective-permute-start | bytes 786440 | tf_op jit(solution)/shard_map/ppermute | solution.py:413
  54.9 3.4 %collective-permute-done.16 = bf16[16,64,128]{2,1,0:T(8,128)(2,1)S(1)} collective-permute-done((bf16[16,64,128]{2,1,0:T(8,128)(2,1)S(1)}, bf16[16,64,128]{2,1,0:T(8,128)(2,1)S(1)}, u32[]{:S(2)}, u32[]{:S(2)}) %collective-permute-start.16) | collective-permute-done | bytes 262176 | tf_op jit(solution)/shard_map/ppermute | solution.py:413
  58.4 1.7 %collective-permute-start.20 = (bf16[16,64,128]{2,1,0:T(8,128)(2,1)S(1)}, bf16[16,64,128]{2,1,0:T(8,128)(2,1)S(1)}, u32[]{:S(2)}, u32[]{:S(2)}) collective-permute-start(bf16[16,64,128]{2,1,0:T(8,128)(2,1)S(1)} %add_convert_fusion.3), channel_id=1, source_target_pairs={{0,4},{1,3},{4,8},{5,1},{8,12},{9,5},{12,14},{13,9},{14,10},{15,13... | collective-permute-start | bytes 786440 | tf_op jit(solution)/shard_map/ppermute | solution.py:413
  61.2 1.7 %collective-permute-start.25 = (bf16[16,64,128]{2,1,0:T(8,128)(2,1)S(1)}, bf16[16,64,128]{2,1,0:T(8,128)(2,1)S(1)}, u32[]{:S(2)}, u32[]{:S(2)}) collective-permute-start(bf16[16,64,128]{2,1,0:T(8,128)(2,1)S(1)} %add_convert_fusion.2), channel_id=1, source_target_pairs={{0,4},{1,3},{4,8},{5,1},{8,12},{9,5},{12,14},{13,9},{14,10},{15,13... | collective-permute-start | bytes 786440 | tf_op jit(solution)/shard_map/ppermute | solution.py:413
  62.9 2.0 %collective-permute-done.20 = bf16[16,64,128]{2,1,0:T(8,128)(2,1)S(1)} collective-permute-done((bf16[16,64,128]{2,1,0:T(8,128)(2,1)S(1)}, bf16[16,64,128]{2,1,0:T(8,128)(2,1)S(1)}, u32[]{:S(2)}, u32[]{:S(2)}) %collective-permute-start.20) | collective-permute-done | bytes 262176 | tf_op jit(solution)/shard_map/ppermute | solution.py:413
  65.0 1.7 %collective-permute-start.24 = (bf16[16,64,128]{2,1,0:T(8,128)(2,1)S(1)}, bf16[16,64,128]{2,1,0:T(8,128)(2,1)S(1)}, u32[]{:S(2)}, u32[]{:S(2)}) collective-permute-start(bf16[16,64,128]{2,1,0:T(8,128)(2,1)S(1)} %add_convert_fusion.1), channel_id=1, source_target_pairs={{0,4},{1,3},{4,8},{5,1},{8,12},{9,5},{12,14},{13,9},{14,10},{15,13... | collective-permute-start | bytes 786440 | tf_op jit(solution)/shard_map/ppermute | solution.py:413
  66.7 1.0 %collective-permute-done.25 = bf16[16,64,128]{2,1,0:T(8,128)(2,1)S(1)} collective-permute-done((bf16[16,64,128]{2,1,0:T(8,128)(2,1)S(1)}, bf16[16,64,128]{2,1,0:T(8,128)(2,1)S(1)}, u32[]{:S(2)}, u32[]{:S(2)}) %collective-permute-start.25) | collective-permute-done | bytes 262176 | tf_op jit(solution)/shard_map/ppermute | solution.py:413
  67.7 2.5 %far.1 = f32[16,64,128]{2,1,0:T(8,128)S(1)} custom-call(bf16[1024,128]{1,0:T(8,128)(2,1)S(1)} %get-tuple-element.46.refs_0_, bf16[1024,128]{1,0:T(8,128)(2,1)S(1)} %collective-permute-done.10.refs_1_, s32[1]{0:T(128)} %bitcast.me_ref.refs_2_, bf16[16,16,256]{2,1,0:T(8,128)(2,1)S(1)} %bitcast.10, s32[1,256]{1,0:T(1,128)S(1)} %bitcast.11, ...), custom_call_target="tpu_custom_call" | custom-call | flops 536870912 | bytes 8388608 | tf_op jit(solution)/shard_map/far/pallas_call | solution.py:489
  70.2 1.2 %collective-permute-done.24 = bf16[16,64,128]{2,1,0:T(8,128)(2,1)S(1)} collective-permute-done((bf16[16,64,128]{2,1,0:T(8,128)(2,1)S(1)}, bf16[16,64,128]{2,1,0:T(8,128)(2,1)S(1)}, u32[]{:S(2)}, u32[]{:S(2)}) %collective-permute-start.24) | collective-permute-done | bytes 262176 | tf_op jit(solution)/shard_map/ppermute | solution.py:413
  71.6 0.8 %add_convert_fusion = bf16[16,64,128]{2,1,0:T(8,128)(2,1)} fusion(f32[16,64,128]{2,1,0:T(8,128)S(1)} %convert_add_fusion, bf16[16,64,128]{2,1,0:T(8,128)(2,1)S(1)} %collective-permute-done.26), kind=kLoop, calls=%fused_computation | loop fusion | flops 393216 | bytes 1048576 | tf_op jit(solution)/shard_map/convert_element_type | solution.py:543
  (44 shorter events, 5.0 us)
Async XLA Ops:
  0.0 18.0 %collective-permute-start.2 = (bf16[128,128,128]{2,1,0:T(8,128)(2,1)}, bf16[128,128,128]{2,1,0:T(8,128)(2,1)}, u32[]{:S(2)}, u32[]{:S(2)}) collective-permute-start(bf16[128,128,128]{2,1,0:T(8,128)(2,1)} %refs_8_.3), channel_id=1, source_target_pairs={{0,1},{1,0},{2,3},{3,2},{4,5},{5,4},{6,7},{7,6},{8,9},{9,8},{10,11... | collective-permute-start | bytes 12582920 | tf_op jit(solution)/shard_map/ppermute | solution.py:413
  2.5 8.2 %collective-permute-start = (bf16[1152,128]{1,0:T(8,128)(2,1)}, bf16[1152,128]{1,0:T(8,128)(2,1)S(1)}, u32[]{:S(2)}, u32[]{:S(2)}) collective-permute-start(bf16[1152,128]{1,0:T(8,128)(2,1)} %get-tuple-element.43), channel_id=1, source_target_pairs={{0,4},{1,3},{4,8},{5,1},{8,12},{9,5},{12,14},{13,9},{14,10},{15,13... | collective-permute-start | bytes 884744 | tf_op jit(solution)/shard_map/ppermute | solution.py:413
  6.0 9.1 %collective-permute-start.5 = (bf16[1152,128]{1,0:T(8,128)(2,1)}, bf16[1152,128]{1,0:T(8,128)(2,1)S(1)}, u32[]{:S(2)}, u32[]{:S(2)}) collective-permute-start(bf16[1152,128]{1,0:T(8,128)(2,1)} %get-tuple-element.43), channel_id=1, source_target_pairs={{0,3},{1,4},{4,1},{5,8},{8,5},{9,12},{12,9},{13,14},{14,13},{15,10... | collective-permute-start | bytes 884744 | tf_op jit(solution)/shard_map/ppermute | solution.py:413
  7.4 9.3 %collective-permute-start.3 = (bf16[1152,128]{1,0:T(8,128)(2,1)}, bf16[1152,128]{1,0:T(8,128)(2,1)S(1)}, u32[]{:S(2)}, u32[]{:S(2)}) collective-permute-start(bf16[1152,128]{1,0:T(8,128)(2,1)} %get-tuple-element.43), channel_id=1, source_target_pairs={{0,1},{1,0},{2,3},{3,2},{4,5},{5,4},{6,7},{7,6},{8,9},{9,8},{10,11... | collective-permute-start | bytes 884744 | tf_op jit(solution)/shard_map/ppermute | solution.py:413
  10.7 7.4 %collective-permute-start.1 = (bf16[1152,128]{1,0:T(8,128)(2,1)S(1)}, bf16[1152,128]{1,0:T(8,128)(2,1)S(1)}, u32[]{:S(2)}, u32[]{:S(2)}) collective-permute-start(bf16[1152,128]{1,0:T(8,128)(2,1)S(1)} %collective-permute-done.refs_1_), channel_id=1, source_target_pairs={{0,4},{1,3},{4,8},{5,1},{8,12},{9,5},{12,14},{13,9},{14,10},{15,13... | collective-permute-start | bytes 884744 | tf_op jit(solution)/shard_map/ppermute | solution.py:413
  13.1 1.4 %collective-permute-start.4 = (s32[8,128]{1,0:T(8,128)}, s32[8,128]{1,0:T(8,128)S(1)}, u32[]{:S(2)}, u32[]{:S(2)}) collective-permute-start(s32[8,128]{1,0:T(8,128)} %get-tuple-element.40), channel_id=1, source_target_pairs={{0,1},{1,0},{2,3},{3,2},{4,5},{5,4},{6,7},{7,6},{8,9},{9,8},{10,11... | collective-permute-start | bytes 12296 | tf_op jit(solution)/shard_map/ppermute | solution.py:413
  15.1 6.7 %collective-permute-start.6 = (bf16[1152,128]{1,0:T(8,128)(2,1)S(1)}, bf16[1152,128]{1,0:T(8,128)(2,1)S(1)}, u32[]{:S(2)}, u32[]{:S(2)}) collective-permute-start(bf16[1152,128]{1,0:T(8,128)(2,1)S(1)} %collective-permute-done.5.refs_2_), channel_id=1, source_target_pairs={{0,4},{1,3},{4,8},{5,1},{8,12},{9,5},{12,14},{13,9},{14,10},{15,13... | collective-permute-start | bytes 884744 | tf_op jit(solution)/shard_map/ppermute | solution.py:413
  18.0 7.0 %collective-permute-start.7 = (bf16[1152,128]{1,0:T(8,128)(2,1)S(1)}, bf16[1152,128]{1,0:T(8,128)(2,1)S(1)}, u32[]{:S(2)}, u32[]{:S(2)}) collective-permute-start(bf16[1152,128]{1,0:T(8,128)(2,1)S(1)} %collective-permute-done.1.refs_3_), channel_id=1, source_target_pairs={{0,4},{1,3},{4,8},{5,1},{8,12},{9,5},{12,14},{13,9},{14,10},{15,13... | collective-permute-start | bytes 884744 | tf_op jit(solution)/shard_map/ppermute | solution.py:413
  21.9 6.7 %collective-permute-start.8 = (bf16[1152,128]{1,0:T(8,128)(2,1)S(1)}, bf16[1152,128]{1,0:T(8,128)(2,1)S(1)}, u32[]{:S(2)}, u32[]{:S(2)}) collective-permute-start(bf16[1152,128]{1,0:T(8,128)(2,1)S(1)} %collective-permute-done.6.refs_4_), channel_id=1, source_target_pairs={{0,4},{1,3},{4,8},{5,1},{8,12},{9,5},{12,14},{13,9},{14,10},{15,13... | collective-permute-start | bytes 884744 | tf_op jit(solution)/shard_map/ppermute | solution.py:413
  25.0 6.7 %collective-permute-start.9 = (bf16[1152,128]{1,0:T(8,128)(2,1)S(1)}, bf16[1152,128]{1,0:T(8,128)(2,1)S(1)}, u32[]{:S(2)}, u32[]{:S(2)}) collective-permute-start(bf16[1152,128]{1,0:T(8,128)(2,1)S(1)} %collective-permute-done.7.refs_5_), channel_id=1, source_target_pairs={{0,4},{1,3},{4,8},{5,1},{8,12},{9,5},{12,14},{13,9},{14,10},{15,13... | collective-permute-start | bytes 884744 | tf_op jit(solution)/shard_map/ppermute | solution.py:413
  37.4 1.6 %collective-permute-start.12 = (bf16[16,64,128]{2,1,0:T(8,128)(2,1)S(1)}, bf16[16,64,128]{2,1,0:T(8,128)(2,1)S(1)}, u32[]{:S(2)}, u32[]{:S(2)}) collective-permute-start(bf16[16,64,128]{2,1,0:T(8,128)(2,1)S(1)} %get-tuple-element.49), channel_id=1, source_target_pairs={{0,1},{1,0},{2,3},{3,2},{4,5},{5,4},{6,7},{7,6},{8,9},{9,8},{10,11... | collective-permute-start | bytes 786440 | tf_op jit(solution)/shard_map/ppermute | solution.py:413
  37.5 1.9 %collective-permute-start.11 = (bf16[16,64,128]{2,1,0:T(8,128)(2,1)S(1)}, bf16[16,64,128]{2,1,0:T(8,128)(2,1)S(1)}, u32[]{:S(2)}, u32[]{:S(2)}) collective-permute-start(bf16[16,64,128]{2,1,0:T(8,128)(2,1)S(1)} %get-tuple-element.48), channel_id=1, source_target_pairs={{0,1},{1,0},{2,3},{3,2},{4,5},{5,4},{6,7},{7,6},{8,9},{9,8},{10,11... | collective-permute-start | bytes 786440 | tf_op jit(solution)/shard_map/ppermute | solution.py:413
  39.6 12.2 %collective-permute-start.14 = (bf16[16,64,128]{2,1,0:T(8,128)(2,1)S(1)}, bf16[16,64,128]{2,1,0:T(8,128)(2,1)S(1)}, u32[]{:S(2)}, u32[]{:S(2)}) collective-permute-start(bf16[16,64,128]{2,1,0:T(8,128)(2,1)S(1)} %get-tuple-element.53), channel_id=1, source_target_pairs={{0,1},{1,0},{2,3},{3,2},{4,5},{5,4},{6,7},{7,6},{8,9},{9,8},{10,11... | collective-permute-start | bytes 786440 | tf_op jit(solution)/shard_map/ppermute | solution.py:413
  39.8 12.0 %collective-permute-start.13 = (bf16[16,64,128]{2,1,0:T(8,128)(2,1)S(1)}, bf16[16,64,128]{2,1,0:T(8,128)(2,1)S(1)}, u32[]{:S(2)}, u32[]{:S(2)}) collective-permute-start(bf16[16,64,128]{2,1,0:T(8,128)(2,1)S(1)} %get-tuple-element.50), channel_id=1, source_target_pairs={{0,4},{1,3},{4,8},{5,1},{8,12},{9,5},{12,14},{13,9},{14,10},{15,13... | collective-permute-start | bytes 786440 | tf_op jit(solution)/shard_map/ppermute | solution.py:413
  42.9 11.2 %collective-permute-start.17 = (bf16[16,64,128]{2,1,0:T(8,128)(2,1)S(1)}, bf16[16,64,128]{2,1,0:T(8,128)(2,1)S(1)}, u32[]{:S(2)}, u32[]{:S(2)}) collective-permute-start(bf16[16,64,128]{2,1,0:T(8,128)(2,1)S(1)} %get-tuple-element.52), channel_id=1, source_target_pairs={{0,4},{1,3},{4,8},{5,1},{8,12},{9,5},{12,14},{13,9},{14,10},{15,13... | collective-permute-start | bytes 786440 | tf_op jit(solution)/shard_map/ppermute | solution.py:413
  45.6 6.3 %collective-permute-start.15 = (bf16[16,64,128]{2,1,0:T(8,128)(2,1)S(1)}, bf16[16,64,128]{2,1,0:T(8,128)(2,1)S(1)}, u32[]{:S(2)}, u32[]{:S(2)}) collective-permute-start(bf16[16,64,128]{2,1,0:T(8,128)(2,1)S(1)} %get-tuple-element.55), channel_id=1, source_target_pairs={{0,1},{1,0},{2,3},{3,2},{4,5},{5,4},{6,7},{7,6},{8,9},{9,8},{10,11... | collective-permute-start | bytes 786440 | tf_op jit(solution)/shard_map/ppermute | solution.py:413
  51.7 2.5 %collective-permute-start.18 = (bf16[16,64,128]{2,1,0:T(8,128)(2,1)S(1)}, bf16[16,64,128]{2,1,0:T(8,128)(2,1)S(1)}, u32[]{:S(2)}, u32[]{:S(2)}) collective-permute-start(bf16[16,64,128]{2,1,0:T(8,128)(2,1)S(1)} %get-tuple-element.60), channel_id=1, source_target_pairs={{0,1},{1,0},{2,3},{3,2},{4,5},{5,4},{6,7},{7,6},{8,9},{9,8},{10,11... | collective-permute-start | bytes 786440 | tf_op jit(solution)/shard_map/ppermute | solution.py:413
  51.9 6.4 %collective-permute-start.16 = (bf16[16,64,128]{2,1,0:T(8,128)(2,1)S(1)}, bf16[16,64,128]{2,1,0:T(8,128)(2,1)S(1)}, u32[]{:S(2)}, u32[]{:S(2)}) collective-permute-start(bf16[16,64,128]{2,1,0:T(8,128)(2,1)S(1)} %add_convert_fusion.5), channel_id=1, source_target_pairs={{0,4},{1,3},{4,8},{5,1},{8,12},{9,5},{12,14},{13,9},{14,10},{15,13... | collective-permute-start | bytes 786440 | tf_op jit(solution)/shard_map/ppermute | solution.py:413
  53.6 4.9 %collective-permute-start.19 = (bf16[16,64,128]{2,1,0:T(8,128)(2,1)S(1)}, bf16[16,64,128]{2,1,0:T(8,128)(2,1)S(1)}, u32[]{:S(2)}, u32[]{:S(2)}) collective-permute-start(bf16[16,64,128]{2,1,0:T(8,128)(2,1)S(1)} %get-tuple-element.62), channel_id=1, source_target_pairs={{0,1},{1,0},{2,3},{3,2},{4,5},{5,4},{6,7},{7,6},{8,9},{9,8},{10,11... | collective-permute-start | bytes 786440 | tf_op jit(solution)/shard_map/ppermute | solution.py:413
  53.6 7.7 %collective-permute-start.22 = (bf16[16,64,128]{2,1,0:T(8,128)(2,1)S(1)}, bf16[16,64,128]{2,1,0:T(8,128)(2,1)S(1)}, u32[]{:S(2)}, u32[]{:S(2)}) collective-permute-start(bf16[16,64,128]{2,1,0:T(8,128)(2,1)S(1)} %get-tuple-element.66), channel_id=1, source_target_pairs={{0,1},{1,0},{2,3},{3,2},{4,5},{5,4},{6,7},{7,6},{8,9},{9,8},{10,11... | collective-permute-start | bytes 786440 | tf_op jit(solution)/shard_map/ppermute | solution.py:413
  54.2 13.5 %copy-start = (bf16[16,16,128]{2,1,0:T(8,128)(2,1)S(1)}, bf16[16,16,128]{2,1,0:T(8,128)(2,1)}, u32[]{:S(2)}) copy-start(bf16[16,16,128]{2,1,0:T(8,128)(2,1)} %refs_7_.1) | copy-start | bytes 196612
  54.2 13.5 %copy-start.1 = (s32[256]{0:T(256)S(1)}, s32[256]{0:T(256)}, u32[]{:S(2)}) copy-start(s32[256]{0:T(256)} %param.17) | copy-start | bytes 3076
  54.2 13.5 %copy-start.2 = (s32[256,1]{0,1:T(1,128)S(1)}, s32[256,1]{0,1:T(1,128)}, u32[]{:S(2)}) copy-start(s32[256,1]{0,1:T(1,128)} %param.18) | copy-start | bytes 3076
  54.2 13.5 %copy-start.3 = (s32[256]{0:T(256)S(1)}, s32[256]{0:T(256)}, u32[]{:S(2)}) copy-start(s32[256]{0:T(256)} %param.19) | copy-start | bytes 3076
  54.2 6.9 %collective-permute-start.21 = (bf16[16,64,128]{2,1,0:T(8,128)(2,1)S(1)}, bf16[16,64,128]{2,1,0:T(8,128)(2,1)S(1)}, u32[]{:S(2)}, u32[]{:S(2)}) collective-permute-start(bf16[16,64,128]{2,1,0:T(8,128)(2,1)S(1)} %add_convert_fusion.4), channel_id=1, source_target_pairs={{0,4},{1,3},{4,8},{5,1},{8,12},{9,5},{12,14},{13,9},{14,10},{15,13... | collective-permute-start | bytes 786440 | tf_op jit(solution)/shard_map/ppermute | solution.py:413
  58.4 6.4 %collective-permute-start.20 = (bf16[16,64,128]{2,1,0:T(8,128)(2,1)S(1)}, bf16[16,64,128]{2,1,0:T(8,128)(2,1)S(1)}, u32[]{:S(2)}, u32[]{:S(2)}) collective-permute-start(bf16[16,64,128]{2,1,0:T(8,128)(2,1)S(1)} %add_convert_fusion.3), channel_id=1, source_target_pairs={{0,4},{1,3},{4,8},{5,1},{8,12},{9,5},{12,14},{13,9},{14,10},{15,13... | collective-permute-start | bytes 786440 | tf_op jit(solution)/shard_map/ppermute | solution.py:413
  60.1 7.6 %collective-permute-start.10 = (bf16[1024,128]{1,0:T(8,128)(2,1)S(1)}, bf16[1024,128]{1,0:T(8,128)(2,1)S(1)}, u32[]{:S(2)}, u32[]{:S(2)}) collective-permute-start(bf16[1024,128]{1,0:T(8,128)(2,1)S(1)} %get-tuple-element.46.refs_0_), channel_id=1, source_target_pairs={{0,1},{1,0},{2,3},{3,2},{4,5},{5,4},{6,7},{7,6},{8,9},{9,8},{10,11... | collective-permute-start | bytes 786440 | tf_op jit(solution)/shard_map/ppermute | solution.py:413
  60.1 4.9 %collective-permute-start.23 = (bf16[16,64,128]{2,1,0:T(8,128)(2,1)S(1)}, bf16[16,64,128]{2,1,0:T(8,128)(2,1)S(1)}, u32[]{:S(2)}, u32[]{:S(2)}) collective-permute-start(bf16[16,64,128]{2,1,0:T(8,128)(2,1)S(1)} %get-tuple-element.68), channel_id=1, source_target_pairs={{0,1},{1,0},{2,3},{3,2},{4,5},{5,4},{6,7},{7,6},{8,9},{9,8},{10,11... | collective-permute-start | bytes 786440 | tf_op jit(solution)/shard_map/ppermute | solution.py:413
  61.2 6.4 %collective-permute-start.25 = (bf16[16,64,128]{2,1,0:T(8,128)(2,1)S(1)}, bf16[16,64,128]{2,1,0:T(8,128)(2,1)S(1)}, u32[]{:S(2)}, u32[]{:S(2)}) collective-permute-start(bf16[16,64,128]{2,1,0:T(8,128)(2,1)S(1)} %add_convert_fusion.2), channel_id=1, source_target_pairs={{0,4},{1,3},{4,8},{5,1},{8,12},{9,5},{12,14},{13,9},{14,10},{15,13... | collective-permute-start | bytes 786440 | tf_op jit(solution)/shard_map/ppermute | solution.py:413
  65.0 6.4 %collective-permute-start.24 = (bf16[16,64,128]{2,1,0:T(8,128)(2,1)S(1)}, bf16[16,64,128]{2,1,0:T(8,128)(2,1)S(1)}, u32[]{:S(2)}, u32[]{:S(2)}) collective-permute-start(bf16[16,64,128]{2,1,0:T(8,128)(2,1)S(1)} %add_convert_fusion.1), channel_id=1, source_target_pairs={{0,4},{1,3},{4,8},{5,1},{8,12},{9,5},{12,14},{13,9},{14,10},{15,13... | collective-permute-start | bytes 786440 | tf_op jit(solution)/shard_map/ppermute | solution.py:413
  67.7 3.9 %collective-permute-start.26 = (bf16[16,64,128]{2,1,0:T(8,128)(2,1)S(1)}, bf16[16,64,128]{2,1,0:T(8,128)(2,1)S(1)}, u32[]{:S(2)}, u32[]{:S(2)}) collective-permute-start(bf16[16,64,128]{2,1,0:T(8,128)(2,1)S(1)} %collective-permute-done.25), channel_id=1, source_target_pairs={{0,1},{1,0},{2,3},{3,2},{4,5},{5,4},{6,7},{7,6},{8,9},{9,8},{10,11... | collective-permute-start | bytes 786440 | tf_op jit(solution)/shard_map/ppermute | solution.py:413

commit v13 on v12

--- a/solution.py
+++ b/solution.py
@@ -121,22 +121,19 @@
     count, me_ref, owner_ref, slot_ref, offset_ref, rhs_ref, basis_ref, payload_ref, list_ref
 ):
     clusters, directions, unknowns = rhs_ref.shape
-    base = clusters * directions
-    payload_ref[0:base, :] = rhs_ref[...].reshape(base, unknowns)
     rank_k = basis_ref.shape[1]
     half = clusters // 2
+    base = clusters * directions
     rows = []
     for c in range(half):
+        pair = jnp.concatenate([rhs_ref[c], rhs_ref[c + half]], axis=0).astype(jnp.float32)
+        tile = jnp.transpose(pair).astype(payload_ref.dtype)
+        payload_ref[c * unknowns : (c + 1) * unknowns, :] = tile
         parts = [
-            lax.dot_general(
-                basis_ref[e],
-                rhs_ref[e],
-                (((1,), (1,)), ((), ())),
-                preferred_element_type=jnp.float32,
-            )
-            for e in (c, c + half)
+            jnp.dot(basis_ref[e], tile, preferred_element_type=jnp.float32) for e in (c, c + half)
         ]
-        rows.append(jnp.concatenate(parts, axis=1))
+        lane = lax.broadcasted_iota(jnp.int32, parts[0].shape, 1)
+        rows.append(jnp.where(lane < directions, *parts))
     payload_ref[base:, :] = jnp.concatenate(
         [row[q : q + 1] for q in range(rank_k) for row in rows], axis=0
     ).astype(payload_ref.dtype)
@@ -173,15 +170,16 @@
     list_ref[...] = values.astype(jnp.int32)
 
 
-def near_kernel(late, batch, lag, shards, sends, list_ref, *refs):
-    shard_refs, (own_hbm, mate_hbm, keep_ref) = refs[:shards], refs[shards : shards + 3]
-    send_refs, refs = refs[shards + 3 : shards + 3 + sends], refs[shards + 3 + sends :]
+def near_kernel(late, batch, lag, shards, kept, sends, list_ref, *refs):
+    shard_refs, (own_hbm, mate_hbm), refs = refs[:shards], refs[shards : shards + 2], refs[shards + 2 :]
+    keep_refs, send_refs, refs = refs[:kept], refs[kept : kept + sends], refs[kept + sends :]
     if not late:
         coef_ref, refs = refs[0], refs[1:]
-    columns, blocks, sums, column_sem, coef_sem, block_sem = refs
-    directions = sums.shape[1]
+    columns, blocks, sums, entries, column_sem, coef_sem, block_sem = refs
+    unknowns, width = sums.shape[1:]
     span = columns.shape[0] // shards
     dummy = sums.shape[0] - 1
+    pairs = span // unknowns
 
     copies = [
         pltpu.make_async_copy(
@@ -200,33 +198,43 @@
             )
             for k, ref in enumerate(shard_refs)
         ]
-    for copy in tails:
-        copy.start()
 
     begin, begin_there = list_ref[3, late], list_ref[11, 2 + late]
     here = list_ref[3, late + 1] - begin
     total = here + list_ref[11, 3 + late] - begin_there
-
-    def entry(j):
-        j = jnp.minimum(j, total - 1)
-        half = (j >= here).astype(jnp.int32)
-        return half, half * 8, j + jnp.where(half == 1, begin_there - here, begin)
-
-    def fetch(j, carry):
-        half, row, at = entry(j)
-
-        for side, source in enumerate((own_hbm, mate_hbm)):
-
-            @pl.when(half == side)
-            def _():
-                pltpu.make_async_copy(
-                    source.at[list_ref[row, at]], blocks.at[j], block_sem.at[j // batch]
-                ).start()
-
+    steps = (total + batch - 1) // batch
+
+    def fetch(source, row, shift, swap):
+        def one(j, carry):
+            at = j + shift
+            place, column = list_ref[row + 1, at], list_ref[row + 2, at]
+            slot, cluster = place & (2 * pairs - 1), column & (2 * pairs - 1)
+            entries[0, j] = (((place // (2 * pairs)) * pairs) ^ swap) + (slot & (pairs - 1))
+            entries[1, j] = (
+                (column // (2 * pairs)) * pairs + (cluster & (pairs - 1))
+            ) * unknowns
+            entries[2, j] = slot // pairs
+            entries[3, j] = ((slot // pairs) ^ (cluster // pairs)) * (width // 2)
+            pltpu.make_async_copy(
+                source.at[list_ref[row, at]], blocks.at[j], block_sem.at[j // batch]
+            ).start()
+            return carry
+
+        return one
+
+    def fill(j, carry):
+        entries[0, j] = dummy
+        entries[1, j] = 0
+        entries[2, j] = 0
+        entries[3, j] = 0
+        pltpu.make_async_copy(own_hbm.at[0], blocks.at[j], block_sem.at[j // batch]).start()
         return carry
 
-    steps = (total + batch - 1) // batch
-    lax.fori_loop(0, steps * batch, fetch, 0)
+    lax.fori_loop(0, here, fetch(own_hbm, 0, begin, 0), 0)
+    lax.fori_loop(here, total, fetch(mate_hbm, 8, begin_there - here, dummy // 2), 0)
+    lax.fori_loop(total, steps * batch, fill, 0)
+    for copy in tails:
+        copy.start()
 
     def clear(i, carry):
         sums[i] = jnp.zeros(sums.shape[1:], sums.dtype)
@@ -235,29 +243,26 @@
     lax.fori_loop(0, dummy, clear, 0)
     for copy in copies:
         copy.wait()
+    lane_half = lax.broadcasted_iota(jnp.int32, (unknowns, width), 1) // (width // 2)
 
     def body(step, carry):
         first = step * batch
-        here_blocks = pl.ds(first, batch)
         pltpu.make_async_copy(
-            own_hbm.at[pl.ds(0, batch)], blocks.at[here_blocks], block_sem.at[step]
+            own_hbm.at[pl.ds(0, batch)], blocks.at[pl.ds(first, batch)], block_sem.at[step]
         ).wait()
         products = []
 
         def add(i):
-            half, row, at = entry(first + i)
-            place = list_ref[row + 1, at] ^ (half * (dummy // 2))
-            place = jnp.where(first + i < total, place, dummy)
-            sums[place] = sums[place] + products[i]
+            product = pltpu.roll(products[i], entries[3, first + i], axis=1)
+            place = entries[0, first + i]
+            sums[place] = sums[place] + jnp.where(lane_half == entries[2, first + i], product, 0.0)
 
         for i in range(batch):
-            half, row, at = entry(first + i)
-            start = pl.multiple_of(list_ref[row + 2, at] * directions, directions)
+            start = pl.multiple_of(entries[1, first + i], unknowns)
             products.append(
-                lax.dot_general(
-                    columns[pl.ds(start, directions)],
+                jnp.dot(
                     blocks[first + i],
-                    (((1,), (1,)), ((), ())),
+                    columns[pl.ds(start, unknowns)],
                     preferred_element_type=jnp.float32,
                 )
             )
@@ -268,28 +273,34 @@
         return carry
 
     lax.fori_loop(0, steps, body, 0)
-
-    def keep(i, carry):
-        keep_ref[i] = sums[i]
-        return carry
-
-    lax.fori_loop(0, dummy // 2, keep, 0, unroll=2)
-    at = dummy // 2
-    for send_ref in send_refs:
-
-        def pack(i, carry, at=at, send_ref=send_ref):
-            send_ref[i] = sums[at + i].astype(send_ref.dtype)
+    at = 0
+    for out_ref in (*keep_refs, *send_refs):
+
+        def pack(i, carry, at=at, out_ref=out_ref):
+            out_ref[i] = sums[at + i].astype(out_ref.dtype)
             return carry
 
-        lax.fori_loop(0, send_ref.shape[0], pack, 0, unroll=2)
-        at += send_ref.shape[0]
+        lax.fori_loop(0, out_ref.shape[0], pack, 0)
+        at += out_ref.shape[0]
     for copy in tails:
         copy.wait()
 
 
+def last_kernel(first_ref, second_ref, rest_ref, out_ref):
+    pairs, unknowns, width = first_ref.shape
+    for p in range(pairs):
+        tile = first_ref[p].astype(jnp.float32) + second_ref[p].astype(jnp.float32)
+        tile = jnp.transpose(tile)
+        for h in range(2):
+            c = h * pairs + p
+            part = tile[h * (width // 2) : (h + 1) * (width // 2)]
+            out_ref[c] = (part + rest_ref[c]).astype(out_ref.dtype)
+
+
 def far_kernel(*refs):
     coef_refs = refs[:2]
-    me_ref, couple_ref, slot_ref, dev_ref, cslot_ref, basis_ref, out_ref = refs[2:]
+    me_ref, couple_ref, slot_ref, dev_ref, cslot_ref, basis_ref = refs[2:8]
+    own_ref, mate_ref, out_ref = refs[8:]
     clusters, rank_k, unknowns = basis_ref.shape
     pairs = couple_ref.shape[2]
     directions = out_ref.shape[1]
@@ -331,9 +342,14 @@
     gathered = jnp.transpose(total)[0:directions, :].astype(jnp.bfloat16).astype(jnp.float32)
     lane = lax.broadcasted_iota(jnp.int32, gathered.shape, 1) // rank_k
     basis = basis_ref[...].reshape(clusters * rank_k, unknowns)
-    for s in range(clusters):
-        own = jnp.where(lane == s, gathered, 0.0).astype(jnp.bfloat16)
-        out_ref[s] = jnp.dot(own, basis, preferred_element_type=jnp.float32)
+    for p in range(half):
+        near = jnp.transpose(own_ref[p] + mate_ref[p].astype(jnp.float32))
+        for h in range(2):
+            s = h * half + p
+            own = jnp.where(lane == s, gathered, 0.0).astype(jnp.bfloat16)
+            out_ref[s] = near[h * directions : (h + 1) * directions] + jnp.dot(
+                own, basis, preferred_element_type=jnp.float32
+            )
 
 
 def ring_device(place, core, chips):
@@ -454,23 +470,26 @@
     quarter = chips // 2
 
     def near(late, lists):
-        pieces = [1] * quarter
-        kept, *sends = pl.pallas_call(
-            functools.partial(near_kernel, late, BATCH, LAG, chips, len(pieces)),
+        keeps = [quarter - 1, 1] if late else [quarter]
+        sends = [1] * quarter
+        outs = pl.pallas_call(
+            functools.partial(near_kernel, late, BATCH, LAG, chips, len(keeps), len(sends)),
             out_shape=[
-                jax.ShapeDtypeStruct((quarter * clusters, directions, unknowns), jnp.float32)
+                jax.ShapeDtypeStruct((part * half, unknowns, 2 * directions), jnp.float32)
+                for part in keeps
             ]
             + [
-                jax.ShapeDtypeStruct((part * clusters, directions, unknowns), jnp.bfloat16)
-                for part in pieces
+                jax.ShapeDtypeStruct((part * half, unknowns, 2 * directions), jnp.bfloat16)
+                for part in sends
             ]
             + [jax.ShapeDtypeStruct((chips * half * rank_k, unknowns), jnp.bfloat16)] * (1 - late),
             in_specs=[whole(pltpu.SMEM)] + [whole(pl.ANY)] * (chips + 2),
-            out_specs=[whole()] * (2 + len(pieces) - late),
+            out_specs=[whole()] * (len(keeps) + len(sends) + 1 - late),
             scratch_shapes=[
                 pltpu.VMEM((chips * base, unknowns), jnp.bfloat16),
                 pltpu.VMEM((2 * stored, unknowns, unknowns), jnp.bfloat16),
-                pltpu.VMEM((2 * quarter * clusters + 1, directions, unknowns), jnp.float32),
+                pltpu.VMEM((2 * quarter * half + 1, unknowns, 2 * directions), jnp.float32),
+                pltpu.SMEM((4, 2 * stored), jnp.int32),
                 pltpu.SemaphoreType.DMA((chips,)),
                 pltpu.SemaphoreType.DMA((chips,)),
                 pltpu.SemaphoreType.DMA((2 * stored // BATCH,)),
@@ -483,13 +502,13 @@
             ),
             name="near",
         )(lists, *shards, near_blocks, mate_blocks)
-        return kept, sends
-
-    def far_field(couple):
+        return outs[: len(keeps)], outs[len(keeps) :]
+
+    def far_field(couple, own, got):
         return pl.pallas_call(
             far_kernel,
             out_shape=jax.ShapeDtypeStruct((clusters, directions, unknowns), jnp.float32),
-            in_specs=[whole()] * 2 + [whole(pltpu.SMEM)] + [whole()] * 5,
+            in_specs=[whole()] * 2 + [whole(pltpu.SMEM)] + [whole()] * 7,
             out_specs=whole(),
             compiler_params=pltpu.CompilerParams(vmem_limit_bytes=FAR_VMEM),
             cost_estimate=pl.CostEstimate(
@@ -506,16 +525,17 @@
             far_dev.reshape(1, pairs),
             far_cslot.reshape(1, pairs),
             basis_out,
+            own,
+            got,
         )
 
-    early, (*sends, coef) = near(0, lists)
+    kept, (*sends, coef) = near(0, lists)
     mates = [move(sends[0], mate), move(sends[1], mate)]
     coefs = [coef, move(coef, mate)]
-    kept = [early]
 
     def term(k):
-        at = k % quarter * clusters
-        return kept[k // quarter][at : at + clusters] + mates[k].astype(jnp.float32)
+        at = k % quarter * half
+        return kept[k // quarter][at : at + half] + mates[k].astype(jnp.float32)
 
     def tied(values, k, *others):
         values, mates[k + 1], *others = lax.optimization_barrier((values, mates[k + 1], *others))
@@ -529,7 +549,7 @@
     mates += [move(after(send, *flow), mate) for send in sends[2:]]
     flow = [move(part, ahead) for part in flow]
     late, sends = near(1, lists)
-    kept.append(late)
+    kept += late
     mates += [move(send, mate) for send in sends]
     for k in range(2, chips - 1):
         x = k % 2
@@ -538,9 +558,14 @@
             couple = after(couple, flow[x])
         flow[x] = move(flow[x], ahead)
     flow[1] = move(flow[1], mate)
-    total = far_field(couple) + term(chips - 1) + flow[0].astype(jnp.float32)
-    total = lax.optimization_barrier(total)
-    return (total + flow[1].astype(jnp.float32)).astype(jnp.bfloat16)
+    rest = far_field(couple, kept[-1], mates[-1])
+    return pl.pallas_call(
+        last_kernel,
+        out_shape=jax.ShapeDtypeStruct(rhs.shape, jnp.bfloat16),
+        in_specs=[whole()] * 3,
+        out_specs=whole(),
+        name="last",
+    )(*flow, rest)
 
 
 def on_device(*args):

time: 71.6 us -> 77.7 us (1.085); the launches traced: 72.3 us -> 76.2 us
  waiting for transfers between devices: 24 us -> 20.3 us
  starting transfers between devices: 28.6 us -> 31.9 us
  Pallas kernels: 16.3 us -> 19.4 us
  local copies, waits for them, and re-layouts: 0.97 us -> 3.14 us
  other arithmetic: 2.26 us -> 1.29 us
    ppermute x27, waiting for transfers between devices: 24 us -> 20.3 us  [move(): return lax.ppermute(values, 'blk', where)]
    ppermute x27, starting transfers between devices: 28.6 us -> 31.9 us  [move(): return lax.ppermute(values, 'blk', where)]
    unnamed x9 -> x15, local copies, waits for them, and re-layouts: 0.97 us -> 3.14 us
    pallas_call x0 -> x1, Pallas kernels: none -> 2.11 us  [stationary(): pl.pallas_call(last_kernel, out_shape=jax.ShapeDtypeStruct(rhs.shape, jnp...]
    pallas_call x2, Pallas kernels: 11.8 us -> 12.7 us  [near(): pl.pallas_call(functools.partial(near_kernel, late, BATCH, LAG, chips, le...]
    convert_element_type x1 -> x0, other arithmetic: 0.78 us -> none  [stationary(): return (total + flow[1].astype(jnp.float32)).astype(jnp.bfloat16)]
where the time goes in v13:
time: 77.7 us; the launch traced here: 76.2 us
  starting transfers between devices  31.9 us (41%)
  waiting for transfers between devices  20.3 us (26%)
  Pallas kernels  19.4 us (25%)
  local copies, waits for them, and re-layouts  3.14 us (4%)
  other arithmetic  1.29 us (2%)
    ppermute x27, starting transfers between devices, move(): return lax.ppermute(values, 'blk', where)  31.9 us
    ppermute x27, waiting for transfers between devices, move(): return lax.ppermute(values, 'blk', where)  20.3 us
    pallas_call x2, Pallas kernels, near(): pl.pallas_call(functools.partial(near_kernel, late, BATCH, LAG, chips, le...  12.7 us
    unnamed x15, local copies, waits for them, and re-layouts  3.14 us
    pallas_call x1, Pallas kernels, far_field(): pl.pallas_call(far_kernel, out_shape=jax.ShapeDtypeStruct((clusters, dire...  2.56 us
    pallas_call x1, Pallas kernels, stationary(): pl.pallas_call(last_kernel, out_shape=jax.ShapeDtypeStruct(rhs.shape, jnp...  2.11 us
    pallas_call x1, Pallas kernels, stationary(): pl.pallas_call(functools.partial(prologue_kernel, count), out_shape=[jax....  2.05 us
  transfers between devices with their start and end apart: 27, of which 14 were waited for; matrix products, arithmetic and copies ran while one was open for 3% of the time, Pallas kernels for 15%

profile of v13, /device:TPU:0, one launch (start us, length us, event | category | flops | bytes accessed | tf_op | source)
XLA Modules:
  0.0 76.2 jit_solution(7176419584886071140)
XLA Ops:
  0.5 2.0 %prologue.1 = (bf16[1152,128]{1,0:T(8,128)(2,1)}, s32[8,128]{1,0:T(8,128)}) custom-call(s32[1]{0:T(128)} %bitcast.me_ref.refs_2_, s32[1,128]{1,0:T(1,128)} %bitcast.14, s32[1,128]{1,0:T(1,128)} %bitcast.15, s32[1,128]{1,0:T(1,128)} %bitcast.16, bf16[16,64,128]{2,1,0:T(8,128)(2,1)} %rhs_ref.1, bf16[16,16,128]{2,1,0:T(8,128)(2,1)} %basis_ref.1), custom_call_target="tpu_custom_call" | custom-call | tf_op jit(solution)/shard_map/prologue/pallas_call | solution.py:436
  2.5 2.6 %collective-permute-start = (bf16[1152,128]{1,0:T(8,128)(2,1)}, bf16[1152,128]{1,0:T(8,128)(2,1)S(1)}, u32[]{:S(2)}, u32[]{:S(2)}) collective-permute-start(bf16[1152,128]{1,0:T(8,128)(2,1)} %get-tuple-element.44), channel_id=1, source_target_pairs={{0,4},{1,3},{4,8},{5,1},{8,12},{9,5},{12,14},{13,9},{14,10},{15,13... | collective-permute-start | bytes 884744 | tf_op jit(solution)/shard_map/ppermute | solution.py:429
  5.1 0.9 %copy.14 = bf16[256,16,16]{0,1,2:T(8,128)(2,1)S(1)} copy(bf16[256,16,16]{0,2,1:T(8,128)(2,1)} %param.16) | data formatting | bytes 262144 | tf_op args[5]
  6.0 1.4 %collective-permute-start.5 = (bf16[1152,128]{1,0:T(8,128)(2,1)}, bf16[1152,128]{1,0:T(8,128)(2,1)S(1)}, u32[]{:S(2)}, u32[]{:S(2)}) collective-permute-start(bf16[1152,128]{1,0:T(8,128)(2,1)} %get-tuple-element.44), channel_id=1, source_target_pairs={{0,3},{1,4},{4,1},{5,8},{8,5},{9,12},{12,9},{13,14},{14,13},{15,10... | collective-permute-start | bytes 884744 | tf_op jit(solution)/shard_map/ppermute | solution.py:429
  7.8 2.9 %collective-permute-done.refs_1_ = bf16[1152,128]{1,0:T(8,128)(2,1)S(1)} collective-permute-done((bf16[1152,128]{1,0:T(8,128)(2,1)}, bf16[1152,128]{1,0:T(8,128)(2,1)S(1)}, u32[]{:S(2)}, u32[]{:S(2)}) %collective-permute-start) | collective-permute-done | bytes 294944 | tf_op jit(solution)/shard_map/ppermute | solution.py:429
  10.7 2.4 %collective-permute-start.1 = (bf16[1152,128]{1,0:T(8,128)(2,1)S(1)}, bf16[1152,128]{1,0:T(8,128)(2,1)S(1)}, u32[]{:S(2)}, u32[]{:S(2)}) collective-permute-start(bf16[1152,128]{1,0:T(8,128)(2,1)S(1)} %collective-permute-done.refs_1_), channel_id=1, source_target_pairs={{0,4},{1,3},{4,8},{5,1},{8,12},{9,5},{12,14},{13,9},{14,10},{15,13... | collective-permute-start | bytes 884744 | tf_op jit(solution)/shard_map/ppermute | solution.py:429
  13.1 1.4 %collective-permute-done.4 = s32[8,128]{1,0:T(8,128)S(1)} collective-permute-done((s32[8,128]{1,0:T(8,128)}, s32[8,128]{1,0:T(8,128)S(1)}, u32[]{:S(2)}, u32[]{:S(2)}) %collective-permute-start.4) | collective-permute-done | bytes 4128 | tf_op jit(solution)/shard_map/ppermute | solution.py:429
  15.2 1.6 %collective-permute-start.6 = (bf16[1152,128]{1,0:T(8,128)(2,1)S(1)}, bf16[1152,128]{1,0:T(8,128)(2,1)S(1)}, u32[]{:S(2)}, u32[]{:S(2)}) collective-permute-start(bf16[1152,128]{1,0:T(8,128)(2,1)S(1)} %collective-permute-done.5.refs_2_), channel_id=1, source_target_pairs={{0,4},{1,3},{4,8},{5,1},{8,12},{9,5},{12,14},{13,9},{14,10},{15,13... | collective-permute-start | bytes 884744 | tf_op jit(solution)/shard_map/ppermute | solution.py:429
  16.7 1.3 %collective-permute-done.1.refs_3_ = bf16[1152,128]{1,0:T(8,128)(2,1)S(1)} collective-permute-done((bf16[1152,128]{1,0:T(8,128)(2,1)S(1)}, bf16[1152,128]{1,0:T(8,128)(2,1)S(1)}, u32[]{:S(2)}, u32[]{:S(2)}) %collective-permute-start.1) | collective-permute-done | bytes 294944 | tf_op jit(solution)/shard_map/ppermute | solution.py:429
  18.1 1.7 %collective-permute-start.7 = (bf16[1152,128]{1,0:T(8,128)(2,1)S(1)}, bf16[1152,128]{1,0:T(8,128)(2,1)S(1)}, u32[]{:S(2)}, u32[]{:S(2)}) collective-permute-start(bf16[1152,128]{1,0:T(8,128)(2,1)S(1)} %collective-permute-done.1.refs_3_), channel_id=1, source_target_pairs={{0,4},{1,3},{4,8},{5,1},{8,12},{9,5},{12,14},{13,9},{14,10},{15,13... | collective-permute-start | bytes 884744 | tf_op jit(solution)/shard_map/ppermute | solution.py:429
  19.8 2.1 %collective-permute-done.6.refs_4_ = bf16[1152,128]{1,0:T(8,128)(2,1)S(1)} collective-permute-done((bf16[1152,128]{1,0:T(8,128)(2,1)S(1)}, bf16[1152,128]{1,0:T(8,128)(2,1)S(1)}, u32[]{:S(2)}, u32[]{:S(2)}) %collective-permute-start.6) | collective-permute-done | bytes 294944 | tf_op jit(solution)/shard_map/ppermute | solution.py:429
  21.9 1.6 %collective-permute-start.8 = (bf16[1152,128]{1,0:T(8,128)(2,1)S(1)}, bf16[1152,128]{1,0:T(8,128)(2,1)S(1)}, u32[]{:S(2)}, u32[]{:S(2)}) collective-permute-start(bf16[1152,128]{1,0:T(8,128)(2,1)S(1)} %collective-permute-done.6.refs_4_), channel_id=1, source_target_pairs={{0,4},{1,3},{4,8},{5,1},{8,12},{9,5},{12,14},{13,9},{14,10},{15,13... | collective-permute-start | bytes 884744 | tf_op jit(solution)/shard_map/ppermute | solution.py:429
  23.5 1.6 %collective-permute-done.7.refs_5_ = bf16[1152,128]{1,0:T(8,128)(2,1)S(1)} collective-permute-done((bf16[1152,128]{1,0:T(8,128)(2,1)S(1)}, bf16[1152,128]{1,0:T(8,128)(2,1)S(1)}, u32[]{:S(2)}, u32[]{:S(2)}) %collective-permute-start.7) | collective-permute-done | bytes 294944 | tf_op jit(solution)/shard_map/ppermute | solution.py:429
  25.0 1.6 %collective-permute-start.9 = (bf16[1152,128]{1,0:T(8,128)(2,1)S(1)}, bf16[1152,128]{1,0:T(8,128)(2,1)S(1)}, u32[]{:S(2)}, u32[]{:S(2)}) collective-permute-start(bf16[1152,128]{1,0:T(8,128)(2,1)S(1)} %collective-permute-done.7.refs_5_), channel_id=1, source_target_pairs={{0,4},{1,3},{4,8},{5,1},{8,12},{9,5},{12,14},{13,9},{14,10},{15,13... | collective-permute-start | bytes 884744 | tf_op jit(solution)/shard_map/ppermute | solution.py:429
  26.6 2.0 %collective-permute-done.8.refs_6_ = bf16[1152,128]{1,0:T(8,128)(2,1)S(1)} collective-permute-done((bf16[1152,128]{1,0:T(8,128)(2,1)S(1)}, bf16[1152,128]{1,0:T(8,128)(2,1)S(1)}, u32[]{:S(2)}, u32[]{:S(2)}) %collective-permute-start.8) | collective-permute-done | bytes 294944 | tf_op jit(solution)/shard_map/ppermute | solution.py:429
  28.6 3.2 %collective-permute-done.9.refs_7_ = bf16[1152,128]{1,0:T(8,128)(2,1)S(1)} collective-permute-done((bf16[1152,128]{1,0:T(8,128)(2,1)S(1)}, bf16[1152,128]{1,0:T(8,128)(2,1)S(1)}, u32[]{:S(2)}, u32[]{:S(2)}) %collective-permute-start.9) | collective-permute-done | bytes 294944 | tf_op jit(solution)/shard_map/ppermute | solution.py:429
  31.8 5.6 %near.2 = (f32[32,128,128]{2,1,0:T(8,128)S(1)}, bf16[8,128,128]{2,1,0:T(8,128)(2,1)S(1)}, bf16[8,128,128]{2,1,0:T(8,128)(2,1)S(1)}, bf16[8,128,128]{2,1,0:T(8,12...) custom-call(s32[16,128]{1,0:T(8,128)S(1)} %pad_add_fusion.list_ref, ...), custom_call_target="tpu_custom_call" | custom-call | flops 2147483648 | bytes 16777216 | tf_op jit(solution)/shard_map/near/pallas_call | solution.py:475
  37.3 0.9 %collective-permute-start.11 = (bf16[8,128,128]{2,1,0:T(8,128)(2,1)S(1)}, bf16[8,128,128]{2,1,0:T(8,128)(2,1)S(1)}, u32[]{:S(2)}, u32[]{:S(2)}) collective-permute-start(bf16[8,128,128]{2,1,0:T(8,128)(2,1)S(1)} %get-tuple-element.49), channel_id=1, source_target_pairs={{0,1},{1,0},{2,3},{3,2},{4,5},{5,4},{6,7},{7,6},{8,9},{9,8},{10,11... | collective-permute-start | bytes 786440 | tf_op jit(solution)/shard_map/ppermute | solution.py:429
  38.3 1.1 %collective-permute-done.11 = bf16[8,128,128]{2,1,0:T(8,128)(2,1)S(1)} collective-permute-done((bf16[8,128,128]{2,1,0:T(8,128)(2,1)S(1)}, bf16[8,128,128]{2,1,0:T(8,128)(2,1)S(1)}, u32[]{:S(2)}, u32[]{:S(2)}) %collective-permute-start.11) | collective-permute-done | bytes 262176 | tf_op jit(solution)/shard_map/ppermute | solution.py:429
  40.3 2.0 %collective-permute-start.12 = (bf16[8,128,128]{2,1,0:T(8,128)(2,1)S(1)}, bf16[8,128,128]{2,1,0:T(8,128)(2,1)S(1)}, u32[]{:S(2)}, u32[]{:S(2)}) collective-permute-start(bf16[8,128,128]{2,1,0:T(8,128)(2,1)S(1)} %get-tuple-element.50), channel_id=1, source_target_pairs={{0,4},{1,3},{4,8},{5,1},{8,12},{9,5},{12,14},{13,9},{14,10},{15,13... | collective-permute-start | bytes 786440 | tf_op jit(solution)/shard_map/ppermute | solution.py:429
  42.3 3.0 %collective-permute-start.16 = (bf16[8,128,128]{2,1,0:T(8,128)(2,1)S(1)}, bf16[8,128,128]{2,1,0:T(8,128)(2,1)S(1)}, u32[]{:S(2)}, u32[]{:S(2)}) collective-permute-start(bf16[8,128,128]{2,1,0:T(8,128)(2,1)S(1)} %get-tuple-element.52), channel_id=1, source_target_pairs={{0,4},{1,3},{4,8},{5,1},{8,12},{9,5},{12,14},{13,9},{14,10},{15,13... | collective-permute-start | bytes 786440 | tf_op jit(solution)/shard_map/ppermute | solution.py:429
  45.3 7.1 %near.3 = (f32[24,128,128]{2,1,0:T(8,128)S(1)}, f32[8,128,128]{2,1,0:T(8,128)S(1)}, bf16[8,128,128]{2,1,0:T(8,128)(2,1)S(1)}, bf16[8,128,128]{2,1,0:T(8,128)(2,1...) custom-call(s32[16,128]{1,0:T(8,128)S(1)} %pad_add_fusion.list_ref, ...), custom_call_target="tpu_custom_call" | custom-call | flops 2147483648 | bytes 16777216 | tf_op jit(solution)/shard_map/near/pallas_call | solution.py:475
  53.2 2.2 %collective-permute-start.15 = (bf16[8,128,128]{2,1,0:T(8,128)(2,1)S(1)}, bf16[8,128,128]{2,1,0:T(8,128)(2,1)S(1)}, u32[]{:S(2)}, u32[]{:S(2)}) collective-permute-start(bf16[8,128,128]{2,1,0:T(8,128)(2,1)S(1)} %add_convert_fusion.4), channel_id=1, source_target_pairs={{0,4},{1,3},{4,8},{5,1},{8,12},{9,5},{12,14},{13,9},{14,10},{15,13... | collective-permute-start | bytes 786440 | tf_op jit(solution)/shard_map/ppermute | solution.py:429
  55.6 1.7 %collective-permute-start.20 = (bf16[8,128,128]{2,1,0:T(8,128)(2,1)S(1)}, bf16[8,128,128]{2,1,0:T(8,128)(2,1)S(1)}, u32[]{:S(2)}, u32[]{:S(2)}) collective-permute-start(bf16[8,128,128]{2,1,0:T(8,128)(2,1)S(1)} %add_convert_fusion.3), channel_id=1, source_target_pairs={{0,4},{1,3},{4,8},{5,1},{8,12},{9,5},{12,14},{13,9},{14,10},{15,13... | collective-permute-start | bytes 786440 | tf_op jit(solution)/shard_map/ppermute | solution.py:429
  57.8 1.8 %collective-permute-done.15 = bf16[8,128,128]{2,1,0:T(8,128)(2,1)S(1)} collective-permute-done((bf16[8,128,128]{2,1,0:T(8,128)(2,1)S(1)}, bf16[8,128,128]{2,1,0:T(8,128)(2,1)S(1)}, u32[]{:S(2)}, u32[]{:S(2)}) %collective-permute-start.15) | collective-permute-done | bytes 262176 | tf_op jit(solution)/shard_map/ppermute | solution.py:429
  59.8 2.2 %collective-permute-start.19 = (bf16[8,128,128]{2,1,0:T(8,128)(2,1)S(1)}, bf16[8,128,128]{2,1,0:T(8,128)(2,1)S(1)}, u32[]{:S(2)}, u32[]{:S(2)}) collective-permute-start(bf16[8,128,128]{2,1,0:T(8,128)(2,1)S(1)} %add_convert_fusion.2), channel_id=1, source_target_pairs={{0,4},{1,3},{4,8},{5,1},{8,12},{9,5},{12,14},{13,9},{14,10},{15,13... | collective-permute-start | bytes 786440 | tf_op jit(solution)/shard_map/ppermute | solution.py:429
  62.6 2.2 %collective-permute-start.24 = (bf16[8,128,128]{2,1,0:T(8,128)(2,1)S(1)}, bf16[8,128,128]{2,1,0:T(8,128)(2,1)S(1)}, u32[]{:S(2)}, u32[]{:S(2)}) collective-permute-start(bf16[8,128,128]{2,1,0:T(8,128)(2,1)S(1)} %add_convert_fusion.1), channel_id=1, source_target_pairs={{0,4},{1,3},{4,8},{5,1},{8,12},{9,5},{12,14},{13,9},{14,10},{15,13... | collective-permute-start | bytes 786440 | tf_op jit(solution)/shard_map/ppermute | solution.py:429
  64.8 1.4 %collective-permute-done.19 = bf16[8,128,128]{2,1,0:T(8,128)(2,1)S(1)} collective-permute-done((bf16[8,128,128]{2,1,0:T(8,128)(2,1)S(1)}, bf16[8,128,128]{2,1,0:T(8,128)(2,1)S(1)}, u32[]{:S(2)}, u32[]{:S(2)}) %collective-permute-start.19) | collective-permute-done | bytes 262176 | tf_op jit(solution)/shard_map/ppermute | solution.py:429
  66.3 2.2 %collective-permute-start.23 = (bf16[8,128,128]{2,1,0:T(8,128)(2,1)S(1)}, bf16[8,128,128]{2,1,0:T(8,128)(2,1)S(1)}, u32[]{:S(2)}, u32[]{:S(2)}) collective-permute-start(bf16[8,128,128]{2,1,0:T(8,128)(2,1)S(1)} %add_convert_fusion), channel_id=1, source_target_pairs={{0,4},{1,3},{4,8},{5,1},{8,12},{9,5},{12,14},{13,9},{14,10},{15,13... | collective-permute-start | bytes 786440 | tf_op jit(solution)/shard_map/ppermute | solution.py:429
  69.0 2.6 %far.1.rest_ref = f32[16,64,128]{2,1,0:T(8,128)S(1)} custom-call(bf16[1024,128]{1,0:T(8,128)(2,1)S(1)} %get-tuple-element.71.refs_0_, bf16[1024,128]{1,0:T(8,128)(2,1)S(1)} %collective-permute-done.26.refs_1_, s32[1]{0:T(128)} %bitcast.me_ref.refs_2_, bf16[16,16,256]{2,1,0:T(8,128)(2,1)S(1)} %bitcast.10, s32[1,256]{1,0:T(1,128)S(1)} %bitcast.11, ...), custom_call_target="tpu_custom_call" | custom-call | flops 536870912 | bytes 8388608 | tf_op jit(solution)/shard_map/far/pallas_call | solution.py:508
  71.6 0.8 %copy-done = f32[16,64,128]{2,1,0:T(8,128)} copy-done((f32[16,64,128]{2,1,0:T(8,128)}, f32[16,64,128]{2,1,0:T(8,128)S(1)}, u32[]{:S(2)}) %copy-start) | copy-done | bytes 524312
  74.1 2.1 %last.1 = bf16[16,64,128]{2,1,0:T(8,128)(2,1)} custom-call(bf16[8,128,128]{2,1,0:T(8,128)(2,1)} %copy-done.5, bf16[8,128,128]{2,1,0:T(8,128)(2,1)} %copy-done.6, f32[16,64,128]{2,1,0:T(8,128)} %copy-done), custom_call_target="tpu_custom_call" | custom-call | tf_op jit(solution)/shard_map/last/pallas_call | solution.py:562
  (49 shorter events, 6.9 us)
Async XLA Ops:
  0.0 18.1 %collective-permute-start.2 = (bf16[128,128,128]{2,1,0:T(8,128)(2,1)}, bf16[128,128,128]{2,1,0:T(8,128)(2,1)}, u32[]{:S(2)}, u32[]{:S(2)}) collective-permute-start(bf16[128,128,128]{2,1,0:T(8,128)(2,1)} %refs_8_.3), channel_id=1, source_target_pairs={{0,1},{1,0},{2,3},{3,2},{4,5},{5,4},{6,7},{7,6},{8,9},{9,8},{10,11... | collective-permute-start | bytes 12582920 | tf_op jit(solution)/shard_map/ppermute | solution.py:429
  2.5 8.2 %collective-permute-start = (bf16[1152,128]{1,0:T(8,128)(2,1)}, bf16[1152,128]{1,0:T(8,128)(2,1)S(1)}, u32[]{:S(2)}, u32[]{:S(2)}) collective-permute-start(bf16[1152,128]{1,0:T(8,128)(2,1)} %get-tuple-element.44), channel_id=1, source_target_pairs={{0,4},{1,3},{4,8},{5,1},{8,12},{9,5},{12,14},{13,9},{14,10},{15,13... | collective-permute-start | bytes 884744 | tf_op jit(solution)/shard_map/ppermute | solution.py:429
  6.0 9.1 %collective-permute-start.5 = (bf16[1152,128]{1,0:T(8,128)(2,1)}, bf16[1152,128]{1,0:T(8,128)(2,1)S(1)}, u32[]{:S(2)}, u32[]{:S(2)}) collective-permute-start(bf16[1152,128]{1,0:T(8,128)(2,1)} %get-tuple-element.44), channel_id=1, source_target_pairs={{0,3},{1,4},{4,1},{5,8},{8,5},{9,12},{12,9},{13,14},{14,13},{15,10... | collective-permute-start | bytes 884744 | tf_op jit(solution)/shard_map/ppermute | solution.py:429
  7.4 9.3 %collective-permute-start.3 = (bf16[1152,128]{1,0:T(8,128)(2,1)}, bf16[1152,128]{1,0:T(8,128)(2,1)S(1)}, u32[]{:S(2)}, u32[]{:S(2)}) collective-permute-start(bf16[1152,128]{1,0:T(8,128)(2,1)} %get-tuple-element.44), channel_id=1, source_target_pairs={{0,1},{1,0},{2,3},{3,2},{4,5},{5,4},{6,7},{7,6},{8,9},{9,8},{10,11... | collective-permute-start | bytes 884744 | tf_op jit(solution)/shard_map/ppermute | solution.py:429
  10.7 7.4 %collective-permute-start.1 = (bf16[1152,128]{1,0:T(8,128)(2,1)S(1)}, bf16[1152,128]{1,0:T(8,128)(2,1)S(1)}, u32[]{:S(2)}, u32[]{:S(2)}) collective-permute-start(bf16[1152,128]{1,0:T(8,128)(2,1)S(1)} %collective-permute-done.refs_1_), channel_id=1, source_target_pairs={{0,4},{1,3},{4,8},{5,1},{8,12},{9,5},{12,14},{13,9},{14,10},{15,13... | collective-permute-start | bytes 884744 | tf_op jit(solution)/shard_map/ppermute | solution.py:429
  13.1 1.4 %collective-permute-start.4 = (s32[8,128]{1,0:T(8,128)}, s32[8,128]{1,0:T(8,128)S(1)}, u32[]{:S(2)}, u32[]{:S(2)}) collective-permute-start(s32[8,128]{1,0:T(8,128)} %get-tuple-element.41), channel_id=1, source_target_pairs={{0,1},{1,0},{2,3},{3,2},{4,5},{5,4},{6,7},{7,6},{8,9},{9,8},{10,11... | collective-permute-start | bytes 12296 | tf_op jit(solution)/shard_map/ppermute | solution.py:429
  15.2 6.7 %collective-permute-start.6 = (bf16[1152,128]{1,0:T(8,128)(2,1)S(1)}, bf16[1152,128]{1,0:T(8,128)(2,1)S(1)}, u32[]{:S(2)}, u32[]{:S(2)}) collective-permute-start(bf16[1152,128]{1,0:T(8,128)(2,1)S(1)} %collective-permute-done.5.refs_2_), channel_id=1, source_target_pairs={{0,4},{1,3},{4,8},{5,1},{8,12},{9,5},{12,14},{13,9},{14,10},{15,13... | collective-permute-start | bytes 884744 | tf_op jit(solution)/shard_map/ppermute | solution.py:429
  18.1 7.0 %collective-permute-start.7 = (bf16[1152,128]{1,0:T(8,128)(2,1)S(1)}, bf16[1152,128]{1,0:T(8,128)(2,1)S(1)}, u32[]{:S(2)}, u32[]{:S(2)}) collective-permute-start(bf16[1152,128]{1,0:T(8,128)(2,1)S(1)} %collective-permute-done.1.refs_3_), channel_id=1, source_target_pairs={{0,4},{1,3},{4,8},{5,1},{8,12},{9,5},{12,14},{13,9},{14,10},{15,13... | collective-permute-start | bytes 884744 | tf_op jit(solution)/shard_map/ppermute | solution.py:429
  21.9 6.7 %collective-permute-start.8 = (bf16[1152,128]{1,0:T(8,128)(2,1)S(1)}, bf16[1152,128]{1,0:T(8,128)(2,1)S(1)}, u32[]{:S(2)}, u32[]{:S(2)}) collective-permute-start(bf16[1152,128]{1,0:T(8,128)(2,1)S(1)} %collective-permute-done.6.refs_4_), channel_id=1, source_target_pairs={{0,4},{1,3},{4,8},{5,1},{8,12},{9,5},{12,14},{13,9},{14,10},{15,13... | collective-permute-start | bytes 884744 | tf_op jit(solution)/shard_map/ppermute | solution.py:429
  25.0 6.7 %collective-permute-start.9 = (bf16[1152,128]{1,0:T(8,128)(2,1)S(1)}, bf16[1152,128]{1,0:T(8,128)(2,1)S(1)}, u32[]{:S(2)}, u32[]{:S(2)}) collective-permute-start(bf16[1152,128]{1,0:T(8,128)(2,1)S(1)} %collective-permute-done.7.refs_5_), channel_id=1, source_target_pairs={{0,4},{1,3},{4,8},{5,1},{8,12},{9,5},{12,14},{13,9},{14,10},{15,13... | collective-permute-start | bytes 884744 | tf_op jit(solution)/shard_map/ppermute | solution.py:429
  37.3 2.0 %collective-permute-start.11 = (bf16[8,128,128]{2,1,0:T(8,128)(2,1)S(1)}, bf16[8,128,128]{2,1,0:T(8,128)(2,1)S(1)}, u32[]{:S(2)}, u32[]{:S(2)}) collective-permute-start(bf16[8,128,128]{2,1,0:T(8,128)(2,1)S(1)} %get-tuple-element.49), channel_id=1, source_target_pairs={{0,1},{1,0},{2,3},{3,2},{4,5},{5,4},{6,7},{7,6},{8,9},{9,8},{10,11... | collective-permute-start | bytes 786440 | tf_op jit(solution)/shard_map/ppermute | solution.py:429
  38.2 1.5 %collective-permute-start.10 = (bf16[8,128,128]{2,1,0:T(8,128)(2,1)S(1)}, bf16[8,128,128]{2,1,0:T(8,128)(2,1)S(1)}, u32[]{:S(2)}, u32[]{:S(2)}) collective-permute-start(bf16[8,128,128]{2,1,0:T(8,128)(2,1)S(1)} %get-tuple-element.48), channel_id=1, source_target_pairs={{0,1},{1,0},{2,3},{3,2},{4,5},{5,4},{6,7},{7,6},{8,9},{9,8},{10,11... | collective-permute-start | bytes 786440 | tf_op jit(solution)/shard_map/ppermute | solution.py:429
  39.9 13.2 %collective-permute-start.13 = (bf16[8,128,128]{2,1,0:T(8,128)(2,1)S(1)}, bf16[8,128,128]{2,1,0:T(8,128)(2,1)S(1)}, u32[]{:S(2)}, u32[]{:S(2)}) collective-permute-start(bf16[8,128,128]{2,1,0:T(8,128)(2,1)S(1)} %get-tuple-element.53), channel_id=1, source_target_pairs={{0,1},{1,0},{2,3},{3,2},{4,5},{5,4},{6,7},{7,6},{8,9},{9,8},{10,11... | collective-permute-start | bytes 786440 | tf_op jit(solution)/shard_map/ppermute | solution.py:429
  40.3 12.8 %collective-permute-start.12 = (bf16[8,128,128]{2,1,0:T(8,128)(2,1)S(1)}, bf16[8,128,128]{2,1,0:T(8,128)(2,1)S(1)}, u32[]{:S(2)}, u32[]{:S(2)}) collective-permute-start(bf16[8,128,128]{2,1,0:T(8,128)(2,1)S(1)} %get-tuple-element.50), channel_id=1, source_target_pairs={{0,4},{1,3},{4,8},{5,1},{8,12},{9,5},{12,14},{13,9},{14,10},{15,13... | collective-permute-start | bytes 786440 | tf_op jit(solution)/shard_map/ppermute | solution.py:429
  42.3 13.2 %collective-permute-start.16 = (bf16[8,128,128]{2,1,0:T(8,128)(2,1)S(1)}, bf16[8,128,128]{2,1,0:T(8,128)(2,1)S(1)}, u32[]{:S(2)}, u32[]{:S(2)}) collective-permute-start(bf16[8,128,128]{2,1,0:T(8,128)(2,1)S(1)} %get-tuple-element.52), channel_id=1, source_target_pairs={{0,4},{1,3},{4,8},{5,1},{8,12},{9,5},{12,14},{13,9},{14,10},{15,13... | collective-permute-start | bytes 786440 | tf_op jit(solution)/shard_map/ppermute | solution.py:429
  45.3 7.9 %collective-permute-start.14 = (bf16[8,128,128]{2,1,0:T(8,128)(2,1)S(1)}, bf16[8,128,128]{2,1,0:T(8,128)(2,1)S(1)}, u32[]{:S(2)}, u32[]{:S(2)}) collective-permute-start(bf16[8,128,128]{2,1,0:T(8,128)(2,1)S(1)} %get-tuple-element.55), channel_id=1, source_target_pairs={{0,1},{1,0},{2,3},{3,2},{4,5},{5,4},{6,7},{7,6},{8,9},{9,8},{10,11... | collective-permute-start | bytes 786440 | tf_op jit(solution)/shard_map/ppermute | solution.py:429
  52.4 3.2 %collective-permute-start.17 = (bf16[8,128,128]{2,1,0:T(8,128)(2,1)S(1)}, bf16[8,128,128]{2,1,0:T(8,128)(2,1)S(1)}, u32[]{:S(2)}, u32[]{:S(2)}) collective-permute-start(bf16[8,128,128]{2,1,0:T(8,128)(2,1)S(1)} %get-tuple-element.60), channel_id=1, source_target_pairs={{0,1},{1,0},{2,3},{3,2},{4,5},{5,4},{6,7},{7,6},{8,9},{9,8},{10,11... | collective-permute-start | bytes 786440 | tf_op jit(solution)/shard_map/ppermute | solution.py:429
  53.2 6.4 %collective-permute-start.15 = (bf16[8,128,128]{2,1,0:T(8,128)(2,1)S(1)}, bf16[8,128,128]{2,1,0:T(8,128)(2,1)S(1)}, u32[]{:S(2)}, u32[]{:S(2)}) collective-permute-start(bf16[8,128,128]{2,1,0:T(8,128)(2,1)S(1)} %add_convert_fusion.4), channel_id=1, source_target_pairs={{0,4},{1,3},{4,8},{5,1},{8,12},{9,5},{12,14},{13,9},{14,10},{15,13... | collective-permute-start | bytes 786440 | tf_op jit(solution)/shard_map/ppermute | solution.py:429
  55.5 4.3 %collective-permute-start.18 = (bf16[8,128,128]{2,1,0:T(8,128)(2,1)S(1)}, bf16[8,128,128]{2,1,0:T(8,128)(2,1)S(1)}, u32[]{:S(2)}, u32[]{:S(2)}) collective-permute-start(bf16[8,128,128]{2,1,0:T(8,128)(2,1)S(1)} %get-tuple-element.62), channel_id=1, source_target_pairs={{0,1},{1,0},{2,3},{3,2},{4,5},{5,4},{6,7},{7,6},{8,9},{9,8},{10,11... | collective-permute-start | bytes 786440 | tf_op jit(solution)/shard_map/ppermute | solution.py:429
  55.6 13.4 %copy-start.1 = (bf16[16,16,128]{2,1,0:T(8,128)(2,1)S(1)}, bf16[16,16,128]{2,1,0:T(8,128)(2,1)}, u32[]{:S(2)}) copy-start(bf16[16,16,128]{2,1,0:T(8,128)(2,1)} %refs_7_.1) | copy-start | bytes 196612
  55.6 13.4 %copy-start.2 = (s32[256]{0:T(256)S(1)}, s32[256]{0:T(256)}, u32[]{:S(2)}) copy-start(s32[256]{0:T(256)} %param.17) | copy-start | bytes 3076
  55.6 13.4 %copy-start.3 = (s32[256,1]{0,1:T(1,128)S(1)}, s32[256,1]{0,1:T(1,128)}, u32[]{:S(2)}) copy-start(s32[256,1]{0,1:T(1,128)} %param.18) | copy-start | bytes 3076
  55.6 13.4 %copy-start.4 = (s32[256]{0:T(256)S(1)}, s32[256]{0:T(256)}, u32[]{:S(2)}) copy-start(s32[256]{0:T(256)} %param.19) | copy-start | bytes 3076
  55.6 6.8 %collective-permute-start.20 = (bf16[8,128,128]{2,1,0:T(8,128)(2,1)S(1)}, bf16[8,128,128]{2,1,0:T(8,128)(2,1)S(1)}, u32[]{:S(2)}, u32[]{:S(2)}) collective-permute-start(bf16[8,128,128]{2,1,0:T(8,128)(2,1)S(1)} %add_convert_fusion.3), channel_id=1, source_target_pairs={{0,4},{1,3},{4,8},{5,1},{8,12},{9,5},{12,14},{13,9},{14,10},{15,13... | collective-permute-start | bytes 786440 | tf_op jit(solution)/shard_map/ppermute | solution.py:429
  57.3 5.3 %collective-permute-start.21 = (bf16[8,128,128]{2,1,0:T(8,128)(2,1)S(1)}, bf16[8,128,128]{2,1,0:T(8,128)(2,1)S(1)}, u32[]{:S(2)}, u32[]{:S(2)}) collective-permute-start(bf16[8,128,128]{2,1,0:T(8,128)(2,1)S(1)} %get-tuple-element.66), channel_id=1, source_target_pairs={{0,1},{1,0},{2,3},{3,2},{4,5},{5,4},{6,7},{7,6},{8,9},{9,8},{10,11... | collective-permute-start | bytes 786440 | tf_op jit(solution)/shard_map/ppermute | solution.py:429
  57.3 9.0 %collective-permute-start.22 = (bf16[8,128,128]{2,1,0:T(8,128)(2,1)S(1)}, bf16[8,128,128]{2,1,0:T(8,128)(2,1)S(1)}, u32[]{:S(2)}, u32[]{:S(2)}) collective-permute-start(bf16[8,128,128]{2,1,0:T(8,128)(2,1)S(1)} %get-tuple-element.68), channel_id=1, source_target_pairs={{0,1},{1,0},{2,3},{3,2},{4,5},{5,4},{6,7},{7,6},{8,9},{9,8},{10,11... | collective-permute-start | bytes 786440 | tf_op jit(solution)/shard_map/ppermute | solution.py:429
  59.8 6.4 %collective-permute-start.19 = (bf16[8,128,128]{2,1,0:T(8,128)(2,1)S(1)}, bf16[8,128,128]{2,1,0:T(8,128)(2,1)S(1)}, u32[]{:S(2)}, u32[]{:S(2)}) collective-permute-start(bf16[8,128,128]{2,1,0:T(8,128)(2,1)S(1)} %add_convert_fusion.2), channel_id=1, source_target_pairs={{0,4},{1,3},{4,8},{5,1},{8,12},{9,5},{12,14},{13,9},{14,10},{15,13... | collective-permute-start | bytes 786440 | tf_op jit(solution)/shard_map/ppermute | solution.py:429
  62.6 6.4 %collective-permute-start.24 = (bf16[8,128,128]{2,1,0:T(8,128)(2,1)S(1)}, bf16[8,128,128]{2,1,0:T(8,128)(2,1)S(1)}, u32[]{:S(2)}, u32[]{:S(2)}) collective-permute-start(bf16[8,128,128]{2,1,0:T(8,128)(2,1)S(1)} %add_convert_fusion.1), channel_id=1, source_target_pairs={{0,4},{1,3},{4,8},{5,1},{8,12},{9,5},{12,14},{13,9},{14,10},{15,13... | collective-permute-start | bytes 786440 | tf_op jit(solution)/shard_map/ppermute | solution.py:429
  64.8 4.2 %collective-permute-start.26 = (bf16[1024,128]{1,0:T(8,128)(2,1)S(1)}, bf16[1024,128]{1,0:T(8,128)(2,1)S(1)}, u32[]{:S(2)}, u32[]{:S(2)}) collective-permute-start(bf16[1024,128]{1,0:T(8,128)(2,1)S(1)} %get-tuple-element.71.refs_0_), channel_id=1, source_target_pairs={{0,1},{1,0},{2,3},{3,2},{4,5},{5,4},{6,7},{7,6},{8,9},{9,8},{10,11... | collective-permute-start | bytes 786440 | tf_op jit(solution)/shard_map/ppermute | solution.py:429
  66.3 6.4 %collective-permute-start.23 = (bf16[8,128,128]{2,1,0:T(8,128)(2,1)S(1)}, bf16[8,128,128]{2,1,0:T(8,128)(2,1)S(1)}, u32[]{:S(2)}, u32[]{:S(2)}) collective-permute-start(bf16[8,128,128]{2,1,0:T(8,128)(2,1)S(1)} %add_convert_fusion), channel_id=1, source_target_pairs={{0,4},{1,3},{4,8},{5,1},{8,12},{9,5},{12,14},{13,9},{14,10},{15,13... | collective-permute-start | bytes 786440 | tf_op jit(solution)/shard_map/ppermute | solution.py:429
  69.0 3.7 %collective-permute-start.25 = (bf16[8,128,128]{2,1,0:T(8,128)(2,1)S(1)}, bf16[8,128,128]{2,1,0:T(8,128)(2,1)S(1)}, u32[]{:S(2)}, u32[]{:S(2)}) collective-permute-start(bf16[8,128,128]{2,1,0:T(8,128)(2,1)S(1)} %collective-permute-done.24), channel_id=1, source_target_pairs={{0,1},{1,0},{2,3},{3,2},{4,5},{5,4},{6,7},{7,6},{8,9},{9,8},{10,11... | collective-permute-start | bytes 786440 | tf_op jit(solution)/shard_map/ppermute | solution.py:429
  71.6 0.8 %copy-start = (f32[16,64,128]{2,1,0:T(8,128)}, f32[16,64,128]{2,1,0:T(8,128)S(1)}, u32[]{:S(2)}) copy-start(f32[16,64,128]{2,1,0:T(8,128)S(1)} %far.1.rest_ref) | copy-start | bytes 1572868
  (2 other events, 1.4 us)

commit v14 on v12

--- a/solution.py
+++ b/solution.py
@@ -178,81 +178,71 @@
     send_refs, refs = refs[shards + 3 : shards + 3 + sends], refs[shards + 3 + sends :]
     if not late:
         coef_ref, refs = refs[0], refs[1:]
-    columns, blocks, sums, column_sem, coef_sem, block_sem = refs
+    columns, blocks, sums, entries, block_sem = refs
     directions = sums.shape[1]
     span = columns.shape[0] // shards
     dummy = sums.shape[0] - 1
 
-    copies = [
-        pltpu.make_async_copy(
-            ref.at[pl.ds(0, span)], columns.at[pl.ds(k * span, span)], column_sem.at[k]
-        )
-        for k, ref in enumerate(shard_refs)
-    ]
-    for copy in copies:
-        copy.start()
-    tails = []
-    if not late:
-        tail = coef_ref.shape[0] // shards
-        tails = [
-            pltpu.make_async_copy(
-                ref.at[pl.ds(span, tail)], coef_ref.at[pl.ds(k * tail, tail)], coef_sem.at[k]
-            )
-            for k, ref in enumerate(shard_refs)
-        ]
-    for copy in tails:
-        copy.start()
-
     begin, begin_there = list_ref[3, late], list_ref[11, 2 + late]
     here = list_ref[3, late + 1] - begin
     total = here + list_ref[11, 3 + late] - begin_there
-
-    def entry(j):
-        j = jnp.minimum(j, total - 1)
-        half = (j >= here).astype(jnp.int32)
-        return half, half * 8, j + jnp.where(half == 1, begin_there - here, begin)
-
-    def fetch(j, carry):
-        half, row, at = entry(j)
-
-        for side, source in enumerate((own_hbm, mate_hbm)):
-
-            @pl.when(half == side)
-            def _():
-                pltpu.make_async_copy(
-                    source.at[list_ref[row, at]], blocks.at[j], block_sem.at[j // batch]
-                ).start()
-
+    steps = (total + batch - 1) // batch
+
+    def fetch(source, row, shift, swap):
+        def one(j, carry):
+            at = j + shift
+            pltpu.make_async_copy(
+                source.at[list_ref[row, at]], blocks.at[j], block_sem.at[j // batch]
+            ).start()
+            entries[0, j] = list_ref[row + 1, at] ^ swap
+            entries[1, j] = list_ref[row + 2, at] * directions
+            return carry
+
+        return one
+
+    def fill(j, carry):
+        pltpu.make_async_copy(own_hbm.at[0], blocks.at[j], block_sem.at[j // batch]).start()
+        entries[0, j] = dummy
+        entries[1, j] = 0
         return carry
 
-    steps = (total + batch - 1) // batch
-    lax.fori_loop(0, steps * batch, fetch, 0)
+    lax.fori_loop(0, here, fetch(own_hbm, 0, begin, 0), 0)
+    lax.fori_loop(here, total, fetch(mate_hbm, 8, begin_there - here, dummy // 2), 0)
+    lax.fori_loop(total, steps * batch, fill, 0)
+
+    for k, ref in enumerate(shard_refs):
+
+        def gather(i, carry, k=k, ref=ref):
+            at = pl.multiple_of(i * directions, directions)
+            columns[pl.ds(pl.multiple_of(k * span + at, directions), directions)] = ref[
+                pl.ds(at, directions)
+            ]
+            return carry
+
+        lax.fori_loop(0, span // directions, gather, 0, unroll=4)
+        if not late:
+            tail = coef_ref.shape[0] // shards
+            coef_ref[k * tail : (k + 1) * tail] = ref[span : span + tail]
 
     def clear(i, carry):
         sums[i] = jnp.zeros(sums.shape[1:], sums.dtype)
         return carry
 
     lax.fori_loop(0, dummy, clear, 0)
-    for copy in copies:
-        copy.wait()
 
     def body(step, carry):
         first = step * batch
-        here_blocks = pl.ds(first, batch)
         pltpu.make_async_copy(
-            own_hbm.at[pl.ds(0, batch)], blocks.at[here_blocks], block_sem.at[step]
+            own_hbm.at[pl.ds(0, batch)], blocks.at[pl.ds(first, batch)], block_sem.at[step]
         ).wait()
         products = []
 
         def add(i):
-            half, row, at = entry(first + i)
-            place = list_ref[row + 1, at] ^ (half * (dummy // 2))
-            place = jnp.where(first + i < total, place, dummy)
+            place = entries[0, first + i]
             sums[place] = sums[place] + products[i]
 
         for i in range(batch):
-            half, row, at = entry(first + i)
-            start = pl.multiple_of(list_ref[row + 2, at] * directions, directions)
+            start = pl.multiple_of(entries[1, first + i], directions)
             products.append(
                 lax.dot_general(
                     columns[pl.ds(start, directions)],
@@ -283,8 +273,6 @@
 
         lax.fori_loop(0, send_ref.shape[0], pack, 0, unroll=2)
         at += send_ref.shape[0]
-    for copy in tails:
-        copy.wait()
 
 
 def far_kernel(*refs):
@@ -465,14 +453,13 @@
                 for part in pieces
             ]
             + [jax.ShapeDtypeStruct((chips * half * rank_k, unknowns), jnp.bfloat16)] * (1 - late),
-            in_specs=[whole(pltpu.SMEM)] + [whole(pl.ANY)] * (chips + 2),
+            in_specs=[whole(pltpu.SMEM)] + [whole()] * chips + [whole(pl.ANY)] * 2,
             out_specs=[whole()] * (2 + len(pieces) - late),
             scratch_shapes=[
                 pltpu.VMEM((chips * base, unknowns), jnp.bfloat16),
                 pltpu.VMEM((2 * stored, unknowns, unknowns), jnp.bfloat16),
                 pltpu.VMEM((2 * quarter * clusters + 1, directions, unknowns), jnp.float32),
-                pltpu.SemaphoreType.DMA((chips,)),
-                pltpu.SemaphoreType.DMA((chips,)),
+                pltpu.SMEM((2, 2 * stored), jnp.int32),
                 pltpu.SemaphoreType.DMA((2 * stored // BATCH,)),
             ],
             compiler_params=pltpu.CompilerParams(vmem_limit_bytes=NEAR_VMEM),

time: 71.6 us -> 71.3 us (level); the launches traced: 72.3 us -> 70.4 us
  starting transfers between devices: 28.6 us -> 27 us
    ppermute x27, starting transfers between devices: 28.6 us -> 27 us  [move(): return lax.ppermute(values, 'blk', where)]
  transfers between devices with their start and end apart: 27 -> 27, of which waited for: 14 -> 14; matrix products, arithmetic and copies ran while one was open for 3% -> 3% of each run, Pallas kernels for 15% -> 13%
where the time goes in v14:
time: 71.3 us; the launch traced here: 70.4 us
  starting transfers between devices  27 us (38%)
  waiting for transfers between devices  24 us (34%)
  Pallas kernels  15.9 us (22%)
  other arithmetic  2.26 us (3%)
  local copies, waits for them, and re-layouts  0.97 us (1%)
    ppermute x27, starting transfers between devices, move(): return lax.ppermute(values, 'blk', where)  27 us
    ppermute x27, waiting for transfers between devices, move(): return lax.ppermute(values, 'blk', where)  24 us
    pallas_call x2, Pallas kernels, near(): pl.pallas_call(functools.partial(near_kernel, late, BATCH, LAG, chips, le...  11.4 us
    pallas_call x1, Pallas kernels, far_field(): pl.pallas_call(far_kernel, out_shape=jax.ShapeDtypeStruct((clusters, dire...  2.51 us
    pallas_call x1, Pallas kernels, stationary(): pl.pallas_call(functools.partial(prologue_kernel, count), out_shape=[jax....  2.03 us
  transfers between devices with their start and end apart: 27, of which 14 were waited for; matrix products, arithmetic and copies ran while one was open for 3% of the time, Pallas kernels for 13%

profile of v14, /device:TPU:0, one launch (start us, length us, event | category | flops | bytes accessed | tf_op | source)
XLA Modules:
  0.0 70.4 jit_solution(5126749140794826968)
XLA Ops:
  0.5 2.0 %prologue.1 = (bf16[1152,128]{1,0:T(8,128)(2,1)}, s32[8,128]{1,0:T(8,128)}) custom-call(s32[1]{0:T(128)} %bitcast.me_ref.refs_2_, s32[1,128]{1,0:T(1,128)} %bitcast.14, s32[1,128]{1,0:T(1,128)} %bitcast.15, s32[1,128]{1,0:T(1,128)} %bitcast.16, bf16[16,64,128]{2,1,0:T(8,128)(2,1)} %rhs_ref.1, bf16[16,16,128]{2,1,0:T(8,128)(2,1)} %basis_ref.1), custom_call_target="tpu_custom_call" | custom-call | tf_op jit(solution)/shard_map/prologue/pallas_call | solution.py:408
  2.5 2.6 %collective-permute-start = (bf16[1152,128]{1,0:T(8,128)(2,1)}, bf16[1152,128]{1,0:T(8,128)(2,1)S(1)}, u32[]{:S(2)}, u32[]{:S(2)}) collective-permute-start(bf16[1152,128]{1,0:T(8,128)(2,1)} %get-tuple-element.43), channel_id=1, source_target_pairs={{0,4},{1,3},{4,8},{5,1},{8,12},{9,5},{12,14},{13,9},{14,10},{15,13... | collective-permute-start | bytes 884744 | tf_op jit(solution)/shard_map/ppermute | solution.py:401
  5.1 0.9 %copy.14 = bf16[256,16,16]{0,1,2:T(8,128)(2,1)S(1)} copy(bf16[256,16,16]{0,2,1:T(8,128)(2,1)} %param.16) | data formatting | bytes 262144 | tf_op args[5]
  6.0 1.4 %collective-permute-start.5 = (bf16[1152,128]{1,0:T(8,128)(2,1)}, bf16[1152,128]{1,0:T(8,128)(2,1)S(1)}, u32[]{:S(2)}, u32[]{:S(2)}) collective-permute-start(bf16[1152,128]{1,0:T(8,128)(2,1)} %get-tuple-element.43), channel_id=1, source_target_pairs={{0,3},{1,4},{4,1},{5,8},{8,5},{9,12},{12,9},{13,14},{14,13},{15,10... | collective-permute-start | bytes 884744 | tf_op jit(solution)/shard_map/ppermute | solution.py:401
  7.8 2.9 %collective-permute-done.refs_1_ = bf16[1152,128]{1,0:T(8,128)(2,1)S(1)} collective-permute-done((bf16[1152,128]{1,0:T(8,128)(2,1)}, bf16[1152,128]{1,0:T(8,128)(2,1)S(1)}, u32[]{:S(2)}, u32[]{:S(2)}) %collective-permute-start) | collective-permute-done | bytes 294944 | tf_op jit(solution)/shard_map/ppermute | solution.py:401
  10.7 2.4 %collective-permute-start.1 = (bf16[1152,128]{1,0:T(8,128)(2,1)S(1)}, bf16[1152,128]{1,0:T(8,128)(2,1)S(1)}, u32[]{:S(2)}, u32[]{:S(2)}) collective-permute-start(bf16[1152,128]{1,0:T(8,128)(2,1)S(1)} %collective-permute-done.refs_1_), channel_id=1, source_target_pairs={{0,4},{1,3},{4,8},{5,1},{8,12},{9,5},{12,14},{13,9},{14,10},{15,13... | collective-permute-start | bytes 884744 | tf_op jit(solution)/shard_map/ppermute | solution.py:401
  13.1 1.4 %collective-permute-done.4 = s32[8,128]{1,0:T(8,128)S(1)} collective-permute-done((s32[8,128]{1,0:T(8,128)}, s32[8,128]{1,0:T(8,128)S(1)}, u32[]{:S(2)}, u32[]{:S(2)}) %collective-permute-start.4) | collective-permute-done | bytes 4128 | tf_op jit(solution)/shard_map/ppermute | solution.py:401
  15.1 1.6 %collective-permute-start.6 = (bf16[1152,128]{1,0:T(8,128)(2,1)S(1)}, bf16[1152,128]{1,0:T(8,128)(2,1)S(1)}, u32[]{:S(2)}, u32[]{:S(2)}) collective-permute-start(bf16[1152,128]{1,0:T(8,128)(2,1)S(1)} %collective-permute-done.5.refs_2_), channel_id=1, source_target_pairs={{0,4},{1,3},{4,8},{5,1},{8,12},{9,5},{12,14},{13,9},{14,10},{15,13... | collective-permute-start | bytes 884744 | tf_op jit(solution)/shard_map/ppermute | solution.py:401
  16.7 1.3 %collective-permute-done.1.refs_3_ = bf16[1152,128]{1,0:T(8,128)(2,1)S(1)} collective-permute-done((bf16[1152,128]{1,0:T(8,128)(2,1)S(1)}, bf16[1152,128]{1,0:T(8,128)(2,1)S(1)}, u32[]{:S(2)}, u32[]{:S(2)}) %collective-permute-start.1) | collective-permute-done | bytes 294944 | tf_op jit(solution)/shard_map/ppermute | solution.py:401
  18.0 1.7 %collective-permute-start.7 = (bf16[1152,128]{1,0:T(8,128)(2,1)S(1)}, bf16[1152,128]{1,0:T(8,128)(2,1)S(1)}, u32[]{:S(2)}, u32[]{:S(2)}) collective-permute-start(bf16[1152,128]{1,0:T(8,128)(2,1)S(1)} %collective-permute-done.1.refs_3_), channel_id=1, source_target_pairs={{0,4},{1,3},{4,8},{5,1},{8,12},{9,5},{12,14},{13,9},{14,10},{15,13... | collective-permute-start | bytes 884744 | tf_op jit(solution)/shard_map/ppermute | solution.py:401
  19.8 2.1 %collective-permute-done.6.refs_4_ = bf16[1152,128]{1,0:T(8,128)(2,1)S(1)} collective-permute-done((bf16[1152,128]{1,0:T(8,128)(2,1)S(1)}, bf16[1152,128]{1,0:T(8,128)(2,1)S(1)}, u32[]{:S(2)}, u32[]{:S(2)}) %collective-permute-start.6) | collective-permute-done | bytes 294944 | tf_op jit(solution)/shard_map/ppermute | solution.py:401
  21.9 1.6 %collective-permute-start.8 = (bf16[1152,128]{1,0:T(8,128)(2,1)S(1)}, bf16[1152,128]{1,0:T(8,128)(2,1)S(1)}, u32[]{:S(2)}, u32[]{:S(2)}) collective-permute-start(bf16[1152,128]{1,0:T(8,128)(2,1)S(1)} %collective-permute-done.6.refs_4_), channel_id=1, source_target_pairs={{0,4},{1,3},{4,8},{5,1},{8,12},{9,5},{12,14},{13,9},{14,10},{15,13... | collective-permute-start | bytes 884744 | tf_op jit(solution)/shard_map/ppermute | solution.py:401
  23.4 1.6 %collective-permute-done.7.refs_5_ = bf16[1152,128]{1,0:T(8,128)(2,1)S(1)} collective-permute-done((bf16[1152,128]{1,0:T(8,128)(2,1)S(1)}, bf16[1152,128]{1,0:T(8,128)(2,1)S(1)}, u32[]{:S(2)}, u32[]{:S(2)}) %collective-permute-start.7) | collective-permute-done | bytes 294944 | tf_op jit(solution)/shard_map/ppermute | solution.py:401
  25.0 1.6 %collective-permute-start.9 = (bf16[1152,128]{1,0:T(8,128)(2,1)S(1)}, bf16[1152,128]{1,0:T(8,128)(2,1)S(1)}, u32[]{:S(2)}, u32[]{:S(2)}) collective-permute-start(bf16[1152,128]{1,0:T(8,128)(2,1)S(1)} %collective-permute-done.7.refs_5_), channel_id=1, source_target_pairs={{0,4},{1,3},{4,8},{5,1},{8,12},{9,5},{12,14},{13,9},{14,10},{15,13... | collective-permute-start | bytes 884744 | tf_op jit(solution)/shard_map/ppermute | solution.py:401
  26.6 2.0 %collective-permute-done.8.refs_6_ = bf16[1152,128]{1,0:T(8,128)(2,1)S(1)} collective-permute-done((bf16[1152,128]{1,0:T(8,128)(2,1)S(1)}, bf16[1152,128]{1,0:T(8,128)(2,1)S(1)}, u32[]{:S(2)}, u32[]{:S(2)}) %collective-permute-start.8) | collective-permute-done | bytes 294944 | tf_op jit(solution)/shard_map/ppermute | solution.py:401
  28.6 3.2 %collective-permute-done.9.refs_7_ = bf16[1152,128]{1,0:T(8,128)(2,1)S(1)} collective-permute-done((bf16[1152,128]{1,0:T(8,128)(2,1)S(1)}, bf16[1152,128]{1,0:T(8,128)(2,1)S(1)}, u32[]{:S(2)}, u32[]{:S(2)}) %collective-permute-start.9) | collective-permute-done | bytes 294944 | tf_op jit(solution)/shard_map/ppermute | solution.py:401
  31.7 6.8 %near.2 = (f32[64,64,128]{2,1,0:T(8,128)S(1)}, bf16[16,64,128]{2,1,0:T(8,128)(2,1)S(1)}, bf16[16,64,128]{2,1,0:T(8,128)(2,1)S(1)}, bf16[16,64,128]{2,1,0:T(8,128...) custom-call(s32[16,128]{1,0:T(8,128)S(1)} %pad_add_fusion.list_ref, ...), custom_call_target="tpu_custom_call" | custom-call | flops 2147483648 | bytes 16777216 | tf_op jit(solution)/shard_map/near/pallas_call | solution.py:446
  39.1 1.0 %collective-permute-done.12 = bf16[16,64,128]{2,1,0:T(8,128)(2,1)S(1)} collective-permute-done((bf16[16,64,128]{2,1,0:T(8,128)(2,1)S(1)}, bf16[16,64,128]{2,1,0:T(8,128)(2,1)S(1)}, u32[]{:S(2)}, u32[]{:S(2)}) %collective-permute-start.12) | collective-permute-done | bytes 262176 | tf_op jit(solution)/shard_map/ppermute | solution.py:401
  40.9 0.8 %collective-permute-start.13 = (bf16[16,64,128]{2,1,0:T(8,128)(2,1)S(1)}, bf16[16,64,128]{2,1,0:T(8,128)(2,1)S(1)}, u32[]{:S(2)}, u32[]{:S(2)}) collective-permute-start(bf16[16,64,128]{2,1,0:T(8,128)(2,1)S(1)} %get-tuple-element.50), channel_id=1, source_target_pairs={{0,4},{1,3},{4,8},{5,1},{8,12},{9,5},{12,14},{13,9},{14,10},{15,13... | collective-permute-start | bytes 786440 | tf_op jit(solution)/shard_map/ppermute | solution.py:401
  41.7 1.4 %collective-permute-start.17 = (bf16[16,64,128]{2,1,0:T(8,128)(2,1)S(1)}, bf16[16,64,128]{2,1,0:T(8,128)(2,1)S(1)}, u32[]{:S(2)}, u32[]{:S(2)}) collective-permute-start(bf16[16,64,128]{2,1,0:T(8,128)(2,1)S(1)} %get-tuple-element.52), channel_id=1, source_target_pairs={{0,4},{1,3},{4,8},{5,1},{8,12},{9,5},{12,14},{13,9},{14,10},{15,13... | collective-permute-start | bytes 786440 | tf_op jit(solution)/shard_map/ppermute | solution.py:401
  43.1 1.4 %collective-permute-start.15 = (bf16[16,64,128]{2,1,0:T(8,128)(2,1)S(1)}, bf16[16,64,128]{2,1,0:T(8,128)(2,1)S(1)}, u32[]{:S(2)}, u32[]{:S(2)}) collective-permute-start(bf16[16,64,128]{2,1,0:T(8,128)(2,1)S(1)} %get-tuple-element.55), channel_id=1, source_target_pairs={{0,1},{1,0},{2,3},{3,2},{4,5},{5,4},{6,7},{7,6},{8,9},{9,8},{10,11... | collective-permute-start | bytes 786440 | tf_op jit(solution)/shard_map/ppermute | solution.py:401
  44.5 4.6 %near.3 = (f32[64,64,128]{2,1,0:T(8,128)S(1)}, bf16[16,64,128]{2,1,0:T(8,128)(2,1)S(1)}, bf16[16,64,128]{2,1,0:T(8,128)(2,1)S(1)}, bf16[16,64,128]{2,1,0:T(8,128)(2,1)S(1)}, bf16[16,64,128]{2,1,0:T(8,128)(2,1)S(1)}) custom-call(s32[16,128]{1,0:T(8,128)S(1)} %pad_add_fusion.list_ref, bf16[1152,128]{1,0:T(8,128)(2,1)S(1)} %collective-permute-done.3.refs_0_, ...), custom_call_target="tpu_custom_call" | custom-call | flops 2147483648 | bytes 16777216 | tf_op jit(solution)/shard_map/near/pallas_call | solution.py:446
  50.0 1.4 %collective-permute-start.16 = (bf16[16,64,128]{2,1,0:T(8,128)(2,1)S(1)}, bf16[16,64,128]{2,1,0:T(8,128)(2,1)S(1)}, u32[]{:S(2)}, u32[]{:S(2)}) collective-permute-start(bf16[16,64,128]{2,1,0:T(8,128)(2,1)S(1)} %add_convert_fusion.5), channel_id=1, source_target_pairs={{0,4},{1,3},{4,8},{5,1},{8,12},{9,5},{12,14},{13,9},{14,10},{15,13... | collective-permute-start | bytes 786440 | tf_op jit(solution)/shard_map/ppermute | solution.py:401
  52.0 1.6 %collective-permute-start.21 = (bf16[16,64,128]{2,1,0:T(8,128)(2,1)S(1)}, bf16[16,64,128]{2,1,0:T(8,128)(2,1)S(1)}, u32[]{:S(2)}, u32[]{:S(2)}) collective-permute-start(bf16[16,64,128]{2,1,0:T(8,128)(2,1)S(1)} %add_convert_fusion.4), channel_id=1, source_target_pairs={{0,4},{1,3},{4,8},{5,1},{8,12},{9,5},{12,14},{13,9},{14,10},{15,13... | collective-permute-start | bytes 786440 | tf_op jit(solution)/shard_map/ppermute | solution.py:401
  53.7 2.7 %collective-permute-done.16 = bf16[16,64,128]{2,1,0:T(8,128)(2,1)S(1)} collective-permute-done((bf16[16,64,128]{2,1,0:T(8,128)(2,1)S(1)}, bf16[16,64,128]{2,1,0:T(8,128)(2,1)S(1)}, u32[]{:S(2)}, u32[]{:S(2)}) %collective-permute-start.16) | collective-permute-done | bytes 262176 | tf_op jit(solution)/shard_map/ppermute | solution.py:401
  56.5 1.4 %collective-permute-start.20 = (bf16[16,64,128]{2,1,0:T(8,128)(2,1)S(1)}, bf16[16,64,128]{2,1,0:T(8,128)(2,1)S(1)}, u32[]{:S(2)}, u32[]{:S(2)}) collective-permute-start(bf16[16,64,128]{2,1,0:T(8,128)(2,1)S(1)} %add_convert_fusion.3), channel_id=1, source_target_pairs={{0,4},{1,3},{4,8},{5,1},{8,12},{9,5},{12,14},{13,9},{14,10},{15,13... | collective-permute-start | bytes 786440 | tf_op jit(solution)/shard_map/ppermute | solution.py:401
  59.3 1.4 %collective-permute-start.25 = (bf16[16,64,128]{2,1,0:T(8,128)(2,1)S(1)}, bf16[16,64,128]{2,1,0:T(8,128)(2,1)S(1)}, u32[]{:S(2)}, u32[]{:S(2)}) collective-permute-start(bf16[16,64,128]{2,1,0:T(8,128)(2,1)S(1)} %add_convert_fusion.2), channel_id=1, source_target_pairs={{0,4},{1,3},{4,8},{5,1},{8,12},{9,5},{12,14},{13,9},{14,10},{15,13... | collective-permute-start | bytes 786440 | tf_op jit(solution)/shard_map/ppermute | solution.py:401
  60.7 2.2 %collective-permute-done.20 = bf16[16,64,128]{2,1,0:T(8,128)(2,1)S(1)} collective-permute-done((bf16[16,64,128]{2,1,0:T(8,128)(2,1)S(1)}, bf16[16,64,128]{2,1,0:T(8,128)(2,1)S(1)}, u32[]{:S(2)}, u32[]{:S(2)}) %collective-permute-start.20) | collective-permute-done | bytes 262176 | tf_op jit(solution)/shard_map/ppermute | solution.py:401
  63.1 1.4 %collective-permute-start.24 = (bf16[16,64,128]{2,1,0:T(8,128)(2,1)S(1)}, bf16[16,64,128]{2,1,0:T(8,128)(2,1)S(1)}, u32[]{:S(2)}, u32[]{:S(2)}) collective-permute-start(bf16[16,64,128]{2,1,0:T(8,128)(2,1)S(1)} %add_convert_fusion.1), channel_id=1, source_target_pairs={{0,4},{1,3},{4,8},{5,1},{8,12},{9,5},{12,14},{13,9},{14,10},{15,13... | collective-permute-start | bytes 786440 | tf_op jit(solution)/shard_map/ppermute | solution.py:401
  64.5 1.3 %collective-permute-done.25 = bf16[16,64,128]{2,1,0:T(8,128)(2,1)S(1)} collective-permute-done((bf16[16,64,128]{2,1,0:T(8,128)(2,1)S(1)}, bf16[16,64,128]{2,1,0:T(8,128)(2,1)S(1)}, u32[]{:S(2)}, u32[]{:S(2)}) %collective-permute-start.25) | collective-permute-done | bytes 262176 | tf_op jit(solution)/shard_map/ppermute | solution.py:401
  65.8 2.5 %far.1 = f32[16,64,128]{2,1,0:T(8,128)S(1)} custom-call(bf16[1024,128]{1,0:T(8,128)(2,1)S(1)} %get-tuple-element.46.refs_0_, bf16[1024,128]{1,0:T(8,128)(2,1)S(1)} %collective-permute-done.10.refs_1_, s32[1]{0:T(128)} %bitcast.me_ref.refs_2_, bf16[16,16,256]{2,1,0:T(8,128)(2,1)S(1)} %bitcast.10, s32[1,256]{1,0:T(1,128)S(1)} %bitcast.11, ...), custom_call_target="tpu_custom_call" | custom-call | flops 536870912 | bytes 8388608 | tf_op jit(solution)/shard_map/far/pallas_call | solution.py:476
  68.3 1.2 %collective-permute-done.24 = bf16[16,64,128]{2,1,0:T(8,128)(2,1)S(1)} collective-permute-done((bf16[16,64,128]{2,1,0:T(8,128)(2,1)S(1)}, bf16[16,64,128]{2,1,0:T(8,128)(2,1)S(1)}, u32[]{:S(2)}, u32[]{:S(2)}) %collective-permute-start.24) | collective-permute-done | bytes 262176 | tf_op jit(solution)/shard_map/ppermute | solution.py:401
  (44 shorter events, 6.8 us)
Async XLA Ops:
  0.0 18.0 %collective-permute-start.2 = (bf16[128,128,128]{2,1,0:T(8,128)(2,1)}, bf16[128,128,128]{2,1,0:T(8,128)(2,1)}, u32[]{:S(2)}, u32[]{:S(2)}) collective-permute-start(bf16[128,128,128]{2,1,0:T(8,128)(2,1)} %refs_8_.3), channel_id=1, source_target_pairs={{0,1},{1,0},{2,3},{3,2},{4,5},{5,4},{6,7},{7,6},{8,9},{9,8},{10,11... | collective-permute-start | bytes 12582920 | tf_op jit(solution)/shard_map/ppermute | solution.py:401
  2.5 8.2 %collective-permute-start = (bf16[1152,128]{1,0:T(8,128)(2,1)}, bf16[1152,128]{1,0:T(8,128)(2,1)S(1)}, u32[]{:S(2)}, u32[]{:S(2)}) collective-permute-start(bf16[1152,128]{1,0:T(8,128)(2,1)} %get-tuple-element.43), channel_id=1, source_target_pairs={{0,4},{1,3},{4,8},{5,1},{8,12},{9,5},{12,14},{13,9},{14,10},{15,13... | collective-permute-start | bytes 884744 | tf_op jit(solution)/shard_map/ppermute | solution.py:401
  6.0 9.1 %collective-permute-start.5 = (bf16[1152,128]{1,0:T(8,128)(2,1)}, bf16[1152,128]{1,0:T(8,128)(2,1)S(1)}, u32[]{:S(2)}, u32[]{:S(2)}) collective-permute-start(bf16[1152,128]{1,0:T(8,128)(2,1)} %get-tuple-element.43), channel_id=1, source_target_pairs={{0,3},{1,4},{4,1},{5,8},{8,5},{9,12},{12,9},{13,14},{14,13},{15,10... | collective-permute-start | bytes 884744 | tf_op jit(solution)/shard_map/ppermute | solution.py:401
  7.4 9.3 %collective-permute-start.3 = (bf16[1152,128]{1,0:T(8,128)(2,1)}, bf16[1152,128]{1,0:T(8,128)(2,1)S(1)}, u32[]{:S(2)}, u32[]{:S(2)}) collective-permute-start(bf16[1152,128]{1,0:T(8,128)(2,1)} %get-tuple-element.43), channel_id=1, source_target_pairs={{0,1},{1,0},{2,3},{3,2},{4,5},{5,4},{6,7},{7,6},{8,9},{9,8},{10,11... | collective-permute-start | bytes 884744 | tf_op jit(solution)/shard_map/ppermute | solution.py:401
  10.7 7.4 %collective-permute-start.1 = (bf16[1152,128]{1,0:T(8,128)(2,1)S(1)}, bf16[1152,128]{1,0:T(8,128)(2,1)S(1)}, u32[]{:S(2)}, u32[]{:S(2)}) collective-permute-start(bf16[1152,128]{1,0:T(8,128)(2,1)S(1)} %collective-permute-done.refs_1_), channel_id=1, source_target_pairs={{0,4},{1,3},{4,8},{5,1},{8,12},{9,5},{12,14},{13,9},{14,10},{15,13... | collective-permute-start | bytes 884744 | tf_op jit(solution)/shard_map/ppermute | solution.py:401
  13.1 1.4 %collective-permute-start.4 = (s32[8,128]{1,0:T(8,128)}, s32[8,128]{1,0:T(8,128)S(1)}, u32[]{:S(2)}, u32[]{:S(2)}) collective-permute-start(s32[8,128]{1,0:T(8,128)} %get-tuple-element.40), channel_id=1, source_target_pairs={{0,1},{1,0},{2,3},{3,2},{4,5},{5,4},{6,7},{7,6},{8,9},{9,8},{10,11... | collective-permute-start | bytes 12296 | tf_op jit(solution)/shard_map/ppermute | solution.py:401
  15.1 6.7 %collective-permute-start.6 = (bf16[1152,128]{1,0:T(8,128)(2,1)S(1)}, bf16[1152,128]{1,0:T(8,128)(2,1)S(1)}, u32[]{:S(2)}, u32[]{:S(2)}) collective-permute-start(bf16[1152,128]{1,0:T(8,128)(2,1)S(1)} %collective-permute-done.5.refs_2_), channel_id=1, source_target_pairs={{0,4},{1,3},{4,8},{5,1},{8,12},{9,5},{12,14},{13,9},{14,10},{15,13... | collective-permute-start | bytes 884744 | tf_op jit(solution)/shard_map/ppermute | solution.py:401
  18.0 7.0 %collective-permute-start.7 = (bf16[1152,128]{1,0:T(8,128)(2,1)S(1)}, bf16[1152,128]{1,0:T(8,128)(2,1)S(1)}, u32[]{:S(2)}, u32[]{:S(2)}) collective-permute-start(bf16[1152,128]{1,0:T(8,128)(2,1)S(1)} %collective-permute-done.1.refs_3_), channel_id=1, source_target_pairs={{0,4},{1,3},{4,8},{5,1},{8,12},{9,5},{12,14},{13,9},{14,10},{15,13... | collective-permute-start | bytes 884744 | tf_op jit(solution)/shard_map/ppermute | solution.py:401
  21.9 6.7 %collective-permute-start.8 = (bf16[1152,128]{1,0:T(8,128)(2,1)S(1)}, bf16[1152,128]{1,0:T(8,128)(2,1)S(1)}, u32[]{:S(2)}, u32[]{:S(2)}) collective-permute-start(bf16[1152,128]{1,0:T(8,128)(2,1)S(1)} %collective-permute-done.6.refs_4_), channel_id=1, source_target_pairs={{0,4},{1,3},{4,8},{5,1},{8,12},{9,5},{12,14},{13,9},{14,10},{15,13... | collective-permute-start | bytes 884744 | tf_op jit(solution)/shard_map/ppermute | solution.py:401
  25.0 6.7 %collective-permute-start.9 = (bf16[1152,128]{1,0:T(8,128)(2,1)S(1)}, bf16[1152,128]{1,0:T(8,128)(2,1)S(1)}, u32[]{:S(2)}, u32[]{:S(2)}) collective-permute-start(bf16[1152,128]{1,0:T(8,128)(2,1)S(1)} %collective-permute-done.7.refs_5_), channel_id=1, source_target_pairs={{0,4},{1,3},{4,8},{5,1},{8,12},{9,5},{12,14},{13,9},{14,10},{15,13... | collective-permute-start | bytes 884744 | tf_op jit(solution)/shard_map/ppermute | solution.py:401
  38.5 1.6 %collective-permute-start.12 = (bf16[16,64,128]{2,1,0:T(8,128)(2,1)S(1)}, bf16[16,64,128]{2,1,0:T(8,128)(2,1)S(1)}, u32[]{:S(2)}, u32[]{:S(2)}) collective-permute-start(bf16[16,64,128]{2,1,0:T(8,128)(2,1)S(1)} %get-tuple-element.49), channel_id=1, source_target_pairs={{0,1},{1,0},{2,3},{3,2},{4,5},{5,4},{6,7},{7,6},{8,9},{9,8},{10,11... | collective-permute-start | bytes 786440 | tf_op jit(solution)/shard_map/ppermute | solution.py:401
  38.6 1.9 %collective-permute-start.11 = (bf16[16,64,128]{2,1,0:T(8,128)(2,1)S(1)}, bf16[16,64,128]{2,1,0:T(8,128)(2,1)S(1)}, u32[]{:S(2)}, u32[]{:S(2)}) collective-permute-start(bf16[16,64,128]{2,1,0:T(8,128)(2,1)S(1)} %get-tuple-element.48), channel_id=1, source_target_pairs={{0,1},{1,0},{2,3},{3,2},{4,5},{5,4},{6,7},{7,6},{8,9},{9,8},{10,11... | collective-permute-start | bytes 786440 | tf_op jit(solution)/shard_map/ppermute | solution.py:401
  40.7 9.2 %collective-permute-start.14 = (bf16[16,64,128]{2,1,0:T(8,128)(2,1)S(1)}, bf16[16,64,128]{2,1,0:T(8,128)(2,1)S(1)}, u32[]{:S(2)}, u32[]{:S(2)}) collective-permute-start(bf16[16,64,128]{2,1,0:T(8,128)(2,1)S(1)} %get-tuple-element.53), channel_id=1, source_target_pairs={{0,1},{1,0},{2,3},{3,2},{4,5},{5,4},{6,7},{7,6},{8,9},{9,8},{10,11... | collective-permute-start | bytes 786440 | tf_op jit(solution)/shard_map/ppermute | solution.py:401
  40.9 9.0 %collective-permute-start.13 = (bf16[16,64,128]{2,1,0:T(8,128)(2,1)S(1)}, bf16[16,64,128]{2,1,0:T(8,128)(2,1)S(1)}, u32[]{:S(2)}, u32[]{:S(2)}) collective-permute-start(bf16[16,64,128]{2,1,0:T(8,128)(2,1)S(1)} %get-tuple-element.50), channel_id=1, source_target_pairs={{0,4},{1,3},{4,8},{5,1},{8,12},{9,5},{12,14},{13,9},{14,10},{15,13... | collective-permute-start | bytes 786440 | tf_op jit(solution)/shard_map/ppermute | solution.py:401
  41.7 10.2 %collective-permute-start.17 = (bf16[16,64,128]{2,1,0:T(8,128)(2,1)S(1)}, bf16[16,64,128]{2,1,0:T(8,128)(2,1)S(1)}, u32[]{:S(2)}, u32[]{:S(2)}) collective-permute-start(bf16[16,64,128]{2,1,0:T(8,128)(2,1)S(1)} %get-tuple-element.52), channel_id=1, source_target_pairs={{0,4},{1,3},{4,8},{5,1},{8,12},{9,5},{12,14},{13,9},{14,10},{15,13... | collective-permute-start | bytes 786440 | tf_op jit(solution)/shard_map/ppermute | solution.py:401
  43.1 6.9 %collective-permute-start.15 = (bf16[16,64,128]{2,1,0:T(8,128)(2,1)S(1)}, bf16[16,64,128]{2,1,0:T(8,128)(2,1)S(1)}, u32[]{:S(2)}, u32[]{:S(2)}) collective-permute-start(bf16[16,64,128]{2,1,0:T(8,128)(2,1)S(1)} %get-tuple-element.55), channel_id=1, source_target_pairs={{0,1},{1,0},{2,3},{3,2},{4,5},{5,4},{6,7},{7,6},{8,9},{9,8},{10,11... | collective-permute-start | bytes 786440 | tf_op jit(solution)/shard_map/ppermute | solution.py:401
  49.1 2.9 %collective-permute-start.18 = (bf16[16,64,128]{2,1,0:T(8,128)(2,1)S(1)}, bf16[16,64,128]{2,1,0:T(8,128)(2,1)S(1)}, u32[]{:S(2)}, u32[]{:S(2)}) collective-permute-start(bf16[16,64,128]{2,1,0:T(8,128)(2,1)S(1)} %get-tuple-element.60), channel_id=1, source_target_pairs={{0,1},{1,0},{2,3},{3,2},{4,5},{5,4},{6,7},{7,6},{8,9},{9,8},{10,11... | collective-permute-start | bytes 786440 | tf_op jit(solution)/shard_map/ppermute | solution.py:401
  50.0 6.4 %collective-permute-start.16 = (bf16[16,64,128]{2,1,0:T(8,128)(2,1)S(1)}, bf16[16,64,128]{2,1,0:T(8,128)(2,1)S(1)}, u32[]{:S(2)}, u32[]{:S(2)}) collective-permute-start(bf16[16,64,128]{2,1,0:T(8,128)(2,1)S(1)} %add_convert_fusion.5), channel_id=1, source_target_pairs={{0,4},{1,3},{4,8},{5,1},{8,12},{9,5},{12,14},{13,9},{14,10},{15,13... | collective-permute-start | bytes 786440 | tf_op jit(solution)/shard_map/ppermute | solution.py:401
  51.4 5.1 %collective-permute-start.19 = (bf16[16,64,128]{2,1,0:T(8,128)(2,1)S(1)}, bf16[16,64,128]{2,1,0:T(8,128)(2,1)S(1)}, u32[]{:S(2)}, u32[]{:S(2)}) collective-permute-start(bf16[16,64,128]{2,1,0:T(8,128)(2,1)S(1)} %get-tuple-element.62), channel_id=1, source_target_pairs={{0,1},{1,0},{2,3},{3,2},{4,5},{5,4},{6,7},{7,6},{8,9},{9,8},{10,11... | collective-permute-start | bytes 786440 | tf_op jit(solution)/shard_map/ppermute | solution.py:401
  51.6 7.7 %collective-permute-start.22 = (bf16[16,64,128]{2,1,0:T(8,128)(2,1)S(1)}, bf16[16,64,128]{2,1,0:T(8,128)(2,1)S(1)}, u32[]{:S(2)}, u32[]{:S(2)}) collective-permute-start(bf16[16,64,128]{2,1,0:T(8,128)(2,1)S(1)} %get-tuple-element.66), channel_id=1, source_target_pairs={{0,1},{1,0},{2,3},{3,2},{4,5},{5,4},{6,7},{7,6},{8,9},{9,8},{10,11... | collective-permute-start | bytes 786440 | tf_op jit(solution)/shard_map/ppermute | solution.py:401
  52.0 13.8 %copy-start = (bf16[16,16,128]{2,1,0:T(8,128)(2,1)S(1)}, bf16[16,16,128]{2,1,0:T(8,128)(2,1)}, u32[]{:S(2)}) copy-start(bf16[16,16,128]{2,1,0:T(8,128)(2,1)} %refs_7_.1) | copy-start | bytes 196612
  52.0 13.8 %copy-start.1 = (s32[256]{0:T(256)S(1)}, s32[256]{0:T(256)}, u32[]{:S(2)}) copy-start(s32[256]{0:T(256)} %param.17) | copy-start | bytes 3076
  52.0 13.8 %copy-start.2 = (s32[256,1]{0,1:T(1,128)S(1)}, s32[256,1]{0,1:T(1,128)}, u32[]{:S(2)}) copy-start(s32[256,1]{0,1:T(1,128)} %param.18) | copy-start | bytes 3076
  52.0 13.8 %copy-start.3 = (s32[256]{0:T(256)S(1)}, s32[256]{0:T(256)}, u32[]{:S(2)}) copy-start(s32[256]{0:T(256)} %param.19) | copy-start | bytes 3076
  52.0 7.2 %collective-permute-start.21 = (bf16[16,64,128]{2,1,0:T(8,128)(2,1)S(1)}, bf16[16,64,128]{2,1,0:T(8,128)(2,1)S(1)}, u32[]{:S(2)}, u32[]{:S(2)}) collective-permute-start(bf16[16,64,128]{2,1,0:T(8,128)(2,1)S(1)} %add_convert_fusion.4), channel_id=1, source_target_pairs={{0,4},{1,3},{4,8},{5,1},{8,12},{9,5},{12,14},{13,9},{14,10},{15,13... | collective-permute-start | bytes 786440 | tf_op jit(solution)/shard_map/ppermute | solution.py:401
  56.5 6.4 %collective-permute-start.20 = (bf16[16,64,128]{2,1,0:T(8,128)(2,1)S(1)}, bf16[16,64,128]{2,1,0:T(8,128)(2,1)S(1)}, u32[]{:S(2)}, u32[]{:S(2)}) collective-permute-start(bf16[16,64,128]{2,1,0:T(8,128)(2,1)S(1)} %add_convert_fusion.3), channel_id=1, source_target_pairs={{0,4},{1,3},{4,8},{5,1},{8,12},{9,5},{12,14},{13,9},{14,10},{15,13... | collective-permute-start | bytes 786440 | tf_op jit(solution)/shard_map/ppermute | solution.py:401
  57.9 7.8 %collective-permute-start.10 = (bf16[1024,128]{1,0:T(8,128)(2,1)S(1)}, bf16[1024,128]{1,0:T(8,128)(2,1)S(1)}, u32[]{:S(2)}, u32[]{:S(2)}) collective-permute-start(bf16[1024,128]{1,0:T(8,128)(2,1)S(1)} %get-tuple-element.46.refs_0_), channel_id=1, source_target_pairs={{0,1},{1,0},{2,3},{3,2},{4,5},{5,4},{6,7},{7,6},{8,9},{9,8},{10,11... | collective-permute-start | bytes 786440 | tf_op jit(solution)/shard_map/ppermute | solution.py:401
  57.9 5.1 %collective-permute-start.23 = (bf16[16,64,128]{2,1,0:T(8,128)(2,1)S(1)}, bf16[16,64,128]{2,1,0:T(8,128)(2,1)S(1)}, u32[]{:S(2)}, u32[]{:S(2)}) collective-permute-start(bf16[16,64,128]{2,1,0:T(8,128)(2,1)S(1)} %get-tuple-element.68), channel_id=1, source_target_pairs={{0,1},{1,0},{2,3},{3,2},{4,5},{5,4},{6,7},{7,6},{8,9},{9,8},{10,11... | collective-permute-start | bytes 786440 | tf_op jit(solution)/shard_map/ppermute | solution.py:401
  59.3 6.4 %collective-permute-start.25 = (bf16[16,64,128]{2,1,0:T(8,128)(2,1)S(1)}, bf16[16,64,128]{2,1,0:T(8,128)(2,1)S(1)}, u32[]{:S(2)}, u32[]{:S(2)}) collective-permute-start(bf16[16,64,128]{2,1,0:T(8,128)(2,1)S(1)} %add_convert_fusion.2), channel_id=1, source_target_pairs={{0,4},{1,3},{4,8},{5,1},{8,12},{9,5},{12,14},{13,9},{14,10},{15,13... | collective-permute-start | bytes 786440 | tf_op jit(solution)/shard_map/ppermute | solution.py:401
  63.1 6.4 %collective-permute-start.24 = (bf16[16,64,128]{2,1,0:T(8,128)(2,1)S(1)}, bf16[16,64,128]{2,1,0:T(8,128)(2,1)S(1)}, u32[]{:S(2)}, u32[]{:S(2)}) collective-permute-start(bf16[16,64,128]{2,1,0:T(8,128)(2,1)S(1)} %add_convert_fusion.1), channel_id=1, source_target_pairs={{0,4},{1,3},{4,8},{5,1},{8,12},{9,5},{12,14},{13,9},{14,10},{15,13... | collective-permute-start | bytes 786440 | tf_op jit(solution)/shard_map/ppermute | solution.py:401
  65.8 3.9 %collective-permute-start.26 = (bf16[16,64,128]{2,1,0:T(8,128)(2,1)S(1)}, bf16[16,64,128]{2,1,0:T(8,128)(2,1)S(1)}, u32[]{:S(2)}, u32[]{:S(2)}) collective-permute-start(bf16[16,64,128]{2,1,0:T(8,128)(2,1)S(1)} %collective-permute-done.25), channel_id=1, source_target_pairs={{0,1},{1,0},{2,3},{3,2},{4,5},{5,4},{6,7},{7,6},{8,9},{9,8},{10,11... | collective-permute-start | bytes 786440 | tf_op jit(solution)/shard_map/ppermute | solution.py:401

commit v15 on v14

--- a/solution.py
+++ b/solution.py
@@ -7,10 +7,12 @@
 from jax.experimental.pallas import tpu as pltpu
 from jax.sharding import PartitionSpec as P
 
-BATCH = 16
+BATCH = 8
+CHUNKS = 4
+LATE = 2
 LAG = 4
 PROLOGUE_VMEM = 58 << 20
-NEAR_VMEM = 48 << 20
+NEAR_VMEM = 20 << 20, 20 << 20
 FAR_VMEM = 16 << 20
 
 
@@ -143,15 +145,13 @@
 
     me, owner, slot = me_ref[0], owner_ref[...], slot_ref[...]
     stored = owner.shape[1]
-    place = scatter_place(owner, me, count)
-    quarter = count // 4
-    late = (place // quarter) & 1
-    place = (place // (2 * quarter) * quarter + (place & (quarter - 1))) * clusters + slot
+    place = scatter_place(owner, me, count) * clusters + slot
     column = (owner * clusters + slot + offset_ref[...]) & (count * clusters - 1)
     shard = gather_place(column // clusters, me, count)
     theirs = (shard == count // 2).astype(jnp.int32)
     shard = jnp.where(theirs == 1, gather_place(column // clusters, me ^ 1, count), shard)
     column_place = shard * clusters + (column & (clusters - 1))
+    late = (shard >= count // 2 - LATE).astype(jnp.int32)
     square = (stored, stored)
     group = jnp.broadcast_to((2 * theirs + late).astype(jnp.float32), square)
     group_of_row = jnp.transpose(group)
@@ -174,43 +174,38 @@
 
 
 def near_kernel(late, batch, lag, shards, sends, list_ref, *refs):
-    shard_refs, (own_hbm, mate_hbm, keep_ref) = refs[:shards], refs[shards : shards + 3]
-    send_refs, refs = refs[shards + 3 : shards + 3 + sends], refs[shards + 3 + sends :]
-    if not late:
-        coef_ref, refs = refs[0], refs[1:]
-    columns, blocks, sums, entries, block_sem = refs
+    used = LATE if late else shards
+    shard_refs, (own_ref, mate_hbm), refs = refs[:shards], refs[shards : shards + 2], refs[shards + 2 :]
+    if late:
+        sums, coef_ref, send_refs, refs = refs[1], refs[2], refs[3 : 3 + sends], refs[3 + sends :]
+    else:
+        sums, refs = refs[0], refs[1:]
+    columns, blocks, block_sem = refs
+    stored = blocks.shape[0]
     directions = sums.shape[1]
-    span = columns.shape[0] // shards
+    span = columns.shape[0] // used
     dummy = sums.shape[0] - 1
-
-    begin, begin_there = list_ref[3, late], list_ref[11, 2 + late]
-    here = list_ref[3, late + 1] - begin
-    total = here + list_ref[11, 3 + late] - begin_there
-    steps = (total + batch - 1) // batch
-
-    def fetch(source, row, shift, swap):
-        def one(j, carry):
-            at = j + shift
-            pltpu.make_async_copy(
-                source.at[list_ref[row, at]], blocks.at[j], block_sem.at[j // batch]
-            ).start()
-            entries[0, j] = list_ref[row + 1, at] ^ swap
-            entries[1, j] = list_ref[row + 2, at] * directions
-            return carry
-
-        return one
-
-    def fill(j, carry):
-        pltpu.make_async_copy(own_hbm.at[0], blocks.at[j], block_sem.at[j // batch]).start()
-        entries[0, j] = dummy
-        entries[1, j] = 0
+    chunk = stored // CHUNKS
+
+    begin, end = list_ref[3, late], list_ref[3, late + 1]
+    begin_there, end_there = list_ref[11, 2 + late], list_ref[11, 3 + late]
+    steps_there = (end_there - begin_there + batch - 1) // batch
+
+    def fetch(j, carry):
+        at = jnp.minimum(begin_there + j, end_there - 1)
+        pltpu.make_async_copy(
+            mate_hbm.at[list_ref[8, at]], blocks.at[j], block_sem.at[j // batch]
+        ).start()
         return carry
 
-    lax.fori_loop(0, here, fetch(own_hbm, 0, begin, 0), 0)
-    lax.fori_loop(here, total, fetch(mate_hbm, 8, begin_there - here, dummy // 2), 0)
-    lax.fori_loop(total, steps * batch, fill, 0)
-
-    for k, ref in enumerate(shard_refs):
+    if late:
+        lax.fori_loop(0, steps_there * batch, fetch, 0)
+    else:
+        for c in range(CHUNKS):
+            at = pl.ds(c * chunk, chunk)
+            pltpu.make_async_copy(mate_hbm.at[at], blocks.at[at], block_sem.at[c]).start()
+
+    for k, ref in enumerate(shard_refs[shards - used :]):
 
         def gather(i, carry, k=k, ref=ref):
             at = pl.multiple_of(i * directions, directions)
@@ -220,50 +215,75 @@
             return carry
 
         lax.fori_loop(0, span // directions, gather, 0, unroll=4)
-        if not late:
-            tail = coef_ref.shape[0] // shards
+    if late:
+        tail = coef_ref.shape[0] // shards
+        for k, ref in enumerate(shard_refs):
             coef_ref[k * tail : (k + 1) * tail] = ref[span : span + tail]
-
-    def clear(i, carry):
-        sums[i] = jnp.zeros(sums.shape[1:], sums.dtype)
+    else:
+
+        def clear(i, carry):
+            sums[i] = jnp.zeros(sums.shape[1:], sums.dtype)
+            return carry
+
+        lax.fori_loop(0, dummy + 1, clear, 0)
+
+    def run(begin, end, row, swap, block_of):
+        def entry(j):
+            return jnp.minimum(begin + j, end - 1)
+
+        def body(step, carry):
+            first = step * batch
+            products = []
+
+            def add(i):
+                place = list_ref[row + 1, entry(first + i)] ^ swap
+                place = jnp.where(begin + first + i < end, place, dummy)
+                sums[place] = sums[place] + products[i]
+
+            take, carry = block_of(first, entry, carry)
+            for i in range(batch):
+                start = list_ref[row + 2, entry(first + i)] * directions - (shards - used) * span
+                products.append(
+                    lax.dot_general(
+                        columns[pl.ds(pl.multiple_of(start, directions), directions)],
+                        take(i),
+                        (((1,), (1,)), ((), ())),
+                        preferred_element_type=jnp.float32,
+                    )
+                )
+                if i >= lag:
+                    add(i - lag)
+            for i in range(batch - lag, batch):
+                add(i)
+            return carry
+
+        return lax.fori_loop(0, (end - begin + batch - 1) // batch, body, 0)
+
+    def own_blocks(first, entry, carry):
+        return lambda i: own_ref[list_ref[0, entry(first + i)]], carry
+
+    def wait(c, carry):
+        at = pl.ds(0, chunk)
+        pltpu.make_async_copy(mate_hbm.at[at], blocks.at[at], block_sem.at[c]).wait()
         return carry
 
-    lax.fori_loop(0, dummy, clear, 0)
-
-    def body(step, carry):
-        first = step * batch
-        pltpu.make_async_copy(
-            own_hbm.at[pl.ds(0, batch)], blocks.at[pl.ds(first, batch)], block_sem.at[step]
-        ).wait()
-        products = []
-
-        def add(i):
-            place = entries[0, first + i]
-            sums[place] = sums[place] + products[i]
-
-        for i in range(batch):
-            start = pl.multiple_of(entries[1, first + i], directions)
-            products.append(
-                lax.dot_general(
-                    columns[pl.ds(start, directions)],
-                    blocks[first + i],
-                    (((1,), (1,)), ((), ())),
-                    preferred_element_type=jnp.float32,
-                )
-            )
-            if i >= lag:
-                add(i - lag)
-        for i in range(batch - lag, batch):
-            add(i)
-        return carry
-
-    lax.fori_loop(0, steps, body, 0)
-
-    def keep(i, carry):
-        keep_ref[i] = sums[i]
-        return carry
-
-    lax.fori_loop(0, dummy // 2, keep, 0, unroll=2)
+    def mate_blocks(first, entry, ready):
+        if late:
+            pltpu.make_async_copy(
+                mate_hbm.at[pl.ds(0, batch)],
+                blocks.at[pl.ds(first, batch)],
+                block_sem.at[first // batch],
+            ).wait()
+            return lambda i: blocks[first + i], ready
+        needed = list_ref[8, entry(first + batch - 1)] // chunk + 1
+        lax.fori_loop(ready, needed, wait, 0)
+        return lambda i: blocks[list_ref[8, entry(first + i)]], jnp.maximum(ready, needed)
+
+    run(begin, end, 0, 0, own_blocks)
+    ready = run(begin_there, end_there, 8, dummy // 2, mate_blocks)
+    if not late:
+        lax.fori_loop(ready, CHUNKS, wait, 0)
+        return
     at = dummy // 2
     for send_ref in send_refs:
 
@@ -439,38 +459,38 @@
         if k < chips - 2:
             flow[x] = move(flow[x], ahead)
 
-    quarter = chips // 2
-
-    def near(late, lists):
-        pieces = [1] * quarter
-        kept, *sends = pl.pallas_call(
-            functools.partial(near_kernel, late, BATCH, LAG, chips, len(pieces)),
-            out_shape=[
-                jax.ShapeDtypeStruct((quarter * clusters, directions, unknowns), jnp.float32)
-            ]
+    pieces = [1, 1, chips - 2]
+    sums_shape = jax.ShapeDtypeStruct((count * clusters + 1, directions, unknowns), jnp.float32)
+
+    def near(late, shards, *sums):
+        sends = pieces if late else []
+        return pl.pallas_call(
+            functools.partial(near_kernel, late, BATCH, LAG, len(shards), len(sends)),
+            out_shape=[sums_shape]
+            + [jax.ShapeDtypeStruct((chips * half * rank_k, unknowns), jnp.bfloat16)] * late
             + [
                 jax.ShapeDtypeStruct((part * clusters, directions, unknowns), jnp.bfloat16)
-                for part in pieces
-            ]
-            + [jax.ShapeDtypeStruct((chips * half * rank_k, unknowns), jnp.bfloat16)] * (1 - late),
-            in_specs=[whole(pltpu.SMEM)] + [whole()] * chips + [whole(pl.ANY)] * 2,
-            out_specs=[whole()] * (2 + len(pieces) - late),
+                for part in sends
+            ],
+            in_specs=[whole(pltpu.SMEM)]
+            + [whole()] * len(shards)
+            + [whole(), whole(pl.ANY)]
+            + [whole()] * late,
+            out_specs=[whole()] * (1 + late + len(sends)),
+            input_output_aliases={len(shards) + 3: 0} if late else {},
             scratch_shapes=[
-                pltpu.VMEM((chips * base, unknowns), jnp.bfloat16),
-                pltpu.VMEM((2 * stored, unknowns, unknowns), jnp.bfloat16),
-                pltpu.VMEM((2 * quarter * clusters + 1, directions, unknowns), jnp.float32),
-                pltpu.SMEM((2, 2 * stored), jnp.int32),
-                pltpu.SemaphoreType.DMA((2 * stored // BATCH,)),
+                pltpu.VMEM(((LATE if late else len(shards)) * base, unknowns), jnp.bfloat16),
+                pltpu.VMEM(near_blocks.shape, jnp.bfloat16),
+                pltpu.SemaphoreType.DMA((max(CHUNKS, stored // BATCH),)),
             ],
-            compiler_params=pltpu.CompilerParams(vmem_limit_bytes=NEAR_VMEM),
+            compiler_params=pltpu.CompilerParams(vmem_limit_bytes=NEAR_VMEM[late]),
             cost_estimate=pl.CostEstimate(
                 flops=16 * stored * directions * unknowns * unknowns,
                 bytes_accessed=16 << 20,
                 transcendentals=0,
             ),
             name="near",
-        )(lists, *shards, near_blocks, mate_blocks)
-        return kept, sends
+        )(lists, *shards, near_blocks, mate_blocks, *sums)
 
     def far_field(couple):
         return pl.pallas_call(
@@ -495,29 +515,26 @@
             basis_out,
         )
 
-    early, (*sends, coef) = near(0, lists)
+    (sums,) = near(0, shards[: chips - LATE])
+    sums, coef, *sends = near(1, shards, sums)
     mates = [move(sends[0], mate), move(sends[1], mate)]
     coefs = [coef, move(coef, mate)]
-    kept = [early]
 
     def term(k):
-        at = k % quarter * clusters
-        return kept[k // quarter][at : at + clusters] + mates[k].astype(jnp.float32)
+        part = min(k, 2)
+        got = mates[part][(k - part) * clusters : (k - part + 1) * clusters]
+        return sums[k * clusters : (k + 1) * clusters] + got.astype(jnp.float32)
 
     def tied(values, k, *others):
-        values, mates[k + 1], *others = lax.optimization_barrier((values, mates[k + 1], *others))
+        values, mates[2], *others = lax.optimization_barrier((values, mates[2], *others))
         return values
 
     def add(flow, k):
         return (flow.astype(jnp.float32) + term(k)).astype(jnp.bfloat16)
 
     flow = lax.optimization_barrier([term(0).astype(jnp.bfloat16), term(1).astype(jnp.bfloat16)])
-    lists = after(lists, *flow)
-    mates += [move(after(send, *flow), mate) for send in sends[2:]]
+    mates.append(move(after(sends[2], *flow), mate))
     flow = [move(part, ahead) for part in flow]
-    late, sends = near(1, lists)
-    kept.append(late)
-    mates += [move(send, mate) for send in sends]
     for k in range(2, chips - 1):
         x = k % 2
         flow[x] = tied(add(flow[x], k), k)

time: 71.3 us -> 68.4 us (0.959)
  waiting for transfers between devices: 24 us -> 16.3 us
  starting transfers between devices: 27 us -> 31.7 us
  Pallas kernels: 15.9 us -> 13.6 us
  local copies, waits for them, and re-layouts: 0.97 us -> 3.15 us
    ppermute x27 -> x22, waiting for transfers between devices: 24 us -> 16.3 us  [move(): return lax.ppermute(values, 'blk', where)]
    ppermute x27 -> x22, starting transfers between devices: 27 us -> 31.7 us  [move(): return lax.ppermute(values, 'blk', where)]
    pallas_call x2, Pallas kernels: 11.4 us -> 9.12 us  [near(): pl.pallas_call(functools.partial(near_kernel, late, BATCH, LAG, len(shard...]
    unnamed x9 -> x11, local copies, waits for them, and re-layouts: 0.97 us -> 3.15 us
  transfers between devices with their start and end apart: 27 -> 22, of which waited for: 14 -> 14; matrix products, arithmetic and copies ran while one was open for 3% -> 3% of each run, Pallas kernels for 13% -> 16%
where the time goes in v15:
time: 68.4 us; the launch traced here: 67.2 us
  starting transfers between devices  31.7 us (46%)
  waiting for transfers between devices  16.3 us (24%)
  Pallas kernels  13.6 us (20%)
  local copies, waits for them, and re-layouts  3.15 us (5%)
  other arithmetic  2.33 us (3%)
    ppermute x22, starting transfers between devices, move(): return lax.ppermute(values, 'blk', where)  31.7 us
    ppermute x22, waiting for transfers between devices, move(): return lax.ppermute(values, 'blk', where)  16.3 us
    pallas_call x2, Pallas kernels, near(): pl.pallas_call(functools.partial(near_kernel, late, BATCH, LAG, len(shard...  9.12 us
    unnamed x11, local copies, waits for them, and re-layouts  3.15 us
    pallas_call x1, Pallas kernels, far_field(): pl.pallas_call(far_kernel, out_shape=jax.ShapeDtypeStruct((clusters, dire...  2.5 us
    pallas_call x1, Pallas kernels, stationary(): pl.pallas_call(functools.partial(prologue_kernel, count), out_shape=[jax....  2.01 us
  transfers between devices with their start and end apart: 22, of which 14 were waited for; matrix products, arithmetic and copies ran while one was open for 3% of the time, Pallas kernels for 16%

profile of v15, /device:TPU:0, one launch (start us, length us, event | category | flops | bytes accessed | tf_op | source)
XLA Modules:
  0.0 67.2 jit_solution(9173841329009748894)
XLA Ops:
  0.5 2.0 %prologue.1 = (bf16[1152,128]{1,0:T(8,128)(2,1)}, s32[8,128]{1,0:T(8,128)}) custom-call(s32[1]{0:T(128)} %bitcast.me_ref.refs_2_, s32[1,128]{1,0:T(1,128)} %bitcast.14, s32[1,128]{1,0:T(1,128)} %bitcast.15, s32[1,128]{1,0:T(1,128)} %bitcast.16, bf16[16,64,128]{2,1,0:T(8,128)(2,1)} %rhs_ref.1, bf16[16,16,128]{2,1,0:T(8,128)(2,1)} %basis_ref.1), custom_call_target="tpu_custom_call" | custom-call | tf_op jit(solution)/shard_map/prologue/pallas_call | solution.py:428
  2.5 2.6 %collective-permute-start = (bf16[1152,128]{1,0:T(8,128)(2,1)}, bf16[1152,128]{1,0:T(8,128)(2,1)S(1)}, u32[]{:S(2)}, u32[]{:S(2)}) collective-permute-start(bf16[1152,128]{1,0:T(8,128)(2,1)} %get-tuple-element.35), channel_id=1, source_target_pairs={{0,4},{1,3},{4,8},{5,1},{8,12},{9,5},{12,14},{13,9},{14,10},{15,13... | collective-permute-start | bytes 884744 | tf_op jit(solution)/shard_map/ppermute | solution.py:421
  5.0 0.9 %copy.15 = bf16[256,16,16]{0,1,2:T(8,128)(2,1)S(1)} copy(bf16[256,16,16]{0,2,1:T(8,128)(2,1)} %param.16) | data formatting | bytes 262144 | tf_op args[5]
  6.0 1.4 %collective-permute-start.5 = (bf16[1152,128]{1,0:T(8,128)(2,1)}, bf16[1152,128]{1,0:T(8,128)(2,1)S(1)}, u32[]{:S(2)}, u32[]{:S(2)}) collective-permute-start(bf16[1152,128]{1,0:T(8,128)(2,1)} %get-tuple-element.35), channel_id=1, source_target_pairs={{0,3},{1,4},{4,1},{5,8},{8,5},{9,12},{12,9},{13,14},{14,13},{15,10... | collective-permute-start | bytes 884744 | tf_op jit(solution)/shard_map/ppermute | solution.py:421
  7.7 2.9 %collective-permute-done.refs_1_ = bf16[1152,128]{1,0:T(8,128)(2,1)S(1)} collective-permute-done((bf16[1152,128]{1,0:T(8,128)(2,1)}, bf16[1152,128]{1,0:T(8,128)(2,1)S(1)}, u32[]{:S(2)}, u32[]{:S(2)}) %collective-permute-start) | collective-permute-done | bytes 294944 | tf_op jit(solution)/shard_map/ppermute | solution.py:421
  10.7 2.4 %collective-permute-start.1 = (bf16[1152,128]{1,0:T(8,128)(2,1)S(1)}, bf16[1152,128]{1,0:T(8,128)(2,1)S(1)}, u32[]{:S(2)}, u32[]{:S(2)}) collective-permute-start(bf16[1152,128]{1,0:T(8,128)(2,1)S(1)} %collective-permute-done.refs_1_), channel_id=1, source_target_pairs={{0,4},{1,3},{4,8},{5,1},{8,12},{9,5},{12,14},{13,9},{14,10},{15,13... | collective-permute-start | bytes 884744 | tf_op jit(solution)/shard_map/ppermute | solution.py:421
  13.1 1.4 %collective-permute-done.4 = s32[8,128]{1,0:T(8,128)S(1)} collective-permute-done((s32[8,128]{1,0:T(8,128)}, s32[8,128]{1,0:T(8,128)S(1)}, u32[]{:S(2)}, u32[]{:S(2)}) %collective-permute-start.4) | collective-permute-done | bytes 4128 | tf_op jit(solution)/shard_map/ppermute | solution.py:421
  14.4 0.7 %pad_add_fusion.list_ref = s32[16,128]{1,0:T(8,128)S(1)} fusion(s32[8,128]{1,0:T(8,128)S(1)} %collective-permute-done.4, s32[8,128]{1,0:T(8,128)} %get-tuple-element.32), kind=kLoop, calls=%fused_computation.10 | loop fusion | flops 2048 | bytes 16384 | tf_op jit(solution)/shard_map/concatenate | solution.py:448
  15.1 1.6 %collective-permute-start.6 = (bf16[1152,128]{1,0:T(8,128)(2,1)S(1)}, bf16[1152,128]{1,0:T(8,128)(2,1)S(1)}, u32[]{:S(2)}, u32[]{:S(2)}) collective-permute-start(bf16[1152,128]{1,0:T(8,128)(2,1)S(1)} %collective-permute-done.5.refs_2_), channel_id=1, source_target_pairs={{0,4},{1,3},{4,8},{5,1},{8,12},{9,5},{12,14},{13,9},{14,10},{15,13... | collective-permute-start | bytes 884744 | tf_op jit(solution)/shard_map/ppermute | solution.py:421
  16.7 1.3 %collective-permute-done.1.refs_3_ = bf16[1152,128]{1,0:T(8,128)(2,1)S(1)} collective-permute-done((bf16[1152,128]{1,0:T(8,128)(2,1)S(1)}, bf16[1152,128]{1,0:T(8,128)(2,1)S(1)}, u32[]{:S(2)}, u32[]{:S(2)}) %collective-permute-start.1) | collective-permute-done | bytes 294944 | tf_op jit(solution)/shard_map/ppermute | solution.py:421
  18.0 1.7 %collective-permute-start.7 = (bf16[1152,128]{1,0:T(8,128)(2,1)S(1)}, bf16[1152,128]{1,0:T(8,128)(2,1)S(1)}, u32[]{:S(2)}, u32[]{:S(2)}) collective-permute-start(bf16[1152,128]{1,0:T(8,128)(2,1)S(1)} %collective-permute-done.1.refs_3_), channel_id=1, source_target_pairs={{0,4},{1,3},{4,8},{5,1},{8,12},{9,5},{12,14},{13,9},{14,10},{15,13... | collective-permute-start | bytes 884744 | tf_op jit(solution)/shard_map/ppermute | solution.py:421
  19.8 2.1 %collective-permute-done.6.refs_4_ = bf16[1152,128]{1,0:T(8,128)(2,1)S(1)} collective-permute-done((bf16[1152,128]{1,0:T(8,128)(2,1)S(1)}, bf16[1152,128]{1,0:T(8,128)(2,1)S(1)}, u32[]{:S(2)}, u32[]{:S(2)}) %collective-permute-start.6) | collective-permute-done | bytes 294944 | tf_op jit(solution)/shard_map/ppermute | solution.py:421
  21.8 1.6 %collective-permute-start.8 = (bf16[1152,128]{1,0:T(8,128)(2,1)S(1)}, bf16[1152,128]{1,0:T(8,128)(2,1)S(1)}, u32[]{:S(2)}, u32[]{:S(2)}) collective-permute-start(bf16[1152,128]{1,0:T(8,128)(2,1)S(1)} %collective-permute-done.6.refs_4_), channel_id=1, source_target_pairs={{0,4},{1,3},{4,8},{5,1},{8,12},{9,5},{12,14},{13,9},{14,10},{15,13... | collective-permute-start | bytes 884744 | tf_op jit(solution)/shard_map/ppermute | solution.py:421
  23.4 1.6 %collective-permute-done.7.refs_5_ = bf16[1152,128]{1,0:T(8,128)(2,1)S(1)} collective-permute-done((bf16[1152,128]{1,0:T(8,128)(2,1)S(1)}, bf16[1152,128]{1,0:T(8,128)(2,1)S(1)}, u32[]{:S(2)}, u32[]{:S(2)}) %collective-permute-start.7) | collective-permute-done | bytes 294944 | tf_op jit(solution)/shard_map/ppermute | solution.py:421
  25.0 1.6 %collective-permute-start.9 = (bf16[1152,128]{1,0:T(8,128)(2,1)S(1)}, bf16[1152,128]{1,0:T(8,128)(2,1)S(1)}, u32[]{:S(2)}, u32[]{:S(2)}) collective-permute-start(bf16[1152,128]{1,0:T(8,128)(2,1)S(1)} %collective-permute-done.7.refs_5_), channel_id=1, source_target_pairs={{0,4},{1,3},{4,8},{5,1},{8,12},{9,5},{12,14},{13,9},{14,10},{15,13... | collective-permute-start | bytes 884744 | tf_op jit(solution)/shard_map/ppermute | solution.py:421
  26.6 2.2 %copy-done = bf16[128,128,128]{2,1,0:T(8,128)(2,1)S(1)} copy-done((bf16[128,128,128]{2,1,0:T(8,128)(2,1)S(1)}, bf16[128,128,128]{2,1,0:T(8,128)(2,1)}, u32[]{:S(2)}) %copy-start) | copy-done | bytes 4194328
  28.8 6.2 %near.2.refs_10_ = f32[257,64,128]{2,1,0:T(8,128)S(1)} custom-call(s32[16,128]{1,0:T(8,128)S(1)} %pad_add_fusion.list_ref, bf16[1152,128]{1,0:T(8,128)(2,1)S(1)} %collective-permute-done.3.refs_0_, bf16[1152,128]{1,0:T(8,128)(2,1)S(1)} %collective-permute-done.refs_1_, bf16[1152,128]{1,0:T(8,128)(2,1)S(1)} %collective-permute-done.5.refs_2_, ...), custom_call_target="tpu_custom_call" | custom-call | flops 2147483648 | bytes 16777216 | tf_op jit(solution)/shard_map/near/pallas_call | solution.py:467
  35.0 2.9 %near.3 = (f32[257,64,128]{2,1,0:T(8,128)S(1)}, bf16[1024,128]{1,0:T(8,128)(2,1)S(1)}, bf16[16,64,128]{2,1,0:T(8,128)(2,1)S(1)}, bf16[16,64,128]{2,1,0:T(8,128)(2,1)S(1)}, bf16[96,64,128]{2,1,0:T(8,128)(2,1)S(1)}) custom-call(s32[16,128]{1,0:T(8,128)S(1)} %pad_add_fusion.list_ref, ...), custom_call_target="tpu_custom_call", output_to_operand_aliasing={{0}: (11, {})} | custom-call | flops 2147483648 | bytes 16777216 | tf_op jit(solution)/shard_map/near/pallas_call | solution.py:467
  38.5 1.0 %collective-permute-done.11 = bf16[16,64,128]{2,1,0:T(8,128)(2,1)S(1)} collective-permute-done((bf16[16,64,128]{2,1,0:T(8,128)(2,1)S(1)}, bf16[16,64,128]{2,1,0:T(8,128)(2,1)S(1)}, u32[]{:S(2)}, u32[]{:S(2)}) %collective-permute-start.11) | collective-permute-done | bytes 262176 | tf_op jit(solution)/shard_map/ppermute | solution.py:421
  40.3 1.6 %collective-permute-start.13 = (bf16[16,64,128]{2,1,0:T(8,128)(2,1)S(1)}, bf16[16,64,128]{2,1,0:T(8,128)(2,1)S(1)}, u32[]{:S(2)}, u32[]{:S(2)}) collective-permute-start(bf16[16,64,128]{2,1,0:T(8,128)(2,1)S(1)} %get-tuple-element.42), channel_id=1, source_target_pairs={{0,4},{1,3},{4,8},{5,1},{8,12},{9,5},{12,14},{13,9},{14,10},{15,13... | collective-permute-start | bytes 786440 | tf_op jit(solution)/shard_map/ppermute | solution.py:421
  41.9 3.3 %collective-permute-start.16 = (bf16[16,64,128]{2,1,0:T(8,128)(2,1)S(1)}, bf16[16,64,128]{2,1,0:T(8,128)(2,1)S(1)}, u32[]{:S(2)}, u32[]{:S(2)}) collective-permute-start(bf16[16,64,128]{2,1,0:T(8,128)(2,1)S(1)} %get-tuple-element.44), channel_id=1, source_target_pairs={{0,4},{1,3},{4,8},{5,1},{8,12},{9,5},{12,14},{13,9},{14,10},{15,13... | collective-permute-start | bytes 786440 | tf_op jit(solution)/shard_map/ppermute | solution.py:421
  45.2 1.5 %collective-permute-done.13 = bf16[16,64,128]{2,1,0:T(8,128)(2,1)S(1)} collective-permute-done((bf16[16,64,128]{2,1,0:T(8,128)(2,1)S(1)}, bf16[16,64,128]{2,1,0:T(8,128)(2,1)S(1)}, u32[]{:S(2)}, u32[]{:S(2)}) %collective-permute-start.13) | collective-permute-done | bytes 262176 | tf_op jit(solution)/shard_map/ppermute | solution.py:421
  46.8 2.5 %collective-permute-start.15 = (bf16[16,64,128]{2,1,0:T(8,128)(2,1)S(1)}, bf16[16,64,128]{2,1,0:T(8,128)(2,1)S(1)}, u32[]{:S(2)}, u32[]{:S(2)}) collective-permute-start(bf16[16,64,128]{2,1,0:T(8,128)(2,1)S(1)} %add_convert_fusion.5), channel_id=1, source_target_pairs={{0,4},{1,3},{4,8},{5,1},{8,12},{9,5},{12,14},{13,9},{14,10},{15,13... | collective-permute-start | bytes 786440 | tf_op jit(solution)/shard_map/ppermute | solution.py:421
  49.6 2.5 %collective-permute-start.18 = (bf16[16,64,128]{2,1,0:T(8,128)(2,1)S(1)}, bf16[16,64,128]{2,1,0:T(8,128)(2,1)S(1)}, u32[]{:S(2)}, u32[]{:S(2)}) collective-permute-start(bf16[16,64,128]{2,1,0:T(8,128)(2,1)S(1)} %add_convert_fusion.4), channel_id=1, source_target_pairs={{0,4},{1,3},{4,8},{5,1},{8,12},{9,5},{12,14},{13,9},{14,10},{15,13... | collective-permute-start | bytes 786440 | tf_op jit(solution)/shard_map/ppermute | solution.py:421
  52.0 1.2 %collective-permute-done.15 = bf16[16,64,128]{2,1,0:T(8,128)(2,1)S(1)} collective-permute-done((bf16[16,64,128]{2,1,0:T(8,128)(2,1)S(1)}, bf16[16,64,128]{2,1,0:T(8,128)(2,1)S(1)}, u32[]{:S(2)}, u32[]{:S(2)}) %collective-permute-start.15) | collective-permute-done | bytes 262176 | tf_op jit(solution)/shard_map/ppermute | solution.py:421
  53.3 2.5 %collective-permute-start.17 = (bf16[16,64,128]{2,1,0:T(8,128)(2,1)S(1)}, bf16[16,64,128]{2,1,0:T(8,128)(2,1)S(1)}, u32[]{:S(2)}, u32[]{:S(2)}) collective-permute-start(bf16[16,64,128]{2,1,0:T(8,128)(2,1)S(1)} %add_convert_fusion.3), channel_id=1, source_target_pairs={{0,4},{1,3},{4,8},{5,1},{8,12},{9,5},{12,14},{13,9},{14,10},{15,13... | collective-permute-start | bytes 786440 | tf_op jit(solution)/shard_map/ppermute | solution.py:421
  56.1 2.5 %collective-permute-start.20 = (bf16[16,64,128]{2,1,0:T(8,128)(2,1)S(1)}, bf16[16,64,128]{2,1,0:T(8,128)(2,1)S(1)}, u32[]{:S(2)}, u32[]{:S(2)}) collective-permute-start(bf16[16,64,128]{2,1,0:T(8,128)(2,1)S(1)} %add_convert_fusion.2), channel_id=1, source_target_pairs={{0,4},{1,3},{4,8},{5,1},{8,12},{9,5},{12,14},{13,9},{14,10},{15,13... | collective-permute-start | bytes 786440 | tf_op jit(solution)/shard_map/ppermute | solution.py:421
  58.6 1.2 %collective-permute-done.17 = bf16[16,64,128]{2,1,0:T(8,128)(2,1)S(1)} collective-permute-done((bf16[16,64,128]{2,1,0:T(8,128)(2,1)S(1)}, bf16[16,64,128]{2,1,0:T(8,128)(2,1)S(1)}, u32[]{:S(2)}, u32[]{:S(2)}) %collective-permute-start.17) | collective-permute-done | bytes 262176 | tf_op jit(solution)/shard_map/ppermute | solution.py:421
  59.9 2.5 %collective-permute-start.19 = (bf16[16,64,128]{2,1,0:T(8,128)(2,1)S(1)}, bf16[16,64,128]{2,1,0:T(8,128)(2,1)S(1)}, u32[]{:S(2)}, u32[]{:S(2)}) collective-permute-start(bf16[16,64,128]{2,1,0:T(8,128)(2,1)S(1)} %add_convert_fusion.1), channel_id=1, source_target_pairs={{0,4},{1,3},{4,8},{5,1},{8,12},{9,5},{12,14},{13,9},{14,10},{15,13... | collective-permute-start | bytes 786440 | tf_op jit(solution)/shard_map/ppermute | solution.py:421
  62.7 2.5 %far.1 = f32[16,64,128]{2,1,0:T(8,128)S(1)} custom-call(bf16[1024,128]{1,0:T(8,128)(2,1)S(1)} %get-tuple-element.38.refs_0_, bf16[1024,128]{1,0:T(8,128)(2,1)S(1)} %collective-permute-done.10.refs_1_, s32[1]{0:T(128)} %bitcast.me_ref.refs_2_, bf16[16,16,256]{2,1,0:T(8,128)(2,1)S(1)} %bitcast.10, s32[1,256]{1,0:T(1,128)S(1)} %bitcast.11, ...), custom_call_target="tpu_custom_call" | custom-call | flops 536870912 | bytes 8388608 | tf_op jit(solution)/shard_map/far/pallas_call | solution.py:496
  65.2 1.1 %collective-permute-done.19 = bf16[16,64,128]{2,1,0:T(8,128)(2,1)S(1)} collective-permute-done((bf16[16,64,128]{2,1,0:T(8,128)(2,1)S(1)}, bf16[16,64,128]{2,1,0:T(8,128)(2,1)S(1)}, u32[]{:S(2)}, u32[]{:S(2)}) %collective-permute-start.19) | collective-permute-done | bytes 262176 | tf_op jit(solution)/shard_map/ppermute | solution.py:421
  66.4 0.8 %add_convert_fusion = bf16[16,64,128]{2,1,0:T(8,128)(2,1)} fusion(f32[16,64,128]{2,1,0:T(8,128)S(1)} %convert_add_fusion, bf16[16,64,128]{2,1,0:T(8,128)(2,1)S(1)} %collective-permute-done.21), kind=kLoop, calls=%fused_computation | loop fusion | flops 393216 | bytes 1048576 | tf_op jit(solution)/shard_map/convert_element_type | solution.py:547
  (36 shorter events, 3.7 us)
Async XLA Ops:
  0.0 18.0 %collective-permute-start.2 = (bf16[128,128,128]{2,1,0:T(8,128)(2,1)}, bf16[128,128,128]{2,1,0:T(8,128)(2,1)}, u32[]{:S(2)}, u32[]{:S(2)}) collective-permute-start(bf16[128,128,128]{2,1,0:T(8,128)(2,1)} %refs_8_.1), channel_id=1, source_target_pairs={{0,1},{1,0},{2,3},{3,2},{4,5},{5,4},{6,7},{7,6},{8,9},{9,8},{10,11... | collective-permute-start | bytes 12582920 | tf_op jit(solution)/shard_map/ppermute | solution.py:421
  2.5 8.2 %collective-permute-start = (bf16[1152,128]{1,0:T(8,128)(2,1)}, bf16[1152,128]{1,0:T(8,128)(2,1)S(1)}, u32[]{:S(2)}, u32[]{:S(2)}) collective-permute-start(bf16[1152,128]{1,0:T(8,128)(2,1)} %get-tuple-element.35), channel_id=1, source_target_pairs={{0,4},{1,3},{4,8},{5,1},{8,12},{9,5},{12,14},{13,9},{14,10},{15,13... | collective-permute-start | bytes 884744 | tf_op jit(solution)/shard_map/ppermute | solution.py:421
  6.0 9.1 %collective-permute-start.5 = (bf16[1152,128]{1,0:T(8,128)(2,1)}, bf16[1152,128]{1,0:T(8,128)(2,1)S(1)}, u32[]{:S(2)}, u32[]{:S(2)}) collective-permute-start(bf16[1152,128]{1,0:T(8,128)(2,1)} %get-tuple-element.35), channel_id=1, source_target_pairs={{0,3},{1,4},{4,1},{5,8},{8,5},{9,12},{12,9},{13,14},{14,13},{15,10... | collective-permute-start | bytes 884744 | tf_op jit(solution)/shard_map/ppermute | solution.py:421
  7.4 9.3 %collective-permute-start.3 = (bf16[1152,128]{1,0:T(8,128)(2,1)}, bf16[1152,128]{1,0:T(8,128)(2,1)S(1)}, u32[]{:S(2)}, u32[]{:S(2)}) collective-permute-start(bf16[1152,128]{1,0:T(8,128)(2,1)} %get-tuple-element.35), channel_id=1, source_target_pairs={{0,1},{1,0},{2,3},{3,2},{4,5},{5,4},{6,7},{7,6},{8,9},{9,8},{10,11... | collective-permute-start | bytes 884744 | tf_op jit(solution)/shard_map/ppermute | solution.py:421
  10.7 7.4 %collective-permute-start.1 = (bf16[1152,128]{1,0:T(8,128)(2,1)S(1)}, bf16[1152,128]{1,0:T(8,128)(2,1)S(1)}, u32[]{:S(2)}, u32[]{:S(2)}) collective-permute-start(bf16[1152,128]{1,0:T(8,128)(2,1)S(1)} %collective-permute-done.refs_1_), channel_id=1, source_target_pairs={{0,4},{1,3},{4,8},{5,1},{8,12},{9,5},{12,14},{13,9},{14,10},{15,13... | collective-permute-start | bytes 884744 | tf_op jit(solution)/shard_map/ppermute | solution.py:421
  13.1 1.4 %collective-permute-start.4 = (s32[8,128]{1,0:T(8,128)}, s32[8,128]{1,0:T(8,128)S(1)}, u32[]{:S(2)}, u32[]{:S(2)}) collective-permute-start(s32[8,128]{1,0:T(8,128)} %get-tuple-element.32), channel_id=1, source_target_pairs={{0,1},{1,0},{2,3},{3,2},{4,5},{5,4},{6,7},{7,6},{8,9},{9,8},{10,11... | collective-permute-start | bytes 12296 | tf_op jit(solution)/shard_map/ppermute | solution.py:421
  15.1 6.7 %collective-permute-start.6 = (bf16[1152,128]{1,0:T(8,128)(2,1)S(1)}, bf16[1152,128]{1,0:T(8,128)(2,1)S(1)}, u32[]{:S(2)}, u32[]{:S(2)}) collective-permute-start(bf16[1152,128]{1,0:T(8,128)(2,1)S(1)} %collective-permute-done.5.refs_2_), channel_id=1, source_target_pairs={{0,4},{1,3},{4,8},{5,1},{8,12},{9,5},{12,14},{13,9},{14,10},{15,13... | collective-permute-start | bytes 884744 | tf_op jit(solution)/shard_map/ppermute | solution.py:421
  18.0 7.0 %collective-permute-start.7 = (bf16[1152,128]{1,0:T(8,128)(2,1)S(1)}, bf16[1152,128]{1,0:T(8,128)(2,1)S(1)}, u32[]{:S(2)}, u32[]{:S(2)}) collective-permute-start(bf16[1152,128]{1,0:T(8,128)(2,1)S(1)} %collective-permute-done.1.refs_3_), channel_id=1, source_target_pairs={{0,4},{1,3},{4,8},{5,1},{8,12},{9,5},{12,14},{13,9},{14,10},{15,13... | collective-permute-start | bytes 884744 | tf_op jit(solution)/shard_map/ppermute | solution.py:421
  21.8 13.2 %collective-permute-start.8 = (bf16[1152,128]{1,0:T(8,128)(2,1)S(1)}, bf16[1152,128]{1,0:T(8,128)(2,1)S(1)}, u32[]{:S(2)}, u32[]{:S(2)}) collective-permute-start(bf16[1152,128]{1,0:T(8,128)(2,1)S(1)} %collective-permute-done.6.refs_4_), channel_id=1, source_target_pairs={{0,4},{1,3},{4,8},{5,1},{8,12},{9,5},{12,14},{13,9},{14,10},{15,13... | collective-permute-start | bytes 884744 | tf_op jit(solution)/shard_map/ppermute | solution.py:421
  25.0 10.0 %collective-permute-start.9 = (bf16[1152,128]{1,0:T(8,128)(2,1)S(1)}, bf16[1152,128]{1,0:T(8,128)(2,1)S(1)}, u32[]{:S(2)}, u32[]{:S(2)}) collective-permute-start(bf16[1152,128]{1,0:T(8,128)(2,1)S(1)} %collective-permute-done.7.refs_5_), channel_id=1, source_target_pairs={{0,4},{1,3},{4,8},{5,1},{8,12},{9,5},{12,14},{13,9},{14,10},{15,13... | collective-permute-start | bytes 884744 | tf_op jit(solution)/shard_map/ppermute | solution.py:421
  26.6 2.2 %copy-start = (bf16[128,128,128]{2,1,0:T(8,128)(2,1)S(1)}, bf16[128,128,128]{2,1,0:T(8,128)(2,1)}, u32[]{:S(2)}) copy-start(bf16[128,128,128]{2,1,0:T(8,128)(2,1)} %refs_8_.1) | copy-start | bytes 12582916
  37.9 1.6 %collective-permute-start.11 = (bf16[16,64,128]{2,1,0:T(8,128)(2,1)S(1)}, bf16[16,64,128]{2,1,0:T(8,128)(2,1)S(1)}, u32[]{:S(2)}, u32[]{:S(2)}) collective-permute-start(bf16[16,64,128]{2,1,0:T(8,128)(2,1)S(1)} %get-tuple-element.40), channel_id=1, source_target_pairs={{0,1},{1,0},{2,3},{3,2},{4,5},{5,4},{6,7},{7,6},{8,9},{9,8},{10,11... | collective-permute-start | bytes 786440 | tf_op jit(solution)/shard_map/ppermute | solution.py:421
  38.0 1.9 %collective-permute-start.12 = (bf16[16,64,128]{2,1,0:T(8,128)(2,1)S(1)}, bf16[16,64,128]{2,1,0:T(8,128)(2,1)S(1)}, u32[]{:S(2)}, u32[]{:S(2)}) collective-permute-start(bf16[16,64,128]{2,1,0:T(8,128)(2,1)S(1)} %get-tuple-element.41), channel_id=1, source_target_pairs={{0,1},{1,0},{2,3},{3,2},{4,5},{5,4},{6,7},{7,6},{8,9},{9,8},{10,11... | collective-permute-start | bytes 786440 | tf_op jit(solution)/shard_map/ppermute | solution.py:421
  39.9 22.8 %copy-start.1 = (bf16[16,16,128]{2,1,0:T(8,128)(2,1)S(1)}, bf16[16,16,128]{2,1,0:T(8,128)(2,1)}, u32[]{:S(2)}) copy-start(bf16[16,16,128]{2,1,0:T(8,128)(2,1)} %refs_7_.1) | copy-start | bytes 196612
  39.9 22.8 %copy-start.2 = (s32[256]{0:T(256)S(1)}, s32[256]{0:T(256)}, u32[]{:S(2)}) copy-start(s32[256]{0:T(256)} %param.17) | copy-start | bytes 3076
  39.9 22.8 %copy-start.3 = (s32[256,1]{0,1:T(1,128)S(1)}, s32[256,1]{0,1:T(1,128)}, u32[]{:S(2)}) copy-start(s32[256,1]{0,1:T(1,128)} %param.18) | copy-start | bytes 3076
  39.9 22.8 %copy-start.4 = (s32[256]{0:T(256)S(1)}, s32[256]{0:T(256)}, u32[]{:S(2)}) copy-start(s32[256]{0:T(256)} %param.19) | copy-start | bytes 3076
  40.1 6.6 %collective-permute-start.14 = (bf16[96,64,128]{2,1,0:T(8,128)(2,1)S(1)}, bf16[96,64,128]{2,1,0:T(8,128)(2,1)S(1)}, u32[]{:S(2)}, u32[]{:S(2)}) collective-permute-start(bf16[96,64,128]{2,1,0:T(8,128)(2,1)S(1)} %get-tuple-element.45), channel_id=1, source_target_pairs={{0,1},{1,0},{2,3},{3,2},{4,5},{5,4},{6,7},{7,6},{8,9},{9,8},{10,11... | collective-permute-start | bytes 4718600 | tf_op jit(solution)/shard_map/ppermute | solution.py:421
  40.3 6.4 %collective-permute-start.13 = (bf16[16,64,128]{2,1,0:T(8,128)(2,1)S(1)}, bf16[16,64,128]{2,1,0:T(8,128)(2,1)S(1)}, u32[]{:S(2)}, u32[]{:S(2)}) collective-permute-start(bf16[16,64,128]{2,1,0:T(8,128)(2,1)S(1)} %get-tuple-element.42), channel_id=1, source_target_pairs={{0,4},{1,3},{4,8},{5,1},{8,12},{9,5},{12,14},{13,9},{14,10},{15,13... | collective-permute-start | bytes 786440 | tf_op jit(solution)/shard_map/ppermute | solution.py:421
  41.9 7.6 %collective-permute-start.16 = (bf16[16,64,128]{2,1,0:T(8,128)(2,1)S(1)}, bf16[16,64,128]{2,1,0:T(8,128)(2,1)S(1)}, u32[]{:S(2)}, u32[]{:S(2)}) collective-permute-start(bf16[16,64,128]{2,1,0:T(8,128)(2,1)S(1)} %get-tuple-element.44), channel_id=1, source_target_pairs={{0,4},{1,3},{4,8},{5,1},{8,12},{9,5},{12,14},{13,9},{14,10},{15,13... | collective-permute-start | bytes 786440 | tf_op jit(solution)/shard_map/ppermute | solution.py:421
  46.8 6.4 %collective-permute-start.15 = (bf16[16,64,128]{2,1,0:T(8,128)(2,1)S(1)}, bf16[16,64,128]{2,1,0:T(8,128)(2,1)S(1)}, u32[]{:S(2)}, u32[]{:S(2)}) collective-permute-start(bf16[16,64,128]{2,1,0:T(8,128)(2,1)S(1)} %add_convert_fusion.5), channel_id=1, source_target_pairs={{0,4},{1,3},{4,8},{5,1},{8,12},{9,5},{12,14},{13,9},{14,10},{15,13... | collective-permute-start | bytes 786440 | tf_op jit(solution)/shard_map/ppermute | solution.py:421
  49.6 6.4 %collective-permute-start.18 = (bf16[16,64,128]{2,1,0:T(8,128)(2,1)S(1)}, bf16[16,64,128]{2,1,0:T(8,128)(2,1)S(1)}, u32[]{:S(2)}, u32[]{:S(2)}) collective-permute-start(bf16[16,64,128]{2,1,0:T(8,128)(2,1)S(1)} %add_convert_fusion.4), channel_id=1, source_target_pairs={{0,4},{1,3},{4,8},{5,1},{8,12},{9,5},{12,14},{13,9},{14,10},{15,13... | collective-permute-start | bytes 786440 | tf_op jit(solution)/shard_map/ppermute | solution.py:421
  53.3 6.4 %collective-permute-start.17 = (bf16[16,64,128]{2,1,0:T(8,128)(2,1)S(1)}, bf16[16,64,128]{2,1,0:T(8,128)(2,1)S(1)}, u32[]{:S(2)}, u32[]{:S(2)}) collective-permute-start(bf16[16,64,128]{2,1,0:T(8,128)(2,1)S(1)} %add_convert_fusion.3), channel_id=1, source_target_pairs={{0,4},{1,3},{4,8},{5,1},{8,12},{9,5},{12,14},{13,9},{14,10},{15,13... | collective-permute-start | bytes 786440 | tf_op jit(solution)/shard_map/ppermute | solution.py:421
  55.8 6.9 %collective-permute-start.10 = (bf16[1024,128]{1,0:T(8,128)(2,1)S(1)}, bf16[1024,128]{1,0:T(8,128)(2,1)S(1)}, u32[]{:S(2)}, u32[]{:S(2)}) collective-permute-start(bf16[1024,128]{1,0:T(8,128)(2,1)S(1)} %get-tuple-element.38.refs_0_), channel_id=1, source_target_pairs={{0,1},{1,0},{2,3},{3,2},{4,5},{5,4},{6,7},{7,6},{8,9},{9,8},{10,11... | collective-permute-start | bytes 786440 | tf_op jit(solution)/shard_map/ppermute | solution.py:421
  56.1 6.4 %collective-permute-start.20 = (bf16[16,64,128]{2,1,0:T(8,128)(2,1)S(1)}, bf16[16,64,128]{2,1,0:T(8,128)(2,1)S(1)}, u32[]{:S(2)}, u32[]{:S(2)}) collective-permute-start(bf16[16,64,128]{2,1,0:T(8,128)(2,1)S(1)} %add_convert_fusion.2), channel_id=1, source_target_pairs={{0,4},{1,3},{4,8},{5,1},{8,12},{9,5},{12,14},{13,9},{14,10},{15,13... | collective-permute-start | bytes 786440 | tf_op jit(solution)/shard_map/ppermute | solution.py:421
  59.9 6.4 %collective-permute-start.19 = (bf16[16,64,128]{2,1,0:T(8,128)(2,1)S(1)}, bf16[16,64,128]{2,1,0:T(8,128)(2,1)S(1)}, u32[]{:S(2)}, u32[]{:S(2)}) collective-permute-start(bf16[16,64,128]{2,1,0:T(8,128)(2,1)S(1)} %add_convert_fusion.1), channel_id=1, source_target_pairs={{0,4},{1,3},{4,8},{5,1},{8,12},{9,5},{12,14},{13,9},{14,10},{15,13... | collective-permute-start | bytes 786440 | tf_op jit(solution)/shard_map/ppermute | solution.py:421
  62.6 3.9 %collective-permute-start.21 = (bf16[16,64,128]{2,1,0:T(8,128)(2,1)S(1)}, bf16[16,64,128]{2,1,0:T(8,128)(2,1)S(1)}, u32[]{:S(2)}, u32[]{:S(2)}) collective-permute-start(bf16[16,64,128]{2,1,0:T(8,128)(2,1)S(1)} %collective-permute-done.20), channel_id=1, source_target_pairs={{0,1},{1,0},{2,3},{3,2},{4,5},{5,4},{6,7},{7,6},{8,9},{9,8},{10,11... | collective-permute-start | bytes 786440 | tf_op jit(solution)/shard_map/ppermute | solution.py:421

commit v16 on v15

--- a/solution.py
+++ b/solution.py
@@ -12,7 +12,7 @@
 LATE = 2
 LAG = 4
 PROLOGUE_VMEM = 58 << 20
-NEAR_VMEM = 20 << 20, 20 << 20
+NEAR_VMEM = 20 << 20
 FAR_VMEM = 16 << 20
 
 
@@ -173,13 +173,19 @@
     list_ref[...] = values.astype(jnp.int32)
 
 
-def near_kernel(late, batch, lag, shards, sends, list_ref, *refs):
+def near_kernel(part, batch, lag, shards, sends, list_ref, *refs):
+    late = int(part == 2)
     used = LATE if late else shards
-    shard_refs, (own_ref, mate_hbm), refs = refs[:shards], refs[shards : shards + 2], refs[shards + 2 :]
+    shard_refs, refs = refs[:shards], refs[shards:]
+    if part > 0:
+        own_ref, refs = refs[0], refs[1:]
+    if part != 1:
+        mate_hbm, refs = refs[0], refs[1:]
+    if part > 0:
+        refs = refs[1:]
+    sums, refs = refs[0], refs[1:]
     if late:
-        sums, coef_ref, send_refs, refs = refs[1], refs[2], refs[3 : 3 + sends], refs[3 + sends :]
-    else:
-        sums, refs = refs[0], refs[1:]
+        coef_ref, send_refs, refs = refs[0], refs[1 : 1 + sends], refs[1 + sends :]
     columns, blocks, block_sem = refs
     stored = blocks.shape[0]
     directions = sums.shape[1]
@@ -200,7 +206,7 @@
 
     if late:
         lax.fori_loop(0, steps_there * batch, fetch, 0)
-    else:
+    elif part == 0:
         for c in range(CHUNKS):
             at = pl.ds(c * chunk, chunk)
             pltpu.make_async_copy(mate_hbm.at[at], blocks.at[at], block_sem.at[c]).start()
@@ -219,7 +225,7 @@
         tail = coef_ref.shape[0] // shards
         for k, ref in enumerate(shard_refs):
             coef_ref[k * tail : (k + 1) * tail] = ref[span : span + tail]
-    else:
+    elif part == 0:
 
         def clear(i, carry):
             sums[i] = jnp.zeros(sums.shape[1:], sums.dtype)
@@ -279,10 +285,13 @@
         lax.fori_loop(ready, needed, wait, 0)
         return lambda i: blocks[list_ref[8, entry(first + i)]], jnp.maximum(ready, needed)
 
-    run(begin, end, 0, 0, own_blocks)
-    ready = run(begin_there, end_there, 8, dummy // 2, mate_blocks)
+    if part > 0:
+        run(begin, end, 0, 0, own_blocks)
+    if part != 1:
+        ready = run(begin_there, end_there, 8, dummy // 2, mate_blocks)
+    if part == 0:
+        lax.fori_loop(ready, CHUNKS, wait, 0)
     if not late:
-        lax.fori_loop(ready, CHUNKS, wait, 0)
         return
     at = dummy // 2
     for send_ref in send_refs:
@@ -445,16 +454,20 @@
     )
     flow = [move(payload, ahead)]
     mate_blocks = move(near_blocks, mate)
-    lists = jnp.concatenate([lists, move(lists, mate)], axis=0)
+    mate_lists = move(lists, mate)
     couple = jnp.transpose(far_coupling, (2, 1, 0))
     flow.append(move(after(payload, couple), cross))
     shards = [move(payload, mate)]
     for k in range(1, chips):
         x = 1 - k % 2
         if k == 3:
-            flow[x], mate_blocks, shards[0], lists = lax.optimization_barrier(
-                (flow[x], mate_blocks, shards[0], lists)
+            flow[x], mate_blocks, shards[0], mate_lists = lax.optimization_barrier(
+                (flow[x], mate_blocks, shards[0], mate_lists)
             )
+        if k == 4:
+            lists = jnp.concatenate([after(lists, flow[x]), mate_lists], axis=0)
+        if k == 5:
+            flow[x], lists = lax.optimization_barrier((flow[x], lists))
         shards.append(flow[x])
         if k < chips - 2:
             flow[x] = move(flow[x], ahead)
@@ -462,35 +475,36 @@
     pieces = [1, 1, chips - 2]
     sums_shape = jax.ShapeDtypeStruct((count * clusters + 1, directions, unknowns), jnp.float32)
 
-    def near(late, shards, *sums):
+    def near(part, shards, sources, *sums):
+        late = int(part == 2)
         sends = pieces if late else []
         return pl.pallas_call(
-            functools.partial(near_kernel, late, BATCH, LAG, len(shards), len(sends)),
+            functools.partial(near_kernel, part, BATCH, LAG, len(shards), len(sends)),
             out_shape=[sums_shape]
             + [jax.ShapeDtypeStruct((chips * half * rank_k, unknowns), jnp.bfloat16)] * late
             + [
-                jax.ShapeDtypeStruct((part * clusters, directions, unknowns), jnp.bfloat16)
-                for part in sends
+                jax.ShapeDtypeStruct((size * clusters, directions, unknowns), jnp.bfloat16)
+                for size in sends
             ],
             in_specs=[whole(pltpu.SMEM)]
             + [whole()] * len(shards)
-            + [whole(), whole(pl.ANY)]
-            + [whole()] * late,
+            + [[whole(pl.ANY)], [whole()], [whole(), whole(pl.ANY)]][part]
+            + [whole()] * len(sums),
             out_specs=[whole()] * (1 + late + len(sends)),
-            input_output_aliases={len(shards) + 3: 0} if late else {},
+            input_output_aliases={1 + len(shards) + len(sources): 0} if sums else {},
             scratch_shapes=[
                 pltpu.VMEM(((LATE if late else len(shards)) * base, unknowns), jnp.bfloat16),
                 pltpu.VMEM(near_blocks.shape, jnp.bfloat16),
                 pltpu.SemaphoreType.DMA((max(CHUNKS, stored // BATCH),)),
             ],
-            compiler_params=pltpu.CompilerParams(vmem_limit_bytes=NEAR_VMEM[late]),
+            compiler_params=pltpu.CompilerParams(vmem_limit_bytes=NEAR_VMEM),
             cost_estimate=pl.CostEstimate(
                 flops=16 * stored * directions * unknowns * unknowns,
                 bytes_accessed=16 << 20,
                 transcendentals=0,
             ),
             name="near",
-        )(lists, *shards, near_blocks, mate_blocks, *sums)
+        )(lists, *shards, *sources, *sums)
 
     def far_field(couple):
         return pl.pallas_call(
@@ -515,8 +529,9 @@
             basis_out,
         )
 
-    (sums,) = near(0, shards[: chips - LATE])
-    sums, coef, *sends = near(1, shards, sums)
+    (sums,) = near(0, shards[: chips - LATE], [mate_blocks])
+    (sums,) = near(1, shards[: chips - LATE], [near_blocks], sums)
+    sums, coef, *sends = near(2, shards, [near_blocks, mate_blocks], sums)
     mates = [move(sends[0], mate), move(sends[1], mate)]
     coefs = [coef, move(coef, mate)]
 

time: 68.4 us -> 67.6 us (0.988); the launches traced: 67.2 us -> 67.2 us
  local copies, waits for them, and re-layouts: 3.15 us -> 0.97 us
  Pallas kernels: 13.6 us -> 15.5 us
  starting transfers between devices: 31.7 us -> 32.5 us
    unnamed x11, local copies, waits for them, and re-layouts: 3.15 us -> 0.97 us
    pallas_call x2 -> x3, Pallas kernels: 9.12 us -> 10.8 us  [near(): pl.pallas_call(functools.partial(near_kernel, part, BATCH, LAG, len(shard...]
    ppermute x22, starting transfers between devices: 31.7 us -> 32.5 us  [move(): return lax.ppermute(values, 'blk', where)]
  transfers between devices with their start and end apart: 22 -> 22, of which waited for: 14 -> 14; matrix products, arithmetic and copies ran while one was open for 3% -> 3% of each run, Pallas kernels for 16% -> 19%
where the time goes in v16:
time: 67.6 us; the launch traced here: 67.2 us
  starting transfers between devices  32.5 us (48%)
  waiting for transfers between devices  15.7 us (23%)
  Pallas kernels  15.5 us (23%)
  other arithmetic  2.29 us (3%)
  local copies, waits for them, and re-layouts  0.97 us (1%)
    ppermute x22, starting transfers between devices, move(): return lax.ppermute(values, 'blk', where)  32.5 us
    ppermute x22, waiting for transfers between devices, move(): return lax.ppermute(values, 'blk', where)  15.7 us
    pallas_call x3, Pallas kernels, near(): pl.pallas_call(functools.partial(near_kernel, part, BATCH, LAG, len(shard...  10.8 us
    pallas_call x1, Pallas kernels, far_field(): pl.pallas_call(far_kernel, out_shape=jax.ShapeDtypeStruct((clusters, dire...  2.51 us
    pallas_call x1, Pallas kernels, stationary(): pl.pallas_call(functools.partial(prologue_kernel, count), out_shape=[jax....  2.16 us
  transfers between devices with their start and end apart: 22, of which 14 were waited for; matrix products, arithmetic and copies ran while one was open for 3% of the time, Pallas kernels for 19%

profile of v16, /device:TPU:0, one launch (start us, length us, event | category | flops | bytes accessed | tf_op | source)
XLA Modules:
  0.0 67.2 jit_solution(13837479598984558271)
XLA Ops:
  0.5 2.2 %prologue.1 = (bf16[1152,128]{1,0:T(8,128)(2,1)}, s32[8,128]{1,0:T(8,128)}) custom-call(s32[1]{0:T(128)} %bitcast.me_ref.refs_2_, s32[1,128]{1,0:T(1,128)} %bitcast.14, s32[1,128]{1,0:T(1,128)} %bitcast.15, s32[1,128]{1,0:T(1,128)} %bitcast.16, bf16[16,64,128]{2,1,0:T(8,128)(2,1)} %rhs_ref.1, bf16[16,16,128]{2,1,0:T(8,128)(2,1)} %basis_ref.1), custom_call_target="tpu_custom_call" | custom-call | tf_op jit(solution)/shard_map/prologue/pallas_call | solution.py:437
  2.6 2.6 %collective-permute-start = (bf16[1152,128]{1,0:T(8,128)(2,1)}, bf16[1152,128]{1,0:T(8,128)(2,1)S(1)}, u32[]{:S(2)}, u32[]{:S(2)}) collective-permute-start(bf16[1152,128]{1,0:T(8,128)(2,1)} %get-tuple-element.37), channel_id=1, source_target_pairs={{0,4},{1,3},{4,8},{5,1},{8,12},{9,5},{12,14},{13,9},{14,10},{15,13... | collective-permute-start | bytes 884744 | tf_op jit(solution)/shard_map/ppermute | solution.py:430
  5.2 0.9 %copy.16 = bf16[256,16,16]{0,1,2:T(8,128)(2,1)S(1)} copy(bf16[256,16,16]{0,2,1:T(8,128)(2,1)} %param.16) | data formatting | bytes 262144 | tf_op args[5]
  6.1 1.4 %collective-permute-start.6 = (bf16[1152,128]{1,0:T(8,128)(2,1)}, bf16[1152,128]{1,0:T(8,128)(2,1)S(1)}, u32[]{:S(2)}, u32[]{:S(2)}) collective-permute-start(bf16[1152,128]{1,0:T(8,128)(2,1)} %get-tuple-element.37), channel_id=1, source_target_pairs={{0,3},{1,4},{4,1},{5,8},{8,5},{9,12},{12,9},{13,14},{14,13},{15,10... | collective-permute-start | bytes 884744 | tf_op jit(solution)/shard_map/ppermute | solution.py:430
  7.9 2.9 %collective-permute-done.refs_1_ = bf16[1152,128]{1,0:T(8,128)(2,1)S(1)} collective-permute-done((bf16[1152,128]{1,0:T(8,128)(2,1)}, bf16[1152,128]{1,0:T(8,128)(2,1)S(1)}, u32[]{:S(2)}, u32[]{:S(2)}) %collective-permute-start) | collective-permute-done | bytes 294944 | tf_op jit(solution)/shard_map/ppermute | solution.py:430
  10.8 2.4 %collective-permute-start.1 = (bf16[1152,128]{1,0:T(8,128)(2,1)S(1)}, bf16[1152,128]{1,0:T(8,128)(2,1)S(1)}, u32[]{:S(2)}, u32[]{:S(2)}) collective-permute-start(bf16[1152,128]{1,0:T(8,128)(2,1)S(1)} %collective-permute-done.refs_1_), channel_id=1, source_target_pairs={{0,4},{1,3},{4,8},{5,1},{8,12},{9,5},{12,14},{13,9},{14,10},{15,13... | collective-permute-start | bytes 884744 | tf_op jit(solution)/shard_map/ppermute | solution.py:430
  13.2 2.1 %collective-permute-start.7 = (bf16[1152,128]{1,0:T(8,128)(2,1)S(1)}, bf16[1152,128]{1,0:T(8,128)(2,1)S(1)}, u32[]{:S(2)}, u32[]{:S(2)}) collective-permute-start(bf16[1152,128]{1,0:T(8,128)(2,1)S(1)} %collective-permute-done.6.refs_2_), channel_id=1, source_target_pairs={{0,4},{1,3},{4,8},{5,1},{8,12},{9,5},{12,14},{13,9},{14,10},{15,13... | collective-permute-start | bytes 884744 | tf_op jit(solution)/shard_map/ppermute | solution.py:430
  15.3 1.4 %collective-permute-done.4 = s32[8,128]{1,0:T(8,128)S(1)} collective-permute-done((s32[8,128]{1,0:T(8,128)}, s32[8,128]{1,0:T(8,128)S(1)}, u32[]{:S(2)}, u32[]{:S(2)}) %collective-permute-start.4) | collective-permute-done | bytes 4128 | tf_op jit(solution)/shard_map/ppermute | solution.py:430
  16.7 1.5 %collective-permute-done.1.refs_3_ = bf16[1152,128]{1,0:T(8,128)(2,1)S(1)} collective-permute-done((bf16[1152,128]{1,0:T(8,128)(2,1)S(1)}, bf16[1152,128]{1,0:T(8,128)(2,1)S(1)}, u32[]{:S(2)}, u32[]{:S(2)}) %collective-permute-start.1) | collective-permute-done | bytes 294944 | tf_op jit(solution)/shard_map/ppermute | solution.py:430
  18.2 1.7 %collective-permute-start.5 = (bf16[1152,128]{1,0:T(8,128)(2,1)S(1)}, bf16[1152,128]{1,0:T(8,128)(2,1)S(1)}, u32[]{:S(2)}, u32[]{:S(2)}) collective-permute-start(bf16[1152,128]{1,0:T(8,128)(2,1)S(1)} %collective-permute-done.1.refs_3_), channel_id=1, source_target_pairs={{0,4},{1,3},{4,8},{5,1},{8,12},{9,5},{12,14},{13,9},{14,10},{15,13... | collective-permute-start | bytes 884744 | tf_op jit(solution)/shard_map/ppermute | solution.py:430
  19.9 1.4 %collective-permute-done.7.refs_4_ = bf16[1152,128]{1,0:T(8,128)(2,1)S(1)} collective-permute-done((bf16[1152,128]{1,0:T(8,128)(2,1)S(1)}, bf16[1152,128]{1,0:T(8,128)(2,1)S(1)}, u32[]{:S(2)}, u32[]{:S(2)}) %collective-permute-start.7) | collective-permute-done | bytes 294944 | tf_op jit(solution)/shard_map/ppermute | solution.py:430
  21.3 1.7 %collective-permute-start.8 = (bf16[1152,128]{1,0:T(8,128)(2,1)S(1)}, bf16[1152,128]{1,0:T(8,128)(2,1)S(1)}, u32[]{:S(2)}, u32[]{:S(2)}) collective-permute-start(bf16[1152,128]{1,0:T(8,128)(2,1)S(1)} %collective-permute-done.7.refs_4_), channel_id=1, source_target_pairs={{0,4},{1,3},{4,8},{5,1},{8,12},{9,5},{12,14},{13,9},{14,10},{15,13... | collective-permute-start | bytes 884744 | tf_op jit(solution)/shard_map/ppermute | solution.py:430
  23.1 0.7 %pad_add_fusion.list_ref = s32[16,128]{1,0:T(8,128)S(1)} fusion(s32[8,128]{1,0:T(8,128)S(1)} %collective-permute-done.4, s32[8,128]{1,0:T(8,128)} %get-tuple-element.38), kind=kLoop, calls=%fused_computation.10 | loop fusion | flops 2048 | bytes 16384 | tf_op jit(solution)/shard_map/concatenate | solution.py:468
  23.8 1.1 %collective-permute-done.5.refs_5_ = bf16[1152,128]{1,0:T(8,128)(2,1)S(1)} collective-permute-done((bf16[1152,128]{1,0:T(8,128)(2,1)S(1)}, bf16[1152,128]{1,0:T(8,128)(2,1)S(1)}, u32[]{:S(2)}, u32[]{:S(2)}) %collective-permute-start.5) | collective-permute-done | bytes 294944 | tf_op jit(solution)/shard_map/ppermute | solution.py:430
  24.9 1.7 %collective-permute-start.9 = (bf16[1152,128]{1,0:T(8,128)(2,1)S(1)}, bf16[1152,128]{1,0:T(8,128)(2,1)S(1)}, u32[]{:S(2)}, u32[]{:S(2)}) collective-permute-start(bf16[1152,128]{1,0:T(8,128)(2,1)S(1)} %collective-permute-done.5.refs_5_), channel_id=1, source_target_pairs={{0,4},{1,3},{4,8},{5,1},{8,12},{9,5},{12,14},{13,9},{14,10},{15,13... | collective-permute-start | bytes 884744 | tf_op jit(solution)/shard_map/ppermute | solution.py:430
  26.7 4.8 %near.3.refs_7_ = f32[257,64,128]{2,1,0:T(8,128)S(1)} custom-call(s32[16,128]{1,0:T(8,128)S(1)} %pad_add_fusion.list_ref, bf16[1152,128]{1,0:T(8,128)(2,1)S(1)} %collective-permute-done.3.refs_0_, bf16[1152,128]{1,0:T(8,128)(2,1)S(1)} %collective-permute-done.refs_1_, bf16[1152,128]{1,0:T(8,128)(2,1)S(1)} %collective-permute-done.6.refs_2_, ...), custom_call_target="tpu_custom_call" | custom-call | flops 2147483648 | bytes 16777216 | tf_op jit(solution)/shard_map/near/pallas_call | solution.py:481
  31.5 3.1 %near.4.refs_10_ = f32[257,64,128]{2,1,0:T(8,128)S(1)} custom-call(s32[16,128]{1,0:T(8,128)S(1)} %pad_add_fusion.list_ref, bf16[1152,128]{1,0:T(8,128)(2,1)S(1)} %collective-permute-done.3.refs_0_, bf16[1152,128]{1,0:T(8,128)(2,1)S(1)} %collective-permute-done.refs_1_, ...), custom_call_target="tpu_custom_call", output_to_operand_aliasing={{}: (8, {})} | custom-call | flops 2147483648 | bytes 16777216 | tf_op jit(solution)/shard_map/near/pallas_call | solution.py:481
  34.6 2.9 %near.5 = (f32[257,64,128]{2,1,0:T(8,128)S(1)}, bf16[1024,128]{1,0:T(8,128)(2,1)S(1)}, bf16[16,64,128]{2,1,0:T(8,128)(2,1)S(1)}, bf16[16,64,128]{2,1,0:T(8,128)(2,1)S(1)}, bf16[96,64,128]{2,1,0:T(8,128)(2,1)S(1)}) custom-call(s32[16,128]{1,0:T(8,128)S(1)} %pad_add_fusion.list_ref, ...), custom_call_target="tpu_custom_call", output_to_operand_aliasing={{0}: (11, {})} | custom-call | flops 2147483648 | bytes 16777216 | tf_op jit(solution)/shard_map/near/pallas_call | solution.py:481
  38.2 1.0 %collective-permute-done.11 = bf16[16,64,128]{2,1,0:T(8,128)(2,1)S(1)} collective-permute-done((bf16[16,64,128]{2,1,0:T(8,128)(2,1)S(1)}, bf16[16,64,128]{2,1,0:T(8,128)(2,1)S(1)}, u32[]{:S(2)}, u32[]{:S(2)}) %collective-permute-start.11) | collective-permute-done | bytes 262176 | tf_op jit(solution)/shard_map/ppermute | solution.py:430
  39.9 2.8 %collective-permute-start.13 = (bf16[16,64,128]{2,1,0:T(8,128)(2,1)S(1)}, bf16[16,64,128]{2,1,0:T(8,128)(2,1)S(1)}, u32[]{:S(2)}, u32[]{:S(2)}) collective-permute-start(bf16[16,64,128]{2,1,0:T(8,128)(2,1)S(1)} %get-tuple-element.48), channel_id=1, source_target_pairs={{0,4},{1,3},{4,8},{5,1},{8,12},{9,5},{12,14},{13,9},{14,10},{15,13... | collective-permute-start | bytes 786440 | tf_op jit(solution)/shard_map/ppermute | solution.py:430
  42.7 1.7 %collective-permute-start.16 = (bf16[16,64,128]{2,1,0:T(8,128)(2,1)S(1)}, bf16[16,64,128]{2,1,0:T(8,128)(2,1)S(1)}, u32[]{:S(2)}, u32[]{:S(2)}) collective-permute-start(bf16[16,64,128]{2,1,0:T(8,128)(2,1)S(1)} %get-tuple-element.50), channel_id=1, source_target_pairs={{0,4},{1,3},{4,8},{5,1},{8,12},{9,5},{12,14},{13,9},{14,10},{15,13... | collective-permute-start | bytes 786440 | tf_op jit(solution)/shard_map/ppermute | solution.py:430
  44.5 2.1 %collective-permute-done.13 = bf16[16,64,128]{2,1,0:T(8,128)(2,1)S(1)} collective-permute-done((bf16[16,64,128]{2,1,0:T(8,128)(2,1)S(1)}, bf16[16,64,128]{2,1,0:T(8,128)(2,1)S(1)}, u32[]{:S(2)}, u32[]{:S(2)}) %collective-permute-start.13) | collective-permute-done | bytes 262176 | tf_op jit(solution)/shard_map/ppermute | solution.py:430
  46.8 2.5 %collective-permute-start.15 = (bf16[16,64,128]{2,1,0:T(8,128)(2,1)S(1)}, bf16[16,64,128]{2,1,0:T(8,128)(2,1)S(1)}, u32[]{:S(2)}, u32[]{:S(2)}) collective-permute-start(bf16[16,64,128]{2,1,0:T(8,128)(2,1)S(1)} %add_convert_fusion.5), channel_id=1, source_target_pairs={{0,4},{1,3},{4,8},{5,1},{8,12},{9,5},{12,14},{13,9},{14,10},{15,13... | collective-permute-start | bytes 786440 | tf_op jit(solution)/shard_map/ppermute | solution.py:430
  49.6 2.5 %collective-permute-start.18 = (bf16[16,64,128]{2,1,0:T(8,128)(2,1)S(1)}, bf16[16,64,128]{2,1,0:T(8,128)(2,1)S(1)}, u32[]{:S(2)}, u32[]{:S(2)}) collective-permute-start(bf16[16,64,128]{2,1,0:T(8,128)(2,1)S(1)} %add_convert_fusion.4), channel_id=1, source_target_pairs={{0,4},{1,3},{4,8},{5,1},{8,12},{9,5},{12,14},{13,9},{14,10},{15,13... | collective-permute-start | bytes 786440 | tf_op jit(solution)/shard_map/ppermute | solution.py:430
  52.1 1.1 %collective-permute-done.15 = bf16[16,64,128]{2,1,0:T(8,128)(2,1)S(1)} collective-permute-done((bf16[16,64,128]{2,1,0:T(8,128)(2,1)S(1)}, bf16[16,64,128]{2,1,0:T(8,128)(2,1)S(1)}, u32[]{:S(2)}, u32[]{:S(2)}) %collective-permute-start.15) | collective-permute-done | bytes 262176 | tf_op jit(solution)/shard_map/ppermute | solution.py:430
  53.3 2.5 %collective-permute-start.17 = (bf16[16,64,128]{2,1,0:T(8,128)(2,1)S(1)}, bf16[16,64,128]{2,1,0:T(8,128)(2,1)S(1)}, u32[]{:S(2)}, u32[]{:S(2)}) collective-permute-start(bf16[16,64,128]{2,1,0:T(8,128)(2,1)S(1)} %add_convert_fusion.3), channel_id=1, source_target_pairs={{0,4},{1,3},{4,8},{5,1},{8,12},{9,5},{12,14},{13,9},{14,10},{15,13... | collective-permute-start | bytes 786440 | tf_op jit(solution)/shard_map/ppermute | solution.py:430
  56.1 2.5 %collective-permute-start.20 = (bf16[16,64,128]{2,1,0:T(8,128)(2,1)S(1)}, bf16[16,64,128]{2,1,0:T(8,128)(2,1)S(1)}, u32[]{:S(2)}, u32[]{:S(2)}) collective-permute-start(bf16[16,64,128]{2,1,0:T(8,128)(2,1)S(1)} %add_convert_fusion.2), channel_id=1, source_target_pairs={{0,4},{1,3},{4,8},{5,1},{8,12},{9,5},{12,14},{13,9},{14,10},{15,13... | collective-permute-start | bytes 786440 | tf_op jit(solution)/shard_map/ppermute | solution.py:430
  58.6 1.1 %collective-permute-done.17 = bf16[16,64,128]{2,1,0:T(8,128)(2,1)S(1)} collective-permute-done((bf16[16,64,128]{2,1,0:T(8,128)(2,1)S(1)}, bf16[16,64,128]{2,1,0:T(8,128)(2,1)S(1)}, u32[]{:S(2)}, u32[]{:S(2)}) %collective-permute-start.17) | collective-permute-done | bytes 262176 | tf_op jit(solution)/shard_map/ppermute | solution.py:430
  59.8 2.5 %collective-permute-start.19 = (bf16[16,64,128]{2,1,0:T(8,128)(2,1)S(1)}, bf16[16,64,128]{2,1,0:T(8,128)(2,1)S(1)}, u32[]{:S(2)}, u32[]{:S(2)}) collective-permute-start(bf16[16,64,128]{2,1,0:T(8,128)(2,1)S(1)} %add_convert_fusion.1), channel_id=1, source_target_pairs={{0,4},{1,3},{4,8},{5,1},{8,12},{9,5},{12,14},{13,9},{14,10},{15,13... | collective-permute-start | bytes 786440 | tf_op jit(solution)/shard_map/ppermute | solution.py:430
  62.6 2.5 %far.1 = f32[16,64,128]{2,1,0:T(8,128)S(1)} custom-call(bf16[1024,128]{1,0:T(8,128)(2,1)S(1)} %get-tuple-element.44.refs_0_, bf16[1024,128]{1,0:T(8,128)(2,1)S(1)} %collective-permute-done.10.refs_1_, s32[1]{0:T(128)} %bitcast.me_ref.refs_2_, bf16[16,16,256]{2,1,0:T(8,128)(2,1)S(1)} %bitcast.10, s32[1,256]{1,0:T(1,128)S(1)} %bitcast.11, ...), custom_call_target="tpu_custom_call" | custom-call | flops 536870912 | bytes 8388608 | tf_op jit(solution)/shard_map/far/pallas_call | solution.py:510
  65.1 1.2 %collective-permute-done.19 = bf16[16,64,128]{2,1,0:T(8,128)(2,1)S(1)} collective-permute-done((bf16[16,64,128]{2,1,0:T(8,128)(2,1)S(1)}, bf16[16,64,128]{2,1,0:T(8,128)(2,1)S(1)}, u32[]{:S(2)}, u32[]{:S(2)}) %collective-permute-start.19) | collective-permute-done | bytes 262176 | tf_op jit(solution)/shard_map/ppermute | solution.py:430
  66.4 0.8 %add_convert_fusion = bf16[16,64,128]{2,1,0:T(8,128)(2,1)} fusion(f32[16,64,128]{2,1,0:T(8,128)S(1)} %convert_add_fusion, bf16[16,64,128]{2,1,0:T(8,128)(2,1)S(1)} %collective-permute-done.21), kind=kLoop, calls=%fused_computation | loop fusion | flops 393216 | bytes 1048576 | tf_op jit(solution)/shard_map/convert_element_type | solution.py:562
  (37 shorter events, 3.3 us)
Async XLA Ops:
  0.0 18.2 %collective-permute-start.2 = (bf16[128,128,128]{2,1,0:T(8,128)(2,1)}, bf16[128,128,128]{2,1,0:T(8,128)(2,1)}, u32[]{:S(2)}, u32[]{:S(2)}) collective-permute-start(bf16[128,128,128]{2,1,0:T(8,128)(2,1)} %refs_8_.1), channel_id=1, source_target_pairs={{0,1},{1,0},{2,3},{3,2},{4,5},{5,4},{6,7},{7,6},{8,9},{9,8},{10,11... | collective-permute-start | bytes 12582920 | tf_op jit(solution)/shard_map/ppermute | solution.py:430
  0.5 31.0 %copy-start = (bf16[128,128,128]{2,1,0:T(8,128)(2,1)S(1)}, bf16[128,128,128]{2,1,0:T(8,128)(2,1)}, u32[]{:S(2)}) copy-start(bf16[128,128,128]{2,1,0:T(8,128)(2,1)} %refs_8_.1) | copy-start | bytes 12582916
  2.6 8.2 %collective-permute-start = (bf16[1152,128]{1,0:T(8,128)(2,1)}, bf16[1152,128]{1,0:T(8,128)(2,1)S(1)}, u32[]{:S(2)}, u32[]{:S(2)}) collective-permute-start(bf16[1152,128]{1,0:T(8,128)(2,1)} %get-tuple-element.37), channel_id=1, source_target_pairs={{0,4},{1,3},{4,8},{5,1},{8,12},{9,5},{12,14},{13,9},{14,10},{15,13... | collective-permute-start | bytes 884744 | tf_op jit(solution)/shard_map/ppermute | solution.py:430
  6.1 7.1 %collective-permute-start.6 = (bf16[1152,128]{1,0:T(8,128)(2,1)}, bf16[1152,128]{1,0:T(8,128)(2,1)S(1)}, u32[]{:S(2)}, u32[]{:S(2)}) collective-permute-start(bf16[1152,128]{1,0:T(8,128)(2,1)} %get-tuple-element.37), channel_id=1, source_target_pairs={{0,3},{1,4},{4,1},{5,8},{8,5},{9,12},{12,9},{13,14},{14,13},{15,10... | collective-permute-start | bytes 884744 | tf_op jit(solution)/shard_map/ppermute | solution.py:430
  7.6 9.1 %collective-permute-start.3 = (bf16[1152,128]{1,0:T(8,128)(2,1)}, bf16[1152,128]{1,0:T(8,128)(2,1)S(1)}, u32[]{:S(2)}, u32[]{:S(2)}) collective-permute-start(bf16[1152,128]{1,0:T(8,128)(2,1)} %get-tuple-element.37), channel_id=1, source_target_pairs={{0,1},{1,0},{2,3},{3,2},{4,5},{5,4},{6,7},{7,6},{8,9},{9,8},{10,11... | collective-permute-start | bytes 884744 | tf_op jit(solution)/shard_map/ppermute | solution.py:430
  10.8 7.4 %collective-permute-start.1 = (bf16[1152,128]{1,0:T(8,128)(2,1)S(1)}, bf16[1152,128]{1,0:T(8,128)(2,1)S(1)}, u32[]{:S(2)}, u32[]{:S(2)}) collective-permute-start(bf16[1152,128]{1,0:T(8,128)(2,1)S(1)} %collective-permute-done.refs_1_), channel_id=1, source_target_pairs={{0,4},{1,3},{4,8},{5,1},{8,12},{9,5},{12,14},{13,9},{14,10},{15,13... | collective-permute-start | bytes 884744 | tf_op jit(solution)/shard_map/ppermute | solution.py:430
  13.2 8.1 %collective-permute-start.7 = (bf16[1152,128]{1,0:T(8,128)(2,1)S(1)}, bf16[1152,128]{1,0:T(8,128)(2,1)S(1)}, u32[]{:S(2)}, u32[]{:S(2)}) collective-permute-start(bf16[1152,128]{1,0:T(8,128)(2,1)S(1)} %collective-permute-done.6.refs_2_), channel_id=1, source_target_pairs={{0,4},{1,3},{4,8},{5,1},{8,12},{9,5},{12,14},{13,9},{14,10},{15,13... | collective-permute-start | bytes 884744 | tf_op jit(solution)/shard_map/ppermute | solution.py:430
  15.3 1.4 %collective-permute-start.4 = (s32[8,128]{1,0:T(8,128)}, s32[8,128]{1,0:T(8,128)S(1)}, u32[]{:S(2)}, u32[]{:S(2)}) collective-permute-start(s32[8,128]{1,0:T(8,128)} %get-tuple-element.38), channel_id=1, source_target_pairs={{0,1},{1,0},{2,3},{3,2},{4,5},{5,4},{6,7},{7,6},{8,9},{9,8},{10,11... | collective-permute-start | bytes 12296 | tf_op jit(solution)/shard_map/ppermute | solution.py:430
  18.2 6.7 %collective-permute-start.5 = (bf16[1152,128]{1,0:T(8,128)(2,1)S(1)}, bf16[1152,128]{1,0:T(8,128)(2,1)S(1)}, u32[]{:S(2)}, u32[]{:S(2)}) collective-permute-start(bf16[1152,128]{1,0:T(8,128)(2,1)S(1)} %collective-permute-done.1.refs_3_), channel_id=1, source_target_pairs={{0,4},{1,3},{4,8},{5,1},{8,12},{9,5},{12,14},{13,9},{14,10},{15,13... | collective-permute-start | bytes 884744 | tf_op jit(solution)/shard_map/ppermute | solution.py:430
  21.3 13.3 %collective-permute-start.8 = (bf16[1152,128]{1,0:T(8,128)(2,1)S(1)}, bf16[1152,128]{1,0:T(8,128)(2,1)S(1)}, u32[]{:S(2)}, u32[]{:S(2)}) collective-permute-start(bf16[1152,128]{1,0:T(8,128)(2,1)S(1)} %collective-permute-done.7.refs_4_), channel_id=1, source_target_pairs={{0,4},{1,3},{4,8},{5,1},{8,12},{9,5},{12,14},{13,9},{14,10},{15,13... | collective-permute-start | bytes 884744 | tf_op jit(solution)/shard_map/ppermute | solution.py:430
  24.9 9.7 %collective-permute-start.9 = (bf16[1152,128]{1,0:T(8,128)(2,1)S(1)}, bf16[1152,128]{1,0:T(8,128)(2,1)S(1)}, u32[]{:S(2)}, u32[]{:S(2)}) collective-permute-start(bf16[1152,128]{1,0:T(8,128)(2,1)S(1)} %collective-permute-done.5.refs_5_), channel_id=1, source_target_pairs={{0,4},{1,3},{4,8},{5,1},{8,12},{9,5},{12,14},{13,9},{14,10},{15,13... | collective-permute-start | bytes 884744 | tf_op jit(solution)/shard_map/ppermute | solution.py:430
  37.5 25.0 %copy-start.1 = (bf16[16,16,128]{2,1,0:T(8,128)(2,1)S(1)}, bf16[16,16,128]{2,1,0:T(8,128)(2,1)}, u32[]{:S(2)}) copy-start(bf16[16,16,128]{2,1,0:T(8,128)(2,1)} %refs_7_.1) | copy-start | bytes 196612
  37.5 25.0 %copy-start.2 = (s32[256]{0:T(256)S(1)}, s32[256]{0:T(256)}, u32[]{:S(2)}) copy-start(s32[256]{0:T(256)} %param.17) | copy-start | bytes 3076
  37.6 25.0 %copy-start.3 = (s32[256,1]{0,1:T(1,128)S(1)}, s32[256,1]{0,1:T(1,128)}, u32[]{:S(2)}) copy-start(s32[256,1]{0,1:T(1,128)} %param.18) | copy-start | bytes 3076
  37.6 25.0 %copy-start.4 = (s32[256]{0:T(256)S(1)}, s32[256]{0:T(256)}, u32[]{:S(2)}) copy-start(s32[256]{0:T(256)} %param.19) | copy-start | bytes 3076
  37.6 1.6 %collective-permute-start.11 = (bf16[16,64,128]{2,1,0:T(8,128)(2,1)S(1)}, bf16[16,64,128]{2,1,0:T(8,128)(2,1)S(1)}, u32[]{:S(2)}, u32[]{:S(2)}) collective-permute-start(bf16[16,64,128]{2,1,0:T(8,128)(2,1)S(1)} %get-tuple-element.46), channel_id=1, source_target_pairs={{0,1},{1,0},{2,3},{3,2},{4,5},{5,4},{6,7},{7,6},{8,9},{9,8},{10,11... | collective-permute-start | bytes 786440 | tf_op jit(solution)/shard_map/ppermute | solution.py:430
  37.7 1.9 %collective-permute-start.12 = (bf16[16,64,128]{2,1,0:T(8,128)(2,1)S(1)}, bf16[16,64,128]{2,1,0:T(8,128)(2,1)S(1)}, u32[]{:S(2)}, u32[]{:S(2)}) collective-permute-start(bf16[16,64,128]{2,1,0:T(8,128)(2,1)S(1)} %get-tuple-element.47), channel_id=1, source_target_pairs={{0,1},{1,0},{2,3},{3,2},{4,5},{5,4},{6,7},{7,6},{8,9},{9,8},{10,11... | collective-permute-start | bytes 786440 | tf_op jit(solution)/shard_map/ppermute | solution.py:430
  39.7 6.9 %collective-permute-start.14 = (bf16[96,64,128]{2,1,0:T(8,128)(2,1)S(1)}, bf16[96,64,128]{2,1,0:T(8,128)(2,1)S(1)}, u32[]{:S(2)}, u32[]{:S(2)}) collective-permute-start(bf16[96,64,128]{2,1,0:T(8,128)(2,1)S(1)} %get-tuple-element.51), channel_id=1, source_target_pairs={{0,1},{1,0},{2,3},{3,2},{4,5},{5,4},{6,7},{7,6},{8,9},{9,8},{10,11... | collective-permute-start | bytes 4718600 | tf_op jit(solution)/shard_map/ppermute | solution.py:430
  39.9 6.7 %collective-permute-start.13 = (bf16[16,64,128]{2,1,0:T(8,128)(2,1)S(1)}, bf16[16,64,128]{2,1,0:T(8,128)(2,1)S(1)}, u32[]{:S(2)}, u32[]{:S(2)}) collective-permute-start(bf16[16,64,128]{2,1,0:T(8,128)(2,1)S(1)} %get-tuple-element.48), channel_id=1, source_target_pairs={{0,4},{1,3},{4,8},{5,1},{8,12},{9,5},{12,14},{13,9},{14,10},{15,13... | collective-permute-start | bytes 786440 | tf_op jit(solution)/shard_map/ppermute | solution.py:430
  42.7 6.7 %collective-permute-start.16 = (bf16[16,64,128]{2,1,0:T(8,128)(2,1)S(1)}, bf16[16,64,128]{2,1,0:T(8,128)(2,1)S(1)}, u32[]{:S(2)}, u32[]{:S(2)}) collective-permute-start(bf16[16,64,128]{2,1,0:T(8,128)(2,1)S(1)} %get-tuple-element.50), channel_id=1, source_target_pairs={{0,4},{1,3},{4,8},{5,1},{8,12},{9,5},{12,14},{13,9},{14,10},{15,13... | collective-permute-start | bytes 786440 | tf_op jit(solution)/shard_map/ppermute | solution.py:430
  46.8 6.4 %collective-permute-start.15 = (bf16[16,64,128]{2,1,0:T(8,128)(2,1)S(1)}, bf16[16,64,128]{2,1,0:T(8,128)(2,1)S(1)}, u32[]{:S(2)}, u32[]{:S(2)}) collective-permute-start(bf16[16,64,128]{2,1,0:T(8,128)(2,1)S(1)} %add_convert_fusion.5), channel_id=1, source_target_pairs={{0,4},{1,3},{4,8},{5,1},{8,12},{9,5},{12,14},{13,9},{14,10},{15,13... | collective-permute-start | bytes 786440 | tf_op jit(solution)/shard_map/ppermute | solution.py:430
  49.6 6.4 %collective-permute-start.18 = (bf16[16,64,128]{2,1,0:T(8,128)(2,1)S(1)}, bf16[16,64,128]{2,1,0:T(8,128)(2,1)S(1)}, u32[]{:S(2)}, u32[]{:S(2)}) collective-permute-start(bf16[16,64,128]{2,1,0:T(8,128)(2,1)S(1)} %add_convert_fusion.4), channel_id=1, source_target_pairs={{0,4},{1,3},{4,8},{5,1},{8,12},{9,5},{12,14},{13,9},{14,10},{15,13... | collective-permute-start | bytes 786440 | tf_op jit(solution)/shard_map/ppermute | solution.py:430
  53.3 6.4 %collective-permute-start.17 = (bf16[16,64,128]{2,1,0:T(8,128)(2,1)S(1)}, bf16[16,64,128]{2,1,0:T(8,128)(2,1)S(1)}, u32[]{:S(2)}, u32[]{:S(2)}) collective-permute-start(bf16[16,64,128]{2,1,0:T(8,128)(2,1)S(1)} %add_convert_fusion.3), channel_id=1, source_target_pairs={{0,4},{1,3},{4,8},{5,1},{8,12},{9,5},{12,14},{13,9},{14,10},{15,13... | collective-permute-start | bytes 786440 | tf_op jit(solution)/shard_map/ppermute | solution.py:430
  55.8 6.7 %collective-permute-start.10 = (bf16[1024,128]{1,0:T(8,128)(2,1)S(1)}, bf16[1024,128]{1,0:T(8,128)(2,1)S(1)}, u32[]{:S(2)}, u32[]{:S(2)}) collective-permute-start(bf16[1024,128]{1,0:T(8,128)(2,1)S(1)} %get-tuple-element.44.refs_0_), channel_id=1, source_target_pairs={{0,1},{1,0},{2,3},{3,2},{4,5},{5,4},{6,7},{7,6},{8,9},{9,8},{10,11... | collective-permute-start | bytes 786440 | tf_op jit(solution)/shard_map/ppermute | solution.py:430
  56.1 6.4 %collective-permute-start.20 = (bf16[16,64,128]{2,1,0:T(8,128)(2,1)S(1)}, bf16[16,64,128]{2,1,0:T(8,128)(2,1)S(1)}, u32[]{:S(2)}, u32[]{:S(2)}) collective-permute-start(bf16[16,64,128]{2,1,0:T(8,128)(2,1)S(1)} %add_convert_fusion.2), channel_id=1, source_target_pairs={{0,4},{1,3},{4,8},{5,1},{8,12},{9,5},{12,14},{13,9},{14,10},{15,13... | collective-permute-start | bytes 786440 | tf_op jit(solution)/shard_map/ppermute | solution.py:430
  59.8 6.4 %collective-permute-start.19 = (bf16[16,64,128]{2,1,0:T(8,128)(2,1)S(1)}, bf16[16,64,128]{2,1,0:T(8,128)(2,1)S(1)}, u32[]{:S(2)}, u32[]{:S(2)}) collective-permute-start(bf16[16,64,128]{2,1,0:T(8,128)(2,1)S(1)} %add_convert_fusion.1), channel_id=1, source_target_pairs={{0,4},{1,3},{4,8},{5,1},{8,12},{9,5},{12,14},{13,9},{14,10},{15,13... | collective-permute-start | bytes 786440 | tf_op jit(solution)/shard_map/ppermute | solution.py:430
  62.5 3.9 %collective-permute-start.21 = (bf16[16,64,128]{2,1,0:T(8,128)(2,1)S(1)}, bf16[16,64,128]{2,1,0:T(8,128)(2,1)S(1)}, u32[]{:S(2)}, u32[]{:S(2)}) collective-permute-start(bf16[16,64,128]{2,1,0:T(8,128)(2,1)S(1)} %collective-permute-done.20), channel_id=1, source_target_pairs={{0,1},{1,0},{2,3},{3,2},{4,5},{5,4},{6,7},{7,6},{8,9},{9,8},{10,11... | collective-permute-start | bytes 786440 | tf_op jit(solution)/shard_map/ppermute | solution.py:430

commit v17 on v16

--- a/solution.py
+++ b/solution.py
@@ -7,10 +7,9 @@
 from jax.experimental.pallas import tpu as pltpu
 from jax.sharding import PartitionSpec as P
 
-BATCH = 8
+BATCH = 16, 16, 8
 CHUNKS = 4
 LATE = 2
-LAG = 4
 PROLOGUE_VMEM = 58 << 20
 NEAR_VMEM = 20 << 20
 FAR_VMEM = 16 << 20
@@ -173,7 +172,7 @@
     list_ref[...] = values.astype(jnp.int32)
 
 
-def near_kernel(part, batch, lag, shards, sends, list_ref, *refs):
+def near_kernel(part, batch, shards, sends, list_ref, *refs):
     late = int(part == 2)
     used = LATE if late else shards
     shard_refs, refs = refs[:shards], refs[shards:]
@@ -257,9 +256,7 @@
                         preferred_element_type=jnp.float32,
                     )
                 )
-                if i >= lag:
-                    add(i - lag)
-            for i in range(batch - lag, batch):
+            for i in range(batch):
                 add(i)
             return carry
 
@@ -472,14 +469,14 @@
         if k < chips - 2:
             flow[x] = move(flow[x], ahead)
 
-    pieces = [1, 1, chips - 2]
+    pieces = [2, chips - 2]
     sums_shape = jax.ShapeDtypeStruct((count * clusters + 1, directions, unknowns), jnp.float32)
 
     def near(part, shards, sources, *sums):
         late = int(part == 2)
         sends = pieces if late else []
         return pl.pallas_call(
-            functools.partial(near_kernel, part, BATCH, LAG, len(shards), len(sends)),
+            functools.partial(near_kernel, part, BATCH[part], len(shards), len(sends)),
             out_shape=[sums_shape]
             + [jax.ShapeDtypeStruct((chips * half * rank_k, unknowns), jnp.bfloat16)] * late
             + [
@@ -495,7 +492,7 @@
             scratch_shapes=[
                 pltpu.VMEM(((LATE if late else len(shards)) * base, unknowns), jnp.bfloat16),
                 pltpu.VMEM(near_blocks.shape, jnp.bfloat16),
-                pltpu.SemaphoreType.DMA((max(CHUNKS, stored // BATCH),)),
+                pltpu.SemaphoreType.DMA((max(CHUNKS, stored // BATCH[part]),)),
             ],
             compiler_params=pltpu.CompilerParams(vmem_limit_bytes=NEAR_VMEM),
             cost_estimate=pl.CostEstimate(
@@ -532,23 +529,23 @@
     (sums,) = near(0, shards[: chips - LATE], [mate_blocks])
     (sums,) = near(1, shards[: chips - LATE], [near_blocks], sums)
     sums, coef, *sends = near(2, shards, [near_blocks, mate_blocks], sums)
-    mates = [move(sends[0], mate), move(sends[1], mate)]
+    mates = [move(sends[0], mate)]
     coefs = [coef, move(coef, mate)]
 
     def term(k):
-        part = min(k, 2)
-        got = mates[part][(k - part) * clusters : (k - part + 1) * clusters]
+        part, at = (0, k) if k < 2 else (1, k - 2)
+        got = mates[part][at * clusters : (at + 1) * clusters]
         return sums[k * clusters : (k + 1) * clusters] + got.astype(jnp.float32)
 
     def tied(values, k, *others):
-        values, mates[2], *others = lax.optimization_barrier((values, mates[2], *others))
+        values, mates[1], *others = lax.optimization_barrier((values, mates[1], *others))
         return values
 
     def add(flow, k):
         return (flow.astype(jnp.float32) + term(k)).astype(jnp.bfloat16)
 
     flow = lax.optimization_barrier([term(0).astype(jnp.bfloat16), term(1).astype(jnp.bfloat16)])
-    mates.append(move(after(sends[2], *flow), mate))
+    mates.append(move(after(sends[1], *flow), mate))
     flow = [move(part, ahead) for part in flow]
     for k in range(2, chips - 1):
         x = k % 2

time: 67.6 us -> 66.7 us (0.987)
  starting transfers between devices: 32.5 us -> 31.1 us
  waiting for transfers between devices: 15.7 us -> 16.8 us
  Pallas kernels: 15.5 us -> 14.5 us
    ppermute x22 -> x21, starting transfers between devices: 32.5 us -> 31.1 us  [move(): return lax.ppermute(values, 'blk', where)]
    ppermute x22 -> x21, waiting for transfers between devices: 15.7 us -> 16.8 us  [move(): return lax.ppermute(values, 'blk', where)]
    pallas_call x3, Pallas kernels: 10.8 us -> 9.77 us  [near(): pl.pallas_call(functools.partial(near_kernel, part, BATCH[part], len(shar...]
  transfers between devices with their start and end apart: 22 -> 21, of which waited for: 14 -> 13; matrix products, arithmetic and copies ran while one was open for 3% -> 4% of each run, Pallas kernels for 19% -> 17%
where the time goes in v17:
time: 66.7 us; the launch traced here: 65.8 us
  starting transfers between devices  31.1 us (47%)
  waiting for transfers between devices  16.8 us (25%)
  Pallas kernels  14.5 us (22%)
  other arithmetic  2.3 us (3%)
  local copies, waits for them, and re-layouts  0.97 us (1%)
    ppermute x21, starting transfers between devices, move(): return lax.ppermute(values, 'blk', where)  31.1 us
    ppermute x21, waiting for transfers between devices, move(): return lax.ppermute(values, 'blk', where)  16.8 us
    pallas_call x3, Pallas kernels, near(): pl.pallas_call(functools.partial(near_kernel, part, BATCH[part], len(shar...  9.77 us
    pallas_call x1, Pallas kernels, far_field(): pl.pallas_call(far_kernel, out_shape=jax.ShapeDtypeStruct((clusters, dire...  2.52 us
    pallas_call x1, Pallas kernels, stationary(): pl.pallas_call(functools.partial(prologue_kernel, count), out_shape=[jax....  2.17 us
  transfers between devices with their start and end apart: 21, of which 13 were waited for; matrix products, arithmetic and copies ran while one was open for 4% of the time, Pallas kernels for 17%

profile of v17, /device:TPU:0, one launch (start us, length us, event | category | flops | bytes accessed | tf_op | source)
XLA Modules:
  0.0 65.8 jit_solution(9084322000402451972)
XLA Ops:
  0.5 2.2 %prologue.1 = (bf16[1152,128]{1,0:T(8,128)(2,1)}, s32[8,128]{1,0:T(8,128)}) custom-call(s32[1]{0:T(128)} %bitcast.me_ref.refs_2_, s32[1,128]{1,0:T(1,128)} %bitcast.14, s32[1,128]{1,0:T(1,128)} %bitcast.15, s32[1,128]{1,0:T(1,128)} %bitcast.16, bf16[16,64,128]{2,1,0:T(8,128)(2,1)} %rhs_ref.1, bf16[16,16,128]{2,1,0:T(8,128)(2,1)} %basis_ref.1), custom_call_target="tpu_custom_call" | custom-call | tf_op jit(solution)/shard_map/prologue/pallas_call | solution.py:434
  2.6 2.6 %collective-permute-start = (bf16[1152,128]{1,0:T(8,128)(2,1)}, bf16[1152,128]{1,0:T(8,128)(2,1)S(1)}, u32[]{:S(2)}, u32[]{:S(2)}) collective-permute-start(bf16[1152,128]{1,0:T(8,128)(2,1)} %get-tuple-element.36), channel_id=1, source_target_pairs={{0,4},{1,3},{4,8},{5,1},{8,12},{9,5},{12,14},{13,9},{14,10},{15,13... | collective-permute-start | bytes 884744 | tf_op jit(solution)/shard_map/ppermute | solution.py:427
  5.2 0.9 %copy.16 = bf16[256,16,16]{0,1,2:T(8,128)(2,1)S(1)} copy(bf16[256,16,16]{0,2,1:T(8,128)(2,1)} %param.16) | data formatting | bytes 262144 | tf_op args[5]
  6.2 1.4 %collective-permute-start.6 = (bf16[1152,128]{1,0:T(8,128)(2,1)}, bf16[1152,128]{1,0:T(8,128)(2,1)S(1)}, u32[]{:S(2)}, u32[]{:S(2)}) collective-permute-start(bf16[1152,128]{1,0:T(8,128)(2,1)} %get-tuple-element.36), channel_id=1, source_target_pairs={{0,3},{1,4},{4,1},{5,8},{8,5},{9,12},{12,9},{13,14},{14,13},{15,10... | collective-permute-start | bytes 884744 | tf_op jit(solution)/shard_map/ppermute | solution.py:427
  7.9 2.9 %collective-permute-done.refs_1_ = bf16[1152,128]{1,0:T(8,128)(2,1)S(1)} collective-permute-done((bf16[1152,128]{1,0:T(8,128)(2,1)}, bf16[1152,128]{1,0:T(8,128)(2,1)S(1)}, u32[]{:S(2)}, u32[]{:S(2)}) %collective-permute-start) | collective-permute-done | bytes 294944 | tf_op jit(solution)/shard_map/ppermute | solution.py:427
  10.8 2.4 %collective-permute-start.1 = (bf16[1152,128]{1,0:T(8,128)(2,1)S(1)}, bf16[1152,128]{1,0:T(8,128)(2,1)S(1)}, u32[]{:S(2)}, u32[]{:S(2)}) collective-permute-start(bf16[1152,128]{1,0:T(8,128)(2,1)S(1)} %collective-permute-done.refs_1_), channel_id=1, source_target_pairs={{0,4},{1,3},{4,8},{5,1},{8,12},{9,5},{12,14},{13,9},{14,10},{15,13... | collective-permute-start | bytes 884744 | tf_op jit(solution)/shard_map/ppermute | solution.py:427
  13.2 2.1 %collective-permute-start.7 = (bf16[1152,128]{1,0:T(8,128)(2,1)S(1)}, bf16[1152,128]{1,0:T(8,128)(2,1)S(1)}, u32[]{:S(2)}, u32[]{:S(2)}) collective-permute-start(bf16[1152,128]{1,0:T(8,128)(2,1)S(1)} %collective-permute-done.6.refs_2_), channel_id=1, source_target_pairs={{0,4},{1,3},{4,8},{5,1},{8,12},{9,5},{12,14},{13,9},{14,10},{15,13... | collective-permute-start | bytes 884744 | tf_op jit(solution)/shard_map/ppermute | solution.py:427
  15.3 1.4 %collective-permute-done.4 = s32[8,128]{1,0:T(8,128)S(1)} collective-permute-done((s32[8,128]{1,0:T(8,128)}, s32[8,128]{1,0:T(8,128)S(1)}, u32[]{:S(2)}, u32[]{:S(2)}) %collective-permute-start.4) | collective-permute-done | bytes 4128 | tf_op jit(solution)/shard_map/ppermute | solution.py:427
  16.7 1.5 %collective-permute-done.1.refs_3_ = bf16[1152,128]{1,0:T(8,128)(2,1)S(1)} collective-permute-done((bf16[1152,128]{1,0:T(8,128)(2,1)S(1)}, bf16[1152,128]{1,0:T(8,128)(2,1)S(1)}, u32[]{:S(2)}, u32[]{:S(2)}) %collective-permute-start.1) | collective-permute-done | bytes 294944 | tf_op jit(solution)/shard_map/ppermute | solution.py:427
  18.2 1.7 %collective-permute-start.5 = (bf16[1152,128]{1,0:T(8,128)(2,1)S(1)}, bf16[1152,128]{1,0:T(8,128)(2,1)S(1)}, u32[]{:S(2)}, u32[]{:S(2)}) collective-permute-start(bf16[1152,128]{1,0:T(8,128)(2,1)S(1)} %collective-permute-done.1.refs_3_), channel_id=1, source_target_pairs={{0,4},{1,3},{4,8},{5,1},{8,12},{9,5},{12,14},{13,9},{14,10},{15,13... | collective-permute-start | bytes 884744 | tf_op jit(solution)/shard_map/ppermute | solution.py:427
  19.9 1.4 %collective-permute-done.7.refs_4_ = bf16[1152,128]{1,0:T(8,128)(2,1)S(1)} collective-permute-done((bf16[1152,128]{1,0:T(8,128)(2,1)S(1)}, bf16[1152,128]{1,0:T(8,128)(2,1)S(1)}, u32[]{:S(2)}, u32[]{:S(2)}) %collective-permute-start.7) | collective-permute-done | bytes 294944 | tf_op jit(solution)/shard_map/ppermute | solution.py:427
  21.4 1.7 %collective-permute-start.8 = (bf16[1152,128]{1,0:T(8,128)(2,1)S(1)}, bf16[1152,128]{1,0:T(8,128)(2,1)S(1)}, u32[]{:S(2)}, u32[]{:S(2)}) collective-permute-start(bf16[1152,128]{1,0:T(8,128)(2,1)S(1)} %collective-permute-done.7.refs_4_), channel_id=1, source_target_pairs={{0,4},{1,3},{4,8},{5,1},{8,12},{9,5},{12,14},{13,9},{14,10},{15,13... | collective-permute-start | bytes 884744 | tf_op jit(solution)/shard_map/ppermute | solution.py:427
  23.1 0.7 %pad_add_fusion.list_ref = s32[16,128]{1,0:T(8,128)S(1)} fusion(s32[8,128]{1,0:T(8,128)S(1)} %collective-permute-done.4, s32[8,128]{1,0:T(8,128)} %get-tuple-element.37), kind=kLoop, calls=%fused_computation.10 | loop fusion | flops 2048 | bytes 16384 | tf_op jit(solution)/shard_map/concatenate | solution.py:465
  23.8 1.1 %collective-permute-done.5.refs_5_ = bf16[1152,128]{1,0:T(8,128)(2,1)S(1)} collective-permute-done((bf16[1152,128]{1,0:T(8,128)(2,1)S(1)}, bf16[1152,128]{1,0:T(8,128)(2,1)S(1)}, u32[]{:S(2)}, u32[]{:S(2)}) %collective-permute-start.5) | collective-permute-done | bytes 294944 | tf_op jit(solution)/shard_map/ppermute | solution.py:427
  24.9 1.7 %collective-permute-start.9 = (bf16[1152,128]{1,0:T(8,128)(2,1)S(1)}, bf16[1152,128]{1,0:T(8,128)(2,1)S(1)}, u32[]{:S(2)}, u32[]{:S(2)}) collective-permute-start(bf16[1152,128]{1,0:T(8,128)(2,1)S(1)} %collective-permute-done.5.refs_5_), channel_id=1, source_target_pairs={{0,4},{1,3},{4,8},{5,1},{8,12},{9,5},{12,14},{13,9},{14,10},{15,13... | collective-permute-start | bytes 884744 | tf_op jit(solution)/shard_map/ppermute | solution.py:427
  26.7 4.0 %near.3.refs_7_ = f32[257,64,128]{2,1,0:T(8,128)S(1)} custom-call(s32[16,128]{1,0:T(8,128)S(1)} %pad_add_fusion.list_ref, bf16[1152,128]{1,0:T(8,128)(2,1)S(1)} %collective-permute-done.3.refs_0_, bf16[1152,128]{1,0:T(8,128)(2,1)S(1)} %collective-permute-done.refs_1_, bf16[1152,128]{1,0:T(8,128)(2,1)S(1)} %collective-permute-done.6.refs_2_, ...), custom_call_target="tpu_custom_call" | custom-call | flops 2147483648 | bytes 16777216 | tf_op jit(solution)/shard_map/near/pallas_call | solution.py:478
  30.7 2.5 %near.4.refs_10_ = f32[257,64,128]{2,1,0:T(8,128)S(1)} custom-call(s32[16,128]{1,0:T(8,128)S(1)} %pad_add_fusion.list_ref, bf16[1152,128]{1,0:T(8,128)(2,1)S(1)} %collective-permute-done.3.refs_0_, bf16[1152,128]{1,0:T(8,128)(2,1)S(1)} %collective-permute-done.refs_1_, ...), custom_call_target="tpu_custom_call", output_to_operand_aliasing={{}: (8, {})} | custom-call | flops 2147483648 | bytes 16777216 | tf_op jit(solution)/shard_map/near/pallas_call | solution.py:478
  33.2 3.3 %near.5 = (f32[257,64,128]{2,1,0:T(8,128)S(1)}, bf16[1024,128]{1,0:T(8,128)(2,1)S(1)}, bf16[32,64,128]{2,1,0:T(8,128)(2,1)S(1)}, bf16[96,64,128]{2,1,0:T(8,128)(2,1)S(1)}) custom-call(s32[16,128]{1,0:T(8,128)S(1)} %pad_add_fusion.list_ref, bf16[1152,128]{1,0:T(8,128)(2,1)S(1)} %collective-permute-done.3.refs_0_, ...), custom_call_target="tpu_custom_call", output_to_operand_aliasing={{0}: (11, {})} | custom-call | flops 2147483648 | bytes 16777216 | tf_op jit(solution)/shard_map/near/pallas_call | solution.py:478
  36.6 1.9 %collective-permute-done.11 = bf16[32,64,128]{2,1,0:T(8,128)(2,1)S(1)} collective-permute-done((bf16[32,64,128]{2,1,0:T(8,128)(2,1)S(1)}, bf16[32,64,128]{2,1,0:T(8,128)(2,1)S(1)}, u32[]{:S(2)}, u32[]{:S(2)}) %collective-permute-start.11) | collective-permute-done | bytes 524320 | tf_op jit(solution)/shard_map/ppermute | solution.py:427
  38.9 1.2 %collective-permute-start.12 = (bf16[16,64,128]{2,1,0:T(8,128)(2,1)S(1)}, bf16[16,64,128]{2,1,0:T(8,128)(2,1)S(1)}, u32[]{:S(2)}, u32[]{:S(2)}) collective-permute-start(bf16[16,64,128]{2,1,0:T(8,128)(2,1)S(1)} %get-tuple-element.46), channel_id=1, source_target_pairs={{0,4},{1,3},{4,8},{5,1},{8,12},{9,5},{12,14},{13,9},{14,10},{15,13... | collective-permute-start | bytes 786440 | tf_op jit(solution)/shard_map/ppermute | solution.py:427
  40.0 3.6 %collective-permute-start.15 = (bf16[16,64,128]{2,1,0:T(8,128)(2,1)S(1)}, bf16[16,64,128]{2,1,0:T(8,128)(2,1)S(1)}, u32[]{:S(2)}, u32[]{:S(2)}) collective-permute-start(bf16[16,64,128]{2,1,0:T(8,128)(2,1)S(1)} %get-tuple-element.48), channel_id=1, source_target_pairs={{0,4},{1,3},{4,8},{5,1},{8,12},{9,5},{12,14},{13,9},{14,10},{15,13... | collective-permute-start | bytes 786440 | tf_op jit(solution)/shard_map/ppermute | solution.py:427
  43.6 1.6 %collective-permute-done.12 = bf16[16,64,128]{2,1,0:T(8,128)(2,1)S(1)} collective-permute-done((bf16[16,64,128]{2,1,0:T(8,128)(2,1)S(1)}, bf16[16,64,128]{2,1,0:T(8,128)(2,1)S(1)}, u32[]{:S(2)}, u32[]{:S(2)}) %collective-permute-start.12) | collective-permute-done | bytes 262176 | tf_op jit(solution)/shard_map/ppermute | solution.py:427
  45.4 2.3 %collective-permute-start.14 = (bf16[16,64,128]{2,1,0:T(8,128)(2,1)S(1)}, bf16[16,64,128]{2,1,0:T(8,128)(2,1)S(1)}, u32[]{:S(2)}, u32[]{:S(2)}) collective-permute-start(bf16[16,64,128]{2,1,0:T(8,128)(2,1)S(1)} %add_convert_fusion.5), channel_id=1, source_target_pairs={{0,4},{1,3},{4,8},{5,1},{8,12},{9,5},{12,14},{13,9},{14,10},{15,13... | collective-permute-start | bytes 786440 | tf_op jit(solution)/shard_map/ppermute | solution.py:427
  48.2 2.3 %collective-permute-start.17 = (bf16[16,64,128]{2,1,0:T(8,128)(2,1)S(1)}, bf16[16,64,128]{2,1,0:T(8,128)(2,1)S(1)}, u32[]{:S(2)}, u32[]{:S(2)}) collective-permute-start(bf16[16,64,128]{2,1,0:T(8,128)(2,1)S(1)} %add_convert_fusion.4), channel_id=1, source_target_pairs={{0,4},{1,3},{4,8},{5,1},{8,12},{9,5},{12,14},{13,9},{14,10},{15,13... | collective-permute-start | bytes 786440 | tf_op jit(solution)/shard_map/ppermute | solution.py:427
  50.5 1.3 %collective-permute-done.14 = bf16[16,64,128]{2,1,0:T(8,128)(2,1)S(1)} collective-permute-done((bf16[16,64,128]{2,1,0:T(8,128)(2,1)S(1)}, bf16[16,64,128]{2,1,0:T(8,128)(2,1)S(1)}, u32[]{:S(2)}, u32[]{:S(2)}) %collective-permute-start.14) | collective-permute-done | bytes 262176 | tf_op jit(solution)/shard_map/ppermute | solution.py:427
  51.9 2.3 %collective-permute-start.16 = (bf16[16,64,128]{2,1,0:T(8,128)(2,1)S(1)}, bf16[16,64,128]{2,1,0:T(8,128)(2,1)S(1)}, u32[]{:S(2)}, u32[]{:S(2)}) collective-permute-start(bf16[16,64,128]{2,1,0:T(8,128)(2,1)S(1)} %add_convert_fusion.3), channel_id=1, source_target_pairs={{0,4},{1,3},{4,8},{5,1},{8,12},{9,5},{12,14},{13,9},{14,10},{15,13... | collective-permute-start | bytes 786440 | tf_op jit(solution)/shard_map/ppermute | solution.py:427
  54.7 2.3 %collective-permute-start.19 = (bf16[16,64,128]{2,1,0:T(8,128)(2,1)S(1)}, bf16[16,64,128]{2,1,0:T(8,128)(2,1)S(1)}, u32[]{:S(2)}, u32[]{:S(2)}) collective-permute-start(bf16[16,64,128]{2,1,0:T(8,128)(2,1)S(1)} %add_convert_fusion.2), channel_id=1, source_target_pairs={{0,4},{1,3},{4,8},{5,1},{8,12},{9,5},{12,14},{13,9},{14,10},{15,13... | collective-permute-start | bytes 786440 | tf_op jit(solution)/shard_map/ppermute | solution.py:427
  57.0 1.3 %collective-permute-done.16 = bf16[16,64,128]{2,1,0:T(8,128)(2,1)S(1)} collective-permute-done((bf16[16,64,128]{2,1,0:T(8,128)(2,1)S(1)}, bf16[16,64,128]{2,1,0:T(8,128)(2,1)S(1)}, u32[]{:S(2)}, u32[]{:S(2)}) %collective-permute-start.16) | collective-permute-done | bytes 262176 | tf_op jit(solution)/shard_map/ppermute | solution.py:427
  58.4 2.3 %collective-permute-start.18 = (bf16[16,64,128]{2,1,0:T(8,128)(2,1)S(1)}, bf16[16,64,128]{2,1,0:T(8,128)(2,1)S(1)}, u32[]{:S(2)}, u32[]{:S(2)}) collective-permute-start(bf16[16,64,128]{2,1,0:T(8,128)(2,1)S(1)} %add_convert_fusion.1), channel_id=1, source_target_pairs={{0,4},{1,3},{4,8},{5,1},{8,12},{9,5},{12,14},{13,9},{14,10},{15,13... | collective-permute-start | bytes 786440 | tf_op jit(solution)/shard_map/ppermute | solution.py:427
  61.2 2.5 %far.1 = f32[16,64,128]{2,1,0:T(8,128)S(1)} custom-call(bf16[1024,128]{1,0:T(8,128)(2,1)S(1)} %get-tuple-element.43.refs_0_, bf16[1024,128]{1,0:T(8,128)(2,1)S(1)} %collective-permute-done.10.refs_1_, s32[1]{0:T(128)} %bitcast.me_ref.refs_2_, bf16[16,16,256]{2,1,0:T(8,128)(2,1)S(1)} %bitcast.10, s32[1,256]{1,0:T(1,128)S(1)} %bitcast.11, ...), custom_call_target="tpu_custom_call" | custom-call | flops 536870912 | bytes 8388608 | tf_op jit(solution)/shard_map/far/pallas_call | solution.py:507
  63.7 1.1 %collective-permute-done.18 = bf16[16,64,128]{2,1,0:T(8,128)(2,1)S(1)} collective-permute-done((bf16[16,64,128]{2,1,0:T(8,128)(2,1)S(1)}, bf16[16,64,128]{2,1,0:T(8,128)(2,1)S(1)}, u32[]{:S(2)}, u32[]{:S(2)}) %collective-permute-start.18) | collective-permute-done | bytes 262176 | tf_op jit(solution)/shard_map/ppermute | solution.py:427
  65.0 0.8 %add_convert_fusion = bf16[16,64,128]{2,1,0:T(8,128)(2,1)} fusion(f32[16,64,128]{2,1,0:T(8,128)S(1)} %convert_add_fusion, bf16[16,64,128]{2,1,0:T(8,128)(2,1)S(1)} %collective-permute-done.20), kind=kLoop, calls=%fused_computation | loop fusion | flops 393216 | bytes 1048576 | tf_op jit(solution)/shard_map/convert_element_type | solution.py:559
  (35 shorter events, 3.1 us)
Async XLA Ops:
  0.0 18.2 %collective-permute-start.2 = (bf16[128,128,128]{2,1,0:T(8,128)(2,1)}, bf16[128,128,128]{2,1,0:T(8,128)(2,1)}, u32[]{:S(2)}, u32[]{:S(2)}) collective-permute-start(bf16[128,128,128]{2,1,0:T(8,128)(2,1)} %refs_8_.1), channel_id=1, source_target_pairs={{0,1},{1,0},{2,3},{3,2},{4,5},{5,4},{6,7},{7,6},{8,9},{9,8},{10,11... | collective-permute-start | bytes 12582920 | tf_op jit(solution)/shard_map/ppermute | solution.py:427
  0.5 30.3 %copy-start = (bf16[128,128,128]{2,1,0:T(8,128)(2,1)S(1)}, bf16[128,128,128]{2,1,0:T(8,128)(2,1)}, u32[]{:S(2)}) copy-start(bf16[128,128,128]{2,1,0:T(8,128)(2,1)} %refs_8_.1) | copy-start | bytes 12582916
  2.6 8.2 %collective-permute-start = (bf16[1152,128]{1,0:T(8,128)(2,1)}, bf16[1152,128]{1,0:T(8,128)(2,1)S(1)}, u32[]{:S(2)}, u32[]{:S(2)}) collective-permute-start(bf16[1152,128]{1,0:T(8,128)(2,1)} %get-tuple-element.36), channel_id=1, source_target_pairs={{0,4},{1,3},{4,8},{5,1},{8,12},{9,5},{12,14},{13,9},{14,10},{15,13... | collective-permute-start | bytes 884744 | tf_op jit(solution)/shard_map/ppermute | solution.py:427
  6.2 7.1 %collective-permute-start.6 = (bf16[1152,128]{1,0:T(8,128)(2,1)}, bf16[1152,128]{1,0:T(8,128)(2,1)S(1)}, u32[]{:S(2)}, u32[]{:S(2)}) collective-permute-start(bf16[1152,128]{1,0:T(8,128)(2,1)} %get-tuple-element.36), channel_id=1, source_target_pairs={{0,3},{1,4},{4,1},{5,8},{8,5},{9,12},{12,9},{13,14},{14,13},{15,10... | collective-permute-start | bytes 884744 | tf_op jit(solution)/shard_map/ppermute | solution.py:427
  7.6 9.1 %collective-permute-start.3 = (bf16[1152,128]{1,0:T(8,128)(2,1)}, bf16[1152,128]{1,0:T(8,128)(2,1)S(1)}, u32[]{:S(2)}, u32[]{:S(2)}) collective-permute-start(bf16[1152,128]{1,0:T(8,128)(2,1)} %get-tuple-element.36), channel_id=1, source_target_pairs={{0,1},{1,0},{2,3},{3,2},{4,5},{5,4},{6,7},{7,6},{8,9},{9,8},{10,11... | collective-permute-start | bytes 884744 | tf_op jit(solution)/shard_map/ppermute | solution.py:427
  10.8 7.4 %collective-permute-start.1 = (bf16[1152,128]{1,0:T(8,128)(2,1)S(1)}, bf16[1152,128]{1,0:T(8,128)(2,1)S(1)}, u32[]{:S(2)}, u32[]{:S(2)}) collective-permute-start(bf16[1152,128]{1,0:T(8,128)(2,1)S(1)} %collective-permute-done.refs_1_), channel_id=1, source_target_pairs={{0,4},{1,3},{4,8},{5,1},{8,12},{9,5},{12,14},{13,9},{14,10},{15,13... | collective-permute-start | bytes 884744 | tf_op jit(solution)/shard_map/ppermute | solution.py:427
  13.2 8.1 %collective-permute-start.7 = (bf16[1152,128]{1,0:T(8,128)(2,1)S(1)}, bf16[1152,128]{1,0:T(8,128)(2,1)S(1)}, u32[]{:S(2)}, u32[]{:S(2)}) collective-permute-start(bf16[1152,128]{1,0:T(8,128)(2,1)S(1)} %collective-permute-done.6.refs_2_), channel_id=1, source_target_pairs={{0,4},{1,3},{4,8},{5,1},{8,12},{9,5},{12,14},{13,9},{14,10},{15,13... | collective-permute-start | bytes 884744 | tf_op jit(solution)/shard_map/ppermute | solution.py:427
  15.3 1.4 %collective-permute-start.4 = (s32[8,128]{1,0:T(8,128)}, s32[8,128]{1,0:T(8,128)S(1)}, u32[]{:S(2)}, u32[]{:S(2)}) collective-permute-start(s32[8,128]{1,0:T(8,128)} %get-tuple-element.37), channel_id=1, source_target_pairs={{0,1},{1,0},{2,3},{3,2},{4,5},{5,4},{6,7},{7,6},{8,9},{9,8},{10,11... | collective-permute-start | bytes 12296 | tf_op jit(solution)/shard_map/ppermute | solution.py:427
  18.2 6.7 %collective-permute-start.5 = (bf16[1152,128]{1,0:T(8,128)(2,1)S(1)}, bf16[1152,128]{1,0:T(8,128)(2,1)S(1)}, u32[]{:S(2)}, u32[]{:S(2)}) collective-permute-start(bf16[1152,128]{1,0:T(8,128)(2,1)S(1)} %collective-permute-done.1.refs_3_), channel_id=1, source_target_pairs={{0,4},{1,3},{4,8},{5,1},{8,12},{9,5},{12,14},{13,9},{14,10},{15,13... | collective-permute-start | bytes 884744 | tf_op jit(solution)/shard_map/ppermute | solution.py:427
  21.4 11.8 %collective-permute-start.8 = (bf16[1152,128]{1,0:T(8,128)(2,1)S(1)}, bf16[1152,128]{1,0:T(8,128)(2,1)S(1)}, u32[]{:S(2)}, u32[]{:S(2)}) collective-permute-start(bf16[1152,128]{1,0:T(8,128)(2,1)S(1)} %collective-permute-done.7.refs_4_), channel_id=1, source_target_pairs={{0,4},{1,3},{4,8},{5,1},{8,12},{9,5},{12,14},{13,9},{14,10},{15,13... | collective-permute-start | bytes 884744 | tf_op jit(solution)/shard_map/ppermute | solution.py:427
  24.9 8.3 %collective-permute-start.9 = (bf16[1152,128]{1,0:T(8,128)(2,1)S(1)}, bf16[1152,128]{1,0:T(8,128)(2,1)S(1)}, u32[]{:S(2)}, u32[]{:S(2)}) collective-permute-start(bf16[1152,128]{1,0:T(8,128)(2,1)S(1)} %collective-permute-done.5.refs_5_), channel_id=1, source_target_pairs={{0,4},{1,3},{4,8},{5,1},{8,12},{9,5},{12,14},{13,9},{14,10},{15,13... | collective-permute-start | bytes 884744 | tf_op jit(solution)/shard_map/ppermute | solution.py:427
  36.5 24.7 %copy-start.1 = (bf16[16,16,128]{2,1,0:T(8,128)(2,1)S(1)}, bf16[16,16,128]{2,1,0:T(8,128)(2,1)}, u32[]{:S(2)}) copy-start(bf16[16,16,128]{2,1,0:T(8,128)(2,1)} %refs_7_.1) | copy-start | bytes 196612
  36.5 24.7 %copy-start.2 = (s32[256]{0:T(256)S(1)}, s32[256]{0:T(256)}, u32[]{:S(2)}) copy-start(s32[256]{0:T(256)} %param.17) | copy-start | bytes 3076
  36.5 24.7 %copy-start.3 = (s32[256,1]{0,1:T(1,128)S(1)}, s32[256,1]{0,1:T(1,128)}, u32[]{:S(2)}) copy-start(s32[256,1]{0,1:T(1,128)} %param.18) | copy-start | bytes 3076
  36.5 24.7 %copy-start.4 = (s32[256]{0:T(256)S(1)}, s32[256]{0:T(256)}, u32[]{:S(2)}) copy-start(s32[256]{0:T(256)} %param.19) | copy-start | bytes 3076
  36.5 2.0 %collective-permute-start.11 = (bf16[32,64,128]{2,1,0:T(8,128)(2,1)S(1)}, bf16[32,64,128]{2,1,0:T(8,128)(2,1)S(1)}, u32[]{:S(2)}, u32[]{:S(2)}) collective-permute-start(bf16[32,64,128]{2,1,0:T(8,128)(2,1)S(1)} %get-tuple-element.45), channel_id=1, source_target_pairs={{0,1},{1,0},{2,3},{3,2},{4,5},{5,4},{6,7},{7,6},{8,9},{9,8},{10,11... | collective-permute-start | bytes 1572872 | tf_op jit(solution)/shard_map/ppermute | solution.py:427
  38.7 6.6 %collective-permute-start.13 = (bf16[96,64,128]{2,1,0:T(8,128)(2,1)S(1)}, bf16[96,64,128]{2,1,0:T(8,128)(2,1)S(1)}, u32[]{:S(2)}, u32[]{:S(2)}) collective-permute-start(bf16[96,64,128]{2,1,0:T(8,128)(2,1)S(1)} %get-tuple-element.49), channel_id=1, source_target_pairs={{0,1},{1,0},{2,3},{3,2},{4,5},{5,4},{6,7},{7,6},{8,9},{9,8},{10,11... | collective-permute-start | bytes 4718600 | tf_op jit(solution)/shard_map/ppermute | solution.py:427
  38.9 6.4 %collective-permute-start.12 = (bf16[16,64,128]{2,1,0:T(8,128)(2,1)S(1)}, bf16[16,64,128]{2,1,0:T(8,128)(2,1)S(1)}, u32[]{:S(2)}, u32[]{:S(2)}) collective-permute-start(bf16[16,64,128]{2,1,0:T(8,128)(2,1)S(1)} %get-tuple-element.46), channel_id=1, source_target_pairs={{0,4},{1,3},{4,8},{5,1},{8,12},{9,5},{12,14},{13,9},{14,10},{15,13... | collective-permute-start | bytes 786440 | tf_op jit(solution)/shard_map/ppermute | solution.py:427
  40.0 8.0 %collective-permute-start.15 = (bf16[16,64,128]{2,1,0:T(8,128)(2,1)S(1)}, bf16[16,64,128]{2,1,0:T(8,128)(2,1)S(1)}, u32[]{:S(2)}, u32[]{:S(2)}) collective-permute-start(bf16[16,64,128]{2,1,0:T(8,128)(2,1)S(1)} %get-tuple-element.48), channel_id=1, source_target_pairs={{0,4},{1,3},{4,8},{5,1},{8,12},{9,5},{12,14},{13,9},{14,10},{15,13... | collective-permute-start | bytes 786440 | tf_op jit(solution)/shard_map/ppermute | solution.py:427
  45.4 6.4 %collective-permute-start.14 = (bf16[16,64,128]{2,1,0:T(8,128)(2,1)S(1)}, bf16[16,64,128]{2,1,0:T(8,128)(2,1)S(1)}, u32[]{:S(2)}, u32[]{:S(2)}) collective-permute-start(bf16[16,64,128]{2,1,0:T(8,128)(2,1)S(1)} %add_convert_fusion.5), channel_id=1, source_target_pairs={{0,4},{1,3},{4,8},{5,1},{8,12},{9,5},{12,14},{13,9},{14,10},{15,13... | collective-permute-start | bytes 786440 | tf_op jit(solution)/shard_map/ppermute | solution.py:427
  48.2 6.4 %collective-permute-start.17 = (bf16[16,64,128]{2,1,0:T(8,128)(2,1)S(1)}, bf16[16,64,128]{2,1,0:T(8,128)(2,1)S(1)}, u32[]{:S(2)}, u32[]{:S(2)}) collective-permute-start(bf16[16,64,128]{2,1,0:T(8,128)(2,1)S(1)} %add_convert_fusion.4), channel_id=1, source_target_pairs={{0,4},{1,3},{4,8},{5,1},{8,12},{9,5},{12,14},{13,9},{14,10},{15,13... | collective-permute-start | bytes 786440 | tf_op jit(solution)/shard_map/ppermute | solution.py:427
  51.9 6.4 %collective-permute-start.16 = (bf16[16,64,128]{2,1,0:T(8,128)(2,1)S(1)}, bf16[16,64,128]{2,1,0:T(8,128)(2,1)S(1)}, u32[]{:S(2)}, u32[]{:S(2)}) collective-permute-start(bf16[16,64,128]{2,1,0:T(8,128)(2,1)S(1)} %add_convert_fusion.3), channel_id=1, source_target_pairs={{0,4},{1,3},{4,8},{5,1},{8,12},{9,5},{12,14},{13,9},{14,10},{15,13... | collective-permute-start | bytes 786440 | tf_op jit(solution)/shard_map/ppermute | solution.py:427
  54.2 6.9 %collective-permute-start.10 = (bf16[1024,128]{1,0:T(8,128)(2,1)S(1)}, bf16[1024,128]{1,0:T(8,128)(2,1)S(1)}, u32[]{:S(2)}, u32[]{:S(2)}) collective-permute-start(bf16[1024,128]{1,0:T(8,128)(2,1)S(1)} %get-tuple-element.43.refs_0_), channel_id=1, source_target_pairs={{0,1},{1,0},{2,3},{3,2},{4,5},{5,4},{6,7},{7,6},{8,9},{9,8},{10,11... | collective-permute-start | bytes 786440 | tf_op jit(solution)/shard_map/ppermute | solution.py:427
  54.7 6.4 %collective-permute-start.19 = (bf16[16,64,128]{2,1,0:T(8,128)(2,1)S(1)}, bf16[16,64,128]{2,1,0:T(8,128)(2,1)S(1)}, u32[]{:S(2)}, u32[]{:S(2)}) collective-permute-start(bf16[16,64,128]{2,1,0:T(8,128)(2,1)S(1)} %add_convert_fusion.2), channel_id=1, source_target_pairs={{0,4},{1,3},{4,8},{5,1},{8,12},{9,5},{12,14},{13,9},{14,10},{15,13... | collective-permute-start | bytes 786440 | tf_op jit(solution)/shard_map/ppermute | solution.py:427
  58.4 6.4 %collective-permute-start.18 = (bf16[16,64,128]{2,1,0:T(8,128)(2,1)S(1)}, bf16[16,64,128]{2,1,0:T(8,128)(2,1)S(1)}, u32[]{:S(2)}, u32[]{:S(2)}) collective-permute-start(bf16[16,64,128]{2,1,0:T(8,128)(2,1)S(1)} %add_convert_fusion.1), channel_id=1, source_target_pairs={{0,4},{1,3},{4,8},{5,1},{8,12},{9,5},{12,14},{13,9},{14,10},{15,13... | collective-permute-start | bytes 786440 | tf_op jit(solution)/shard_map/ppermute | solution.py:427
  61.1 3.9 %collective-permute-start.20 = (bf16[16,64,128]{2,1,0:T(8,128)(2,1)S(1)}, bf16[16,64,128]{2,1,0:T(8,128)(2,1)S(1)}, u32[]{:S(2)}, u32[]{:S(2)}) collective-permute-start(bf16[16,64,128]{2,1,0:T(8,128)(2,1)S(1)} %collective-permute-done.19), channel_id=1, source_target_pairs={{0,1},{1,0},{2,3},{3,2},{4,5},{5,4},{6,7},{7,6},{8,9},{9,8},{10,11... | collective-permute-start | bytes 786440 | tf_op jit(solution)/shard_map/ppermute | solution.py:427

commit v18 on v17

--- a/solution.py
+++ b/solution.py
@@ -118,9 +118,7 @@
     return pl.BlockSpec(memory_space=space)
 
 
-def prologue_kernel(
-    count, me_ref, owner_ref, slot_ref, offset_ref, rhs_ref, basis_ref, payload_ref, list_ref
-):
+def payload_kernel(rhs_ref, basis_ref, payload_ref):
     clusters, directions, unknowns = rhs_ref.shape
     base = clusters * directions
     payload_ref[0:base, :] = rhs_ref[...].reshape(base, unknowns)
@@ -138,10 +136,17 @@
             for e in (c, c + half)
         ]
         rows.append(jnp.concatenate(parts, axis=1))
-    payload_ref[base:, :] = jnp.concatenate(
-        [row[q : q + 1] for q in range(rank_k) for row in rows], axis=0
+    rows = jnp.concatenate(rows, axis=0).astype(payload_ref.dtype)
+    square = (rows.shape[0], rows.shape[0])
+    row = lax.broadcasted_iota(jnp.int32, square, 0)
+    source = (row & (half - 1)) * rank_k + row // half
+    order = jnp.where(lax.broadcasted_iota(jnp.int32, square, 1) == source, 1.0, 0.0)
+    payload_ref[base:, :] = jnp.dot(
+        order.astype(rows.dtype), rows, preferred_element_type=jnp.float32
     ).astype(payload_ref.dtype)
 
+
+def list_kernel(count, clusters, me_ref, owner_ref, slot_ref, offset_ref, list_ref):
     me, owner, slot = me_ref[0], owner_ref[...], slot_ref[...]
     stored = owner.shape[1]
     place = scatter_place(owner, me, count) * clusters + slot
@@ -150,7 +155,7 @@
     theirs = (shard == count // 2).astype(jnp.int32)
     shard = jnp.where(theirs == 1, gather_place(column // clusters, me ^ 1, count), shard)
     column_place = shard * clusters + (column & (clusters - 1))
-    late = (shard >= count // 2 - LATE).astype(jnp.int32)
+    late = (shard >= count // 2 - LATE + 1 - theirs).astype(jnp.int32)
     square = (stored, stored)
     group = jnp.broadcast_to((2 * theirs + late).astype(jnp.float32), square)
     group_of_row = jnp.transpose(group)
@@ -219,7 +224,7 @@
             ]
             return carry
 
-        lax.fori_loop(0, span // directions, gather, 0, unroll=4)
+        lax.fori_loop(0, span // directions, gather, 0, unroll=8)
     if late:
         tail = coef_ref.shape[0] // shards
         for k, ref in enumerate(shard_refs):
@@ -230,7 +235,8 @@
             sums[i] = jnp.zeros(sums.shape[1:], sums.dtype)
             return carry
 
-        lax.fori_loop(0, dummy + 1, clear, 0)
+        lax.fori_loop(0, dummy, clear, 0, unroll=8)
+        clear(dummy, 0)
 
     def run(begin, end, row, swap, block_of):
         def entry(j):
@@ -297,7 +303,7 @@
             send_ref[i] = sums[at + i].astype(send_ref.dtype)
             return carry
 
-        lax.fori_loop(0, send_ref.shape[0], pack, 0, unroll=2)
+        lax.fori_loop(0, send_ref.shape[0], pack, 0, unroll=8)
         at += send_ref.shape[0]
 
 
@@ -431,29 +437,33 @@
 
     here = me.astype(jnp.int32).reshape(1)
     base = clusters * directions
-    payload, lists = pl.pallas_call(
-        functools.partial(prologue_kernel, count),
-        out_shape=[
-            jax.ShapeDtypeStruct((base + half * rank_k, unknowns), jnp.bfloat16),
-            jax.ShapeDtypeStruct((8, stored), jnp.int32),
-        ],
-        in_specs=[whole(pltpu.SMEM)] + [whole()] * 5,
-        out_specs=[whole()] * 2,
-        compiler_params=pltpu.CompilerParams(vmem_limit_bytes=PROLOGUE_VMEM),
-        name="prologue",
+    params = pltpu.CompilerParams(vmem_limit_bytes=PROLOGUE_VMEM)
+    payload = pl.pallas_call(
+        payload_kernel,
+        out_shape=jax.ShapeDtypeStruct((base + half * rank_k, unknowns), jnp.bfloat16),
+        in_specs=[whole()] * 2,
+        out_specs=whole(),
+        compiler_params=params,
+        name="payload",
+    )(rhs, basis_in)
+    lists = pl.pallas_call(
+        functools.partial(list_kernel, count, clusters),
+        out_shape=jax.ShapeDtypeStruct((8, stored), jnp.int32),
+        in_specs=[whole(pltpu.SMEM)] + [whole()] * 3,
+        out_specs=whole(),
+        compiler_params=params,
+        name="lists",
     )(
-        here,
+        after(here, payload),
         near_owner.reshape(1, stored),
         near_slot.reshape(1, stored),
         near_offset.reshape(1, stored),
-        rhs,
-        basis_in,
     )
     flow = [move(payload, ahead)]
     mate_blocks = move(near_blocks, mate)
     mate_lists = move(lists, mate)
     couple = jnp.transpose(far_coupling, (2, 1, 0))
-    flow.append(move(after(payload, couple), cross))
+    flow.append(move(after(payload, couple, lists), cross))
     shards = [move(payload, mate)]
     for k in range(1, chips):
         x = 1 - k % 2
@@ -527,7 +537,7 @@
         )
 
     (sums,) = near(0, shards[: chips - LATE], [mate_blocks])
-    (sums,) = near(1, shards[: chips - LATE], [near_blocks], sums)
+    (sums,) = near(1, shards[: chips - LATE + 1], [near_blocks], sums)
     sums, coef, *sends = near(2, shards, [near_blocks, mate_blocks], sums)
     mates = [move(sends[0], mate)]
     coefs = [coef, move(coef, mate)]

time: 66.7 us -> 66.5 us (level); the launches traced: 65.8 us -> 66.3 us
  starting transfers between devices: 31.1 us -> 19.1 us
  waiting for transfers between devices: 16.8 us -> 27.7 us
  Pallas kernels: 14.5 us -> 16 us
    ppermute x21, starting transfers between devices: 31.1 us -> 19.1 us  [move(): return lax.ppermute(values, 'blk', where)]
    ppermute x21, waiting for transfers between devices: 16.8 us -> 27.7 us  [move(): return lax.ppermute(values, 'blk', where)]
    pallas_call x1 -> x2, Pallas kernels: 2.17 us -> 3.99 us  [the longest x1 2.13 us: stationary(): pl.pallas_call(payload_kernel, out_shape=jax.ShapeDtypeStruct((base + hal...]
  transfers between devices with their start and end apart: 21 -> 21, of which waited for: 13 -> 13; matrix products, arithmetic and copies ran while one was open for 4% -> 4% of each run, Pallas kernels for 17% -> 20%
where the time goes in v18:
time: 66.5 us; the launch traced here: 66.3 us
  waiting for transfers between devices  27.7 us (42%)
  starting transfers between devices  19.1 us (29%)
  Pallas kernels  16 us (24%)
  other arithmetic  2.32 us (3%)
  local copies, waits for them, and re-layouts  1.12 us (2%)
    ppermute x21, waiting for transfers between devices, move(): return lax.ppermute(values, 'blk', where)  27.7 us
    ppermute x21, starting transfers between devices, move(): return lax.ppermute(values, 'blk', where)  19.1 us
    pallas_call x3, Pallas kernels, near(): pl.pallas_call(functools.partial(near_kernel, part, BATCH[part], len(shar...  9.47 us
    pallas_call x1, Pallas kernels, far_field(): pl.pallas_call(far_kernel, out_shape=jax.ShapeDtypeStruct((clusters, dire...  2.51 us
    pallas_call x1, Pallas kernels, stationary(): pl.pallas_call(payload_kernel, out_shape=jax.ShapeDtypeStruct((base + hal...  2.13 us
    pallas_call x1, Pallas kernels, stationary(): pl.pallas_call(functools.partial(list_kernel, count, clusters), out_shape...  1.86 us
  transfers between devices with their start and end apart: 21, of which 13 were waited for; matrix products, arithmetic and copies ran while one was open for 4% of the time, Pallas kernels for 20%

profile of v18, /device:TPU:0, one launch (start us, length us, event | category | flops | bytes accessed | tf_op | source)
XLA Modules:
  0.0 66.3 jit_solution(11333342637533175287)
XLA Ops:
  0.5 2.1 %payload.1 = bf16[1152,128]{1,0:T(8,128)(2,1)} custom-call(bf16[16,64,128]{2,1,0:T(8,128)(2,1)} %rhs_ref.1, bf16[16,16,128]{2,1,0:T(8,128)(2,1)} %basis_ref.1), custom_call_target="tpu_custom_call" | custom-call | tf_op jit(solution)/shard_map/payload/pallas_call | solution.py:441
  2.6 2.6 %collective-permute-start = (bf16[1152,128]{1,0:T(8,128)(2,1)}, bf16[1152,128]{1,0:T(8,128)(2,1)S(1)}, u32[]{:S(2)}, u32[]{:S(2)}) collective-permute-start(bf16[1152,128]{1,0:T(8,128)(2,1)} %payload.1), channel_id=1, source_target_pairs={{0,4},{1,3},{4,8},{5,1},{8,12},{9,5},{12,14},{13,9},{14,10},{15,13... | collective-permute-start | bytes 884744 | tf_op jit(solution)/shard_map/ppermute | solution.py:433
  5.2 1.1 %copy.16 = bf16[256,16,16]{0,1,2:T(8,128)(2,1)S(1)} copy(bf16[256,16,16]{0,2,1:T(8,128)(2,1)} %param.16) | data formatting | bytes 262144 | tf_op args[5]
  6.3 1.9 %lists.1 = s32[8,128]{1,0:T(8,128)} custom-call(s32[1]{0:T(128)} %bitcast.me_ref.refs_2_, s32[1,128]{1,0:T(1,128)} %bitcast.14, s32[1,128]{1,0:T(1,128)} %bitcast.15, s32[1,128]{1,0:T(1,128)} %bitcast.16), custom_call_target="tpu_custom_call" | custom-call | tf_op jit(solution)/shard_map/lists/pallas_call | solution.py:449
  8.1 1.4 %collective-permute-start.6 = (bf16[1152,128]{1,0:T(8,128)(2,1)}, bf16[1152,128]{1,0:T(8,128)(2,1)S(1)}, u32[]{:S(2)}, u32[]{:S(2)}) collective-permute-start(bf16[1152,128]{1,0:T(8,128)(2,1)} %payload.1), channel_id=1, source_target_pairs={{0,3},{1,4},{4,1},{5,8},{8,5},{9,12},{12,9},{13,14},{14,13},{15,10... | collective-permute-start | bytes 884744 | tf_op jit(solution)/shard_map/ppermute | solution.py:433
  10.0 2.1 %collective-permute-start.1 = (bf16[1152,128]{1,0:T(8,128)(2,1)S(1)}, bf16[1152,128]{1,0:T(8,128)(2,1)S(1)}, u32[]{:S(2)}, u32[]{:S(2)}) collective-permute-start(bf16[1152,128]{1,0:T(8,128)(2,1)S(1)} %collective-permute-done.refs_1_), channel_id=1, source_target_pairs={{0,4},{1,3},{4,8},{5,1},{8,12},{9,5},{12,14},{13,9},{14,10},{15,13... | collective-permute-start | bytes 884744 | tf_op jit(solution)/shard_map/ppermute | solution.py:433
  12.1 4.0 %collective-permute-done.6.refs_2_ = bf16[1152,128]{1,0:T(8,128)(2,1)S(1)} collective-permute-done((bf16[1152,128]{1,0:T(8,128)(2,1)}, bf16[1152,128]{1,0:T(8,128)(2,1)S(1)}, u32[]{:S(2)}, u32[]{:S(2)}) %collective-permute-start.6) | collective-permute-done | bytes 294944 | tf_op jit(solution)/shard_map/ppermute | solution.py:433
  16.7 1.6 %collective-permute-start.4 = (s32[8,128]{1,0:T(8,128)}, s32[8,128]{1,0:T(8,128)S(1)}, u32[]{:S(2)}, u32[]{:S(2)}) collective-permute-start(s32[8,128]{1,0:T(8,128)} %lists.1), channel_id=1, source_target_pairs={{0,1},{1,0},{2,3},{3,2},{4,5},{5,4},{6,7},{7,6},{8,9},{9,8},{10,11... | collective-permute-start | bytes 12296 | tf_op jit(solution)/shard_map/ppermute | solution.py:433
  18.4 1.0 %collective-permute-done.4 = s32[8,128]{1,0:T(8,128)S(1)} collective-permute-done((s32[8,128]{1,0:T(8,128)}, s32[8,128]{1,0:T(8,128)S(1)}, u32[]{:S(2)}, u32[]{:S(2)}) %collective-permute-start.4) | collective-permute-done | bytes 4128 | tf_op jit(solution)/shard_map/ppermute | solution.py:433
  20.0 2.8 %collective-permute-done.7.refs_4_ = bf16[1152,128]{1,0:T(8,128)(2,1)S(1)} collective-permute-done((bf16[1152,128]{1,0:T(8,128)(2,1)S(1)}, bf16[1152,128]{1,0:T(8,128)(2,1)S(1)}, u32[]{:S(2)}, u32[]{:S(2)}) %collective-permute-start.7) | collective-permute-done | bytes 294944 | tf_op jit(solution)/shard_map/ppermute | solution.py:433
  23.4 0.7 %pad_add_fusion.list_ref = s32[16,128]{1,0:T(8,128)S(1)} fusion(s32[8,128]{1,0:T(8,128)S(1)} %collective-permute-done.4, s32[8,128]{1,0:T(8,128)} %lists.1), kind=kLoop, calls=%fused_computation.10 | loop fusion | flops 2048 | bytes 16384 | tf_op jit(solution)/shard_map/concatenate | solution.py:475
  24.1 2.0 %collective-permute-done.5.refs_5_ = bf16[1152,128]{1,0:T(8,128)(2,1)S(1)} collective-permute-done((bf16[1152,128]{1,0:T(8,128)(2,1)S(1)}, bf16[1152,128]{1,0:T(8,128)(2,1)S(1)}, u32[]{:S(2)}, u32[]{:S(2)}) %collective-permute-start.5) | collective-permute-done | bytes 294944 | tf_op jit(solution)/shard_map/ppermute | solution.py:433
  26.8 3.5 %near.3.refs_8_ = f32[257,64,128]{2,1,0:T(8,128)S(1)} custom-call(s32[16,128]{1,0:T(8,128)S(1)} %pad_add_fusion.list_ref, bf16[1152,128]{1,0:T(8,128)(2,1)S(1)} %collective-permute-done.3.refs_0_, bf16[1152,128]{1,0:T(8,128)(2,1)S(1)} %collective-permute-done.refs_1_, bf16[1152,128]{1,0:T(8,128)(2,1)S(1)} %collective-permute-done.6.refs_2_, ...), custom_call_target="tpu_custom_call" | custom-call | flops 2147483648 | bytes 16777216 | tf_op jit(solution)/shard_map/near/pallas_call | solution.py:488
  30.3 2.9 %near.4.refs_10_ = f32[257,64,128]{2,1,0:T(8,128)S(1)} custom-call(s32[16,128]{1,0:T(8,128)S(1)} %pad_add_fusion.list_ref, bf16[1152,128]{1,0:T(8,128)(2,1)S(1)} %collective-permute-done.3.refs_0_, bf16[1152,128]{1,0:T(8,128)(2,1)S(1)} %collective-permute-done.refs_1_, ...), custom_call_target="tpu_custom_call", output_to_operand_aliasing={{}: (9, {})} | custom-call | flops 2147483648 | bytes 16777216 | tf_op jit(solution)/shard_map/near/pallas_call | solution.py:488
  33.3 3.0 %near.5 = (f32[257,64,128]{2,1,0:T(8,128)S(1)}, bf16[1024,128]{1,0:T(8,128)(2,1)S(1)}, bf16[32,64,128]{2,1,0:T(8,128)(2,1)S(1)}, bf16[96,64,128]{2,1,0:T(8,128)(2,1)S(1)}) custom-call(s32[16,128]{1,0:T(8,128)S(1)} %pad_add_fusion.list_ref, bf16[1152,128]{1,0:T(8,128)(2,1)S(1)} %collective-permute-done.3.refs_0_, ...), custom_call_target="tpu_custom_call", output_to_operand_aliasing={{0}: (11, {})} | custom-call | flops 2147483648 | bytes 16777216 | tf_op jit(solution)/shard_map/near/pallas_call | solution.py:488
  36.3 0.9 %collective-permute-start.11 = (bf16[32,64,128]{2,1,0:T(8,128)(2,1)S(1)}, bf16[32,64,128]{2,1,0:T(8,128)(2,1)S(1)}, u32[]{:S(2)}, u32[]{:S(2)}) collective-permute-start(bf16[32,64,128]{2,1,0:T(8,128)(2,1)S(1)} %get-tuple-element.43), channel_id=1, source_target_pairs={{0,1},{1,0},{2,3},{3,2},{4,5},{5,4},{6,7},{7,6},{8,9},{9,8},{10,11... | collective-permute-start | bytes 1572872 | tf_op jit(solution)/shard_map/ppermute | solution.py:433
  37.2 1.5 %collective-permute-done.11 = bf16[32,64,128]{2,1,0:T(8,128)(2,1)S(1)} collective-permute-done((bf16[32,64,128]{2,1,0:T(8,128)(2,1)S(1)}, bf16[32,64,128]{2,1,0:T(8,128)(2,1)S(1)}, u32[]{:S(2)}, u32[]{:S(2)}) %collective-permute-start.11) | collective-permute-done | bytes 524320 | tf_op jit(solution)/shard_map/ppermute | solution.py:433
  39.4 1.0 %collective-permute-start.12 = (bf16[16,64,128]{2,1,0:T(8,128)(2,1)S(1)}, bf16[16,64,128]{2,1,0:T(8,128)(2,1)S(1)}, u32[]{:S(2)}, u32[]{:S(2)}) collective-permute-start(bf16[16,64,128]{2,1,0:T(8,128)(2,1)S(1)} %get-tuple-element.44), channel_id=1, source_target_pairs={{0,4},{1,3},{4,8},{5,1},{8,12},{9,5},{12,14},{13,9},{14,10},{15,13... | collective-permute-start | bytes 786440 | tf_op jit(solution)/shard_map/ppermute | solution.py:433
  40.9 4.8 %collective-permute-done.12 = bf16[16,64,128]{2,1,0:T(8,128)(2,1)S(1)} collective-permute-done((bf16[16,64,128]{2,1,0:T(8,128)(2,1)S(1)}, bf16[16,64,128]{2,1,0:T(8,128)(2,1)S(1)}, u32[]{:S(2)}, u32[]{:S(2)}) %collective-permute-start.12) | collective-permute-done | bytes 262176 | tf_op jit(solution)/shard_map/ppermute | solution.py:433
  45.9 1.1 %collective-permute-start.14 = (bf16[16,64,128]{2,1,0:T(8,128)(2,1)S(1)}, bf16[16,64,128]{2,1,0:T(8,128)(2,1)S(1)}, u32[]{:S(2)}, u32[]{:S(2)}) collective-permute-start(bf16[16,64,128]{2,1,0:T(8,128)(2,1)S(1)} %add_convert_fusion.5), channel_id=1, source_target_pairs={{0,4},{1,3},{4,8},{5,1},{8,12},{9,5},{12,14},{13,9},{14,10},{15,13... | collective-permute-start | bytes 786440 | tf_op jit(solution)/shard_map/ppermute | solution.py:433
  47.0 1.6 %collective-permute-done.15 = bf16[16,64,128]{2,1,0:T(8,128)(2,1)S(1)} collective-permute-done((bf16[16,64,128]{2,1,0:T(8,128)(2,1)S(1)}, bf16[16,64,128]{2,1,0:T(8,128)(2,1)S(1)}, u32[]{:S(2)}, u32[]{:S(2)}) %collective-permute-start.15) | collective-permute-done | bytes 262176 | tf_op jit(solution)/shard_map/ppermute | solution.py:433
  48.7 1.1 %collective-permute-start.17 = (bf16[16,64,128]{2,1,0:T(8,128)(2,1)S(1)}, bf16[16,64,128]{2,1,0:T(8,128)(2,1)S(1)}, u32[]{:S(2)}, u32[]{:S(2)}) collective-permute-start(bf16[16,64,128]{2,1,0:T(8,128)(2,1)S(1)} %add_convert_fusion.4), channel_id=1, source_target_pairs={{0,4},{1,3},{4,8},{5,1},{8,12},{9,5},{12,14},{13,9},{14,10},{15,13... | collective-permute-start | bytes 786440 | tf_op jit(solution)/shard_map/ppermute | solution.py:433
  49.8 2.5 %collective-permute-done.14 = bf16[16,64,128]{2,1,0:T(8,128)(2,1)S(1)} collective-permute-done((bf16[16,64,128]{2,1,0:T(8,128)(2,1)S(1)}, bf16[16,64,128]{2,1,0:T(8,128)(2,1)S(1)}, u32[]{:S(2)}, u32[]{:S(2)}) %collective-permute-start.14) | collective-permute-done | bytes 262176 | tf_op jit(solution)/shard_map/ppermute | solution.py:433
  52.4 1.1 %collective-permute-start.16 = (bf16[16,64,128]{2,1,0:T(8,128)(2,1)S(1)}, bf16[16,64,128]{2,1,0:T(8,128)(2,1)S(1)}, u32[]{:S(2)}, u32[]{:S(2)}) collective-permute-start(bf16[16,64,128]{2,1,0:T(8,128)(2,1)S(1)} %add_convert_fusion.3), channel_id=1, source_target_pairs={{0,4},{1,3},{4,8},{5,1},{8,12},{9,5},{12,14},{13,9},{14,10},{15,13... | collective-permute-start | bytes 786440 | tf_op jit(solution)/shard_map/ppermute | solution.py:433
  53.5 1.6 %collective-permute-done.17 = bf16[16,64,128]{2,1,0:T(8,128)(2,1)S(1)} collective-permute-done((bf16[16,64,128]{2,1,0:T(8,128)(2,1)S(1)}, bf16[16,64,128]{2,1,0:T(8,128)(2,1)S(1)}, u32[]{:S(2)}, u32[]{:S(2)}) %collective-permute-start.17) | collective-permute-done | bytes 262176 | tf_op jit(solution)/shard_map/ppermute | solution.py:433
  55.2 1.1 %collective-permute-start.19 = (bf16[16,64,128]{2,1,0:T(8,128)(2,1)S(1)}, bf16[16,64,128]{2,1,0:T(8,128)(2,1)S(1)}, u32[]{:S(2)}, u32[]{:S(2)}) collective-permute-start(bf16[16,64,128]{2,1,0:T(8,128)(2,1)S(1)} %add_convert_fusion.2), channel_id=1, source_target_pairs={{0,4},{1,3},{4,8},{5,1},{8,12},{9,5},{12,14},{13,9},{14,10},{15,13... | collective-permute-start | bytes 786440 | tf_op jit(solution)/shard_map/ppermute | solution.py:433
  56.3 2.5 %collective-permute-done.16 = bf16[16,64,128]{2,1,0:T(8,128)(2,1)S(1)} collective-permute-done((bf16[16,64,128]{2,1,0:T(8,128)(2,1)S(1)}, bf16[16,64,128]{2,1,0:T(8,128)(2,1)S(1)}, u32[]{:S(2)}, u32[]{:S(2)}) %collective-permute-start.16) | collective-permute-done | bytes 262176 | tf_op jit(solution)/shard_map/ppermute | solution.py:433
  59.0 1.1 %collective-permute-start.18 = (bf16[16,64,128]{2,1,0:T(8,128)(2,1)S(1)}, bf16[16,64,128]{2,1,0:T(8,128)(2,1)S(1)}, u32[]{:S(2)}, u32[]{:S(2)}) collective-permute-start(bf16[16,64,128]{2,1,0:T(8,128)(2,1)S(1)} %add_convert_fusion.1), channel_id=1, source_target_pairs={{0,4},{1,3},{4,8},{5,1},{8,12},{9,5},{12,14},{13,9},{14,10},{15,13... | collective-permute-start | bytes 786440 | tf_op jit(solution)/shard_map/ppermute | solution.py:433
  60.0 1.6 %collective-permute-done.19 = bf16[16,64,128]{2,1,0:T(8,128)(2,1)S(1)} collective-permute-done((bf16[16,64,128]{2,1,0:T(8,128)(2,1)S(1)}, bf16[16,64,128]{2,1,0:T(8,128)(2,1)S(1)}, u32[]{:S(2)}, u32[]{:S(2)}) %collective-permute-start.19) | collective-permute-done | bytes 262176 | tf_op jit(solution)/shard_map/ppermute | solution.py:433
  61.7 2.5 %far.1 = f32[16,64,128]{2,1,0:T(8,128)S(1)} custom-call(bf16[1024,128]{1,0:T(8,128)(2,1)S(1)} %get-tuple-element.41.refs_0_, bf16[1024,128]{1,0:T(8,128)(2,1)S(1)} %collective-permute-done.10.refs_1_, s32[1]{0:T(128)} %bitcast.me_ref.refs_2_, bf16[16,16,256]{2,1,0:T(8,128)(2,1)S(1)} %bitcast.10, s32[1,256]{1,0:T(1,128)S(1)} %bitcast.11, ...), custom_call_target="tpu_custom_call" | custom-call | flops 536870912 | bytes 8388608 | tf_op jit(solution)/shard_map/far/pallas_call | solution.py:517
  64.2 1.2 %collective-permute-done.18 = bf16[16,64,128]{2,1,0:T(8,128)(2,1)S(1)} collective-permute-done((bf16[16,64,128]{2,1,0:T(8,128)(2,1)S(1)}, bf16[16,64,128]{2,1,0:T(8,128)(2,1)S(1)}, u32[]{:S(2)}, u32[]{:S(2)}) %collective-permute-start.18) | collective-permute-done | bytes 262176 | tf_op jit(solution)/shard_map/ppermute | solution.py:433
  65.5 0.8 %add_convert_fusion = bf16[16,64,128]{2,1,0:T(8,128)(2,1)} fusion(f32[16,64,128]{2,1,0:T(8,128)S(1)} %convert_add_fusion, bf16[16,64,128]{2,1,0:T(8,128)(2,1)S(1)} %collective-permute-done.20), kind=kLoop, calls=%fused_computation | loop fusion | flops 393216 | bytes 1048576 | tf_op jit(solution)/shard_map/convert_element_type | solution.py:569
  (36 shorter events, 5.2 us)
Async XLA Ops:
  0.0 19.4 %collective-permute-start.2 = (bf16[128,128,128]{2,1,0:T(8,128)(2,1)}, bf16[128,128,128]{2,1,0:T(8,128)(2,1)}, u32[]{:S(2)}, u32[]{:S(2)}) collective-permute-start(bf16[128,128,128]{2,1,0:T(8,128)(2,1)} %refs_8_.1), channel_id=1, source_target_pairs={{0,1},{1,0},{2,3},{3,2},{4,5},{5,4},{6,7},{7,6},{8,9},{9,8},{10,11... | collective-permute-start | bytes 12582920 | tf_op jit(solution)/shard_map/ppermute | solution.py:433
  2.6 7.4 %collective-permute-start = (bf16[1152,128]{1,0:T(8,128)(2,1)}, bf16[1152,128]{1,0:T(8,128)(2,1)S(1)}, u32[]{:S(2)}, u32[]{:S(2)}) collective-permute-start(bf16[1152,128]{1,0:T(8,128)(2,1)} %payload.1), channel_id=1, source_target_pairs={{0,4},{1,3},{4,8},{5,1},{8,12},{9,5},{12,14},{13,9},{14,10},{15,13... | collective-permute-start | bytes 884744 | tf_op jit(solution)/shard_map/ppermute | solution.py:433
  5.2 25.2 %copy-start = (bf16[128,128,128]{2,1,0:T(8,128)(2,1)S(1)}, bf16[128,128,128]{2,1,0:T(8,128)(2,1)}, u32[]{:S(2)}) copy-start(bf16[128,128,128]{2,1,0:T(8,128)(2,1)} %refs_8_.1) | copy-start | bytes 12582916
  8.1 8.0 %collective-permute-start.6 = (bf16[1152,128]{1,0:T(8,128)(2,1)}, bf16[1152,128]{1,0:T(8,128)(2,1)S(1)}, u32[]{:S(2)}, u32[]{:S(2)}) collective-permute-start(bf16[1152,128]{1,0:T(8,128)(2,1)} %payload.1), channel_id=1, source_target_pairs={{0,3},{1,4},{4,1},{5,8},{8,5},{9,12},{12,9},{13,14},{14,13},{15,10... | collective-permute-start | bytes 884744 | tf_op jit(solution)/shard_map/ppermute | solution.py:433
  9.5 9.9 %collective-permute-start.3 = (bf16[1152,128]{1,0:T(8,128)(2,1)}, bf16[1152,128]{1,0:T(8,128)(2,1)S(1)}, u32[]{:S(2)}, u32[]{:S(2)}) collective-permute-start(bf16[1152,128]{1,0:T(8,128)(2,1)} %payload.1), channel_id=1, source_target_pairs={{0,1},{1,0},{2,3},{3,2},{4,5},{5,4},{6,7},{7,6},{8,9},{9,8},{10,11... | collective-permute-start | bytes 884744 | tf_op jit(solution)/shard_map/ppermute | solution.py:433
  10.0 9.4 %collective-permute-start.1 = (bf16[1152,128]{1,0:T(8,128)(2,1)S(1)}, bf16[1152,128]{1,0:T(8,128)(2,1)S(1)}, u32[]{:S(2)}, u32[]{:S(2)}) collective-permute-start(bf16[1152,128]{1,0:T(8,128)(2,1)S(1)} %collective-permute-done.refs_1_), channel_id=1, source_target_pairs={{0,4},{1,3},{4,8},{5,1},{8,12},{9,5},{12,14},{13,9},{14,10},{15,13... | collective-permute-start | bytes 884744 | tf_op jit(solution)/shard_map/ppermute | solution.py:433
  16.1 6.7 %collective-permute-start.7 = (bf16[1152,128]{1,0:T(8,128)(2,1)S(1)}, bf16[1152,128]{1,0:T(8,128)(2,1)S(1)}, u32[]{:S(2)}, u32[]{:S(2)}) collective-permute-start(bf16[1152,128]{1,0:T(8,128)(2,1)S(1)} %collective-permute-done.6.refs_2_), channel_id=1, source_target_pairs={{0,4},{1,3},{4,8},{5,1},{8,12},{9,5},{12,14},{13,9},{14,10},{15,13... | collective-permute-start | bytes 884744 | tf_op jit(solution)/shard_map/ppermute | solution.py:433
  16.7 2.7 %collective-permute-start.4 = (s32[8,128]{1,0:T(8,128)}, s32[8,128]{1,0:T(8,128)S(1)}, u32[]{:S(2)}, u32[]{:S(2)}) collective-permute-start(s32[8,128]{1,0:T(8,128)} %lists.1), channel_id=1, source_target_pairs={{0,1},{1,0},{2,3},{3,2},{4,5},{5,4},{6,7},{7,6},{8,9},{9,8},{10,11... | collective-permute-start | bytes 12296 | tf_op jit(solution)/shard_map/ppermute | solution.py:433
  19.4 6.8 %collective-permute-start.5 = (bf16[1152,128]{1,0:T(8,128)(2,1)S(1)}, bf16[1152,128]{1,0:T(8,128)(2,1)S(1)}, u32[]{:S(2)}, u32[]{:S(2)}) collective-permute-start(bf16[1152,128]{1,0:T(8,128)(2,1)S(1)} %collective-permute-done.1.refs_3_), channel_id=1, source_target_pairs={{0,4},{1,3},{4,8},{5,1},{8,12},{9,5},{12,14},{13,9},{14,10},{15,13... | collective-permute-start | bytes 884744 | tf_op jit(solution)/shard_map/ppermute | solution.py:433
  22.9 7.4 %collective-permute-start.8 = (bf16[1152,128]{1,0:T(8,128)(2,1)S(1)}, bf16[1152,128]{1,0:T(8,128)(2,1)S(1)}, u32[]{:S(2)}, u32[]{:S(2)}) collective-permute-start(bf16[1152,128]{1,0:T(8,128)(2,1)S(1)} %collective-permute-done.7.refs_4_), channel_id=1, source_target_pairs={{0,4},{1,3},{4,8},{5,1},{8,12},{9,5},{12,14},{13,9},{14,10},{15,13... | collective-permute-start | bytes 884744 | tf_op jit(solution)/shard_map/ppermute | solution.py:433
  26.2 7.1 %collective-permute-start.9 = (bf16[1152,128]{1,0:T(8,128)(2,1)S(1)}, bf16[1152,128]{1,0:T(8,128)(2,1)S(1)}, u32[]{:S(2)}, u32[]{:S(2)}) collective-permute-start(bf16[1152,128]{1,0:T(8,128)(2,1)S(1)} %collective-permute-done.5.refs_5_), channel_id=1, source_target_pairs={{0,4},{1,3},{4,8},{5,1},{8,12},{9,5},{12,14},{13,9},{14,10},{15,13... | collective-permute-start | bytes 884744 | tf_op jit(solution)/shard_map/ppermute | solution.py:433
  36.3 25.4 %copy-start.1 = (bf16[16,16,128]{2,1,0:T(8,128)(2,1)S(1)}, bf16[16,16,128]{2,1,0:T(8,128)(2,1)}, u32[]{:S(2)}) copy-start(bf16[16,16,128]{2,1,0:T(8,128)(2,1)} %refs_7_.3) | copy-start | bytes 196612
  36.3 25.4 %copy-start.2 = (s32[256]{0:T(256)S(1)}, s32[256]{0:T(256)}, u32[]{:S(2)}) copy-start(s32[256]{0:T(256)} %param.17) | copy-start | bytes 3076
  36.3 25.4 %copy-start.3 = (s32[256,1]{0,1:T(1,128)S(1)}, s32[256,1]{0,1:T(1,128)}, u32[]{:S(2)}) copy-start(s32[256,1]{0,1:T(1,128)} %param.18) | copy-start | bytes 3076
  36.3 25.4 %copy-start.4 = (s32[256]{0:T(256)S(1)}, s32[256]{0:T(256)}, u32[]{:S(2)}) copy-start(s32[256]{0:T(256)} %param.19) | copy-start | bytes 3076
  36.3 2.5 %collective-permute-start.11 = (bf16[32,64,128]{2,1,0:T(8,128)(2,1)S(1)}, bf16[32,64,128]{2,1,0:T(8,128)(2,1)S(1)}, u32[]{:S(2)}, u32[]{:S(2)}) collective-permute-start(bf16[32,64,128]{2,1,0:T(8,128)(2,1)S(1)} %get-tuple-element.43), channel_id=1, source_target_pairs={{0,1},{1,0},{2,3},{3,2},{4,5},{5,4},{6,7},{7,6},{8,9},{9,8},{10,11... | collective-permute-start | bytes 1572872 | tf_op jit(solution)/shard_map/ppermute | solution.py:433
  38.9 6.8 %collective-permute-start.13 = (bf16[96,64,128]{2,1,0:T(8,128)(2,1)S(1)}, bf16[96,64,128]{2,1,0:T(8,128)(2,1)S(1)}, u32[]{:S(2)}, u32[]{:S(2)}) collective-permute-start(bf16[96,64,128]{2,1,0:T(8,128)(2,1)S(1)} %get-tuple-element.47), channel_id=1, source_target_pairs={{0,1},{1,0},{2,3},{3,2},{4,5},{5,4},{6,7},{7,6},{8,9},{9,8},{10,11... | collective-permute-start | bytes 4718600 | tf_op jit(solution)/shard_map/ppermute | solution.py:433
  39.4 6.4 %collective-permute-start.12 = (bf16[16,64,128]{2,1,0:T(8,128)(2,1)S(1)}, bf16[16,64,128]{2,1,0:T(8,128)(2,1)S(1)}, u32[]{:S(2)}, u32[]{:S(2)}) collective-permute-start(bf16[16,64,128]{2,1,0:T(8,128)(2,1)S(1)} %get-tuple-element.44), channel_id=1, source_target_pairs={{0,4},{1,3},{4,8},{5,1},{8,12},{9,5},{12,14},{13,9},{14,10},{15,13... | collective-permute-start | bytes 786440 | tf_op jit(solution)/shard_map/ppermute | solution.py:433
  40.4 8.2 %collective-permute-start.15 = (bf16[16,64,128]{2,1,0:T(8,128)(2,1)S(1)}, bf16[16,64,128]{2,1,0:T(8,128)(2,1)S(1)}, u32[]{:S(2)}, u32[]{:S(2)}) collective-permute-start(bf16[16,64,128]{2,1,0:T(8,128)(2,1)S(1)} %get-tuple-element.46), channel_id=1, source_target_pairs={{0,4},{1,3},{4,8},{5,1},{8,12},{9,5},{12,14},{13,9},{14,10},{15,13... | collective-permute-start | bytes 786440 | tf_op jit(solution)/shard_map/ppermute | solution.py:433
  45.9 6.4 %collective-permute-start.14 = (bf16[16,64,128]{2,1,0:T(8,128)(2,1)S(1)}, bf16[16,64,128]{2,1,0:T(8,128)(2,1)S(1)}, u32[]{:S(2)}, u32[]{:S(2)}) collective-permute-start(bf16[16,64,128]{2,1,0:T(8,128)(2,1)S(1)} %add_convert_fusion.5), channel_id=1, source_target_pairs={{0,4},{1,3},{4,8},{5,1},{8,12},{9,5},{12,14},{13,9},{14,10},{15,13... | collective-permute-start | bytes 786440 | tf_op jit(solution)/shard_map/ppermute | solution.py:433
  48.7 6.4 %collective-permute-start.17 = (bf16[16,64,128]{2,1,0:T(8,128)(2,1)S(1)}, bf16[16,64,128]{2,1,0:T(8,128)(2,1)S(1)}, u32[]{:S(2)}, u32[]{:S(2)}) collective-permute-start(bf16[16,64,128]{2,1,0:T(8,128)(2,1)S(1)} %add_convert_fusion.4), channel_id=1, source_target_pairs={{0,4},{1,3},{4,8},{5,1},{8,12},{9,5},{12,14},{13,9},{14,10},{15,13... | collective-permute-start | bytes 786440 | tf_op jit(solution)/shard_map/ppermute | solution.py:433
  52.4 6.4 %collective-permute-start.16 = (bf16[16,64,128]{2,1,0:T(8,128)(2,1)S(1)}, bf16[16,64,128]{2,1,0:T(8,128)(2,1)S(1)}, u32[]{:S(2)}, u32[]{:S(2)}) collective-permute-start(bf16[16,64,128]{2,1,0:T(8,128)(2,1)S(1)} %add_convert_fusion.3), channel_id=1, source_target_pairs={{0,4},{1,3},{4,8},{5,1},{8,12},{9,5},{12,14},{13,9},{14,10},{15,13... | collective-permute-start | bytes 786440 | tf_op jit(solution)/shard_map/ppermute | solution.py:433
  53.5 8.2 %collective-permute-start.10 = (bf16[1024,128]{1,0:T(8,128)(2,1)S(1)}, bf16[1024,128]{1,0:T(8,128)(2,1)S(1)}, u32[]{:S(2)}, u32[]{:S(2)}) collective-permute-start(bf16[1024,128]{1,0:T(8,128)(2,1)S(1)} %get-tuple-element.41.refs_0_), channel_id=1, source_target_pairs={{0,1},{1,0},{2,3},{3,2},{4,5},{5,4},{6,7},{7,6},{8,9},{9,8},{10,11... | collective-permute-start | bytes 786440 | tf_op jit(solution)/shard_map/ppermute | solution.py:433
  55.2 6.4 %collective-permute-start.19 = (bf16[16,64,128]{2,1,0:T(8,128)(2,1)S(1)}, bf16[16,64,128]{2,1,0:T(8,128)(2,1)S(1)}, u32[]{:S(2)}, u32[]{:S(2)}) collective-permute-start(bf16[16,64,128]{2,1,0:T(8,128)(2,1)S(1)} %add_convert_fusion.2), channel_id=1, source_target_pairs={{0,4},{1,3},{4,8},{5,1},{8,12},{9,5},{12,14},{13,9},{14,10},{15,13... | collective-permute-start | bytes 786440 | tf_op jit(solution)/shard_map/ppermute | solution.py:433
  59.0 6.4 %collective-permute-start.18 = (bf16[16,64,128]{2,1,0:T(8,128)(2,1)S(1)}, bf16[16,64,128]{2,1,0:T(8,128)(2,1)S(1)}, u32[]{:S(2)}, u32[]{:S(2)}) collective-permute-start(bf16[16,64,128]{2,1,0:T(8,128)(2,1)S(1)} %add_convert_fusion.1), channel_id=1, source_target_pairs={{0,4},{1,3},{4,8},{5,1},{8,12},{9,5},{12,14},{13,9},{14,10},{15,13... | collective-permute-start | bytes 786440 | tf_op jit(solution)/shard_map/ppermute | solution.py:433
  61.7 3.9 %collective-permute-start.20 = (bf16[16,64,128]{2,1,0:T(8,128)(2,1)S(1)}, bf16[16,64,128]{2,1,0:T(8,128)(2,1)S(1)}, u32[]{:S(2)}, u32[]{:S(2)}) collective-permute-start(bf16[16,64,128]{2,1,0:T(8,128)(2,1)S(1)} %collective-permute-done.19), channel_id=1, source_target_pairs={{0,1},{1,0},{2,3},{3,2},{4,5},{5,4},{6,7},{7,6},{8,9},{9,8},{10,11... | collective-permute-start | bytes 786440 | tf_op jit(solution)/shard_map/ppermute | solution.py:433

commit v19 on v17

--- a/solution.py
+++ b/solution.py
@@ -10,6 +10,7 @@
 BATCH = 16, 16, 8
 CHUNKS = 4
 LATE = 2
+UNITS = 1
 PROLOGUE_VMEM = 58 << 20
 NEAR_VMEM = 20 << 20
 FAR_VMEM = 16 << 20
@@ -138,8 +139,13 @@
             for e in (c, c + half)
         ]
         rows.append(jnp.concatenate(parts, axis=1))
-    payload_ref[base:, :] = jnp.concatenate(
-        [row[q : q + 1] for q in range(rank_k) for row in rows], axis=0
+    rows = jnp.concatenate(rows, axis=0).astype(payload_ref.dtype)
+    square = (rows.shape[0], rows.shape[0])
+    row = lax.broadcasted_iota(jnp.int32, square, 0)
+    source = (row & (half - 1)) * rank_k + row // half
+    order = jnp.where(lax.broadcasted_iota(jnp.int32, square, 1) == source, 1.0, 0.0)
+    payload_ref[base:, :] = jnp.dot(
+        order.astype(rows.dtype), rows, preferred_element_type=jnp.float32
     ).astype(payload_ref.dtype)
 
     me, owner, slot = me_ref[0], owner_ref[...], slot_ref[...]
@@ -150,7 +156,7 @@
     theirs = (shard == count // 2).astype(jnp.int32)
     shard = jnp.where(theirs == 1, gather_place(column // clusters, me ^ 1, count), shard)
     column_place = shard * clusters + (column & (clusters - 1))
-    late = (shard >= count // 2 - LATE).astype(jnp.int32)
+    late = (shard >= count // 2 - LATE + 1 - theirs).astype(jnp.int32)
     square = (stored, stored)
     group = jnp.broadcast_to((2 * theirs + late).astype(jnp.float32), square)
     group_of_row = jnp.transpose(group)
@@ -219,7 +225,7 @@
             ]
             return carry
 
-        lax.fori_loop(0, span // directions, gather, 0, unroll=4)
+        lax.fori_loop(0, span // directions, gather, 0, unroll=8)
     if late:
         tail = coef_ref.shape[0] // shards
         for k, ref in enumerate(shard_refs):
@@ -230,7 +236,8 @@
             sums[i] = jnp.zeros(sums.shape[1:], sums.dtype)
             return carry
 
-        lax.fori_loop(0, dummy + 1, clear, 0)
+        lax.fori_loop(0, dummy, clear, 0, unroll=8)
+        clear(dummy, 0)
 
     def run(begin, end, row, swap, block_of):
         def entry(j):
@@ -297,7 +304,7 @@
             send_ref[i] = sums[at + i].astype(send_ref.dtype)
             return carry
 
-        lax.fori_loop(0, send_ref.shape[0], pack, 0, unroll=2)
+        lax.fori_loop(0, send_ref.shape[0], pack, 0, unroll=8)
         at += send_ref.shape[0]
 
 
@@ -527,36 +534,37 @@
         )
 
     (sums,) = near(0, shards[: chips - LATE], [mate_blocks])
-    (sums,) = near(1, shards[: chips - LATE], [near_blocks], sums)
+    (sums,) = near(1, shards[: chips - LATE + 1], [near_blocks], sums)
     sums, coef, *sends = near(2, shards, [near_blocks, mate_blocks], sums)
     mates = [move(sends[0], mate)]
     coefs = [coef, move(coef, mate)]
 
-    def term(k):
+    piece = clusters // UNITS
+
+    def term(k, h):
         part, at = (0, k) if k < 2 else (1, k - 2)
-        got = mates[part][at * clusters : (at + 1) * clusters]
-        return sums[k * clusters : (k + 1) * clusters] + got.astype(jnp.float32)
-
-    def tied(values, k, *others):
-        values, mates[1], *others = lax.optimization_barrier((values, mates[1], *others))
-        return values
-
-    def add(flow, k):
-        return (flow.astype(jnp.float32) + term(k)).astype(jnp.bfloat16)
-
-    flow = lax.optimization_barrier([term(0).astype(jnp.bfloat16), term(1).astype(jnp.bfloat16)])
-    mates.append(move(after(sends[1], *flow), mate))
-    flow = [move(part, ahead) for part in flow]
+        got = mates[part][at * clusters + h * piece : at * clusters + (h + 1) * piece]
+        at = k * clusters + h * piece
+        return sums[at : at + piece] + got.astype(jnp.float32)
+
+    flow = lax.optimization_barrier(
+        [[term(k, h).astype(jnp.bfloat16) for h in range(UNITS)] for k in range(2)]
+    )
+    mates.append(move(after(sends[1], *flow[0], *flow[1]), mate))
+    flow = [[move(unit, ahead) for unit in units] for units in flow]
     for k in range(2, chips - 1):
-        x = k % 2
-        flow[x] = tied(add(flow[x], k), k)
-        if k == chips - 2:
-            couple = after(couple, flow[x])
-        flow[x] = move(flow[x], ahead)
-    flow[1] = move(flow[1], mate)
-    total = far_field(couple) + term(chips - 1) + flow[0].astype(jnp.float32)
+        for h in range(UNITS):
+            unit = (flow[k % 2][h].astype(jnp.float32) + term(k, h)).astype(jnp.bfloat16)
+            unit, mates[1] = lax.optimization_barrier((unit, mates[1]))
+            if (k, h) == (chips - 2, UNITS - 1):
+                couple = after(couple, unit)
+            flow[k % 2][h] = move(unit, ahead)
+    last = [move(unit, mate) for unit in flow[1]]
+    own = sums[(chips - 1) * clusters : chips * clusters]
+    total = far_field(couple) + own + mates[1][(chips - 3) * clusters :].astype(jnp.float32)
+    total = total + jnp.concatenate(flow[0], axis=0).astype(jnp.float32)
     total = lax.optimization_barrier(total)
-    return (total + flow[1].astype(jnp.float32)).astype(jnp.bfloat16)
+    return (total + jnp.concatenate(last, axis=0).astype(jnp.float32)).astype(jnp.bfloat16)
 
 
 def on_device(*args):

time: 66.7 us -> 66 us (0.990); the launches traced: 65.8 us -> 65.9 us
  starting transfers between devices: 31.1 us -> 26.4 us
  waiting for transfers between devices: 16.8 us -> 21.5 us
    ppermute x21, starting transfers between devices: 31.1 us -> 26.4 us  [move(): return lax.ppermute(values, 'blk', where)]
    ppermute x21, waiting for transfers between devices: 16.8 us -> 21.5 us  [move(): return lax.ppermute(values, 'blk', where)]
  transfers between devices with their start and end apart: 21 -> 21, of which waited for: 13 -> 13; matrix products, arithmetic and copies ran while one was open for 4% -> 4% of each run, Pallas kernels for 17% -> 18%
where the time goes in v19:
time: 66 us; the launch traced here: 65.9 us
  starting transfers between devices  26.4 us (40%)
  waiting for transfers between devices  21.5 us (33%)
  Pallas kernels  14.6 us (22%)
  other arithmetic  2.32 us (4%)
  local copies, waits for them, and re-layouts  0.97 us (1%)
    ppermute x21, starting transfers between devices, move(): return lax.ppermute(values, 'blk', where)  26.4 us
    ppermute x21, waiting for transfers between devices, move(): return lax.ppermute(values, 'blk', where)  21.5 us
    pallas_call x3, Pallas kernels, near(): pl.pallas_call(functools.partial(near_kernel, part, BATCH[part], len(shar...  9.74 us
    pallas_call x1, Pallas kernels, far_field(): pl.pallas_call(far_kernel, out_shape=jax.ShapeDtypeStruct((clusters, dire...  2.51 us
    pallas_call x1, Pallas kernels, stationary(): pl.pallas_call(functools.partial(prologue_kernel, count), out_shape=[jax....  2.3 us
  transfers between devices with their start and end apart: 21, of which 13 were waited for; matrix products, arithmetic and copies ran while one was open for 4% of the time, Pallas kernels for 18%

profile of v19, /device:TPU:0, one launch (start us, length us, event | category | flops | bytes accessed | tf_op | source)
XLA Modules:
  0.0 65.9 jit_solution(11170297040985105723)
XLA Ops:
  0.5 2.3 %prologue.1 = (bf16[1152,128]{1,0:T(8,128)(2,1)}, s32[8,128]{1,0:T(8,128)}) custom-call(s32[1]{0:T(128)} %bitcast.me_ref.refs_2_, s32[1,128]{1,0:T(1,128)} %bitcast.14, s32[1,128]{1,0:T(1,128)} %bitcast.15, s32[1,128]{1,0:T(1,128)} %bitcast.16, bf16[16,64,128]{2,1,0:T(8,128)(2,1)} %rhs_ref.1, bf16[16,16,128]{2,1,0:T(8,128)(2,1)} %basis_ref.1), custom_call_target="tpu_custom_call" | custom-call | tf_op jit(solution)/shard_map/prologue/pallas_call | solution.py:441
  2.8 2.6 %collective-permute-start = (bf16[1152,128]{1,0:T(8,128)(2,1)}, bf16[1152,128]{1,0:T(8,128)(2,1)S(1)}, u32[]{:S(2)}, u32[]{:S(2)}) collective-permute-start(bf16[1152,128]{1,0:T(8,128)(2,1)} %get-tuple-element.36), channel_id=1, source_target_pairs={{0,4},{1,3},{4,8},{5,1},{8,12},{9,5},{12,14},{13,9},{14,10},{15,13... | collective-permute-start | bytes 884744 | tf_op jit(solution)/shard_map/ppermute | solution.py:434
  6.3 1.4 %collective-permute-start.6 = (bf16[1152,128]{1,0:T(8,128)(2,1)}, bf16[1152,128]{1,0:T(8,128)(2,1)S(1)}, u32[]{:S(2)}, u32[]{:S(2)}) collective-permute-start(bf16[1152,128]{1,0:T(8,128)(2,1)} %get-tuple-element.36), channel_id=1, source_target_pairs={{0,3},{1,4},{4,1},{5,8},{8,5},{9,12},{12,9},{13,14},{14,13},{15,10... | collective-permute-start | bytes 884744 | tf_op jit(solution)/shard_map/ppermute | solution.py:434
  8.0 2.9 %collective-permute-done.refs_1_ = bf16[1152,128]{1,0:T(8,128)(2,1)S(1)} collective-permute-done((bf16[1152,128]{1,0:T(8,128)(2,1)}, bf16[1152,128]{1,0:T(8,128)(2,1)S(1)}, u32[]{:S(2)}, u32[]{:S(2)}) %collective-permute-start) | collective-permute-done | bytes 294944 | tf_op jit(solution)/shard_map/ppermute | solution.py:434
  11.0 2.4 %collective-permute-start.1 = (bf16[1152,128]{1,0:T(8,128)(2,1)S(1)}, bf16[1152,128]{1,0:T(8,128)(2,1)S(1)}, u32[]{:S(2)}, u32[]{:S(2)}) collective-permute-start(bf16[1152,128]{1,0:T(8,128)(2,1)S(1)} %collective-permute-done.refs_1_), channel_id=1, source_target_pairs={{0,4},{1,3},{4,8},{5,1},{8,12},{9,5},{12,14},{13,9},{14,10},{15,13... | collective-permute-start | bytes 884744 | tf_op jit(solution)/shard_map/ppermute | solution.py:434
  13.3 2.1 %collective-permute-start.7 = (bf16[1152,128]{1,0:T(8,128)(2,1)S(1)}, bf16[1152,128]{1,0:T(8,128)(2,1)S(1)}, u32[]{:S(2)}, u32[]{:S(2)}) collective-permute-start(bf16[1152,128]{1,0:T(8,128)(2,1)S(1)} %collective-permute-done.6.refs_2_), channel_id=1, source_target_pairs={{0,4},{1,3},{4,8},{5,1},{8,12},{9,5},{12,14},{13,9},{14,10},{15,13... | collective-permute-start | bytes 884744 | tf_op jit(solution)/shard_map/ppermute | solution.py:434
  15.4 1.4 %collective-permute-done.4 = s32[8,128]{1,0:T(8,128)S(1)} collective-permute-done((s32[8,128]{1,0:T(8,128)}, s32[8,128]{1,0:T(8,128)S(1)}, u32[]{:S(2)}, u32[]{:S(2)}) %collective-permute-start.4) | collective-permute-done | bytes 4128 | tf_op jit(solution)/shard_map/ppermute | solution.py:434
  16.8 1.5 %collective-permute-done.1.refs_3_ = bf16[1152,128]{1,0:T(8,128)(2,1)S(1)} collective-permute-done((bf16[1152,128]{1,0:T(8,128)(2,1)S(1)}, bf16[1152,128]{1,0:T(8,128)(2,1)S(1)}, u32[]{:S(2)}, u32[]{:S(2)}) %collective-permute-start.1) | collective-permute-done | bytes 294944 | tf_op jit(solution)/shard_map/ppermute | solution.py:434
  18.3 1.7 %collective-permute-start.5 = (bf16[1152,128]{1,0:T(8,128)(2,1)S(1)}, bf16[1152,128]{1,0:T(8,128)(2,1)S(1)}, u32[]{:S(2)}, u32[]{:S(2)}) collective-permute-start(bf16[1152,128]{1,0:T(8,128)(2,1)S(1)} %collective-permute-done.1.refs_3_), channel_id=1, source_target_pairs={{0,4},{1,3},{4,8},{5,1},{8,12},{9,5},{12,14},{13,9},{14,10},{15,13... | collective-permute-start | bytes 884744 | tf_op jit(solution)/shard_map/ppermute | solution.py:434
  20.1 1.4 %collective-permute-done.7.refs_4_ = bf16[1152,128]{1,0:T(8,128)(2,1)S(1)} collective-permute-done((bf16[1152,128]{1,0:T(8,128)(2,1)S(1)}, bf16[1152,128]{1,0:T(8,128)(2,1)S(1)}, u32[]{:S(2)}, u32[]{:S(2)}) %collective-permute-start.7) | collective-permute-done | bytes 294944 | tf_op jit(solution)/shard_map/ppermute | solution.py:434
  21.5 1.7 %collective-permute-start.8 = (bf16[1152,128]{1,0:T(8,128)(2,1)S(1)}, bf16[1152,128]{1,0:T(8,128)(2,1)S(1)}, u32[]{:S(2)}, u32[]{:S(2)}) collective-permute-start(bf16[1152,128]{1,0:T(8,128)(2,1)S(1)} %collective-permute-done.7.refs_4_), channel_id=1, source_target_pairs={{0,4},{1,3},{4,8},{5,1},{8,12},{9,5},{12,14},{13,9},{14,10},{15,13... | collective-permute-start | bytes 884744 | tf_op jit(solution)/shard_map/ppermute | solution.py:434
  23.9 1.1 %collective-permute-done.5.refs_5_ = bf16[1152,128]{1,0:T(8,128)(2,1)S(1)} collective-permute-done((bf16[1152,128]{1,0:T(8,128)(2,1)S(1)}, bf16[1152,128]{1,0:T(8,128)(2,1)S(1)}, u32[]{:S(2)}, u32[]{:S(2)}) %collective-permute-start.5) | collective-permute-done | bytes 294944 | tf_op jit(solution)/shard_map/ppermute | solution.py:434
  25.0 1.7 %collective-permute-start.9 = (bf16[1152,128]{1,0:T(8,128)(2,1)S(1)}, bf16[1152,128]{1,0:T(8,128)(2,1)S(1)}, u32[]{:S(2)}, u32[]{:S(2)}) collective-permute-start(bf16[1152,128]{1,0:T(8,128)(2,1)S(1)} %collective-permute-done.5.refs_5_), channel_id=1, source_target_pairs={{0,4},{1,3},{4,8},{5,1},{8,12},{9,5},{12,14},{13,9},{14,10},{15,13... | collective-permute-start | bytes 884744 | tf_op jit(solution)/shard_map/ppermute | solution.py:434
  26.8 4.2 %near.3.refs_8_ = f32[257,64,128]{2,1,0:T(8,128)S(1)} custom-call(s32[16,128]{1,0:T(8,128)S(1)} %pad_add_fusion.list_ref, bf16[1152,128]{1,0:T(8,128)(2,1)S(1)} %collective-permute-done.3.refs_0_, bf16[1152,128]{1,0:T(8,128)(2,1)S(1)} %collective-permute-done.refs_1_, bf16[1152,128]{1,0:T(8,128)(2,1)S(1)} %collective-permute-done.6.refs_2_, ...), custom_call_target="tpu_custom_call" | custom-call | flops 2147483648 | bytes 16777216 | tf_op jit(solution)/shard_map/near/pallas_call | solution.py:485
  31.0 2.9 %near.4.refs_10_ = f32[257,64,128]{2,1,0:T(8,128)S(1)} custom-call(s32[16,128]{1,0:T(8,128)S(1)} %pad_add_fusion.list_ref, bf16[1152,128]{1,0:T(8,128)(2,1)S(1)} %collective-permute-done.3.refs_0_, bf16[1152,128]{1,0:T(8,128)(2,1)S(1)} %collective-permute-done.refs_1_, ...), custom_call_target="tpu_custom_call", output_to_operand_aliasing={{}: (9, {})} | custom-call | flops 2147483648 | bytes 16777216 | tf_op jit(solution)/shard_map/near/pallas_call | solution.py:485
  34.0 2.6 %near.5 = (f32[257,64,128]{2,1,0:T(8,128)S(1)}, bf16[1024,128]{1,0:T(8,128)(2,1)S(1)}, bf16[32,64,128]{2,1,0:T(8,128)(2,1)S(1)}, bf16[96,64,128]{2,1,0:T(8,128)(2,1)S(1)}) custom-call(s32[16,128]{1,0:T(8,128)S(1)} %pad_add_fusion.list_ref, bf16[1152,128]{1,0:T(8,128)(2,1)S(1)} %collective-permute-done.3.refs_0_, ...), custom_call_target="tpu_custom_call", output_to_operand_aliasing={{0}: (11, {})} | custom-call | flops 2147483648 | bytes 16777216 | tf_op jit(solution)/shard_map/near/pallas_call | solution.py:485
  36.7 1.9 %collective-permute-done.11 = bf16[32,64,128]{2,1,0:T(8,128)(2,1)S(1)} collective-permute-done((bf16[32,64,128]{2,1,0:T(8,128)(2,1)S(1)}, bf16[32,64,128]{2,1,0:T(8,128)(2,1)S(1)}, u32[]{:S(2)}, u32[]{:S(2)}) %collective-permute-start.11) | collective-permute-done | bytes 524320 | tf_op jit(solution)/shard_map/ppermute | solution.py:434
  39.0 1.6 %collective-permute-start.12 = (bf16[16,64,128]{2,1,0:T(8,128)(2,1)S(1)}, bf16[16,64,128]{2,1,0:T(8,128)(2,1)S(1)}, u32[]{:S(2)}, u32[]{:S(2)}) collective-permute-start(bf16[16,64,128]{2,1,0:T(8,128)(2,1)S(1)} %get-tuple-element.46), channel_id=1, source_target_pairs={{0,4},{1,3},{4,8},{5,1},{8,12},{9,5},{12,14},{13,9},{14,10},{15,13... | collective-permute-start | bytes 786440 | tf_op jit(solution)/shard_map/ppermute | solution.py:434
  40.6 1.9 %collective-permute-start.15 = (bf16[16,64,128]{2,1,0:T(8,128)(2,1)S(1)}, bf16[16,64,128]{2,1,0:T(8,128)(2,1)S(1)}, u32[]{:S(2)}, u32[]{:S(2)}) collective-permute-start(bf16[16,64,128]{2,1,0:T(8,128)(2,1)S(1)} %get-tuple-element.48), channel_id=1, source_target_pairs={{0,4},{1,3},{4,8},{5,1},{8,12},{9,5},{12,14},{13,9},{14,10},{15,13... | collective-permute-start | bytes 786440 | tf_op jit(solution)/shard_map/ppermute | solution.py:434
  42.5 2.9 %collective-permute-done.12 = bf16[16,64,128]{2,1,0:T(8,128)(2,1)S(1)} collective-permute-done((bf16[16,64,128]{2,1,0:T(8,128)(2,1)S(1)}, bf16[16,64,128]{2,1,0:T(8,128)(2,1)S(1)}, u32[]{:S(2)}, u32[]{:S(2)}) %collective-permute-start.12) | collective-permute-done | bytes 262176 | tf_op jit(solution)/shard_map/ppermute | solution.py:434
  45.5 1.6 %collective-permute-start.14 = (bf16[16,64,128]{2,1,0:T(8,128)(2,1)S(1)}, bf16[16,64,128]{2,1,0:T(8,128)(2,1)S(1)}, u32[]{:S(2)}, u32[]{:S(2)}) collective-permute-start(bf16[16,64,128]{2,1,0:T(8,128)(2,1)S(1)} %add_convert_fusion.5), channel_id=1, source_target_pairs={{0,4},{1,3},{4,8},{5,1},{8,12},{9,5},{12,14},{13,9},{14,10},{15,13... | collective-permute-start | bytes 786440 | tf_op jit(solution)/shard_map/ppermute | solution.py:434
  47.1 1.1 %collective-permute-done.15 = bf16[16,64,128]{2,1,0:T(8,128)(2,1)S(1)} collective-permute-done((bf16[16,64,128]{2,1,0:T(8,128)(2,1)S(1)}, bf16[16,64,128]{2,1,0:T(8,128)(2,1)S(1)}, u32[]{:S(2)}, u32[]{:S(2)}) %collective-permute-start.15) | collective-permute-done | bytes 262176 | tf_op jit(solution)/shard_map/ppermute | solution.py:434
  48.3 1.6 %collective-permute-start.17 = (bf16[16,64,128]{2,1,0:T(8,128)(2,1)S(1)}, bf16[16,64,128]{2,1,0:T(8,128)(2,1)S(1)}, u32[]{:S(2)}, u32[]{:S(2)}) collective-permute-start(bf16[16,64,128]{2,1,0:T(8,128)(2,1)S(1)} %add_convert_fusion.4), channel_id=1, source_target_pairs={{0,4},{1,3},{4,8},{5,1},{8,12},{9,5},{12,14},{13,9},{14,10},{15,13... | collective-permute-start | bytes 786440 | tf_op jit(solution)/shard_map/ppermute | solution.py:434
  49.9 2.0 %collective-permute-done.14 = bf16[16,64,128]{2,1,0:T(8,128)(2,1)S(1)} collective-permute-done((bf16[16,64,128]{2,1,0:T(8,128)(2,1)S(1)}, bf16[16,64,128]{2,1,0:T(8,128)(2,1)S(1)}, u32[]{:S(2)}, u32[]{:S(2)}) %collective-permute-start.14) | collective-permute-done | bytes 262176 | tf_op jit(solution)/shard_map/ppermute | solution.py:434
  52.0 1.6 %collective-permute-start.16 = (bf16[16,64,128]{2,1,0:T(8,128)(2,1)S(1)}, bf16[16,64,128]{2,1,0:T(8,128)(2,1)S(1)}, u32[]{:S(2)}, u32[]{:S(2)}) collective-permute-start(bf16[16,64,128]{2,1,0:T(8,128)(2,1)S(1)} %add_convert_fusion.3), channel_id=1, source_target_pairs={{0,4},{1,3},{4,8},{5,1},{8,12},{9,5},{12,14},{13,9},{14,10},{15,13... | collective-permute-start | bytes 786440 | tf_op jit(solution)/shard_map/ppermute | solution.py:434
  53.6 1.1 %collective-permute-done.17 = bf16[16,64,128]{2,1,0:T(8,128)(2,1)S(1)} collective-permute-done((bf16[16,64,128]{2,1,0:T(8,128)(2,1)S(1)}, bf16[16,64,128]{2,1,0:T(8,128)(2,1)S(1)}, u32[]{:S(2)}, u32[]{:S(2)}) %collective-permute-start.17) | collective-permute-done | bytes 262176 | tf_op jit(solution)/shard_map/ppermute | solution.py:434
  54.8 1.6 %collective-permute-start.19 = (bf16[16,64,128]{2,1,0:T(8,128)(2,1)S(1)}, bf16[16,64,128]{2,1,0:T(8,128)(2,1)S(1)}, u32[]{:S(2)}, u32[]{:S(2)}) collective-permute-start(bf16[16,64,128]{2,1,0:T(8,128)(2,1)S(1)} %add_convert_fusion.2), channel_id=1, source_target_pairs={{0,4},{1,3},{4,8},{5,1},{8,12},{9,5},{12,14},{13,9},{14,10},{15,13... | collective-permute-start | bytes 786440 | tf_op jit(solution)/shard_map/ppermute | solution.py:434
  56.5 2.0 %collective-permute-done.16 = bf16[16,64,128]{2,1,0:T(8,128)(2,1)S(1)} collective-permute-done((bf16[16,64,128]{2,1,0:T(8,128)(2,1)S(1)}, bf16[16,64,128]{2,1,0:T(8,128)(2,1)S(1)}, u32[]{:S(2)}, u32[]{:S(2)}) %collective-permute-start.16) | collective-permute-done | bytes 262176 | tf_op jit(solution)/shard_map/ppermute | solution.py:434
  58.6 1.6 %collective-permute-start.18 = (bf16[16,64,128]{2,1,0:T(8,128)(2,1)S(1)}, bf16[16,64,128]{2,1,0:T(8,128)(2,1)S(1)}, u32[]{:S(2)}, u32[]{:S(2)}) collective-permute-start(bf16[16,64,128]{2,1,0:T(8,128)(2,1)S(1)} %add_convert_fusion.1), channel_id=1, source_target_pairs={{0,4},{1,3},{4,8},{5,1},{8,12},{9,5},{12,14},{13,9},{14,10},{15,13... | collective-permute-start | bytes 786440 | tf_op jit(solution)/shard_map/ppermute | solution.py:434
  60.2 1.1 %collective-permute-done.19 = bf16[16,64,128]{2,1,0:T(8,128)(2,1)S(1)} collective-permute-done((bf16[16,64,128]{2,1,0:T(8,128)(2,1)S(1)}, bf16[16,64,128]{2,1,0:T(8,128)(2,1)S(1)}, u32[]{:S(2)}, u32[]{:S(2)}) %collective-permute-start.19) | collective-permute-done | bytes 262176 | tf_op jit(solution)/shard_map/ppermute | solution.py:434
  61.3 2.5 %far.1 = f32[16,64,128]{2,1,0:T(8,128)S(1)} custom-call(bf16[1024,128]{1,0:T(8,128)(2,1)S(1)} %get-tuple-element.43.refs_0_, bf16[1024,128]{1,0:T(8,128)(2,1)S(1)} %collective-permute-done.10.refs_1_, s32[1]{0:T(128)} %bitcast.me_ref.refs_2_, bf16[16,16,256]{2,1,0:T(8,128)(2,1)S(1)} %bitcast.10, s32[1,256]{1,0:T(1,128)S(1)} %bitcast.11, ...), custom_call_target="tpu_custom_call" | custom-call | flops 536870912 | bytes 8388608 | tf_op jit(solution)/shard_map/far/pallas_call | solution.py:514
  63.8 1.2 %collective-permute-done.18 = bf16[16,64,128]{2,1,0:T(8,128)(2,1)S(1)} collective-permute-done((bf16[16,64,128]{2,1,0:T(8,128)(2,1)S(1)}, bf16[16,64,128]{2,1,0:T(8,128)(2,1)S(1)}, u32[]{:S(2)}, u32[]{:S(2)}) %collective-permute-start.18) | collective-permute-done | bytes 262176 | tf_op jit(solution)/shard_map/ppermute | solution.py:434
  (35 shorter events, 4.4 us)
Async XLA Ops:
  0.0 18.3 %collective-permute-start.2 = (bf16[128,128,128]{2,1,0:T(8,128)(2,1)}, bf16[128,128,128]{2,1,0:T(8,128)(2,1)}, u32[]{:S(2)}, u32[]{:S(2)}) collective-permute-start(bf16[128,128,128]{2,1,0:T(8,128)(2,1)} %refs_8_.1), channel_id=1, source_target_pairs={{0,1},{1,0},{2,3},{3,2},{4,5},{5,4},{6,7},{7,6},{8,9},{9,8},{10,11... | collective-permute-start | bytes 12582920 | tf_op jit(solution)/shard_map/ppermute | solution.py:434
  0.5 30.6 %copy-start = (bf16[128,128,128]{2,1,0:T(8,128)(2,1)S(1)}, bf16[128,128,128]{2,1,0:T(8,128)(2,1)}, u32[]{:S(2)}) copy-start(bf16[128,128,128]{2,1,0:T(8,128)(2,1)} %refs_8_.1) | copy-start | bytes 12582916
  2.8 8.2 %collective-permute-start = (bf16[1152,128]{1,0:T(8,128)(2,1)}, bf16[1152,128]{1,0:T(8,128)(2,1)S(1)}, u32[]{:S(2)}, u32[]{:S(2)}) collective-permute-start(bf16[1152,128]{1,0:T(8,128)(2,1)} %get-tuple-element.36), channel_id=1, source_target_pairs={{0,4},{1,3},{4,8},{5,1},{8,12},{9,5},{12,14},{13,9},{14,10},{15,13... | collective-permute-start | bytes 884744 | tf_op jit(solution)/shard_map/ppermute | solution.py:434
  6.3 7.1 %collective-permute-start.6 = (bf16[1152,128]{1,0:T(8,128)(2,1)}, bf16[1152,128]{1,0:T(8,128)(2,1)S(1)}, u32[]{:S(2)}, u32[]{:S(2)}) collective-permute-start(bf16[1152,128]{1,0:T(8,128)(2,1)} %get-tuple-element.36), channel_id=1, source_target_pairs={{0,3},{1,4},{4,1},{5,8},{8,5},{9,12},{12,9},{13,14},{14,13},{15,10... | collective-permute-start | bytes 884744 | tf_op jit(solution)/shard_map/ppermute | solution.py:434
  7.7 9.1 %collective-permute-start.3 = (bf16[1152,128]{1,0:T(8,128)(2,1)}, bf16[1152,128]{1,0:T(8,128)(2,1)S(1)}, u32[]{:S(2)}, u32[]{:S(2)}) collective-permute-start(bf16[1152,128]{1,0:T(8,128)(2,1)} %get-tuple-element.36), channel_id=1, source_target_pairs={{0,1},{1,0},{2,3},{3,2},{4,5},{5,4},{6,7},{7,6},{8,9},{9,8},{10,11... | collective-permute-start | bytes 884744 | tf_op jit(solution)/shard_map/ppermute | solution.py:434
  11.0 7.4 %collective-permute-start.1 = (bf16[1152,128]{1,0:T(8,128)(2,1)S(1)}, bf16[1152,128]{1,0:T(8,128)(2,1)S(1)}, u32[]{:S(2)}, u32[]{:S(2)}) collective-permute-start(bf16[1152,128]{1,0:T(8,128)(2,1)S(1)} %collective-permute-done.refs_1_), channel_id=1, source_target_pairs={{0,4},{1,3},{4,8},{5,1},{8,12},{9,5},{12,14},{13,9},{14,10},{15,13... | collective-permute-start | bytes 884744 | tf_op jit(solution)/shard_map/ppermute | solution.py:434
  13.3 8.1 %collective-permute-start.7 = (bf16[1152,128]{1,0:T(8,128)(2,1)S(1)}, bf16[1152,128]{1,0:T(8,128)(2,1)S(1)}, u32[]{:S(2)}, u32[]{:S(2)}) collective-permute-start(bf16[1152,128]{1,0:T(8,128)(2,1)S(1)} %collective-permute-done.6.refs_2_), channel_id=1, source_target_pairs={{0,4},{1,3},{4,8},{5,1},{8,12},{9,5},{12,14},{13,9},{14,10},{15,13... | collective-permute-start | bytes 884744 | tf_op jit(solution)/shard_map/ppermute | solution.py:434
  15.4 1.4 %collective-permute-start.4 = (s32[8,128]{1,0:T(8,128)}, s32[8,128]{1,0:T(8,128)S(1)}, u32[]{:S(2)}, u32[]{:S(2)}) collective-permute-start(s32[8,128]{1,0:T(8,128)} %get-tuple-element.37), channel_id=1, source_target_pairs={{0,1},{1,0},{2,3},{3,2},{4,5},{5,4},{6,7},{7,6},{8,9},{9,8},{10,11... | collective-permute-start | bytes 12296 | tf_op jit(solution)/shard_map/ppermute | solution.py:434
  18.3 6.7 %collective-permute-start.5 = (bf16[1152,128]{1,0:T(8,128)(2,1)S(1)}, bf16[1152,128]{1,0:T(8,128)(2,1)S(1)}, u32[]{:S(2)}, u32[]{:S(2)}) collective-permute-start(bf16[1152,128]{1,0:T(8,128)(2,1)S(1)} %collective-permute-done.1.refs_3_), channel_id=1, source_target_pairs={{0,4},{1,3},{4,8},{5,1},{8,12},{9,5},{12,14},{13,9},{14,10},{15,13... | collective-permute-start | bytes 884744 | tf_op jit(solution)/shard_map/ppermute | solution.py:434
  21.5 9.5 %collective-permute-start.8 = (bf16[1152,128]{1,0:T(8,128)(2,1)S(1)}, bf16[1152,128]{1,0:T(8,128)(2,1)S(1)}, u32[]{:S(2)}, u32[]{:S(2)}) collective-permute-start(bf16[1152,128]{1,0:T(8,128)(2,1)S(1)} %collective-permute-done.7.refs_4_), channel_id=1, source_target_pairs={{0,4},{1,3},{4,8},{5,1},{8,12},{9,5},{12,14},{13,9},{14,10},{15,13... | collective-permute-start | bytes 884744 | tf_op jit(solution)/shard_map/ppermute | solution.py:434
  25.0 8.9 %collective-permute-start.9 = (bf16[1152,128]{1,0:T(8,128)(2,1)S(1)}, bf16[1152,128]{1,0:T(8,128)(2,1)S(1)}, u32[]{:S(2)}, u32[]{:S(2)}) collective-permute-start(bf16[1152,128]{1,0:T(8,128)(2,1)S(1)} %collective-permute-done.5.refs_5_), channel_id=1, source_target_pairs={{0,4},{1,3},{4,8},{5,1},{8,12},{9,5},{12,14},{13,9},{14,10},{15,13... | collective-permute-start | bytes 884744 | tf_op jit(solution)/shard_map/ppermute | solution.py:434
  36.6 24.7 %copy-start.1 = (bf16[16,16,128]{2,1,0:T(8,128)(2,1)S(1)}, bf16[16,16,128]{2,1,0:T(8,128)(2,1)}, u32[]{:S(2)}) copy-start(bf16[16,16,128]{2,1,0:T(8,128)(2,1)} %refs_7_.3) | copy-start | bytes 196612
  36.6 24.7 %copy-start.2 = (s32[256]{0:T(256)S(1)}, s32[256]{0:T(256)}, u32[]{:S(2)}) copy-start(s32[256]{0:T(256)} %param.17) | copy-start | bytes 3076
  36.6 24.7 %copy-start.3 = (s32[256,1]{0,1:T(1,128)S(1)}, s32[256,1]{0,1:T(1,128)}, u32[]{:S(2)}) copy-start(s32[256,1]{0,1:T(1,128)} %param.18) | copy-start | bytes 3076
  36.6 24.7 %copy-start.4 = (s32[256]{0:T(256)S(1)}, s32[256]{0:T(256)}, u32[]{:S(2)}) copy-start(s32[256]{0:T(256)} %param.19) | copy-start | bytes 3076
  36.6 2.0 %collective-permute-start.11 = (bf16[32,64,128]{2,1,0:T(8,128)(2,1)S(1)}, bf16[32,64,128]{2,1,0:T(8,128)(2,1)S(1)}, u32[]{:S(2)}, u32[]{:S(2)}) collective-permute-start(bf16[32,64,128]{2,1,0:T(8,128)(2,1)S(1)} %get-tuple-element.45), channel_id=1, source_target_pairs={{0,1},{1,0},{2,3},{3,2},{4,5},{5,4},{6,7},{7,6},{8,9},{9,8},{10,11... | collective-permute-start | bytes 1572872 | tf_op jit(solution)/shard_map/ppermute | solution.py:434
  38.8 6.6 %collective-permute-start.13 = (bf16[96,64,128]{2,1,0:T(8,128)(2,1)S(1)}, bf16[96,64,128]{2,1,0:T(8,128)(2,1)S(1)}, u32[]{:S(2)}, u32[]{:S(2)}) collective-permute-start(bf16[96,64,128]{2,1,0:T(8,128)(2,1)S(1)} %get-tuple-element.49), channel_id=1, source_target_pairs={{0,1},{1,0},{2,3},{3,2},{4,5},{5,4},{6,7},{7,6},{8,9},{9,8},{10,11... | collective-permute-start | bytes 4718600 | tf_op jit(solution)/shard_map/ppermute | solution.py:434
  39.0 6.4 %collective-permute-start.12 = (bf16[16,64,128]{2,1,0:T(8,128)(2,1)S(1)}, bf16[16,64,128]{2,1,0:T(8,128)(2,1)S(1)}, u32[]{:S(2)}, u32[]{:S(2)}) collective-permute-start(bf16[16,64,128]{2,1,0:T(8,128)(2,1)S(1)} %get-tuple-element.46), channel_id=1, source_target_pairs={{0,4},{1,3},{4,8},{5,1},{8,12},{9,5},{12,14},{13,9},{14,10},{15,13... | collective-permute-start | bytes 786440 | tf_op jit(solution)/shard_map/ppermute | solution.py:434
  40.6 7.6 %collective-permute-start.15 = (bf16[16,64,128]{2,1,0:T(8,128)(2,1)S(1)}, bf16[16,64,128]{2,1,0:T(8,128)(2,1)S(1)}, u32[]{:S(2)}, u32[]{:S(2)}) collective-permute-start(bf16[16,64,128]{2,1,0:T(8,128)(2,1)S(1)} %get-tuple-element.48), channel_id=1, source_target_pairs={{0,4},{1,3},{4,8},{5,1},{8,12},{9,5},{12,14},{13,9},{14,10},{15,13... | collective-permute-start | bytes 786440 | tf_op jit(solution)/shard_map/ppermute | solution.py:434
  45.5 6.4 %collective-permute-start.14 = (bf16[16,64,128]{2,1,0:T(8,128)(2,1)S(1)}, bf16[16,64,128]{2,1,0:T(8,128)(2,1)S(1)}, u32[]{:S(2)}, u32[]{:S(2)}) collective-permute-start(bf16[16,64,128]{2,1,0:T(8,128)(2,1)S(1)} %add_convert_fusion.5), channel_id=1, source_target_pairs={{0,4},{1,3},{4,8},{5,1},{8,12},{9,5},{12,14},{13,9},{14,10},{15,13... | collective-permute-start | bytes 786440 | tf_op jit(solution)/shard_map/ppermute | solution.py:434
  48.3 6.4 %collective-permute-start.17 = (bf16[16,64,128]{2,1,0:T(8,128)(2,1)S(1)}, bf16[16,64,128]{2,1,0:T(8,128)(2,1)S(1)}, u32[]{:S(2)}, u32[]{:S(2)}) collective-permute-start(bf16[16,64,128]{2,1,0:T(8,128)(2,1)S(1)} %add_convert_fusion.4), channel_id=1, source_target_pairs={{0,4},{1,3},{4,8},{5,1},{8,12},{9,5},{12,14},{13,9},{14,10},{15,13... | collective-permute-start | bytes 786440 | tf_op jit(solution)/shard_map/ppermute | solution.py:434
  52.0 6.4 %collective-permute-start.16 = (bf16[16,64,128]{2,1,0:T(8,128)(2,1)S(1)}, bf16[16,64,128]{2,1,0:T(8,128)(2,1)S(1)}, u32[]{:S(2)}, u32[]{:S(2)}) collective-permute-start(bf16[16,64,128]{2,1,0:T(8,128)(2,1)S(1)} %add_convert_fusion.3), channel_id=1, source_target_pairs={{0,4},{1,3},{4,8},{5,1},{8,12},{9,5},{12,14},{13,9},{14,10},{15,13... | collective-permute-start | bytes 786440 | tf_op jit(solution)/shard_map/ppermute | solution.py:434
  53.6 7.6 %collective-permute-start.10 = (bf16[1024,128]{1,0:T(8,128)(2,1)S(1)}, bf16[1024,128]{1,0:T(8,128)(2,1)S(1)}, u32[]{:S(2)}, u32[]{:S(2)}) collective-permute-start(bf16[1024,128]{1,0:T(8,128)(2,1)S(1)} %get-tuple-element.43.refs_0_), channel_id=1, source_target_pairs={{0,1},{1,0},{2,3},{3,2},{4,5},{5,4},{6,7},{7,6},{8,9},{9,8},{10,11... | collective-permute-start | bytes 786440 | tf_op jit(solution)/shard_map/ppermute | solution.py:434
  54.8 6.4 %collective-permute-start.19 = (bf16[16,64,128]{2,1,0:T(8,128)(2,1)S(1)}, bf16[16,64,128]{2,1,0:T(8,128)(2,1)S(1)}, u32[]{:S(2)}, u32[]{:S(2)}) collective-permute-start(bf16[16,64,128]{2,1,0:T(8,128)(2,1)S(1)} %add_convert_fusion.2), channel_id=1, source_target_pairs={{0,4},{1,3},{4,8},{5,1},{8,12},{9,5},{12,14},{13,9},{14,10},{15,13... | collective-permute-start | bytes 786440 | tf_op jit(solution)/shard_map/ppermute | solution.py:434
  58.6 6.4 %collective-permute-start.18 = (bf16[16,64,128]{2,1,0:T(8,128)(2,1)S(1)}, bf16[16,64,128]{2,1,0:T(8,128)(2,1)S(1)}, u32[]{:S(2)}, u32[]{:S(2)}) collective-permute-start(bf16[16,64,128]{2,1,0:T(8,128)(2,1)S(1)} %add_convert_fusion.1), channel_id=1, source_target_pairs={{0,4},{1,3},{4,8},{5,1},{8,12},{9,5},{12,14},{13,9},{14,10},{15,13... | collective-permute-start | bytes 786440 | tf_op jit(solution)/shard_map/ppermute | solution.py:434
  61.3 3.9 %collective-permute-start.20 = (bf16[16,64,128]{2,1,0:T(8,128)(2,1)S(1)}, bf16[16,64,128]{2,1,0:T(8,128)(2,1)S(1)}, u32[]{:S(2)}, u32[]{:S(2)}) collective-permute-start(bf16[16,64,128]{2,1,0:T(8,128)(2,1)S(1)} %collective-permute-done.19), channel_id=1, source_target_pairs={{0,1},{1,0},{2,3},{3,2},{4,5},{5,4},{6,7},{7,6},{8,9},{9,8},{10,11... | collective-permute-start | bytes 786440 | tf_op jit(solution)/shard_map/ppermute | solution.py:434

commit v20 on v19

--- a/solution.py
+++ b/solution.py
@@ -178,6 +178,15 @@
     list_ref[...] = values.astype(jnp.int32)
 
 
+def clear_kernel(token_ref, sums):
+    def clear(i, carry):
+        sums[i] = jnp.zeros(sums.shape[1:], sums.dtype)
+        return carry
+
+    lax.fori_loop(0, sums.shape[0] - 1, clear, 0, unroll=8)
+    clear(sums.shape[0] - 1, 0)
+
+
 def near_kernel(part, batch, shards, sends, list_ref, *refs):
     late = int(part == 2)
     used = LATE if late else shards
@@ -186,9 +195,7 @@
         own_ref, refs = refs[0], refs[1:]
     if part != 1:
         mate_hbm, refs = refs[0], refs[1:]
-    if part > 0:
-        refs = refs[1:]
-    sums, refs = refs[0], refs[1:]
+    sums, refs = refs[1], refs[2:]
     if late:
         coef_ref, send_refs, refs = refs[0], refs[1 : 1 + sends], refs[1 + sends :]
     columns, blocks, block_sem = refs
@@ -230,14 +237,6 @@
         tail = coef_ref.shape[0] // shards
         for k, ref in enumerate(shard_refs):
             coef_ref[k * tail : (k + 1) * tail] = ref[span : span + tail]
-    elif part == 0:
-
-        def clear(i, carry):
-            sums[i] = jnp.zeros(sums.shape[1:], sums.dtype)
-            return carry
-
-        lax.fori_loop(0, dummy, clear, 0, unroll=8)
-        clear(dummy, 0)
 
     def run(begin, end, row, swap, block_of):
         def entry(j):
@@ -457,11 +456,20 @@
         basis_in,
     )
     flow = [move(payload, ahead)]
+    mate_lists = move(lists, mate)
+    couple = jnp.transpose(after(far_coupling, payload), (2, 1, 0))
     mate_blocks = move(near_blocks, mate)
-    mate_lists = move(lists, mate)
-    couple = jnp.transpose(far_coupling, (2, 1, 0))
     flow.append(move(after(payload, couple), cross))
     shards = [move(payload, mate)]
+    sums_shape = jax.ShapeDtypeStruct((count * clusters + 1, directions, unknowns), jnp.float32)
+    sums = pl.pallas_call(
+        clear_kernel,
+        out_shape=sums_shape,
+        in_specs=[whole(pltpu.SMEM)],
+        out_specs=whole(),
+        name="clear",
+    )(after(here, couple))
+    flow[0], sums = lax.optimization_barrier((flow[0], sums))
     for k in range(1, chips):
         x = 1 - k % 2
         if k == 3:
@@ -477,9 +485,8 @@
             flow[x] = move(flow[x], ahead)
 
     pieces = [2, chips - 2]
-    sums_shape = jax.ShapeDtypeStruct((count * clusters + 1, directions, unknowns), jnp.float32)
-
-    def near(part, shards, sources, *sums):
+
+    def near(part, shards, sources, sums):
         late = int(part == 2)
         sends = pieces if late else []
         return pl.pallas_call(
@@ -493,9 +500,9 @@
             in_specs=[whole(pltpu.SMEM)]
             + [whole()] * len(shards)
             + [[whole(pl.ANY)], [whole()], [whole(), whole(pl.ANY)]][part]
-            + [whole()] * len(sums),
+            + [whole()],
             out_specs=[whole()] * (1 + late + len(sends)),
-            input_output_aliases={1 + len(shards) + len(sources): 0} if sums else {},
+            input_output_aliases={1 + len(shards) + len(sources): 0},
             scratch_shapes=[
                 pltpu.VMEM(((LATE if late else len(shards)) * base, unknowns), jnp.bfloat16),
                 pltpu.VMEM(near_blocks.shape, jnp.bfloat16),
@@ -508,7 +515,7 @@
                 transcendentals=0,
             ),
             name="near",
-        )(lists, *shards, *sources, *sums)
+        )(lists, *shards, *sources, sums)
 
     def far_field(couple):
         return pl.pallas_call(
@@ -533,7 +540,7 @@
             basis_out,
         )
 
-    (sums,) = near(0, shards[: chips - LATE], [mate_blocks])
+    (sums,) = near(0, shards[: chips - LATE], [mate_blocks], sums)
     (sums,) = near(1, shards[: chips - LATE + 1], [near_blocks], sums)
     sums, coef, *sends = near(2, shards, [near_blocks, mate_blocks], sums)
     mates = [move(sends[0], mate)]

time: 66 us -> 69.8 us (1.058)
  Pallas kernels: 14.6 us -> 18.6 us
  local copies, waits for them, and re-layouts: 0.97 us -> 4.37 us
  waiting for transfers between devices: 21.5 us -> 18.3 us
  other arithmetic: 2.32 us -> 1.54 us
    pallas_call x0 -> x1, Pallas kernels: none -> 3.86 us  [stationary(): pl.pallas_call(clear_kernel, out_shape=sums_shape, in_specs=[whole(pltpu....]
    ppermute x21, waiting for transfers between devices: 21.5 us -> 18.3 us  [move(): return lax.ppermute(values, 'blk', where)]
    unnamed x11 -> x14, local copies, waits for them, and re-layouts: 0.97 us -> 3.42 us
    optimization_barrier x0 -> x1, local copies, waits for them, and re-layouts: none -> 0.95 us  [after(): return lax.optimization_barrier((values, *others))[0]]
  transfers between devices with their start and end apart: 21 -> 21, of which waited for: 13 -> 12; matrix products, arithmetic and copies ran while one was open for 4% -> 2% of each run, Pallas kernels for 18% -> 23%
where the time goes in v20:
time: 69.8 us; the launch traced here: 69.5 us
  starting transfers between devices  26.5 us (38%)
  Pallas kernels  18.6 us (27%)
  waiting for transfers between devices  18.3 us (26%)
  local copies, waits for them, and re-layouts  4.37 us (6%)
  other arithmetic  1.54 us (2%)
    ppermute x21, starting transfers between devices, move(): return lax.ppermute(values, 'blk', where)  26.5 us
    ppermute x21, waiting for transfers between devices, move(): return lax.ppermute(values, 'blk', where)  18.3 us
    pallas_call x3, Pallas kernels, near(): pl.pallas_call(functools.partial(near_kernel, part, BATCH[part], len(shar...  10.1 us
    pallas_call x1, Pallas kernels, stationary(): pl.pallas_call(clear_kernel, out_shape=sums_shape, in_specs=[whole(pltpu....  3.86 us
    unnamed x14, local copies, waits for them, and re-layouts  3.42 us
    pallas_call x1, Pallas kernels, far_field(): pl.pallas_call(far_kernel, out_shape=jax.ShapeDtypeStruct((clusters, dire...  2.51 us
    pallas_call x1, Pallas kernels, stationary(): pl.pallas_call(functools.partial(prologue_kernel, count), out_shape=[jax....  2.15 us
  transfers between devices with their start and end apart: 21, of which 12 were waited for; matrix products, arithmetic and copies ran while one was open for 2% of the time, Pallas kernels for 23%

profile of v20, /device:TPU:0, one launch (start us, length us, event | category | flops | bytes accessed | tf_op | source)
XLA Modules:
  0.0 69.5 jit_solution(5214230794978843726)
XLA Ops:
  0.5 2.1 %prologue.1 = (bf16[1152,128]{1,0:T(8,128)(2,1)}, s32[8,128]{1,0:T(8,128)}) custom-call(s32[1]{0:T(128)} %bitcast.me_ref.token_ref.refs_2_, s32[1,128]{1,0:T(1,128)} %bitcast.14, s32[1,128]{1,0:T(1,128)} %bitcast.15, s32[1,128]{1,0:T(1,128)} %bitcast.16, bf16[16,64,128]{2,1,0:T(8,128)(2,1)} %rhs_ref.1, bf16[16,16,128]{2,1,0:T(8,128)(2,1)} %basis_ref.1), custom_call_target="tpu_custom_call" | custom-call | tf_op jit(solution)/shard_map/prologue/pallas_call | solution.py:440
  2.6 2.6 %collective-permute-start = (bf16[1152,128]{1,0:T(8,128)(2,1)}, bf16[1152,128]{1,0:T(8,128)(2,1)S(1)}, u32[]{:S(2)}, u32[]{:S(2)}) collective-permute-start(bf16[1152,128]{1,0:T(8,128)(2,1)} %get-tuple-element.43), channel_id=1, source_target_pairs={{0,4},{1,3},{4,8},{5,1},{8,12},{9,5},{12,14},{13,9},{14,10},{15,13... | collective-permute-start | bytes 884744 | tf_op jit(solution)/shard_map/ppermute | solution.py:433
  5.2 0.9 %copy.17 = bf16[256,16,16]{0,1,2:T(8,128)(2,1)S(1)} copy(bf16[256,16,16]{0,2,1:T(8,128)(2,1)} %param.16) | data formatting | bytes 262144 | tf_op jit(solution)/shard_map/optimization_barrier | solution.py:436
  6.1 1.4 %collective-permute-start.6 = (bf16[1152,128]{1,0:T(8,128)(2,1)}, bf16[1152,128]{1,0:T(8,128)(2,1)S(1)}, u32[]{:S(2)}, u32[]{:S(2)}) collective-permute-start(bf16[1152,128]{1,0:T(8,128)(2,1)} %get-tuple-element.43), channel_id=1, source_target_pairs={{0,3},{1,4},{4,1},{5,8},{8,5},{9,12},{12,9},{13,14},{14,13},{15,10... | collective-permute-start | bytes 884744 | tf_op jit(solution)/shard_map/ppermute | solution.py:433
  7.9 3.9 %clear.1.refs_7_ = f32[257,64,128]{2,1,0:T(8,128)} custom-call(s32[1]{0:T(128)} %bitcast.me_ref.token_ref.refs_2_), custom_call_target="tpu_custom_call" | custom-call | tf_op jit(solution)/shard_map/clear/pallas_call | solution.py:465
  11.7 1.6 %collective-permute-start.1 = (bf16[1152,128]{1,0:T(8,128)(2,1)S(1)}, bf16[1152,128]{1,0:T(8,128)(2,1)S(1)}, u32[]{:S(2)}, u32[]{:S(2)}) collective-permute-start(bf16[1152,128]{1,0:T(8,128)(2,1)S(1)} %collective-permute-done.refs_1_), channel_id=1, source_target_pairs={{0,4},{1,3},{4,8},{5,1},{8,12},{9,5},{12,14},{13,9},{14,10},{15,13... | collective-permute-start | bytes 884744 | tf_op jit(solution)/shard_map/ppermute | solution.py:433
  13.3 1.9 %collective-permute-start.7 = (bf16[1152,128]{1,0:T(8,128)(2,1)S(1)}, bf16[1152,128]{1,0:T(8,128)(2,1)S(1)}, u32[]{:S(2)}, u32[]{:S(2)}) collective-permute-start(bf16[1152,128]{1,0:T(8,128)(2,1)S(1)} %collective-permute-done.6.refs_2_), channel_id=1, source_target_pairs={{0,4},{1,3},{4,8},{5,1},{8,12},{9,5},{12,14},{13,9},{14,10},{15,13... | collective-permute-start | bytes 884744 | tf_op jit(solution)/shard_map/ppermute | solution.py:433
  15.3 1.2 %collective-permute-done.4 = s32[8,128]{1,0:T(8,128)S(1)} collective-permute-done((s32[8,128]{1,0:T(8,128)S(1)}, s32[8,128]{1,0:T(8,128)S(1)}, u32[]{:S(2)}, u32[]{:S(2)}) %collective-permute-start.4) | collective-permute-done | bytes 4128 | tf_op jit(solution)/shard_map/ppermute | solution.py:433
  16.4 2.0 %collective-permute-done.1.refs_3_ = bf16[1152,128]{1,0:T(8,128)(2,1)S(1)} collective-permute-done((bf16[1152,128]{1,0:T(8,128)(2,1)S(1)}, bf16[1152,128]{1,0:T(8,128)(2,1)S(1)}, u32[]{:S(2)}, u32[]{:S(2)}) %collective-permute-start.1) | collective-permute-done | bytes 294944 | tf_op jit(solution)/shard_map/ppermute | solution.py:433
  18.5 1.6 %collective-permute-start.5 = (bf16[1152,128]{1,0:T(8,128)(2,1)S(1)}, bf16[1152,128]{1,0:T(8,128)(2,1)S(1)}, u32[]{:S(2)}, u32[]{:S(2)}) collective-permute-start(bf16[1152,128]{1,0:T(8,128)(2,1)S(1)} %collective-permute-done.1.refs_3_), channel_id=1, source_target_pairs={{0,4},{1,3},{4,8},{5,1},{8,12},{9,5},{12,14},{13,9},{14,10},{15,13... | collective-permute-start | bytes 884744 | tf_op jit(solution)/shard_map/ppermute | solution.py:433
  20.1 1.6 %collective-permute-done.7.refs_4_ = bf16[1152,128]{1,0:T(8,128)(2,1)S(1)} collective-permute-done((bf16[1152,128]{1,0:T(8,128)(2,1)S(1)}, bf16[1152,128]{1,0:T(8,128)(2,1)S(1)}, u32[]{:S(2)}, u32[]{:S(2)}) %collective-permute-start.7) | collective-permute-done | bytes 294944 | tf_op jit(solution)/shard_map/ppermute | solution.py:433
  21.6 1.6 %collective-permute-start.8 = (bf16[1152,128]{1,0:T(8,128)(2,1)S(1)}, bf16[1152,128]{1,0:T(8,128)(2,1)S(1)}, u32[]{:S(2)}, u32[]{:S(2)}) collective-permute-start(bf16[1152,128]{1,0:T(8,128)(2,1)S(1)} %collective-permute-done.7.refs_4_), channel_id=1, source_target_pairs={{0,4},{1,3},{4,8},{5,1},{8,12},{9,5},{12,14},{13,9},{14,10},{15,13... | collective-permute-start | bytes 884744 | tf_op jit(solution)/shard_map/ppermute | solution.py:433
  23.2 2.0 %collective-permute-done.5.refs_5_ = bf16[1152,128]{1,0:T(8,128)(2,1)S(1)} collective-permute-done((bf16[1152,128]{1,0:T(8,128)(2,1)S(1)}, bf16[1152,128]{1,0:T(8,128)(2,1)S(1)}, u32[]{:S(2)}, u32[]{:S(2)}) %collective-permute-start.5) | collective-permute-done | bytes 294944 | tf_op jit(solution)/shard_map/ppermute | solution.py:433
  25.2 1.6 %collective-permute-start.9 = (bf16[1152,128]{1,0:T(8,128)(2,1)S(1)}, bf16[1152,128]{1,0:T(8,128)(2,1)S(1)}, u32[]{:S(2)}, u32[]{:S(2)}) collective-permute-start(bf16[1152,128]{1,0:T(8,128)(2,1)S(1)} %collective-permute-done.5.refs_5_), channel_id=1, source_target_pairs={{0,4},{1,3},{4,8},{5,1},{8,12},{9,5},{12,14},{13,9},{14,10},{15,13... | collective-permute-start | bytes 884744 | tf_op jit(solution)/shard_map/ppermute | solution.py:433
  26.8 3.4 %copy-done = f32[257,64,128]{2,1,0:T(8,128)S(1)} copy-done((f32[257,64,128]{2,1,0:T(8,128)S(1)}, f32[257,64,128]{2,1,0:T(8,128)}, u32[]{:S(2)}) %copy-start) | copy-done | bytes 8421400
  30.2 4.5 %near.3.refs_8_ = f32[257,64,128]{2,1,0:T(8,128)S(1)} custom-call(s32[16,128]{1,0:T(8,128)S(1)} %pad_add_fusion.list_ref, bf16[1152,128]{1,0:T(8,128)(2,1)S(1)} %collective-permute-done.3.refs_0_, bf16[1152,128]{1,0:T(8,128)(2,1)S(1)} %collective-permute-done.refs_1_, ...), custom_call_target="tpu_custom_call", output_to_operand_aliasing={{}: (8, {})} | custom-call | flops 2147483648 | bytes 16777216 | tf_op jit(solution)/shard_map/near/pallas_call | solution.py:492
  34.7 2.9 %near.4.refs_10_ = f32[257,64,128]{2,1,0:T(8,128)S(1)} custom-call(s32[16,128]{1,0:T(8,128)S(1)} %pad_add_fusion.list_ref, bf16[1152,128]{1,0:T(8,128)(2,1)S(1)} %collective-permute-done.3.refs_0_, bf16[1152,128]{1,0:T(8,128)(2,1)S(1)} %collective-permute-done.refs_1_, ...), custom_call_target="tpu_custom_call", output_to_operand_aliasing={{}: (9, {})} | custom-call | flops 2147483648 | bytes 16777216 | tf_op jit(solution)/shard_map/near/pallas_call | solution.py:492
  37.7 2.6 %near.5 = (f32[257,64,128]{2,1,0:T(8,128)S(1)}, bf16[1024,128]{1,0:T(8,128)(2,1)S(1)}, bf16[32,64,128]{2,1,0:T(8,128)(2,1)S(1)}, bf16[96,64,128]{2,1,0:T(8,128)(2,1)S(1)}) custom-call(s32[16,128]{1,0:T(8,128)S(1)} %pad_add_fusion.list_ref, bf16[1152,128]{1,0:T(8,128)(2,1)S(1)} %collective-permute-done.3.refs_0_, ...), custom_call_target="tpu_custom_call", output_to_operand_aliasing={{0}: (11, {})} | custom-call | flops 2147483648 | bytes 16777216 | tf_op jit(solution)/shard_map/near/pallas_call | solution.py:492
  40.4 1.9 %collective-permute-done.11 = bf16[32,64,128]{2,1,0:T(8,128)(2,1)S(1)} collective-permute-done((bf16[32,64,128]{2,1,0:T(8,128)(2,1)S(1)}, bf16[32,64,128]{2,1,0:T(8,128)(2,1)S(1)}, u32[]{:S(2)}, u32[]{:S(2)}) %collective-permute-start.11) | collective-permute-done | bytes 524320 | tf_op jit(solution)/shard_map/ppermute | solution.py:433
  42.7 1.9 %collective-permute-start.12 = (bf16[16,64,128]{2,1,0:T(8,128)(2,1)S(1)}, bf16[16,64,128]{2,1,0:T(8,128)(2,1)S(1)}, u32[]{:S(2)}, u32[]{:S(2)}) collective-permute-start(bf16[16,64,128]{2,1,0:T(8,128)(2,1)S(1)} %get-tuple-element.54), channel_id=1, source_target_pairs={{0,4},{1,3},{4,8},{5,1},{8,12},{9,5},{12,14},{13,9},{14,10},{15,13... | collective-permute-start | bytes 786440 | tf_op jit(solution)/shard_map/ppermute | solution.py:433
  44.6 1.5 %collective-permute-start.15 = (bf16[16,64,128]{2,1,0:T(8,128)(2,1)S(1)}, bf16[16,64,128]{2,1,0:T(8,128)(2,1)S(1)}, u32[]{:S(2)}, u32[]{:S(2)}) collective-permute-start(bf16[16,64,128]{2,1,0:T(8,128)(2,1)S(1)} %get-tuple-element.56), channel_id=1, source_target_pairs={{0,4},{1,3},{4,8},{5,1},{8,12},{9,5},{12,14},{13,9},{14,10},{15,13... | collective-permute-start | bytes 786440 | tf_op jit(solution)/shard_map/ppermute | solution.py:433
  46.1 3.0 %collective-permute-done.12 = bf16[16,64,128]{2,1,0:T(8,128)(2,1)S(1)} collective-permute-done((bf16[16,64,128]{2,1,0:T(8,128)(2,1)S(1)}, bf16[16,64,128]{2,1,0:T(8,128)(2,1)S(1)}, u32[]{:S(2)}, u32[]{:S(2)}) %collective-permute-start.12) | collective-permute-done | bytes 262176 | tf_op jit(solution)/shard_map/ppermute | solution.py:433
  49.2 2.0 %collective-permute-start.14 = (bf16[16,64,128]{2,1,0:T(8,128)(2,1)S(1)}, bf16[16,64,128]{2,1,0:T(8,128)(2,1)S(1)}, u32[]{:S(2)}, u32[]{:S(2)}) collective-permute-start(bf16[16,64,128]{2,1,0:T(8,128)(2,1)S(1)} %add_convert_fusion.5), channel_id=1, source_target_pairs={{0,4},{1,3},{4,8},{5,1},{8,12},{9,5},{12,14},{13,9},{14,10},{15,13... | collective-permute-start | bytes 786440 | tf_op jit(solution)/shard_map/ppermute | solution.py:433
  52.0 2.0 %collective-permute-start.17 = (bf16[16,64,128]{2,1,0:T(8,128)(2,1)S(1)}, bf16[16,64,128]{2,1,0:T(8,128)(2,1)S(1)}, u32[]{:S(2)}, u32[]{:S(2)}) collective-permute-start(bf16[16,64,128]{2,1,0:T(8,128)(2,1)S(1)} %add_convert_fusion.4), channel_id=1, source_target_pairs={{0,4},{1,3},{4,8},{5,1},{8,12},{9,5},{12,14},{13,9},{14,10},{15,13... | collective-permute-start | bytes 786440 | tf_op jit(solution)/shard_map/ppermute | solution.py:433
  53.9 1.7 %collective-permute-done.14 = bf16[16,64,128]{2,1,0:T(8,128)(2,1)S(1)} collective-permute-done((bf16[16,64,128]{2,1,0:T(8,128)(2,1)S(1)}, bf16[16,64,128]{2,1,0:T(8,128)(2,1)S(1)}, u32[]{:S(2)}, u32[]{:S(2)}) %collective-permute-start.14) | collective-permute-done | bytes 262176 | tf_op jit(solution)/shard_map/ppermute | solution.py:433
  55.7 2.0 %collective-permute-start.16 = (bf16[16,64,128]{2,1,0:T(8,128)(2,1)S(1)}, bf16[16,64,128]{2,1,0:T(8,128)(2,1)S(1)}, u32[]{:S(2)}, u32[]{:S(2)}) collective-permute-start(bf16[16,64,128]{2,1,0:T(8,128)(2,1)S(1)} %add_convert_fusion.3), channel_id=1, source_target_pairs={{0,4},{1,3},{4,8},{5,1},{8,12},{9,5},{12,14},{13,9},{14,10},{15,13... | collective-permute-start | bytes 786440 | tf_op jit(solution)/shard_map/ppermute | solution.py:433
  58.5 2.0 %collective-permute-start.19 = (bf16[16,64,128]{2,1,0:T(8,128)(2,1)S(1)}, bf16[16,64,128]{2,1,0:T(8,128)(2,1)S(1)}, u32[]{:S(2)}, u32[]{:S(2)}) collective-permute-start(bf16[16,64,128]{2,1,0:T(8,128)(2,1)S(1)} %add_convert_fusion.2), channel_id=1, source_target_pairs={{0,4},{1,3},{4,8},{5,1},{8,12},{9,5},{12,14},{13,9},{14,10},{15,13... | collective-permute-start | bytes 786440 | tf_op jit(solution)/shard_map/ppermute | solution.py:433
  60.5 1.6 %collective-permute-done.16 = bf16[16,64,128]{2,1,0:T(8,128)(2,1)S(1)} collective-permute-done((bf16[16,64,128]{2,1,0:T(8,128)(2,1)S(1)}, bf16[16,64,128]{2,1,0:T(8,128)(2,1)S(1)}, u32[]{:S(2)}, u32[]{:S(2)}) %collective-permute-start.16) | collective-permute-done | bytes 262176 | tf_op jit(solution)/shard_map/ppermute | solution.py:433
  62.2 2.0 %collective-permute-start.18 = (bf16[16,64,128]{2,1,0:T(8,128)(2,1)S(1)}, bf16[16,64,128]{2,1,0:T(8,128)(2,1)S(1)}, u32[]{:S(2)}, u32[]{:S(2)}) collective-permute-start(bf16[16,64,128]{2,1,0:T(8,128)(2,1)S(1)} %add_convert_fusion.1), channel_id=1, source_target_pairs={{0,4},{1,3},{4,8},{5,1},{8,12},{9,5},{12,14},{13,9},{14,10},{15,13... | collective-permute-start | bytes 786440 | tf_op jit(solution)/shard_map/ppermute | solution.py:433
  65.0 2.5 %far.1 = f32[16,64,128]{2,1,0:T(8,128)S(1)} custom-call(bf16[1024,128]{1,0:T(8,128)(2,1)S(1)} %get-tuple-element.51.refs_0_, bf16[1024,128]{1,0:T(8,128)(2,1)S(1)} %collective-permute-done.10.refs_1_, s32[1]{0:T(128)} %bitcast.me_ref.token_ref.refs_2_, bf16[16,16,256]{2,1,0:T(8,128)(2,1)S(1)} %bitcast.10, s32[1,256]{1,0:T(1,128)S(1)} %bitcast.11, ...), custom_call_target="tpu_custom_call" | custom-call | flops 536870912 | bytes 8388608 | tf_op jit(solution)/shard_map/far/pallas_call | solution.py:521
  67.5 1.2 %collective-permute-done.18 = bf16[16,64,128]{2,1,0:T(8,128)(2,1)S(1)} collective-permute-done((bf16[16,64,128]{2,1,0:T(8,128)(2,1)S(1)}, bf16[16,64,128]{2,1,0:T(8,128)(2,1)S(1)}, u32[]{:S(2)}, u32[]{:S(2)}) %collective-permute-start.18) | collective-permute-done | bytes 262176 | tf_op jit(solution)/shard_map/ppermute | solution.py:433
  68.8 0.8 %add_convert_fusion = bf16[16,64,128]{2,1,0:T(8,128)(2,1)} fusion(f32[16,64,128]{2,1,0:T(8,128)S(1)} %convert_add_fusion, bf16[16,64,128]{2,1,0:T(8,128)(2,1)S(1)} %collective-permute-done.20), kind=kLoop, calls=%fused_computation | loop fusion | flops 393216 | bytes 1048576 | tf_op jit(solution)/shard_map/convert_element_type | solution.py:574
  (40 shorter events, 4.1 us)
Async XLA Ops:
  0.0 18.5 %collective-permute-start.2 = (bf16[128,128,128]{2,1,0:T(8,128)(2,1)}, bf16[128,128,128]{2,1,0:T(8,128)(2,1)}, u32[]{:S(2)}, u32[]{:S(2)}) collective-permute-start(bf16[128,128,128]{2,1,0:T(8,128)(2,1)} %refs_8_.1), channel_id=1, source_target_pairs={{0,1},{1,0},{2,3},{3,2},{4,5},{5,4},{6,7},{7,6},{8,9},{9,8},{10,11... | collective-permute-start | bytes 12582920 | tf_op jit(solution)/shard_map/ppermute | solution.py:433
  2.6 12.7 %copy-start.6 = (s32[8,128]{1,0:T(8,128)S(1)}, s32[8,128]{1,0:T(8,128)}, u32[]{:S(2)}) copy-start(s32[8,128]{1,0:T(8,128)} %get-tuple-element.44) | copy-start | bytes 12292
  2.6 9.1 %collective-permute-start = (bf16[1152,128]{1,0:T(8,128)(2,1)}, bf16[1152,128]{1,0:T(8,128)(2,1)S(1)}, u32[]{:S(2)}, u32[]{:S(2)}) collective-permute-start(bf16[1152,128]{1,0:T(8,128)(2,1)} %get-tuple-element.43), channel_id=1, source_target_pairs={{0,4},{1,3},{4,8},{5,1},{8,12},{9,5},{12,14},{13,9},{14,10},{15,13... | collective-permute-start | bytes 884744 | tf_op jit(solution)/shard_map/ppermute | solution.py:433
  6.1 7.2 %collective-permute-start.6 = (bf16[1152,128]{1,0:T(8,128)(2,1)}, bf16[1152,128]{1,0:T(8,128)(2,1)S(1)}, u32[]{:S(2)}, u32[]{:S(2)}) collective-permute-start(bf16[1152,128]{1,0:T(8,128)(2,1)} %get-tuple-element.43), channel_id=1, source_target_pairs={{0,3},{1,4},{4,1},{5,8},{8,5},{9,12},{12,9},{13,14},{14,13},{15,10... | collective-permute-start | bytes 884744 | tf_op jit(solution)/shard_map/ppermute | solution.py:433
  7.5 8.9 %collective-permute-start.3 = (bf16[1152,128]{1,0:T(8,128)(2,1)}, bf16[1152,128]{1,0:T(8,128)(2,1)S(1)}, u32[]{:S(2)}, u32[]{:S(2)}) collective-permute-start(bf16[1152,128]{1,0:T(8,128)(2,1)} %get-tuple-element.43), channel_id=1, source_target_pairs={{0,1},{1,0},{2,3},{3,2},{4,5},{5,4},{6,7},{7,6},{8,9},{9,8},{10,11... | collective-permute-start | bytes 884744 | tf_op jit(solution)/shard_map/ppermute | solution.py:433
  11.7 6.7 %collective-permute-start.1 = (bf16[1152,128]{1,0:T(8,128)(2,1)S(1)}, bf16[1152,128]{1,0:T(8,128)(2,1)S(1)}, u32[]{:S(2)}, u32[]{:S(2)}) collective-permute-start(bf16[1152,128]{1,0:T(8,128)(2,1)S(1)} %collective-permute-done.refs_1_), channel_id=1, source_target_pairs={{0,4},{1,3},{4,8},{5,1},{8,12},{9,5},{12,14},{13,9},{14,10},{15,13... | collective-permute-start | bytes 884744 | tf_op jit(solution)/shard_map/ppermute | solution.py:433
  13.3 8.3 %collective-permute-start.7 = (bf16[1152,128]{1,0:T(8,128)(2,1)S(1)}, bf16[1152,128]{1,0:T(8,128)(2,1)S(1)}, u32[]{:S(2)}, u32[]{:S(2)}) collective-permute-start(bf16[1152,128]{1,0:T(8,128)(2,1)S(1)} %collective-permute-done.6.refs_2_), channel_id=1, source_target_pairs={{0,4},{1,3},{4,8},{5,1},{8,12},{9,5},{12,14},{13,9},{14,10},{15,13... | collective-permute-start | bytes 884744 | tf_op jit(solution)/shard_map/ppermute | solution.py:433
  15.3 1.2 %collective-permute-start.4 = (s32[8,128]{1,0:T(8,128)S(1)}, s32[8,128]{1,0:T(8,128)S(1)}, u32[]{:S(2)}, u32[]{:S(2)}) collective-permute-start(s32[8,128]{1,0:T(8,128)S(1)} %copy-done.6), channel_id=1, source_target_pairs={{0,1},{1,0},{2,3},{3,2},{4,5},{5,4},{6,7},{7,6},{8,9},{9,8},{10,11... | collective-permute-start | bytes 12296 | tf_op jit(solution)/shard_map/ppermute | solution.py:433
  18.5 6.7 %collective-permute-start.5 = (bf16[1152,128]{1,0:T(8,128)(2,1)S(1)}, bf16[1152,128]{1,0:T(8,128)(2,1)S(1)}, u32[]{:S(2)}, u32[]{:S(2)}) collective-permute-start(bf16[1152,128]{1,0:T(8,128)(2,1)S(1)} %collective-permute-done.1.refs_3_), channel_id=1, source_target_pairs={{0,4},{1,3},{4,8},{5,1},{8,12},{9,5},{12,14},{13,9},{14,10},{15,13... | collective-permute-start | bytes 884744 | tf_op jit(solution)/shard_map/ppermute | solution.py:433
  21.6 13.1 %collective-permute-start.8 = (bf16[1152,128]{1,0:T(8,128)(2,1)S(1)}, bf16[1152,128]{1,0:T(8,128)(2,1)S(1)}, u32[]{:S(2)}, u32[]{:S(2)}) collective-permute-start(bf16[1152,128]{1,0:T(8,128)(2,1)S(1)} %collective-permute-done.7.refs_4_), channel_id=1, source_target_pairs={{0,4},{1,3},{4,8},{5,1},{8,12},{9,5},{12,14},{13,9},{14,10},{15,13... | collective-permute-start | bytes 884744 | tf_op jit(solution)/shard_map/ppermute | solution.py:433
  25.2 12.5 %collective-permute-start.9 = (bf16[1152,128]{1,0:T(8,128)(2,1)S(1)}, bf16[1152,128]{1,0:T(8,128)(2,1)S(1)}, u32[]{:S(2)}, u32[]{:S(2)}) collective-permute-start(bf16[1152,128]{1,0:T(8,128)(2,1)S(1)} %collective-permute-done.5.refs_5_), channel_id=1, source_target_pairs={{0,4},{1,3},{4,8},{5,1},{8,12},{9,5},{12,14},{13,9},{14,10},{15,13... | collective-permute-start | bytes 884744 | tf_op jit(solution)/shard_map/ppermute | solution.py:433
  26.8 3.4 %copy-start = (f32[257,64,128]{2,1,0:T(8,128)S(1)}, f32[257,64,128]{2,1,0:T(8,128)}, u32[]{:S(2)}) copy-start(f32[257,64,128]{2,1,0:T(8,128)} %clear.1.refs_7_) | copy-start | bytes 25264132
  30.2 4.6 %copy-start.1 = (bf16[128,128,128]{2,1,0:T(8,128)(2,1)S(1)}, bf16[128,128,128]{2,1,0:T(8,128)(2,1)}, u32[]{:S(2)}) copy-start(bf16[128,128,128]{2,1,0:T(8,128)(2,1)} %refs_8_.1) | copy-start | bytes 12582916
  40.3 24.6 %copy-start.2 = (bf16[16,16,128]{2,1,0:T(8,128)(2,1)S(1)}, bf16[16,16,128]{2,1,0:T(8,128)(2,1)}, u32[]{:S(2)}) copy-start(bf16[16,16,128]{2,1,0:T(8,128)(2,1)} %refs_7_.3) | copy-start | bytes 196612
  40.3 24.6 %copy-start.3 = (s32[256]{0:T(256)S(1)}, s32[256]{0:T(256)}, u32[]{:S(2)}) copy-start(s32[256]{0:T(256)} %param.17) | copy-start | bytes 3076
  40.3 24.6 %copy-start.4 = (s32[256,1]{0,1:T(1,128)S(1)}, s32[256,1]{0,1:T(1,128)}, u32[]{:S(2)}) copy-start(s32[256,1]{0,1:T(1,128)} %param.18) | copy-start | bytes 3076
  40.3 24.6 %copy-start.5 = (s32[256]{0:T(256)S(1)}, s32[256]{0:T(256)}, u32[]{:S(2)}) copy-start(s32[256]{0:T(256)} %param.19) | copy-start | bytes 3076
  40.3 2.0 %collective-permute-start.11 = (bf16[32,64,128]{2,1,0:T(8,128)(2,1)S(1)}, bf16[32,64,128]{2,1,0:T(8,128)(2,1)S(1)}, u32[]{:S(2)}, u32[]{:S(2)}) collective-permute-start(bf16[32,64,128]{2,1,0:T(8,128)(2,1)S(1)} %get-tuple-element.53), channel_id=1, source_target_pairs={{0,1},{1,0},{2,3},{3,2},{4,5},{5,4},{6,7},{7,6},{8,9},{9,8},{10,11... | collective-permute-start | bytes 1572872 | tf_op jit(solution)/shard_map/ppermute | solution.py:433
  42.5 6.6 %collective-permute-start.13 = (bf16[96,64,128]{2,1,0:T(8,128)(2,1)S(1)}, bf16[96,64,128]{2,1,0:T(8,128)(2,1)S(1)}, u32[]{:S(2)}, u32[]{:S(2)}) collective-permute-start(bf16[96,64,128]{2,1,0:T(8,128)(2,1)S(1)} %get-tuple-element.57), channel_id=1, source_target_pairs={{0,1},{1,0},{2,3},{3,2},{4,5},{5,4},{6,7},{7,6},{8,9},{9,8},{10,11... | collective-permute-start | bytes 4718600 | tf_op jit(solution)/shard_map/ppermute | solution.py:433
  42.7 6.4 %collective-permute-start.12 = (bf16[16,64,128]{2,1,0:T(8,128)(2,1)S(1)}, bf16[16,64,128]{2,1,0:T(8,128)(2,1)S(1)}, u32[]{:S(2)}, u32[]{:S(2)}) collective-permute-start(bf16[16,64,128]{2,1,0:T(8,128)(2,1)S(1)} %get-tuple-element.54), channel_id=1, source_target_pairs={{0,4},{1,3},{4,8},{5,1},{8,12},{9,5},{12,14},{13,9},{14,10},{15,13... | collective-permute-start | bytes 786440 | tf_op jit(solution)/shard_map/ppermute | solution.py:433
  44.6 7.3 %collective-permute-start.15 = (bf16[16,64,128]{2,1,0:T(8,128)(2,1)S(1)}, bf16[16,64,128]{2,1,0:T(8,128)(2,1)S(1)}, u32[]{:S(2)}, u32[]{:S(2)}) collective-permute-start(bf16[16,64,128]{2,1,0:T(8,128)(2,1)S(1)} %get-tuple-element.56), channel_id=1, source_target_pairs={{0,4},{1,3},{4,8},{5,1},{8,12},{9,5},{12,14},{13,9},{14,10},{15,13... | collective-permute-start | bytes 786440 | tf_op jit(solution)/shard_map/ppermute | solution.py:433
  49.2 6.4 %collective-permute-start.14 = (bf16[16,64,128]{2,1,0:T(8,128)(2,1)S(1)}, bf16[16,64,128]{2,1,0:T(8,128)(2,1)S(1)}, u32[]{:S(2)}, u32[]{:S(2)}) collective-permute-start(bf16[16,64,128]{2,1,0:T(8,128)(2,1)S(1)} %add_convert_fusion.5), channel_id=1, source_target_pairs={{0,4},{1,3},{4,8},{5,1},{8,12},{9,5},{12,14},{13,9},{14,10},{15,13... | collective-permute-start | bytes 786440 | tf_op jit(solution)/shard_map/ppermute | solution.py:433
  52.0 6.4 %collective-permute-start.17 = (bf16[16,64,128]{2,1,0:T(8,128)(2,1)S(1)}, bf16[16,64,128]{2,1,0:T(8,128)(2,1)S(1)}, u32[]{:S(2)}, u32[]{:S(2)}) collective-permute-start(bf16[16,64,128]{2,1,0:T(8,128)(2,1)S(1)} %add_convert_fusion.4), channel_id=1, source_target_pairs={{0,4},{1,3},{4,8},{5,1},{8,12},{9,5},{12,14},{13,9},{14,10},{15,13... | collective-permute-start | bytes 786440 | tf_op jit(solution)/shard_map/ppermute | solution.py:433
  55.7 6.4 %collective-permute-start.16 = (bf16[16,64,128]{2,1,0:T(8,128)(2,1)S(1)}, bf16[16,64,128]{2,1,0:T(8,128)(2,1)S(1)}, u32[]{:S(2)}, u32[]{:S(2)}) collective-permute-start(bf16[16,64,128]{2,1,0:T(8,128)(2,1)S(1)} %add_convert_fusion.3), channel_id=1, source_target_pairs={{0,4},{1,3},{4,8},{5,1},{8,12},{9,5},{12,14},{13,9},{14,10},{15,13... | collective-permute-start | bytes 786440 | tf_op jit(solution)/shard_map/ppermute | solution.py:433
  57.6 7.3 %collective-permute-start.10 = (bf16[1024,128]{1,0:T(8,128)(2,1)S(1)}, bf16[1024,128]{1,0:T(8,128)(2,1)S(1)}, u32[]{:S(2)}, u32[]{:S(2)}) collective-permute-start(bf16[1024,128]{1,0:T(8,128)(2,1)S(1)} %get-tuple-element.51.refs_0_), channel_id=1, source_target_pairs={{0,1},{1,0},{2,3},{3,2},{4,5},{5,4},{6,7},{7,6},{8,9},{9,8},{10,11... | collective-permute-start | bytes 786440 | tf_op jit(solution)/shard_map/ppermute | solution.py:433
  58.5 6.4 %collective-permute-start.19 = (bf16[16,64,128]{2,1,0:T(8,128)(2,1)S(1)}, bf16[16,64,128]{2,1,0:T(8,128)(2,1)S(1)}, u32[]{:S(2)}, u32[]{:S(2)}) collective-permute-start(bf16[16,64,128]{2,1,0:T(8,128)(2,1)S(1)} %add_convert_fusion.2), channel_id=1, source_target_pairs={{0,4},{1,3},{4,8},{5,1},{8,12},{9,5},{12,14},{13,9},{14,10},{15,13... | collective-permute-start | bytes 786440 | tf_op jit(solution)/shard_map/ppermute | solution.py:433
  62.2 6.4 %collective-permute-start.18 = (bf16[16,64,128]{2,1,0:T(8,128)(2,1)S(1)}, bf16[16,64,128]{2,1,0:T(8,128)(2,1)S(1)}, u32[]{:S(2)}, u32[]{:S(2)}) collective-permute-start(bf16[16,64,128]{2,1,0:T(8,128)(2,1)S(1)} %add_convert_fusion.1), channel_id=1, source_target_pairs={{0,4},{1,3},{4,8},{5,1},{8,12},{9,5},{12,14},{13,9},{14,10},{15,13... | collective-permute-start | bytes 786440 | tf_op jit(solution)/shard_map/ppermute | solution.py:433
  64.9 3.8 %collective-permute-start.20 = (bf16[16,64,128]{2,1,0:T(8,128)(2,1)S(1)}, bf16[16,64,128]{2,1,0:T(8,128)(2,1)S(1)}, u32[]{:S(2)}, u32[]{:S(2)}) collective-permute-start(bf16[16,64,128]{2,1,0:T(8,128)(2,1)S(1)} %collective-permute-done.19), channel_id=1, source_target_pairs={{0,1},{1,0},{2,3},{3,2},{4,5},{5,4},{6,7},{7,6},{8,9},{9,8},{10,11... | collective-permute-start | bytes 786440 | tf_op jit(solution)/shard_map/ppermute | solution.py:433

commit v21 on v19

--- a/solution.py
+++ b/solution.py
@@ -7,7 +7,7 @@
 from jax.experimental.pallas import tpu as pltpu
 from jax.sharding import PartitionSpec as P
 
-BATCH = 16, 16, 8
+BATCH = 16, 8
 CHUNKS = 4
 LATE = 2
 UNITS = 1
@@ -156,7 +156,7 @@
     theirs = (shard == count // 2).astype(jnp.int32)
     shard = jnp.where(theirs == 1, gather_place(column // clusters, me ^ 1, count), shard)
     column_place = shard * clusters + (column & (clusters - 1))
-    late = (shard >= count // 2 - LATE + 1 - theirs).astype(jnp.int32)
+    late = (shard >= count // 2 - LATE).astype(jnp.int32)
     square = (stored, stored)
     group = jnp.broadcast_to((2 * theirs + late).astype(jnp.float32), square)
     group_of_row = jnp.transpose(group)
@@ -178,16 +178,16 @@
     list_ref[...] = values.astype(jnp.int32)
 
 
-def near_kernel(part, batch, shards, sends, list_ref, *refs):
-    late = int(part == 2)
+def join_kernel(first_ref, second_ref, out_ref):
+    rows = first_ref.shape[0]
+    out_ref[0:rows] = first_ref[...]
+    out_ref[rows:] = second_ref[...]
+
+
+def near_kernel(late, batch, shards, sends, list_ref, *refs):
     used = LATE if late else shards
     shard_refs, refs = refs[:shards], refs[shards:]
-    if part > 0:
-        own_ref, refs = refs[0], refs[1:]
-    if part != 1:
-        mate_hbm, refs = refs[0], refs[1:]
-    if part > 0:
-        refs = refs[1:]
+    (own_ref, mate_hbm), refs = refs[:2], refs[2 + late :]
     sums, refs = refs[0], refs[1:]
     if late:
         coef_ref, send_refs, refs = refs[0], refs[1 : 1 + sends], refs[1 + sends :]
@@ -211,7 +211,7 @@
 
     if late:
         lax.fori_loop(0, steps_there * batch, fetch, 0)
-    elif part == 0:
+    else:
         for c in range(CHUNKS):
             at = pl.ds(c * chunk, chunk)
             pltpu.make_async_copy(mate_hbm.at[at], blocks.at[at], block_sem.at[c]).start()
@@ -230,7 +230,7 @@
         tail = coef_ref.shape[0] // shards
         for k, ref in enumerate(shard_refs):
             coef_ref[k * tail : (k + 1) * tail] = ref[span : span + tail]
-    elif part == 0:
+    else:
 
         def clear(i, carry):
             sums[i] = jnp.zeros(sums.shape[1:], sums.dtype)
@@ -289,13 +289,10 @@
         lax.fori_loop(ready, needed, wait, 0)
         return lambda i: blocks[list_ref[8, entry(first + i)]], jnp.maximum(ready, needed)
 
-    if part > 0:
-        run(begin, end, 0, 0, own_blocks)
-    if part != 1:
-        ready = run(begin_there, end_there, 8, dummy // 2, mate_blocks)
-    if part == 0:
+    run(begin, end, 0, 0, own_blocks)
+    ready = run(begin_there, end_there, 8, dummy // 2, mate_blocks)
+    if not late:
         lax.fori_loop(ready, CHUNKS, wait, 0)
-    if not late:
         return
     at = dummy // 2
     for send_ref in send_refs:
@@ -462,6 +459,11 @@
     couple = jnp.transpose(far_coupling, (2, 1, 0))
     flow.append(move(after(payload, couple), cross))
     shards = [move(payload, mate)]
+    cost = pl.CostEstimate(
+        flops=16 * stored * directions * unknowns * unknowns,
+        bytes_accessed=16 << 20,
+        transcendentals=0,
+    )
     for k in range(1, chips):
         x = 1 - k % 2
         if k == 3:
@@ -469,7 +471,14 @@
                 (flow[x], mate_blocks, shards[0], mate_lists)
             )
         if k == 4:
-            lists = jnp.concatenate([after(lists, flow[x]), mate_lists], axis=0)
+            lists = pl.pallas_call(
+                join_kernel,
+                out_shape=jax.ShapeDtypeStruct((16, stored), jnp.int32),
+                in_specs=[whole()] * 2,
+                out_specs=whole(),
+                cost_estimate=cost,
+                name="join",
+            )(after(lists, flow[x]), mate_lists)
         if k == 5:
             flow[x], lists = lax.optimization_barrier((flow[x], lists))
         shards.append(flow[x])
@@ -479,11 +488,10 @@
     pieces = [2, chips - 2]
     sums_shape = jax.ShapeDtypeStruct((count * clusters + 1, directions, unknowns), jnp.float32)
 
-    def near(part, shards, sources, *sums):
-        late = int(part == 2)
+    def near(late, shards, *sums):
         sends = pieces if late else []
         return pl.pallas_call(
-            functools.partial(near_kernel, part, BATCH[part], len(shards), len(sends)),
+            functools.partial(near_kernel, late, BATCH[late], len(shards), len(sends)),
             out_shape=[sums_shape]
             + [jax.ShapeDtypeStruct((chips * half * rank_k, unknowns), jnp.bfloat16)] * late
             + [
@@ -492,23 +500,19 @@
             ],
             in_specs=[whole(pltpu.SMEM)]
             + [whole()] * len(shards)
-            + [[whole(pl.ANY)], [whole()], [whole(), whole(pl.ANY)]][part]
+            + [whole(), whole(pl.ANY)]
             + [whole()] * len(sums),
             out_specs=[whole()] * (1 + late + len(sends)),
-            input_output_aliases={1 + len(shards) + len(sources): 0} if sums else {},
+            input_output_aliases={3 + len(shards): 0} if sums else {},
             scratch_shapes=[
                 pltpu.VMEM(((LATE if late else len(shards)) * base, unknowns), jnp.bfloat16),
                 pltpu.VMEM(near_blocks.shape, jnp.bfloat16),
-                pltpu.SemaphoreType.DMA((max(CHUNKS, stored // BATCH[part]),)),
+                pltpu.SemaphoreType.DMA((max(CHUNKS, stored // BATCH[late]),)),
             ],
             compiler_params=pltpu.CompilerParams(vmem_limit_bytes=NEAR_VMEM),
-            cost_estimate=pl.CostEstimate(
-                flops=16 * stored * directions * unknowns * unknowns,
-                bytes_accessed=16 << 20,
-                transcendentals=0,
-            ),
+            cost_estimate=cost,
             name="near",
-        )(lists, *shards, *sources, *sums)
+        )(lists, *shards, near_blocks, mate_blocks, *sums)
 
     def far_field(couple):
         return pl.pallas_call(
@@ -533,9 +537,8 @@
             basis_out,
         )
 
-    (sums,) = near(0, shards[: chips - LATE], [mate_blocks])
-    (sums,) = near(1, shards[: chips - LATE + 1], [near_blocks], sums)
-    sums, coef, *sends = near(2, shards, [near_blocks, mate_blocks], sums)
+    (sums,) = near(0, shards[: chips - LATE])
+    sums, coef, *sends = near(1, shards, sums)
     mates = [move(sends[0], mate)]
     coefs = [coef, move(coef, mate)]
 

time: 66 us -> 67.3 us (1.020)
  local copies, waits for them, and re-layouts: 0.97 us -> 3.85 us
  waiting for transfers between devices: 21.5 us -> 19.5 us
  starting transfers between devices: 26.4 us -> 27.8 us
  other arithmetic: 2.32 us -> 1.64 us
    unnamed x11 -> x15, local copies, waits for them, and re-layouts: 0.97 us -> 3.85 us
    ppermute x21, waiting for transfers between devices: 21.5 us -> 19.5 us  [move(): return lax.ppermute(values, 'blk', where)]
    ppermute x21, starting transfers between devices: 26.4 us -> 27.8 us  [move(): return lax.ppermute(values, 'blk', where)]
    concatenate x1 -> x0, other arithmetic: 0.69 us -> none  [stationary(): lists = jnp.concatenate([after(lists, flow[x]), mate_lists], axis=0)]
  transfers between devices with their start and end apart: 21 -> 21, of which waited for: 13 -> 13; matrix products, arithmetic and copies ran while one was open for 4% -> 2% of each run, Pallas kernels for 18% -> 16%
where the time goes in v21:
time: 67.3 us; the launch traced here: 67.1 us
  starting transfers between devices  27.8 us (41%)
  waiting for transfers between devices  19.5 us (29%)
  Pallas kernels  14.2 us (21%)
  local copies, waits for them, and re-layouts  3.85 us (6%)
  other arithmetic  1.64 us (2%)
    ppermute x21, starting transfers between devices, move(): return lax.ppermute(values, 'blk', where)  27.8 us
    ppermute x21, waiting for transfers between devices, move(): return lax.ppermute(values, 'blk', where)  19.5 us
    pallas_call x2, Pallas kernels, near(): pl.pallas_call(functools.partial(near_kernel, late, BATCH[late], len(shar...  8.26 us
    unnamed x15, local copies, waits for them, and re-layouts  3.85 us
    pallas_call x1, Pallas kernels, far_field(): pl.pallas_call(far_kernel, out_shape=jax.ShapeDtypeStruct((clusters, dire...  2.51 us
    pallas_call x1, Pallas kernels, stationary(): pl.pallas_call(functools.partial(prologue_kernel, count), out_shape=[jax....  2.14 us
  transfers between devices with their start and end apart: 21, of which 13 were waited for; matrix products, arithmetic and copies ran while one was open for 2% of the time, Pallas kernels for 16%

profile of v21, /device:TPU:0, one launch (start us, length us, event | category | flops | bytes accessed | tf_op | source)
XLA Modules:
  0.0 67.1 jit_solution(1040147310748474471)
XLA Ops:
  0.5 2.1 %prologue.1 = (bf16[1152,128]{1,0:T(8,128)(2,1)}, s32[8,128]{1,0:T(8,128)}) custom-call(s32[1]{0:T(128)} %bitcast.me_ref.refs_2_, s32[1,128]{1,0:T(1,128)} %bitcast.14, s32[1,128]{1,0:T(1,128)} %bitcast.15, s32[1,128]{1,0:T(1,128)} %bitcast.16, bf16[16,64,128]{2,1,0:T(8,128)(2,1)} %rhs_ref.1, bf16[16,16,128]{2,1,0:T(8,128)(2,1)} %basis_ref.1), custom_call_target="tpu_custom_call" | custom-call | tf_op jit(solution)/shard_map/prologue/pallas_call | solution.py:438
  2.6 2.6 %collective-permute-start = (bf16[1152,128]{1,0:T(8,128)(2,1)}, bf16[1152,128]{1,0:T(8,128)(2,1)S(1)}, u32[]{:S(2)}, u32[]{:S(2)}) collective-permute-start(bf16[1152,128]{1,0:T(8,128)(2,1)} %get-tuple-element.36), channel_id=1, source_target_pairs={{0,4},{1,3},{4,8},{5,1},{8,12},{9,5},{12,14},{13,9},{14,10},{15,13... | collective-permute-start | bytes 884744 | tf_op jit(solution)/shard_map/ppermute | solution.py:431
  5.2 0.9 %copy.15 = bf16[256,16,16]{0,1,2:T(8,128)(2,1)S(1)} copy(bf16[256,16,16]{0,2,1:T(8,128)(2,1)} %param.16) | data formatting | bytes 262144 | tf_op args[5]
  6.1 1.4 %collective-permute-start.6 = (bf16[1152,128]{1,0:T(8,128)(2,1)}, bf16[1152,128]{1,0:T(8,128)(2,1)S(1)}, u32[]{:S(2)}, u32[]{:S(2)}) collective-permute-start(bf16[1152,128]{1,0:T(8,128)(2,1)} %get-tuple-element.36), channel_id=1, source_target_pairs={{0,3},{1,4},{4,1},{5,8},{8,5},{9,12},{12,9},{13,14},{14,13},{15,10... | collective-permute-start | bytes 884744 | tf_op jit(solution)/shard_map/ppermute | solution.py:431
  7.9 2.9 %collective-permute-done.refs_1_ = bf16[1152,128]{1,0:T(8,128)(2,1)S(1)} collective-permute-done((bf16[1152,128]{1,0:T(8,128)(2,1)}, bf16[1152,128]{1,0:T(8,128)(2,1)S(1)}, u32[]{:S(2)}, u32[]{:S(2)}) %collective-permute-start) | collective-permute-done | bytes 294944 | tf_op jit(solution)/shard_map/ppermute | solution.py:431
  10.8 2.4 %collective-permute-start.1 = (bf16[1152,128]{1,0:T(8,128)(2,1)S(1)}, bf16[1152,128]{1,0:T(8,128)(2,1)S(1)}, u32[]{:S(2)}, u32[]{:S(2)}) collective-permute-start(bf16[1152,128]{1,0:T(8,128)(2,1)S(1)} %collective-permute-done.refs_1_), channel_id=1, source_target_pairs={{0,4},{1,3},{4,8},{5,1},{8,12},{9,5},{12,14},{13,9},{14,10},{15,13... | collective-permute-start | bytes 884744 | tf_op jit(solution)/shard_map/ppermute | solution.py:431
  13.2 2.1 %collective-permute-start.7 = (bf16[1152,128]{1,0:T(8,128)(2,1)S(1)}, bf16[1152,128]{1,0:T(8,128)(2,1)S(1)}, u32[]{:S(2)}, u32[]{:S(2)}) collective-permute-start(bf16[1152,128]{1,0:T(8,128)(2,1)S(1)} %collective-permute-done.6.refs_2_), channel_id=1, source_target_pairs={{0,4},{1,3},{4,8},{5,1},{8,12},{9,5},{12,14},{13,9},{14,10},{15,13... | collective-permute-start | bytes 884744 | tf_op jit(solution)/shard_map/ppermute | solution.py:431
  15.3 1.4 %collective-permute-done.4.second_ref = s32[8,128]{1,0:T(8,128)S(1)} collective-permute-done((s32[8,128]{1,0:T(8,128)}, s32[8,128]{1,0:T(8,128)S(1)}, u32[]{:S(2)}, u32[]{:S(2)}) %collective-permute-start.4) | collective-permute-done | bytes 4128 | tf_op jit(solution)/shard_map/ppermute | solution.py:431
  16.6 1.5 %collective-permute-done.1.refs_3_ = bf16[1152,128]{1,0:T(8,128)(2,1)S(1)} collective-permute-done((bf16[1152,128]{1,0:T(8,128)(2,1)S(1)}, bf16[1152,128]{1,0:T(8,128)(2,1)S(1)}, u32[]{:S(2)}, u32[]{:S(2)}) %collective-permute-start.1) | collective-permute-done | bytes 294944 | tf_op jit(solution)/shard_map/ppermute | solution.py:431
  18.2 1.7 %collective-permute-start.5 = (bf16[1152,128]{1,0:T(8,128)(2,1)S(1)}, bf16[1152,128]{1,0:T(8,128)(2,1)S(1)}, u32[]{:S(2)}, u32[]{:S(2)}) collective-permute-start(bf16[1152,128]{1,0:T(8,128)(2,1)S(1)} %collective-permute-done.1.refs_3_), channel_id=1, source_target_pairs={{0,4},{1,3},{4,8},{5,1},{8,12},{9,5},{12,14},{13,9},{14,10},{15,13... | collective-permute-start | bytes 884744 | tf_op jit(solution)/shard_map/ppermute | solution.py:431
  19.9 1.4 %collective-permute-done.7.refs_4_ = bf16[1152,128]{1,0:T(8,128)(2,1)S(1)} collective-permute-done((bf16[1152,128]{1,0:T(8,128)(2,1)S(1)}, bf16[1152,128]{1,0:T(8,128)(2,1)S(1)}, u32[]{:S(2)}, u32[]{:S(2)}) %collective-permute-start.7) | collective-permute-done | bytes 294944 | tf_op jit(solution)/shard_map/ppermute | solution.py:431
  21.3 1.7 %collective-permute-start.8 = (bf16[1152,128]{1,0:T(8,128)(2,1)S(1)}, bf16[1152,128]{1,0:T(8,128)(2,1)S(1)}, u32[]{:S(2)}, u32[]{:S(2)}) collective-permute-start(bf16[1152,128]{1,0:T(8,128)(2,1)S(1)} %collective-permute-done.7.refs_4_), channel_id=1, source_target_pairs={{0,4},{1,3},{4,8},{5,1},{8,12},{9,5},{12,14},{13,9},{14,10},{15,13... | collective-permute-start | bytes 884744 | tf_op jit(solution)/shard_map/ppermute | solution.py:431
  23.1 1.3 %join.1.list_ref = s32[16,128]{1,0:T(8,128)} custom-call(s32[8,128]{1,0:T(8,128)} %get-tuple-element.37.first_ref, s32[8,128]{1,0:T(8,128)} %copy-done.6), custom_call_target="tpu_custom_call" | custom-call | flops 2147483648 | bytes 16777216 | tf_op jit(solution)/shard_map/join/pallas_call | solution.py:474
  24.9 1.7 %collective-permute-start.9 = (bf16[1152,128]{1,0:T(8,128)(2,1)S(1)}, bf16[1152,128]{1,0:T(8,128)(2,1)S(1)}, u32[]{:S(2)}, u32[]{:S(2)}) collective-permute-start(bf16[1152,128]{1,0:T(8,128)(2,1)S(1)} %collective-permute-done.5.refs_5_), channel_id=1, source_target_pairs={{0,4},{1,3},{4,8},{5,1},{8,12},{9,5},{12,14},{13,9},{14,10},{15,13... | collective-permute-start | bytes 884744 | tf_op jit(solution)/shard_map/ppermute | solution.py:431
  26.6 2.2 %copy-done = bf16[128,128,128]{2,1,0:T(8,128)(2,1)S(1)} copy-done((bf16[128,128,128]{2,1,0:T(8,128)(2,1)S(1)}, bf16[128,128,128]{2,1,0:T(8,128)(2,1)}, u32[]{:S(2)}) %copy-start) | copy-done | bytes 4194328
  28.8 0.7 %copy-done.1 = s32[16,128]{1,0:T(8,128)S(1)} copy-done((s32[16,128]{1,0:T(8,128)S(1)}, s32[16,128]{1,0:T(8,128)}, u32[]{:S(2)}) %copy-start.1) | copy-done | bytes 8216
  29.5 5.0 %near.2.refs_10_ = f32[257,64,128]{2,1,0:T(8,128)S(1)} custom-call(s32[16,128]{1,0:T(8,128)S(1)} %copy-done.1, bf16[1152,128]{1,0:T(8,128)(2,1)S(1)} %collective-permute-done.3.refs_0_, bf16[1152,128]{1,0:T(8,128)(2,1)S(1)} %collective-permute-done.refs_1_, bf16[1152,128]{1,0:T(8,128)(2,1)S(1)} %collective-permute-done.6.refs_2_, ...), custom_call_target="tpu_custom_call" | custom-call | flops 2147483648 | bytes 16777216 | tf_op jit(solution)/shard_map/near/pallas_call | solution.py:493
  34.5 3.3 %near.3 = (f32[257,64,128]{2,1,0:T(8,128)S(1)}, bf16[1024,128]{1,0:T(8,128)(2,1)S(1)}, bf16[32,64,128]{2,1,0:T(8,128)(2,1)S(1)}, bf16[96,64,128]{2,1,0:T(8,128)(2,1)S(1)}) custom-call(s32[16,128]{1,0:T(8,128)S(1)} %copy-done.1, bf16[1152,128]{1,0:T(8,128)(2,1)S(1)} %collective-permute-done.3.refs_0_, ...), custom_call_target="tpu_custom_call", output_to_operand_aliasing={{0}: (11, {})} | custom-call | flops 2147483648 | bytes 16777216 | tf_op jit(solution)/shard_map/near/pallas_call | solution.py:493
  37.9 1.9 %collective-permute-done.11 = bf16[32,64,128]{2,1,0:T(8,128)(2,1)S(1)} collective-permute-done((bf16[32,64,128]{2,1,0:T(8,128)(2,1)S(1)}, bf16[32,64,128]{2,1,0:T(8,128)(2,1)S(1)}, u32[]{:S(2)}, u32[]{:S(2)}) %collective-permute-start.11) | collective-permute-done | bytes 524320 | tf_op jit(solution)/shard_map/ppermute | solution.py:431
  40.2 1.9 %collective-permute-start.12 = (bf16[16,64,128]{2,1,0:T(8,128)(2,1)S(1)}, bf16[16,64,128]{2,1,0:T(8,128)(2,1)S(1)}, u32[]{:S(2)}, u32[]{:S(2)}) collective-permute-start(bf16[16,64,128]{2,1,0:T(8,128)(2,1)S(1)} %get-tuple-element.46), channel_id=1, source_target_pairs={{0,4},{1,3},{4,8},{5,1},{8,12},{9,5},{12,14},{13,9},{14,10},{15,13... | collective-permute-start | bytes 786440 | tf_op jit(solution)/shard_map/ppermute | solution.py:431
  42.1 1.1 %collective-permute-start.15 = (bf16[16,64,128]{2,1,0:T(8,128)(2,1)S(1)}, bf16[16,64,128]{2,1,0:T(8,128)(2,1)S(1)}, u32[]{:S(2)}, u32[]{:S(2)}) collective-permute-start(bf16[16,64,128]{2,1,0:T(8,128)(2,1)S(1)} %get-tuple-element.48), channel_id=1, source_target_pairs={{0,4},{1,3},{4,8},{5,1},{8,12},{9,5},{12,14},{13,9},{14,10},{15,13... | collective-permute-start | bytes 786440 | tf_op jit(solution)/shard_map/ppermute | solution.py:431
  43.2 3.4 %collective-permute-done.12 = bf16[16,64,128]{2,1,0:T(8,128)(2,1)S(1)} collective-permute-done((bf16[16,64,128]{2,1,0:T(8,128)(2,1)S(1)}, bf16[16,64,128]{2,1,0:T(8,128)(2,1)S(1)}, u32[]{:S(2)}, u32[]{:S(2)}) %collective-permute-start.12) | collective-permute-done | bytes 262176 | tf_op jit(solution)/shard_map/ppermute | solution.py:431
  46.7 2.0 %collective-permute-start.14 = (bf16[16,64,128]{2,1,0:T(8,128)(2,1)S(1)}, bf16[16,64,128]{2,1,0:T(8,128)(2,1)S(1)}, u32[]{:S(2)}, u32[]{:S(2)}) collective-permute-start(bf16[16,64,128]{2,1,0:T(8,128)(2,1)S(1)} %add_convert_fusion.5), channel_id=1, source_target_pairs={{0,4},{1,3},{4,8},{5,1},{8,12},{9,5},{12,14},{13,9},{14,10},{15,13... | collective-permute-start | bytes 786440 | tf_op jit(solution)/shard_map/ppermute | solution.py:431
  49.5 2.0 %collective-permute-start.17 = (bf16[16,64,128]{2,1,0:T(8,128)(2,1)S(1)}, bf16[16,64,128]{2,1,0:T(8,128)(2,1)S(1)}, u32[]{:S(2)}, u32[]{:S(2)}) collective-permute-start(bf16[16,64,128]{2,1,0:T(8,128)(2,1)S(1)} %add_convert_fusion.4), channel_id=1, source_target_pairs={{0,4},{1,3},{4,8},{5,1},{8,12},{9,5},{12,14},{13,9},{14,10},{15,13... | collective-permute-start | bytes 786440 | tf_op jit(solution)/shard_map/ppermute | solution.py:431
  51.5 1.6 %collective-permute-done.14 = bf16[16,64,128]{2,1,0:T(8,128)(2,1)S(1)} collective-permute-done((bf16[16,64,128]{2,1,0:T(8,128)(2,1)S(1)}, bf16[16,64,128]{2,1,0:T(8,128)(2,1)S(1)}, u32[]{:S(2)}, u32[]{:S(2)}) %collective-permute-start.14) | collective-permute-done | bytes 262176 | tf_op jit(solution)/shard_map/ppermute | solution.py:431
  53.2 2.0 %collective-permute-start.16 = (bf16[16,64,128]{2,1,0:T(8,128)(2,1)S(1)}, bf16[16,64,128]{2,1,0:T(8,128)(2,1)S(1)}, u32[]{:S(2)}, u32[]{:S(2)}) collective-permute-start(bf16[16,64,128]{2,1,0:T(8,128)(2,1)S(1)} %add_convert_fusion.3), channel_id=1, source_target_pairs={{0,4},{1,3},{4,8},{5,1},{8,12},{9,5},{12,14},{13,9},{14,10},{15,13... | collective-permute-start | bytes 786440 | tf_op jit(solution)/shard_map/ppermute | solution.py:431
  56.0 2.0 %collective-permute-start.19 = (bf16[16,64,128]{2,1,0:T(8,128)(2,1)S(1)}, bf16[16,64,128]{2,1,0:T(8,128)(2,1)S(1)}, u32[]{:S(2)}, u32[]{:S(2)}) collective-permute-start(bf16[16,64,128]{2,1,0:T(8,128)(2,1)S(1)} %add_convert_fusion.2), channel_id=1, source_target_pairs={{0,4},{1,3},{4,8},{5,1},{8,12},{9,5},{12,14},{13,9},{14,10},{15,13... | collective-permute-start | bytes 786440 | tf_op jit(solution)/shard_map/ppermute | solution.py:431
  58.0 1.6 %collective-permute-done.16 = bf16[16,64,128]{2,1,0:T(8,128)(2,1)S(1)} collective-permute-done((bf16[16,64,128]{2,1,0:T(8,128)(2,1)S(1)}, bf16[16,64,128]{2,1,0:T(8,128)(2,1)S(1)}, u32[]{:S(2)}, u32[]{:S(2)}) %collective-permute-start.16) | collective-permute-done | bytes 262176 | tf_op jit(solution)/shard_map/ppermute | solution.py:431
  59.7 2.0 %collective-permute-start.18 = (bf16[16,64,128]{2,1,0:T(8,128)(2,1)S(1)}, bf16[16,64,128]{2,1,0:T(8,128)(2,1)S(1)}, u32[]{:S(2)}, u32[]{:S(2)}) collective-permute-start(bf16[16,64,128]{2,1,0:T(8,128)(2,1)S(1)} %add_convert_fusion.1), channel_id=1, source_target_pairs={{0,4},{1,3},{4,8},{5,1},{8,12},{9,5},{12,14},{13,9},{14,10},{15,13... | collective-permute-start | bytes 786440 | tf_op jit(solution)/shard_map/ppermute | solution.py:431
  62.5 2.5 %far.1 = f32[16,64,128]{2,1,0:T(8,128)S(1)} custom-call(bf16[1024,128]{1,0:T(8,128)(2,1)S(1)} %get-tuple-element.43.refs_0_, bf16[1024,128]{1,0:T(8,128)(2,1)S(1)} %collective-permute-done.10.refs_1_, s32[1]{0:T(128)} %bitcast.me_ref.refs_2_, bf16[16,16,256]{2,1,0:T(8,128)(2,1)S(1)} %bitcast.10, s32[1,256]{1,0:T(1,128)S(1)} %bitcast.11, ...), custom_call_target="tpu_custom_call" | custom-call | flops 536870912 | bytes 8388608 | tf_op jit(solution)/shard_map/far/pallas_call | solution.py:518
  65.0 1.2 %collective-permute-done.18 = bf16[16,64,128]{2,1,0:T(8,128)(2,1)S(1)} collective-permute-done((bf16[16,64,128]{2,1,0:T(8,128)(2,1)S(1)}, bf16[16,64,128]{2,1,0:T(8,128)(2,1)S(1)}, u32[]{:S(2)}, u32[]{:S(2)}) %collective-permute-start.18) | collective-permute-done | bytes 262176 | tf_op jit(solution)/shard_map/ppermute | solution.py:431
  66.3 0.8 %add_convert_fusion = bf16[16,64,128]{2,1,0:T(8,128)(2,1)} fusion(f32[16,64,128]{2,1,0:T(8,128)S(1)} %convert_add_fusion, bf16[16,64,128]{2,1,0:T(8,128)(2,1)S(1)} %collective-permute-done.20), kind=kLoop, calls=%fused_computation | loop fusion | flops 393216 | bytes 1048576 | tf_op jit(solution)/shard_map/convert_element_type | solution.py:570
  (38 shorter events, 4.6 us)
Async XLA Ops:
  0.0 18.2 %collective-permute-start.2 = (bf16[128,128,128]{2,1,0:T(8,128)(2,1)}, bf16[128,128,128]{2,1,0:T(8,128)(2,1)}, u32[]{:S(2)}, u32[]{:S(2)}) collective-permute-start(bf16[128,128,128]{2,1,0:T(8,128)(2,1)} %refs_8_.1), channel_id=1, source_target_pairs={{0,1},{1,0},{2,3},{3,2},{4,5},{5,4},{6,7},{7,6},{8,9},{9,8},{10,11... | collective-permute-start | bytes 12582920 | tf_op jit(solution)/shard_map/ppermute | solution.py:431
  2.6 8.2 %collective-permute-start = (bf16[1152,128]{1,0:T(8,128)(2,1)}, bf16[1152,128]{1,0:T(8,128)(2,1)S(1)}, u32[]{:S(2)}, u32[]{:S(2)}) collective-permute-start(bf16[1152,128]{1,0:T(8,128)(2,1)} %get-tuple-element.36), channel_id=1, source_target_pairs={{0,4},{1,3},{4,8},{5,1},{8,12},{9,5},{12,14},{13,9},{14,10},{15,13... | collective-permute-start | bytes 884744 | tf_op jit(solution)/shard_map/ppermute | solution.py:431
  6.1 7.1 %collective-permute-start.6 = (bf16[1152,128]{1,0:T(8,128)(2,1)}, bf16[1152,128]{1,0:T(8,128)(2,1)S(1)}, u32[]{:S(2)}, u32[]{:S(2)}) collective-permute-start(bf16[1152,128]{1,0:T(8,128)(2,1)} %get-tuple-element.36), channel_id=1, source_target_pairs={{0,3},{1,4},{4,1},{5,8},{8,5},{9,12},{12,9},{13,14},{14,13},{15,10... | collective-permute-start | bytes 884744 | tf_op jit(solution)/shard_map/ppermute | solution.py:431
  7.5 9.1 %collective-permute-start.3 = (bf16[1152,128]{1,0:T(8,128)(2,1)}, bf16[1152,128]{1,0:T(8,128)(2,1)S(1)}, u32[]{:S(2)}, u32[]{:S(2)}) collective-permute-start(bf16[1152,128]{1,0:T(8,128)(2,1)} %get-tuple-element.36), channel_id=1, source_target_pairs={{0,1},{1,0},{2,3},{3,2},{4,5},{5,4},{6,7},{7,6},{8,9},{9,8},{10,11... | collective-permute-start | bytes 884744 | tf_op jit(solution)/shard_map/ppermute | solution.py:431
  10.8 7.4 %collective-permute-start.1 = (bf16[1152,128]{1,0:T(8,128)(2,1)S(1)}, bf16[1152,128]{1,0:T(8,128)(2,1)S(1)}, u32[]{:S(2)}, u32[]{:S(2)}) collective-permute-start(bf16[1152,128]{1,0:T(8,128)(2,1)S(1)} %collective-permute-done.refs_1_), channel_id=1, source_target_pairs={{0,4},{1,3},{4,8},{5,1},{8,12},{9,5},{12,14},{13,9},{14,10},{15,13... | collective-permute-start | bytes 884744 | tf_op jit(solution)/shard_map/ppermute | solution.py:431
  13.2 8.1 %collective-permute-start.7 = (bf16[1152,128]{1,0:T(8,128)(2,1)S(1)}, bf16[1152,128]{1,0:T(8,128)(2,1)S(1)}, u32[]{:S(2)}, u32[]{:S(2)}) collective-permute-start(bf16[1152,128]{1,0:T(8,128)(2,1)S(1)} %collective-permute-done.6.refs_2_), channel_id=1, source_target_pairs={{0,4},{1,3},{4,8},{5,1},{8,12},{9,5},{12,14},{13,9},{14,10},{15,13... | collective-permute-start | bytes 884744 | tf_op jit(solution)/shard_map/ppermute | solution.py:431
  15.3 1.4 %collective-permute-start.4 = (s32[8,128]{1,0:T(8,128)}, s32[8,128]{1,0:T(8,128)S(1)}, u32[]{:S(2)}, u32[]{:S(2)}) collective-permute-start(s32[8,128]{1,0:T(8,128)} %get-tuple-element.37.first_ref), channel_id=1, source_target_pairs={{0,1},{1,0},{2,3},{3,2},{4,5},{5,4},{6,7},{7,6},{8,9},{9,8},{10,11... | collective-permute-start | bytes 12296 | tf_op jit(solution)/shard_map/ppermute | solution.py:431
  16.6 6.4 %copy-start.6 = (s32[8,128]{1,0:T(8,128)}, s32[8,128]{1,0:T(8,128)S(1)}, u32[]{:S(2)}) copy-start(s32[8,128]{1,0:T(8,128)S(1)} %collective-permute-done.4.second_ref) | copy-start | bytes 12292
  18.2 6.7 %collective-permute-start.5 = (bf16[1152,128]{1,0:T(8,128)(2,1)S(1)}, bf16[1152,128]{1,0:T(8,128)(2,1)S(1)}, u32[]{:S(2)}, u32[]{:S(2)}) collective-permute-start(bf16[1152,128]{1,0:T(8,128)(2,1)S(1)} %collective-permute-done.1.refs_3_), channel_id=1, source_target_pairs={{0,4},{1,3},{4,8},{5,1},{8,12},{9,5},{12,14},{13,9},{14,10},{15,13... | collective-permute-start | bytes 884744 | tf_op jit(solution)/shard_map/ppermute | solution.py:431
  21.3 13.2 %collective-permute-start.8 = (bf16[1152,128]{1,0:T(8,128)(2,1)S(1)}, bf16[1152,128]{1,0:T(8,128)(2,1)S(1)}, u32[]{:S(2)}, u32[]{:S(2)}) collective-permute-start(bf16[1152,128]{1,0:T(8,128)(2,1)S(1)} %collective-permute-done.7.refs_4_), channel_id=1, source_target_pairs={{0,4},{1,3},{4,8},{5,1},{8,12},{9,5},{12,14},{13,9},{14,10},{15,13... | collective-permute-start | bytes 884744 | tf_op jit(solution)/shard_map/ppermute | solution.py:431
  24.9 9.6 %collective-permute-start.9 = (bf16[1152,128]{1,0:T(8,128)(2,1)S(1)}, bf16[1152,128]{1,0:T(8,128)(2,1)S(1)}, u32[]{:S(2)}, u32[]{:S(2)}) collective-permute-start(bf16[1152,128]{1,0:T(8,128)(2,1)S(1)} %collective-permute-done.5.refs_5_), channel_id=1, source_target_pairs={{0,4},{1,3},{4,8},{5,1},{8,12},{9,5},{12,14},{13,9},{14,10},{15,13... | collective-permute-start | bytes 884744 | tf_op jit(solution)/shard_map/ppermute | solution.py:431
  26.6 2.2 %copy-start = (bf16[128,128,128]{2,1,0:T(8,128)(2,1)S(1)}, bf16[128,128,128]{2,1,0:T(8,128)(2,1)}, u32[]{:S(2)}) copy-start(bf16[128,128,128]{2,1,0:T(8,128)(2,1)} %refs_8_.1) | copy-start | bytes 12582916
  28.8 0.7 %copy-start.1 = (s32[16,128]{1,0:T(8,128)S(1)}, s32[16,128]{1,0:T(8,128)}, u32[]{:S(2)}) copy-start(s32[16,128]{1,0:T(8,128)} %join.1.list_ref) | copy-start | bytes 24580
  37.8 2.0 %collective-permute-start.11 = (bf16[32,64,128]{2,1,0:T(8,128)(2,1)S(1)}, bf16[32,64,128]{2,1,0:T(8,128)(2,1)S(1)}, u32[]{:S(2)}, u32[]{:S(2)}) collective-permute-start(bf16[32,64,128]{2,1,0:T(8,128)(2,1)S(1)} %get-tuple-element.45), channel_id=1, source_target_pairs={{0,1},{1,0},{2,3},{3,2},{4,5},{5,4},{6,7},{7,6},{8,9},{9,8},{10,11... | collective-permute-start | bytes 1572872 | tf_op jit(solution)/shard_map/ppermute | solution.py:431
  39.8 22.7 %copy-start.2 = (bf16[16,16,128]{2,1,0:T(8,128)(2,1)S(1)}, bf16[16,16,128]{2,1,0:T(8,128)(2,1)}, u32[]{:S(2)}) copy-start(bf16[16,16,128]{2,1,0:T(8,128)(2,1)} %refs_7_.1) | copy-start | bytes 196612
  39.8 22.7 %copy-start.3 = (s32[256]{0:T(256)S(1)}, s32[256]{0:T(256)}, u32[]{:S(2)}) copy-start(s32[256]{0:T(256)} %param.17) | copy-start | bytes 3076
  39.8 22.7 %copy-start.4 = (s32[256,1]{0,1:T(1,128)S(1)}, s32[256,1]{0,1:T(1,128)}, u32[]{:S(2)}) copy-start(s32[256,1]{0,1:T(1,128)} %param.18) | copy-start | bytes 3076
  39.8 22.7 %copy-start.5 = (s32[256]{0:T(256)S(1)}, s32[256]{0:T(256)}, u32[]{:S(2)}) copy-start(s32[256]{0:T(256)} %param.19) | copy-start | bytes 3076
  40.0 6.6 %collective-permute-start.13 = (bf16[96,64,128]{2,1,0:T(8,128)(2,1)S(1)}, bf16[96,64,128]{2,1,0:T(8,128)(2,1)S(1)}, u32[]{:S(2)}, u32[]{:S(2)}) collective-permute-start(bf16[96,64,128]{2,1,0:T(8,128)(2,1)S(1)} %get-tuple-element.49), channel_id=1, source_target_pairs={{0,1},{1,0},{2,3},{3,2},{4,5},{5,4},{6,7},{7,6},{8,9},{9,8},{10,11... | collective-permute-start | bytes 4718600 | tf_op jit(solution)/shard_map/ppermute | solution.py:431
  40.2 6.4 %collective-permute-start.12 = (bf16[16,64,128]{2,1,0:T(8,128)(2,1)S(1)}, bf16[16,64,128]{2,1,0:T(8,128)(2,1)S(1)}, u32[]{:S(2)}, u32[]{:S(2)}) collective-permute-start(bf16[16,64,128]{2,1,0:T(8,128)(2,1)S(1)} %get-tuple-element.46), channel_id=1, source_target_pairs={{0,4},{1,3},{4,8},{5,1},{8,12},{9,5},{12,14},{13,9},{14,10},{15,13... | collective-permute-start | bytes 786440 | tf_op jit(solution)/shard_map/ppermute | solution.py:431
  42.1 7.2 %collective-permute-start.15 = (bf16[16,64,128]{2,1,0:T(8,128)(2,1)S(1)}, bf16[16,64,128]{2,1,0:T(8,128)(2,1)S(1)}, u32[]{:S(2)}, u32[]{:S(2)}) collective-permute-start(bf16[16,64,128]{2,1,0:T(8,128)(2,1)S(1)} %get-tuple-element.48), channel_id=1, source_target_pairs={{0,4},{1,3},{4,8},{5,1},{8,12},{9,5},{12,14},{13,9},{14,10},{15,13... | collective-permute-start | bytes 786440 | tf_op jit(solution)/shard_map/ppermute | solution.py:431
  46.7 6.4 %collective-permute-start.14 = (bf16[16,64,128]{2,1,0:T(8,128)(2,1)S(1)}, bf16[16,64,128]{2,1,0:T(8,128)(2,1)S(1)}, u32[]{:S(2)}, u32[]{:S(2)}) collective-permute-start(bf16[16,64,128]{2,1,0:T(8,128)(2,1)S(1)} %add_convert_fusion.5), channel_id=1, source_target_pairs={{0,4},{1,3},{4,8},{5,1},{8,12},{9,5},{12,14},{13,9},{14,10},{15,13... | collective-permute-start | bytes 786440 | tf_op jit(solution)/shard_map/ppermute | solution.py:431
  49.5 6.4 %collective-permute-start.17 = (bf16[16,64,128]{2,1,0:T(8,128)(2,1)S(1)}, bf16[16,64,128]{2,1,0:T(8,128)(2,1)S(1)}, u32[]{:S(2)}, u32[]{:S(2)}) collective-permute-start(bf16[16,64,128]{2,1,0:T(8,128)(2,1)S(1)} %add_convert_fusion.4), channel_id=1, source_target_pairs={{0,4},{1,3},{4,8},{5,1},{8,12},{9,5},{12,14},{13,9},{14,10},{15,13... | collective-permute-start | bytes 786440 | tf_op jit(solution)/shard_map/ppermute | solution.py:431
  53.2 6.4 %collective-permute-start.16 = (bf16[16,64,128]{2,1,0:T(8,128)(2,1)S(1)}, bf16[16,64,128]{2,1,0:T(8,128)(2,1)S(1)}, u32[]{:S(2)}, u32[]{:S(2)}) collective-permute-start(bf16[16,64,128]{2,1,0:T(8,128)(2,1)S(1)} %add_convert_fusion.3), channel_id=1, source_target_pairs={{0,4},{1,3},{4,8},{5,1},{8,12},{9,5},{12,14},{13,9},{14,10},{15,13... | collective-permute-start | bytes 786440 | tf_op jit(solution)/shard_map/ppermute | solution.py:431
  55.2 7.2 %collective-permute-start.10 = (bf16[1024,128]{1,0:T(8,128)(2,1)S(1)}, bf16[1024,128]{1,0:T(8,128)(2,1)S(1)}, u32[]{:S(2)}, u32[]{:S(2)}) collective-permute-start(bf16[1024,128]{1,0:T(8,128)(2,1)S(1)} %get-tuple-element.43.refs_0_), channel_id=1, source_target_pairs={{0,1},{1,0},{2,3},{3,2},{4,5},{5,4},{6,7},{7,6},{8,9},{9,8},{10,11... | collective-permute-start | bytes 786440 | tf_op jit(solution)/shard_map/ppermute | solution.py:431
  56.0 6.4 %collective-permute-start.19 = (bf16[16,64,128]{2,1,0:T(8,128)(2,1)S(1)}, bf16[16,64,128]{2,1,0:T(8,128)(2,1)S(1)}, u32[]{:S(2)}, u32[]{:S(2)}) collective-permute-start(bf16[16,64,128]{2,1,0:T(8,128)(2,1)S(1)} %add_convert_fusion.2), channel_id=1, source_target_pairs={{0,4},{1,3},{4,8},{5,1},{8,12},{9,5},{12,14},{13,9},{14,10},{15,13... | collective-permute-start | bytes 786440 | tf_op jit(solution)/shard_map/ppermute | solution.py:431
  59.7 6.4 %collective-permute-start.18 = (bf16[16,64,128]{2,1,0:T(8,128)(2,1)S(1)}, bf16[16,64,128]{2,1,0:T(8,128)(2,1)S(1)}, u32[]{:S(2)}, u32[]{:S(2)}) collective-permute-start(bf16[16,64,128]{2,1,0:T(8,128)(2,1)S(1)} %add_convert_fusion.1), channel_id=1, source_target_pairs={{0,4},{1,3},{4,8},{5,1},{8,12},{9,5},{12,14},{13,9},{14,10},{15,13... | collective-permute-start | bytes 786440 | tf_op jit(solution)/shard_map/ppermute | solution.py:431
  62.4 3.9 %collective-permute-start.20 = (bf16[16,64,128]{2,1,0:T(8,128)(2,1)S(1)}, bf16[16,64,128]{2,1,0:T(8,128)(2,1)S(1)}, u32[]{:S(2)}, u32[]{:S(2)}) collective-permute-start(bf16[16,64,128]{2,1,0:T(8,128)(2,1)S(1)} %collective-permute-done.19), channel_id=1, source_target_pairs={{0,1},{1,0},{2,3},{3,2},{4,5},{5,4},{6,7},{7,6},{8,9},{9,8},{10,11... | collective-permute-start | bytes 786440 | tf_op jit(solution)/shard_map/ppermute | solution.py:431

commit v22 on v21

--- a/solution.py
+++ b/solution.py
@@ -178,16 +178,19 @@
     list_ref[...] = values.astype(jnp.int32)
 
 
-def join_kernel(first_ref, second_ref, out_ref):
-    rows = first_ref.shape[0]
-    out_ref[0:rows] = first_ref[...]
-    out_ref[rows:] = second_ref[...]
+def open_kernel(token_ref, sums):
+    def clear(i, carry):
+        sums[i] = jnp.zeros(sums.shape[1:], sums.dtype)
+        return carry
+
+    lax.fori_loop(0, sums.shape[0] - 1, clear, 0, unroll=8)
+    clear(sums.shape[0] - 1, 0)
 
 
 def near_kernel(late, batch, shards, sends, list_ref, *refs):
     used = LATE if late else shards
     shard_refs, refs = refs[:shards], refs[shards:]
-    (own_ref, mate_hbm), refs = refs[:2], refs[2 + late :]
+    (own_ref, mate_hbm), refs = refs[:2], refs[3:]
     sums, refs = refs[0], refs[1:]
     if late:
         coef_ref, send_refs, refs = refs[0], refs[1 : 1 + sends], refs[1 + sends :]
@@ -230,15 +233,6 @@
         tail = coef_ref.shape[0] // shards
         for k, ref in enumerate(shard_refs):
             coef_ref[k * tail : (k + 1) * tail] = ref[span : span + tail]
-    else:
-
-        def clear(i, carry):
-            sums[i] = jnp.zeros(sums.shape[1:], sums.dtype)
-            return carry
-
-        lax.fori_loop(0, dummy, clear, 0, unroll=8)
-        clear(dummy, 0)
-
     def run(begin, end, row, swap, block_of):
         def entry(j):
             return jnp.minimum(begin + j, end - 1)
@@ -471,14 +465,7 @@
                 (flow[x], mate_blocks, shards[0], mate_lists)
             )
         if k == 4:
-            lists = pl.pallas_call(
-                join_kernel,
-                out_shape=jax.ShapeDtypeStruct((16, stored), jnp.int32),
-                in_specs=[whole()] * 2,
-                out_specs=whole(),
-                cost_estimate=cost,
-                name="join",
-            )(after(lists, flow[x]), mate_lists)
+            lists = jnp.concatenate([after(lists, flow[x]), mate_lists], axis=0)
         if k == 5:
             flow[x], lists = lax.optimization_barrier((flow[x], lists))
         shards.append(flow[x])
@@ -488,7 +475,7 @@
     pieces = [2, chips - 2]
     sums_shape = jax.ShapeDtypeStruct((count * clusters + 1, directions, unknowns), jnp.float32)
 
-    def near(late, shards, *sums):
+    def near(late, shards, sums):
         sends = pieces if late else []
         return pl.pallas_call(
             functools.partial(near_kernel, late, BATCH[late], len(shards), len(sends)),
@@ -500,10 +487,9 @@
             ],
             in_specs=[whole(pltpu.SMEM)]
             + [whole()] * len(shards)
-            + [whole(), whole(pl.ANY)]
-            + [whole()] * len(sums),
+            + [whole(), whole(pl.ANY), whole()],
             out_specs=[whole()] * (1 + late + len(sends)),
-            input_output_aliases={3 + len(shards): 0} if sums else {},
+            input_output_aliases={3 + len(shards): 0},
             scratch_shapes=[
                 pltpu.VMEM(((LATE if late else len(shards)) * base, unknowns), jnp.bfloat16),
                 pltpu.VMEM(near_blocks.shape, jnp.bfloat16),
@@ -512,7 +498,7 @@
             compiler_params=pltpu.CompilerParams(vmem_limit_bytes=NEAR_VMEM),
             cost_estimate=cost,
             name="near",
-        )(lists, *shards, near_blocks, mate_blocks, *sums)
+        )(lists, *shards, near_blocks, mate_blocks, sums)
 
     def far_field(couple):
         return pl.pallas_call(
@@ -537,7 +523,15 @@
             basis_out,
         )
 
-    (sums,) = near(0, shards[: chips - LATE])
+    sums = pl.pallas_call(
+        open_kernel,
+        out_shape=sums_shape,
+        in_specs=[whole()],
+        out_specs=whole(),
+        cost_estimate=cost,
+        name="open",
+    )(lists)
+    (sums,) = near(0, shards[: chips - LATE], sums)
     sums, coef, *sends = near(1, shards, sums)
     mates = [move(sends[0], mate)]
     coefs = [coef, move(coef, mate)]

time: 67.3 us -> 74 us (1.100)
  local copies, waits for them, and re-layouts: 3.85 us -> 6.55 us
  Pallas kernels: 14.2 us -> 16.6 us
  starting transfers between devices: 27.8 us -> 30.1 us
  waiting for transfers between devices: 19.5 us -> 17.2 us
  other arithmetic: 1.64 us -> 2.91 us
    pallas_call x1, Pallas kernels: 1.29 us -> 4.56 us  [stationary(): pl.pallas_call(open_kernel, out_shape=sums_shape, in_specs=[whole()], out...]
    unnamed x15, local copies, waits for them, and re-layouts: 3.85 us -> 6.55 us
    ppermute x21, starting transfers between devices: 27.8 us -> 30.1 us  [move(): return lax.ppermute(values, 'blk', where)]
    ppermute x21, waiting for transfers between devices: 19.5 us -> 17.2 us  [move(): return lax.ppermute(values, 'blk', where)]
    concatenate x0 -> x1, other arithmetic: none -> 1.27 us  [stationary(): lists = jnp.concatenate([after(lists, flow[x]), mate_lists], axis=0)]
    pallas_call x2, Pallas kernels: 8.26 us -> 7.45 us  [near(): pl.pallas_call(functools.partial(near_kernel, late, BATCH[late], len(shar...]
  transfers between devices with their start and end apart: 21 -> 21, of which waited for: 13 -> 13; matrix products, arithmetic and copies ran while one was open for 2% -> 4% of each run, Pallas kernels for 16% -> 19%
where the time goes in v22:
time: 74 us; the launch traced here: 73.6 us
  starting transfers between devices  30.1 us (41%)
  waiting for transfers between devices  17.2 us (23%)
  Pallas kernels  16.6 us (22%)
  local copies, waits for them, and re-layouts  6.55 us (9%)
  other arithmetic  2.91 us (4%)
    ppermute x21, starting transfers between devices, move(): return lax.ppermute(values, 'blk', where)  30.1 us
    ppermute x21, waiting for transfers between devices, move(): return lax.ppermute(values, 'blk', where)  17.2 us
    pallas_call x2, Pallas kernels, near(): pl.pallas_call(functools.partial(near_kernel, late, BATCH[late], len(shar...  7.45 us
    unnamed x15, local copies, waits for them, and re-layouts  6.55 us
    pallas_call x1, Pallas kernels, stationary(): pl.pallas_call(open_kernel, out_shape=sums_shape, in_specs=[whole()], out...  4.56 us
    pallas_call x1, Pallas kernels, far_field(): pl.pallas_call(far_kernel, out_shape=jax.ShapeDtypeStruct((clusters, dire...  2.51 us
    pallas_call x1, Pallas kernels, stationary(): pl.pallas_call(functools.partial(prologue_kernel, count), out_shape=[jax....  2.13 us
  transfers between devices with their start and end apart: 21, of which 13 were waited for; matrix products, arithmetic and copies ran while one was open for 4% of the time, Pallas kernels for 19%

profile of v22, /device:TPU:0, one launch (start us, length us, event | category | flops | bytes accessed | tf_op | source)
XLA Modules:
  0.0 73.6 jit_solution(749256126814881992)
XLA Ops:
  0.5 2.1 %prologue.1 = (bf16[1152,128]{1,0:T(8,128)(2,1)}, s32[8,128]{1,0:T(8,128)}) custom-call(s32[1]{0:T(128)} %bitcast.me_ref.refs_2_, s32[1,128]{1,0:T(1,128)} %bitcast.14, s32[1,128]{1,0:T(1,128)} %bitcast.15, s32[1,128]{1,0:T(1,128)} %bitcast.16, bf16[16,64,128]{2,1,0:T(8,128)(2,1)} %rhs_ref.1, bf16[16,16,128]{2,1,0:T(8,128)(2,1)} %basis_ref.1), custom_call_target="tpu_custom_call" | custom-call | tf_op jit(solution)/shard_map/prologue/pallas_call | solution.py:432
  2.6 2.6 %collective-permute-start = (bf16[1152,128]{1,0:T(8,128)(2,1)}, bf16[1152,128]{1,0:T(8,128)(2,1)S(1)}, u32[]{:S(2)}, u32[]{:S(2)}) collective-permute-start(bf16[1152,128]{1,0:T(8,128)(2,1)} %get-tuple-element.36), channel_id=1, source_target_pairs={{0,4},{1,3},{4,8},{5,1},{8,12},{9,5},{12,14},{13,9},{14,10},{15,13... | collective-permute-start | bytes 884744 | tf_op jit(solution)/shard_map/ppermute | solution.py:425
  5.2 0.9 %copy.16 = bf16[256,16,16]{0,1,2:T(8,128)(2,1)S(1)} copy(bf16[256,16,16]{0,2,1:T(8,128)(2,1)} %param.16) | data formatting | bytes 262144 | tf_op args[5]
  6.1 1.4 %collective-permute-start.6 = (bf16[1152,128]{1,0:T(8,128)(2,1)}, bf16[1152,128]{1,0:T(8,128)(2,1)S(1)}, u32[]{:S(2)}, u32[]{:S(2)}) collective-permute-start(bf16[1152,128]{1,0:T(8,128)(2,1)} %get-tuple-element.36), channel_id=1, source_target_pairs={{0,3},{1,4},{4,1},{5,8},{8,5},{9,12},{12,9},{13,14},{14,13},{15,10... | collective-permute-start | bytes 884744 | tf_op jit(solution)/shard_map/ppermute | solution.py:425
  7.9 2.9 %collective-permute-done.refs_1_ = bf16[1152,128]{1,0:T(8,128)(2,1)S(1)} collective-permute-done((bf16[1152,128]{1,0:T(8,128)(2,1)}, bf16[1152,128]{1,0:T(8,128)(2,1)S(1)}, u32[]{:S(2)}, u32[]{:S(2)}) %collective-permute-start) | collective-permute-done | bytes 294944 | tf_op jit(solution)/shard_map/ppermute | solution.py:425
  10.8 2.4 %collective-permute-start.1 = (bf16[1152,128]{1,0:T(8,128)(2,1)S(1)}, bf16[1152,128]{1,0:T(8,128)(2,1)S(1)}, u32[]{:S(2)}, u32[]{:S(2)}) collective-permute-start(bf16[1152,128]{1,0:T(8,128)(2,1)S(1)} %collective-permute-done.refs_1_), channel_id=1, source_target_pairs={{0,4},{1,3},{4,8},{5,1},{8,12},{9,5},{12,14},{13,9},{14,10},{15,13... | collective-permute-start | bytes 884744 | tf_op jit(solution)/shard_map/ppermute | solution.py:425
  13.2 2.1 %collective-permute-start.7 = (bf16[1152,128]{1,0:T(8,128)(2,1)S(1)}, bf16[1152,128]{1,0:T(8,128)(2,1)S(1)}, u32[]{:S(2)}, u32[]{:S(2)}) collective-permute-start(bf16[1152,128]{1,0:T(8,128)(2,1)S(1)} %collective-permute-done.6.refs_2_), channel_id=1, source_target_pairs={{0,4},{1,3},{4,8},{5,1},{8,12},{9,5},{12,14},{13,9},{14,10},{15,13... | collective-permute-start | bytes 884744 | tf_op jit(solution)/shard_map/ppermute | solution.py:425
  15.3 1.4 %collective-permute-done.4 = s32[8,128]{1,0:T(8,128)S(1)} collective-permute-done((s32[8,128]{1,0:T(8,128)}, s32[8,128]{1,0:T(8,128)S(1)}, u32[]{:S(2)}, u32[]{:S(2)}) %collective-permute-start.4) | collective-permute-done | bytes 4128 | tf_op jit(solution)/shard_map/ppermute | solution.py:425
  16.6 1.5 %collective-permute-done.1.refs_3_ = bf16[1152,128]{1,0:T(8,128)(2,1)S(1)} collective-permute-done((bf16[1152,128]{1,0:T(8,128)(2,1)S(1)}, bf16[1152,128]{1,0:T(8,128)(2,1)S(1)}, u32[]{:S(2)}, u32[]{:S(2)}) %collective-permute-start.1) | collective-permute-done | bytes 294944 | tf_op jit(solution)/shard_map/ppermute | solution.py:425
  18.1 1.7 %collective-permute-start.5 = (bf16[1152,128]{1,0:T(8,128)(2,1)S(1)}, bf16[1152,128]{1,0:T(8,128)(2,1)S(1)}, u32[]{:S(2)}, u32[]{:S(2)}) collective-permute-start(bf16[1152,128]{1,0:T(8,128)(2,1)S(1)} %collective-permute-done.1.refs_3_), channel_id=1, source_target_pairs={{0,4},{1,3},{4,8},{5,1},{8,12},{9,5},{12,14},{13,9},{14,10},{15,13... | collective-permute-start | bytes 884744 | tf_op jit(solution)/shard_map/ppermute | solution.py:425
  19.9 1.4 %collective-permute-done.7.refs_4_ = bf16[1152,128]{1,0:T(8,128)(2,1)S(1)} collective-permute-done((bf16[1152,128]{1,0:T(8,128)(2,1)S(1)}, bf16[1152,128]{1,0:T(8,128)(2,1)S(1)}, u32[]{:S(2)}, u32[]{:S(2)}) %collective-permute-start.7) | collective-permute-done | bytes 294944 | tf_op jit(solution)/shard_map/ppermute | solution.py:425
  21.3 1.7 %collective-permute-start.8 = (bf16[1152,128]{1,0:T(8,128)(2,1)S(1)}, bf16[1152,128]{1,0:T(8,128)(2,1)S(1)}, u32[]{:S(2)}, u32[]{:S(2)}) collective-permute-start(bf16[1152,128]{1,0:T(8,128)(2,1)S(1)} %collective-permute-done.7.refs_4_), channel_id=1, source_target_pairs={{0,4},{1,3},{4,8},{5,1},{8,12},{9,5},{12,14},{13,9},{14,10},{15,13... | collective-permute-start | bytes 884744 | tf_op jit(solution)/shard_map/ppermute | solution.py:425
  23.1 1.3 %pad_add_fusion.token_ref.list_ref = s32[16,128]{1,0:T(8,128)} fusion(s32[8,128]{1,0:T(8,128)S(1)} %collective-permute-done.4, s32[8,128]{1,0:T(8,128)} %get-tuple-element.37), kind=kLoop, calls=%fused_computation.10 | loop fusion | flops 2048 | bytes 16384 | tf_op jit(solution)/shard_map/concatenate | solution.py:468
  24.9 1.7 %collective-permute-start.9 = (bf16[1152,128]{1,0:T(8,128)(2,1)S(1)}, bf16[1152,128]{1,0:T(8,128)(2,1)S(1)}, u32[]{:S(2)}, u32[]{:S(2)}) collective-permute-start(bf16[1152,128]{1,0:T(8,128)(2,1)S(1)} %collective-permute-done.5.refs_5_), channel_id=1, source_target_pairs={{0,4},{1,3},{4,8},{5,1},{8,12},{9,5},{12,14},{13,9},{14,10},{15,13... | collective-permute-start | bytes 884744 | tf_op jit(solution)/shard_map/ppermute | solution.py:425
  26.6 4.6 %open.1.refs_8_ = f32[257,64,128]{2,1,0:T(8,128)} custom-call(s32[16,128]{1,0:T(8,128)} %pad_add_fusion.token_ref.list_ref), custom_call_target="tpu_custom_call" | custom-call | flops 2147483648 | bytes 16777216 | tf_op jit(solution)/shard_map/open/pallas_call | solution.py:526
  31.2 3.4 %copy-done = f32[257,64,128]{2,1,0:T(8,128)S(1)} copy-done((f32[257,64,128]{2,1,0:T(8,128)S(1)}, f32[257,64,128]{2,1,0:T(8,128)}, u32[]{:S(2)}) %copy-start) | copy-done | bytes 8421400
  34.6 2.2 %copy-done.1 = bf16[128,128,128]{2,1,0:T(8,128)(2,1)S(1)} copy-done((bf16[128,128,128]{2,1,0:T(8,128)(2,1)S(1)}, bf16[128,128,128]{2,1,0:T(8,128)(2,1)}, u32[]{:S(2)}) %copy-start.1) | copy-done | bytes 4194328
  36.8 4.9 %near.2.refs_10_ = f32[257,64,128]{2,1,0:T(8,128)S(1)} custom-call(s32[16,128]{1,0:T(8,128)S(1)} %copy-done.2, bf16[1152,128]{1,0:T(8,128)(2,1)S(1)} %collective-permute-done.3.refs_0_, bf16[1152,128]{1,0:T(8,128)(2,1)S(1)} %collective-permute-done.refs_1_, bf16[1152,128]{1,0:T(8,128)(2,1)S(1)} %collective-permute-done.6.refs_2_, ...), custom_call_target="tpu_custom_call", output_to_operand_aliasing={{}: (9, {})} | custom-call | flops 2147483648 | bytes 16777216 | tf_op jit(solution)/shard_map/near/pallas_call | solution.py:480
  41.6 2.6 %near.3 = (f32[257,64,128]{2,1,0:T(8,128)S(1)}, bf16[1024,128]{1,0:T(8,128)(2,1)S(1)}, bf16[32,64,128]{2,1,0:T(8,128)(2,1)S(1)}, bf16[96,64,128]{2,1,0:T(8,128)(2,1)S(1)}) custom-call(s32[16,128]{1,0:T(8,128)S(1)} %copy-done.2, bf16[1152,128]{1,0:T(8,128)(2,1)S(1)} %collective-permute-done.3.refs_0_, ...), custom_call_target="tpu_custom_call", output_to_operand_aliasing={{0}: (11, {})} | custom-call | flops 2147483648 | bytes 16777216 | tf_op jit(solution)/shard_map/near/pallas_call | solution.py:480
  44.4 1.9 %collective-permute-done.11 = bf16[32,64,128]{2,1,0:T(8,128)(2,1)S(1)} collective-permute-done((bf16[32,64,128]{2,1,0:T(8,128)(2,1)S(1)}, bf16[32,64,128]{2,1,0:T(8,128)(2,1)S(1)}, u32[]{:S(2)}, u32[]{:S(2)}) %collective-permute-start.11) | collective-permute-done | bytes 524320 | tf_op jit(solution)/shard_map/ppermute | solution.py:425
  46.6 2.3 %collective-permute-start.12 = (bf16[16,64,128]{2,1,0:T(8,128)(2,1)S(1)}, bf16[16,64,128]{2,1,0:T(8,128)(2,1)S(1)}, u32[]{:S(2)}, u32[]{:S(2)}) collective-permute-start(bf16[16,64,128]{2,1,0:T(8,128)(2,1)S(1)} %get-tuple-element.46), channel_id=1, source_target_pairs={{0,4},{1,3},{4,8},{5,1},{8,12},{9,5},{12,14},{13,9},{14,10},{15,13... | collective-permute-start | bytes 786440 | tf_op jit(solution)/shard_map/ppermute | solution.py:425
  48.9 1.5 %collective-permute-start.15 = (bf16[16,64,128]{2,1,0:T(8,128)(2,1)S(1)}, bf16[16,64,128]{2,1,0:T(8,128)(2,1)S(1)}, u32[]{:S(2)}, u32[]{:S(2)}) collective-permute-start(bf16[16,64,128]{2,1,0:T(8,128)(2,1)S(1)} %get-tuple-element.48), channel_id=1, source_target_pairs={{0,4},{1,3},{4,8},{5,1},{8,12},{9,5},{12,14},{13,9},{14,10},{15,13... | collective-permute-start | bytes 786440 | tf_op jit(solution)/shard_map/ppermute | solution.py:425
  50.4 2.6 %collective-permute-done.12 = bf16[16,64,128]{2,1,0:T(8,128)(2,1)S(1)} collective-permute-done((bf16[16,64,128]{2,1,0:T(8,128)(2,1)S(1)}, bf16[16,64,128]{2,1,0:T(8,128)(2,1)S(1)}, u32[]{:S(2)}, u32[]{:S(2)}) %collective-permute-start.12) | collective-permute-done | bytes 262176 | tf_op jit(solution)/shard_map/ppermute | solution.py:425
  53.1 2.3 %collective-permute-start.14 = (bf16[16,64,128]{2,1,0:T(8,128)(2,1)S(1)}, bf16[16,64,128]{2,1,0:T(8,128)(2,1)S(1)}, u32[]{:S(2)}, u32[]{:S(2)}) collective-permute-start(bf16[16,64,128]{2,1,0:T(8,128)(2,1)S(1)} %add_convert_fusion.5), channel_id=1, source_target_pairs={{0,4},{1,3},{4,8},{5,1},{8,12},{9,5},{12,14},{13,9},{14,10},{15,13... | collective-permute-start | bytes 786440 | tf_op jit(solution)/shard_map/ppermute | solution.py:425
  55.9 2.3 %collective-permute-start.17 = (bf16[16,64,128]{2,1,0:T(8,128)(2,1)S(1)}, bf16[16,64,128]{2,1,0:T(8,128)(2,1)S(1)}, u32[]{:S(2)}, u32[]{:S(2)}) collective-permute-start(bf16[16,64,128]{2,1,0:T(8,128)(2,1)S(1)} %add_convert_fusion.4), channel_id=1, source_target_pairs={{0,4},{1,3},{4,8},{5,1},{8,12},{9,5},{12,14},{13,9},{14,10},{15,13... | collective-permute-start | bytes 786440 | tf_op jit(solution)/shard_map/ppermute | solution.py:425
  58.2 1.3 %collective-permute-done.14 = bf16[16,64,128]{2,1,0:T(8,128)(2,1)S(1)} collective-permute-done((bf16[16,64,128]{2,1,0:T(8,128)(2,1)S(1)}, bf16[16,64,128]{2,1,0:T(8,128)(2,1)S(1)}, u32[]{:S(2)}, u32[]{:S(2)}) %collective-permute-start.14) | collective-permute-done | bytes 262176 | tf_op jit(solution)/shard_map/ppermute | solution.py:425
  59.7 2.3 %collective-permute-start.16 = (bf16[16,64,128]{2,1,0:T(8,128)(2,1)S(1)}, bf16[16,64,128]{2,1,0:T(8,128)(2,1)S(1)}, u32[]{:S(2)}, u32[]{:S(2)}) collective-permute-start(bf16[16,64,128]{2,1,0:T(8,128)(2,1)S(1)} %add_convert_fusion.3), channel_id=1, source_target_pairs={{0,4},{1,3},{4,8},{5,1},{8,12},{9,5},{12,14},{13,9},{14,10},{15,13... | collective-permute-start | bytes 786440 | tf_op jit(solution)/shard_map/ppermute | solution.py:425
  62.5 2.3 %collective-permute-start.19 = (bf16[16,64,128]{2,1,0:T(8,128)(2,1)S(1)}, bf16[16,64,128]{2,1,0:T(8,128)(2,1)S(1)}, u32[]{:S(2)}, u32[]{:S(2)}) collective-permute-start(bf16[16,64,128]{2,1,0:T(8,128)(2,1)S(1)} %add_convert_fusion.2), channel_id=1, source_target_pairs={{0,4},{1,3},{4,8},{5,1},{8,12},{9,5},{12,14},{13,9},{14,10},{15,13... | collective-permute-start | bytes 786440 | tf_op jit(solution)/shard_map/ppermute | solution.py:425
  64.8 1.3 %collective-permute-done.16 = bf16[16,64,128]{2,1,0:T(8,128)(2,1)S(1)} collective-permute-done((bf16[16,64,128]{2,1,0:T(8,128)(2,1)S(1)}, bf16[16,64,128]{2,1,0:T(8,128)(2,1)S(1)}, u32[]{:S(2)}, u32[]{:S(2)}) %collective-permute-start.16) | collective-permute-done | bytes 262176 | tf_op jit(solution)/shard_map/ppermute | solution.py:425
  66.2 2.3 %collective-permute-start.18 = (bf16[16,64,128]{2,1,0:T(8,128)(2,1)S(1)}, bf16[16,64,128]{2,1,0:T(8,128)(2,1)S(1)}, u32[]{:S(2)}, u32[]{:S(2)}) collective-permute-start(bf16[16,64,128]{2,1,0:T(8,128)(2,1)S(1)} %add_convert_fusion.1), channel_id=1, source_target_pairs={{0,4},{1,3},{4,8},{5,1},{8,12},{9,5},{12,14},{13,9},{14,10},{15,13... | collective-permute-start | bytes 786440 | tf_op jit(solution)/shard_map/ppermute | solution.py:425
  69.0 2.5 %far.1 = f32[16,64,128]{2,1,0:T(8,128)S(1)} custom-call(bf16[1024,128]{1,0:T(8,128)(2,1)S(1)} %get-tuple-element.43.refs_0_, bf16[1024,128]{1,0:T(8,128)(2,1)S(1)} %collective-permute-done.10.refs_1_, s32[1]{0:T(128)} %bitcast.me_ref.refs_2_, bf16[16,16,256]{2,1,0:T(8,128)(2,1)S(1)} %bitcast.10, s32[1,256]{1,0:T(1,128)S(1)} %bitcast.11, ...), custom_call_target="tpu_custom_call" | custom-call | flops 536870912 | bytes 8388608 | tf_op jit(solution)/shard_map/far/pallas_call | solution.py:504
  71.5 1.2 %collective-permute-done.18 = bf16[16,64,128]{2,1,0:T(8,128)(2,1)S(1)} collective-permute-done((bf16[16,64,128]{2,1,0:T(8,128)(2,1)S(1)}, bf16[16,64,128]{2,1,0:T(8,128)(2,1)S(1)}, u32[]{:S(2)}, u32[]{:S(2)}) %collective-permute-start.18) | collective-permute-done | bytes 262176 | tf_op jit(solution)/shard_map/ppermute | solution.py:425
  (39 shorter events, 4.5 us)
Async XLA Ops:
  0.0 18.1 %collective-permute-start.2 = (bf16[128,128,128]{2,1,0:T(8,128)(2,1)}, bf16[128,128,128]{2,1,0:T(8,128)(2,1)}, u32[]{:S(2)}, u32[]{:S(2)}) collective-permute-start(bf16[128,128,128]{2,1,0:T(8,128)(2,1)} %refs_8_.1), channel_id=1, source_target_pairs={{0,1},{1,0},{2,3},{3,2},{4,5},{5,4},{6,7},{7,6},{8,9},{9,8},{10,11... | collective-permute-start | bytes 12582920 | tf_op jit(solution)/shard_map/ppermute | solution.py:425
  2.6 8.2 %collective-permute-start = (bf16[1152,128]{1,0:T(8,128)(2,1)}, bf16[1152,128]{1,0:T(8,128)(2,1)S(1)}, u32[]{:S(2)}, u32[]{:S(2)}) collective-permute-start(bf16[1152,128]{1,0:T(8,128)(2,1)} %get-tuple-element.36), channel_id=1, source_target_pairs={{0,4},{1,3},{4,8},{5,1},{8,12},{9,5},{12,14},{13,9},{14,10},{15,13... | collective-permute-start | bytes 884744 | tf_op jit(solution)/shard_map/ppermute | solution.py:425
  6.1 7.1 %collective-permute-start.6 = (bf16[1152,128]{1,0:T(8,128)(2,1)}, bf16[1152,128]{1,0:T(8,128)(2,1)S(1)}, u32[]{:S(2)}, u32[]{:S(2)}) collective-permute-start(bf16[1152,128]{1,0:T(8,128)(2,1)} %get-tuple-element.36), channel_id=1, source_target_pairs={{0,3},{1,4},{4,1},{5,8},{8,5},{9,12},{12,9},{13,14},{14,13},{15,10... | collective-permute-start | bytes 884744 | tf_op jit(solution)/shard_map/ppermute | solution.py:425
  7.5 9.1 %collective-permute-start.3 = (bf16[1152,128]{1,0:T(8,128)(2,1)}, bf16[1152,128]{1,0:T(8,128)(2,1)S(1)}, u32[]{:S(2)}, u32[]{:S(2)}) collective-permute-start(bf16[1152,128]{1,0:T(8,128)(2,1)} %get-tuple-element.36), channel_id=1, source_target_pairs={{0,1},{1,0},{2,3},{3,2},{4,5},{5,4},{6,7},{7,6},{8,9},{9,8},{10,11... | collective-permute-start | bytes 884744 | tf_op jit(solution)/shard_map/ppermute | solution.py:425
  10.8 7.4 %collective-permute-start.1 = (bf16[1152,128]{1,0:T(8,128)(2,1)S(1)}, bf16[1152,128]{1,0:T(8,128)(2,1)S(1)}, u32[]{:S(2)}, u32[]{:S(2)}) collective-permute-start(bf16[1152,128]{1,0:T(8,128)(2,1)S(1)} %collective-permute-done.refs_1_), channel_id=1, source_target_pairs={{0,4},{1,3},{4,8},{5,1},{8,12},{9,5},{12,14},{13,9},{14,10},{15,13... | collective-permute-start | bytes 884744 | tf_op jit(solution)/shard_map/ppermute | solution.py:425
  13.2 8.1 %collective-permute-start.7 = (bf16[1152,128]{1,0:T(8,128)(2,1)S(1)}, bf16[1152,128]{1,0:T(8,128)(2,1)S(1)}, u32[]{:S(2)}, u32[]{:S(2)}) collective-permute-start(bf16[1152,128]{1,0:T(8,128)(2,1)S(1)} %collective-permute-done.6.refs_2_), channel_id=1, source_target_pairs={{0,4},{1,3},{4,8},{5,1},{8,12},{9,5},{12,14},{13,9},{14,10},{15,13... | collective-permute-start | bytes 884744 | tf_op jit(solution)/shard_map/ppermute | solution.py:425
  15.3 1.4 %collective-permute-start.4 = (s32[8,128]{1,0:T(8,128)}, s32[8,128]{1,0:T(8,128)S(1)}, u32[]{:S(2)}, u32[]{:S(2)}) collective-permute-start(s32[8,128]{1,0:T(8,128)} %get-tuple-element.37), channel_id=1, source_target_pairs={{0,1},{1,0},{2,3},{3,2},{4,5},{5,4},{6,7},{7,6},{8,9},{9,8},{10,11... | collective-permute-start | bytes 12296 | tf_op jit(solution)/shard_map/ppermute | solution.py:425
  18.1 6.7 %collective-permute-start.5 = (bf16[1152,128]{1,0:T(8,128)(2,1)S(1)}, bf16[1152,128]{1,0:T(8,128)(2,1)S(1)}, u32[]{:S(2)}, u32[]{:S(2)}) collective-permute-start(bf16[1152,128]{1,0:T(8,128)(2,1)S(1)} %collective-permute-done.1.refs_3_), channel_id=1, source_target_pairs={{0,4},{1,3},{4,8},{5,1},{8,12},{9,5},{12,14},{13,9},{14,10},{15,13... | collective-permute-start | bytes 884744 | tf_op jit(solution)/shard_map/ppermute | solution.py:425
  21.3 20.3 %collective-permute-start.8 = (bf16[1152,128]{1,0:T(8,128)(2,1)S(1)}, bf16[1152,128]{1,0:T(8,128)(2,1)S(1)}, u32[]{:S(2)}, u32[]{:S(2)}) collective-permute-start(bf16[1152,128]{1,0:T(8,128)(2,1)S(1)} %collective-permute-done.7.refs_4_), channel_id=1, source_target_pairs={{0,4},{1,3},{4,8},{5,1},{8,12},{9,5},{12,14},{13,9},{14,10},{15,13... | collective-permute-start | bytes 884744 | tf_op jit(solution)/shard_map/ppermute | solution.py:425
  24.3 6.9 %copy-start.2 = (s32[16,128]{1,0:T(8,128)S(1)}, s32[16,128]{1,0:T(8,128)}, u32[]{:S(2)}) copy-start(s32[16,128]{1,0:T(8,128)} %pad_add_fusion.token_ref.list_ref) | copy-start | bytes 24580
  24.9 16.8 %collective-permute-start.9 = (bf16[1152,128]{1,0:T(8,128)(2,1)S(1)}, bf16[1152,128]{1,0:T(8,128)(2,1)S(1)}, u32[]{:S(2)}, u32[]{:S(2)}) collective-permute-start(bf16[1152,128]{1,0:T(8,128)(2,1)S(1)} %collective-permute-done.5.refs_5_), channel_id=1, source_target_pairs={{0,4},{1,3},{4,8},{5,1},{8,12},{9,5},{12,14},{13,9},{14,10},{15,13... | collective-permute-start | bytes 884744 | tf_op jit(solution)/shard_map/ppermute | solution.py:425
  31.2 3.4 %copy-start = (f32[257,64,128]{2,1,0:T(8,128)S(1)}, f32[257,64,128]{2,1,0:T(8,128)}, u32[]{:S(2)}) copy-start(f32[257,64,128]{2,1,0:T(8,128)} %open.1.refs_8_) | copy-start | bytes 25264132
  34.6 2.2 %copy-start.1 = (bf16[128,128,128]{2,1,0:T(8,128)(2,1)S(1)}, bf16[128,128,128]{2,1,0:T(8,128)(2,1)}, u32[]{:S(2)}) copy-start(bf16[128,128,128]{2,1,0:T(8,128)(2,1)} %refs_8_.1) | copy-start | bytes 12582916
  44.2 24.7 %copy-start.3 = (bf16[16,16,128]{2,1,0:T(8,128)(2,1)S(1)}, bf16[16,16,128]{2,1,0:T(8,128)(2,1)}, u32[]{:S(2)}) copy-start(bf16[16,16,128]{2,1,0:T(8,128)(2,1)} %refs_7_.1) | copy-start | bytes 196612
  44.3 24.7 %copy-start.4 = (s32[256]{0:T(256)S(1)}, s32[256]{0:T(256)}, u32[]{:S(2)}) copy-start(s32[256]{0:T(256)} %param.17) | copy-start | bytes 3076
  44.3 24.7 %copy-start.5 = (s32[256,1]{0,1:T(1,128)S(1)}, s32[256,1]{0,1:T(1,128)}, u32[]{:S(2)}) copy-start(s32[256,1]{0,1:T(1,128)} %param.18) | copy-start | bytes 3076
  44.3 24.7 %copy-start.6 = (s32[256]{0:T(256)S(1)}, s32[256]{0:T(256)}, u32[]{:S(2)}) copy-start(s32[256]{0:T(256)} %param.19) | copy-start | bytes 3076
  44.3 2.0 %collective-permute-start.11 = (bf16[32,64,128]{2,1,0:T(8,128)(2,1)S(1)}, bf16[32,64,128]{2,1,0:T(8,128)(2,1)S(1)}, u32[]{:S(2)}, u32[]{:S(2)}) collective-permute-start(bf16[32,64,128]{2,1,0:T(8,128)(2,1)S(1)} %get-tuple-element.45), channel_id=1, source_target_pairs={{0,1},{1,0},{2,3},{3,2},{4,5},{5,4},{6,7},{7,6},{8,9},{9,8},{10,11... | collective-permute-start | bytes 1572872 | tf_op jit(solution)/shard_map/ppermute | solution.py:425
  46.4 6.6 %collective-permute-start.13 = (bf16[96,64,128]{2,1,0:T(8,128)(2,1)S(1)}, bf16[96,64,128]{2,1,0:T(8,128)(2,1)S(1)}, u32[]{:S(2)}, u32[]{:S(2)}) collective-permute-start(bf16[96,64,128]{2,1,0:T(8,128)(2,1)S(1)} %get-tuple-element.49), channel_id=1, source_target_pairs={{0,1},{1,0},{2,3},{3,2},{4,5},{5,4},{6,7},{7,6},{8,9},{9,8},{10,11... | collective-permute-start | bytes 4718600 | tf_op jit(solution)/shard_map/ppermute | solution.py:425
  46.6 6.4 %collective-permute-start.12 = (bf16[16,64,128]{2,1,0:T(8,128)(2,1)S(1)}, bf16[16,64,128]{2,1,0:T(8,128)(2,1)S(1)}, u32[]{:S(2)}, u32[]{:S(2)}) collective-permute-start(bf16[16,64,128]{2,1,0:T(8,128)(2,1)S(1)} %get-tuple-element.46), channel_id=1, source_target_pairs={{0,4},{1,3},{4,8},{5,1},{8,12},{9,5},{12,14},{13,9},{14,10},{15,13... | collective-permute-start | bytes 786440 | tf_op jit(solution)/shard_map/ppermute | solution.py:425
  48.9 6.9 %collective-permute-start.15 = (bf16[16,64,128]{2,1,0:T(8,128)(2,1)S(1)}, bf16[16,64,128]{2,1,0:T(8,128)(2,1)S(1)}, u32[]{:S(2)}, u32[]{:S(2)}) collective-permute-start(bf16[16,64,128]{2,1,0:T(8,128)(2,1)S(1)} %get-tuple-element.48), channel_id=1, source_target_pairs={{0,4},{1,3},{4,8},{5,1},{8,12},{9,5},{12,14},{13,9},{14,10},{15,13... | collective-permute-start | bytes 786440 | tf_op jit(solution)/shard_map/ppermute | solution.py:425
  53.1 6.4 %collective-permute-start.14 = (bf16[16,64,128]{2,1,0:T(8,128)(2,1)S(1)}, bf16[16,64,128]{2,1,0:T(8,128)(2,1)S(1)}, u32[]{:S(2)}, u32[]{:S(2)}) collective-permute-start(bf16[16,64,128]{2,1,0:T(8,128)(2,1)S(1)} %add_convert_fusion.5), channel_id=1, source_target_pairs={{0,4},{1,3},{4,8},{5,1},{8,12},{9,5},{12,14},{13,9},{14,10},{15,13... | collective-permute-start | bytes 786440 | tf_op jit(solution)/shard_map/ppermute | solution.py:425
  55.9 6.4 %collective-permute-start.17 = (bf16[16,64,128]{2,1,0:T(8,128)(2,1)S(1)}, bf16[16,64,128]{2,1,0:T(8,128)(2,1)S(1)}, u32[]{:S(2)}, u32[]{:S(2)}) collective-permute-start(bf16[16,64,128]{2,1,0:T(8,128)(2,1)S(1)} %add_convert_fusion.4), channel_id=1, source_target_pairs={{0,4},{1,3},{4,8},{5,1},{8,12},{9,5},{12,14},{13,9},{14,10},{15,13... | collective-permute-start | bytes 786440 | tf_op jit(solution)/shard_map/ppermute | solution.py:425
  59.7 6.4 %collective-permute-start.16 = (bf16[16,64,128]{2,1,0:T(8,128)(2,1)S(1)}, bf16[16,64,128]{2,1,0:T(8,128)(2,1)S(1)}, u32[]{:S(2)}, u32[]{:S(2)}) collective-permute-start(bf16[16,64,128]{2,1,0:T(8,128)(2,1)S(1)} %add_convert_fusion.3), channel_id=1, source_target_pairs={{0,4},{1,3},{4,8},{5,1},{8,12},{9,5},{12,14},{13,9},{14,10},{15,13... | collective-permute-start | bytes 786440 | tf_op jit(solution)/shard_map/ppermute | solution.py:425
  62.0 6.9 %collective-permute-start.10 = (bf16[1024,128]{1,0:T(8,128)(2,1)S(1)}, bf16[1024,128]{1,0:T(8,128)(2,1)S(1)}, u32[]{:S(2)}, u32[]{:S(2)}) collective-permute-start(bf16[1024,128]{1,0:T(8,128)(2,1)S(1)} %get-tuple-element.43.refs_0_), channel_id=1, source_target_pairs={{0,1},{1,0},{2,3},{3,2},{4,5},{5,4},{6,7},{7,6},{8,9},{9,8},{10,11... | collective-permute-start | bytes 786440 | tf_op jit(solution)/shard_map/ppermute | solution.py:425
  62.5 6.4 %collective-permute-start.19 = (bf16[16,64,128]{2,1,0:T(8,128)(2,1)S(1)}, bf16[16,64,128]{2,1,0:T(8,128)(2,1)S(1)}, u32[]{:S(2)}, u32[]{:S(2)}) collective-permute-start(bf16[16,64,128]{2,1,0:T(8,128)(2,1)S(1)} %add_convert_fusion.2), channel_id=1, source_target_pairs={{0,4},{1,3},{4,8},{5,1},{8,12},{9,5},{12,14},{13,9},{14,10},{15,13... | collective-permute-start | bytes 786440 | tf_op jit(solution)/shard_map/ppermute | solution.py:425
  66.2 6.4 %collective-permute-start.18 = (bf16[16,64,128]{2,1,0:T(8,128)(2,1)S(1)}, bf16[16,64,128]{2,1,0:T(8,128)(2,1)S(1)}, u32[]{:S(2)}, u32[]{:S(2)}) collective-permute-start(bf16[16,64,128]{2,1,0:T(8,128)(2,1)S(1)} %add_convert_fusion.1), channel_id=1, source_target_pairs={{0,4},{1,3},{4,8},{5,1},{8,12},{9,5},{12,14},{13,9},{14,10},{15,13... | collective-permute-start | bytes 786440 | tf_op jit(solution)/shard_map/ppermute | solution.py:425
  68.9 3.9 %collective-permute-start.20 = (bf16[16,64,128]{2,1,0:T(8,128)(2,1)S(1)}, bf16[16,64,128]{2,1,0:T(8,128)(2,1)S(1)}, u32[]{:S(2)}, u32[]{:S(2)}) collective-permute-start(bf16[16,64,128]{2,1,0:T(8,128)(2,1)S(1)} %collective-permute-done.19), channel_id=1, source_target_pairs={{0,1},{1,0},{2,3},{3,2},{4,5},{5,4},{6,7},{7,6},{8,9},{9,8},{10,11... | collective-permute-start | bytes 786440 | tf_op jit(solution)/shard_map/ppermute | solution.py:425

commit v23 on v22

--- a/solution.py
+++ b/solution.py
@@ -458,6 +458,17 @@
         bytes_accessed=16 << 20,
         transcendentals=0,
     )
+    sums_shape = jax.ShapeDtypeStruct((count * clusters + 1, directions, unknowns), jnp.float32)
+    sums = pl.pallas_call(
+        open_kernel,
+        out_shape=sums_shape,
+        in_specs=[whole(pltpu.SMEM)],
+        out_specs=whole(),
+        compiler_params=pltpu.CompilerParams(vmem_limit_bytes=NEAR_VMEM),
+        cost_estimate=cost,
+        name="open",
+    )(after(here, couple))
+    flow[0], sums = lax.optimization_barrier((flow[0], sums))
     for k in range(1, chips):
         x = 1 - k % 2
         if k == 3:
@@ -473,7 +484,6 @@
             flow[x] = move(flow[x], ahead)
 
     pieces = [2, chips - 2]
-    sums_shape = jax.ShapeDtypeStruct((count * clusters + 1, directions, unknowns), jnp.float32)
 
     def near(late, shards, sums):
         sends = pieces if late else []
@@ -523,14 +533,6 @@
             basis_out,
         )
 
-    sums = pl.pallas_call(
-        open_kernel,
-        out_shape=sums_shape,
-        in_specs=[whole()],
-        out_specs=whole(),
-        cost_estimate=cost,
-        name="open",
-    )(lists)
     (sums,) = near(0, shards[: chips - LATE], sums)
     sums, coef, *sends = near(1, shards, sums)
     mates = [move(sends[0], mate)]

time: 74 us -> 64.3 us (0.87)
  local copies, waits for them, and re-layouts: 6.55 us -> 0.98 us
  Pallas kernels: 16.6 us -> 12.1 us
  other arithmetic: 2.91 us -> 1.64 us
  starting transfers between devices: 30.1 us -> 31.2 us
    unnamed x15 -> x13, local copies, waits for them, and re-layouts: 6.55 us -> 0.98 us
    pallas_call x1, Pallas kernels: 4.56 us -> 0.57 us  [stationary(): pl.pallas_call(open_kernel, out_shape=sums_shape, in_specs=[whole(pltpu.S...]
    concatenate x1, other arithmetic: 1.27 us -> 0.01 us  [stationary(): lists = jnp.concatenate([after(lists, flow[x]), mate_lists], axis=0)]
    ppermute x21, starting transfers between devices: 30.1 us -> 31.2 us  [move(): return lax.ppermute(values, 'blk', where)]
  transfers between devices with their start and end apart: 21 -> 21, of which waited for: 13 -> 14; matrix products, arithmetic and copies ran while one was open for 4% -> 3% of each run, Pallas kernels for 19% -> 15%
where the time goes in v23:
time: 64.3 us; the launch traced here: 63.6 us
  starting transfers between devices  31.2 us (49%)
  waiting for transfers between devices  17.5 us (27%)
  Pallas kernels  12.1 us (19%)
  other arithmetic  1.64 us (3%)
  local copies, waits for them, and re-layouts  0.98 us (2%)
    ppermute x21, starting transfers between devices, move(): return lax.ppermute(values, 'blk', where)  31.2 us
    ppermute x21, waiting for transfers between devices, move(): return lax.ppermute(values, 'blk', where)  17.5 us
    pallas_call x2, Pallas kernels, near(): pl.pallas_call(functools.partial(near_kernel, late, BATCH[late], len(shar...  6.78 us
    pallas_call x1, Pallas kernels, far_field(): pl.pallas_call(far_kernel, out_shape=jax.ShapeDtypeStruct((clusters, dire...  2.5 us
    pallas_call x1, Pallas kernels, stationary(): pl.pallas_call(functools.partial(prologue_kernel, count), out_shape=[jax....  2.29 us
  transfers between devices with their start and end apart: 21, of which 14 were waited for; matrix products, arithmetic and copies ran while one was open for 3% of the time, Pallas kernels for 15%

profile of v23, /device:TPU:0, one launch (start us, length us, event | category | flops | bytes accessed | tf_op | source)
XLA Modules:
  0.0 63.6 jit_solution(4756047870133933016)
XLA Ops:
  0.5 2.3 %prologue.1 = (bf16[1152,128]{1,0:T(8,128)(2,1)}, s32[8,128]{1,0:T(8,128)}) custom-call(s32[1]{0:T(128)} %bitcast.me_ref.token_ref.refs_2_, s32[1,128]{1,0:T(1,128)} %bitcast.14, s32[1,128]{1,0:T(1,128)} %bitcast.15, s32[1,128]{1,0:T(1,128)} %bitcast.16, bf16[16,64,128]{2,1,0:T(8,128)(2,1)} %rhs_ref.1, bf16[16,16,128]{2,1,0:T(8,128)(2,1)} %basis_ref.1), custom_call_target="tpu_custom_call" | custom-call | tf_op jit(solution)/shard_map/prologue/pallas_call | solution.py:432
  2.7 2.6 %collective-permute-start = (bf16[1152,128]{1,0:T(8,128)(2,1)}, bf16[1152,128]{1,0:T(8,128)(2,1)S(1)}, u32[]{:S(2)}, u32[]{:S(2)}) collective-permute-start(bf16[1152,128]{1,0:T(8,128)(2,1)} %get-tuple-element.41), channel_id=1, source_target_pairs={{0,4},{1,3},{4,8},{5,1},{8,12},{9,5},{12,14},{13,9},{14,10},{15,13... | collective-permute-start | bytes 884744 | tf_op jit(solution)/shard_map/ppermute | solution.py:425
  5.5 0.9 %copy.16 = bf16[256,16,16]{0,1,2:T(8,128)(2,1)S(1)} copy(bf16[256,16,16]{0,2,1:T(8,128)(2,1)} %param.16) | data formatting | bytes 262144 | tf_op args[5]
  6.4 1.2 %collective-permute-start.6 = (bf16[1152,128]{1,0:T(8,128)(2,1)}, bf16[1152,128]{1,0:T(8,128)(2,1)S(1)}, u32[]{:S(2)}, u32[]{:S(2)}) collective-permute-start(bf16[1152,128]{1,0:T(8,128)(2,1)} %get-tuple-element.41), channel_id=1, source_target_pairs={{0,3},{1,4},{4,1},{5,8},{8,5},{9,12},{12,9},{13,14},{14,13},{15,10... | collective-permute-start | bytes 884744 | tf_op jit(solution)/shard_map/ppermute | solution.py:425
  7.7 0.6 open.1.refs_8_
  8.3 2.7 %collective-permute-done.refs_1_ = bf16[1152,128]{1,0:T(8,128)(2,1)S(1)} collective-permute-done((bf16[1152,128]{1,0:T(8,128)(2,1)}, bf16[1152,128]{1,0:T(8,128)(2,1)S(1)}, u32[]{:S(2)}, u32[]{:S(2)}) %collective-permute-start) | collective-permute-done | bytes 294944 | tf_op jit(solution)/shard_map/ppermute | solution.py:425
  11.0 2.4 %collective-permute-start.1 = (bf16[1152,128]{1,0:T(8,128)(2,1)S(1)}, bf16[1152,128]{1,0:T(8,128)(2,1)S(1)}, u32[]{:S(2)}, u32[]{:S(2)}) collective-permute-start(bf16[1152,128]{1,0:T(8,128)(2,1)S(1)} %collective-permute-done.refs_1_), channel_id=1, source_target_pairs={{0,4},{1,3},{4,8},{5,1},{8,12},{9,5},{12,14},{13,9},{14,10},{15,13... | collective-permute-start | bytes 884744 | tf_op jit(solution)/shard_map/ppermute | solution.py:425
  13.3 2.1 %collective-permute-start.7 = (bf16[1152,128]{1,0:T(8,128)(2,1)S(1)}, bf16[1152,128]{1,0:T(8,128)(2,1)S(1)}, u32[]{:S(2)}, u32[]{:S(2)}) collective-permute-start(bf16[1152,128]{1,0:T(8,128)(2,1)S(1)} %collective-permute-done.6.refs_2_), channel_id=1, source_target_pairs={{0,4},{1,3},{4,8},{5,1},{8,12},{9,5},{12,14},{13,9},{14,10},{15,13... | collective-permute-start | bytes 884744 | tf_op jit(solution)/shard_map/ppermute | solution.py:425
  15.4 1.2 %collective-permute-done.4 = s32[8,128]{1,0:T(8,128)S(1)} collective-permute-done((s32[8,128]{1,0:T(8,128)S(1)}, s32[8,128]{1,0:T(8,128)S(1)}, u32[]{:S(2)}, u32[]{:S(2)}) %collective-permute-start.4) | collective-permute-done | bytes 4128 | tf_op jit(solution)/shard_map/ppermute | solution.py:425
  16.6 1.2 %collective-permute-done.1.refs_3_ = bf16[1152,128]{1,0:T(8,128)(2,1)S(1)} collective-permute-done((bf16[1152,128]{1,0:T(8,128)(2,1)S(1)}, bf16[1152,128]{1,0:T(8,128)(2,1)S(1)}, u32[]{:S(2)}, u32[]{:S(2)}) %collective-permute-start.1) | collective-permute-done | bytes 294944 | tf_op jit(solution)/shard_map/ppermute | solution.py:425
  17.8 2.3 %collective-permute-start.5 = (bf16[1152,128]{1,0:T(8,128)(2,1)S(1)}, bf16[1152,128]{1,0:T(8,128)(2,1)S(1)}, u32[]{:S(2)}, u32[]{:S(2)}) collective-permute-start(bf16[1152,128]{1,0:T(8,128)(2,1)S(1)} %collective-permute-done.1.refs_3_), channel_id=1, source_target_pairs={{0,4},{1,3},{4,8},{5,1},{8,12},{9,5},{12,14},{13,9},{14,10},{15,13... | collective-permute-start | bytes 884744 | tf_op jit(solution)/shard_map/ppermute | solution.py:425
  20.1 0.9 %collective-permute-done.7.refs_4_ = bf16[1152,128]{1,0:T(8,128)(2,1)S(1)} collective-permute-done((bf16[1152,128]{1,0:T(8,128)(2,1)S(1)}, bf16[1152,128]{1,0:T(8,128)(2,1)S(1)}, u32[]{:S(2)}, u32[]{:S(2)}) %collective-permute-start.7) | collective-permute-done | bytes 294944 | tf_op jit(solution)/shard_map/ppermute | solution.py:425
  20.9 2.3 %collective-permute-start.8 = (bf16[1152,128]{1,0:T(8,128)(2,1)S(1)}, bf16[1152,128]{1,0:T(8,128)(2,1)S(1)}, u32[]{:S(2)}, u32[]{:S(2)}) collective-permute-start(bf16[1152,128]{1,0:T(8,128)(2,1)S(1)} %collective-permute-done.7.refs_4_), channel_id=1, source_target_pairs={{0,4},{1,3},{4,8},{5,1},{8,12},{9,5},{12,14},{13,9},{14,10},{15,13... | collective-permute-start | bytes 884744 | tf_op jit(solution)/shard_map/ppermute | solution.py:425
  23.2 1.3 %collective-permute-done.5.refs_5_ = bf16[1152,128]{1,0:T(8,128)(2,1)S(1)} collective-permute-done((bf16[1152,128]{1,0:T(8,128)(2,1)S(1)}, bf16[1152,128]{1,0:T(8,128)(2,1)S(1)}, u32[]{:S(2)}, u32[]{:S(2)}) %collective-permute-start.5) | collective-permute-done | bytes 294944 | tf_op jit(solution)/shard_map/ppermute | solution.py:425
  24.5 2.3 %collective-permute-start.9 = (bf16[1152,128]{1,0:T(8,128)(2,1)S(1)}, bf16[1152,128]{1,0:T(8,128)(2,1)S(1)}, u32[]{:S(2)}, u32[]{:S(2)}) collective-permute-start(bf16[1152,128]{1,0:T(8,128)(2,1)S(1)} %collective-permute-done.5.refs_5_), channel_id=1, source_target_pairs={{0,4},{1,3},{4,8},{5,1},{8,12},{9,5},{12,14},{13,9},{14,10},{15,13... | collective-permute-start | bytes 884744 | tf_op jit(solution)/shard_map/ppermute | solution.py:425
  26.8 3.9 %near.2.refs_10_ = f32[257,64,128]{2,1,0:T(8,128)S(1)} custom-call(s32[16,128]{1,0:T(8,128)S(1)} %pad_add_fusion.list_ref, bf16[1152,128]{1,0:T(8,128)(2,1)S(1)} %collective-permute-done.3.refs_0_, bf16[1152,128]{1,0:T(8,128)(2,1)S(1)} %collective-permute-done.refs_1_, ...), custom_call_target="tpu_custom_call", output_to_operand_aliasing={{}: (9, {})} | custom-call | flops 2147483648 | bytes 16777216 | tf_op jit(solution)/shard_map/near/pallas_call | solution.py:490
  30.7 0.5 collective-permute-done.9.refs_7_
  31.2 2.9 %near.3 = (f32[257,64,128]{2,1,0:T(8,128)S(1)}, bf16[1024,128]{1,0:T(8,128)(2,1)S(1)}, bf16[32,64,128]{2,1,0:T(8,128)(2,1)S(1)}, bf16[96,64,128]{2,1,0:T(8,128)(2,1)S(1)}) custom-call(s32[16,128]{1,0:T(8,128)S(1)} %pad_add_fusion.list_ref, bf16[1152,128]{1,0:T(8,128)(2,1)S(1)} %collective-permute-done.3.refs_0_, ...), custom_call_target="tpu_custom_call", output_to_operand_aliasing={{0}: (11, {})} | custom-call | flops 2147483648 | bytes 16777216 | tf_op jit(solution)/shard_map/near/pallas_call | solution.py:490
  34.2 1.9 %collective-permute-done.11 = bf16[32,64,128]{2,1,0:T(8,128)(2,1)S(1)} collective-permute-done((bf16[32,64,128]{2,1,0:T(8,128)(2,1)S(1)}, bf16[32,64,128]{2,1,0:T(8,128)(2,1)S(1)}, u32[]{:S(2)}, u32[]{:S(2)}) %collective-permute-start.11) | collective-permute-done | bytes 524320 | tf_op jit(solution)/shard_map/ppermute | solution.py:425
  36.5 2.3 %collective-permute-start.12 = (bf16[16,64,128]{2,1,0:T(8,128)(2,1)S(1)}, bf16[16,64,128]{2,1,0:T(8,128)(2,1)S(1)}, u32[]{:S(2)}, u32[]{:S(2)}) collective-permute-start(bf16[16,64,128]{2,1,0:T(8,128)(2,1)S(1)} %get-tuple-element.52), channel_id=1, source_target_pairs={{0,4},{1,3},{4,8},{5,1},{8,12},{9,5},{12,14},{13,9},{14,10},{15,13... | collective-permute-start | bytes 786440 | tf_op jit(solution)/shard_map/ppermute | solution.py:425
  38.8 1.6 %collective-permute-start.15 = (bf16[16,64,128]{2,1,0:T(8,128)(2,1)S(1)}, bf16[16,64,128]{2,1,0:T(8,128)(2,1)S(1)}, u32[]{:S(2)}, u32[]{:S(2)}) collective-permute-start(bf16[16,64,128]{2,1,0:T(8,128)(2,1)S(1)} %get-tuple-element.54), channel_id=1, source_target_pairs={{0,4},{1,3},{4,8},{5,1},{8,12},{9,5},{12,14},{13,9},{14,10},{15,13... | collective-permute-start | bytes 786440 | tf_op jit(solution)/shard_map/ppermute | solution.py:425
  40.3 2.6 %collective-permute-done.12 = bf16[16,64,128]{2,1,0:T(8,128)(2,1)S(1)} collective-permute-done((bf16[16,64,128]{2,1,0:T(8,128)(2,1)S(1)}, bf16[16,64,128]{2,1,0:T(8,128)(2,1)S(1)}, u32[]{:S(2)}, u32[]{:S(2)}) %collective-permute-start.12) | collective-permute-done | bytes 262176 | tf_op jit(solution)/shard_map/ppermute | solution.py:425
  43.1 2.2 %collective-permute-start.14 = (bf16[16,64,128]{2,1,0:T(8,128)(2,1)S(1)}, bf16[16,64,128]{2,1,0:T(8,128)(2,1)S(1)}, u32[]{:S(2)}, u32[]{:S(2)}) collective-permute-start(bf16[16,64,128]{2,1,0:T(8,128)(2,1)S(1)} %add_convert_fusion.5), channel_id=1, source_target_pairs={{0,4},{1,3},{4,8},{5,1},{8,12},{9,5},{12,14},{13,9},{14,10},{15,13... | collective-permute-start | bytes 786440 | tf_op jit(solution)/shard_map/ppermute | solution.py:425
  45.9 2.2 %collective-permute-start.17 = (bf16[16,64,128]{2,1,0:T(8,128)(2,1)S(1)}, bf16[16,64,128]{2,1,0:T(8,128)(2,1)S(1)}, u32[]{:S(2)}, u32[]{:S(2)}) collective-permute-start(bf16[16,64,128]{2,1,0:T(8,128)(2,1)S(1)} %add_convert_fusion.4), channel_id=1, source_target_pairs={{0,4},{1,3},{4,8},{5,1},{8,12},{9,5},{12,14},{13,9},{14,10},{15,13... | collective-permute-start | bytes 786440 | tf_op jit(solution)/shard_map/ppermute | solution.py:425
  48.1 1.4 %collective-permute-done.14 = bf16[16,64,128]{2,1,0:T(8,128)(2,1)S(1)} collective-permute-done((bf16[16,64,128]{2,1,0:T(8,128)(2,1)S(1)}, bf16[16,64,128]{2,1,0:T(8,128)(2,1)S(1)}, u32[]{:S(2)}, u32[]{:S(2)}) %collective-permute-start.14) | collective-permute-done | bytes 262176 | tf_op jit(solution)/shard_map/ppermute | solution.py:425
  49.6 2.2 %collective-permute-start.16 = (bf16[16,64,128]{2,1,0:T(8,128)(2,1)S(1)}, bf16[16,64,128]{2,1,0:T(8,128)(2,1)S(1)}, u32[]{:S(2)}, u32[]{:S(2)}) collective-permute-start(bf16[16,64,128]{2,1,0:T(8,128)(2,1)S(1)} %add_convert_fusion.3), channel_id=1, source_target_pairs={{0,4},{1,3},{4,8},{5,1},{8,12},{9,5},{12,14},{13,9},{14,10},{15,13... | collective-permute-start | bytes 786440 | tf_op jit(solution)/shard_map/ppermute | solution.py:425
  52.4 2.2 %collective-permute-start.19 = (bf16[16,64,128]{2,1,0:T(8,128)(2,1)S(1)}, bf16[16,64,128]{2,1,0:T(8,128)(2,1)S(1)}, u32[]{:S(2)}, u32[]{:S(2)}) collective-permute-start(bf16[16,64,128]{2,1,0:T(8,128)(2,1)S(1)} %add_convert_fusion.2), channel_id=1, source_target_pairs={{0,4},{1,3},{4,8},{5,1},{8,12},{9,5},{12,14},{13,9},{14,10},{15,13... | collective-permute-start | bytes 786440 | tf_op jit(solution)/shard_map/ppermute | solution.py:425
  54.7 1.4 %collective-permute-done.16 = bf16[16,64,128]{2,1,0:T(8,128)(2,1)S(1)} collective-permute-done((bf16[16,64,128]{2,1,0:T(8,128)(2,1)S(1)}, bf16[16,64,128]{2,1,0:T(8,128)(2,1)S(1)}, u32[]{:S(2)}, u32[]{:S(2)}) %collective-permute-start.16) | collective-permute-done | bytes 262176 | tf_op jit(solution)/shard_map/ppermute | solution.py:425
  56.1 2.2 %collective-permute-start.18 = (bf16[16,64,128]{2,1,0:T(8,128)(2,1)S(1)}, bf16[16,64,128]{2,1,0:T(8,128)(2,1)S(1)}, u32[]{:S(2)}, u32[]{:S(2)}) collective-permute-start(bf16[16,64,128]{2,1,0:T(8,128)(2,1)S(1)} %add_convert_fusion.1), channel_id=1, source_target_pairs={{0,4},{1,3},{4,8},{5,1},{8,12},{9,5},{12,14},{13,9},{14,10},{15,13... | collective-permute-start | bytes 786440 | tf_op jit(solution)/shard_map/ppermute | solution.py:425
  58.9 2.5 %far.1 = f32[16,64,128]{2,1,0:T(8,128)S(1)} custom-call(bf16[1024,128]{1,0:T(8,128)(2,1)S(1)} %get-tuple-element.49.refs_0_, bf16[1024,128]{1,0:T(8,128)(2,1)S(1)} %collective-permute-done.10.refs_1_, s32[1]{0:T(128)} %bitcast.me_ref.token_ref.refs_2_, bf16[16,16,256]{2,1,0:T(8,128)(2,1)S(1)} %bitcast.10, s32[1,256]{1,0:T(1,128)S(1)} %bitcast.11, ...), custom_call_target="tpu_custom_call" | custom-call | flops 536870912 | bytes 8388608 | tf_op jit(solution)/shard_map/far/pallas_call | solution.py:514
  61.4 1.2 %collective-permute-done.18 = bf16[16,64,128]{2,1,0:T(8,128)(2,1)S(1)} collective-permute-done((bf16[16,64,128]{2,1,0:T(8,128)(2,1)S(1)}, bf16[16,64,128]{2,1,0:T(8,128)(2,1)S(1)}, u32[]{:S(2)}, u32[]{:S(2)}) %collective-permute-start.18) | collective-permute-done | bytes 262176 | tf_op jit(solution)/shard_map/ppermute | solution.py:425
  62.8 0.8 %add_convert_fusion = bf16[16,64,128]{2,1,0:T(8,128)(2,1)} fusion(f32[16,64,128]{2,1,0:T(8,128)S(1)} %convert_add_fusion, bf16[16,64,128]{2,1,0:T(8,128)(2,1)S(1)} %collective-permute-done.20), kind=kLoop, calls=%fused_computation | loop fusion | flops 393216 | bytes 1048576 | tf_op jit(solution)/shard_map/convert_element_type | solution.py:566
  (37 shorter events, 3.2 us)
Async XLA Ops:
  0.0 17.8 %collective-permute-start.2 = (bf16[128,128,128]{2,1,0:T(8,128)(2,1)}, bf16[128,128,128]{2,1,0:T(8,128)(2,1)}, u32[]{:S(2)}, u32[]{:S(2)}) collective-permute-start(bf16[128,128,128]{2,1,0:T(8,128)(2,1)} %refs_8_.1), channel_id=1, source_target_pairs={{0,1},{1,0},{2,3},{3,2},{4,5},{5,4},{6,7},{7,6},{8,9},{9,8},{10,11... | collective-permute-start | bytes 12582920 | tf_op jit(solution)/shard_map/ppermute | solution.py:425
  0.5 26.3 %copy-start = (bf16[128,128,128]{2,1,0:T(8,128)(2,1)S(1)}, bf16[128,128,128]{2,1,0:T(8,128)(2,1)}, u32[]{:S(2)}) copy-start(bf16[128,128,128]{2,1,0:T(8,128)(2,1)} %refs_8_.1) | copy-start | bytes 12582916
  2.7 12.7 %copy-start.5 = (s32[8,128]{1,0:T(8,128)S(1)}, s32[8,128]{1,0:T(8,128)}, u32[]{:S(2)}) copy-start(s32[8,128]{1,0:T(8,128)} %get-tuple-element.42) | copy-start | bytes 12292
  2.7 8.2 %collective-permute-start = (bf16[1152,128]{1,0:T(8,128)(2,1)}, bf16[1152,128]{1,0:T(8,128)(2,1)S(1)}, u32[]{:S(2)}, u32[]{:S(2)}) collective-permute-start(bf16[1152,128]{1,0:T(8,128)(2,1)} %get-tuple-element.41), channel_id=1, source_target_pairs={{0,4},{1,3},{4,8},{5,1},{8,12},{9,5},{12,14},{13,9},{14,10},{15,13... | collective-permute-start | bytes 884744 | tf_op jit(solution)/shard_map/ppermute | solution.py:425
  5.3 11.3 %collective-permute-start.3 = (bf16[1152,128]{1,0:T(8,128)(2,1)}, bf16[1152,128]{1,0:T(8,128)(2,1)S(1)}, u32[]{:S(2)}, u32[]{:S(2)}) collective-permute-start(bf16[1152,128]{1,0:T(8,128)(2,1)} %get-tuple-element.41), channel_id=1, source_target_pairs={{0,1},{1,0},{2,3},{3,2},{4,5},{5,4},{6,7},{7,6},{8,9},{9,8},{10,11... | collective-permute-start | bytes 884744 | tf_op jit(solution)/shard_map/ppermute | solution.py:425
  6.4 6.9 %collective-permute-start.6 = (bf16[1152,128]{1,0:T(8,128)(2,1)}, bf16[1152,128]{1,0:T(8,128)(2,1)S(1)}, u32[]{:S(2)}, u32[]{:S(2)}) collective-permute-start(bf16[1152,128]{1,0:T(8,128)(2,1)} %get-tuple-element.41), channel_id=1, source_target_pairs={{0,3},{1,4},{4,1},{5,8},{8,5},{9,12},{12,9},{13,14},{14,13},{15,10... | collective-permute-start | bytes 884744 | tf_op jit(solution)/shard_map/ppermute | solution.py:425
  11.0 6.8 %collective-permute-start.1 = (bf16[1152,128]{1,0:T(8,128)(2,1)S(1)}, bf16[1152,128]{1,0:T(8,128)(2,1)S(1)}, u32[]{:S(2)}, u32[]{:S(2)}) collective-permute-start(bf16[1152,128]{1,0:T(8,128)(2,1)S(1)} %collective-permute-done.refs_1_), channel_id=1, source_target_pairs={{0,4},{1,3},{4,8},{5,1},{8,12},{9,5},{12,14},{13,9},{14,10},{15,13... | collective-permute-start | bytes 884744 | tf_op jit(solution)/shard_map/ppermute | solution.py:425
  13.3 7.6 %collective-permute-start.7 = (bf16[1152,128]{1,0:T(8,128)(2,1)S(1)}, bf16[1152,128]{1,0:T(8,128)(2,1)S(1)}, u32[]{:S(2)}, u32[]{:S(2)}) collective-permute-start(bf16[1152,128]{1,0:T(8,128)(2,1)S(1)} %collective-permute-done.6.refs_2_), channel_id=1, source_target_pairs={{0,4},{1,3},{4,8},{5,1},{8,12},{9,5},{12,14},{13,9},{14,10},{15,13... | collective-permute-start | bytes 884744 | tf_op jit(solution)/shard_map/ppermute | solution.py:425
  15.4 1.2 %collective-permute-start.4 = (s32[8,128]{1,0:T(8,128)S(1)}, s32[8,128]{1,0:T(8,128)S(1)}, u32[]{:S(2)}, u32[]{:S(2)}) collective-permute-start(s32[8,128]{1,0:T(8,128)S(1)} %copy-done.5), channel_id=1, source_target_pairs={{0,1},{1,0},{2,3},{3,2},{4,5},{5,4},{6,7},{7,6},{8,9},{9,8},{10,11... | collective-permute-start | bytes 12296 | tf_op jit(solution)/shard_map/ppermute | solution.py:425
  17.8 6.7 %collective-permute-start.5 = (bf16[1152,128]{1,0:T(8,128)(2,1)S(1)}, bf16[1152,128]{1,0:T(8,128)(2,1)S(1)}, u32[]{:S(2)}, u32[]{:S(2)}) collective-permute-start(bf16[1152,128]{1,0:T(8,128)(2,1)S(1)} %collective-permute-done.1.refs_3_), channel_id=1, source_target_pairs={{0,4},{1,3},{4,8},{5,1},{8,12},{9,5},{12,14},{13,9},{14,10},{15,13... | collective-permute-start | bytes 884744 | tf_op jit(solution)/shard_map/ppermute | solution.py:425
  20.9 9.8 %collective-permute-start.8 = (bf16[1152,128]{1,0:T(8,128)(2,1)S(1)}, bf16[1152,128]{1,0:T(8,128)(2,1)S(1)}, u32[]{:S(2)}, u32[]{:S(2)}) collective-permute-start(bf16[1152,128]{1,0:T(8,128)(2,1)S(1)} %collective-permute-done.7.refs_4_), channel_id=1, source_target_pairs={{0,4},{1,3},{4,8},{5,1},{8,12},{9,5},{12,14},{13,9},{14,10},{15,13... | collective-permute-start | bytes 884744 | tf_op jit(solution)/shard_map/ppermute | solution.py:425
  24.5 6.7 %collective-permute-start.9 = (bf16[1152,128]{1,0:T(8,128)(2,1)S(1)}, bf16[1152,128]{1,0:T(8,128)(2,1)S(1)}, u32[]{:S(2)}, u32[]{:S(2)}) collective-permute-start(bf16[1152,128]{1,0:T(8,128)(2,1)S(1)} %collective-permute-done.5.refs_5_), channel_id=1, source_target_pairs={{0,4},{1,3},{4,8},{5,1},{8,12},{9,5},{12,14},{13,9},{14,10},{15,13... | collective-permute-start | bytes 884744 | tf_op jit(solution)/shard_map/ppermute | solution.py:425
  34.1 24.8 %copy-start.1 = (bf16[16,16,128]{2,1,0:T(8,128)(2,1)S(1)}, bf16[16,16,128]{2,1,0:T(8,128)(2,1)}, u32[]{:S(2)}) copy-start(bf16[16,16,128]{2,1,0:T(8,128)(2,1)} %refs_7_.1) | copy-start | bytes 196612
  34.1 24.8 %copy-start.2 = (s32[256]{0:T(256)S(1)}, s32[256]{0:T(256)}, u32[]{:S(2)}) copy-start(s32[256]{0:T(256)} %param.17) | copy-start | bytes 3076
  34.1 24.8 %copy-start.3 = (s32[256,1]{0,1:T(1,128)S(1)}, s32[256,1]{0,1:T(1,128)}, u32[]{:S(2)}) copy-start(s32[256,1]{0,1:T(1,128)} %param.18) | copy-start | bytes 3076
  34.1 24.8 %copy-start.4 = (s32[256]{0:T(256)S(1)}, s32[256]{0:T(256)}, u32[]{:S(2)}) copy-start(s32[256]{0:T(256)} %param.19) | copy-start | bytes 3076
  34.1 2.0 %collective-permute-start.11 = (bf16[32,64,128]{2,1,0:T(8,128)(2,1)S(1)}, bf16[32,64,128]{2,1,0:T(8,128)(2,1)S(1)}, u32[]{:S(2)}, u32[]{:S(2)}) collective-permute-start(bf16[32,64,128]{2,1,0:T(8,128)(2,1)S(1)} %get-tuple-element.51), channel_id=1, source_target_pairs={{0,1},{1,0},{2,3},{3,2},{4,5},{5,4},{6,7},{7,6},{8,9},{9,8},{10,11... | collective-permute-start | bytes 1572872 | tf_op jit(solution)/shard_map/ppermute | solution.py:425
  36.3 6.7 %collective-permute-start.13 = (bf16[96,64,128]{2,1,0:T(8,128)(2,1)S(1)}, bf16[96,64,128]{2,1,0:T(8,128)(2,1)S(1)}, u32[]{:S(2)}, u32[]{:S(2)}) collective-permute-start(bf16[96,64,128]{2,1,0:T(8,128)(2,1)S(1)} %get-tuple-element.55), channel_id=1, source_target_pairs={{0,1},{1,0},{2,3},{3,2},{4,5},{5,4},{6,7},{7,6},{8,9},{9,8},{10,11... | collective-permute-start | bytes 4718600 | tf_op jit(solution)/shard_map/ppermute | solution.py:425
  36.5 6.5 %collective-permute-start.12 = (bf16[16,64,128]{2,1,0:T(8,128)(2,1)S(1)}, bf16[16,64,128]{2,1,0:T(8,128)(2,1)S(1)}, u32[]{:S(2)}, u32[]{:S(2)}) collective-permute-start(bf16[16,64,128]{2,1,0:T(8,128)(2,1)S(1)} %get-tuple-element.52), channel_id=1, source_target_pairs={{0,4},{1,3},{4,8},{5,1},{8,12},{9,5},{12,14},{13,9},{14,10},{15,13... | collective-permute-start | bytes 786440 | tf_op jit(solution)/shard_map/ppermute | solution.py:425
  38.8 7.0 %collective-permute-start.15 = (bf16[16,64,128]{2,1,0:T(8,128)(2,1)S(1)}, bf16[16,64,128]{2,1,0:T(8,128)(2,1)S(1)}, u32[]{:S(2)}, u32[]{:S(2)}) collective-permute-start(bf16[16,64,128]{2,1,0:T(8,128)(2,1)S(1)} %get-tuple-element.54), channel_id=1, source_target_pairs={{0,4},{1,3},{4,8},{5,1},{8,12},{9,5},{12,14},{13,9},{14,10},{15,13... | collective-permute-start | bytes 786440 | tf_op jit(solution)/shard_map/ppermute | solution.py:425
  43.1 6.4 %collective-permute-start.14 = (bf16[16,64,128]{2,1,0:T(8,128)(2,1)S(1)}, bf16[16,64,128]{2,1,0:T(8,128)(2,1)S(1)}, u32[]{:S(2)}, u32[]{:S(2)}) collective-permute-start(bf16[16,64,128]{2,1,0:T(8,128)(2,1)S(1)} %add_convert_fusion.5), channel_id=1, source_target_pairs={{0,4},{1,3},{4,8},{5,1},{8,12},{9,5},{12,14},{13,9},{14,10},{15,13... | collective-permute-start | bytes 786440 | tf_op jit(solution)/shard_map/ppermute | solution.py:425
  45.9 6.4 %collective-permute-start.17 = (bf16[16,64,128]{2,1,0:T(8,128)(2,1)S(1)}, bf16[16,64,128]{2,1,0:T(8,128)(2,1)S(1)}, u32[]{:S(2)}, u32[]{:S(2)}) collective-permute-start(bf16[16,64,128]{2,1,0:T(8,128)(2,1)S(1)} %add_convert_fusion.4), channel_id=1, source_target_pairs={{0,4},{1,3},{4,8},{5,1},{8,12},{9,5},{12,14},{13,9},{14,10},{15,13... | collective-permute-start | bytes 786440 | tf_op jit(solution)/shard_map/ppermute | solution.py:425
  49.6 6.4 %collective-permute-start.16 = (bf16[16,64,128]{2,1,0:T(8,128)(2,1)S(1)}, bf16[16,64,128]{2,1,0:T(8,128)(2,1)S(1)}, u32[]{:S(2)}, u32[]{:S(2)}) collective-permute-start(bf16[16,64,128]{2,1,0:T(8,128)(2,1)S(1)} %add_convert_fusion.3), channel_id=1, source_target_pairs={{0,4},{1,3},{4,8},{5,1},{8,12},{9,5},{12,14},{13,9},{14,10},{15,13... | collective-permute-start | bytes 786440 | tf_op jit(solution)/shard_map/ppermute | solution.py:425
  51.8 7.0 %collective-permute-start.10 = (bf16[1024,128]{1,0:T(8,128)(2,1)S(1)}, bf16[1024,128]{1,0:T(8,128)(2,1)S(1)}, u32[]{:S(2)}, u32[]{:S(2)}) collective-permute-start(bf16[1024,128]{1,0:T(8,128)(2,1)S(1)} %get-tuple-element.49.refs_0_), channel_id=1, source_target_pairs={{0,1},{1,0},{2,3},{3,2},{4,5},{5,4},{6,7},{7,6},{8,9},{9,8},{10,11... | collective-permute-start | bytes 786440 | tf_op jit(solution)/shard_map/ppermute | solution.py:425
  52.4 6.4 %collective-permute-start.19 = (bf16[16,64,128]{2,1,0:T(8,128)(2,1)S(1)}, bf16[16,64,128]{2,1,0:T(8,128)(2,1)S(1)}, u32[]{:S(2)}, u32[]{:S(2)}) collective-permute-start(bf16[16,64,128]{2,1,0:T(8,128)(2,1)S(1)} %add_convert_fusion.2), channel_id=1, source_target_pairs={{0,4},{1,3},{4,8},{5,1},{8,12},{9,5},{12,14},{13,9},{14,10},{15,13... | collective-permute-start | bytes 786440 | tf_op jit(solution)/shard_map/ppermute | solution.py:425
  56.1 6.5 %collective-permute-start.18 = (bf16[16,64,128]{2,1,0:T(8,128)(2,1)S(1)}, bf16[16,64,128]{2,1,0:T(8,128)(2,1)S(1)}, u32[]{:S(2)}, u32[]{:S(2)}) collective-permute-start(bf16[16,64,128]{2,1,0:T(8,128)(2,1)S(1)} %add_convert_fusion.1), channel_id=1, source_target_pairs={{0,4},{1,3},{4,8},{5,1},{8,12},{9,5},{12,14},{13,9},{14,10},{15,13... | collective-permute-start | bytes 786440 | tf_op jit(solution)/shard_map/ppermute | solution.py:425
  58.8 3.9 %collective-permute-start.20 = (bf16[16,64,128]{2,1,0:T(8,128)(2,1)S(1)}, bf16[16,64,128]{2,1,0:T(8,128)(2,1)S(1)}, u32[]{:S(2)}, u32[]{:S(2)}) collective-permute-start(bf16[16,64,128]{2,1,0:T(8,128)(2,1)S(1)} %collective-permute-done.19), channel_id=1, source_target_pairs={{0,1},{1,0},{2,3},{3,2},{4,5},{5,4},{6,7},{7,6},{8,9},{9,8},{10,11... | collective-permute-start | bytes 786440 | tf_op jit(solution)/shard_map/ppermute | solution.py:425

commit v24 on v23

--- a/solution.py
+++ b/solution.py
@@ -447,17 +447,15 @@
         rhs,
         basis_in,
     )
+    cost = pl.CostEstimate(
+        flops=16 * stored * directions * unknowns * unknowns,
+        bytes_accessed=16 << 20,
+        transcendentals=0,
+    )
     flow = [move(payload, ahead)]
     mate_blocks = move(near_blocks, mate)
     mate_lists = move(lists, mate)
     couple = jnp.transpose(far_coupling, (2, 1, 0))
-    flow.append(move(after(payload, couple), cross))
-    shards = [move(payload, mate)]
-    cost = pl.CostEstimate(
-        flops=16 * stored * directions * unknowns * unknowns,
-        bytes_accessed=16 << 20,
-        transcendentals=0,
-    )
     sums_shape = jax.ShapeDtypeStruct((count * clusters + 1, directions, unknowns), jnp.float32)
     sums = pl.pallas_call(
         open_kernel,
@@ -468,6 +466,8 @@
         cost_estimate=cost,
         name="open",
     )(after(here, couple))
+    flow.append(move(after(payload, couple, sums), cross))
+    shards = [move(payload, mate)]
     flow[0], sums = lax.optimization_barrier((flow[0], sums))
     for k in range(1, chips):
         x = 1 - k % 2

time: 64.3 us -> 64.5 us (level)
  waiting for transfers between devices: 17.5 us -> 25.6 us
  starting transfers between devices: 31.2 us -> 23.9 us
    ppermute x21, waiting for transfers between devices: 17.5 us -> 25.6 us  [move(): return lax.ppermute(values, 'blk', where)]
    ppermute x21, starting transfers between devices: 31.2 us -> 23.9 us  [move(): return lax.ppermute(values, 'blk', where)]
  transfers between devices with their start and end apart: 21 -> 21, of which waited for: 14 -> 15; matrix products, arithmetic and copies ran while one was open for 3% -> 3% of each run, Pallas kernels for 15% -> 14%
where the time goes in v24:
time: 64.5 us; the launch traced here: 64.1 us
  waiting for transfers between devices  25.6 us (40%)
  starting transfers between devices  23.9 us (37%)
  Pallas kernels  11.9 us (18%)
  other arithmetic  1.64 us (3%)
  local copies, waits for them, and re-layouts  0.98 us (2%)
    ppermute x21, waiting for transfers between devices, move(): return lax.ppermute(values, 'blk', where)  25.6 us
    ppermute x21, starting transfers between devices, move(): return lax.ppermute(values, 'blk', where)  23.9 us
    pallas_call x2, Pallas kernels, near(): pl.pallas_call(functools.partial(near_kernel, late, BATCH[late], len(shar...  6.52 us
    pallas_call x1, Pallas kernels, far_field(): pl.pallas_call(far_kernel, out_shape=jax.ShapeDtypeStruct((clusters, dire...  2.5 us
    pallas_call x1, Pallas kernels, stationary(): pl.pallas_call(functools.partial(prologue_kernel, count), out_shape=[jax....  2.29 us
  transfers between devices with their start and end apart: 21, of which 15 were waited for; matrix products, arithmetic and copies ran while one was open for 3% of the time, Pallas kernels for 14%

profile of v24, /device:TPU:0, one launch (start us, length us, event | category | flops | bytes accessed | tf_op | source)
XLA Modules:
  0.0 64.1 jit_solution(10065349246477978237)
XLA Ops:
  0.5 2.3 %prologue.1 = (bf16[1152,128]{1,0:T(8,128)(2,1)}, s32[8,128]{1,0:T(8,128)}) custom-call(s32[1]{0:T(128)} %bitcast.me_ref.token_ref.refs_2_, s32[1,128]{1,0:T(1,128)} %bitcast.14, s32[1,128]{1,0:T(1,128)} %bitcast.15, s32[1,128]{1,0:T(1,128)} %bitcast.16, bf16[16,64,128]{2,1,0:T(8,128)(2,1)} %rhs_ref.1, bf16[16,16,128]{2,1,0:T(8,128)(2,1)} %basis_ref.1), custom_call_target="tpu_custom_call" | custom-call | tf_op jit(solution)/shard_map/prologue/pallas_call | solution.py:432
  2.7 2.6 %collective-permute-start = (bf16[1152,128]{1,0:T(8,128)(2,1)}, bf16[1152,128]{1,0:T(8,128)(2,1)S(1)}, u32[]{:S(2)}, u32[]{:S(2)}) collective-permute-start(bf16[1152,128]{1,0:T(8,128)(2,1)} %get-tuple-element.41), channel_id=1, source_target_pairs={{0,4},{1,3},{4,8},{5,1},{8,12},{9,5},{12,14},{13,9},{14,10},{15,13... | collective-permute-start | bytes 884744 | tf_op jit(solution)/shard_map/ppermute | solution.py:425
  6.9 1.4 %collective-permute-start.6 = (bf16[1152,128]{1,0:T(8,128)(2,1)S(1)}, bf16[1152,128]{1,0:T(8,128)(2,1)S(1)}, u32[]{:S(2)}, u32[]{:S(2)}) collective-permute-start(bf16[1152,128]{1,0:T(8,128)(2,1)S(1)} %copy-done.6), channel_id=1, source_target_pairs={{0,3},{1,4},{4,1},{5,8},{8,5},{9,12},{12,9},{13,14},{14,13},{15,10... | collective-permute-start | bytes 884744 | tf_op jit(solution)/shard_map/ppermute | solution.py:425
  8.6 1.9 %collective-permute-done.refs_1_ = bf16[1152,128]{1,0:T(8,128)(2,1)S(1)} collective-permute-done((bf16[1152,128]{1,0:T(8,128)(2,1)}, bf16[1152,128]{1,0:T(8,128)(2,1)S(1)}, u32[]{:S(2)}, u32[]{:S(2)}) %collective-permute-start) | collective-permute-done | bytes 294944 | tf_op jit(solution)/shard_map/ppermute | solution.py:425
  10.6 2.4 %collective-permute-start.1 = (bf16[1152,128]{1,0:T(8,128)(2,1)S(1)}, bf16[1152,128]{1,0:T(8,128)(2,1)S(1)}, u32[]{:S(2)}, u32[]{:S(2)}) collective-permute-start(bf16[1152,128]{1,0:T(8,128)(2,1)S(1)} %collective-permute-done.refs_1_), channel_id=1, source_target_pairs={{0,4},{1,3},{4,8},{5,1},{8,12},{9,5},{12,14},{13,9},{14,10},{15,13... | collective-permute-start | bytes 884744 | tf_op jit(solution)/shard_map/ppermute | solution.py:425
  13.4 2.0 %collective-permute-start.7 = (bf16[1152,128]{1,0:T(8,128)(2,1)S(1)}, bf16[1152,128]{1,0:T(8,128)(2,1)S(1)}, u32[]{:S(2)}, u32[]{:S(2)}) collective-permute-start(bf16[1152,128]{1,0:T(8,128)(2,1)S(1)} %collective-permute-done.6.refs_2_), channel_id=1, source_target_pairs={{0,4},{1,3},{4,8},{5,1},{8,12},{9,5},{12,14},{13,9},{14,10},{15,13... | collective-permute-start | bytes 884744 | tf_op jit(solution)/shard_map/ppermute | solution.py:425
  15.4 1.2 %collective-permute-done.4 = s32[8,128]{1,0:T(8,128)S(1)} collective-permute-done((s32[8,128]{1,0:T(8,128)S(1)}, s32[8,128]{1,0:T(8,128)S(1)}, u32[]{:S(2)}, u32[]{:S(2)}) %collective-permute-start.4) | collective-permute-done | bytes 4128 | tf_op jit(solution)/shard_map/ppermute | solution.py:425
  16.6 1.3 %collective-permute-done.1.refs_3_ = bf16[1152,128]{1,0:T(8,128)(2,1)S(1)} collective-permute-done((bf16[1152,128]{1,0:T(8,128)(2,1)S(1)}, bf16[1152,128]{1,0:T(8,128)(2,1)S(1)}, u32[]{:S(2)}, u32[]{:S(2)}) %collective-permute-start.1) | collective-permute-done | bytes 294944 | tf_op jit(solution)/shard_map/ppermute | solution.py:425
  17.9 1.7 %collective-permute-start.5 = (bf16[1152,128]{1,0:T(8,128)(2,1)S(1)}, bf16[1152,128]{1,0:T(8,128)(2,1)S(1)}, u32[]{:S(2)}, u32[]{:S(2)}) collective-permute-start(bf16[1152,128]{1,0:T(8,128)(2,1)S(1)} %collective-permute-done.1.refs_3_), channel_id=1, source_target_pairs={{0,4},{1,3},{4,8},{5,1},{8,12},{9,5},{12,14},{13,9},{14,10},{15,13... | collective-permute-start | bytes 884744 | tf_op jit(solution)/shard_map/ppermute | solution.py:425
  19.7 1.4 %collective-permute-done.7.refs_4_ = bf16[1152,128]{1,0:T(8,128)(2,1)S(1)} collective-permute-done((bf16[1152,128]{1,0:T(8,128)(2,1)S(1)}, bf16[1152,128]{1,0:T(8,128)(2,1)S(1)}, u32[]{:S(2)}, u32[]{:S(2)}) %collective-permute-start.7) | collective-permute-done | bytes 294944 | tf_op jit(solution)/shard_map/ppermute | solution.py:425
  21.1 1.7 %collective-permute-start.8 = (bf16[1152,128]{1,0:T(8,128)(2,1)S(1)}, bf16[1152,128]{1,0:T(8,128)(2,1)S(1)}, u32[]{:S(2)}, u32[]{:S(2)}) collective-permute-start(bf16[1152,128]{1,0:T(8,128)(2,1)S(1)} %collective-permute-done.7.refs_4_), channel_id=1, source_target_pairs={{0,4},{1,3},{4,8},{5,1},{8,12},{9,5},{12,14},{13,9},{14,10},{15,13... | collective-permute-start | bytes 884744 | tf_op jit(solution)/shard_map/ppermute | solution.py:425
  22.8 1.8 %collective-permute-done.5.refs_5_ = bf16[1152,128]{1,0:T(8,128)(2,1)S(1)} collective-permute-done((bf16[1152,128]{1,0:T(8,128)(2,1)S(1)}, bf16[1152,128]{1,0:T(8,128)(2,1)S(1)}, u32[]{:S(2)}, u32[]{:S(2)}) %collective-permute-start.5) | collective-permute-done | bytes 294944 | tf_op jit(solution)/shard_map/ppermute | solution.py:425
  24.7 1.7 %collective-permute-start.9 = (bf16[1152,128]{1,0:T(8,128)(2,1)S(1)}, bf16[1152,128]{1,0:T(8,128)(2,1)S(1)}, u32[]{:S(2)}, u32[]{:S(2)}) collective-permute-start(bf16[1152,128]{1,0:T(8,128)(2,1)S(1)} %collective-permute-done.5.refs_5_), channel_id=1, source_target_pairs={{0,4},{1,3},{4,8},{5,1},{8,12},{9,5},{12,14},{13,9},{14,10},{15,13... | collective-permute-start | bytes 884744 | tf_op jit(solution)/shard_map/ppermute | solution.py:425
  26.4 3.9 %near.2.refs_10_ = f32[257,64,128]{2,1,0:T(8,128)S(1)} custom-call(s32[16,128]{1,0:T(8,128)S(1)} %pad_add_fusion.list_ref, bf16[1152,128]{1,0:T(8,128)(2,1)S(1)} %collective-permute-done.3.refs_0_, bf16[1152,128]{1,0:T(8,128)(2,1)S(1)} %collective-permute-done.refs_1_, ...), custom_call_target="tpu_custom_call", output_to_operand_aliasing={{}: (9, {})} | custom-call | flops 2147483648 | bytes 16777216 | tf_op jit(solution)/shard_map/near/pallas_call | solution.py:490
  30.3 1.0 %collective-permute-done.9.refs_7_ = bf16[1152,128]{1,0:T(8,128)(2,1)S(1)} collective-permute-done((bf16[1152,128]{1,0:T(8,128)(2,1)S(1)}, bf16[1152,128]{1,0:T(8,128)(2,1)S(1)}, u32[]{:S(2)}, u32[]{:S(2)}) %collective-permute-start.9) | collective-permute-done | bytes 294944 | tf_op jit(solution)/shard_map/ppermute | solution.py:425
  31.4 2.6 %near.3 = (f32[257,64,128]{2,1,0:T(8,128)S(1)}, bf16[1024,128]{1,0:T(8,128)(2,1)S(1)}, bf16[32,64,128]{2,1,0:T(8,128)(2,1)S(1)}, bf16[96,64,128]{2,1,0:T(8,128)(2,1)S(1)}) custom-call(s32[16,128]{1,0:T(8,128)S(1)} %pad_add_fusion.list_ref, bf16[1152,128]{1,0:T(8,128)(2,1)S(1)} %collective-permute-done.3.refs_0_, ...), custom_call_target="tpu_custom_call", output_to_operand_aliasing={{0}: (11, {})} | custom-call | flops 2147483648 | bytes 16777216 | tf_op jit(solution)/shard_map/near/pallas_call | solution.py:490
  34.1 1.9 %collective-permute-done.11 = bf16[32,64,128]{2,1,0:T(8,128)(2,1)S(1)} collective-permute-done((bf16[32,64,128]{2,1,0:T(8,128)(2,1)S(1)}, bf16[32,64,128]{2,1,0:T(8,128)(2,1)S(1)}, u32[]{:S(2)}, u32[]{:S(2)}) %collective-permute-start.11) | collective-permute-done | bytes 524320 | tf_op jit(solution)/shard_map/ppermute | solution.py:425
  36.4 1.7 %collective-permute-start.12 = (bf16[16,64,128]{2,1,0:T(8,128)(2,1)S(1)}, bf16[16,64,128]{2,1,0:T(8,128)(2,1)S(1)}, u32[]{:S(2)}, u32[]{:S(2)}) collective-permute-start(bf16[16,64,128]{2,1,0:T(8,128)(2,1)S(1)} %get-tuple-element.52), channel_id=1, source_target_pairs={{0,4},{1,3},{4,8},{5,1},{8,12},{9,5},{12,14},{13,9},{14,10},{15,13... | collective-permute-start | bytes 786440 | tf_op jit(solution)/shard_map/ppermute | solution.py:425
  38.1 1.9 %collective-permute-start.15 = (bf16[16,64,128]{2,1,0:T(8,128)(2,1)S(1)}, bf16[16,64,128]{2,1,0:T(8,128)(2,1)S(1)}, u32[]{:S(2)}, u32[]{:S(2)}) collective-permute-start(bf16[16,64,128]{2,1,0:T(8,128)(2,1)S(1)} %get-tuple-element.54), channel_id=1, source_target_pairs={{0,4},{1,3},{4,8},{5,1},{8,12},{9,5},{12,14},{13,9},{14,10},{15,13... | collective-permute-start | bytes 786440 | tf_op jit(solution)/shard_map/ppermute | solution.py:425
  40.0 3.4 %collective-permute-done.12 = bf16[16,64,128]{2,1,0:T(8,128)(2,1)S(1)} collective-permute-done((bf16[16,64,128]{2,1,0:T(8,128)(2,1)S(1)}, bf16[16,64,128]{2,1,0:T(8,128)(2,1)S(1)}, u32[]{:S(2)}, u32[]{:S(2)}) %collective-permute-start.12) | collective-permute-done | bytes 262176 | tf_op jit(solution)/shard_map/ppermute | solution.py:425
  43.5 1.1 %collective-permute-start.14 = (bf16[16,64,128]{2,1,0:T(8,128)(2,1)S(1)}, bf16[16,64,128]{2,1,0:T(8,128)(2,1)S(1)}, u32[]{:S(2)}, u32[]{:S(2)}) collective-permute-start(bf16[16,64,128]{2,1,0:T(8,128)(2,1)S(1)} %add_convert_fusion.5), channel_id=1, source_target_pairs={{0,4},{1,3},{4,8},{5,1},{8,12},{9,5},{12,14},{13,9},{14,10},{15,13... | collective-permute-start | bytes 786440 | tf_op jit(solution)/shard_map/ppermute | solution.py:425
  44.6 1.6 %collective-permute-done.15 = bf16[16,64,128]{2,1,0:T(8,128)(2,1)S(1)} collective-permute-done((bf16[16,64,128]{2,1,0:T(8,128)(2,1)S(1)}, bf16[16,64,128]{2,1,0:T(8,128)(2,1)S(1)}, u32[]{:S(2)}, u32[]{:S(2)}) %collective-permute-start.15) | collective-permute-done | bytes 262176 | tf_op jit(solution)/shard_map/ppermute | solution.py:425
  46.3 1.1 %collective-permute-start.17 = (bf16[16,64,128]{2,1,0:T(8,128)(2,1)S(1)}, bf16[16,64,128]{2,1,0:T(8,128)(2,1)S(1)}, u32[]{:S(2)}, u32[]{:S(2)}) collective-permute-start(bf16[16,64,128]{2,1,0:T(8,128)(2,1)S(1)} %add_convert_fusion.4), channel_id=1, source_target_pairs={{0,4},{1,3},{4,8},{5,1},{8,12},{9,5},{12,14},{13,9},{14,10},{15,13... | collective-permute-start | bytes 786440 | tf_op jit(solution)/shard_map/ppermute | solution.py:425
  47.5 2.5 %collective-permute-done.14 = bf16[16,64,128]{2,1,0:T(8,128)(2,1)S(1)} collective-permute-done((bf16[16,64,128]{2,1,0:T(8,128)(2,1)S(1)}, bf16[16,64,128]{2,1,0:T(8,128)(2,1)S(1)}, u32[]{:S(2)}, u32[]{:S(2)}) %collective-permute-start.14) | collective-permute-done | bytes 262176 | tf_op jit(solution)/shard_map/ppermute | solution.py:425
  50.1 1.1 %collective-permute-start.16 = (bf16[16,64,128]{2,1,0:T(8,128)(2,1)S(1)}, bf16[16,64,128]{2,1,0:T(8,128)(2,1)S(1)}, u32[]{:S(2)}, u32[]{:S(2)}) collective-permute-start(bf16[16,64,128]{2,1,0:T(8,128)(2,1)S(1)} %add_convert_fusion.3), channel_id=1, source_target_pairs={{0,4},{1,3},{4,8},{5,1},{8,12},{9,5},{12,14},{13,9},{14,10},{15,13... | collective-permute-start | bytes 786440 | tf_op jit(solution)/shard_map/ppermute | solution.py:425
  51.2 1.6 %collective-permute-done.17 = bf16[16,64,128]{2,1,0:T(8,128)(2,1)S(1)} collective-permute-done((bf16[16,64,128]{2,1,0:T(8,128)(2,1)S(1)}, bf16[16,64,128]{2,1,0:T(8,128)(2,1)S(1)}, u32[]{:S(2)}, u32[]{:S(2)}) %collective-permute-start.17) | collective-permute-done | bytes 262176 | tf_op jit(solution)/shard_map/ppermute | solution.py:425
  52.9 1.1 %collective-permute-start.19 = (bf16[16,64,128]{2,1,0:T(8,128)(2,1)S(1)}, bf16[16,64,128]{2,1,0:T(8,128)(2,1)S(1)}, u32[]{:S(2)}, u32[]{:S(2)}) collective-permute-start(bf16[16,64,128]{2,1,0:T(8,128)(2,1)S(1)} %add_convert_fusion.2), channel_id=1, source_target_pairs={{0,4},{1,3},{4,8},{5,1},{8,12},{9,5},{12,14},{13,9},{14,10},{15,13... | collective-permute-start | bytes 786440 | tf_op jit(solution)/shard_map/ppermute | solution.py:425
  54.0 2.5 %collective-permute-done.16 = bf16[16,64,128]{2,1,0:T(8,128)(2,1)S(1)} collective-permute-done((bf16[16,64,128]{2,1,0:T(8,128)(2,1)S(1)}, bf16[16,64,128]{2,1,0:T(8,128)(2,1)S(1)}, u32[]{:S(2)}, u32[]{:S(2)}) %collective-permute-start.16) | collective-permute-done | bytes 262176 | tf_op jit(solution)/shard_map/ppermute | solution.py:425
  56.6 1.1 %collective-permute-start.18 = (bf16[16,64,128]{2,1,0:T(8,128)(2,1)S(1)}, bf16[16,64,128]{2,1,0:T(8,128)(2,1)S(1)}, u32[]{:S(2)}, u32[]{:S(2)}) collective-permute-start(bf16[16,64,128]{2,1,0:T(8,128)(2,1)S(1)} %add_convert_fusion.1), channel_id=1, source_target_pairs={{0,4},{1,3},{4,8},{5,1},{8,12},{9,5},{12,14},{13,9},{14,10},{15,13... | collective-permute-start | bytes 786440 | tf_op jit(solution)/shard_map/ppermute | solution.py:425
  57.7 1.6 %collective-permute-done.19 = bf16[16,64,128]{2,1,0:T(8,128)(2,1)S(1)} collective-permute-done((bf16[16,64,128]{2,1,0:T(8,128)(2,1)S(1)}, bf16[16,64,128]{2,1,0:T(8,128)(2,1)S(1)}, u32[]{:S(2)}, u32[]{:S(2)}) %collective-permute-start.19) | collective-permute-done | bytes 262176 | tf_op jit(solution)/shard_map/ppermute | solution.py:425
  59.3 2.5 %far.1 = f32[16,64,128]{2,1,0:T(8,128)S(1)} custom-call(bf16[1024,128]{1,0:T(8,128)(2,1)S(1)} %get-tuple-element.49.refs_0_, bf16[1024,128]{1,0:T(8,128)(2,1)S(1)} %collective-permute-done.10.refs_1_, s32[1]{0:T(128)} %bitcast.me_ref.token_ref.refs_2_, bf16[16,16,256]{2,1,0:T(8,128)(2,1)S(1)} %bitcast.10, s32[1,256]{1,0:T(1,128)S(1)} %bitcast.11, ...), custom_call_target="tpu_custom_call" | custom-call | flops 536870912 | bytes 8388608 | tf_op jit(solution)/shard_map/far/pallas_call | solution.py:514
  61.9 1.3 %collective-permute-done.18 = bf16[16,64,128]{2,1,0:T(8,128)(2,1)S(1)} collective-permute-done((bf16[16,64,128]{2,1,0:T(8,128)(2,1)S(1)}, bf16[16,64,128]{2,1,0:T(8,128)(2,1)S(1)}, u32[]{:S(2)}, u32[]{:S(2)}) %collective-permute-start.18) | collective-permute-done | bytes 262176 | tf_op jit(solution)/shard_map/ppermute | solution.py:425
  (39 shorter events, 4.7 us)
Async XLA Ops:
  0.0 17.9 %collective-permute-start.2 = (bf16[128,128,128]{2,1,0:T(8,128)(2,1)}, bf16[128,128,128]{2,1,0:T(8,128)(2,1)}, u32[]{:S(2)}, u32[]{:S(2)}) collective-permute-start(bf16[128,128,128]{2,1,0:T(8,128)(2,1)} %refs_8_.1), channel_id=1, source_target_pairs={{0,1},{1,0},{2,3},{3,2},{4,5},{5,4},{6,7},{7,6},{8,9},{9,8},{10,11... | collective-permute-start | bytes 12582920 | tf_op jit(solution)/shard_map/ppermute | solution.py:425
  0.5 25.9 %copy-start = (bf16[128,128,128]{2,1,0:T(8,128)(2,1)S(1)}, bf16[128,128,128]{2,1,0:T(8,128)(2,1)}, u32[]{:S(2)}) copy-start(bf16[128,128,128]{2,1,0:T(8,128)(2,1)} %refs_8_.1) | copy-start | bytes 12582916
  2.7 4.1 %copy-start.6 = (bf16[1152,128]{1,0:T(8,128)(2,1)S(1)}, bf16[1152,128]{1,0:T(8,128)(2,1)}, u32[]{:S(2)}) copy-start(bf16[1152,128]{1,0:T(8,128)(2,1)} %get-tuple-element.41) | copy-start | bytes 884740
  2.7 12.7 %copy-start.5 = (s32[8,128]{1,0:T(8,128)S(1)}, s32[8,128]{1,0:T(8,128)}, u32[]{:S(2)}) copy-start(s32[8,128]{1,0:T(8,128)} %get-tuple-element.42) | copy-start | bytes 12292
  2.7 7.8 %collective-permute-start = (bf16[1152,128]{1,0:T(8,128)(2,1)}, bf16[1152,128]{1,0:T(8,128)(2,1)S(1)}, u32[]{:S(2)}, u32[]{:S(2)}) collective-permute-start(bf16[1152,128]{1,0:T(8,128)(2,1)} %get-tuple-element.41), channel_id=1, source_target_pairs={{0,4},{1,3},{4,8},{5,1},{8,12},{9,5},{12,14},{13,9},{14,10},{15,13... | collective-permute-start | bytes 884744 | tf_op jit(solution)/shard_map/ppermute | solution.py:425
  6.9 6.5 %collective-permute-start.6 = (bf16[1152,128]{1,0:T(8,128)(2,1)S(1)}, bf16[1152,128]{1,0:T(8,128)(2,1)S(1)}, u32[]{:S(2)}, u32[]{:S(2)}) collective-permute-start(bf16[1152,128]{1,0:T(8,128)(2,1)S(1)} %copy-done.6), channel_id=1, source_target_pairs={{0,3},{1,4},{4,1},{5,8},{8,5},{9,12},{12,9},{13,14},{14,13},{15,10... | collective-permute-start | bytes 884744 | tf_op jit(solution)/shard_map/ppermute | solution.py:425
  8.3 8.3 %collective-permute-start.3 = (bf16[1152,128]{1,0:T(8,128)(2,1)S(1)}, bf16[1152,128]{1,0:T(8,128)(2,1)S(1)}, u32[]{:S(2)}, u32[]{:S(2)}) collective-permute-start(bf16[1152,128]{1,0:T(8,128)(2,1)S(1)} %copy-done.6), channel_id=1, source_target_pairs={{0,1},{1,0},{2,3},{3,2},{4,5},{5,4},{6,7},{7,6},{8,9},{9,8},{10,11... | collective-permute-start | bytes 884744 | tf_op jit(solution)/shard_map/ppermute | solution.py:425
  10.6 7.4 %collective-permute-start.1 = (bf16[1152,128]{1,0:T(8,128)(2,1)S(1)}, bf16[1152,128]{1,0:T(8,128)(2,1)S(1)}, u32[]{:S(2)}, u32[]{:S(2)}) collective-permute-start(bf16[1152,128]{1,0:T(8,128)(2,1)S(1)} %collective-permute-done.refs_1_), channel_id=1, source_target_pairs={{0,4},{1,3},{4,8},{5,1},{8,12},{9,5},{12,14},{13,9},{14,10},{15,13... | collective-permute-start | bytes 884744 | tf_op jit(solution)/shard_map/ppermute | solution.py:425
  13.4 7.7 %collective-permute-start.7 = (bf16[1152,128]{1,0:T(8,128)(2,1)S(1)}, bf16[1152,128]{1,0:T(8,128)(2,1)S(1)}, u32[]{:S(2)}, u32[]{:S(2)}) collective-permute-start(bf16[1152,128]{1,0:T(8,128)(2,1)S(1)} %collective-permute-done.6.refs_2_), channel_id=1, source_target_pairs={{0,4},{1,3},{4,8},{5,1},{8,12},{9,5},{12,14},{13,9},{14,10},{15,13... | collective-permute-start | bytes 884744 | tf_op jit(solution)/shard_map/ppermute | solution.py:425
  15.4 1.2 %collective-permute-start.4 = (s32[8,128]{1,0:T(8,128)S(1)}, s32[8,128]{1,0:T(8,128)S(1)}, u32[]{:S(2)}, u32[]{:S(2)}) collective-permute-start(s32[8,128]{1,0:T(8,128)S(1)} %copy-done.5), channel_id=1, source_target_pairs={{0,1},{1,0},{2,3},{3,2},{4,5},{5,4},{6,7},{7,6},{8,9},{9,8},{10,11... | collective-permute-start | bytes 12296 | tf_op jit(solution)/shard_map/ppermute | solution.py:425
  17.9 6.7 %collective-permute-start.5 = (bf16[1152,128]{1,0:T(8,128)(2,1)S(1)}, bf16[1152,128]{1,0:T(8,128)(2,1)S(1)}, u32[]{:S(2)}, u32[]{:S(2)}) collective-permute-start(bf16[1152,128]{1,0:T(8,128)(2,1)S(1)} %collective-permute-done.1.refs_3_), channel_id=1, source_target_pairs={{0,4},{1,3},{4,8},{5,1},{8,12},{9,5},{12,14},{13,9},{14,10},{15,13... | collective-permute-start | bytes 884744 | tf_op jit(solution)/shard_map/ppermute | solution.py:425
  21.1 9.2 %collective-permute-start.8 = (bf16[1152,128]{1,0:T(8,128)(2,1)S(1)}, bf16[1152,128]{1,0:T(8,128)(2,1)S(1)}, u32[]{:S(2)}, u32[]{:S(2)}) collective-permute-start(bf16[1152,128]{1,0:T(8,128)(2,1)S(1)} %collective-permute-done.7.refs_4_), channel_id=1, source_target_pairs={{0,4},{1,3},{4,8},{5,1},{8,12},{9,5},{12,14},{13,9},{14,10},{15,13... | collective-permute-start | bytes 884744 | tf_op jit(solution)/shard_map/ppermute | solution.py:425
  24.7 6.7 %collective-permute-start.9 = (bf16[1152,128]{1,0:T(8,128)(2,1)S(1)}, bf16[1152,128]{1,0:T(8,128)(2,1)S(1)}, u32[]{:S(2)}, u32[]{:S(2)}) collective-permute-start(bf16[1152,128]{1,0:T(8,128)(2,1)S(1)} %collective-permute-done.5.refs_5_), channel_id=1, source_target_pairs={{0,4},{1,3},{4,8},{5,1},{8,12},{9,5},{12,14},{13,9},{14,10},{15,13... | collective-permute-start | bytes 884744 | tf_op jit(solution)/shard_map/ppermute | solution.py:425
  34.0 25.3 %copy-start.1 = (bf16[16,16,128]{2,1,0:T(8,128)(2,1)S(1)}, bf16[16,16,128]{2,1,0:T(8,128)(2,1)}, u32[]{:S(2)}) copy-start(bf16[16,16,128]{2,1,0:T(8,128)(2,1)} %refs_7_.1) | copy-start | bytes 196612
  34.0 25.3 %copy-start.2 = (s32[256]{0:T(256)S(1)}, s32[256]{0:T(256)}, u32[]{:S(2)}) copy-start(s32[256]{0:T(256)} %param.17) | copy-start | bytes 3076
  34.0 25.3 %copy-start.3 = (s32[256,1]{0,1:T(1,128)S(1)}, s32[256,1]{0,1:T(1,128)}, u32[]{:S(2)}) copy-start(s32[256,1]{0,1:T(1,128)} %param.18) | copy-start | bytes 3076
  34.0 25.3 %copy-start.4 = (s32[256]{0:T(256)S(1)}, s32[256]{0:T(256)}, u32[]{:S(2)}) copy-start(s32[256]{0:T(256)} %param.19) | copy-start | bytes 3076
  34.0 2.0 %collective-permute-start.11 = (bf16[32,64,128]{2,1,0:T(8,128)(2,1)S(1)}, bf16[32,64,128]{2,1,0:T(8,128)(2,1)S(1)}, u32[]{:S(2)}, u32[]{:S(2)}) collective-permute-start(bf16[32,64,128]{2,1,0:T(8,128)(2,1)S(1)} %get-tuple-element.51), channel_id=1, source_target_pairs={{0,1},{1,0},{2,3},{3,2},{4,5},{5,4},{6,7},{7,6},{8,9},{9,8},{10,11... | collective-permute-start | bytes 1572872 | tf_op jit(solution)/shard_map/ppermute | solution.py:425
  36.2 7.2 %collective-permute-start.13 = (bf16[96,64,128]{2,1,0:T(8,128)(2,1)S(1)}, bf16[96,64,128]{2,1,0:T(8,128)(2,1)S(1)}, u32[]{:S(2)}, u32[]{:S(2)}) collective-permute-start(bf16[96,64,128]{2,1,0:T(8,128)(2,1)S(1)} %get-tuple-element.55), channel_id=1, source_target_pairs={{0,1},{1,0},{2,3},{3,2},{4,5},{5,4},{6,7},{7,6},{8,9},{9,8},{10,11... | collective-permute-start | bytes 4718600 | tf_op jit(solution)/shard_map/ppermute | solution.py:425
  36.4 7.0 %collective-permute-start.12 = (bf16[16,64,128]{2,1,0:T(8,128)(2,1)S(1)}, bf16[16,64,128]{2,1,0:T(8,128)(2,1)S(1)}, u32[]{:S(2)}, u32[]{:S(2)}) collective-permute-start(bf16[16,64,128]{2,1,0:T(8,128)(2,1)S(1)} %get-tuple-element.52), channel_id=1, source_target_pairs={{0,4},{1,3},{4,8},{5,1},{8,12},{9,5},{12,14},{13,9},{14,10},{15,13... | collective-permute-start | bytes 786440 | tf_op jit(solution)/shard_map/ppermute | solution.py:425
  38.1 8.1 %collective-permute-start.15 = (bf16[16,64,128]{2,1,0:T(8,128)(2,1)S(1)}, bf16[16,64,128]{2,1,0:T(8,128)(2,1)S(1)}, u32[]{:S(2)}, u32[]{:S(2)}) collective-permute-start(bf16[16,64,128]{2,1,0:T(8,128)(2,1)S(1)} %get-tuple-element.54), channel_id=1, source_target_pairs={{0,4},{1,3},{4,8},{5,1},{8,12},{9,5},{12,14},{13,9},{14,10},{15,13... | collective-permute-start | bytes 786440 | tf_op jit(solution)/shard_map/ppermute | solution.py:425
  43.5 6.4 %collective-permute-start.14 = (bf16[16,64,128]{2,1,0:T(8,128)(2,1)S(1)}, bf16[16,64,128]{2,1,0:T(8,128)(2,1)S(1)}, u32[]{:S(2)}, u32[]{:S(2)}) collective-permute-start(bf16[16,64,128]{2,1,0:T(8,128)(2,1)S(1)} %add_convert_fusion.5), channel_id=1, source_target_pairs={{0,4},{1,3},{4,8},{5,1},{8,12},{9,5},{12,14},{13,9},{14,10},{15,13... | collective-permute-start | bytes 786440 | tf_op jit(solution)/shard_map/ppermute | solution.py:425
  46.3 6.4 %collective-permute-start.17 = (bf16[16,64,128]{2,1,0:T(8,128)(2,1)S(1)}, bf16[16,64,128]{2,1,0:T(8,128)(2,1)S(1)}, u32[]{:S(2)}, u32[]{:S(2)}) collective-permute-start(bf16[16,64,128]{2,1,0:T(8,128)(2,1)S(1)} %add_convert_fusion.4), channel_id=1, source_target_pairs={{0,4},{1,3},{4,8},{5,1},{8,12},{9,5},{12,14},{13,9},{14,10},{15,13... | collective-permute-start | bytes 786440 | tf_op jit(solution)/shard_map/ppermute | solution.py:425
  50.1 6.4 %collective-permute-start.16 = (bf16[16,64,128]{2,1,0:T(8,128)(2,1)S(1)}, bf16[16,64,128]{2,1,0:T(8,128)(2,1)S(1)}, u32[]{:S(2)}, u32[]{:S(2)}) collective-permute-start(bf16[16,64,128]{2,1,0:T(8,128)(2,1)S(1)} %add_convert_fusion.3), channel_id=1, source_target_pairs={{0,4},{1,3},{4,8},{5,1},{8,12},{9,5},{12,14},{13,9},{14,10},{15,13... | collective-permute-start | bytes 786440 | tf_op jit(solution)/shard_map/ppermute | solution.py:425
  51.2 8.1 %collective-permute-start.10 = (bf16[1024,128]{1,0:T(8,128)(2,1)S(1)}, bf16[1024,128]{1,0:T(8,128)(2,1)S(1)}, u32[]{:S(2)}, u32[]{:S(2)}) collective-permute-start(bf16[1024,128]{1,0:T(8,128)(2,1)S(1)} %get-tuple-element.49.refs_0_), channel_id=1, source_target_pairs={{0,1},{1,0},{2,3},{3,2},{4,5},{5,4},{6,7},{7,6},{8,9},{9,8},{10,11... | collective-permute-start | bytes 786440 | tf_op jit(solution)/shard_map/ppermute | solution.py:425
  52.9 6.4 %collective-permute-start.19 = (bf16[16,64,128]{2,1,0:T(8,128)(2,1)S(1)}, bf16[16,64,128]{2,1,0:T(8,128)(2,1)S(1)}, u32[]{:S(2)}, u32[]{:S(2)}) collective-permute-start(bf16[16,64,128]{2,1,0:T(8,128)(2,1)S(1)} %add_convert_fusion.2), channel_id=1, source_target_pairs={{0,4},{1,3},{4,8},{5,1},{8,12},{9,5},{12,14},{13,9},{14,10},{15,13... | collective-permute-start | bytes 786440 | tf_op jit(solution)/shard_map/ppermute | solution.py:425
  56.6 6.6 %collective-permute-start.18 = (bf16[16,64,128]{2,1,0:T(8,128)(2,1)S(1)}, bf16[16,64,128]{2,1,0:T(8,128)(2,1)S(1)}, u32[]{:S(2)}, u32[]{:S(2)}) collective-permute-start(bf16[16,64,128]{2,1,0:T(8,128)(2,1)S(1)} %add_convert_fusion.1), channel_id=1, source_target_pairs={{0,4},{1,3},{4,8},{5,1},{8,12},{9,5},{12,14},{13,9},{14,10},{15,13... | collective-permute-start | bytes 786440 | tf_op jit(solution)/shard_map/ppermute | solution.py:425
  59.3 4.0 %collective-permute-start.20 = (bf16[16,64,128]{2,1,0:T(8,128)(2,1)S(1)}, bf16[16,64,128]{2,1,0:T(8,128)(2,1)S(1)}, u32[]{:S(2)}, u32[]{:S(2)}) collective-permute-start(bf16[16,64,128]{2,1,0:T(8,128)(2,1)S(1)} %collective-permute-done.19), channel_id=1, source_target_pairs={{0,1},{1,0},{2,3},{3,2},{4,5},{5,4},{6,7},{7,6},{8,9},{9,8},{10,11... | collective-permute-start | bytes 786440 | tf_op jit(solution)/shard_map/ppermute | solution.py:425

commit v25 on v24

--- a/solution.py
+++ b/solution.py
@@ -193,8 +193,10 @@
     (own_ref, mate_hbm), refs = refs[:2], refs[3:]
     sums, refs = refs[0], refs[1:]
     if late:
-        coef_ref, send_refs, refs = refs[0], refs[1 : 1 + sends], refs[1 + sends :]
-    columns, blocks, block_sem = refs
+        coef_ref, send_refs, (columns,) = refs[0], refs[1 : 1 + sends], refs[1 + sends :]
+        blocks = mate_hbm
+    else:
+        blocks, columns, block_sem = refs
     stored = blocks.shape[0]
     directions = sums.shape[1]
     span = columns.shape[0] // used
@@ -203,18 +205,7 @@
 
     begin, end = list_ref[3, late], list_ref[3, late + 1]
     begin_there, end_there = list_ref[11, 2 + late], list_ref[11, 3 + late]
-    steps_there = (end_there - begin_there + batch - 1) // batch
-
-    def fetch(j, carry):
-        at = jnp.minimum(begin_there + j, end_there - 1)
-        pltpu.make_async_copy(
-            mate_hbm.at[list_ref[8, at]], blocks.at[j], block_sem.at[j // batch]
-        ).start()
-        return carry
-
-    if late:
-        lax.fori_loop(0, steps_there * batch, fetch, 0)
-    else:
+    if not late:
         for c in range(CHUNKS):
             at = pl.ds(c * chunk, chunk)
             pltpu.make_async_copy(mate_hbm.at[at], blocks.at[at], block_sem.at[c]).start()
@@ -272,16 +263,12 @@
         return carry
 
     def mate_blocks(first, entry, ready):
+        take = lambda i: blocks[list_ref[8, entry(first + i)]]
         if late:
-            pltpu.make_async_copy(
-                mate_hbm.at[pl.ds(0, batch)],
-                blocks.at[pl.ds(first, batch)],
-                block_sem.at[first // batch],
-            ).wait()
-            return lambda i: blocks[first + i], ready
+            return take, ready
         needed = list_ref[8, entry(first + batch - 1)] // chunk + 1
         lax.fori_loop(ready, needed, wait, 0)
-        return lambda i: blocks[list_ref[8, entry(first + i)]], jnp.maximum(ready, needed)
+        return take, jnp.maximum(ready, needed)
 
     run(begin, end, 0, 0, own_blocks)
     ready = run(begin_there, end_there, 8, dummy // 2, mate_blocks)
@@ -485,11 +472,12 @@
 
     pieces = [2, chips - 2]
 
-    def near(late, shards, sums):
+    def near(late, shards, theirs, sums):
         sends = pieces if late else []
         return pl.pallas_call(
             functools.partial(near_kernel, late, BATCH[late], len(shards), len(sends)),
             out_shape=[sums_shape]
+            + [jax.ShapeDtypeStruct(near_blocks.shape, near_blocks.dtype)] * (1 - late)
             + [jax.ShapeDtypeStruct((chips * half * rank_k, unknowns), jnp.bfloat16)] * late
             + [
                 jax.ShapeDtypeStruct((size * clusters, directions, unknowns), jnp.bfloat16)
@@ -497,18 +485,17 @@
             ],
             in_specs=[whole(pltpu.SMEM)]
             + [whole()] * len(shards)
-            + [whole(), whole(pl.ANY), whole()],
-            out_specs=[whole()] * (1 + late + len(sends)),
+            + [whole(), whole() if late else whole(pl.ANY), whole()],
+            out_specs=[whole()] * (2 + len(sends)),
             input_output_aliases={3 + len(shards): 0},
             scratch_shapes=[
                 pltpu.VMEM(((LATE if late else len(shards)) * base, unknowns), jnp.bfloat16),
-                pltpu.VMEM(near_blocks.shape, jnp.bfloat16),
-                pltpu.SemaphoreType.DMA((max(CHUNKS, stored // BATCH[late]),)),
-            ],
+            ]
+            + [pltpu.SemaphoreType.DMA((CHUNKS,))] * (1 - late),
             compiler_params=pltpu.CompilerParams(vmem_limit_bytes=NEAR_VMEM),
             cost_estimate=cost,
             name="near",
-        )(lists, *shards, near_blocks, mate_blocks, sums)
+        )(lists, *shards, near_blocks, theirs, sums)
 
     def far_field(couple):
         return pl.pallas_call(
@@ -533,8 +520,8 @@
             basis_out,
         )
 
-    (sums,) = near(0, shards[: chips - LATE], sums)
-    sums, coef, *sends = near(1, shards, sums)
+    sums, mate_blocks = near(0, shards[: chips - LATE], mate_blocks, sums)
+    sums, coef, *sends = near(1, shards, mate_blocks, sums)
     mates = [move(sends[0], mate)]
     coefs = [coef, move(coef, mate)]
 

time: 64.5 us -> 63.2 us (0.980)
  waiting for transfers between devices: 25.6 us -> 19.8 us
  starting transfers between devices: 23.9 us -> 28.2 us
    ppermute x21, waiting for transfers between devices: 25.6 us -> 19.8 us  [move(): return lax.ppermute(values, 'blk', where)]
    ppermute x21, starting transfers between devices: 23.9 us -> 28.2 us  [move(): return lax.ppermute(values, 'blk', where)]
  transfers between devices with their start and end apart: 21 -> 21, of which waited for: 15 -> 15; matrix products, arithmetic and copies ran while one was open for 3% -> 3% of each run, Pallas kernels for 14% -> 15%
where the time goes in v25:
time: 63.2 us; the launch traced here: 62.9 us
  starting transfers between devices  28.2 us (45%)
  waiting for transfers between devices  19.8 us (31%)
  Pallas kernels  11.7 us (19%)
  other arithmetic  1.62 us (3%)
  local copies, waits for them, and re-layouts  1.32 us (2%)
    ppermute x21, starting transfers between devices, move(): return lax.ppermute(values, 'blk', where)  28.2 us
    ppermute x21, waiting for transfers between devices, move(): return lax.ppermute(values, 'blk', where)  19.8 us
    pallas_call x2, Pallas kernels, near(): pl.pallas_call(functools.partial(near_kernel, late, BATCH[late], len(shar...  6.53 us
    pallas_call x1, Pallas kernels, far_field(): pl.pallas_call(far_kernel, out_shape=jax.ShapeDtypeStruct((clusters, dire...  2.5 us
    pallas_call x1, Pallas kernels, stationary(): pl.pallas_call(functools.partial(prologue_kernel, count), out_shape=[jax....  2.13 us
    unnamed x15, local copies, waits for them, and re-layouts  1.32 us
  transfers between devices with their start and end apart: 21, of which 15 were waited for; matrix products, arithmetic and copies ran while one was open for 3% of the time, Pallas kernels for 15%

profile of v25, /device:TPU:0, one launch (start us, length us, event | category | flops | bytes accessed | tf_op | source)
XLA Modules:
  0.0 62.9 jit_solution(14025519061277517867)
XLA Ops:
  0.5 2.1 %prologue.1 = (bf16[1152,128]{1,0:T(8,128)(2,1)}, s32[8,128]{1,0:T(8,128)}) custom-call(s32[1]{0:T(128)} %bitcast.me_ref.token_ref.refs_2_, s32[1,128]{1,0:T(1,128)} %bitcast.14, s32[1,128]{1,0:T(1,128)} %bitcast.15, s32[1,128]{1,0:T(1,128)} %bitcast.16, bf16[16,64,128]{2,1,0:T(8,128)(2,1)} %rhs_ref.1, bf16[16,16,128]{2,1,0:T(8,128)(2,1)} %basis_ref.1), custom_call_target="tpu_custom_call" | custom-call | tf_op jit(solution)/shard_map/prologue/pallas_call | solution.py:419
  2.6 2.6 %collective-permute-start = (bf16[1152,128]{1,0:T(8,128)(2,1)}, bf16[1152,128]{1,0:T(8,128)(2,1)S(1)}, u32[]{:S(2)}, u32[]{:S(2)}) collective-permute-start(bf16[1152,128]{1,0:T(8,128)(2,1)} %get-tuple-element.43), channel_id=1, source_target_pairs={{0,4},{1,3},{4,8},{5,1},{8,12},{9,5},{12,14},{13,9},{14,10},{15,13... | collective-permute-start | bytes 884744 | tf_op jit(solution)/shard_map/ppermute | solution.py:412
  5.2 0.9 %copy.16 = bf16[256,16,16]{0,1,2:T(8,128)(2,1)S(1)} copy(bf16[256,16,16]{0,2,1:T(8,128)(2,1)} %param.16) | data formatting | bytes 262144 | tf_op args[5]
  7.1 1.4 %collective-permute-start.6 = (bf16[1152,128]{1,0:T(8,128)(2,1)S(1)}, bf16[1152,128]{1,0:T(8,128)(2,1)S(1)}, u32[]{:S(2)}, u32[]{:S(2)}) collective-permute-start(bf16[1152,128]{1,0:T(8,128)(2,1)S(1)} %copy-done.6), channel_id=1, source_target_pairs={{0,3},{1,4},{4,1},{5,8},{8,5},{9,12},{12,9},{13,14},{14,13},{15,10... | collective-permute-start | bytes 884744 | tf_op jit(solution)/shard_map/ppermute | solution.py:412
  8.8 1.3 %collective-permute-done.refs_1_ = bf16[1152,128]{1,0:T(8,128)(2,1)S(1)} collective-permute-done((bf16[1152,128]{1,0:T(8,128)(2,1)}, bf16[1152,128]{1,0:T(8,128)(2,1)S(1)}, u32[]{:S(2)}, u32[]{:S(2)}) %collective-permute-start) | collective-permute-done | bytes 294944 | tf_op jit(solution)/shard_map/ppermute | solution.py:412
  10.1 2.4 %collective-permute-start.1 = (bf16[1152,128]{1,0:T(8,128)(2,1)S(1)}, bf16[1152,128]{1,0:T(8,128)(2,1)S(1)}, u32[]{:S(2)}, u32[]{:S(2)}) collective-permute-start(bf16[1152,128]{1,0:T(8,128)(2,1)S(1)} %collective-permute-done.refs_1_), channel_id=1, source_target_pairs={{0,4},{1,3},{4,8},{5,1},{8,12},{9,5},{12,14},{13,9},{14,10},{15,13... | collective-permute-start | bytes 884744 | tf_op jit(solution)/shard_map/ppermute | solution.py:412
  12.5 1.0 %collective-permute-done.6.refs_2_ = bf16[1152,128]{1,0:T(8,128)(2,1)S(1)} collective-permute-done((bf16[1152,128]{1,0:T(8,128)(2,1)S(1)}, bf16[1152,128]{1,0:T(8,128)(2,1)S(1)}, u32[]{:S(2)}, u32[]{:S(2)}) %collective-permute-start.6) | collective-permute-done | bytes 294944 | tf_op jit(solution)/shard_map/ppermute | solution.py:412
  13.5 1.8 %collective-permute-start.7 = (bf16[1152,128]{1,0:T(8,128)(2,1)S(1)}, bf16[1152,128]{1,0:T(8,128)(2,1)S(1)}, u32[]{:S(2)}, u32[]{:S(2)}) collective-permute-start(bf16[1152,128]{1,0:T(8,128)(2,1)S(1)} %collective-permute-done.6.refs_2_), channel_id=1, source_target_pairs={{0,4},{1,3},{4,8},{5,1},{8,12},{9,5},{12,14},{13,9},{14,10},{15,13... | collective-permute-start | bytes 884744 | tf_op jit(solution)/shard_map/ppermute | solution.py:412
  15.5 0.9 %collective-permute-done.4 = s32[8,128]{1,0:T(8,128)S(1)} collective-permute-done((s32[8,128]{1,0:T(8,128)S(1)}, s32[8,128]{1,0:T(8,128)S(1)}, u32[]{:S(2)}, u32[]{:S(2)}) %collective-permute-start.4) | collective-permute-done | bytes 4128 | tf_op jit(solution)/shard_map/ppermute | solution.py:412
  16.4 1.0 %collective-permute-done.1.refs_3_ = bf16[1152,128]{1,0:T(8,128)(2,1)S(1)} collective-permute-done((bf16[1152,128]{1,0:T(8,128)(2,1)S(1)}, bf16[1152,128]{1,0:T(8,128)(2,1)S(1)}, u32[]{:S(2)}, u32[]{:S(2)}) %collective-permute-start.1) | collective-permute-done | bytes 294944 | tf_op jit(solution)/shard_map/ppermute | solution.py:412
  17.5 1.7 %collective-permute-start.5 = (bf16[1152,128]{1,0:T(8,128)(2,1)S(1)}, bf16[1152,128]{1,0:T(8,128)(2,1)S(1)}, u32[]{:S(2)}, u32[]{:S(2)}) collective-permute-start(bf16[1152,128]{1,0:T(8,128)(2,1)S(1)} %collective-permute-done.1.refs_3_), channel_id=1, source_target_pairs={{0,4},{1,3},{4,8},{5,1},{8,12},{9,5},{12,14},{13,9},{14,10},{15,13... | collective-permute-start | bytes 884744 | tf_op jit(solution)/shard_map/ppermute | solution.py:412
  19.2 1.4 %collective-permute-done.7.refs_4_ = bf16[1152,128]{1,0:T(8,128)(2,1)S(1)} collective-permute-done((bf16[1152,128]{1,0:T(8,128)(2,1)S(1)}, bf16[1152,128]{1,0:T(8,128)(2,1)S(1)}, u32[]{:S(2)}, u32[]{:S(2)}) %collective-permute-start.7) | collective-permute-done | bytes 294944 | tf_op jit(solution)/shard_map/ppermute | solution.py:412
  20.6 1.7 %collective-permute-start.8 = (bf16[1152,128]{1,0:T(8,128)(2,1)S(1)}, bf16[1152,128]{1,0:T(8,128)(2,1)S(1)}, u32[]{:S(2)}, u32[]{:S(2)}) collective-permute-start(bf16[1152,128]{1,0:T(8,128)(2,1)S(1)} %collective-permute-done.7.refs_4_), channel_id=1, source_target_pairs={{0,4},{1,3},{4,8},{5,1},{8,12},{9,5},{12,14},{13,9},{14,10},{15,13... | collective-permute-start | bytes 884744 | tf_op jit(solution)/shard_map/ppermute | solution.py:412
  22.4 1.8 %collective-permute-done.5.refs_5_ = bf16[1152,128]{1,0:T(8,128)(2,1)S(1)} collective-permute-done((bf16[1152,128]{1,0:T(8,128)(2,1)S(1)}, bf16[1152,128]{1,0:T(8,128)(2,1)S(1)}, u32[]{:S(2)}, u32[]{:S(2)}) %collective-permute-start.5) | collective-permute-done | bytes 294944 | tf_op jit(solution)/shard_map/ppermute | solution.py:412
  24.2 1.7 %collective-permute-start.9 = (bf16[1152,128]{1,0:T(8,128)(2,1)S(1)}, bf16[1152,128]{1,0:T(8,128)(2,1)S(1)}, u32[]{:S(2)}, u32[]{:S(2)}) collective-permute-start(bf16[1152,128]{1,0:T(8,128)(2,1)S(1)} %collective-permute-done.5.refs_5_), channel_id=1, source_target_pairs={{0,4},{1,3},{4,8},{5,1},{8,12},{9,5},{12,14},{13,9},{14,10},{15,13... | collective-permute-start | bytes 884744 | tf_op jit(solution)/shard_map/ppermute | solution.py:412
  25.9 4.0 %near.2 = (f32[257,64,128]{2,1,0:T(8,128)S(1)}, bf16[128,128,128]{2,1,0:T(8,128)(2,1)S(1)}) custom-call(s32[16,128]{1,0:T(8,128)S(1)} %pad_add_fusion.list_ref, bf16[1152,128]{1,0:T(8,128)(2,1)S(1)} %collective-permute-done.3.refs_0_, bf16[1152,128]{1,0:T(8,128)(2,1)S(1)} %collective-permute-done.refs_1_, ...), custom_call_target="tpu_custom_call", output_to_operand_aliasing={{0}: (9, {})} | custom-call | flops 2147483648 | bytes 16777216 | tf_op jit(solution)/shard_map/near/pallas_call | solution.py:477
  30.0 1.0 %collective-permute-done.9.refs_7_ = bf16[1152,128]{1,0:T(8,128)(2,1)S(1)} collective-permute-done((bf16[1152,128]{1,0:T(8,128)(2,1)S(1)}, bf16[1152,128]{1,0:T(8,128)(2,1)S(1)}, u32[]{:S(2)}, u32[]{:S(2)}) %collective-permute-start.9) | collective-permute-done | bytes 294944 | tf_op jit(solution)/shard_map/ppermute | solution.py:412
  30.9 2.5 %near.3 = (f32[257,64,128]{2,1,0:T(8,128)S(1)}, bf16[1024,128]{1,0:T(8,128)(2,1)S(1)}, bf16[32,64,128]{2,1,0:T(8,128)(2,1)S(1)}, bf16[96,64,128]{2,1,0:T(8,128)(2,1)S(1)}) custom-call(s32[16,128]{1,0:T(8,128)S(1)} %pad_add_fusion.list_ref, bf16[1152,128]{1,0:T(8,128)(2,1)S(1)} %collective-permute-done.3.refs_0_, ...), custom_call_target="tpu_custom_call", output_to_operand_aliasing={{0}: (11, {})} | custom-call | flops 2147483648 | bytes 16777216 | tf_op jit(solution)/shard_map/near/pallas_call | solution.py:477
  33.5 1.9 %collective-permute-done.11 = bf16[32,64,128]{2,1,0:T(8,128)(2,1)S(1)} collective-permute-done((bf16[32,64,128]{2,1,0:T(8,128)(2,1)S(1)}, bf16[32,64,128]{2,1,0:T(8,128)(2,1)S(1)}, u32[]{:S(2)}, u32[]{:S(2)}) %collective-permute-start.11) | collective-permute-done | bytes 524320 | tf_op jit(solution)/shard_map/ppermute | solution.py:412
  35.8 2.0 %collective-permute-start.12 = (bf16[16,64,128]{2,1,0:T(8,128)(2,1)S(1)}, bf16[16,64,128]{2,1,0:T(8,128)(2,1)S(1)}, u32[]{:S(2)}, u32[]{:S(2)}) collective-permute-start(bf16[16,64,128]{2,1,0:T(8,128)(2,1)S(1)} %get-tuple-element.56), channel_id=1, source_target_pairs={{0,4},{1,3},{4,8},{5,1},{8,12},{9,5},{12,14},{13,9},{14,10},{15,13... | collective-permute-start | bytes 786440 | tf_op jit(solution)/shard_map/ppermute | solution.py:412
  37.8 1.3 %collective-permute-start.15 = (bf16[16,64,128]{2,1,0:T(8,128)(2,1)S(1)}, bf16[16,64,128]{2,1,0:T(8,128)(2,1)S(1)}, u32[]{:S(2)}, u32[]{:S(2)}) collective-permute-start(bf16[16,64,128]{2,1,0:T(8,128)(2,1)S(1)} %get-tuple-element.58), channel_id=1, source_target_pairs={{0,4},{1,3},{4,8},{5,1},{8,12},{9,5},{12,14},{13,9},{14,10},{15,13... | collective-permute-start | bytes 786440 | tf_op jit(solution)/shard_map/ppermute | solution.py:412
  39.1 3.1 %collective-permute-done.12 = bf16[16,64,128]{2,1,0:T(8,128)(2,1)S(1)} collective-permute-done((bf16[16,64,128]{2,1,0:T(8,128)(2,1)S(1)}, bf16[16,64,128]{2,1,0:T(8,128)(2,1)S(1)}, u32[]{:S(2)}, u32[]{:S(2)}) %collective-permute-start.12) | collective-permute-done | bytes 262176 | tf_op jit(solution)/shard_map/ppermute | solution.py:412
  42.3 2.1 %collective-permute-start.14 = (bf16[16,64,128]{2,1,0:T(8,128)(2,1)S(1)}, bf16[16,64,128]{2,1,0:T(8,128)(2,1)S(1)}, u32[]{:S(2)}, u32[]{:S(2)}) collective-permute-start(bf16[16,64,128]{2,1,0:T(8,128)(2,1)S(1)} %add_convert_fusion.5), channel_id=1, source_target_pairs={{0,4},{1,3},{4,8},{5,1},{8,12},{9,5},{12,14},{13,9},{14,10},{15,13... | collective-permute-start | bytes 786440 | tf_op jit(solution)/shard_map/ppermute | solution.py:412
  45.1 2.1 %collective-permute-start.17 = (bf16[16,64,128]{2,1,0:T(8,128)(2,1)S(1)}, bf16[16,64,128]{2,1,0:T(8,128)(2,1)S(1)}, u32[]{:S(2)}, u32[]{:S(2)}) collective-permute-start(bf16[16,64,128]{2,1,0:T(8,128)(2,1)S(1)} %add_convert_fusion.4), channel_id=1, source_target_pairs={{0,4},{1,3},{4,8},{5,1},{8,12},{9,5},{12,14},{13,9},{14,10},{15,13... | collective-permute-start | bytes 786440 | tf_op jit(solution)/shard_map/ppermute | solution.py:412
  47.2 1.5 %collective-permute-done.14 = bf16[16,64,128]{2,1,0:T(8,128)(2,1)S(1)} collective-permute-done((bf16[16,64,128]{2,1,0:T(8,128)(2,1)S(1)}, bf16[16,64,128]{2,1,0:T(8,128)(2,1)S(1)}, u32[]{:S(2)}, u32[]{:S(2)}) %collective-permute-start.14) | collective-permute-done | bytes 262176 | tf_op jit(solution)/shard_map/ppermute | solution.py:412
  48.8 2.1 %collective-permute-start.16 = (bf16[16,64,128]{2,1,0:T(8,128)(2,1)S(1)}, bf16[16,64,128]{2,1,0:T(8,128)(2,1)S(1)}, u32[]{:S(2)}, u32[]{:S(2)}) collective-permute-start(bf16[16,64,128]{2,1,0:T(8,128)(2,1)S(1)} %add_convert_fusion.3), channel_id=1, source_target_pairs={{0,4},{1,3},{4,8},{5,1},{8,12},{9,5},{12,14},{13,9},{14,10},{15,13... | collective-permute-start | bytes 786440 | tf_op jit(solution)/shard_map/ppermute | solution.py:412
  51.6 2.1 %collective-permute-start.19 = (bf16[16,64,128]{2,1,0:T(8,128)(2,1)S(1)}, bf16[16,64,128]{2,1,0:T(8,128)(2,1)S(1)}, u32[]{:S(2)}, u32[]{:S(2)}) collective-permute-start(bf16[16,64,128]{2,1,0:T(8,128)(2,1)S(1)} %add_convert_fusion.2), channel_id=1, source_target_pairs={{0,4},{1,3},{4,8},{5,1},{8,12},{9,5},{12,14},{13,9},{14,10},{15,13... | collective-permute-start | bytes 786440 | tf_op jit(solution)/shard_map/ppermute | solution.py:412
  53.7 1.7 %collective-permute-done.16 = bf16[16,64,128]{2,1,0:T(8,128)(2,1)S(1)} collective-permute-done((bf16[16,64,128]{2,1,0:T(8,128)(2,1)S(1)}, bf16[16,64,128]{2,1,0:T(8,128)(2,1)S(1)}, u32[]{:S(2)}, u32[]{:S(2)}) %collective-permute-start.16) | collective-permute-done | bytes 262176 | tf_op jit(solution)/shard_map/ppermute | solution.py:412
  55.6 1.9 %collective-permute-start.18 = (bf16[16,64,128]{2,1,0:T(8,128)(2,1)S(1)}, bf16[16,64,128]{2,1,0:T(8,128)(2,1)S(1)}, u32[]{:S(2)}, u32[]{:S(2)}) collective-permute-start(bf16[16,64,128]{2,1,0:T(8,128)(2,1)S(1)} %add_convert_fusion.1), channel_id=1, source_target_pairs={{0,4},{1,3},{4,8},{5,1},{8,12},{9,5},{12,14},{13,9},{14,10},{15,13... | collective-permute-start | bytes 786440 | tf_op jit(solution)/shard_map/ppermute | solution.py:412
  57.5 0.8 %collective-permute-done.19 = bf16[16,64,128]{2,1,0:T(8,128)(2,1)S(1)} collective-permute-done((bf16[16,64,128]{2,1,0:T(8,128)(2,1)S(1)}, bf16[16,64,128]{2,1,0:T(8,128)(2,1)S(1)}, u32[]{:S(2)}, u32[]{:S(2)}) %collective-permute-start.19) | collective-permute-done | bytes 262176 | tf_op jit(solution)/shard_map/ppermute | solution.py:412
  58.3 2.5 %far.1 = f32[16,64,128]{2,1,0:T(8,128)S(1)} custom-call(bf16[1024,128]{1,0:T(8,128)(2,1)S(1)} %get-tuple-element.53.refs_0_, bf16[1024,128]{1,0:T(8,128)(2,1)S(1)} %collective-permute-done.10.refs_1_, s32[1]{0:T(128)} %bitcast.me_ref.token_ref.refs_2_, bf16[16,16,256]{2,1,0:T(8,128)(2,1)S(1)} %bitcast.10, s32[1,256]{1,0:T(1,128)S(1)} %bitcast.11, ...), custom_call_target="tpu_custom_call" | custom-call | flops 536870912 | bytes 8388608 | tf_op jit(solution)/shard_map/far/pallas_call | solution.py:501
  60.8 1.2 %collective-permute-done.18 = bf16[16,64,128]{2,1,0:T(8,128)(2,1)S(1)} collective-permute-done((bf16[16,64,128]{2,1,0:T(8,128)(2,1)S(1)}, bf16[16,64,128]{2,1,0:T(8,128)(2,1)S(1)}, u32[]{:S(2)}, u32[]{:S(2)}) %collective-permute-start.18) | collective-permute-done | bytes 262176 | tf_op jit(solution)/shard_map/ppermute | solution.py:412
  (39 shorter events, 5.1 us)
Async XLA Ops:
  0.0 17.5 %collective-permute-start.2 = (bf16[128,128,128]{2,1,0:T(8,128)(2,1)}, bf16[128,128,128]{2,1,0:T(8,128)(2,1)}, u32[]{:S(2)}, u32[]{:S(2)}) collective-permute-start(bf16[128,128,128]{2,1,0:T(8,128)(2,1)} %refs_8_.1), channel_id=1, source_target_pairs={{0,1},{1,0},{2,3},{3,2},{4,5},{5,4},{6,7},{7,6},{8,9},{9,8},{10,11... | collective-permute-start | bytes 12582920 | tf_op jit(solution)/shard_map/ppermute | solution.py:412
  2.6 7.5 %collective-permute-start = (bf16[1152,128]{1,0:T(8,128)(2,1)}, bf16[1152,128]{1,0:T(8,128)(2,1)S(1)}, u32[]{:S(2)}, u32[]{:S(2)}) collective-permute-start(bf16[1152,128]{1,0:T(8,128)(2,1)} %get-tuple-element.43), channel_id=1, source_target_pairs={{0,4},{1,3},{4,8},{5,1},{8,12},{9,5},{12,14},{13,9},{14,10},{15,13... | collective-permute-start | bytes 884744 | tf_op jit(solution)/shard_map/ppermute | solution.py:412
  6.1 1.0 %copy-start.6 = (bf16[1152,128]{1,0:T(8,128)(2,1)S(1)}, bf16[1152,128]{1,0:T(8,128)(2,1)}, u32[]{:S(2)}) copy-start(bf16[1152,128]{1,0:T(8,128)(2,1)} %get-tuple-element.43) | copy-start | bytes 884740
  6.1 9.1 %copy-start.5 = (s32[8,128]{1,0:T(8,128)S(1)}, s32[8,128]{1,0:T(8,128)}, u32[]{:S(2)}) copy-start(s32[8,128]{1,0:T(8,128)} %get-tuple-element.44) | copy-start | bytes 12292
  6.1 19.8 %copy-start = (bf16[128,128,128]{2,1,0:T(8,128)(2,1)S(1)}, bf16[128,128,128]{2,1,0:T(8,128)(2,1)}, u32[]{:S(2)}) copy-start(bf16[128,128,128]{2,1,0:T(8,128)(2,1)} %refs_8_.1) | copy-start | bytes 12582916
  7.1 6.4 %collective-permute-start.6 = (bf16[1152,128]{1,0:T(8,128)(2,1)S(1)}, bf16[1152,128]{1,0:T(8,128)(2,1)S(1)}, u32[]{:S(2)}, u32[]{:S(2)}) collective-permute-start(bf16[1152,128]{1,0:T(8,128)(2,1)S(1)} %copy-done.6), channel_id=1, source_target_pairs={{0,3},{1,4},{4,1},{5,8},{8,5},{9,12},{12,9},{13,14},{14,13},{15,10... | collective-permute-start | bytes 884744 | tf_op jit(solution)/shard_map/ppermute | solution.py:412
  8.4 8.0 %collective-permute-start.3 = (bf16[1152,128]{1,0:T(8,128)(2,1)S(1)}, bf16[1152,128]{1,0:T(8,128)(2,1)S(1)}, u32[]{:S(2)}, u32[]{:S(2)}) collective-permute-start(bf16[1152,128]{1,0:T(8,128)(2,1)S(1)} %copy-done.6), channel_id=1, source_target_pairs={{0,1},{1,0},{2,3},{3,2},{4,5},{5,4},{6,7},{7,6},{8,9},{9,8},{10,11... | collective-permute-start | bytes 884744 | tf_op jit(solution)/shard_map/ppermute | solution.py:412
  10.1 7.4 %collective-permute-start.1 = (bf16[1152,128]{1,0:T(8,128)(2,1)S(1)}, bf16[1152,128]{1,0:T(8,128)(2,1)S(1)}, u32[]{:S(2)}, u32[]{:S(2)}) collective-permute-start(bf16[1152,128]{1,0:T(8,128)(2,1)S(1)} %collective-permute-done.refs_1_), channel_id=1, source_target_pairs={{0,4},{1,3},{4,8},{5,1},{8,12},{9,5},{12,14},{13,9},{14,10},{15,13... | collective-permute-start | bytes 884744 | tf_op jit(solution)/shard_map/ppermute | solution.py:412
  13.5 7.2 %collective-permute-start.7 = (bf16[1152,128]{1,0:T(8,128)(2,1)S(1)}, bf16[1152,128]{1,0:T(8,128)(2,1)S(1)}, u32[]{:S(2)}, u32[]{:S(2)}) collective-permute-start(bf16[1152,128]{1,0:T(8,128)(2,1)S(1)} %collective-permute-done.6.refs_2_), channel_id=1, source_target_pairs={{0,4},{1,3},{4,8},{5,1},{8,12},{9,5},{12,14},{13,9},{14,10},{15,13... | collective-permute-start | bytes 884744 | tf_op jit(solution)/shard_map/ppermute | solution.py:412
  15.3 1.2 %collective-permute-start.4 = (s32[8,128]{1,0:T(8,128)S(1)}, s32[8,128]{1,0:T(8,128)S(1)}, u32[]{:S(2)}, u32[]{:S(2)}) collective-permute-start(s32[8,128]{1,0:T(8,128)S(1)} %copy-done.5), channel_id=1, source_target_pairs={{0,1},{1,0},{2,3},{3,2},{4,5},{5,4},{6,7},{7,6},{8,9},{9,8},{10,11... | collective-permute-start | bytes 12296 | tf_op jit(solution)/shard_map/ppermute | solution.py:412
  17.5 6.7 %collective-permute-start.5 = (bf16[1152,128]{1,0:T(8,128)(2,1)S(1)}, bf16[1152,128]{1,0:T(8,128)(2,1)S(1)}, u32[]{:S(2)}, u32[]{:S(2)}) collective-permute-start(bf16[1152,128]{1,0:T(8,128)(2,1)S(1)} %collective-permute-done.1.refs_3_), channel_id=1, source_target_pairs={{0,4},{1,3},{4,8},{5,1},{8,12},{9,5},{12,14},{13,9},{14,10},{15,13... | collective-permute-start | bytes 884744 | tf_op jit(solution)/shard_map/ppermute | solution.py:412
  20.6 9.3 %collective-permute-start.8 = (bf16[1152,128]{1,0:T(8,128)(2,1)S(1)}, bf16[1152,128]{1,0:T(8,128)(2,1)S(1)}, u32[]{:S(2)}, u32[]{:S(2)}) collective-permute-start(bf16[1152,128]{1,0:T(8,128)(2,1)S(1)} %collective-permute-done.7.refs_4_), channel_id=1, source_target_pairs={{0,4},{1,3},{4,8},{5,1},{8,12},{9,5},{12,14},{13,9},{14,10},{15,13... | collective-permute-start | bytes 884744 | tf_op jit(solution)/shard_map/ppermute | solution.py:412
  24.2 6.7 %collective-permute-start.9 = (bf16[1152,128]{1,0:T(8,128)(2,1)S(1)}, bf16[1152,128]{1,0:T(8,128)(2,1)S(1)}, u32[]{:S(2)}, u32[]{:S(2)}) collective-permute-start(bf16[1152,128]{1,0:T(8,128)(2,1)S(1)} %collective-permute-done.5.refs_5_), channel_id=1, source_target_pairs={{0,4},{1,3},{4,8},{5,1},{8,12},{9,5},{12,14},{13,9},{14,10},{15,13... | collective-permute-start | bytes 884744 | tf_op jit(solution)/shard_map/ppermute | solution.py:412
  33.4 2.0 %collective-permute-start.11 = (bf16[32,64,128]{2,1,0:T(8,128)(2,1)S(1)}, bf16[32,64,128]{2,1,0:T(8,128)(2,1)S(1)}, u32[]{:S(2)}, u32[]{:S(2)}) collective-permute-start(bf16[32,64,128]{2,1,0:T(8,128)(2,1)S(1)} %get-tuple-element.55), channel_id=1, source_target_pairs={{0,1},{1,0},{2,3},{3,2},{4,5},{5,4},{6,7},{7,6},{8,9},{9,8},{10,11... | collective-permute-start | bytes 1572872 | tf_op jit(solution)/shard_map/ppermute | solution.py:412
  35.4 22.8 %copy-start.1 = (bf16[16,16,128]{2,1,0:T(8,128)(2,1)S(1)}, bf16[16,16,128]{2,1,0:T(8,128)(2,1)}, u32[]{:S(2)}) copy-start(bf16[16,16,128]{2,1,0:T(8,128)(2,1)} %refs_7_.1) | copy-start | bytes 196612
  35.4 22.8 %copy-start.2 = (s32[256]{0:T(256)S(1)}, s32[256]{0:T(256)}, u32[]{:S(2)}) copy-start(s32[256]{0:T(256)} %param.17) | copy-start | bytes 3076
  35.4 22.8 %copy-start.3 = (s32[256,1]{0,1:T(1,128)S(1)}, s32[256,1]{0,1:T(1,128)}, u32[]{:S(2)}) copy-start(s32[256,1]{0,1:T(1,128)} %param.18) | copy-start | bytes 3076
  35.4 22.9 %copy-start.4 = (s32[256]{0:T(256)S(1)}, s32[256]{0:T(256)}, u32[]{:S(2)}) copy-start(s32[256]{0:T(256)} %param.19) | copy-start | bytes 3076
  35.6 6.6 %collective-permute-start.13 = (bf16[96,64,128]{2,1,0:T(8,128)(2,1)S(1)}, bf16[96,64,128]{2,1,0:T(8,128)(2,1)S(1)}, u32[]{:S(2)}, u32[]{:S(2)}) collective-permute-start(bf16[96,64,128]{2,1,0:T(8,128)(2,1)S(1)} %get-tuple-element.59), channel_id=1, source_target_pairs={{0,1},{1,0},{2,3},{3,2},{4,5},{5,4},{6,7},{7,6},{8,9},{9,8},{10,11... | collective-permute-start | bytes 4718600 | tf_op jit(solution)/shard_map/ppermute | solution.py:412
  35.8 6.4 %collective-permute-start.12 = (bf16[16,64,128]{2,1,0:T(8,128)(2,1)S(1)}, bf16[16,64,128]{2,1,0:T(8,128)(2,1)S(1)}, u32[]{:S(2)}, u32[]{:S(2)}) collective-permute-start(bf16[16,64,128]{2,1,0:T(8,128)(2,1)S(1)} %get-tuple-element.56), channel_id=1, source_target_pairs={{0,4},{1,3},{4,8},{5,1},{8,12},{9,5},{12,14},{13,9},{14,10},{15,13... | collective-permute-start | bytes 786440 | tf_op jit(solution)/shard_map/ppermute | solution.py:412
  37.8 7.1 %collective-permute-start.15 = (bf16[16,64,128]{2,1,0:T(8,128)(2,1)S(1)}, bf16[16,64,128]{2,1,0:T(8,128)(2,1)S(1)}, u32[]{:S(2)}, u32[]{:S(2)}) collective-permute-start(bf16[16,64,128]{2,1,0:T(8,128)(2,1)S(1)} %get-tuple-element.58), channel_id=1, source_target_pairs={{0,4},{1,3},{4,8},{5,1},{8,12},{9,5},{12,14},{13,9},{14,10},{15,13... | collective-permute-start | bytes 786440 | tf_op jit(solution)/shard_map/ppermute | solution.py:412
  42.3 6.4 %collective-permute-start.14 = (bf16[16,64,128]{2,1,0:T(8,128)(2,1)S(1)}, bf16[16,64,128]{2,1,0:T(8,128)(2,1)S(1)}, u32[]{:S(2)}, u32[]{:S(2)}) collective-permute-start(bf16[16,64,128]{2,1,0:T(8,128)(2,1)S(1)} %add_convert_fusion.5), channel_id=1, source_target_pairs={{0,4},{1,3},{4,8},{5,1},{8,12},{9,5},{12,14},{13,9},{14,10},{15,13... | collective-permute-start | bytes 786440 | tf_op jit(solution)/shard_map/ppermute | solution.py:412
  45.1 6.4 %collective-permute-start.17 = (bf16[16,64,128]{2,1,0:T(8,128)(2,1)S(1)}, bf16[16,64,128]{2,1,0:T(8,128)(2,1)S(1)}, u32[]{:S(2)}, u32[]{:S(2)}) collective-permute-start(bf16[16,64,128]{2,1,0:T(8,128)(2,1)S(1)} %add_convert_fusion.4), channel_id=1, source_target_pairs={{0,4},{1,3},{4,8},{5,1},{8,12},{9,5},{12,14},{13,9},{14,10},{15,13... | collective-permute-start | bytes 786440 | tf_op jit(solution)/shard_map/ppermute | solution.py:412
  48.8 6.6 %collective-permute-start.16 = (bf16[16,64,128]{2,1,0:T(8,128)(2,1)S(1)}, bf16[16,64,128]{2,1,0:T(8,128)(2,1)S(1)}, u32[]{:S(2)}, u32[]{:S(2)}) collective-permute-start(bf16[16,64,128]{2,1,0:T(8,128)(2,1)S(1)} %add_convert_fusion.3), channel_id=1, source_target_pairs={{0,4},{1,3},{4,8},{5,1},{8,12},{9,5},{12,14},{13,9},{14,10},{15,13... | collective-permute-start | bytes 786440 | tf_op jit(solution)/shard_map/ppermute | solution.py:412
  50.9 7.3 %collective-permute-start.10 = (bf16[1024,128]{1,0:T(8,128)(2,1)S(1)}, bf16[1024,128]{1,0:T(8,128)(2,1)S(1)}, u32[]{:S(2)}, u32[]{:S(2)}) collective-permute-start(bf16[1024,128]{1,0:T(8,128)(2,1)S(1)} %get-tuple-element.53.refs_0_), channel_id=1, source_target_pairs={{0,1},{1,0},{2,3},{3,2},{4,5},{5,4},{6,7},{7,6},{8,9},{9,8},{10,11... | collective-permute-start | bytes 786440 | tf_op jit(solution)/shard_map/ppermute | solution.py:412
  51.6 6.6 %collective-permute-start.19 = (bf16[16,64,128]{2,1,0:T(8,128)(2,1)S(1)}, bf16[16,64,128]{2,1,0:T(8,128)(2,1)S(1)}, u32[]{:S(2)}, u32[]{:S(2)}) collective-permute-start(bf16[16,64,128]{2,1,0:T(8,128)(2,1)S(1)} %add_convert_fusion.2), channel_id=1, source_target_pairs={{0,4},{1,3},{4,8},{5,1},{8,12},{9,5},{12,14},{13,9},{14,10},{15,13... | collective-permute-start | bytes 786440 | tf_op jit(solution)/shard_map/ppermute | solution.py:412
  55.6 6.4 %collective-permute-start.18 = (bf16[16,64,128]{2,1,0:T(8,128)(2,1)S(1)}, bf16[16,64,128]{2,1,0:T(8,128)(2,1)S(1)}, u32[]{:S(2)}, u32[]{:S(2)}) collective-permute-start(bf16[16,64,128]{2,1,0:T(8,128)(2,1)S(1)} %add_convert_fusion.1), channel_id=1, source_target_pairs={{0,4},{1,3},{4,8},{5,1},{8,12},{9,5},{12,14},{13,9},{14,10},{15,13... | collective-permute-start | bytes 786440 | tf_op jit(solution)/shard_map/ppermute | solution.py:412
  58.3 3.9 %collective-permute-start.20 = (bf16[16,64,128]{2,1,0:T(8,128)(2,1)S(1)}, bf16[16,64,128]{2,1,0:T(8,128)(2,1)S(1)}, u32[]{:S(2)}, u32[]{:S(2)}) collective-permute-start(bf16[16,64,128]{2,1,0:T(8,128)(2,1)S(1)} %collective-permute-done.19), channel_id=1, source_target_pairs={{0,1},{1,0},{2,3},{3,2},{4,5},{5,4},{6,7},{7,6},{8,9},{9,8},{10,11... | collective-permute-start | bytes 786440 | tf_op jit(solution)/shard_map/ppermute | solution.py:412

commit v26 on v25

--- a/solution.py
+++ b/solution.py
@@ -7,7 +7,7 @@
 from jax.experimental.pallas import tpu as pltpu
 from jax.sharding import PartitionSpec as P
 
-BATCH = 16, 8
+BATCH = 16, 16
 CHUNKS = 4
 LATE = 2
 UNITS = 1

time: 63.2 us -> 63.2 us (level)
  starting transfers between devices: 28.2 us -> 23.6 us
  waiting for transfers between devices: 19.8 us -> 23.9 us
  Pallas kernels: 11.7 us -> 12.5 us
    ppermute x21, starting transfers between devices: 28.2 us -> 23.6 us  [move(): return lax.ppermute(values, 'blk', where)]
    ppermute x21, waiting for transfers between devices: 19.8 us -> 23.9 us  [move(): return lax.ppermute(values, 'blk', where)]
    pallas_call x2, Pallas kernels: 6.53 us -> 7.32 us  [near(): pl.pallas_call(functools.partial(near_kernel, late, BATCH[late], len(shar...]
where the time goes in v26:
time: 63.2 us; the launch traced here: 63.1 us
  waiting for transfers between devices  23.9 us (38%)
  starting transfers between devices  23.6 us (37%)
  Pallas kernels  12.5 us (20%)
  other arithmetic  1.62 us (3%)
  local copies, waits for them, and re-layouts  1.32 us (2%)
    ppermute x21, waiting for transfers between devices, move(): return lax.ppermute(values, 'blk', where)  23.9 us
    ppermute x21, starting transfers between devices, move(): return lax.ppermute(values, 'blk', where)  23.6 us
    pallas_call x2, Pallas kernels, near(): pl.pallas_call(functools.partial(near_kernel, late, BATCH[late], len(shar...  7.32 us
    pallas_call x1, Pallas kernels, far_field(): pl.pallas_call(far_kernel, out_shape=jax.ShapeDtypeStruct((clusters, dire...  2.51 us
    pallas_call x1, Pallas kernels, stationary(): pl.pallas_call(functools.partial(prologue_kernel, count), out_shape=[jax....  2.13 us
    unnamed x15, local copies, waits for them, and re-layouts  1.32 us
  transfers between devices with their start and end apart: 21, of which 15 were waited for; matrix products, arithmetic and copies ran while one was open for 3% of the time, Pallas kernels for 15%

profile of v26, /device:TPU:0, one launch (start us, length us, event | category | flops | bytes accessed | tf_op | source)
XLA Modules:
  0.0 63.1 jit_solution(14083693560934980397)
XLA Ops:
  0.5 2.1 %prologue.1 = (bf16[1152,128]{1,0:T(8,128)(2,1)}, s32[8,128]{1,0:T(8,128)}) custom-call(s32[1]{0:T(128)} %bitcast.me_ref.token_ref.refs_2_, s32[1,128]{1,0:T(1,128)} %bitcast.14, s32[1,128]{1,0:T(1,128)} %bitcast.15, s32[1,128]{1,0:T(1,128)} %bitcast.16, bf16[16,64,128]{2,1,0:T(8,128)(2,1)} %rhs_ref.1, bf16[16,16,128]{2,1,0:T(8,128)(2,1)} %basis_ref.1), custom_call_target="tpu_custom_call" | custom-call | tf_op jit(solution)/shard_map/prologue/pallas_call | solution.py:419
  2.6 2.6 %collective-permute-start = (bf16[1152,128]{1,0:T(8,128)(2,1)}, bf16[1152,128]{1,0:T(8,128)(2,1)S(1)}, u32[]{:S(2)}, u32[]{:S(2)}) collective-permute-start(bf16[1152,128]{1,0:T(8,128)(2,1)} %get-tuple-element.43), channel_id=1, source_target_pairs={{0,4},{1,3},{4,8},{5,1},{8,12},{9,5},{12,14},{13,9},{14,10},{15,13... | collective-permute-start | bytes 884744 | tf_op jit(solution)/shard_map/ppermute | solution.py:412
  5.2 0.9 %copy.16 = bf16[256,16,16]{0,1,2:T(8,128)(2,1)S(1)} copy(bf16[256,16,16]{0,2,1:T(8,128)(2,1)} %param.16) | data formatting | bytes 262144 | tf_op args[5]
  7.1 1.4 %collective-permute-start.6 = (bf16[1152,128]{1,0:T(8,128)(2,1)S(1)}, bf16[1152,128]{1,0:T(8,128)(2,1)S(1)}, u32[]{:S(2)}, u32[]{:S(2)}) collective-permute-start(bf16[1152,128]{1,0:T(8,128)(2,1)S(1)} %copy-done.6), channel_id=1, source_target_pairs={{0,3},{1,4},{4,1},{5,8},{8,5},{9,12},{12,9},{13,14},{14,13},{15,10... | collective-permute-start | bytes 884744 | tf_op jit(solution)/shard_map/ppermute | solution.py:412
  8.8 1.3 %collective-permute-done.refs_1_ = bf16[1152,128]{1,0:T(8,128)(2,1)S(1)} collective-permute-done((bf16[1152,128]{1,0:T(8,128)(2,1)}, bf16[1152,128]{1,0:T(8,128)(2,1)S(1)}, u32[]{:S(2)}, u32[]{:S(2)}) %collective-permute-start) | collective-permute-done | bytes 294944 | tf_op jit(solution)/shard_map/ppermute | solution.py:412
  10.1 2.4 %collective-permute-start.1 = (bf16[1152,128]{1,0:T(8,128)(2,1)S(1)}, bf16[1152,128]{1,0:T(8,128)(2,1)S(1)}, u32[]{:S(2)}, u32[]{:S(2)}) collective-permute-start(bf16[1152,128]{1,0:T(8,128)(2,1)S(1)} %collective-permute-done.refs_1_), channel_id=1, source_target_pairs={{0,4},{1,3},{4,8},{5,1},{8,12},{9,5},{12,14},{13,9},{14,10},{15,13... | collective-permute-start | bytes 884744 | tf_op jit(solution)/shard_map/ppermute | solution.py:412
  12.5 1.0 %collective-permute-done.6.refs_2_ = bf16[1152,128]{1,0:T(8,128)(2,1)S(1)} collective-permute-done((bf16[1152,128]{1,0:T(8,128)(2,1)S(1)}, bf16[1152,128]{1,0:T(8,128)(2,1)S(1)}, u32[]{:S(2)}, u32[]{:S(2)}) %collective-permute-start.6) | collective-permute-done | bytes 294944 | tf_op jit(solution)/shard_map/ppermute | solution.py:412
  13.5 1.8 %collective-permute-start.7 = (bf16[1152,128]{1,0:T(8,128)(2,1)S(1)}, bf16[1152,128]{1,0:T(8,128)(2,1)S(1)}, u32[]{:S(2)}, u32[]{:S(2)}) collective-permute-start(bf16[1152,128]{1,0:T(8,128)(2,1)S(1)} %collective-permute-done.6.refs_2_), channel_id=1, source_target_pairs={{0,4},{1,3},{4,8},{5,1},{8,12},{9,5},{12,14},{13,9},{14,10},{15,13... | collective-permute-start | bytes 884744 | tf_op jit(solution)/shard_map/ppermute | solution.py:412
  16.4 1.0 %collective-permute-done.1.refs_3_ = bf16[1152,128]{1,0:T(8,128)(2,1)S(1)} collective-permute-done((bf16[1152,128]{1,0:T(8,128)(2,1)S(1)}, bf16[1152,128]{1,0:T(8,128)(2,1)S(1)}, u32[]{:S(2)}, u32[]{:S(2)}) %collective-permute-start.1) | collective-permute-done | bytes 294944 | tf_op jit(solution)/shard_map/ppermute | solution.py:412
  17.5 1.7 %collective-permute-start.5 = (bf16[1152,128]{1,0:T(8,128)(2,1)S(1)}, bf16[1152,128]{1,0:T(8,128)(2,1)S(1)}, u32[]{:S(2)}, u32[]{:S(2)}) collective-permute-start(bf16[1152,128]{1,0:T(8,128)(2,1)S(1)} %collective-permute-done.1.refs_3_), channel_id=1, source_target_pairs={{0,4},{1,3},{4,8},{5,1},{8,12},{9,5},{12,14},{13,9},{14,10},{15,13... | collective-permute-start | bytes 884744 | tf_op jit(solution)/shard_map/ppermute | solution.py:412
  19.2 1.4 %collective-permute-done.7.refs_4_ = bf16[1152,128]{1,0:T(8,128)(2,1)S(1)} collective-permute-done((bf16[1152,128]{1,0:T(8,128)(2,1)S(1)}, bf16[1152,128]{1,0:T(8,128)(2,1)S(1)}, u32[]{:S(2)}, u32[]{:S(2)}) %collective-permute-start.7) | collective-permute-done | bytes 294944 | tf_op jit(solution)/shard_map/ppermute | solution.py:412
  20.6 1.7 %collective-permute-start.8 = (bf16[1152,128]{1,0:T(8,128)(2,1)S(1)}, bf16[1152,128]{1,0:T(8,128)(2,1)S(1)}, u32[]{:S(2)}, u32[]{:S(2)}) collective-permute-start(bf16[1152,128]{1,0:T(8,128)(2,1)S(1)} %collective-permute-done.7.refs_4_), channel_id=1, source_target_pairs={{0,4},{1,3},{4,8},{5,1},{8,12},{9,5},{12,14},{13,9},{14,10},{15,13... | collective-permute-start | bytes 884744 | tf_op jit(solution)/shard_map/ppermute | solution.py:412
  22.4 1.8 %collective-permute-done.5.refs_5_ = bf16[1152,128]{1,0:T(8,128)(2,1)S(1)} collective-permute-done((bf16[1152,128]{1,0:T(8,128)(2,1)S(1)}, bf16[1152,128]{1,0:T(8,128)(2,1)S(1)}, u32[]{:S(2)}, u32[]{:S(2)}) %collective-permute-start.5) | collective-permute-done | bytes 294944 | tf_op jit(solution)/shard_map/ppermute | solution.py:412
  24.2 1.7 %collective-permute-start.9 = (bf16[1152,128]{1,0:T(8,128)(2,1)S(1)}, bf16[1152,128]{1,0:T(8,128)(2,1)S(1)}, u32[]{:S(2)}, u32[]{:S(2)}) collective-permute-start(bf16[1152,128]{1,0:T(8,128)(2,1)S(1)} %collective-permute-done.5.refs_5_), channel_id=1, source_target_pairs={{0,4},{1,3},{4,8},{5,1},{8,12},{9,5},{12,14},{13,9},{14,10},{15,13... | collective-permute-start | bytes 884744 | tf_op jit(solution)/shard_map/ppermute | solution.py:412
  25.9 4.4 %near.2 = (f32[257,64,128]{2,1,0:T(8,128)S(1)}, bf16[128,128,128]{2,1,0:T(8,128)(2,1)S(1)}) custom-call(s32[16,128]{1,0:T(8,128)S(1)} %pad_add_fusion.list_ref, bf16[1152,128]{1,0:T(8,128)(2,1)S(1)} %collective-permute-done.3.refs_0_, bf16[1152,128]{1,0:T(8,128)(2,1)S(1)} %collective-permute-done.refs_1_, ...), custom_call_target="tpu_custom_call", output_to_operand_aliasing={{0}: (9, {})} | custom-call | flops 2147483648 | bytes 16777216 | tf_op jit(solution)/shard_map/near/pallas_call | solution.py:477
  30.9 3.0 %near.3 = (f32[257,64,128]{2,1,0:T(8,128)S(1)}, bf16[1024,128]{1,0:T(8,128)(2,1)S(1)}, bf16[32,64,128]{2,1,0:T(8,128)(2,1)S(1)}, bf16[96,64,128]{2,1,0:T(8,128)(2,1)S(1)}) custom-call(s32[16,128]{1,0:T(8,128)S(1)} %pad_add_fusion.list_ref, bf16[1152,128]{1,0:T(8,128)(2,1)S(1)} %collective-permute-done.3.refs_0_, ...), custom_call_target="tpu_custom_call", output_to_operand_aliasing={{0}: (11, {})} | custom-call | flops 2147483648 | bytes 16777216 | tf_op jit(solution)/shard_map/near/pallas_call | solution.py:477
  34.0 1.9 %collective-permute-done.11 = bf16[32,64,128]{2,1,0:T(8,128)(2,1)S(1)} collective-permute-done((bf16[32,64,128]{2,1,0:T(8,128)(2,1)S(1)}, bf16[32,64,128]{2,1,0:T(8,128)(2,1)S(1)}, u32[]{:S(2)}, u32[]{:S(2)}) %collective-permute-start.11) | collective-permute-done | bytes 524320 | tf_op jit(solution)/shard_map/ppermute | solution.py:412
  36.2 1.3 %collective-permute-start.12 = (bf16[16,64,128]{2,1,0:T(8,128)(2,1)S(1)}, bf16[16,64,128]{2,1,0:T(8,128)(2,1)S(1)}, u32[]{:S(2)}, u32[]{:S(2)}) collective-permute-start(bf16[16,64,128]{2,1,0:T(8,128)(2,1)S(1)} %get-tuple-element.56), channel_id=1, source_target_pairs={{0,4},{1,3},{4,8},{5,1},{8,12},{9,5},{12,14},{13,9},{14,10},{15,13... | collective-permute-start | bytes 786440 | tf_op jit(solution)/shard_map/ppermute | solution.py:412
  37.5 1.1 %collective-permute-start.15 = (bf16[16,64,128]{2,1,0:T(8,128)(2,1)S(1)}, bf16[16,64,128]{2,1,0:T(8,128)(2,1)S(1)}, u32[]{:S(2)}, u32[]{:S(2)}) collective-permute-start(bf16[16,64,128]{2,1,0:T(8,128)(2,1)S(1)} %get-tuple-element.58), channel_id=1, source_target_pairs={{0,4},{1,3},{4,8},{5,1},{8,12},{9,5},{12,14},{13,9},{14,10},{15,13... | collective-permute-start | bytes 786440 | tf_op jit(solution)/shard_map/ppermute | solution.py:412
  38.6 4.0 %collective-permute-done.12 = bf16[16,64,128]{2,1,0:T(8,128)(2,1)S(1)} collective-permute-done((bf16[16,64,128]{2,1,0:T(8,128)(2,1)S(1)}, bf16[16,64,128]{2,1,0:T(8,128)(2,1)S(1)}, u32[]{:S(2)}, u32[]{:S(2)}) %collective-permute-start.12) | collective-permute-done | bytes 262176 | tf_op jit(solution)/shard_map/ppermute | solution.py:412
  42.7 1.3 %collective-permute-start.14 = (bf16[16,64,128]{2,1,0:T(8,128)(2,1)S(1)}, bf16[16,64,128]{2,1,0:T(8,128)(2,1)S(1)}, u32[]{:S(2)}, u32[]{:S(2)}) collective-permute-start(bf16[16,64,128]{2,1,0:T(8,128)(2,1)S(1)} %add_convert_fusion.5), channel_id=1, source_target_pairs={{0,4},{1,3},{4,8},{5,1},{8,12},{9,5},{12,14},{13,9},{14,10},{15,13... | collective-permute-start | bytes 786440 | tf_op jit(solution)/shard_map/ppermute | solution.py:412
  44.0 1.4 %collective-permute-done.15 = bf16[16,64,128]{2,1,0:T(8,128)(2,1)S(1)} collective-permute-done((bf16[16,64,128]{2,1,0:T(8,128)(2,1)S(1)}, bf16[16,64,128]{2,1,0:T(8,128)(2,1)S(1)}, u32[]{:S(2)}, u32[]{:S(2)}) %collective-permute-start.15) | collective-permute-done | bytes 262176 | tf_op jit(solution)/shard_map/ppermute | solution.py:412
  45.5 1.3 %collective-permute-start.17 = (bf16[16,64,128]{2,1,0:T(8,128)(2,1)S(1)}, bf16[16,64,128]{2,1,0:T(8,128)(2,1)S(1)}, u32[]{:S(2)}, u32[]{:S(2)}) collective-permute-start(bf16[16,64,128]{2,1,0:T(8,128)(2,1)S(1)} %add_convert_fusion.4), channel_id=1, source_target_pairs={{0,4},{1,3},{4,8},{5,1},{8,12},{9,5},{12,14},{13,9},{14,10},{15,13... | collective-permute-start | bytes 786440 | tf_op jit(solution)/shard_map/ppermute | solution.py:412
  46.8 2.3 %collective-permute-done.14 = bf16[16,64,128]{2,1,0:T(8,128)(2,1)S(1)} collective-permute-done((bf16[16,64,128]{2,1,0:T(8,128)(2,1)S(1)}, bf16[16,64,128]{2,1,0:T(8,128)(2,1)S(1)}, u32[]{:S(2)}, u32[]{:S(2)}) %collective-permute-start.14) | collective-permute-done | bytes 262176 | tf_op jit(solution)/shard_map/ppermute | solution.py:412
  49.2 1.3 %collective-permute-start.16 = (bf16[16,64,128]{2,1,0:T(8,128)(2,1)S(1)}, bf16[16,64,128]{2,1,0:T(8,128)(2,1)S(1)}, u32[]{:S(2)}, u32[]{:S(2)}) collective-permute-start(bf16[16,64,128]{2,1,0:T(8,128)(2,1)S(1)} %add_convert_fusion.3), channel_id=1, source_target_pairs={{0,4},{1,3},{4,8},{5,1},{8,12},{9,5},{12,14},{13,9},{14,10},{15,13... | collective-permute-start | bytes 786440 | tf_op jit(solution)/shard_map/ppermute | solution.py:412
  50.6 1.4 %collective-permute-done.17 = bf16[16,64,128]{2,1,0:T(8,128)(2,1)S(1)} collective-permute-done((bf16[16,64,128]{2,1,0:T(8,128)(2,1)S(1)}, bf16[16,64,128]{2,1,0:T(8,128)(2,1)S(1)}, u32[]{:S(2)}, u32[]{:S(2)}) %collective-permute-start.17) | collective-permute-done | bytes 262176 | tf_op jit(solution)/shard_map/ppermute | solution.py:412
  52.1 1.3 %collective-permute-start.19 = (bf16[16,64,128]{2,1,0:T(8,128)(2,1)S(1)}, bf16[16,64,128]{2,1,0:T(8,128)(2,1)S(1)}, u32[]{:S(2)}, u32[]{:S(2)}) collective-permute-start(bf16[16,64,128]{2,1,0:T(8,128)(2,1)S(1)} %add_convert_fusion.2), channel_id=1, source_target_pairs={{0,4},{1,3},{4,8},{5,1},{8,12},{9,5},{12,14},{13,9},{14,10},{15,13... | collective-permute-start | bytes 786440 | tf_op jit(solution)/shard_map/ppermute | solution.py:412
  53.4 2.3 %collective-permute-done.16 = bf16[16,64,128]{2,1,0:T(8,128)(2,1)S(1)} collective-permute-done((bf16[16,64,128]{2,1,0:T(8,128)(2,1)S(1)}, bf16[16,64,128]{2,1,0:T(8,128)(2,1)S(1)}, u32[]{:S(2)}, u32[]{:S(2)}) %collective-permute-start.16) | collective-permute-done | bytes 262176 | tf_op jit(solution)/shard_map/ppermute | solution.py:412
  55.8 1.3 %collective-permute-start.18 = (bf16[16,64,128]{2,1,0:T(8,128)(2,1)S(1)}, bf16[16,64,128]{2,1,0:T(8,128)(2,1)S(1)}, u32[]{:S(2)}, u32[]{:S(2)}) collective-permute-start(bf16[16,64,128]{2,1,0:T(8,128)(2,1)S(1)} %add_convert_fusion.1), channel_id=1, source_target_pairs={{0,4},{1,3},{4,8},{5,1},{8,12},{9,5},{12,14},{13,9},{14,10},{15,13... | collective-permute-start | bytes 786440 | tf_op jit(solution)/shard_map/ppermute | solution.py:412
  57.1 1.4 %collective-permute-done.19 = bf16[16,64,128]{2,1,0:T(8,128)(2,1)S(1)} collective-permute-done((bf16[16,64,128]{2,1,0:T(8,128)(2,1)S(1)}, bf16[16,64,128]{2,1,0:T(8,128)(2,1)S(1)}, u32[]{:S(2)}, u32[]{:S(2)}) %collective-permute-start.19) | collective-permute-done | bytes 262176 | tf_op jit(solution)/shard_map/ppermute | solution.py:412
  58.5 2.5 %far.1 = f32[16,64,128]{2,1,0:T(8,128)S(1)} custom-call(bf16[1024,128]{1,0:T(8,128)(2,1)S(1)} %get-tuple-element.53.refs_0_, bf16[1024,128]{1,0:T(8,128)(2,1)S(1)} %collective-permute-done.10.refs_1_, s32[1]{0:T(128)} %bitcast.me_ref.token_ref.refs_2_, bf16[16,16,256]{2,1,0:T(8,128)(2,1)S(1)} %bitcast.10, s32[1,256]{1,0:T(1,128)S(1)} %bitcast.11, ...), custom_call_target="tpu_custom_call" | custom-call | flops 536870912 | bytes 8388608 | tf_op jit(solution)/shard_map/far/pallas_call | solution.py:501
  61.0 1.2 %collective-permute-done.18 = bf16[16,64,128]{2,1,0:T(8,128)(2,1)S(1)} collective-permute-done((bf16[16,64,128]{2,1,0:T(8,128)(2,1)S(1)}, bf16[16,64,128]{2,1,0:T(8,128)(2,1)S(1)}, u32[]{:S(2)}, u32[]{:S(2)}) %collective-permute-start.18) | collective-permute-done | bytes 262176 | tf_op jit(solution)/shard_map/ppermute | solution.py:412
  (39 shorter events, 5.4 us)
Async XLA Ops:
  0.0 17.5 %collective-permute-start.2 = (bf16[128,128,128]{2,1,0:T(8,128)(2,1)}, bf16[128,128,128]{2,1,0:T(8,128)(2,1)}, u32[]{:S(2)}, u32[]{:S(2)}) collective-permute-start(bf16[128,128,128]{2,1,0:T(8,128)(2,1)} %refs_8_.1), channel_id=1, source_target_pairs={{0,1},{1,0},{2,3},{3,2},{4,5},{5,4},{6,7},{7,6},{8,9},{9,8},{10,11... | collective-permute-start | bytes 12582920 | tf_op jit(solution)/shard_map/ppermute | solution.py:412
  2.6 7.5 %collective-permute-start = (bf16[1152,128]{1,0:T(8,128)(2,1)}, bf16[1152,128]{1,0:T(8,128)(2,1)S(1)}, u32[]{:S(2)}, u32[]{:S(2)}) collective-permute-start(bf16[1152,128]{1,0:T(8,128)(2,1)} %get-tuple-element.43), channel_id=1, source_target_pairs={{0,4},{1,3},{4,8},{5,1},{8,12},{9,5},{12,14},{13,9},{14,10},{15,13... | collective-permute-start | bytes 884744 | tf_op jit(solution)/shard_map/ppermute | solution.py:412
  6.1 1.0 %copy-start.6 = (bf16[1152,128]{1,0:T(8,128)(2,1)S(1)}, bf16[1152,128]{1,0:T(8,128)(2,1)}, u32[]{:S(2)}) copy-start(bf16[1152,128]{1,0:T(8,128)(2,1)} %get-tuple-element.43) | copy-start | bytes 884740
  6.1 9.1 %copy-start.5 = (s32[8,128]{1,0:T(8,128)S(1)}, s32[8,128]{1,0:T(8,128)}, u32[]{:S(2)}) copy-start(s32[8,128]{1,0:T(8,128)} %get-tuple-element.44) | copy-start | bytes 12292
  6.1 19.8 %copy-start = (bf16[128,128,128]{2,1,0:T(8,128)(2,1)S(1)}, bf16[128,128,128]{2,1,0:T(8,128)(2,1)}, u32[]{:S(2)}) copy-start(bf16[128,128,128]{2,1,0:T(8,128)(2,1)} %refs_8_.1) | copy-start | bytes 12582916
  7.1 6.4 %collective-permute-start.6 = (bf16[1152,128]{1,0:T(8,128)(2,1)S(1)}, bf16[1152,128]{1,0:T(8,128)(2,1)S(1)}, u32[]{:S(2)}, u32[]{:S(2)}) collective-permute-start(bf16[1152,128]{1,0:T(8,128)(2,1)S(1)} %copy-done.6), channel_id=1, source_target_pairs={{0,3},{1,4},{4,1},{5,8},{8,5},{9,12},{12,9},{13,14},{14,13},{15,10... | collective-permute-start | bytes 884744 | tf_op jit(solution)/shard_map/ppermute | solution.py:412
  8.4 8.0 %collective-permute-start.3 = (bf16[1152,128]{1,0:T(8,128)(2,1)S(1)}, bf16[1152,128]{1,0:T(8,128)(2,1)S(1)}, u32[]{:S(2)}, u32[]{:S(2)}) collective-permute-start(bf16[1152,128]{1,0:T(8,128)(2,1)S(1)} %copy-done.6), channel_id=1, source_target_pairs={{0,1},{1,0},{2,3},{3,2},{4,5},{5,4},{6,7},{7,6},{8,9},{9,8},{10,11... | collective-permute-start | bytes 884744 | tf_op jit(solution)/shard_map/ppermute | solution.py:412
  10.1 7.4 %collective-permute-start.1 = (bf16[1152,128]{1,0:T(8,128)(2,1)S(1)}, bf16[1152,128]{1,0:T(8,128)(2,1)S(1)}, u32[]{:S(2)}, u32[]{:S(2)}) collective-permute-start(bf16[1152,128]{1,0:T(8,128)(2,1)S(1)} %collective-permute-done.refs_1_), channel_id=1, source_target_pairs={{0,4},{1,3},{4,8},{5,1},{8,12},{9,5},{12,14},{13,9},{14,10},{15,13... | collective-permute-start | bytes 884744 | tf_op jit(solution)/shard_map/ppermute | solution.py:412
  13.5 7.2 %collective-permute-start.7 = (bf16[1152,128]{1,0:T(8,128)(2,1)S(1)}, bf16[1152,128]{1,0:T(8,128)(2,1)S(1)}, u32[]{:S(2)}, u32[]{:S(2)}) collective-permute-start(bf16[1152,128]{1,0:T(8,128)(2,1)S(1)} %collective-permute-done.6.refs_2_), channel_id=1, source_target_pairs={{0,4},{1,3},{4,8},{5,1},{8,12},{9,5},{12,14},{13,9},{14,10},{15,13... | collective-permute-start | bytes 884744 | tf_op jit(solution)/shard_map/ppermute | solution.py:412
  15.3 1.2 %collective-permute-start.4 = (s32[8,128]{1,0:T(8,128)S(1)}, s32[8,128]{1,0:T(8,128)S(1)}, u32[]{:S(2)}, u32[]{:S(2)}) collective-permute-start(s32[8,128]{1,0:T(8,128)S(1)} %copy-done.5), channel_id=1, source_target_pairs={{0,1},{1,0},{2,3},{3,2},{4,5},{5,4},{6,7},{7,6},{8,9},{9,8},{10,11... | collective-permute-start | bytes 12296 | tf_op jit(solution)/shard_map/ppermute | solution.py:412
  17.5 6.7 %collective-permute-start.5 = (bf16[1152,128]{1,0:T(8,128)(2,1)S(1)}, bf16[1152,128]{1,0:T(8,128)(2,1)S(1)}, u32[]{:S(2)}, u32[]{:S(2)}) collective-permute-start(bf16[1152,128]{1,0:T(8,128)(2,1)S(1)} %collective-permute-done.1.refs_3_), channel_id=1, source_target_pairs={{0,4},{1,3},{4,8},{5,1},{8,12},{9,5},{12,14},{13,9},{14,10},{15,13... | collective-permute-start | bytes 884744 | tf_op jit(solution)/shard_map/ppermute | solution.py:412
  20.6 9.7 %collective-permute-start.8 = (bf16[1152,128]{1,0:T(8,128)(2,1)S(1)}, bf16[1152,128]{1,0:T(8,128)(2,1)S(1)}, u32[]{:S(2)}, u32[]{:S(2)}) collective-permute-start(bf16[1152,128]{1,0:T(8,128)(2,1)S(1)} %collective-permute-done.7.refs_4_), channel_id=1, source_target_pairs={{0,4},{1,3},{4,8},{5,1},{8,12},{9,5},{12,14},{13,9},{14,10},{15,13... | collective-permute-start | bytes 884744 | tf_op jit(solution)/shard_map/ppermute | solution.py:412
  24.2 6.7 %collective-permute-start.9 = (bf16[1152,128]{1,0:T(8,128)(2,1)S(1)}, bf16[1152,128]{1,0:T(8,128)(2,1)S(1)}, u32[]{:S(2)}, u32[]{:S(2)}) collective-permute-start(bf16[1152,128]{1,0:T(8,128)(2,1)S(1)} %collective-permute-done.5.refs_5_), channel_id=1, source_target_pairs={{0,4},{1,3},{4,8},{5,1},{8,12},{9,5},{12,14},{13,9},{14,10},{15,13... | collective-permute-start | bytes 884744 | tf_op jit(solution)/shard_map/ppermute | solution.py:412
  33.9 2.0 %collective-permute-start.11 = (bf16[32,64,128]{2,1,0:T(8,128)(2,1)S(1)}, bf16[32,64,128]{2,1,0:T(8,128)(2,1)S(1)}, u32[]{:S(2)}, u32[]{:S(2)}) collective-permute-start(bf16[32,64,128]{2,1,0:T(8,128)(2,1)S(1)} %get-tuple-element.55), channel_id=1, source_target_pairs={{0,1},{1,0},{2,3},{3,2},{4,5},{5,4},{6,7},{7,6},{8,9},{9,8},{10,11... | collective-permute-start | bytes 1572872 | tf_op jit(solution)/shard_map/ppermute | solution.py:412
  35.9 22.6 %copy-start.1 = (bf16[16,16,128]{2,1,0:T(8,128)(2,1)S(1)}, bf16[16,16,128]{2,1,0:T(8,128)(2,1)}, u32[]{:S(2)}) copy-start(bf16[16,16,128]{2,1,0:T(8,128)(2,1)} %refs_7_.1) | copy-start | bytes 196612
  35.9 22.6 %copy-start.2 = (s32[256]{0:T(256)S(1)}, s32[256]{0:T(256)}, u32[]{:S(2)}) copy-start(s32[256]{0:T(256)} %param.17) | copy-start | bytes 3076
  35.9 22.7 %copy-start.3 = (s32[256,1]{0,1:T(1,128)S(1)}, s32[256,1]{0,1:T(1,128)}, u32[]{:S(2)}) copy-start(s32[256,1]{0,1:T(1,128)} %param.18) | copy-start | bytes 3076
  35.9 22.7 %copy-start.4 = (s32[256]{0:T(256)S(1)}, s32[256]{0:T(256)}, u32[]{:S(2)}) copy-start(s32[256]{0:T(256)} %param.19) | copy-start | bytes 3076
  36.0 6.6 %collective-permute-start.13 = (bf16[96,64,128]{2,1,0:T(8,128)(2,1)S(1)}, bf16[96,64,128]{2,1,0:T(8,128)(2,1)S(1)}, u32[]{:S(2)}, u32[]{:S(2)}) collective-permute-start(bf16[96,64,128]{2,1,0:T(8,128)(2,1)S(1)} %get-tuple-element.59), channel_id=1, source_target_pairs={{0,1},{1,0},{2,3},{3,2},{4,5},{5,4},{6,7},{7,6},{8,9},{9,8},{10,11... | collective-permute-start | bytes 4718600 | tf_op jit(solution)/shard_map/ppermute | solution.py:412
  36.2 6.4 %collective-permute-start.12 = (bf16[16,64,128]{2,1,0:T(8,128)(2,1)S(1)}, bf16[16,64,128]{2,1,0:T(8,128)(2,1)S(1)}, u32[]{:S(2)}, u32[]{:S(2)}) collective-permute-start(bf16[16,64,128]{2,1,0:T(8,128)(2,1)S(1)} %get-tuple-element.56), channel_id=1, source_target_pairs={{0,4},{1,3},{4,8},{5,1},{8,12},{9,5},{12,14},{13,9},{14,10},{15,13... | collective-permute-start | bytes 786440 | tf_op jit(solution)/shard_map/ppermute | solution.py:412
  37.5 7.9 %collective-permute-start.15 = (bf16[16,64,128]{2,1,0:T(8,128)(2,1)S(1)}, bf16[16,64,128]{2,1,0:T(8,128)(2,1)S(1)}, u32[]{:S(2)}, u32[]{:S(2)}) collective-permute-start(bf16[16,64,128]{2,1,0:T(8,128)(2,1)S(1)} %get-tuple-element.58), channel_id=1, source_target_pairs={{0,4},{1,3},{4,8},{5,1},{8,12},{9,5},{12,14},{13,9},{14,10},{15,13... | collective-permute-start | bytes 786440 | tf_op jit(solution)/shard_map/ppermute | solution.py:412
  42.7 6.4 %collective-permute-start.14 = (bf16[16,64,128]{2,1,0:T(8,128)(2,1)S(1)}, bf16[16,64,128]{2,1,0:T(8,128)(2,1)S(1)}, u32[]{:S(2)}, u32[]{:S(2)}) collective-permute-start(bf16[16,64,128]{2,1,0:T(8,128)(2,1)S(1)} %add_convert_fusion.5), channel_id=1, source_target_pairs={{0,4},{1,3},{4,8},{5,1},{8,12},{9,5},{12,14},{13,9},{14,10},{15,13... | collective-permute-start | bytes 786440 | tf_op jit(solution)/shard_map/ppermute | solution.py:412
  45.5 6.4 %collective-permute-start.17 = (bf16[16,64,128]{2,1,0:T(8,128)(2,1)S(1)}, bf16[16,64,128]{2,1,0:T(8,128)(2,1)S(1)}, u32[]{:S(2)}, u32[]{:S(2)}) collective-permute-start(bf16[16,64,128]{2,1,0:T(8,128)(2,1)S(1)} %add_convert_fusion.4), channel_id=1, source_target_pairs={{0,4},{1,3},{4,8},{5,1},{8,12},{9,5},{12,14},{13,9},{14,10},{15,13... | collective-permute-start | bytes 786440 | tf_op jit(solution)/shard_map/ppermute | solution.py:412
  49.2 6.4 %collective-permute-start.16 = (bf16[16,64,128]{2,1,0:T(8,128)(2,1)S(1)}, bf16[16,64,128]{2,1,0:T(8,128)(2,1)S(1)}, u32[]{:S(2)}, u32[]{:S(2)}) collective-permute-start(bf16[16,64,128]{2,1,0:T(8,128)(2,1)S(1)} %add_convert_fusion.3), channel_id=1, source_target_pairs={{0,4},{1,3},{4,8},{5,1},{8,12},{9,5},{12,14},{13,9},{14,10},{15,13... | collective-permute-start | bytes 786440 | tf_op jit(solution)/shard_map/ppermute | solution.py:412
  50.6 7.9 %collective-permute-start.10 = (bf16[1024,128]{1,0:T(8,128)(2,1)S(1)}, bf16[1024,128]{1,0:T(8,128)(2,1)S(1)}, u32[]{:S(2)}, u32[]{:S(2)}) collective-permute-start(bf16[1024,128]{1,0:T(8,128)(2,1)S(1)} %get-tuple-element.53.refs_0_), channel_id=1, source_target_pairs={{0,1},{1,0},{2,3},{3,2},{4,5},{5,4},{6,7},{7,6},{8,9},{9,8},{10,11... | collective-permute-start | bytes 786440 | tf_op jit(solution)/shard_map/ppermute | solution.py:412
  52.1 6.4 %collective-permute-start.19 = (bf16[16,64,128]{2,1,0:T(8,128)(2,1)S(1)}, bf16[16,64,128]{2,1,0:T(8,128)(2,1)S(1)}, u32[]{:S(2)}, u32[]{:S(2)}) collective-permute-start(bf16[16,64,128]{2,1,0:T(8,128)(2,1)S(1)} %add_convert_fusion.2), channel_id=1, source_target_pairs={{0,4},{1,3},{4,8},{5,1},{8,12},{9,5},{12,14},{13,9},{14,10},{15,13... | collective-permute-start | bytes 786440 | tf_op jit(solution)/shard_map/ppermute | solution.py:412
  55.8 6.4 %collective-permute-start.18 = (bf16[16,64,128]{2,1,0:T(8,128)(2,1)S(1)}, bf16[16,64,128]{2,1,0:T(8,128)(2,1)S(1)}, u32[]{:S(2)}, u32[]{:S(2)}) collective-permute-start(bf16[16,64,128]{2,1,0:T(8,128)(2,1)S(1)} %add_convert_fusion.1), channel_id=1, source_target_pairs={{0,4},{1,3},{4,8},{5,1},{8,12},{9,5},{12,14},{13,9},{14,10},{15,13... | collective-permute-start | bytes 786440 | tf_op jit(solution)/shard_map/ppermute | solution.py:412
  58.5 3.9 %collective-permute-start.20 = (bf16[16,64,128]{2,1,0:T(8,128)(2,1)S(1)}, bf16[16,64,128]{2,1,0:T(8,128)(2,1)S(1)}, u32[]{:S(2)}, u32[]{:S(2)}) collective-permute-start(bf16[16,64,128]{2,1,0:T(8,128)(2,1)S(1)} %collective-permute-done.19), channel_id=1, source_target_pairs={{0,1},{1,0},{2,3},{3,2},{4,5},{5,4},{6,7},{7,6},{8,9},{9,8},{10,11... | collective-permute-start | bytes 786440 | tf_op jit(solution)/shard_map/ppermute | solution.py:412

commit v27 on v25

--- a/solution.py
+++ b/solution.py
@@ -282,7 +282,7 @@
             send_ref[i] = sums[at + i].astype(send_ref.dtype)
             return carry
 
-        lax.fori_loop(0, send_ref.shape[0], pack, 0, unroll=8)
+        lax.fori_loop(0, send_ref.shape[0], pack, 0, unroll=16)
         at += send_ref.shape[0]
 
 

time: 63.2 us -> 63.3 us (level)
  waiting for transfers between devices: 19.8 us -> 21.2 us
  starting transfers between devices: 28.2 us -> 26.9 us
    ppermute x21, waiting for transfers between devices: 19.8 us -> 21.2 us  [move(): return lax.ppermute(values, 'blk', where)]
    ppermute x21, starting transfers between devices: 28.2 us -> 26.9 us  [move(): return lax.ppermute(values, 'blk', where)]
where the time goes in v27:
time: 63.3 us; the launch traced here: 63 us
  starting transfers between devices  26.9 us (42%)
  waiting for transfers between devices  21.2 us (33%)
  Pallas kernels  11.7 us (18%)
  other arithmetic  1.62 us (3%)
  local copies, waits for them, and re-layouts  1.32 us (2%)
    ppermute x21, starting transfers between devices, move(): return lax.ppermute(values, 'blk', where)  26.9 us
    ppermute x21, waiting for transfers between devices, move(): return lax.ppermute(values, 'blk', where)  21.2 us
    pallas_call x2, Pallas kernels, near(): pl.pallas_call(functools.partial(near_kernel, late, BATCH[late], len(shar...  6.49 us
    pallas_call x1, Pallas kernels, far_field(): pl.pallas_call(far_kernel, out_shape=jax.ShapeDtypeStruct((clusters, dire...  2.5 us
    pallas_call x1, Pallas kernels, stationary(): pl.pallas_call(functools.partial(prologue_kernel, count), out_shape=[jax....  2.13 us
    unnamed x15, local copies, waits for them, and re-layouts  1.32 us
  transfers between devices with their start and end apart: 21, of which 15 were waited for; matrix products, arithmetic and copies ran while one was open for 3% of the time, Pallas kernels for 15%

profile of v27, /device:TPU:0, one launch (start us, length us, event | category | flops | bytes accessed | tf_op | source)
XLA Modules:
  0.0 63.0 jit_solution(6610175204709019531)
XLA Ops:
  0.5 2.1 %prologue.1 = (bf16[1152,128]{1,0:T(8,128)(2,1)}, s32[8,128]{1,0:T(8,128)}) custom-call(s32[1]{0:T(128)} %bitcast.me_ref.token_ref.refs_2_, s32[1,128]{1,0:T(1,128)} %bitcast.14, s32[1,128]{1,0:T(1,128)} %bitcast.15, s32[1,128]{1,0:T(1,128)} %bitcast.16, bf16[16,64,128]{2,1,0:T(8,128)(2,1)} %rhs_ref.1, bf16[16,16,128]{2,1,0:T(8,128)(2,1)} %basis_ref.1), custom_call_target="tpu_custom_call" | custom-call | tf_op jit(solution)/shard_map/prologue/pallas_call | solution.py:419
  2.6 2.6 %collective-permute-start = (bf16[1152,128]{1,0:T(8,128)(2,1)}, bf16[1152,128]{1,0:T(8,128)(2,1)S(1)}, u32[]{:S(2)}, u32[]{:S(2)}) collective-permute-start(bf16[1152,128]{1,0:T(8,128)(2,1)} %get-tuple-element.43), channel_id=1, source_target_pairs={{0,4},{1,3},{4,8},{5,1},{8,12},{9,5},{12,14},{13,9},{14,10},{15,13... | collective-permute-start | bytes 884744 | tf_op jit(solution)/shard_map/ppermute | solution.py:412
  5.2 0.9 %copy.16 = bf16[256,16,16]{0,1,2:T(8,128)(2,1)S(1)} copy(bf16[256,16,16]{0,2,1:T(8,128)(2,1)} %param.16) | data formatting | bytes 262144 | tf_op args[5]
  7.1 1.4 %collective-permute-start.6 = (bf16[1152,128]{1,0:T(8,128)(2,1)S(1)}, bf16[1152,128]{1,0:T(8,128)(2,1)S(1)}, u32[]{:S(2)}, u32[]{:S(2)}) collective-permute-start(bf16[1152,128]{1,0:T(8,128)(2,1)S(1)} %copy-done.6), channel_id=1, source_target_pairs={{0,3},{1,4},{4,1},{5,8},{8,5},{9,12},{12,9},{13,14},{14,13},{15,10... | collective-permute-start | bytes 884744 | tf_op jit(solution)/shard_map/ppermute | solution.py:412
  8.8 1.3 %collective-permute-done.refs_1_ = bf16[1152,128]{1,0:T(8,128)(2,1)S(1)} collective-permute-done((bf16[1152,128]{1,0:T(8,128)(2,1)}, bf16[1152,128]{1,0:T(8,128)(2,1)S(1)}, u32[]{:S(2)}, u32[]{:S(2)}) %collective-permute-start) | collective-permute-done | bytes 294944 | tf_op jit(solution)/shard_map/ppermute | solution.py:412
  10.1 2.4 %collective-permute-start.1 = (bf16[1152,128]{1,0:T(8,128)(2,1)S(1)}, bf16[1152,128]{1,0:T(8,128)(2,1)S(1)}, u32[]{:S(2)}, u32[]{:S(2)}) collective-permute-start(bf16[1152,128]{1,0:T(8,128)(2,1)S(1)} %collective-permute-done.refs_1_), channel_id=1, source_target_pairs={{0,4},{1,3},{4,8},{5,1},{8,12},{9,5},{12,14},{13,9},{14,10},{15,13... | collective-permute-start | bytes 884744 | tf_op jit(solution)/shard_map/ppermute | solution.py:412
  12.5 1.0 %collective-permute-done.6.refs_2_ = bf16[1152,128]{1,0:T(8,128)(2,1)S(1)} collective-permute-done((bf16[1152,128]{1,0:T(8,128)(2,1)S(1)}, bf16[1152,128]{1,0:T(8,128)(2,1)S(1)}, u32[]{:S(2)}, u32[]{:S(2)}) %collective-permute-start.6) | collective-permute-done | bytes 294944 | tf_op jit(solution)/shard_map/ppermute | solution.py:412
  13.5 1.8 %collective-permute-start.7 = (bf16[1152,128]{1,0:T(8,128)(2,1)S(1)}, bf16[1152,128]{1,0:T(8,128)(2,1)S(1)}, u32[]{:S(2)}, u32[]{:S(2)}) collective-permute-start(bf16[1152,128]{1,0:T(8,128)(2,1)S(1)} %collective-permute-done.6.refs_2_), channel_id=1, source_target_pairs={{0,4},{1,3},{4,8},{5,1},{8,12},{9,5},{12,14},{13,9},{14,10},{15,13... | collective-permute-start | bytes 884744 | tf_op jit(solution)/shard_map/ppermute | solution.py:412
  15.5 0.9 %collective-permute-done.4 = s32[8,128]{1,0:T(8,128)S(1)} collective-permute-done((s32[8,128]{1,0:T(8,128)S(1)}, s32[8,128]{1,0:T(8,128)S(1)}, u32[]{:S(2)}, u32[]{:S(2)}) %collective-permute-start.4) | collective-permute-done | bytes 4128 | tf_op jit(solution)/shard_map/ppermute | solution.py:412
  16.4 1.0 %collective-permute-done.1.refs_3_ = bf16[1152,128]{1,0:T(8,128)(2,1)S(1)} collective-permute-done((bf16[1152,128]{1,0:T(8,128)(2,1)S(1)}, bf16[1152,128]{1,0:T(8,128)(2,1)S(1)}, u32[]{:S(2)}, u32[]{:S(2)}) %collective-permute-start.1) | collective-permute-done | bytes 294944 | tf_op jit(solution)/shard_map/ppermute | solution.py:412
  17.5 1.7 %collective-permute-start.5 = (bf16[1152,128]{1,0:T(8,128)(2,1)S(1)}, bf16[1152,128]{1,0:T(8,128)(2,1)S(1)}, u32[]{:S(2)}, u32[]{:S(2)}) collective-permute-start(bf16[1152,128]{1,0:T(8,128)(2,1)S(1)} %collective-permute-done.1.refs_3_), channel_id=1, source_target_pairs={{0,4},{1,3},{4,8},{5,1},{8,12},{9,5},{12,14},{13,9},{14,10},{15,13... | collective-permute-start | bytes 884744 | tf_op jit(solution)/shard_map/ppermute | solution.py:412
  19.2 1.4 %collective-permute-done.7.refs_4_ = bf16[1152,128]{1,0:T(8,128)(2,1)S(1)} collective-permute-done((bf16[1152,128]{1,0:T(8,128)(2,1)S(1)}, bf16[1152,128]{1,0:T(8,128)(2,1)S(1)}, u32[]{:S(2)}, u32[]{:S(2)}) %collective-permute-start.7) | collective-permute-done | bytes 294944 | tf_op jit(solution)/shard_map/ppermute | solution.py:412
  20.6 1.7 %collective-permute-start.8 = (bf16[1152,128]{1,0:T(8,128)(2,1)S(1)}, bf16[1152,128]{1,0:T(8,128)(2,1)S(1)}, u32[]{:S(2)}, u32[]{:S(2)}) collective-permute-start(bf16[1152,128]{1,0:T(8,128)(2,1)S(1)} %collective-permute-done.7.refs_4_), channel_id=1, source_target_pairs={{0,4},{1,3},{4,8},{5,1},{8,12},{9,5},{12,14},{13,9},{14,10},{15,13... | collective-permute-start | bytes 884744 | tf_op jit(solution)/shard_map/ppermute | solution.py:412
  22.4 1.8 %collective-permute-done.5.refs_5_ = bf16[1152,128]{1,0:T(8,128)(2,1)S(1)} collective-permute-done((bf16[1152,128]{1,0:T(8,128)(2,1)S(1)}, bf16[1152,128]{1,0:T(8,128)(2,1)S(1)}, u32[]{:S(2)}, u32[]{:S(2)}) %collective-permute-start.5) | collective-permute-done | bytes 294944 | tf_op jit(solution)/shard_map/ppermute | solution.py:412
  24.2 1.7 %collective-permute-start.9 = (bf16[1152,128]{1,0:T(8,128)(2,1)S(1)}, bf16[1152,128]{1,0:T(8,128)(2,1)S(1)}, u32[]{:S(2)}, u32[]{:S(2)}) collective-permute-start(bf16[1152,128]{1,0:T(8,128)(2,1)S(1)} %collective-permute-done.5.refs_5_), channel_id=1, source_target_pairs={{0,4},{1,3},{4,8},{5,1},{8,12},{9,5},{12,14},{13,9},{14,10},{15,13... | collective-permute-start | bytes 884744 | tf_op jit(solution)/shard_map/ppermute | solution.py:412
  25.9 4.0 %near.2 = (f32[257,64,128]{2,1,0:T(8,128)S(1)}, bf16[128,128,128]{2,1,0:T(8,128)(2,1)S(1)}) custom-call(s32[16,128]{1,0:T(8,128)S(1)} %pad_add_fusion.list_ref, bf16[1152,128]{1,0:T(8,128)(2,1)S(1)} %collective-permute-done.3.refs_0_, bf16[1152,128]{1,0:T(8,128)(2,1)S(1)} %collective-permute-done.refs_1_, ...), custom_call_target="tpu_custom_call", output_to_operand_aliasing={{0}: (9, {})} | custom-call | flops 2147483648 | bytes 16777216 | tf_op jit(solution)/shard_map/near/pallas_call | solution.py:477
  30.0 1.0 %collective-permute-done.9.refs_7_ = bf16[1152,128]{1,0:T(8,128)(2,1)S(1)} collective-permute-done((bf16[1152,128]{1,0:T(8,128)(2,1)S(1)}, bf16[1152,128]{1,0:T(8,128)(2,1)S(1)}, u32[]{:S(2)}, u32[]{:S(2)}) %collective-permute-start.9) | collective-permute-done | bytes 294944 | tf_op jit(solution)/shard_map/ppermute | solution.py:412
  30.9 2.5 %near.3 = (f32[257,64,128]{2,1,0:T(8,128)S(1)}, bf16[1024,128]{1,0:T(8,128)(2,1)S(1)}, bf16[32,64,128]{2,1,0:T(8,128)(2,1)S(1)}, bf16[96,64,128]{2,1,0:T(8,128)(2,1)S(1)}) custom-call(s32[16,128]{1,0:T(8,128)S(1)} %pad_add_fusion.list_ref, bf16[1152,128]{1,0:T(8,128)(2,1)S(1)} %collective-permute-done.3.refs_0_, ...), custom_call_target="tpu_custom_call", output_to_operand_aliasing={{0}: (11, {})} | custom-call | flops 2147483648 | bytes 16777216 | tf_op jit(solution)/shard_map/near/pallas_call | solution.py:477
  33.5 1.9 %collective-permute-done.11 = bf16[32,64,128]{2,1,0:T(8,128)(2,1)S(1)} collective-permute-done((bf16[32,64,128]{2,1,0:T(8,128)(2,1)S(1)}, bf16[32,64,128]{2,1,0:T(8,128)(2,1)S(1)}, u32[]{:S(2)}, u32[]{:S(2)}) %collective-permute-start.11) | collective-permute-done | bytes 524320 | tf_op jit(solution)/shard_map/ppermute | solution.py:412
  35.7 2.0 %collective-permute-start.12 = (bf16[16,64,128]{2,1,0:T(8,128)(2,1)S(1)}, bf16[16,64,128]{2,1,0:T(8,128)(2,1)S(1)}, u32[]{:S(2)}, u32[]{:S(2)}) collective-permute-start(bf16[16,64,128]{2,1,0:T(8,128)(2,1)S(1)} %get-tuple-element.56), channel_id=1, source_target_pairs={{0,4},{1,3},{4,8},{5,1},{8,12},{9,5},{12,14},{13,9},{14,10},{15,13... | collective-permute-start | bytes 786440 | tf_op jit(solution)/shard_map/ppermute | solution.py:412
  37.8 1.3 %collective-permute-start.15 = (bf16[16,64,128]{2,1,0:T(8,128)(2,1)S(1)}, bf16[16,64,128]{2,1,0:T(8,128)(2,1)S(1)}, u32[]{:S(2)}, u32[]{:S(2)}) collective-permute-start(bf16[16,64,128]{2,1,0:T(8,128)(2,1)S(1)} %get-tuple-element.58), channel_id=1, source_target_pairs={{0,4},{1,3},{4,8},{5,1},{8,12},{9,5},{12,14},{13,9},{14,10},{15,13... | collective-permute-start | bytes 786440 | tf_op jit(solution)/shard_map/ppermute | solution.py:412
  39.1 3.3 %collective-permute-done.12 = bf16[16,64,128]{2,1,0:T(8,128)(2,1)S(1)} collective-permute-done((bf16[16,64,128]{2,1,0:T(8,128)(2,1)S(1)}, bf16[16,64,128]{2,1,0:T(8,128)(2,1)S(1)}, u32[]{:S(2)}, u32[]{:S(2)}) %collective-permute-start.12) | collective-permute-done | bytes 262176 | tf_op jit(solution)/shard_map/ppermute | solution.py:412
  42.5 1.8 %collective-permute-start.14 = (bf16[16,64,128]{2,1,0:T(8,128)(2,1)S(1)}, bf16[16,64,128]{2,1,0:T(8,128)(2,1)S(1)}, u32[]{:S(2)}, u32[]{:S(2)}) collective-permute-start(bf16[16,64,128]{2,1,0:T(8,128)(2,1)S(1)} %add_convert_fusion.5), channel_id=1, source_target_pairs={{0,4},{1,3},{4,8},{5,1},{8,12},{9,5},{12,14},{13,9},{14,10},{15,13... | collective-permute-start | bytes 786440 | tf_op jit(solution)/shard_map/ppermute | solution.py:412
  45.3 1.8 %collective-permute-start.17 = (bf16[16,64,128]{2,1,0:T(8,128)(2,1)S(1)}, bf16[16,64,128]{2,1,0:T(8,128)(2,1)S(1)}, u32[]{:S(2)}, u32[]{:S(2)}) collective-permute-start(bf16[16,64,128]{2,1,0:T(8,128)(2,1)S(1)} %add_convert_fusion.4), channel_id=1, source_target_pairs={{0,4},{1,3},{4,8},{5,1},{8,12},{9,5},{12,14},{13,9},{14,10},{15,13... | collective-permute-start | bytes 786440 | tf_op jit(solution)/shard_map/ppermute | solution.py:412
  47.1 1.8 %collective-permute-done.14 = bf16[16,64,128]{2,1,0:T(8,128)(2,1)S(1)} collective-permute-done((bf16[16,64,128]{2,1,0:T(8,128)(2,1)S(1)}, bf16[16,64,128]{2,1,0:T(8,128)(2,1)S(1)}, u32[]{:S(2)}, u32[]{:S(2)}) %collective-permute-start.14) | collective-permute-done | bytes 262176 | tf_op jit(solution)/shard_map/ppermute | solution.py:412
  49.1 1.8 %collective-permute-start.16 = (bf16[16,64,128]{2,1,0:T(8,128)(2,1)S(1)}, bf16[16,64,128]{2,1,0:T(8,128)(2,1)S(1)}, u32[]{:S(2)}, u32[]{:S(2)}) collective-permute-start(bf16[16,64,128]{2,1,0:T(8,128)(2,1)S(1)} %add_convert_fusion.3), channel_id=1, source_target_pairs={{0,4},{1,3},{4,8},{5,1},{8,12},{9,5},{12,14},{13,9},{14,10},{15,13... | collective-permute-start | bytes 786440 | tf_op jit(solution)/shard_map/ppermute | solution.py:412
  51.9 1.8 %collective-permute-start.19 = (bf16[16,64,128]{2,1,0:T(8,128)(2,1)S(1)}, bf16[16,64,128]{2,1,0:T(8,128)(2,1)S(1)}, u32[]{:S(2)}, u32[]{:S(2)}) collective-permute-start(bf16[16,64,128]{2,1,0:T(8,128)(2,1)S(1)} %add_convert_fusion.2), channel_id=1, source_target_pairs={{0,4},{1,3},{4,8},{5,1},{8,12},{9,5},{12,14},{13,9},{14,10},{15,13... | collective-permute-start | bytes 786440 | tf_op jit(solution)/shard_map/ppermute | solution.py:412
  53.7 1.8 %collective-permute-done.16 = bf16[16,64,128]{2,1,0:T(8,128)(2,1)S(1)} collective-permute-done((bf16[16,64,128]{2,1,0:T(8,128)(2,1)S(1)}, bf16[16,64,128]{2,1,0:T(8,128)(2,1)S(1)}, u32[]{:S(2)}, u32[]{:S(2)}) %collective-permute-start.16) | collective-permute-done | bytes 262176 | tf_op jit(solution)/shard_map/ppermute | solution.py:412
  55.6 1.8 %collective-permute-start.18 = (bf16[16,64,128]{2,1,0:T(8,128)(2,1)S(1)}, bf16[16,64,128]{2,1,0:T(8,128)(2,1)S(1)}, u32[]{:S(2)}, u32[]{:S(2)}) collective-permute-start(bf16[16,64,128]{2,1,0:T(8,128)(2,1)S(1)} %add_convert_fusion.1), channel_id=1, source_target_pairs={{0,4},{1,3},{4,8},{5,1},{8,12},{9,5},{12,14},{13,9},{14,10},{15,13... | collective-permute-start | bytes 786440 | tf_op jit(solution)/shard_map/ppermute | solution.py:412
  57.4 0.9 %collective-permute-done.19 = bf16[16,64,128]{2,1,0:T(8,128)(2,1)S(1)} collective-permute-done((bf16[16,64,128]{2,1,0:T(8,128)(2,1)S(1)}, bf16[16,64,128]{2,1,0:T(8,128)(2,1)S(1)}, u32[]{:S(2)}, u32[]{:S(2)}) %collective-permute-start.19) | collective-permute-done | bytes 262176 | tf_op jit(solution)/shard_map/ppermute | solution.py:412
  58.4 2.5 %far.1 = f32[16,64,128]{2,1,0:T(8,128)S(1)} custom-call(bf16[1024,128]{1,0:T(8,128)(2,1)S(1)} %get-tuple-element.53.refs_0_, bf16[1024,128]{1,0:T(8,128)(2,1)S(1)} %collective-permute-done.10.refs_1_, s32[1]{0:T(128)} %bitcast.me_ref.token_ref.refs_2_, bf16[16,16,256]{2,1,0:T(8,128)(2,1)S(1)} %bitcast.10, s32[1,256]{1,0:T(1,128)S(1)} %bitcast.11, ...), custom_call_target="tpu_custom_call" | custom-call | flops 536870912 | bytes 8388608 | tf_op jit(solution)/shard_map/far/pallas_call | solution.py:501
  60.9 1.2 %collective-permute-done.18 = bf16[16,64,128]{2,1,0:T(8,128)(2,1)S(1)} collective-permute-done((bf16[16,64,128]{2,1,0:T(8,128)(2,1)S(1)}, bf16[16,64,128]{2,1,0:T(8,128)(2,1)S(1)}, u32[]{:S(2)}, u32[]{:S(2)}) %collective-permute-start.18) | collective-permute-done | bytes 262176 | tf_op jit(solution)/shard_map/ppermute | solution.py:412
  (39 shorter events, 5.7 us)
Async XLA Ops:
  0.0 17.5 %collective-permute-start.2 = (bf16[128,128,128]{2,1,0:T(8,128)(2,1)}, bf16[128,128,128]{2,1,0:T(8,128)(2,1)}, u32[]{:S(2)}, u32[]{:S(2)}) collective-permute-start(bf16[128,128,128]{2,1,0:T(8,128)(2,1)} %refs_8_.1), channel_id=1, source_target_pairs={{0,1},{1,0},{2,3},{3,2},{4,5},{5,4},{6,7},{7,6},{8,9},{9,8},{10,11... | collective-permute-start | bytes 12582920 | tf_op jit(solution)/shard_map/ppermute | solution.py:412
  2.6 7.5 %collective-permute-start = (bf16[1152,128]{1,0:T(8,128)(2,1)}, bf16[1152,128]{1,0:T(8,128)(2,1)S(1)}, u32[]{:S(2)}, u32[]{:S(2)}) collective-permute-start(bf16[1152,128]{1,0:T(8,128)(2,1)} %get-tuple-element.43), channel_id=1, source_target_pairs={{0,4},{1,3},{4,8},{5,1},{8,12},{9,5},{12,14},{13,9},{14,10},{15,13... | collective-permute-start | bytes 884744 | tf_op jit(solution)/shard_map/ppermute | solution.py:412
  6.1 1.0 %copy-start.6 = (bf16[1152,128]{1,0:T(8,128)(2,1)S(1)}, bf16[1152,128]{1,0:T(8,128)(2,1)}, u32[]{:S(2)}) copy-start(bf16[1152,128]{1,0:T(8,128)(2,1)} %get-tuple-element.43) | copy-start | bytes 884740
  6.1 9.1 %copy-start.5 = (s32[8,128]{1,0:T(8,128)S(1)}, s32[8,128]{1,0:T(8,128)}, u32[]{:S(2)}) copy-start(s32[8,128]{1,0:T(8,128)} %get-tuple-element.44) | copy-start | bytes 12292
  6.1 19.8 %copy-start = (bf16[128,128,128]{2,1,0:T(8,128)(2,1)S(1)}, bf16[128,128,128]{2,1,0:T(8,128)(2,1)}, u32[]{:S(2)}) copy-start(bf16[128,128,128]{2,1,0:T(8,128)(2,1)} %refs_8_.1) | copy-start | bytes 12582916
  7.1 6.4 %collective-permute-start.6 = (bf16[1152,128]{1,0:T(8,128)(2,1)S(1)}, bf16[1152,128]{1,0:T(8,128)(2,1)S(1)}, u32[]{:S(2)}, u32[]{:S(2)}) collective-permute-start(bf16[1152,128]{1,0:T(8,128)(2,1)S(1)} %copy-done.6), channel_id=1, source_target_pairs={{0,3},{1,4},{4,1},{5,8},{8,5},{9,12},{12,9},{13,14},{14,13},{15,10... | collective-permute-start | bytes 884744 | tf_op jit(solution)/shard_map/ppermute | solution.py:412
  8.4 8.0 %collective-permute-start.3 = (bf16[1152,128]{1,0:T(8,128)(2,1)S(1)}, bf16[1152,128]{1,0:T(8,128)(2,1)S(1)}, u32[]{:S(2)}, u32[]{:S(2)}) collective-permute-start(bf16[1152,128]{1,0:T(8,128)(2,1)S(1)} %copy-done.6), channel_id=1, source_target_pairs={{0,1},{1,0},{2,3},{3,2},{4,5},{5,4},{6,7},{7,6},{8,9},{9,8},{10,11... | collective-permute-start | bytes 884744 | tf_op jit(solution)/shard_map/ppermute | solution.py:412
  10.1 7.4 %collective-permute-start.1 = (bf16[1152,128]{1,0:T(8,128)(2,1)S(1)}, bf16[1152,128]{1,0:T(8,128)(2,1)S(1)}, u32[]{:S(2)}, u32[]{:S(2)}) collective-permute-start(bf16[1152,128]{1,0:T(8,128)(2,1)S(1)} %collective-permute-done.refs_1_), channel_id=1, source_target_pairs={{0,4},{1,3},{4,8},{5,1},{8,12},{9,5},{12,14},{13,9},{14,10},{15,13... | collective-permute-start | bytes 884744 | tf_op jit(solution)/shard_map/ppermute | solution.py:412
  13.5 7.2 %collective-permute-start.7 = (bf16[1152,128]{1,0:T(8,128)(2,1)S(1)}, bf16[1152,128]{1,0:T(8,128)(2,1)S(1)}, u32[]{:S(2)}, u32[]{:S(2)}) collective-permute-start(bf16[1152,128]{1,0:T(8,128)(2,1)S(1)} %collective-permute-done.6.refs_2_), channel_id=1, source_target_pairs={{0,4},{1,3},{4,8},{5,1},{8,12},{9,5},{12,14},{13,9},{14,10},{15,13... | collective-permute-start | bytes 884744 | tf_op jit(solution)/shard_map/ppermute | solution.py:412
  15.3 1.2 %collective-permute-start.4 = (s32[8,128]{1,0:T(8,128)S(1)}, s32[8,128]{1,0:T(8,128)S(1)}, u32[]{:S(2)}, u32[]{:S(2)}) collective-permute-start(s32[8,128]{1,0:T(8,128)S(1)} %copy-done.5), channel_id=1, source_target_pairs={{0,1},{1,0},{2,3},{3,2},{4,5},{5,4},{6,7},{7,6},{8,9},{9,8},{10,11... | collective-permute-start | bytes 12296 | tf_op jit(solution)/shard_map/ppermute | solution.py:412
  17.5 6.7 %collective-permute-start.5 = (bf16[1152,128]{1,0:T(8,128)(2,1)S(1)}, bf16[1152,128]{1,0:T(8,128)(2,1)S(1)}, u32[]{:S(2)}, u32[]{:S(2)}) collective-permute-start(bf16[1152,128]{1,0:T(8,128)(2,1)S(1)} %collective-permute-done.1.refs_3_), channel_id=1, source_target_pairs={{0,4},{1,3},{4,8},{5,1},{8,12},{9,5},{12,14},{13,9},{14,10},{15,13... | collective-permute-start | bytes 884744 | tf_op jit(solution)/shard_map/ppermute | solution.py:412
  20.6 9.3 %collective-permute-start.8 = (bf16[1152,128]{1,0:T(8,128)(2,1)S(1)}, bf16[1152,128]{1,0:T(8,128)(2,1)S(1)}, u32[]{:S(2)}, u32[]{:S(2)}) collective-permute-start(bf16[1152,128]{1,0:T(8,128)(2,1)S(1)} %collective-permute-done.7.refs_4_), channel_id=1, source_target_pairs={{0,4},{1,3},{4,8},{5,1},{8,12},{9,5},{12,14},{13,9},{14,10},{15,13... | collective-permute-start | bytes 884744 | tf_op jit(solution)/shard_map/ppermute | solution.py:412
  24.2 6.7 %collective-permute-start.9 = (bf16[1152,128]{1,0:T(8,128)(2,1)S(1)}, bf16[1152,128]{1,0:T(8,128)(2,1)S(1)}, u32[]{:S(2)}, u32[]{:S(2)}) collective-permute-start(bf16[1152,128]{1,0:T(8,128)(2,1)S(1)} %collective-permute-done.5.refs_5_), channel_id=1, source_target_pairs={{0,4},{1,3},{4,8},{5,1},{8,12},{9,5},{12,14},{13,9},{14,10},{15,13... | collective-permute-start | bytes 884744 | tf_op jit(solution)/shard_map/ppermute | solution.py:412
  33.4 2.0 %collective-permute-start.11 = (bf16[32,64,128]{2,1,0:T(8,128)(2,1)S(1)}, bf16[32,64,128]{2,1,0:T(8,128)(2,1)S(1)}, u32[]{:S(2)}, u32[]{:S(2)}) collective-permute-start(bf16[32,64,128]{2,1,0:T(8,128)(2,1)S(1)} %get-tuple-element.55), channel_id=1, source_target_pairs={{0,1},{1,0},{2,3},{3,2},{4,5},{5,4},{6,7},{7,6},{8,9},{9,8},{10,11... | collective-permute-start | bytes 1572872 | tf_op jit(solution)/shard_map/ppermute | solution.py:412
  35.4 22.9 %copy-start.1 = (bf16[16,16,128]{2,1,0:T(8,128)(2,1)S(1)}, bf16[16,16,128]{2,1,0:T(8,128)(2,1)}, u32[]{:S(2)}) copy-start(bf16[16,16,128]{2,1,0:T(8,128)(2,1)} %refs_7_.1) | copy-start | bytes 196612
  35.4 22.9 %copy-start.2 = (s32[256]{0:T(256)S(1)}, s32[256]{0:T(256)}, u32[]{:S(2)}) copy-start(s32[256]{0:T(256)} %param.17) | copy-start | bytes 3076
  35.4 23.0 %copy-start.3 = (s32[256,1]{0,1:T(1,128)S(1)}, s32[256,1]{0,1:T(1,128)}, u32[]{:S(2)}) copy-start(s32[256,1]{0,1:T(1,128)} %param.18) | copy-start | bytes 3076
  35.4 23.0 %copy-start.4 = (s32[256]{0:T(256)S(1)}, s32[256]{0:T(256)}, u32[]{:S(2)}) copy-start(s32[256]{0:T(256)} %param.19) | copy-start | bytes 3076
  35.5 6.9 %collective-permute-start.13 = (bf16[96,64,128]{2,1,0:T(8,128)(2,1)S(1)}, bf16[96,64,128]{2,1,0:T(8,128)(2,1)S(1)}, u32[]{:S(2)}, u32[]{:S(2)}) collective-permute-start(bf16[96,64,128]{2,1,0:T(8,128)(2,1)S(1)} %get-tuple-element.59), channel_id=1, source_target_pairs={{0,1},{1,0},{2,3},{3,2},{4,5},{5,4},{6,7},{7,6},{8,9},{9,8},{10,11... | collective-permute-start | bytes 4718600 | tf_op jit(solution)/shard_map/ppermute | solution.py:412
  35.7 6.7 %collective-permute-start.12 = (bf16[16,64,128]{2,1,0:T(8,128)(2,1)S(1)}, bf16[16,64,128]{2,1,0:T(8,128)(2,1)S(1)}, u32[]{:S(2)}, u32[]{:S(2)}) collective-permute-start(bf16[16,64,128]{2,1,0:T(8,128)(2,1)S(1)} %get-tuple-element.56), channel_id=1, source_target_pairs={{0,4},{1,3},{4,8},{5,1},{8,12},{9,5},{12,14},{13,9},{14,10},{15,13... | collective-permute-start | bytes 786440 | tf_op jit(solution)/shard_map/ppermute | solution.py:412
  37.8 7.4 %collective-permute-start.15 = (bf16[16,64,128]{2,1,0:T(8,128)(2,1)S(1)}, bf16[16,64,128]{2,1,0:T(8,128)(2,1)S(1)}, u32[]{:S(2)}, u32[]{:S(2)}) collective-permute-start(bf16[16,64,128]{2,1,0:T(8,128)(2,1)S(1)} %get-tuple-element.58), channel_id=1, source_target_pairs={{0,4},{1,3},{4,8},{5,1},{8,12},{9,5},{12,14},{13,9},{14,10},{15,13... | collective-permute-start | bytes 786440 | tf_op jit(solution)/shard_map/ppermute | solution.py:412
  42.5 6.4 %collective-permute-start.14 = (bf16[16,64,128]{2,1,0:T(8,128)(2,1)S(1)}, bf16[16,64,128]{2,1,0:T(8,128)(2,1)S(1)}, u32[]{:S(2)}, u32[]{:S(2)}) collective-permute-start(bf16[16,64,128]{2,1,0:T(8,128)(2,1)S(1)} %add_convert_fusion.5), channel_id=1, source_target_pairs={{0,4},{1,3},{4,8},{5,1},{8,12},{9,5},{12,14},{13,9},{14,10},{15,13... | collective-permute-start | bytes 786440 | tf_op jit(solution)/shard_map/ppermute | solution.py:412
  45.3 6.4 %collective-permute-start.17 = (bf16[16,64,128]{2,1,0:T(8,128)(2,1)S(1)}, bf16[16,64,128]{2,1,0:T(8,128)(2,1)S(1)}, u32[]{:S(2)}, u32[]{:S(2)}) collective-permute-start(bf16[16,64,128]{2,1,0:T(8,128)(2,1)S(1)} %add_convert_fusion.4), channel_id=1, source_target_pairs={{0,4},{1,3},{4,8},{5,1},{8,12},{9,5},{12,14},{13,9},{14,10},{15,13... | collective-permute-start | bytes 786440 | tf_op jit(solution)/shard_map/ppermute | solution.py:412
  49.1 6.4 %collective-permute-start.16 = (bf16[16,64,128]{2,1,0:T(8,128)(2,1)S(1)}, bf16[16,64,128]{2,1,0:T(8,128)(2,1)S(1)}, u32[]{:S(2)}, u32[]{:S(2)}) collective-permute-start(bf16[16,64,128]{2,1,0:T(8,128)(2,1)S(1)} %add_convert_fusion.3), channel_id=1, source_target_pairs={{0,4},{1,3},{4,8},{5,1},{8,12},{9,5},{12,14},{13,9},{14,10},{15,13... | collective-permute-start | bytes 786440 | tf_op jit(solution)/shard_map/ppermute | solution.py:412
  50.9 7.4 %collective-permute-start.10 = (bf16[1024,128]{1,0:T(8,128)(2,1)S(1)}, bf16[1024,128]{1,0:T(8,128)(2,1)S(1)}, u32[]{:S(2)}, u32[]{:S(2)}) collective-permute-start(bf16[1024,128]{1,0:T(8,128)(2,1)S(1)} %get-tuple-element.53.refs_0_), channel_id=1, source_target_pairs={{0,1},{1,0},{2,3},{3,2},{4,5},{5,4},{6,7},{7,6},{8,9},{9,8},{10,11... | collective-permute-start | bytes 786440 | tf_op jit(solution)/shard_map/ppermute | solution.py:412
  51.9 6.4 %collective-permute-start.19 = (bf16[16,64,128]{2,1,0:T(8,128)(2,1)S(1)}, bf16[16,64,128]{2,1,0:T(8,128)(2,1)S(1)}, u32[]{:S(2)}, u32[]{:S(2)}) collective-permute-start(bf16[16,64,128]{2,1,0:T(8,128)(2,1)S(1)} %add_convert_fusion.2), channel_id=1, source_target_pairs={{0,4},{1,3},{4,8},{5,1},{8,12},{9,5},{12,14},{13,9},{14,10},{15,13... | collective-permute-start | bytes 786440 | tf_op jit(solution)/shard_map/ppermute | solution.py:412
  55.6 6.4 %collective-permute-start.18 = (bf16[16,64,128]{2,1,0:T(8,128)(2,1)S(1)}, bf16[16,64,128]{2,1,0:T(8,128)(2,1)S(1)}, u32[]{:S(2)}, u32[]{:S(2)}) collective-permute-start(bf16[16,64,128]{2,1,0:T(8,128)(2,1)S(1)} %add_convert_fusion.1), channel_id=1, source_target_pairs={{0,4},{1,3},{4,8},{5,1},{8,12},{9,5},{12,14},{13,9},{14,10},{15,13... | collective-permute-start | bytes 786440 | tf_op jit(solution)/shard_map/ppermute | solution.py:412
  58.3 3.9 %collective-permute-start.20 = (bf16[16,64,128]{2,1,0:T(8,128)(2,1)S(1)}, bf16[16,64,128]{2,1,0:T(8,128)(2,1)S(1)}, u32[]{:S(2)}, u32[]{:S(2)}) collective-permute-start(bf16[16,64,128]{2,1,0:T(8,128)(2,1)S(1)} %collective-permute-done.19), channel_id=1, source_target_pairs={{0,1},{1,0},{2,3},{3,2},{4,5},{5,4},{6,7},{7,6},{8,9},{9,8},{10,11... | collective-permute-start | bytes 786440 | tf_op jit(solution)/shard_map/ppermute | solution.py:412
